TPU v7x, 32 devices: a whole 2x2x4 slice. The times are simulated.
32 devices in a mesh: pole: 2 (over y), wave: 16 (over z, x, core).
Axes of the slice: x: 2, y: 2, z: 4, core: 2. Of those that a mesh axis runs over, the one named last changes fastest.
Arguments:
- tendency: bfloat16 [6, 2560, 32, 128], P('pole', 'wave'), may hold values from -6 to 6
- spectral_state: bfloat16 [6, 32, 128, 1280], P('pole', 'wave'), may hold values from -6 to 6
- legendre: bfloat16 [32, 1280, 2560], P('wave'), may hold values from -0.15625 to 0.15625
- gauss_weights: float32 [2560], P('wave'), may hold values from 0.35 to 1.05
- block_inverses: bfloat16 [64, 18, 32, 1280], P('pole', None, 'wave'), may hold values from -0.21875 to 0.21875
- pole_coeffs: float32 [64, 2], P('pole'), may hold values from -4 to 4
- wavenumbers: int32 [32], P('wave'), may hold values from 0 to 1279, as said below
Outputs:
- grid_state: bfloat16 [6, 2560, 32, 128], P('pole', 'wave')
Inputs may be any that keep to these rules, and one draw needn't show every extreme that they name: `wavenumbers`: entries 2 i and 2 i + 1 hold w and 1279 - w for some w below 640; all entries differ, and 0 is among them.
All inputs are finite; a program needn't handle non-finite values.
Results may differ from a plain program's by a relative error of at most 0.0062.
Values may be sent and summed in bfloat16 or wider, within the bound.
No kernel may reach another device: no remote copies, remote signals or barrier semaphores. Data moves between devices by JAX's collectives and lax.ppermute only.
A program may use at most 128 MiB of HBM per device.

v0:
```python
import jax
import jax.numpy as jnp
from jax import lax
from jax.sharding import PartitionSpec as P


def mix_rows(real_matrix, imag_matrix, leading, trailing, orientation):
    summed = jnp.zeros(leading.shape, jnp.float32)
    for column in range(3):
        summed = summed + real_matrix[:, column, :, None, :] * leading[column][None]
        summed = summed + orientation * imag_matrix[:, column, :, None, :] * trailing[column][None]
    return summed


def per_device(
    tendency, spectral_state, legendre, gauss_weights, block_inverses, pole_coeffs, wavenumbers
):
    weighted = (tendency.astype(jnp.float32) * gauss_weights[None, :, None, None]).astype(
        jnp.bfloat16
    )
    received = lax.all_to_all(weighted, "wave", split_axis=2, concat_axis=1, tiled=True)
    spectral_tend = jnp.einsum(
        "rjse,snj->rsen", received, legendre, preferred_element_type=jnp.float32
    )
    degree = lax.broadcasted_iota(jnp.int32, (legendre.shape[0], legendre.shape[1]), 1)
    live_mask = (degree >= wavenumbers[:, None]).astype(jnp.float32)
    forced = (
        (spectral_state.astype(jnp.float32) + spectral_tend) * live_mask[None, :, None, :]
    ).astype(jnp.bfloat16)
    full_forced = lax.all_gather(forced, "pole", axis=0, tiled=True)
    pole_index = lax.axis_index("pole")
    local_pairs = block_inverses.shape[0]
    flat_inverse = block_inverses.reshape(local_pairs, -1).astype(jnp.float32)
    weighted_sums = jnp.dot(pole_coeffs.T, flat_inverse, precision=lax.Precision.HIGHEST)
    weighted_sums = weighted_sums.reshape(
        2, 2, 3, 3, block_inverses.shape[2], block_inverses.shape[3]
    )
    real_matrix = weighted_sums[0, 0] - weighted_sums[1, 1]
    imag_matrix = weighted_sums[0, 1] + weighted_sums[1, 0]
    forced_wide = full_forced.astype(jnp.float32)
    real_matrix, imag_matrix = lax.psum((real_matrix, imag_matrix), "pole")
    leading = lax.dynamic_slice_in_dim(forced_wide, pole_index * 3, 3, 0)
    trailing = lax.dynamic_slice_in_dim(forced_wide, (1 - pole_index) * 3, 3, 0)
    orientation = (2 * pole_index - 1).astype(jnp.float32)
    advanced_rows = mix_rows(real_matrix, imag_matrix, leading, trailing, orientation)
    advanced = advanced_rows.astype(jnp.bfloat16)
    synthesized = jnp.einsum(
        "rsen,snj->rjse", advanced, legendre, preferred_element_type=jnp.float32
    ).astype(jnp.bfloat16)
    return lax.all_to_all(synthesized, "wave", split_axis=1, concat_axis=2, tiled=True)


def solution(mesh):
    in_specs = (
        P("pole", "wave", None, None),
        P("pole", "wave", None, None),
        P("wave", None, None),
        P("wave"),
        P("pole", None, "wave", None),
        P("pole", None),
        P("wave"),
    )
    out_specs = P("pole", "wave", None, None)
    return jax.shard_map(
        per_device, mesh=mesh, in_specs=in_specs, out_specs=out_specs, check_vma=False
    )
```

profile of v0, /device:TPU:8, one launch (start us, length us, event | category | flops | bytes accessed | tf_op | source)
XLA Modules:
  0.0 303.2 jit_solution(7973632448971455525)
XLA Ops:
  6.5 0.0 copy-start
  6.5 5.6 %multiply_convert_fusion = bf16[3,160,32,128]{3,1,0,2:T(8,128)(2,1)} fusion(bf16[3,160,32,128]{3,2,1,0:T(8,128)(2,1)} %param.7, f32[160]{0:T(256)} %param.10), kind=kLoop, calls=%fused_computation.4 | loop fusion | flops 5898240 | bytes 7864960 | tf_op jit(solution)/shard_map/convert_element_type | solution.py:18
  12.1 0.0 copy-start.2
  12.1 6.5 %all-to-all-start = ((bf16[3,160,32,128]{3,1,0,2:T(8,128)(2,1)}), bf16[3,160,32,128]{3,1,0,2:T(8,128)(2,1)}, u32[]{:S(2)}, u32[]{:S(2)}) async-start(bf16[3,160,32,128]{3,1,0,2:T(8,128)(2,1)} %multiply_convert_fusion), calls=%async_computation | async-start | bytes 7864320 | tf_op jit(solution)/shard_map/all_to_all | solution.py:21
  18.7 0.0 all-reduce.3.cloned.1.call-start
  18.7 0.0 copy-done.2
  18.7 3.5 %reshape.54 = bf16[32,46080]{1,0:T(8,128)(2,1)} reshape(bf16[32,18,2,1280]{3,2,1,0:T(2,128)(2,1)S(1)} %copy-done.2) | data formatting | bytes 5898240 | tf_op jit(solution)/shard_map/reshape | solution.py:33
  22.2 0.0 copy-start.3
  22.2 4.0 %dot_general.14 = bf16[2,3,3,2,1280,32]{4,3,2,1,0,5:T(2,128)(2,1)S(1)} reshape(bf16[46080,32]{0,1:T(8,128)(2,1)} %bitcast.67) | data formatting | bytes 5898240 | tf_op jit(solution)/shard_map/dot_general | solution.py:34
  26.3 0.0 copy-done
  26.3 1.3 fusion.17
  27.5 0.2 slice_subtract_fusion
  27.7 0.8 copy_bitcast_fusion
  28.5 0.0 all-reduce.3.cloned.1.call-update
  28.5 0.2 all-gather.2.cloned.1.call-start
  28.8 0.0 copy-done.3
  28.8 0.1 compare_convert_fusion
  28.8 75.0 %all-to-all-done = bf16[3,160,32,128]{3,1,0,2:T(8,128)(2,1)} async-done(((bf16[3,160,32,128]{3,1,0,2:T(8,128)(2,1)}), bf16[3,160,32,128]{3,1,0,2:T(8,128)(2,1)}, u32[]{:S(2)}, u32[]{:S(2)}) %all-to-all-start) | async-done | bytes 3932192 | tf_op jit(solution)/shard_map/all_to_all | solution.py:21
  103.9 0.0 copy-start.4
  103.9 2.6 copy.62
  106.5 0.1 copy-done.4
  106.6 10.4 %fusion.11 = bf16[3,2,128,1280]{3,2,0,1:T(8,128)(2,1)} fusion(bf16[2,1280,2560]{2,1,0:T(8,128)(2,1)} %param.9, bf16[3,2560,2,128]{3,1,2,0:T(8,128)(2,1)S(1)} %bitcast.68, bf16[3,2,128,1280]{3,2,1,0:T(8,128)(2,1)S(1)} %copy-done.4, f32[2,1280]{1,0:T(2,128)S(1)} %compare_convert_fusion), kind=kOutput, calls=%fused_computation.9 | convolution fusion | flops 5037096960 | bytes 20981760 | tf_op jit(solution)/shard_map/rjse,snj->rsen/dot_general | solution.py:22
  117.0 0.0 all-gather.2.cloned.1.call-update
  117.0 0.0 all-reduce.3.cloned.1.call-done
  117.1 0.8 fusion.33
  118.0 0.8 slice_bitcast_fusion.2
  118.8 53.6 %all-gather.2.cloned.1.call-done = bf16[6,2,128,1280]{3,2,0,1:T(8,128)(2,1)} async-done(((bf16[3,2,128,1280]{3,2,0,1:T(8,128)(2,1)}), bf16[6,2,128,1280]{3,2,0,1:T(8,128)(2,1)}) %all-gather.2.cloned.1.call-update) | async-done | bytes 3932176 | tf_op jit(solution)/shard_map/all_gather | solution.py:30
  172.4 2.9 convert_element_type.40
  175.3 0.5 dynamic-slice_bitcast_fusion.5
  175.9 12.3 %fusion.7 = bf16[3,2560,2,128]{1,3,0,2:T(8,128)(2,1)} fusion(bf16[2,1280,2560]{2,1,0:T(8,128)(2,1)} %param.9, f32[2,128,1280]{2,1,0:T(8,128)S(1)} %get-tuple-element.11, f32[3,2,1280]{2,0,1:T(4,128)S(1)} %copy.68, f32[2,128,1280]{2,1,0:T(8,128)S(1)} %get-tuple-element.12, f32[3,2,1280]{2,0,1:T(4,128)S(1)} %copy.67, ...), kind=kOutput, calls=%fused_computation.6 | convolution fusion | flops 5046927360 | bytes 25088000 | tf_op jit(solution)/shard_map/rsen,snj->rjse/dot_general | solution.py:47
  188.2 10.6 %copy.69 = bf16[3,2560,2,128]{3,2,0,1:T(2,128)(2,1)} copy(bf16[3,2560,2,128]{1,3,0,2:T(8,128)(2,1)} %fusion.7) | data formatting | bytes 7864320 | tf_op jit(solution)/shard_map/convert_element_type | solution.py:49
  198.8 93.1 %all_to_all.36 = bf16[3,2560,2,128]{3,2,0,1:T(2,128)(2,1)S(1)} all-to-all(bf16[3,2560,2,128]{3,2,0,1:T(2,128)(2,1)} %copy.69), channel_id=1, replica_groups=mesh['pole'=2,'wave'=16] {'wave'}, dimensions={1} | all-to-all | bytes 7864320 | tf_op jit(solution)/shard_map/all_to_all | solution.py:50
  291.9 0.5 copy.70
  292.4 0.5 copy.71
  292.9 0.0 copy-start.1
  292.9 3.4 %copy.72 = bf16[3,160,32,128]{3,2,1,0:T(8,128)(2,1)} copy(bf16[3,160,32,128]{3,1,2,0:T(8,128)(2,1)S(1)} %bitcast.66) | data formatting | bytes 7864320 | tf_op jit(solution)/shard_map/all_to_all | solution.py:50
  296.4 0.0 copy-done.1
  (6 shorter events, 0.1 us)
Async XLA Ops:
  6.5 19.7 %copy-start = (f32[32,2]{0,1:T(2,128)S(1)}, f32[32,2]{0,1:T(2,128)}, u32[]{:S(2)}) copy-start(f32[32,2]{0,1:T(2,128)} %param.12) | copy-start | bytes 772
  12.1 6.6 %copy-start.2 = (bf16[32,18,2,1280]{3,2,1,0:T(2,128)(2,1)S(1)}, bf16[32,18,2,1280]{3,2,1,0:T(2,128)(2,1)}, u32[]{:S(2)}) copy-start(bf16[32,18,2,1280]{3,2,1,0:T(2,128)(2,1)} %param.11) | copy-start | bytes 8847364
  12.1 91.7 %all-to-all-start = ((bf16[3,160,32,128]{3,1,0,2:T(8,128)(2,1)}), bf16[3,160,32,128]{3,1,0,2:T(8,128)(2,1)}, u32[]{:S(2)}, u32[]{:S(2)}) async-start(bf16[3,160,32,128]{3,1,0,2:T(8,128)(2,1)} %multiply_convert_fusion), calls=%async_computation | async-start | bytes 7864320 | tf_op jit(solution)/shard_map/all_to_all | solution.py:21
  18.7 98.4 %all-reduce.3.cloned.1.call-start = ((), (), s32[]{:S(2)}) async-start(), calls=%async_computation.3 | async-start | bytes 368640 | tf_op jit(solution)/shard_map/psum | solution.py:41
  22.2 6.5 %copy-start.3 = (s32[2]{0:T(128)S(1)}, s32[2]{0:T(128)}, u32[]{:S(2)}) copy-start(s32[2]{0:T(128)} %param.13) | copy-start | bytes 28
  28.5 143.9 %all-gather.2.cloned.1.call-start = ((), (), s32[]{:S(2)}) async-start(), calls=%async_computation.2 | async-start | bytes 5898240 | tf_op jit(solution)/shard_map/all_gather | solution.py:30
  103.9 2.7 copy-start.4
  292.9 3.5 %copy-start.1 = (f32[32,2]{0,1:T(2,128)S(1)}, f32[32,2]{0,1:T(2,128)}, u32[]{:S(2)}) copy-start(f32[32,2]{0,1:T(2,128)} %param.12) | copy-start | bytes 772
Sparse Core Ops, SparseCore 0:
  28.7 23.2 all-reduce.2
  117.2 55.2 all-gather.1
where the time goes:
time: 306 us; the launch traced here: 303 us
  waiting for transfers between devices  129 us (42%)
  blocking collectives  93.1 us (30%)
  local copies, waits for them, and re-layouts  27.6 us (9%)
  matrix products  24 us (8%)
  between operations  13.6 us (4%)
  other arithmetic  9.56 us (3%)
  starting transfers between devices  6.79 us (2%)
    all_to_all x1, blocking collectives, per_device(): lax.all_to_all(synthesized, 'wave', split_axis=1, concat_axis=2, tiled=True)  93.1 us
    all_to_all x1, waiting for transfers between devices, per_device(): lax.all_to_all(weighted, 'wave', split_axis=2, concat_axis=1, tiled=True)  75 us
    all_gather x1, waiting for transfers between devices, per_device(): full_forced = lax.all_gather(forced, 'pole', axis=0, tiled=True)  53.6 us
    dot_general x1, matrix products, per_device(): jnp.einsum('rsen,snj->rjse', advanced, legendre, preferred_element_type=j...  12.3 us
    convert_element_type x1, local copies, waits for them, and re-layouts, per_device(): synthesized = jnp.einsum('rsen,snj->rjse', advanced, legendre, preferred_...  10.6 us
    dot_general x1, matrix products, per_device(): jnp.einsum('rjse,snj->rsen', received, legendre, preferred_element_type=j...  10.4 us
    all_to_all x1, starting transfers between devices, per_device(): lax.all_to_all(weighted, 'wave', split_axis=2, concat_axis=1, tiled=True)  6.53 us
  transfers between devices with their start and end apart: 3, of which 2 were waited for; matrix products, arithmetic and copies ran while one was open for 8% of the time, Pallas kernels for 0%

commit v1 on v0

v1 whole, which is shorter than its diff:
```python
import jax
import jax.numpy as jnp
from jax import lax
from jax.sharding import PartitionSpec as P


def mix_rows(real_matrix, imag_matrix, leading, trailing, orientation):
    summed = 0.0
    for column in range(3):
        summed = summed + real_matrix[:, column, None, :] * leading[column][None]
        summed = summed + (orientation * imag_matrix[:, column, None, :]) * trailing[column][None]
    return summed


def per_device(
    tendency, spectral_state, legendre, gauss_weights, block_inverses, pole_coeffs, wavenumbers
):
    rows, lats, slots, members = tendency.shape
    local_slots, nspec = legendre.shape[:2]
    owners = slots // local_slots
    pole_index = lax.axis_index("pole")
    orientation = (2 * pole_index - 1).astype(jnp.float32)
    split = tendency.reshape(rows, lats, owners, local_slots, members)

    def send(slot):
        weighted = (split[:, :, :, slot, :].astype(jnp.float32) * gauss_weights[None, :, None, None]).astype(
            jnp.bfloat16
        )
        return lax.all_to_all(weighted, "wave", split_axis=2, concat_axis=1, tiled=True)

    received = [send(slot) for slot in range(local_slots)]

    local_pairs = block_inverses.shape[0]
    flat_inverse = block_inverses.reshape(local_pairs, -1).astype(jnp.float32)
    weighted_sums = jnp.dot(pole_coeffs.T, flat_inverse, precision=lax.Precision.HIGHEST)
    weighted_sums = weighted_sums.reshape(2, 2, 3, 3, local_slots, nspec)
    real_matrix = weighted_sums[0, 0] - weighted_sums[1, 1]
    imag_matrix = weighted_sums[0, 1] + weighted_sums[1, 0]
    real_matrix, imag_matrix = lax.psum((real_matrix, imag_matrix), "pole")

    degree = jnp.arange(nspec, dtype=jnp.int32)
    outputs = []
    for slot in range(local_slots):
        grid = received[slot].reshape(rows, -1, members)
        spectral_tend = jnp.einsum(
            "rje,nj->ren", grid, legendre[slot], preferred_element_type=jnp.float32
        )
        live = (degree >= wavenumbers[slot]).astype(jnp.float32)
        forced = ((spectral_state[:, slot].astype(jnp.float32) + spectral_tend) * live).astype(jnp.bfloat16)
        other = lax.ppermute(forced, "pole", [(0, 1), (1, 0)])
        advanced = mix_rows(
            real_matrix[:, :, slot],
            imag_matrix[:, :, slot],
            forced.astype(jnp.float32),
            other.astype(jnp.float32),
            orientation,
        ).astype(jnp.bfloat16)
        synthesized = jnp.einsum(
            "ren,nj->rje", advanced, legendre[slot], preferred_element_type=jnp.float32
        ).astype(jnp.bfloat16)
        outputs.append(
            lax.all_to_all(
                synthesized.reshape(rows, -1, 1, members), "wave", split_axis=1, concat_axis=2, tiled=True
            )
        )
    return jnp.stack(outputs, axis=3).reshape(tendency.shape)


def solution(mesh):
    in_specs = (
        P("pole", "wave", None, None),
        P("pole", "wave", None, None),
        P("wave", None, None),
        P("wave"),
        P("pole", None, "wave", None),
        P("pole", None),
        P("wave"),
    )
    out_specs = P("pole", "wave", None, None)
    return jax.shard_map(
        per_device, mesh=mesh, in_specs=in_specs, out_specs=out_specs, check_vma=False
    )
```

time: 306 us -> 257 us (0.84)
  blocking collectives: 93.1 us -> 0 us
  starting transfers between devices: 6.79 us -> 29.2 us
  local copies, waits for them, and re-layouts: 27.6 us -> 42.1 us
  waiting for transfers between devices: 129 us -> 143 us
  other arithmetic: 9.56 us -> 4.39 us
    all_to_all x1 -> x0, blocking collectives: 93.1 us -> none  [per_device(): lax.all_to_all(synthesized, 'wave', split_axis=1, concat_axis=2, tiled=True)]
    all_gather x1 -> x0, waiting for transfers between devices: 53.6 us -> none  [per_device(): full_forced = lax.all_gather(forced, 'pole', axis=0, tiled=True)]
    ppermute x0 -> x2, waiting for transfers between devices: none -> 44.1 us  [per_device(): other = lax.ppermute(forced, 'pole', [(0, 1), (1, 0)])]
    all_to_all x1 -> x4, starting transfers between devices: 6.53 us -> 26 us  [the longest x2 13.1 us: send(): lax.all_to_all(weighted, 'wave', split_axis=2, concat_axis=1, tiled=True)]
    psum x1, waiting for transfers between devices: 0.02 us -> 18.4 us  [per_device(): real_matrix, imag_matrix = lax.psum((real_matrix, imag_matrix), 'pole')]
    reshape x0 -> x3, local copies, waits for them, and re-layouts: none -> 13.6 us  [the longest x2 10.1 us: per_device(): synthesized.reshape(rows, -1, 1, members)]
    convert_element_type x1 -> x2, local copies, waits for them, and re-layouts: 10.6 us -> 4.37 us  [send(): (split[:, :, :, slot, :].astype(jnp.float32) * gauss_weights[None, :, Non...]
    all_to_all x1 -> x4, waiting for transfers between devices: 75 us -> 80.8 us  [the longest x2 70.8 us: per_device(): lax.all_to_all(synthesized.reshape(rows, -1, 1, members), 'wave', split_a...]
  transfers between devices with their start and end apart: 3 -> 7, of which waited for: 2 -> 7; matrix products, arithmetic and copies ran while one was open for 8% -> 21% of each run, Pallas kernels for 0% -> 0%
where the time goes in v1:
time: 257 us; the launch traced here: 255 us
  waiting for transfers between devices  143 us (56%)
  local copies, waits for them, and re-layouts  42.1 us (16%)
  starting transfers between devices  29.2 us (11%)
  matrix products  21.8 us (8%)
  between operations  13.9 us (5%)
  other arithmetic  4.39 us (2%)
    all_to_all x2, waiting for transfers between devices, per_device(): lax.all_to_all(synthesized.reshape(rows, -1, 1, members), 'wave', split_a...  70.8 us
    ppermute x2, waiting for transfers between devices, per_device(): other = lax.ppermute(forced, 'pole', [(0, 1), (1, 0)])  44.1 us
    psum x1, waiting for transfers between devices, per_device(): real_matrix, imag_matrix = lax.psum((real_matrix, imag_matrix), 'pole')  18.4 us
    all_to_all x2, starting transfers between devices, send(): lax.all_to_all(weighted, 'wave', split_axis=2, concat_axis=1, tiled=True)  13.1 us
    all_to_all x2, starting transfers between devices, per_device(): lax.all_to_all(synthesized.reshape(rows, -1, 1, members), 'wave', split_a...  12.9 us
    dot_general x2, matrix products, per_device(): jnp.einsum('rje,nj->ren', grid, legendre[slot], preferred_element_type=jn...  11.6 us
    reshape x2, local copies, waits for them, and re-layouts, per_device(): synthesized.reshape(rows, -1, 1, members)  10.1 us
    all_to_all x2, waiting for transfers between devices, send(): lax.all_to_all(weighted, 'wave', split_axis=2, concat_axis=1, tiled=True)  10 us
  transfers between devices with their start and end apart: 7, of which 7 were waited for; matrix products, arithmetic and copies ran while one was open for 21% of the time, Pallas kernels for 0%

profile of v1, /device:TPU:8, one launch (start us, length us, event | category | flops | bytes accessed | tf_op | source)
XLA Modules:
  0.0 254.7 jit_solution(16183377386257237340)
XLA Ops:
  6.5 0.0 copy-start
  6.5 3.7 %copy.36 = bf16[3,160,32,128]{3,1,2,0:T(8,128)(2,1)S(1)} copy(bf16[3,160,32,128]{3,2,1,0:T(8,128)(2,1)} %param.7) | data formatting | bytes 7864320 | tf_op args[0]
  10.2 0.0 copy-done.7
  10.2 2.1 fusion.19
  12.4 1.4 copy.38
  13.8 6.5 %all-to-all-start = ((bf16[3,160,16,128]{3,1,0,2:T(8,128)(2,1)}), bf16[3,160,16,128]{3,1,0,2:T(8,128)(2,1)}, u32[]{:S(2)}, u32[]{:S(2)}) async-start(bf16[3,160,16,128]{3,1,0,2:T(8,128)(2,1)} %copy.38), calls=%async_computation | async-start | bytes 3932160 | tf_op jit(solution)/shard_map/all_to_all | solution.py:29
  20.3 0.0 all-reduce.3.cloned.1.call-start
  20.4 3.5 %reshape.48 = bf16[32,46080]{1,0:T(8,128)(2,1)} reshape(bf16[32,18,2,1280]{3,2,1,0:T(2,128)(2,1)S(1)} %copy-done.4) | data formatting | bytes 5898240 | tf_op jit(solution)/shard_map/reshape | solution.py:34
  23.9 4.0 %dot_general.20 = bf16[2,3,3,2,1280,32]{4,3,2,1,0,5:T(2,128)(2,1)S(1)} reshape(bf16[46080,32]{0,1:T(8,128)(2,1)} %bitcast.174) | data formatting | bytes 5898240 | tf_op jit(solution)/shard_map/dot_general | solution.py:35
  27.9 1.3 fusion.38
  29.1 0.2 slice_subtract_fusion
  29.4 0.8 copy_bitcast_fusion
  30.1 0.0 all-reduce.3.cloned.1.call-update
  30.1 0.0 copy-start.6
  30.2 2.9 %copy.45 = bf16[3,160,16,128]{3,1,0,2:T(8,128)(2,1)} copy(bf16[3,160,16,128]{3,1,2,0:T(8,128)(2,1)} %get-tuple-element.8) | data formatting | bytes 3932160 | tf_op jit(solution)/shard_map/convert_element_type | solution.py:26
  33.1 0.7 fusion.77
  33.8 0.6 fusion.70
  34.4 0.7 fusion.71
  35.1 18.4 %all-reduce.3.cloned.1.call-done = (f32[3,3,2,1280]{3,2,1,0:T(2,128)}, f32[3,3,2,1280]{3,2,1,0:T(2,128)}) async-done(((f32[3,3,2,1280]{3,2,1,0:T(2,128)}, f32[3,3,2,1280]{3,2,1,0:T(2,128)}), (f32[3,3,2,1280]{3,2,1,0:T(2,128)}, f32[3,3,2,1280]{3,2,1,0:T(2,128)})) %all-reduce.3.cloned.1.call-update) | async-done | bytes 184336 | tf_op jit(solution)/shard_map/psum | solution.py:39
  53.5 1.0 fusion.74
  54.7 8.7 %all-to-all-done = bf16[3,160,16,128]{3,1,0,2:T(8,128)(2,1)} async-done(((bf16[3,160,16,128]{3,1,0,2:T(8,128)(2,1)}), bf16[3,160,16,128]{3,1,0,2:T(8,128)(2,1)}, u32[]{:S(2)}, u32[]{:S(2)}) %all-to-all-start) | async-done | bytes 1966112 | tf_op jit(solution)/shard_map/all_to_all | solution.py:29
  63.4 6.6 %all-to-all-start.2 = ((bf16[3,160,16,128]{3,1,0,2:T(8,128)(2,1)}), bf16[3,160,16,128]{3,1,0,2:T(8,128)(2,1)S(1)}, u32[]{:S(2)}, u32[]{:S(2)}) async-start(bf16[3,160,16,128]{3,1,0,2:T(8,128)(2,1)} %copy.45), calls=%async_computation.2 | async-start | bytes 3932160 | tf_op jit(solution)/shard_map/all_to_all | solution.py:29
  69.9 0.0 copy-done.5
  69.9 0.1 fusion.73
  70.1 0.0 copy-start.8
  70.1 1.8 copy.39
  71.9 0.3 copy-done.8
  72.2 5.8 %fusion.79 = (f32[3,128,1280]{2,1,0:T(8,128)S(1)}, bf16[3,128,1280]{2,1,0:T(8,128)(2,1)S(1)}) fusion(f32[1280]{0:T(1024)S(1)} %fusion.70, bf16[3,2560,128]{2,1,0:T(8,128)(2,1)S(1)} %bitcast.177, bf16[2,1280,2560]{2,1,0:T(8,128)(2,1)} %param.9, bf16[3,2,128,1280]{3,2,1,0:T(8,128)(2,1)S(1)} %copy-done.8), kind=kOutput, calls=%fused_computation.106 | convolution fusion | flops 2519040000 | bytes 12456960 | tf_op jit(solution)/shard_map/rje,nj->ren/dot_general | solution.py:45
  78.0 1.6 collective-permute-start
  79.7 0.0 slice-start.3
  79.7 0.1 slice_bitcast_fusion.13
  79.8 22.0 %collective-permute-done = bf16[3,128,1280]{2,1,0:T(8,128)(2,1)S(1)} collective-permute-done((bf16[3,128,1280]{2,1,0:T(8,128)(2,1)S(1)}, bf16[3,128,1280]{2,1,0:T(8,128)(2,1)S(1)}, u32[]{:S(2)}, u32[]{:S(2)}) %collective-permute-start) | collective-permute-done | bytes 983072 | tf_op jit(solution)/shard_map/ppermute | solution.py:50
  101.9 0.1 convert_element_type.93
  102.0 0.1 slice_bitcast_fusion.12
  102.2 4.4 %fusion.23 = bf16[3,2560,1,128]{1,3,0,2:T(8,128)(2,1)} fusion(bf16[2,1280,2560]{2,1,0:T(8,128)(2,1)S(1)} %bitcast.196, f32[128,1280]{1,0:T(8,128)S(1)} %get-tuple-element.13, f32[3,1280]{1,0:T(4,128)S(1)} %bitcast.183, f32[128,1280]{1,0:T(8,128)S(1)} %get-tuple-element.10, f32[3,1280]{1,0:T(4,128)S(1)} %bitcast.189, f32[128,1280]{1,0:T(8,128)S(1)} %get-tuple-element.14, ...), kind=kOutput, calls=%fused_computation.20 | convolution fusion | flops 2523463680 | bytes 12574720 | tf_op jit(solution)/shard_map/ren,nj->rje/dot_general | solution.py:58
  106.7 5.1 %copy.42 = bf16[3,2560,1,128]{3,0,2,1:T(4,128)(2,1)} copy(bf16[3,2560,1,128]{1,3,0,2:T(8,128)(2,1)} %fusion.23) | data formatting | bytes 3932160 | tf_op jit(solution)/shard_map/reshape | solution.py:63
  111.7 1.3 all-to-all-done.2
  113.0 1.3 copy-done.2
  114.3 6.4 %all-to-all-start.1 = ((bf16[3,2560,1,128]{3,0,2,1:T(4,128)(2,1)}), bf16[3,2560,1,128]{3,0,2,1:T(4,128)(2,1)S(1)}, u32[]{:S(2)}, u32[]{:S(2)}) async-start(bf16[3,2560,1,128]{3,0,2,1:T(4,128)(2,1)} %copy.42), calls=%async_computation.1 | async-start | bytes 5242880 | tf_op jit(solution)/shard_map/all_to_all | solution.py:62
  120.8 0.0 copy-start.9
  120.9 1.8 copy.46
  122.7 0.3 copy-done.9
  123.0 5.8 %fusion.78 = (f32[3,128,1280]{2,1,0:T(8,128)S(1)}, bf16[3,128,1280]{2,1,0:T(8,128)(2,1)S(1)}) fusion(f32[1280]{0:T(1024)S(1)} %fusion.71, bf16[3,2560,128]{2,1,0:T(8,128)(2,1)S(1)} %bitcast.178, bf16[2,1280,2560]{2,1,0:T(8,128)(2,1)} %param.9, bf16[3,2,128,1280]{3,2,1,0:T(8,128)(2,1)S(1)} %copy-done.9), kind=kOutput, calls=%fused_computation.105 | convolution fusion | flops 2519040000 | bytes 12456960 | tf_op jit(solution)/shard_map/rje,nj->ren/dot_general | solution.py:45
  128.8 1.6 collective-permute-start.1
  130.4 0.0 slice-start.7
  130.5 0.1 slice_bitcast_fusion.7
  130.6 22.0 %collective-permute-done.1 = bf16[3,128,1280]{2,1,0:T(8,128)(2,1)S(1)} collective-permute-done((bf16[3,128,1280]{2,1,0:T(8,128)(2,1)S(1)}, bf16[3,128,1280]{2,1,0:T(8,128)(2,1)S(1)}, u32[]{:S(2)}, u32[]{:S(2)}) %collective-permute-start.1) | collective-permute-done | bytes 983072 | tf_op jit(solution)/shard_map/ppermute | solution.py:50
  152.6 0.1 convert_element_type.105
  152.8 0.1 slice_bitcast_fusion.6
  153.0 0.0 slice-done.4
  153.0 0.0 slice-done.5
  153.0 0.0 slice-done.6
  153.0 0.0 slice-done.7
  153.0 4.5 %fusion.20 = bf16[3,2560,1,128]{1,3,0,2:T(8,128)(2,1)} fusion(bf16[2,1280,2560]{2,1,0:T(8,128)(2,1)S(1)} %bitcast.198, f32[128,1280]{1,0:T(8,128)S(1)} %get-tuple-element.19, f32[3,1280]{1,0:T(4,128)S(1)} %bitcast.186, f32[128,1280]{1,0:T(8,128)S(1)} %get-tuple-element.16, f32[3,1280]{1,0:T(4,128)S(1)} %bitcast.192, f32[128,1280]{1,0:T(8,128)S(1)} %get-tuple-element.20, ...), kind=kOutput, calls=%fused_computation.19 | convolution fusion | flops 2523463680 | bytes 12574720 | tf_op jit(solution)/shard_map/ren,nj->rje/dot_general | solution.py:58
  157.5 5.1 %copy.48 = bf16[3,2560,1,128]{3,0,2,1:T(4,128)(2,1)} copy(bf16[3,2560,1,128]{1,3,0,2:T(8,128)(2,1)} %fusion.20) | data formatting | bytes 3932160 | tf_op jit(solution)/shard_map/reshape | solution.py:63
  162.6 15.3 %all-to-all-done.1 = bf16[3,2560,1,128]{3,0,2,1:T(4,128)(2,1)S(1)} async-done(((bf16[3,2560,1,128]{3,0,2,1:T(4,128)(2,1)}), bf16[3,2560,1,128]{3,0,2,1:T(4,128)(2,1)S(1)}, u32[]{:S(2)}, u32[]{:S(2)}) %all-to-all-start.1) | async-done | bytes 1966112 | tf_op jit(solution)/shard_map/all_to_all | solution.py:62
  177.8 6.4 %all-to-all-start.3 = ((bf16[3,2560,1,128]{3,0,2,1:T(4,128)(2,1)}), bf16[3,2560,1,128]{3,0,2,1:T(4,128)(2,1)}, u32[]{:S(2)}, u32[]{:S(2)}) async-start(bf16[3,2560,1,128]{3,0,2,1:T(4,128)(2,1)} %copy.48), calls=%async_computation.3 | async-start | bytes 5242880 | tf_op jit(solution)/shard_map/all_to_all | solution.py:62
  184.3 1.6 copy.43
  185.9 55.5 %all-to-all-done.3 = bf16[3,2560,1,128]{3,0,2,1:T(4,128)(2,1)} async-done(((bf16[3,2560,1,128]{3,0,2,1:T(4,128)(2,1)}), bf16[3,2560,1,128]{3,0,2,1:T(4,128)(2,1)}, u32[]{:S(2)}, u32[]{:S(2)}) %all-to-all-start.3) | async-done | bytes 1966112 | tf_op jit(solution)/shard_map/all_to_all | solution.py:62
  241.4 2.0 copy.49
  243.4 0.4 pad_maximum_fusion
  243.8 0.5 copy.50
  244.4 0.0 copy-start.1
  244.4 3.4 %copy.51 = bf16[3,160,32,128]{3,2,1,0:T(8,128)(2,1)} copy(bf16[3,160,32,128]{3,1,2,0:T(8,128)(2,1)S(1)} %bitcast.173) | data formatting | bytes 7864320 | tf_op jit(solution)/shard_map/reshape | solution.py:66
  (42 shorter events, 0.3 us)
Async XLA Ops:
  6.5 21.3 %copy-start = (f32[32,2]{0,1:T(2,128)S(1)}, f32[32,2]{0,1:T(2,128)}, u32[]{:S(2)}) copy-start(f32[32,2]{0,1:T(2,128)} %param.12) | copy-start | bytes 772
  6.5 3.7 %copy-start.7 = (f32[160]{0:T(256)S(1)}, f32[160]{0:T(256)}, u32[]{:S(2)}) copy-start(f32[160]{0:T(256)} %param.10) | copy-start | bytes 1924
  13.8 6.6 %copy-start.4 = (bf16[32,18,2,1280]{3,2,1,0:T(2,128)(2,1)S(1)}, bf16[32,18,2,1280]{3,2,1,0:T(2,128)(2,1)}, u32[]{:S(2)}) copy-start(bf16[32,18,2,1280]{3,2,1,0:T(2,128)(2,1)} %param.11) | copy-start | bytes 8847364
  13.8 49.6 %all-to-all-start = ((bf16[3,160,16,128]{3,1,0,2:T(8,128)(2,1)}), bf16[3,160,16,128]{3,1,0,2:T(8,128)(2,1)}, u32[]{:S(2)}, u32[]{:S(2)}) async-start(bf16[3,160,16,128]{3,1,0,2:T(8,128)(2,1)} %copy.38), calls=%async_computation | async-start | bytes 3932160 | tf_op jit(solution)/shard_map/all_to_all | solution.py:29
  20.3 33.2 %all-reduce.3.cloned.1.call-start = ((), (), s32[]{:S(2)}) async-start(), calls=%async_computation.4 | async-start | bytes 368640 | tf_op jit(solution)/shard_map/psum | solution.py:39
  30.1 3.0 %copy-start.6 = (s32[2]{0:T(128)S(1)}, s32[2]{0:T(128)}, u32[]{:S(2)}) copy-start(s32[2]{0:T(128)} %param.13) | copy-start | bytes 28
  54.7 15.3 %copy-start.5 = (f32[3,3,2,1280]{3,2,1,0:T(2,128)S(1)}, f32[3,3,2,1280]{3,2,1,0:T(2,128)}, u32[]{:S(2)}) copy-start(f32[3,3,2,1280]{3,2,1,0:T(2,128)} %get-tuple-element.6) | copy-start | bytes 276484
  63.4 49.6 %all-to-all-start.2 = ((bf16[3,160,16,128]{3,1,0,2:T(8,128)(2,1)}), bf16[3,160,16,128]{3,1,0,2:T(8,128)(2,1)S(1)}, u32[]{:S(2)}, u32[]{:S(2)}) async-start(bf16[3,160,16,128]{3,1,0,2:T(8,128)(2,1)} %copy.45), calls=%async_computation.2 | async-start | bytes 3932160 | tf_op jit(solution)/shard_map/all_to_all | solution.py:29
  70.1 2.1 copy-start.8
  72.2 30.0 %slice-start = ((s8[13107200]{0:T(1024)(128)(4,1)}), s8[4194304]{0:T(1024)(128)(4,1)S(1)}, s32[]{:S(2)}) async-start(s8[13107200]{0:T(1024)(128)(4,1)} %bitcast.195), calls=%async_computation.5 | async-start | bytes 8388608
  72.2 30.0 %slice-start.1 = ((s8[13107200]{0:T(1024)(128)(4,1)}), s8[4194304]{0:T(1024)(128)(4,1)S(1)}, s32[]{:S(2)}) async-start(s8[13107200]{0:T(1024)(128)(4,1)} %bitcast.195), calls=%async_computation.6 | async-start | bytes 8388608
  72.2 30.0 %slice-start.2 = ((s8[13107200]{0:T(1024)(128)(4,1)}), s8[4194304]{0:T(1024)(128)(4,1)S(1)}, s32[]{:S(2)}) async-start(s8[13107200]{0:T(1024)(128)(4,1)} %bitcast.195), calls=%async_computation.7 | async-start | bytes 8388608
  78.0 23.9 %collective-permute-start = (bf16[3,128,1280]{2,1,0:T(8,128)(2,1)S(1)}, bf16[3,128,1280]{2,1,0:T(8,128)(2,1)S(1)}, u32[]{:S(2)}, u32[]{:S(2)}) collective-permute-start(bf16[3,128,1280]{2,1,0:T(8,128)(2,1)S(1)} %get-tuple-element.44), channel_id=1, source_target_pairs={{0,16},{16,0},{1,17},{17,1},{2,18},{18,2},{3,19},{19,3},{4,20},{20... | collective-permute-start | bytes 2949128 | tf_op jit(solution)/shard_map/ppermute | solution.py:50
  79.7 22.5 %slice-start.3 = ((s8[13107200]{0:T(1024)(128)(4,1)}), s8[524288]{0:T(1024)(128)(4,1)S(1)}, s32[]{:S(2)}) async-start(s8[13107200]{0:T(1024)(128)(4,1)} %bitcast.195), calls=%async_computation.8 | async-start | bytes 1048576
  113.0 1.3 copy-start.2
  114.3 63.6 %all-to-all-start.1 = ((bf16[3,2560,1,128]{3,0,2,1:T(4,128)(2,1)}), bf16[3,2560,1,128]{3,0,2,1:T(4,128)(2,1)S(1)}, u32[]{:S(2)}, u32[]{:S(2)}) async-start(bf16[3,2560,1,128]{3,0,2,1:T(4,128)(2,1)} %copy.42), calls=%async_computation.1 | async-start | bytes 5242880 | tf_op jit(solution)/shard_map/all_to_all | solution.py:62
  120.8 2.1 copy-start.9
  123.0 30.0 %slice-start.4 = ((s8[13107200]{0:T(1024)(128)(4,1)}), s8[4194304]{0:T(1024)(128)(4,1)S(1)}, s32[]{:S(2)}) async-start(s8[13107200]{0:T(1024)(128)(4,1)} %bitcast.197), calls=%async_computation.9 | async-start | bytes 8388608
  123.0 30.0 %slice-start.5 = ((s8[13107200]{0:T(1024)(128)(4,1)}), s8[4194304]{0:T(1024)(128)(4,1)S(1)}, s32[]{:S(2)}) async-start(s8[13107200]{0:T(1024)(128)(4,1)} %bitcast.197), calls=%async_computation.10 | async-start | bytes 8388608
  123.0 30.0 %slice-start.6 = ((s8[13107200]{0:T(1024)(128)(4,1)}), s8[4194304]{0:T(1024)(128)(4,1)S(1)}, s32[]{:S(2)}) async-start(s8[13107200]{0:T(1024)(128)(4,1)} %bitcast.197), calls=%async_computation.11 | async-start | bytes 8388608
  128.8 23.9 %collective-permute-start.1 = (bf16[3,128,1280]{2,1,0:T(8,128)(2,1)S(1)}, bf16[3,128,1280]{2,1,0:T(8,128)(2,1)S(1)}, u32[]{:S(2)}, u32[]{:S(2)}) collective-permute-start(bf16[3,128,1280]{2,1,0:T(8,128)(2,1)S(1)} %get-tuple-element.42), channel_id=1, source_target_pairs={{0,16},{16,0},{1,17},{17,1},{2,18},{18,2},{3,19},{19,3},{4,20},{20... | collective-permute-start | bytes 2949128 | tf_op jit(solution)/shard_map/ppermute | solution.py:50
  130.4 22.5 %slice-start.7 = ((s8[13107200]{0:T(1024)(128)(4,1)}), s8[524288]{0:T(1024)(128)(4,1)S(1)}, s32[]{:S(2)}) async-start(s8[13107200]{0:T(1024)(128)(4,1)} %bitcast.197), calls=%async_computation.12 | async-start | bytes 1048576
  177.8 63.6 %all-to-all-start.3 = ((bf16[3,2560,1,128]{3,0,2,1:T(4,128)(2,1)}), bf16[3,2560,1,128]{3,0,2,1:T(4,128)(2,1)}, u32[]{:S(2)}, u32[]{:S(2)}) async-start(bf16[3,2560,1,128]{3,0,2,1:T(4,128)(2,1)} %copy.48), calls=%async_computation.3 | async-start | bytes 5242880 | tf_op jit(solution)/shard_map/all_to_all | solution.py:62
  185.9 57.5 %copy-start.3 = (bf16[3,2560,1,128]{3,1,0,2:T(8,128)(2,1)S(1)}, bf16[3,2560,1,128]{3,1,0,2:T(8,128)(2,1)}, u32[]{:S(2)}) copy-start(bf16[3,2560,1,128]{3,1,0,2:T(8,128)(2,1)} %copy.43) | copy-start | bytes 5898244
  244.4 3.5 %copy-start.1 = (f32[32,2]{0,1:T(2,128)S(1)}, f32[32,2]{0,1:T(2,128)}, u32[]{:S(2)}) copy-start(f32[32,2]{0,1:T(2,128)} %param.12) | copy-start | bytes 772
Sparse Core Ops, SparseCore 0:
  30.3 23.2 all-reduce.2

commit v2 on v1

v2 whole, which is shorter than its diff:
```python
import jax
import jax.numpy as jnp
from jax import lax
from jax.sharding import PartitionSpec as P


def mix_rows(real_matrix, imag_matrix, leading, trailing, orientation):
    summed = 0.0
    for column in range(3):
        summed = summed + real_matrix[:, column, None, :] * leading[column][None]
        summed = summed + (orientation * imag_matrix[:, column, None, :]) * trailing[column][None]
    return summed


def exchange_blocks(blocks, me, owners):
    pieces = [lax.dynamic_index_in_dim(blocks, me, 0, keepdims=False)]
    order = sorted(range(1, owners), key=lambda k: -k)
    got = {0: pieces[0]}
    for k in order:
        sent = lax.dynamic_index_in_dim(blocks, me ^ k, 0, keepdims=False)
        got[k] = lax.ppermute(sent, "wave", [(d, d ^ k) for d in range(owners)])
    stacked = jnp.stack([got[k] for k in range(owners)])
    return jnp.take(stacked, me ^ jnp.arange(owners), axis=0, unique_indices=True, mode="clip")


def per_device(
    tendency, spectral_state, legendre, gauss_weights, block_inverses, pole_coeffs, wavenumbers
):
    rows, lats, slots, members = tendency.shape
    local_slots, nspec, nlat = legendre.shape
    owners = slots // local_slots
    pole_index = lax.axis_index("pole")
    me = lax.axis_index("wave")
    orientation = (2 * pole_index - 1).astype(jnp.float32)
    weighted = (tendency.astype(jnp.float32) * gauss_weights[None, :, None, None]).astype(jnp.bfloat16)
    weighted = jnp.transpose(weighted, (2, 0, 1, 3)).reshape(owners, local_slots, rows, lats, members)

    def swap(blocks, slot):
        if slot == 0:
            return lax.all_to_all(blocks, "wave", split_axis=0, concat_axis=0, tiled=True)
        return exchange_blocks(blocks, me, owners)

    received = [swap(weighted[:, slot], slot) for slot in range(local_slots)]

    local_pairs = block_inverses.shape[0]
    flat_inverse = block_inverses.reshape(local_pairs, -1).astype(jnp.float32)
    weighted_sums = jnp.dot(pole_coeffs.T, flat_inverse, precision=lax.Precision.HIGHEST)
    weighted_sums = weighted_sums.reshape(2, 2, 3, 3, local_slots, nspec)
    real_matrix = weighted_sums[0, 0] - weighted_sums[1, 1]
    imag_matrix = weighted_sums[0, 1] + weighted_sums[1, 0]
    real_matrix, imag_matrix = lax.psum((real_matrix, imag_matrix), "pole")

    outputs = []
    for slot in range(local_slots):
        low = nspec // 2 if slot % 2 else 0
        degree = jnp.arange(low, nspec, dtype=jnp.int32)
        table = legendre[slot, low:]
        grid = jnp.transpose(received[slot], (1, 0, 2, 3)).reshape(rows, nlat, members)
        spectral_tend = jnp.einsum("rje,nj->ren", grid, table, preferred_element_type=jnp.float32)
        live = (degree >= wavenumbers[slot]).astype(jnp.float32)
        forced = ((spectral_state[:, slot, :, low:].astype(jnp.float32) + spectral_tend) * live).astype(jnp.bfloat16)
        other = lax.ppermute(forced, "pole", [(0, 1), (1, 0)])
        advanced = mix_rows(
            real_matrix[:, :, slot, low:],
            imag_matrix[:, :, slot, low:],
            forced.astype(jnp.float32),
            other.astype(jnp.float32),
            orientation,
        ).astype(jnp.bfloat16)
        synthesized = jnp.einsum("ren,nj->rje", advanced, table, preferred_element_type=jnp.float32)
        blocks = synthesized.astype(jnp.bfloat16).reshape(rows, owners, lats, members)
        outputs.append(swap(jnp.transpose(blocks, (1, 0, 2, 3)), slot))
    out = jnp.stack(outputs, axis=1).reshape(slots, rows, lats, members)
    return jnp.transpose(out, (1, 2, 0, 3))


def solution(mesh):
    in_specs = (
        P("pole", "wave", None, None),
        P("pole", "wave", None, None),
        P("wave", None, None),
        P("wave"),
        P("pole", None, "wave", None),
        P("pole", None),
        P("wave"),
    )
    out_specs = P("pole", "wave", None, None)
    return jax.shard_map(
        per_device, mesh=mesh, in_specs=in_specs, out_specs=out_specs, check_vma=False
    )
```

time: 257 us -> 320 us (1.25)
  starting transfers between devices: 29.2 us -> 72.4 us
  local copies, waits for them, and re-layouts: 42.1 us -> 65.2 us
  waiting for transfers between devices: 143 us -> 132 us
    ppermute x0 -> x30, waiting for transfers between devices: none -> 110 us  [exchange_blocks(): got[k] = lax.ppermute(sent, 'wave', [(d, d ^ k) for d in range(owners)])]
    all_to_all x4 -> x2, waiting for transfers between devices: 80.8 us -> 0.01 us  [swap(): lax.all_to_all(blocks, 'wave', split_axis=0, concat_axis=0, tiled=True)]
    ppermute x0 -> x30, starting transfers between devices: none -> 55.6 us  [exchange_blocks(): got[k] = lax.ppermute(sent, 'wave', [(d, d ^ k) for d in range(owners)])]
    ppermute x2, waiting for transfers between devices: 44.1 us -> 21.3 us  [per_device(): other = lax.ppermute(forced, 'pole', [(0, 1), (1, 0)])]
    psum x1, waiting for transfers between devices: 18.4 us -> 0.02 us  [per_device(): real_matrix, imag_matrix = lax.psum((real_matrix, imag_matrix), 'pole')]
    unnamed x54 -> x71, local copies, waits for them, and re-layouts: 6.5 us -> 24.5 us
    all_to_all x4 -> x2, starting transfers between devices: 26 us -> 13.7 us  [swap(): lax.all_to_all(blocks, 'wave', split_axis=0, concat_axis=0, tiled=True)]
    reshape x3 -> x1, local copies, waits for them, and re-layouts: 13.6 us -> 2.97 us  [per_device(): synthesized.astype(jnp.bfloat16).reshape(rows, owners, lats, members)]
  transfers between devices with their start and end apart: 7 -> 35, of which waited for: 7 -> 22; matrix products, arithmetic and copies ran while one was open for 21% -> 20% of each run, Pallas kernels for 0% -> 0%
where the time goes in v2:
time: 320 us; the launch traced here: 315 us
  waiting for transfers between devices  132 us (41%)
  starting transfers between devices  72.4 us (23%)
  local copies, waits for them, and re-layouts  65.2 us (20%)
  matrix products  24.6 us (8%)
  between operations  14 us (4%)
  other arithmetic  7.38 us (2%)
    ppermute x30, waiting for transfers between devices, exchange_blocks(): got[k] = lax.ppermute(sent, 'wave', [(d, d ^ k) for d in range(owners)])  110 us
    ppermute x30, starting transfers between devices, exchange_blocks(): got[k] = lax.ppermute(sent, 'wave', [(d, d ^ k) for d in range(owners)])  55.6 us
    unnamed x71, local copies, waits for them, and re-layouts  24.5 us
    ppermute x2, waiting for transfers between devices, per_device(): other = lax.ppermute(forced, 'pole', [(0, 1), (1, 0)])  21.3 us
    all_to_all x2, starting transfers between devices, swap(): lax.all_to_all(blocks, 'wave', split_axis=0, concat_axis=0, tiled=True)  13.7 us
    dot_general x2, matrix products, per_device(): jnp.einsum('ren,nj->rje', advanced, table, preferred_element_type=jnp.flo...  12.4 us
    dot_general x2, matrix products, per_device(): jnp.einsum('rje,nj->ren', grid, table, preferred_element_type=jnp.float32)  11 us
    convert_element_type x2, local copies, waits for them, and re-layouts, per_device(): synthesized.astype(jnp.bfloat16).reshape(rows, owners, lats, members)  7.01 us
  transfers between devices with their start and end apart: 35, of which 22 were waited for; matrix products, arithmetic and copies ran while one was open for 20% of the time, Pallas kernels for 0%

profile of v2, /device:TPU:8, one launch (start us, length us, event | category | flops | bytes accessed | tf_op | source)
XLA Modules:
  0.0 315.3 jit_solution(14787181529598612708)
XLA Ops:
  6.5 3.7 %multiply_convert_fusion = bf16[3,160,32,128]{3,1,0,2:T(8,128)(2,1)S(1)} fusion(bf16[3,160,32,128]{3,2,1,0:T(8,128)(2,1)} %param.7, f32[160]{0:T(256)} %param.10), kind=kLoop, calls=%fused_computation.2 | loop fusion | flops 5898240 | bytes 7864960 | tf_op jit(solution)/shard_map/convert_element_type | solution.py:35
  10.2 1.6 slice_bitcast_fusion
  11.8 6.3 %all-to-all-start = ((bf16[16,3,160,128]{3,2,1,0:T(8,128)(2,1)}), bf16[16,3,160,128]{3,2,1,0:T(8,128)(2,1)}, u32[]{:S(2)}, u32[]{:S(2)}) async-start(bf16[16,3,160,128]{3,2,1,0:T(8,128)(2,1)} %get-tuple-element.7), calls=%async_computation | async-start | bytes 3932160 | tf_op jit(solution)/shard_map/all_to_all | solution.py:40
  18.2 1.4 dynamic-slice_bitcast_fusion.15
  19.6 2.1 collective-permute-start.15
  24.1 5.2 %reshape.110 = bf16[32,46080]{1,0:T(8,128)(2,1)} reshape(bf16[32,18,2,1280]{3,2,1,0:T(2,128)(2,1)} %param.11) | data formatting | bytes 5898240 | tf_op jit(solution)/shard_map/reshape | solution.py:46
  29.3 4.0 %dot_general.20 = bf16[2,3,3,2,1280,32]{4,3,2,1,0,5:T(2,128)(2,1)S(1)} reshape(bf16[46080,32]{0,1:T(8,128)(2,1)} %bitcast.281) | data formatting | bytes 5898240 | tf_op jit(solution)/shard_map/dot_general | solution.py:47
  37.7 1.6 bitcast_dynamic-update-slice_fusion.31
  39.3 1.5 collective-permute-start.2
  40.7 1.6 bitcast_dynamic-update-slice_fusion.30
  42.3 4.7 %collective-permute-done.2 = bf16[3,160,128]{2,1,0:T(8,128)(2,1)S(1)} collective-permute-done((bf16[3,160,128]{2,1,0:T(8,128)(2,1)}, bf16[3,160,128]{2,1,0:T(8,128)(2,1)S(1)}, u32[]{:S(2)}, u32[]{:S(2)}) %collective-permute-start.2) | collective-permute-done | bytes 122912 | tf_op jit(solution)/shard_map/ppermute | solution.py:21
  47.6 7.4 %collective-permute-done.3 = bf16[3,160,128]{2,1,0:T(8,128)(2,1)S(1)} collective-permute-done((bf16[3,160,128]{2,1,0:T(8,128)(2,1)}, bf16[3,160,128]{2,1,0:T(8,128)(2,1)S(1)}, u32[]{:S(2)}, u32[]{:S(2)}) %collective-permute-start.3) | collective-permute-done | bytes 122912 | tf_op jit(solution)/shard_map/ppermute | solution.py:21
  55.0 8.8 %collective-permute-start.4 = (bf16[3,160,128]{2,1,0:T(8,128)(2,1)}, bf16[3,160,128]{2,1,0:T(8,128)(2,1)S(1)}, u32[]{:S(2)}, u32[]{:S(2)}) collective-permute-start(bf16[3,160,128]{2,1,0:T(8,128)(2,1)} %get-tuple-element.41), channel_id=1, source_target_pairs={{0,4},{1,5},{2,6},{3,7},{4,0},{5,1},{6,2},{7,3},{8,12},{9,13},{10,... | collective-permute-start | bytes 368648 | tf_op jit(solution)/shard_map/ppermute | solution.py:21
  64.5 5.5 %collective-permute-done.4 = bf16[3,160,128]{2,1,0:T(8,128)(2,1)S(1)} collective-permute-done((bf16[3,160,128]{2,1,0:T(8,128)(2,1)}, bf16[3,160,128]{2,1,0:T(8,128)(2,1)S(1)}, u32[]{:S(2)}, u32[]{:S(2)}) %collective-permute-start.4) | collective-permute-done | bytes 122912 | tf_op jit(solution)/shard_map/ppermute | solution.py:21
  70.0 2.0 collective-permute-start.5
  72.7 2.8 collective-permute-done.5
  75.5 3.2 %collective-permute-start.6 = (bf16[3,160,128]{2,1,0:T(8,128)(2,1)S(1)}, bf16[3,160,128]{2,1,0:T(8,128)(2,1)S(1)}, u32[]{:S(2)}, u32[]{:S(2)}) collective-permute-start(bf16[3,160,128]{2,1,0:T(8,128)(2,1)S(1)} %copy-done.8), channel_id=1, source_target_pairs={{0,6},{1,7},{2,4},{3,5},{4,2},{5,3},{6,0},{7,1},{8,14},{9,15},{10,... | collective-permute-start | bytes 368648 | tf_op jit(solution)/shard_map/ppermute | solution.py:21
  79.4 3.2 %collective-permute-done.6 = bf16[3,160,128]{2,1,0:T(8,128)(2,1)S(1)} collective-permute-done((bf16[3,160,128]{2,1,0:T(8,128)(2,1)S(1)}, bf16[3,160,128]{2,1,0:T(8,128)(2,1)S(1)}, u32[]{:S(2)}, u32[]{:S(2)}) %collective-permute-start.6) | collective-permute-done | bytes 122912 | tf_op jit(solution)/shard_map/ppermute | solution.py:21
  84.5 4.6 %collective-permute-done.7 = bf16[3,160,128]{2,1,0:T(8,128)(2,1)S(1)} collective-permute-done((bf16[3,160,128]{2,1,0:T(8,128)(2,1)S(1)}, bf16[3,160,128]{2,1,0:T(8,128)(2,1)S(1)}, u32[]{:S(2)}, u32[]{:S(2)}) %collective-permute-start.7) | collective-permute-done | bytes 122912 | tf_op jit(solution)/shard_map/ppermute | solution.py:21
  90.5 5.0 %collective-permute-done.8 = bf16[3,160,128]{2,1,0:T(8,128)(2,1)S(1)} collective-permute-done((bf16[3,160,128]{2,1,0:T(8,128)(2,1)S(1)}, bf16[3,160,128]{2,1,0:T(8,128)(2,1)S(1)}, u32[]{:S(2)}, u32[]{:S(2)}) %collective-permute-start.8) | collective-permute-done | bytes 122912 | tf_op jit(solution)/shard_map/ppermute | solution.py:21
  95.5 2.3 collective-permute-start.9
  98.4 4.8 %collective-permute-done.9 = bf16[3,160,128]{2,1,0:T(8,128)(2,1)S(1)} collective-permute-done((bf16[3,160,128]{2,1,0:T(8,128)(2,1)S(1)}, bf16[3,160,128]{2,1,0:T(8,128)(2,1)S(1)}, u32[]{:S(2)}, u32[]{:S(2)}) %collective-permute-start.9) | collective-permute-done | bytes 122912 | tf_op jit(solution)/shard_map/ppermute | solution.py:21
  103.2 2.6 collective-permute-start.10
  106.4 4.0 %collective-permute-done.10 = bf16[3,160,128]{2,1,0:T(8,128)(2,1)S(1)} collective-permute-done((bf16[3,160,128]{2,1,0:T(8,128)(2,1)S(1)}, bf16[3,160,128]{2,1,0:T(8,128)(2,1)S(1)}, u32[]{:S(2)}, u32[]{:S(2)}) %collective-permute-start.10) | collective-permute-done | bytes 122912 | tf_op jit(solution)/shard_map/ppermute | solution.py:21
  111.1 6.3 %collective-permute-done.11 = bf16[3,160,128]{2,1,0:T(8,128)(2,1)S(1)} collective-permute-done((bf16[3,160,128]{2,1,0:T(8,128)(2,1)S(1)}, bf16[3,160,128]{2,1,0:T(8,128)(2,1)S(1)}, u32[]{:S(2)}, u32[]{:S(2)}) %collective-permute-start.11) | collective-permute-done | bytes 122912 | tf_op jit(solution)/shard_map/ppermute | solution.py:21
  118.0 1.6 bitcast_dynamic-update-slice_fusion.19
  119.5 1.6 bitcast_dynamic-update-slice_fusion.18
  122.4 2.5 gather_fusion
  125.0 3.8 %fusion.68 = (f32[3,128,640]{2,1,0:T(8,128)S(1)}, bf16[3,128,640]{2,1,0:T(8,128)(2,1)S(1)}) fusion(f32[640]{0:T(1024)S(1)} %fusion.63, bf16[3,2560,128]{2,1,0:T(8,128)(2,1)S(1)} %bitcast.288, bf16[2,1280,2560]{2,1,0:T(8,128)(2,1)} %param.9, bf16[3,2,128,1280]{3,2,1,0:T(8,128)(2,1)} %param.8), kind=kOutput, calls=%fused_computation.165 | convolution fusion | flops 1259520000 | bytes 7211520 | tf_op jit(solution)/shard_map/rje,nj->ren/dot_general | solution.py:59
  128.8 1.6 collective-permute-start.16
  134.4 8.6 %collective-permute-done.16 = bf16[3,128,640]{2,1,0:T(8,128)(2,1)S(1)} collective-permute-done((bf16[3,128,640]{2,1,0:T(8,128)(2,1)S(1)}, bf16[3,128,640]{2,1,0:T(8,128)(2,1)S(1)}, u32[]{:S(2)}, u32[]{:S(2)}) %collective-permute-start.16) | collective-permute-done | bytes 491552 | tf_op jit(solution)/shard_map/ppermute | solution.py:62
  143.1 1.8 copy.24
  145.2 7.2 %fusion.69 = (f32[3,128,1280]{2,1,0:T(8,128)}, bf16[3,128,1280]{2,1,0:T(8,128)(2,1)}) fusion(f32[1280]{0:T(1024)S(1)} %fusion.62, bf16[3,2560,128]{2,1,0:T(8,128)(2,1)S(1)} %bitcast.289, bf16[2,1280,2560]{2,1,0:T(8,128)(2,1)} %param.9, bf16[3,2,128,1280]{3,2,1,0:T(8,128)(2,1)S(1)} %copy-done.11), kind=kOutput, calls=%fused_computation.166 | convolution fusion | flops 2519040000 | bytes 12456960 | tf_op jit(solution)/shard_map/rje,nj->ren/dot_general | solution.py:59
  152.4 1.5 collective-permute-start
  154.0 5.1 %fusion.9 = bf16[3,2560,128]{1,2,0:T(8,128)(2,1)} fusion(bf16[2,1280,2560]{2,1,0:T(8,128)(2,1)} %param.9, f32[128,640]{1,0:T(8,128)S(1)} %get-tuple-element.49, f32[3,640]{1,0:T(4,128)S(1)} %bitcast.301, f32[128,640]{1,0:T(8,128)S(1)} %get-tuple-element.46, f32[3,640]{1,0:T(4,128)S(1)} %bitcast.304, f32[128,640]{1,0:T(8,128)S(1)} %get-tuple-element.50, ...), kind=kOutput, calls=%fused_computation.12 | convolution fusion | flops 1262223360 | bytes 7255040 | tf_op jit(solution)/shard_map/ren,nj->rje/dot_general | solution.py:70
  159.0 3.1 copy.31
  162.1 1.6 slice_bitcast_fusion.6
  163.7 12.7 %collective-permute-done = bf16[3,128,1280]{2,1,0:T(8,128)(2,1)S(1)} collective-permute-done((bf16[3,128,1280]{2,1,0:T(8,128)(2,1)}, bf16[3,128,1280]{2,1,0:T(8,128)(2,1)S(1)}, u32[]{:S(2)}, u32[]{:S(2)}) %collective-permute-start) | collective-permute-done | bytes 983072 | tf_op jit(solution)/shard_map/ppermute | solution.py:62
  176.7 7.3 %fusion.10 = bf16[3,2560,128]{1,2,0:T(8,128)(2,1)} fusion(bf16[2,1280,2560]{2,1,0:T(8,128)(2,1)} %param.9, f32[128,1280]{1,0:T(8,128)S(1)} %get-tuple-element.13, f32[3,1280]{1,0:T(4,128)S(1)} %bitcast.295, f32[128,1280]{1,0:T(8,128)S(1)} %get-tuple-element.10, f32[3,1280]{1,0:T(4,128)S(1)} %bitcast.298, f32[128,1280]{1,0:T(8,128)S(1)} %get-tuple-element.14, ...), kind=kOutput, calls=%fused_computation.13 | convolution fusion | flops 2523463680 | bytes 12544000 | tf_op jit(solution)/shard_map/ren,nj->rje/dot_general | solution.py:70
  184.1 4.0 %copy.26 = bf16[3,2560,128]{2,1,0:T(8,128)(2,1)} copy(bf16[3,2560,128]{1,2,0:T(8,128)(2,1)} %fusion.10) | data formatting | bytes 3932160 | tf_op jit(solution)/shard_map/convert_element_type | solution.py:71
  188.0 3.0 copy.79
  191.0 7.4 %all-to-all-start.1 = ((bf16[16,3,160,128]{3,2,1,0:T(8,128)(2,1)}), bf16[16,3,160,128]{3,2,1,0:T(8,128)(2,1)}, u32[]{:S(2)}, u32[]{:S(2)}) async-start(bf16[16,3,160,128]{3,2,1,0:T(8,128)(2,1)} %bitcast.284), calls=%async_computation.1 | async-start | bytes 3932160 | tf_op jit(solution)/shard_map/all_to_all | solution.py:40
  198.9 2.3 collective-permute-start.31
  204.0 1.5 collective-permute-start.18
  206.1 6.2 %collective-permute-done.18 = bf16[3,160,128]{2,1,0:T(8,128)(2,1)S(1)} collective-permute-done((bf16[3,160,128]{2,1,0:T(8,128)(2,1)S(1)}, bf16[3,160,128]{2,1,0:T(8,128)(2,1)S(1)}, u32[]{:S(2)}, u32[]{:S(2)}) %collective-permute-start.18) | collective-permute-done | bytes 122912 | tf_op jit(solution)/shard_map/ppermute | solution.py:21
  212.3 1.6 collective-permute-start.19
  214.6 6.0 %collective-permute-done.19 = bf16[3,160,128]{2,1,0:T(8,128)(2,1)S(1)} collective-permute-done((bf16[3,160,128]{2,1,0:T(8,128)(2,1)S(1)}, bf16[3,160,128]{2,1,0:T(8,128)(2,1)S(1)}, u32[]{:S(2)}, u32[]{:S(2)}) %collective-permute-start.19) | collective-permute-done | bytes 122912 | tf_op jit(solution)/shard_map/ppermute | solution.py:21
  220.5 2.8 collective-permute-start.20
  224.0 21.0 %collective-permute-done.20 = bf16[3,160,128]{2,1,0:T(8,128)(2,1)S(1)} collective-permute-done((bf16[3,160,128]{2,1,0:T(8,128)(2,1)S(1)}, bf16[3,160,128]{2,1,0:T(8,128)(2,1)S(1)}, u32[]{:S(2)}, u32[]{:S(2)}) %collective-permute-start.20) | collective-permute-done | bytes 122912 | tf_op jit(solution)/shard_map/ppermute | solution.py:21
  245.7 4.9 %collective-permute-done.21 = bf16[3,160,128]{2,1,0:T(8,128)(2,1)S(1)} collective-permute-done((bf16[3,160,128]{2,1,0:T(8,128)(2,1)S(1)}, bf16[3,160,128]{2,1,0:T(8,128)(2,1)S(1)}, u32[]{:S(2)}, u32[]{:S(2)}) %collective-permute-start.21) | collective-permute-done | bytes 122912 | tf_op jit(solution)/shard_map/ppermute | solution.py:21
  250.5 3.0 collective-permute-start.22
  254.2 5.2 %collective-permute-done.22 = bf16[3,160,128]{2,1,0:T(8,128)(2,1)S(1)} collective-permute-done((bf16[3,160,128]{2,1,0:T(8,128)(2,1)S(1)}, bf16[3,160,128]{2,1,0:T(8,128)(2,1)S(1)}, u32[]{:S(2)}, u32[]{:S(2)}) %collective-permute-start.22) | collective-permute-done | bytes 122912 | tf_op jit(solution)/shard_map/ppermute | solution.py:21
  260.1 5.1 %collective-permute-done.23 = bf16[3,160,128]{2,1,0:T(8,128)(2,1)S(1)} collective-permute-done((bf16[3,160,128]{2,1,0:T(8,128)(2,1)S(1)}, bf16[3,160,128]{2,1,0:T(8,128)(2,1)S(1)}, u32[]{:S(2)}, u32[]{:S(2)}) %collective-permute-start.23) | collective-permute-done | bytes 122912 | tf_op jit(solution)/shard_map/ppermute | solution.py:21
  265.2 4.5 %collective-permute-start.24 = (bf16[3,160,128]{2,1,0:T(8,128)(2,1)S(1)}, bf16[3,160,128]{2,1,0:T(8,128)(2,1)S(1)}, u32[]{:S(2)}, u32[]{:S(2)}) collective-permute-start(bf16[3,160,128]{2,1,0:T(8,128)(2,1)S(1)} %get-tuple-element.22), channel_id=1, source_target_pairs={{0,8},{1,9},{2,10},{3,11},{4,12},{5,13},{6,14},{7,15},{8,0},{9,1},... | collective-permute-start | bytes 368648 | tf_op jit(solution)/shard_map/ppermute | solution.py:21
  270.3 3.3 %collective-permute-done.24 = bf16[3,160,128]{2,1,0:T(8,128)(2,1)S(1)} collective-permute-done((bf16[3,160,128]{2,1,0:T(8,128)(2,1)S(1)}, bf16[3,160,128]{2,1,0:T(8,128)(2,1)S(1)}, u32[]{:S(2)}, u32[]{:S(2)}) %collective-permute-start.24) | collective-permute-done | bytes 122912 | tf_op jit(solution)/shard_map/ppermute | solution.py:21
  273.7 2.3 collective-permute-start.25
  276.7 4.2 %collective-permute-done.25 = bf16[3,160,128]{2,1,0:T(8,128)(2,1)S(1)} collective-permute-done((bf16[3,160,128]{2,1,0:T(8,128)(2,1)S(1)}, bf16[3,160,128]{2,1,0:T(8,128)(2,1)S(1)}, u32[]{:S(2)}, u32[]{:S(2)}) %collective-permute-start.25) | collective-permute-done | bytes 122912 | tf_op jit(solution)/shard_map/ppermute | solution.py:21
  280.9 4.6 %collective-permute-start.26 = (bf16[3,160,128]{2,1,0:T(8,128)(2,1)S(1)}, bf16[3,160,128]{2,1,0:T(8,128)(2,1)S(1)}, u32[]{:S(2)}, u32[]{:S(2)}) collective-permute-start(bf16[3,160,128]{2,1,0:T(8,128)(2,1)S(1)} %get-tuple-element.20), channel_id=1, source_target_pairs={{0,10},{1,11},{2,8},{3,9},{4,14},{5,15},{6,12},{7,13},{8,2},{9,3},... | collective-permute-start | bytes 368648 | tf_op jit(solution)/shard_map/ppermute | solution.py:21
  286.2 3.1 collective-permute-done.26
  289.3 3.9 %collective-permute-start.27 = (bf16[3,160,128]{2,1,0:T(8,128)(2,1)S(1)}, bf16[3,160,128]{2,1,0:T(8,128)(2,1)S(1)}, u32[]{:S(2)}, u32[]{:S(2)}) collective-permute-start(bf16[3,160,128]{2,1,0:T(8,128)(2,1)S(1)} %get-tuple-element.19), channel_id=1, source_target_pairs={{0,11},{1,10},{2,9},{3,8},{4,15},{5,14},{6,13},{7,12},{8,3},{9,2},... | collective-permute-start | bytes 368648 | tf_op jit(solution)/shard_map/ppermute | solution.py:21
  293.8 2.9 collective-permute-done.27
  300.1 2.5 gather_fusion.1
  302.6 1.9 pad_maximum_fusion
  305.0 3.4 %copy.33 = bf16[3,160,32,128]{3,2,1,0:T(8,128)(2,1)} copy(bf16[3,160,32,128]{3,1,0,2:T(8,128)(2,1)S(1)} %bitcast.280) | data formatting | bytes 7864320 | tf_op jit(solution)/shard_map/transpose | solution.py:74
  (121 shorter events, 34.8 us)
Async XLA Ops:
  6.5 26.8 %copy-start = (f32[32,2]{0,1:T(2,128)S(1)}, f32[32,2]{0,1:T(2,128)}, u32[]{:S(2)}) copy-start(f32[32,2]{0,1:T(2,128)} %param.12) | copy-start | bytes 772
  11.8 6.4 %copy-start.2 = (bf16[16,1,3,160,128]{4,3,2,1,0:T(8,128)(2,1)}, bf16[16,1,3,160,128]{4,3,2,1,0:T(8,128)(2,1)S(1)}, u32[]{:S(2)}) copy-start(bf16[16,1,3,160,128]{4,3,2,1,0:T(8,128)(2,1)S(1)} %get-tuple-element.8) | copy-start | bytes 5898244
  11.8 131.3 %all-to-all-start = ((bf16[16,3,160,128]{3,2,1,0:T(8,128)(2,1)}), bf16[16,3,160,128]{3,2,1,0:T(8,128)(2,1)}, u32[]{:S(2)}, u32[]{:S(2)}) async-start(bf16[16,3,160,128]{3,2,1,0:T(8,128)(2,1)} %get-tuple-element.7), calls=%async_computation | async-start | bytes 3932160 | tf_op jit(solution)/shard_map/all_to_all | solution.py:40
  18.1 112.4 %all-reduce.3.cloned.1.call-start = ((), (), s32[]{:S(2)}) async-start(), calls=%async_computation.2 | async-start | bytes 368640 | tf_op jit(solution)/shard_map/psum | solution.py:51
  19.6 102.2 %collective-permute-start.15 = (bf16[3,160,128]{2,1,0:T(8,128)(2,1)S(1)}, bf16[3,160,128]{2,1,0:T(8,128)(2,1)S(1)}, u32[]{:S(2)}, u32[]{:S(2)}) collective-permute-start(bf16[3,160,128]{2,1,0:T(8,128)(2,1)S(1)} %get-tuple-element.30), channel_id=1, source_target_pairs={{0,15},{1,14},{2,13},{3,12},{4,11},{5,10},{6,9},{7,8},{8,7},{9,6},... | collective-permute-start | bytes 368648 | tf_op jit(solution)/shard_map/ppermute | solution.py:21
  21.7 99.4 %collective-permute-start.14 = (bf16[3,160,128]{2,1,0:T(8,128)(2,1)S(1)}, bf16[3,160,128]{2,1,0:T(8,128)(2,1)S(1)}, u32[]{:S(2)}, u32[]{:S(2)}) collective-permute-start(bf16[3,160,128]{2,1,0:T(8,128)(2,1)S(1)} %get-tuple-element.31), channel_id=1, source_target_pairs={{0,14},{1,15},{2,12},{3,13},{4,10},{5,11},{6,8},{7,9},{8,6},{9,7},... | collective-permute-start | bytes 368648 | tf_op jit(solution)/shard_map/ppermute | solution.py:21
  22.3 97.3 %collective-permute-start.13 = (bf16[3,160,128]{2,1,0:T(8,128)(2,1)}, bf16[3,160,128]{2,1,0:T(8,128)(2,1)}, u32[]{:S(2)}, u32[]{:S(2)}) collective-permute-start(bf16[3,160,128]{2,1,0:T(8,128)(2,1)} %get-tuple-element.32), channel_id=1, source_target_pairs={{0,13},{1,12},{2,15},{3,14},{4,9},{5,8},{6,11},{7,10},{8,5},{9,4},... | collective-permute-start | bytes 368648 | tf_op jit(solution)/shard_map/ppermute | solution.py:21
  23.4 94.6 %collective-permute-start.12 = (bf16[3,160,128]{2,1,0:T(8,128)(2,1)}, bf16[3,160,128]{2,1,0:T(8,128)(2,1)}, u32[]{:S(2)}, u32[]{:S(2)}) collective-permute-start(bf16[3,160,128]{2,1,0:T(8,128)(2,1)} %get-tuple-element.33), channel_id=1, source_target_pairs={{0,12},{1,13},{2,14},{3,15},{4,8},{5,9},{6,10},{7,11},{8,4},{9,5},... | collective-permute-start | bytes 368648 | tf_op jit(solution)/shard_map/ppermute | solution.py:21
  24.0 15.3 %collective-permute-start.1 = (bf16[3,160,128]{2,1,0:T(8,128)(2,1)}, bf16[3,160,128]{2,1,0:T(8,128)(2,1)}, u32[]{:S(2)}, u32[]{:S(2)}) collective-permute-start(bf16[3,160,128]{2,1,0:T(8,128)(2,1)} %get-tuple-element.44), channel_id=1, source_target_pairs={{0,1},{1,0},{2,3},{3,2},{4,5},{5,4},{6,7},{7,6},{8,9},{9,8},{10,11... | collective-permute-start | bytes 368648 | tf_op jit(solution)/shard_map/ppermute | solution.py:21
  33.3 2.4 copy-start.10
  34.6 35.4 %copy-start.9 = (bf16[3,160,128]{2,1,0:T(8,128)(2,1)S(1)}, bf16[3,160,128]{2,1,0:T(8,128)(2,1)}, u32[]{:S(2)}) copy-start(bf16[3,160,128]{2,1,0:T(8,128)(2,1)} %get-tuple-element.40) | copy-start | bytes 368644
  34.6 40.9 %copy-start.8 = (bf16[3,160,128]{2,1,0:T(8,128)(2,1)S(1)}, bf16[3,160,128]{2,1,0:T(8,128)(2,1)}, u32[]{:S(2)}) copy-start(bf16[3,160,128]{2,1,0:T(8,128)(2,1)} %get-tuple-element.39) | copy-start | bytes 368644
  34.6 48.0 %copy-start.7 = (bf16[3,160,128]{2,1,0:T(8,128)(2,1)S(1)}, bf16[3,160,128]{2,1,0:T(8,128)(2,1)}, u32[]{:S(2)}) copy-start(bf16[3,160,128]{2,1,0:T(8,128)(2,1)} %get-tuple-element.38) | copy-start | bytes 368644
  34.6 54.5 %copy-start.6 = (bf16[3,160,128]{2,1,0:T(8,128)(2,1)S(1)}, bf16[3,160,128]{2,1,0:T(8,128)(2,1)}, u32[]{:S(2)}) copy-start(bf16[3,160,128]{2,1,0:T(8,128)(2,1)} %get-tuple-element.37) | copy-start | bytes 368644
  34.6 60.8 %copy-start.5 = (bf16[3,160,128]{2,1,0:T(8,128)(2,1)S(1)}, bf16[3,160,128]{2,1,0:T(8,128)(2,1)}, u32[]{:S(2)}) copy-start(bf16[3,160,128]{2,1,0:T(8,128)(2,1)} %get-tuple-element.36) | copy-start | bytes 368644
  34.7 68.5 %copy-start.4 = (bf16[3,160,128]{2,1,0:T(8,128)(2,1)S(1)}, bf16[3,160,128]{2,1,0:T(8,128)(2,1)}, u32[]{:S(2)}) copy-start(bf16[3,160,128]{2,1,0:T(8,128)(2,1)} %get-tuple-element.35) | copy-start | bytes 368644
  34.7 75.7 %copy-start.3 = (bf16[3,160,128]{2,1,0:T(8,128)(2,1)S(1)}, bf16[3,160,128]{2,1,0:T(8,128)(2,1)}, u32[]{:S(2)}) copy-start(bf16[3,160,128]{2,1,0:T(8,128)(2,1)} %get-tuple-element.34) | copy-start | bytes 368644
  39.3 7.7 %collective-permute-start.2 = (bf16[3,160,128]{2,1,0:T(8,128)(2,1)}, bf16[3,160,128]{2,1,0:T(8,128)(2,1)S(1)}, u32[]{:S(2)}, u32[]{:S(2)}) collective-permute-start(bf16[3,160,128]{2,1,0:T(8,128)(2,1)} %get-tuple-element.43), channel_id=1, source_target_pairs={{0,2},{1,3},{2,0},{3,1},{4,6},{5,7},{6,4},{7,5},{8,10},{9,11},{10,... | collective-permute-start | bytes 368648 | tf_op jit(solution)/shard_map/ppermute | solution.py:21
  47.0 8.1 %collective-permute-start.3 = (bf16[3,160,128]{2,1,0:T(8,128)(2,1)}, bf16[3,160,128]{2,1,0:T(8,128)(2,1)S(1)}, u32[]{:S(2)}, u32[]{:S(2)}) collective-permute-start(bf16[3,160,128]{2,1,0:T(8,128)(2,1)} %get-tuple-element.42), channel_id=1, source_target_pairs={{0,3},{1,2},{2,1},{3,0},{4,7},{5,6},{6,5},{7,4},{8,11},{9,10},{10,... | collective-permute-start | bytes 368648 | tf_op jit(solution)/shard_map/ppermute | solution.py:21
  55.0 15.0 %collective-permute-start.4 = (bf16[3,160,128]{2,1,0:T(8,128)(2,1)}, bf16[3,160,128]{2,1,0:T(8,128)(2,1)S(1)}, u32[]{:S(2)}, u32[]{:S(2)}) collective-permute-start(bf16[3,160,128]{2,1,0:T(8,128)(2,1)} %get-tuple-element.41), channel_id=1, source_target_pairs={{0,4},{1,5},{2,6},{3,7},{4,0},{5,1},{6,2},{7,3},{8,12},{9,13},{10,... | collective-permute-start | bytes 368648 | tf_op jit(solution)/shard_map/ppermute | solution.py:21
  70.0 5.5 %collective-permute-start.5 = (bf16[3,160,128]{2,1,0:T(8,128)(2,1)S(1)}, bf16[3,160,128]{2,1,0:T(8,128)(2,1)S(1)}, u32[]{:S(2)}, u32[]{:S(2)}) collective-permute-start(bf16[3,160,128]{2,1,0:T(8,128)(2,1)S(1)} %copy-done.9), channel_id=1, source_target_pairs={{0,5},{1,4},{2,7},{3,6},{4,1},{5,0},{6,3},{7,2},{8,13},{9,12},{10,... | collective-permute-start | bytes 368648 | tf_op jit(solution)/shard_map/ppermute | solution.py:21
  75.5 7.1 %collective-permute-start.6 = (bf16[3,160,128]{2,1,0:T(8,128)(2,1)S(1)}, bf16[3,160,128]{2,1,0:T(8,128)(2,1)S(1)}, u32[]{:S(2)}, u32[]{:S(2)}) collective-permute-start(bf16[3,160,128]{2,1,0:T(8,128)(2,1)S(1)} %copy-done.8), channel_id=1, source_target_pairs={{0,6},{1,7},{2,4},{3,5},{4,2},{5,3},{6,0},{7,1},{8,14},{9,15},{10,... | collective-permute-start | bytes 368648 | tf_op jit(solution)/shard_map/ppermute | solution.py:21
  82.6 6.5 %collective-permute-start.7 = (bf16[3,160,128]{2,1,0:T(8,128)(2,1)S(1)}, bf16[3,160,128]{2,1,0:T(8,128)(2,1)S(1)}, u32[]{:S(2)}, u32[]{:S(2)}) collective-permute-start(bf16[3,160,128]{2,1,0:T(8,128)(2,1)S(1)} %copy-done.7), channel_id=1, source_target_pairs={{0,7},{1,6},{2,5},{3,4},{4,3},{5,2},{6,1},{7,0},{8,15},{9,14},{10,... | collective-permute-start | bytes 368648 | tf_op jit(solution)/shard_map/ppermute | solution.py:21
  89.1 6.3 %collective-permute-start.8 = (bf16[3,160,128]{2,1,0:T(8,128)(2,1)S(1)}, bf16[3,160,128]{2,1,0:T(8,128)(2,1)S(1)}, u32[]{:S(2)}, u32[]{:S(2)}) collective-permute-start(bf16[3,160,128]{2,1,0:T(8,128)(2,1)S(1)} %copy-done.6), channel_id=1, source_target_pairs={{0,8},{1,9},{2,10},{3,11},{4,12},{5,13},{6,14},{7,15},{8,0},{9,1},... | collective-permute-start | bytes 368648 | tf_op jit(solution)/shard_map/ppermute | solution.py:21
  95.5 7.7 %collective-permute-start.9 = (bf16[3,160,128]{2,1,0:T(8,128)(2,1)S(1)}, bf16[3,160,128]{2,1,0:T(8,128)(2,1)S(1)}, u32[]{:S(2)}, u32[]{:S(2)}) collective-permute-start(bf16[3,160,128]{2,1,0:T(8,128)(2,1)S(1)} %copy-done.5), channel_id=1, source_target_pairs={{0,9},{1,8},{2,11},{3,10},{4,13},{5,12},{6,15},{7,14},{8,1},{9,0},... | collective-permute-start | bytes 368648 | tf_op jit(solution)/shard_map/ppermute | solution.py:21
  103.2 7.2 %collective-permute-start.10 = (bf16[3,160,128]{2,1,0:T(8,128)(2,1)S(1)}, bf16[3,160,128]{2,1,0:T(8,128)(2,1)S(1)}, u32[]{:S(2)}, u32[]{:S(2)}) collective-permute-start(bf16[3,160,128]{2,1,0:T(8,128)(2,1)S(1)} %copy-done.4), channel_id=1, source_target_pairs={{0,10},{1,11},{2,8},{3,9},{4,14},{5,15},{6,12},{7,13},{8,2},{9,3},... | collective-permute-start | bytes 368648 | tf_op jit(solution)/shard_map/ppermute | solution.py:21
  110.4 6.9 %collective-permute-start.11 = (bf16[3,160,128]{2,1,0:T(8,128)(2,1)S(1)}, bf16[3,160,128]{2,1,0:T(8,128)(2,1)S(1)}, u32[]{:S(2)}, u32[]{:S(2)}) collective-permute-start(bf16[3,160,128]{2,1,0:T(8,128)(2,1)S(1)} %copy-done.3), channel_id=1, source_target_pairs={{0,11},{1,10},{2,9},{3,8},{4,15},{5,14},{6,13},{7,12},{8,3},{9,2},... | collective-permute-start | bytes 368648 | tf_op jit(solution)/shard_map/ppermute | solution.py:21
  128.8 14.1 %collective-permute-start.16 = (bf16[3,128,640]{2,1,0:T(8,128)(2,1)S(1)}, bf16[3,128,640]{2,1,0:T(8,128)(2,1)S(1)}, u32[]{:S(2)}, u32[]{:S(2)}) collective-permute-start(bf16[3,128,640]{2,1,0:T(8,128)(2,1)S(1)} %get-tuple-element.68), channel_id=1, source_target_pairs={{0,16},{16,0},{1,17},{17,1},{2,18},{18,2},{3,19},{19,3},{4,20},{20... | collective-permute-start | bytes 1474568 | tf_op jit(solution)/shard_map/ppermute | solution.py:62
  143.1 2.1 copy-start.11
  152.4 24.0 %collective-permute-start = (bf16[3,128,1280]{2,1,0:T(8,128)(2,1)}, bf16[3,128,1280]{2,1,0:T(8,128)(2,1)S(1)}, u32[]{:S(2)}, u32[]{:S(2)}) collective-permute-start(bf16[3,128,1280]{2,1,0:T(8,128)(2,1)} %get-tuple-element.70), channel_id=1, source_target_pairs={{0,16},{16,0},{1,17},{17,1},{2,18},{18,2},{3,19},{19,3},{4,20},{20... | collective-permute-start | bytes 2949128 | tf_op jit(solution)/shard_map/ppermute | solution.py:62
  191.0 111.6 %all-to-all-start.1 = ((bf16[16,3,160,128]{3,2,1,0:T(8,128)(2,1)}), bf16[16,3,160,128]{3,2,1,0:T(8,128)(2,1)}, u32[]{:S(2)}, u32[]{:S(2)}) async-start(bf16[16,3,160,128]{3,2,1,0:T(8,128)(2,1)} %bitcast.284), calls=%async_computation.1 | async-start | bytes 3932160 | tf_op jit(solution)/shard_map/all_to_all | solution.py:40
  198.7 5.3 %collective-permute-start.17 = (bf16[3,160,128]{2,1,0:T(8,128)(2,1)S(1)}, bf16[3,160,128]{2,1,0:T(8,128)(2,1)S(1)}, u32[]{:S(2)}, u32[]{:S(2)}) collective-permute-start(bf16[3,160,128]{2,1,0:T(8,128)(2,1)S(1)} %get-tuple-element.29), channel_id=1, source_target_pairs={{0,1},{1,0},{2,3},{3,2},{4,5},{5,4},{6,7},{7,6},{8,9},{9,8},{10,11... | collective-permute-start | bytes 368648 | tf_op jit(solution)/shard_map/ppermute | solution.py:21
  198.9 100.5 %collective-permute-start.31 = (bf16[3,160,128]{2,1,0:T(8,128)(2,1)S(1)}, bf16[3,160,128]{2,1,0:T(8,128)(2,1)S(1)}, u32[]{:S(2)}, u32[]{:S(2)}) collective-permute-start(bf16[3,160,128]{2,1,0:T(8,128)(2,1)S(1)} %get-tuple-element.15), channel_id=1, source_target_pairs={{0,15},{1,14},{2,13},{3,12},{4,11},{5,10},{6,9},{7,8},{8,7},{9,6},... | collective-permute-start | bytes 368648 | tf_op jit(solution)/shard_map/ppermute | solution.py:21
  201.3 97.5 %collective-permute-start.30 = (bf16[3,160,128]{2,1,0:T(8,128)(2,1)S(1)}, bf16[3,160,128]{2,1,0:T(8,128)(2,1)S(1)}, u32[]{:S(2)}, u32[]{:S(2)}) collective-permute-start(bf16[3,160,128]{2,1,0:T(8,128)(2,1)S(1)} %get-tuple-element.16), channel_id=1, source_target_pairs={{0,14},{1,15},{2,12},{3,13},{4,10},{5,11},{6,8},{7,9},{8,6},{9,7},... | collective-permute-start | bytes 368648 | tf_op jit(solution)/shard_map/ppermute | solution.py:21
  201.8 96.3 %collective-permute-start.29 = (bf16[3,160,128]{2,1,0:T(8,128)(2,1)S(1)}, bf16[3,160,128]{2,1,0:T(8,128)(2,1)S(1)}, u32[]{:S(2)}, u32[]{:S(2)}) collective-permute-start(bf16[3,160,128]{2,1,0:T(8,128)(2,1)S(1)} %get-tuple-element.17), channel_id=1, source_target_pairs={{0,13},{1,12},{2,15},{3,14},{4,9},{5,8},{6,11},{7,10},{8,5},{9,4},... | collective-permute-start | bytes 368648 | tf_op jit(solution)/shard_map/ppermute | solution.py:21
  202.8 94.7 %collective-permute-start.28 = (bf16[3,160,128]{2,1,0:T(8,128)(2,1)S(1)}, bf16[3,160,128]{2,1,0:T(8,128)(2,1)S(1)}, u32[]{:S(2)}, u32[]{:S(2)}) collective-permute-start(bf16[3,160,128]{2,1,0:T(8,128)(2,1)S(1)} %get-tuple-element.18), channel_id=1, source_target_pairs={{0,12},{1,13},{2,14},{3,15},{4,8},{5,9},{6,10},{7,11},{8,4},{9,5},... | collective-permute-start | bytes 368648 | tf_op jit(solution)/shard_map/ppermute | solution.py:21
  204.0 8.3 %collective-permute-start.18 = (bf16[3,160,128]{2,1,0:T(8,128)(2,1)S(1)}, bf16[3,160,128]{2,1,0:T(8,128)(2,1)S(1)}, u32[]{:S(2)}, u32[]{:S(2)}) collective-permute-start(bf16[3,160,128]{2,1,0:T(8,128)(2,1)S(1)} %get-tuple-element.28), channel_id=1, source_target_pairs={{0,2},{1,3},{2,0},{3,1},{4,6},{5,7},{6,4},{7,5},{8,10},{9,11},{10,... | collective-permute-start | bytes 368648 | tf_op jit(solution)/shard_map/ppermute | solution.py:21
  212.3 8.2 %collective-permute-start.19 = (bf16[3,160,128]{2,1,0:T(8,128)(2,1)S(1)}, bf16[3,160,128]{2,1,0:T(8,128)(2,1)S(1)}, u32[]{:S(2)}, u32[]{:S(2)}) collective-permute-start(bf16[3,160,128]{2,1,0:T(8,128)(2,1)S(1)} %get-tuple-element.27), channel_id=1, source_target_pairs={{0,3},{1,2},{2,1},{3,0},{4,7},{5,6},{6,5},{7,4},{8,11},{9,10},{10,... | collective-permute-start | bytes 368648 | tf_op jit(solution)/shard_map/ppermute | solution.py:21
  220.5 24.5 %collective-permute-start.20 = (bf16[3,160,128]{2,1,0:T(8,128)(2,1)S(1)}, bf16[3,160,128]{2,1,0:T(8,128)(2,1)S(1)}, u32[]{:S(2)}, u32[]{:S(2)}) collective-permute-start(bf16[3,160,128]{2,1,0:T(8,128)(2,1)S(1)} %get-tuple-element.26), channel_id=1, source_target_pairs={{0,4},{1,5},{2,6},{3,7},{4,0},{5,1},{6,2},{7,3},{8,12},{9,13},{10,... | collective-permute-start | bytes 368648 | tf_op jit(solution)/shard_map/ppermute | solution.py:21
  245.0 5.5 %collective-permute-start.21 = (bf16[3,160,128]{2,1,0:T(8,128)(2,1)S(1)}, bf16[3,160,128]{2,1,0:T(8,128)(2,1)S(1)}, u32[]{:S(2)}, u32[]{:S(2)}) collective-permute-start(bf16[3,160,128]{2,1,0:T(8,128)(2,1)S(1)} %get-tuple-element.25), channel_id=1, source_target_pairs={{0,5},{1,4},{2,7},{3,6},{4,1},{5,0},{6,3},{7,2},{8,13},{9,12},{10,... | collective-permute-start | bytes 368648 | tf_op jit(solution)/shard_map/ppermute | solution.py:21
  250.5 8.9 %collective-permute-start.22 = (bf16[3,160,128]{2,1,0:T(8,128)(2,1)S(1)}, bf16[3,160,128]{2,1,0:T(8,128)(2,1)S(1)}, u32[]{:S(2)}, u32[]{:S(2)}) collective-permute-start(bf16[3,160,128]{2,1,0:T(8,128)(2,1)S(1)} %get-tuple-element.24), channel_id=1, source_target_pairs={{0,6},{1,7},{2,4},{3,5},{4,2},{5,3},{6,0},{7,1},{8,14},{9,15},{10,... | collective-permute-start | bytes 368648 | tf_op jit(solution)/shard_map/ppermute | solution.py:21
  259.4 5.7 %collective-permute-start.23 = (bf16[3,160,128]{2,1,0:T(8,128)(2,1)S(1)}, bf16[3,160,128]{2,1,0:T(8,128)(2,1)S(1)}, u32[]{:S(2)}, u32[]{:S(2)}) collective-permute-start(bf16[3,160,128]{2,1,0:T(8,128)(2,1)S(1)} %get-tuple-element.23), channel_id=1, source_target_pairs={{0,7},{1,6},{2,5},{3,4},{4,3},{5,2},{6,1},{7,0},{8,15},{9,14},{10,... | collective-permute-start | bytes 368648 | tf_op jit(solution)/shard_map/ppermute | solution.py:21
  265.2 8.5 %collective-permute-start.24 = (bf16[3,160,128]{2,1,0:T(8,128)(2,1)S(1)}, bf16[3,160,128]{2,1,0:T(8,128)(2,1)S(1)}, u32[]{:S(2)}, u32[]{:S(2)}) collective-permute-start(bf16[3,160,128]{2,1,0:T(8,128)(2,1)S(1)} %get-tuple-element.22), channel_id=1, source_target_pairs={{0,8},{1,9},{2,10},{3,11},{4,12},{5,13},{6,14},{7,15},{8,0},{9,1},... | collective-permute-start | bytes 368648 | tf_op jit(solution)/shard_map/ppermute | solution.py:21
  273.7 7.2 %collective-permute-start.25 = (bf16[3,160,128]{2,1,0:T(8,128)(2,1)S(1)}, bf16[3,160,128]{2,1,0:T(8,128)(2,1)S(1)}, u32[]{:S(2)}, u32[]{:S(2)}) collective-permute-start(bf16[3,160,128]{2,1,0:T(8,128)(2,1)S(1)} %get-tuple-element.21), channel_id=1, source_target_pairs={{0,9},{1,8},{2,11},{3,10},{4,13},{5,12},{6,15},{7,14},{8,1},{9,0},... | collective-permute-start | bytes 368648 | tf_op jit(solution)/shard_map/ppermute | solution.py:21
  280.9 8.4 %collective-permute-start.26 = (bf16[3,160,128]{2,1,0:T(8,128)(2,1)S(1)}, bf16[3,160,128]{2,1,0:T(8,128)(2,1)S(1)}, u32[]{:S(2)}, u32[]{:S(2)}) collective-permute-start(bf16[3,160,128]{2,1,0:T(8,128)(2,1)S(1)} %get-tuple-element.20), channel_id=1, source_target_pairs={{0,10},{1,11},{2,8},{3,9},{4,14},{5,15},{6,12},{7,13},{8,2},{9,3},... | collective-permute-start | bytes 368648 | tf_op jit(solution)/shard_map/ppermute | solution.py:21
  289.3 7.5 %collective-permute-start.27 = (bf16[3,160,128]{2,1,0:T(8,128)(2,1)S(1)}, bf16[3,160,128]{2,1,0:T(8,128)(2,1)S(1)}, u32[]{:S(2)}, u32[]{:S(2)}) collective-permute-start(bf16[3,160,128]{2,1,0:T(8,128)(2,1)S(1)} %get-tuple-element.19), channel_id=1, source_target_pairs={{0,11},{1,10},{2,9},{3,8},{4,15},{5,14},{6,13},{7,12},{8,3},{9,2},... | collective-permute-start | bytes 368648 | tf_op jit(solution)/shard_map/ppermute | solution.py:21
  305.0 3.5 %copy-start.1 = (f32[32,2]{0,1:T(2,128)S(1)}, f32[32,2]{0,1:T(2,128)}, u32[]{:S(2)}) copy-start(f32[32,2]{0,1:T(2,128)} %param.12) | copy-start | bytes 772
Sparse Core Ops, SparseCore 0:
  35.8 26.8 all-reduce.2

commit v3 on v0

v3 whole, which is shorter than its diff:
```python
import functools

import jax
import jax.numpy as jnp
from jax import lax
from jax.experimental import pallas as pl
from jax.experimental.pallas import tpu as pltpu
from jax.sharding import PartitionSpec as P

BF16 = jnp.bfloat16
F32 = jnp.float32
VMEM_LIMIT = 56 * 1024 * 1024
CORES = 2
ROWS = 16


def params(semantics=None):
    return pltpu.CompilerParams(vmem_limit_bytes=VMEM_LIMIT, dimension_semantics=semantics)


def weigh_kernel(slot, local_slots, me_ref, gauss_ref, tendency_ref, *rest):
    outs, wide = rest[:-1], rest[-1]
    _, lats, slots, members = tendency_ref.shape
    wide[...] = tendency_ref[0].astype(F32).reshape(lats * slots, members)
    chip = me_ref[0] // CORES
    for k, out in enumerate(outs):
        for core in range(CORES):
            row = ((chip ^ k) * CORES + core) * local_slots + slot
            picked = wide[pl.ds(row, lats, stride=slots), :]
            out[core, 0] = (picked * gauss_ref[...]).astype(BF16)


def weigh(tendency, gauss, me, slot, local_slots):
    rows, lats, slots, members = tendency.shape
    chips = slots // local_slots // CORES
    piece = pl.BlockSpec((CORES, 1, lats, members), lambda r, m: (0, r, 0, 0))
    return pl.pallas_call(
        functools.partial(weigh_kernel, slot, local_slots),
        out_shape=[jax.ShapeDtypeStruct((CORES, rows, lats, members), BF16)] * chips,
        grid_spec=pltpu.PrefetchScalarGridSpec(
            num_scalar_prefetch=1,
            grid=(rows,),
            in_specs=[
                pl.BlockSpec((lats, members), lambda r, m: (0, 0)),
                pl.BlockSpec((1, lats, slots, members), lambda r, m: (r, 0, 0, 0)),
            ],
            out_specs=[piece] * chips,
            scratch_shapes=[pltpu.VMEM((lats * slots, members), F32)],
        ),
        compiler_params=params(),
        cost_estimate=pl.CostEstimate(flops=tendency.size, bytes_accessed=3 * tendency.size, transcendentals=0),
        name="weigh",
    )(me, gauss, tendency)


def run_copies(copies):
    for copy in copies:
        copy.start()
    for copy in copies:
        copy.wait()


def pick_kernel(me_ref, *rest):
    ins, out, sems = rest[:-2], rest[-2], rest[-1]
    mate = (CORES - 1) - me_ref[0] % CORES
    run_copies([pltpu.make_async_copy(ref.at[mate], out.at[k], sems.at[k]) for k, ref in enumerate(ins)])


def pick(messages, me):
    anywhere = pl.BlockSpec(memory_space=pl.ANY)
    shape = (len(messages),) + messages[0].shape[1:]
    size = 4 * len(messages) * messages[0].size // CORES
    return pl.pallas_call(
        pick_kernel,
        out_shape=jax.ShapeDtypeStruct(shape, BF16),
        in_specs=[pl.BlockSpec(memory_space=pltpu.SMEM)] + [anywhere] * len(messages),
        out_specs=anywhere,
        scratch_shapes=[pltpu.SemaphoreType.DMA((len(messages),))],
        compiler_params=params(),
        cost_estimate=pl.CostEstimate(flops=0, bytes_accessed=size, transcendentals=0),
        name="pick",
    )(me, *messages)


def pair_kernel(own, mate, *rest):
    outs, sems = rest[:-1], rest[-1]
    copies = []
    for k, out in enumerate(outs):
        copies.append(pltpu.make_async_copy(own.at[k], out.at[0], sems.at[0, k]))
        copies.append(pltpu.make_async_copy(mate.at[k], out.at[1], sems.at[1, k]))
    run_copies(copies)


def pair(own, mate):
    anywhere = pl.BlockSpec(memory_space=pl.ANY)
    chips = own.shape[0]
    return pl.pallas_call(
        pair_kernel,
        out_shape=[jax.ShapeDtypeStruct((CORES,) + own.shape[1:], BF16)] * chips,
        in_specs=[anywhere] * 2,
        out_specs=[anywhere] * chips,
        scratch_shapes=[pltpu.SemaphoreType.DMA((CORES, chips))],
        compiler_params=params(),
        cost_estimate=pl.CostEstimate(flops=0, bytes_accessed=8 * own.size, transcendentals=0),
        name="pair",
    )(own, mate)


def ordered(here, chips):
    owner = jnp.arange(chips * CORES, dtype=jnp.int32)
    return ((owner // CORES) ^ (here // CORES)) * CORES + (owner % CORES ^ here % CORES)


def analyse_kernel(slot, low, chips, lats, me_ref, wave_ref, table_ref, state_ref, *rest):
    messages, mate, out, grid, sems = rest[:-4], rest[-4], rest[-3], rest[-2], rest[-1]
    rows = out.shape[0]
    members = out.shape[1]
    width = table_ref.shape[1]
    step = pl.program_id(0)

    @pl.when(step == 0)
    def _():
        chip, core = me_ref[0] // CORES, me_ref[0] % CORES
        copies = []
        if not messages:
            copies.append(pltpu.make_async_copy(mate, grid, sems.at[0, 0, 0]))
        for k in range(len(messages)):
            for source in range(CORES):
                origin = (chip ^ k) * CORES + (core if source == 0 else CORES - 1 - core)
                start = pl.multiple_of(origin * lats, lats)
                block = messages[k].at[core] if source == 0 else mate.at[k]
                for r in range(rows):
                    target = grid.at[pl.ds(start, lats), pl.ds(r * members, members)]
                    copies.append(pltpu.make_async_copy(block.at[r], target, sems.at[source, k, r]))
        run_copies(copies)

    sums = jnp.dot(table_ref[0], grid[...], preferred_element_type=F32)
    degree = lax.broadcasted_iota(jnp.int32, (members, width), 1) + (low + step * width)
    live = degree >= wave_ref[slot]
    for r in range(rows):
        tend = sums[:, r * members : (r + 1) * members].T
        total = state_ref[r, 0].astype(F32) + tend
        out[r] = jnp.where(live, total, 0.0).astype(BF16)


def analyse(messages, mate, table, state, wave, me, slot, low, width):
    chips = len(messages)
    _, rows, lats, members = messages[0].shape
    nspec, nlat = table.shape[1:]
    first = low // width
    if lats % ROWS:
        own = jnp.stack([lax.dynamic_index_in_dim(m, me[0] % CORES, 0, keepdims=False) for m in messages])
        blocks = jnp.stack([own, mate], axis=1).reshape(chips * CORES, rows, lats, members)
        blocks = jnp.take(blocks, ordered(me[0], chips), axis=0)
        messages, mate = [], jnp.transpose(blocks, (0, 2, 1, 3)).reshape(nlat, rows * members)
    anywhere = pl.BlockSpec(memory_space=pl.ANY)
    smem = pl.BlockSpec(memory_space=pltpu.SMEM)
    return pl.pallas_call(
        functools.partial(analyse_kernel, slot, low, chips, lats),
        out_shape=jax.ShapeDtypeStruct((rows, members, nspec - low), BF16),
        grid=((nspec - low) // width,),
        in_specs=[
            smem,
            smem,
            pl.BlockSpec((1, width, nlat), lambda i: (slot, first + i, 0)),
            pl.BlockSpec((rows, 1, members, width), lambda i: (0, slot, 0, first + i)),
        ]
        + [anywhere] * (len(messages) + 1),
        out_specs=pl.BlockSpec((rows, members, width), lambda i: (0, 0, i)),
        scratch_shapes=[
            pltpu.VMEM((nlat, rows * members), BF16),
            pltpu.SemaphoreType.DMA((CORES, chips, rows)),
        ],
        compiler_params=params(),
        cost_estimate=pl.CostEstimate(
            flops=2 * (nspec - low) * nlat * rows * members, bytes_accessed=2 * nspec * nlat, transcendentals=0
        ),
        name="analyse",
    )(me, wave, table, state, *messages, mate)


def synthesise_kernel(chips, lats, me_ref, matrix_ref, own_ref, other_ref, table_ref, *rest):
    outs, (mixed, grid, sems) = rest[:-3], rest[-3:]
    rows, members, _ = own_ref.shape
    width = table_ref.shape[2]
    step = pl.program_id(0)

    @pl.when(step == 0)
    def _():
        for f in range(rows):
            total = 0.0
            for g in range(rows):
                total = total + matrix_ref[f * rows + g : f * rows + g + 1, :] * own_ref[g].astype(F32)
                line = rows * rows + f * rows + g
                total = total + matrix_ref[line : line + 1, :] * other_ref[g].astype(F32)
            mixed[f * members : (f + 1) * members, :] = total.astype(BF16)

    sums = jnp.dot(mixed[...], table_ref[0], preferred_element_type=F32)
    start = pl.multiple_of(step * width, width)
    for r in range(rows):
        grid[r, pl.ds(start, width), :] = sums[r * members : (r + 1) * members, :].T.astype(BF16)

    @pl.when(step == pl.num_programs(0) - 1)
    def _():
        chip, core = me_ref[0] // CORES, me_ref[0] % CORES
        copies = []
        if len(outs) == 1:
            copies.append(pltpu.make_async_copy(grid, outs[0], sems.at[0, 0, 0]))
        for k in range(chips if len(outs) > 1 else 0):
            for target, out in enumerate(outs):
                owner = (chip ^ k) * CORES + (core if target == 0 else CORES - 1 - core)
                here = pl.ds(pl.multiple_of(owner * lats, lats), lats)
                for r in range(rows):
                    copies.append(pltpu.make_async_copy(grid.at[r, here, :], out.at[k, r], sems.at[target, k, r]))
        run_copies(copies)


def synthesise(matrix, own, other, table, me, slot, low, chips, width):
    rows, members, count = own.shape
    nlat = table.shape[2]
    lats = nlat // chips // CORES
    anywhere = pl.BlockSpec(memory_space=pl.ANY)
    whole = pl.BlockSpec((rows, members, count), lambda j: (0, 0, 0))
    shapes = [jax.ShapeDtypeStruct((chips, rows, lats, members), BF16)] * CORES
    if lats % ROWS:
        shapes = [jax.ShapeDtypeStruct((rows, nlat, members), BF16)]
    outs = pl.pallas_call(
        functools.partial(synthesise_kernel, chips, lats),
        out_shape=shapes,
        grid=(nlat // width,),
        in_specs=[
            pl.BlockSpec(memory_space=pltpu.SMEM),
            pl.BlockSpec(matrix.shape, lambda j: (0, 0)),
            whole,
            whole,
            pl.BlockSpec((1, count, width), lambda j: (slot, low // count, j)),
        ],
        out_specs=[anywhere] * len(shapes),
        scratch_shapes=[
            pltpu.VMEM((rows * members, count), BF16),
            pltpu.VMEM((rows, nlat, members), BF16),
            pltpu.SemaphoreType.DMA((CORES, chips, rows)),
        ],
        compiler_params=params(),
        cost_estimate=pl.CostEstimate(
            flops=2 * count * nlat * rows * members, bytes_accessed=2 * count * nlat, transcendentals=0
        ),
        name="synthesise",
    )(me, matrix, own, other, table)
    if lats % ROWS:
        blocks = jnp.transpose(outs[0].reshape(rows, chips * CORES, lats, members), (1, 0, 2, 3))
        blocks = jnp.take(blocks, ordered(me[0], chips), axis=0).reshape(chips, CORES, rows, lats, members)
        outs = [blocks[:, 0], blocks[:, 1]]
    return outs


def assemble_kernel(chips, local_slots, me_ref, *rest):
    ins, out, wide = rest[:-2], rest[-2], rest[-1]
    _, lats, slots, members = out.shape
    chip, core = me_ref[0] // CORES, me_ref[0] % CORES
    for slot in range(local_slots):
        for k in range(chips):
            for source in range(CORES):
                origin = (chip ^ k) * CORES + (core if source == 0 else CORES - 1 - core)
                block = ins[slot * chips + k][source, 0]
                wide[pl.ds(origin * local_slots + slot, lats, stride=slots), :] = block.astype(F32)
    out[0] = wide[...].astype(BF16).reshape(lats, slots, members)


def assemble(pieces, me):
    local_slots, chips = len(pieces), len(pieces[0])
    _, rows, lats, members = pieces[0][0].shape
    slots = local_slots * chips * CORES
    piece = pl.BlockSpec((CORES, 1, lats, members), lambda r, m: (0, r, 0, 0))
    return pl.pallas_call(
        functools.partial(assemble_kernel, chips, local_slots),
        out_shape=jax.ShapeDtypeStruct((rows, lats, slots, members), BF16),
        grid_spec=pltpu.PrefetchScalarGridSpec(
            num_scalar_prefetch=1,
            grid=(rows,),
            in_specs=[piece] * (chips * local_slots),
            out_specs=pl.BlockSpec((1, lats, slots, members), lambda r, m: (r, 0, 0, 0)),
            scratch_shapes=[pltpu.VMEM((lats * slots, members), F32)],
        ),
        compiler_params=params(),
        name="assemble",
    )(me, *[block for slot in pieces for block in slot])


def between_chips(messages, chips):
    half = chips // 2
    order = []
    for near, far in zip([0] + list(range(1, half)), range(half, chips)):
        order += [far, near]
    got = {0: messages[0]}
    for k in [k for k in order if k > 0]:
        moves = [(d, d ^ (k * CORES)) for d in range(chips * CORES)]
        got[k] = lax.ppermute(messages[k], "wave", moves)
    return [got[k] for k in range(chips)]


def between_cores(blocks, owners):
    return lax.ppermute(blocks, "wave", [(d, d ^ 1) for d in range(owners)])


def per_device(
    tendency, spectral_state, legendre, gauss_weights, block_inverses, pole_coeffs, wavenumbers
):
    rows, lats, slots, members = tendency.shape
    local_slots, nspec, nlat = legendre.shape
    owners = slots // local_slots
    chips = owners // CORES
    me = lax.axis_index("wave").astype(jnp.int32).reshape(1)
    pole_index = lax.axis_index("pole")
    orientation = (2 * pole_index - 1).astype(F32)
    gauss = jnp.broadcast_to(gauss_weights[:, None], (lats, members))
    received = [
        between_chips(weigh(tendency, gauss, me, slot, local_slots), chips) for slot in range(local_slots)
    ]

    local_pairs = block_inverses.shape[0]
    flat_inverse = block_inverses.reshape(local_pairs, -1).astype(F32)
    weighted_sums = jnp.dot(pole_coeffs.T, flat_inverse, precision=lax.Precision.HIGHEST)
    weighted_sums = weighted_sums.reshape(2, 2, rows, rows, local_slots, nspec)
    real_matrix = weighted_sums[0, 0] - weighted_sums[1, 1]
    imag_matrix = weighted_sums[0, 1] + weighted_sums[1, 0]
    real_matrix, imag_matrix = lax.psum((real_matrix, imag_matrix), "pole")
    matrices = jnp.concatenate([real_matrix, orientation * imag_matrix]).reshape(2 * rows * rows, local_slots, nspec)

    sent = []
    for slot in range(local_slots):
        low = nspec // 2 if slot % 2 else 0
        mate = between_cores(pick(received[slot], me), owners)
        forced = analyse(received[slot], mate, legendre, spectral_state, wavenumbers, me, slot, low, nspec // 2)
        other = lax.ppermute(forced, "pole", [(0, 1), (1, 0)])
        own, for_mate = synthesise(matrices[:, slot, low:], forced, other, legendre, me, slot, low, chips, nlat // 5)
        sent.append(between_chips(pair(own, between_cores(for_mate, owners)), chips))
    return assemble(sent, me)


def solution(mesh):
    in_specs = (
        P("pole", "wave", None, None),
        P("pole", "wave", None, None),
        P("wave", None, None),
        P("wave"),
        P("pole", None, "wave", None),
        P("pole", None),
        P("wave"),
    )
    out_specs = P("pole", "wave", None, None)
    return jax.shard_map(
        per_device, mesh=mesh, in_specs=in_specs, out_specs=out_specs, check_vma=False
    )
```

time: 306 us -> 436 us (1.42)
  Pallas kernels: 0 us -> 242 us
  blocking collectives: 93.1 us -> 0 us
  starting transfers between devices: 6.79 us -> 43.9 us
  matrix products: 24 us -> 1.26 us
  waiting for transfers between devices: 129 us -> 114 us
  local copies, waits for them, and re-layouts: 27.6 us -> 16.2 us
  other arithmetic: 9.56 us -> 2.84 us
    pallas_call x0 -> x11, Pallas kernels: none -> 242 us  [the longest x2 122 us: pair(): pl.pallas_call(pair_kernel, out_shape=[jax.ShapeDtypeStruct((CORES,) + ow...]
    ppermute x0 -> x34, waiting for transfers between devices: none -> 110 us  [the longest x28 90 us: between_chips(): got[k] = lax.ppermute(messages[k], 'wave', moves)]
    all_to_all x1 -> x0, blocking collectives: 93.1 us -> none  [per_device(): lax.all_to_all(synthesized, 'wave', split_axis=1, concat_axis=2, tiled=True)]
    all_to_all x1 -> x0, waiting for transfers between devices: 75 us -> none  [per_device(): lax.all_to_all(weighted, 'wave', split_axis=2, concat_axis=1, tiled=True)]
    all_gather x1 -> x0, waiting for transfers between devices: 53.6 us -> none  [per_device(): full_forced = lax.all_gather(forced, 'pole', axis=0, tiled=True)]
    ppermute x0 -> x34, starting transfers between devices: none -> 43.9 us  [the longest x28 41 us: between_chips(): got[k] = lax.ppermute(messages[k], 'wave', moves)]
    dot_general x2 -> x0, matrix products: 22.7 us -> none  [the longest x1 12.3 us: per_device(): jnp.einsum('rsen,snj->rjse', advanced, legendre, preferred_element_type=j...]
    convert_element_type x1 -> x0, local copies, waits for them, and re-layouts: 10.6 us -> none  [per_device(): synthesized = jnp.einsum('rsen,snj->rjse', advanced, legendre, preferred_...]
  transfers between devices with their start and end apart: 3 -> 35, of which waited for: 2 -> 14; matrix products, arithmetic and copies ran while one was open for 8% -> 3% of each run, Pallas kernels for 0% -> 52%
where the time goes in v3:
time: 436 us; the launch traced here: 434 us
  Pallas kernels  242 us (56%)
  waiting for transfers between devices  114 us (26%)
  starting transfers between devices  43.9 us (10%)
  local copies, waits for them, and re-layouts  16.2 us (4%)
  between operations  13.8 us (3%)
    pallas_call x2, Pallas kernels, pair(): pl.pallas_call(pair_kernel, out_shape=[jax.ShapeDtypeStruct((CORES,) + ow...  122 us
    ppermute x28, waiting for transfers between devices, between_chips(): got[k] = lax.ppermute(messages[k], 'wave', moves)  90 us
    pallas_call x2, Pallas kernels, pick(): pl.pallas_call(pick_kernel, out_shape=jax.ShapeDtypeStruct(shape, BF16),...  61.9 us
    ppermute x28, starting transfers between devices, between_chips(): got[k] = lax.ppermute(messages[k], 'wave', moves)  41 us
    ppermute x2, waiting for transfers between devices, per_device(): other = lax.ppermute(forced, 'pole', [(0, 1), (1, 0)])  19.5 us
    pallas_call x2, Pallas kernels, synthesise(): pl.pallas_call(functools.partial(synthesise_kernel, chips, lats), out_sha...  17.3 us
    pallas_call x2, Pallas kernels, analyse(): pl.pallas_call(functools.partial(analyse_kernel, slot, low, chips, lats),...  15.8 us
    pallas_call x2, Pallas kernels, weigh(): pl.pallas_call(functools.partial(weigh_kernel, slot, local_slots), out_sh...  13.9 us
  transfers between devices with their start and end apart: 35, of which 14 were waited for; matrix products, arithmetic and copies ran while one was open for 3% of the time, Pallas kernels for 52%

profile of v3, /device:TPU:8, one launch (start us, length us, event | category | flops | bytes accessed | tf_op | source)
XLA Modules:
  0.0 434.1 jit_solution(9813268965267555707)
XLA Ops:
  6.5 1.4 broadcast_in_dim.2.gauss_ref
  7.9 6.9 %weigh.2 = (bf16[2,3,160,128]{3,2,1,0:T(8,128)(2,1)}, bf16[2,3,160,128]{3,2,1,0:T(8,128)(2,1)}, bf16[2,3,160,128]{3,2,1,0:T(8,128)(2,1)}, bf16[2,3,160,128]{3,2,...) custom-call(s32[1]{0:T(128)} %bitcast.me_ref, ...), custom_call_target="tpu_custom_call" | custom-call | flops 1966080 | bytes 5898240 | tf_op jit(solution)/shard_map/weigh/pallas_call | solution.py:37
  14.9 1.6 collective-permute-start
  16.9 1.6 collective-permute-start.2
  18.4 2.6 collective-permute-start.3
  21.0 1.3 collective-permute-start.4
  22.3 0.8 collective-permute-done.rest_1_
  23.1 1.6 collective-permute-start.5
  24.7 8.5 %collective-permute-done.1.rest_2_ = bf16[2,3,160,128]{3,2,1,0:T(8,128)(2,1)S(1)} collective-permute-done((bf16[2,3,160,128]{3,2,1,0:T(8,128)(2,1)}, bf16[2,3,160,128]{3,2,1,0:T(8,128)(2,1)S(1)}, u32[]{:S(2)}, u32[]{:S(2)}) %collective-permute-start.1) | collective-permute-done | bytes 245792 | tf_op jit(solution)/shard_map/ppermute | solution.py:298
  33.4 7.0 %weigh.3 = (bf16[2,3,160,128]{3,2,1,0:T(8,128)(2,1)}, bf16[2,3,160,128]{3,2,1,0:T(8,128)(2,1)}, bf16[2,3,160,128]{3,2,1,0:T(8,128)(2,1)}, bf16[2,3,160,128]{3,2,...) custom-call(s32[1]{0:T(128)} %bitcast.me_ref, ...), custom_call_target="tpu_custom_call" | custom-call | flops 1966080 | bytes 5898240 | tf_op jit(solution)/shard_map/weigh/pallas_call | solution.py:37
  40.3 2.5 collective-permute-start.17
  42.9 3.3 collective-permute-start.18
  46.1 8.1 %collective-permute-done.4.rest_5_ = bf16[2,3,160,128]{3,2,1,0:T(8,128)(2,1)} collective-permute-done((bf16[2,3,160,128]{3,2,1,0:T(8,128)(2,1)}, bf16[2,3,160,128]{3,2,1,0:T(8,128)(2,1)}, u32[]{:S(2)}, u32[]{:S(2)}) %collective-permute-start.4) | collective-permute-done | bytes 245792 | tf_op jit(solution)/shard_map/ppermute | solution.py:298
  54.2 1.8 collective-permute-start.19
  56.0 3.5 reshape.15
  59.5 4.1 dot_general.8
  63.6 2.6 collective-permute-start.20
  66.2 7.5 %collective-permute-done.6.rest_7_ = bf16[2,3,160,128]{3,2,1,0:T(8,128)(2,1)} collective-permute-done((bf16[2,3,160,128]{3,2,1,0:T(8,128)(2,1)}, bf16[2,3,160,128]{3,2,1,0:T(8,128)(2,1)}, u32[]{:S(2)}, u32[]{:S(2)}) %collective-permute-start.6) | collective-permute-done | bytes 245792 | tf_op jit(solution)/shard_map/ppermute | solution.py:298
  73.7 31.0 %pick.2 = bf16[8,3,160,128]{3,2,1,0:T(8,128)(2,1)} custom-call(s32[1]{0:T(128)} %bitcast.me_ref, bf16[2,3,160,128]{3,2,1,0:T(8,128)(2,1)} %get-tuple-element.41.rest_0_, bf16[2,3,160,128]{3,2,1,0:T(8,128)(2,1)} %copy-done.2, bf16[2,3,160,128]{3,2,1,0:T(8,128)(2,1)} %copy-done.3, bf16[2,3,160,128]{3,2,1,0:T(8,128)(2,1)} %collective-permute-done.2.rest_3_, ...), custom_call_target="tpu_custom_call" | custom-call | bytes 1966080 | tf_op jit(solution)/shard_map/pick/pallas_call | solution.py:73
  104.6 3.3 collective-permute-start.22
  108.2 1.3 fusion
  109.5 4.7 %collective-permute-done.22.rest_6_ = bf16[2,3,160,128]{3,2,1,0:T(8,128)(2,1)S(1)} collective-permute-done((bf16[2,3,160,128]{3,2,1,0:T(8,128)(2,1)S(1)}, bf16[2,3,160,128]{3,2,1,0:T(8,128)(2,1)S(1)}, u32[]{:S(2)}, u32[]{:S(2)}) %collective-permute-start.22) | collective-permute-done | bytes 245792 | tf_op jit(solution)/shard_map/ppermute | solution.py:298
  114.2 6.0 %collective-permute-done.23.rest_7_ = bf16[2,3,160,128]{3,2,1,0:T(8,128)(2,1)S(1)} collective-permute-done((bf16[2,3,160,128]{3,2,1,0:T(8,128)(2,1)S(1)}, bf16[2,3,160,128]{3,2,1,0:T(8,128)(2,1)S(1)}, u32[]{:S(2)}, u32[]{:S(2)}) %collective-permute-start.23) | collective-permute-done | bytes 245792 | tf_op jit(solution)/shard_map/ppermute | solution.py:298
  120.3 0.7 copy-done.7
  121.0 31.0 %pick.3 = bf16[8,3,160,128]{3,2,1,0:T(8,128)(2,1)} custom-call(s32[1]{0:T(128)} %bitcast.me_ref, bf16[2,3,160,128]{3,2,1,0:T(8,128)(2,1)} %get-tuple-element.59.rest_0_, bf16[2,3,160,128]{3,2,1,0:T(8,128)(2,1)} %collective-permute-done.17.rest_1_, bf16[2,3,160,128]{3,2,1,0:T(8,128)(2,1)} %collective-permute-done.18.rest_2_, ...), custom_call_target="tpu_custom_call" | custom-call | bytes 1966080 | tf_op jit(solution)/shard_map/pick/pallas_call | solution.py:73
  152.3 0.7 copy.32
  153.0 0.7 fusion.2
  153.7 9.1 %analyse.2.own_ref = bf16[3,128,1280]{2,1,0:T(8,128)(2,1)} custom-call(s32[1]{0:T(128)} %bitcast.me_ref, s32[2]{0:T(128)} %wave_ref.3, bf16[2,1280,2560]{2,1,0:T(8,128)(2,1)} %table_ref.7, bf16[3,2,128,1280]{3,2,1,0:T(8,128)(2,1)} %state_ref.3, bf16[2,3,160,128]{3,2,1,0:T(8,128)(2,1)} %get-tuple-element.41.rest_0_, bf16[2,3,160,128]{3,2,1,0:T(8,128)(2,1)} %copy-done.2, ...), custom_call_target="tpu_custom_call" | custom-call | flops 2516582400 | bytes 6553600 | tf_op jit(solution)/shard_map/analyse/pallas_call | solution.py:158
  162.8 1.6 collective-permute-start.8
  164.4 1.0 copy-done.9
  165.4 6.7 %analyse.3.own_ref = bf16[3,128,640]{2,1,0:T(8,128)(2,1)} custom-call(s32[1]{0:T(128)} %bitcast.me_ref, s32[2]{0:T(128)} %wave_ref.3, bf16[2,1280,2560]{2,1,0:T(8,128)(2,1)} %table_ref.7, bf16[3,2,128,1280]{3,2,1,0:T(8,128)(2,1)} %state_ref.3, bf16[2,3,160,128]{3,2,1,0:T(8,128)(2,1)} %get-tuple-element.59.rest_0_, ...), custom_call_target="tpu_custom_call" | custom-call | flops 1258291200 | bytes 6553600 | tf_op jit(solution)/shard_map/analyse/pallas_call | solution.py:158
  172.2 0.6 collective-permute-start.25
  172.7 4.9 %all-reduce.3.cloned.1.call-done = (f32[3,3,2,1280]{3,2,1,0:T(2,128)}, f32[3,3,2,1280]{3,2,1,0:T(2,128)}) async-done(((f32[3,3,2,1280]{3,2,1,0:T(2,128)}, f32[3,3,2,1280]{3,2,1,0:T(2,128)}), (f32[3,3,2,1280]{3,2,1,0:T(2,128)}, f32[3,3,2,1280]{3,2,1,0:T(2,128)})) %all-reduce.3.cloned.1.call-update) | async-done | bytes 184336 | tf_op jit(solution)/shard_map/psum | solution.py:327
  177.6 0.9 broadcast_multiply_fusion
  178.5 1.0 pad_maximum_fusion
  179.6 0.6 copy.33
  180.2 19.5 %collective-permute-done.25.other_ref = bf16[3,128,640]{2,1,0:T(8,128)(2,1)S(1)} collective-permute-done((bf16[3,128,640]{2,1,0:T(8,128)(2,1)}, bf16[3,128,640]{2,1,0:T(8,128)(2,1)S(1)}, u32[]{:S(2)}, u32[]{:S(2)}) %collective-permute-start.25) | collective-permute-done | bytes 491552 | tf_op jit(solution)/shard_map/ppermute | solution.py:335
  199.7 0.8 copy-done.12
  200.5 7.6 %synthesise.3 = (bf16[8,3,160,128]{3,2,1,0:T(8,128)(2,1)}, bf16[8,3,160,128]{3,2,1,0:T(8,128)(2,1)}) custom-call(s32[1]{0:T(128)} %bitcast.me_ref, f32[18,640]{1,0:T(8,128)} %bitcast.26, bf16[3,128,640]{2,1,0:T(8,128)(2,1)} %analyse.3.own_ref, bf16[3,128,640]{2,1,0:T(8,128)(2,1)} %copy-done.12, bf16[2,1280,2560]{2,1,0:T(8,128)(2,1)} %table_ref.7), custom_call_target="tpu_custom_call" | custom-call | flops 1258291200 | bytes 3276800 | tf_op jit(solution)/shard_map/synthesise/pallas_call | solution.py:227
  208.3 0.7 copy.31
  209.0 1.0 copy-done.8
  209.9 9.7 %synthesise.2 = (bf16[8,3,160,128]{3,2,1,0:T(8,128)(2,1)}, bf16[8,3,160,128]{3,2,1,0:T(8,128)(2,1)}) custom-call(s32[1]{0:T(128)} %bitcast.me_ref, f32[18,1280]{1,0:T(8,128)} %bitcast.24, bf16[3,128,1280]{2,1,0:T(8,128)(2,1)} %analyse.2.own_ref, bf16[3,128,1280]{2,1,0:T(8,128)(2,1)} %copy-done.8, bf16[2,1280,2560]{2,1,0:T(8,128)(2,1)} %table_ref.7), custom_call_target="tpu_custom_call" | custom-call | flops 2516582400 | bytes 6553600 | tf_op jit(solution)/shard_map/synthesise/pallas_call | solution.py:227
  219.6 0.6 collective-permute-start.9
  220.2 0.9 copy-done.11
  221.1 60.8 %pair.3 = (bf16[2,3,160,128]{3,2,1,0:T(8,128)(2,1)}, bf16[2,3,160,128]{3,2,1,0:T(8,128)(2,1)}, bf16[2,3,160,128]{3,2,1,0:T(8,128)(2,1)}, bf16[2,3,160,128]{3,2,1...) custom-call(bf16[8,3,160,128]{3,2,1,0:T(8,128)(2,1)} %get-tuple-elem, ...), custom_call_target="tpu_custom_call" | custom-call | bytes 3932160 | tf_op jit(solution)/shard_map/pair/pallas_call | solution.py:97
  282.0 1.2 collective-permute-start.27
  283.5 2.0 collective-permute-start.29
  285.5 1.4 collective-permute-start.30
  286.9 2.2 collective-permute-start.31
  289.1 60.8 %pair.2 = (bf16[2,3,160,128]{3,2,1,0:T(8,128)(2,1)}, bf16[2,3,160,128]{3,2,1,0:T(8,128)(2,1)}, bf16[2,3,160,128]{3,2,1,0:T(8,128)(2,1)}, bf16[2,3,160,128]{3,2,1...) custom-call(bf16[8,3,160,128]{3,2,1,0:T(8,128)(2,1)} %get-tuple-elem, ...), custom_call_target="tpu_custom_call" | custom-call | bytes 3932160 | tf_op jit(solution)/shard_map/pair/pallas_call | solution.py:97
  349.9 2.1 collective-permute-start.32
  352.3 1.3 collective-permute-start.10
  353.5 2.5 collective-permute-start.11
  356.0 0.8 collective-permute-start.12
  356.8 11.9 %collective-permute-done.32.rest_14_ = bf16[2,3,160,128]{3,2,1,0:T(8,128)(2,1)S(1)} collective-permute-done((bf16[2,3,160,128]{3,2,1,0:T(8,128)(2,1)}, bf16[2,3,160,128]{3,2,1,0:T(8,128)(2,1)S(1)}, u32[]{:S(2)}, u32[]{:S(2)}) %collective-permute-start.32) | collective-permute-done | bytes 245792 | tf_op jit(solution)/shard_map/ppermute | solution.py:298
  368.7 18.4 %collective-permute-done.33.rest_15_ = bf16[2,3,160,128]{3,2,1,0:T(8,128)(2,1)S(1)} collective-permute-done((bf16[2,3,160,128]{3,2,1,0:T(8,128)(2,1)}, bf16[2,3,160,128]{3,2,1,0:T(8,128)(2,1)S(1)}, u32[]{:S(2)}, u32[]{:S(2)}) %collective-permute-start.33) | collective-permute-done | bytes 245792 | tf_op jit(solution)/shard_map/ppermute | solution.py:298
  387.1 2.7 collective-permute-start.15
  389.8 1.5 collective-permute-start.16
  391.3 1.2 collective-permute-done.13.rest_4_
  392.5 13.2 %collective-permute-done.14.rest_5_ = bf16[2,3,160,128]{3,2,1,0:T(8,128)(2,1)S(1)} collective-permute-done((bf16[2,3,160,128]{3,2,1,0:T(8,128)(2,1)}, bf16[2,3,160,128]{3,2,1,0:T(8,128)(2,1)S(1)}, u32[]{:S(2)}, u32[]{:S(2)}) %collective-permute-start.14) | collective-permute-done | bytes 245792 | tf_op jit(solution)/shard_map/ppermute | solution.py:298
  405.7 6.3 %collective-permute-done.15.rest_6_ = bf16[2,3,160,128]{3,2,1,0:T(8,128)(2,1)S(1)} collective-permute-done((bf16[2,3,160,128]{3,2,1,0:T(8,128)(2,1)}, bf16[2,3,160,128]{3,2,1,0:T(8,128)(2,1)S(1)}, u32[]{:S(2)}, u32[]{:S(2)}) %collective-permute-start.15) | collective-permute-done | bytes 245792 | tf_op jit(solution)/shard_map/ppermute | solution.py:298
  412.0 3.5 collective-permute-done.16.rest_7_
  415.5 0.6 copy-done.26
  416.1 11.1 %assemble.1 = bf16[3,160,32,128]{3,2,1,0:T(8,128)(2,1)} custom-call(s32[1]{0:T(128)} %bitcast.me_ref, bf16[2,3,160,128]{3,2,1,0:T(8,128)(2,1)} %get-tuple-element.51.rest_0_, bf16[2,3,160,128]{3,2,1,0:T(8,128)(2,1)} %copy-done.20, bf16[2,3,160,128]{3,2,1,0:T(8,128)(2,1)} %copy-done.21, bf16[2,3,160,128]{3,2,1,0:T(8,128)(2,1)} %copy-done.22, ...), custom_call_target="tpu_custom_call" | custom-call | tf_op jit(solution)/shard_map/assemble/pallas_call | solution.py:275
  (93 shorter events, 2.2 us)
Async XLA Ops:
  6.5 101.7 %copy-start = (f32[32,2]{0,1:T(2,128)S(1)}, f32[32,2]{0,1:T(2,128)}, u32[]{:S(2)}) copy-start(f32[32,2]{0,1:T(2,128)} %param.12) | copy-start | bytes 772
  6.5 171.1 %all-reduce.3.cloned.1.call-start = ((), (), s32[]{:S(2)}) async-start(), calls=%async_computation | async-start | bytes 368640 | tf_op jit(solution)/shard_map/psum | solution.py:327
  14.9 41.1 %copy-start.1 = (bf16[32,18,2,1280]{3,2,1,0:T(2,128)(2,1)S(1)}, bf16[32,18,2,1280]{3,2,1,0:T(2,128)(2,1)}, u32[]{:S(2)}) copy-start(bf16[32,18,2,1280]{3,2,1,0:T(2,128)(2,1)} %param.11) | copy-start | bytes 8847364
  14.9 8.3 %collective-permute-start = (bf16[2,3,160,128]{3,2,1,0:T(8,128)(2,1)}, bf16[2,3,160,128]{3,2,1,0:T(8,128)(2,1)S(1)}, u32[]{:S(2)}, u32[]{:S(2)}) collective-permute-start(bf16[2,3,160,128]{3,2,1,0:T(8,128)(2,1)} %get-tuple-element.42), channel_id=1, source_target_pairs={{0,2},{1,3},{2,0},{3,1},{4,6},{5,7},{6,4},{7,5},{8,10},{9,11},{10,... | collective-permute-start | bytes 737288 | tf_op jit(solution)/shard_map/ppermute | solution.py:298
  16.4 16.7 %collective-permute-start.1 = (bf16[2,3,160,128]{3,2,1,0:T(8,128)(2,1)}, bf16[2,3,160,128]{3,2,1,0:T(8,128)(2,1)S(1)}, u32[]{:S(2)}, u32[]{:S(2)}) collective-permute-start(bf16[2,3,160,128]{3,2,1,0:T(8,128)(2,1)} %get-tuple-element.43), channel_id=1, source_target_pairs={{0,4},{1,5},{2,6},{3,7},{4,0},{5,1},{6,2},{7,3},{8,12},{9,13},{10,... | collective-permute-start | bytes 737288 | tf_op jit(solution)/shard_map/ppermute | solution.py:298
  16.9 23.4 %collective-permute-start.2 = (bf16[2,3,160,128]{3,2,1,0:T(8,128)(2,1)}, bf16[2,3,160,128]{3,2,1,0:T(8,128)(2,1)}, u32[]{:S(2)}, u32[]{:S(2)}) collective-permute-start(bf16[2,3,160,128]{3,2,1,0:T(8,128)(2,1)} %get-tuple-element.44), channel_id=1, source_target_pairs={{0,6},{1,7},{2,4},{3,5},{4,2},{5,3},{6,0},{7,1},{8,14},{9,15},{10,... | collective-permute-start | bytes 737288 | tf_op jit(solution)/shard_map/ppermute | solution.py:298
  18.4 24.4 %collective-permute-start.3 = (bf16[2,3,160,128]{3,2,1,0:T(8,128)(2,1)}, bf16[2,3,160,128]{3,2,1,0:T(8,128)(2,1)}, u32[]{:S(2)}, u32[]{:S(2)}) collective-permute-start(bf16[2,3,160,128]{3,2,1,0:T(8,128)(2,1)} %get-tuple-element.45), channel_id=1, source_target_pairs={{0,8},{1,9},{2,10},{3,11},{4,12},{5,13},{6,14},{7,15},{8,0},{9,1},... | collective-permute-start | bytes 737288 | tf_op jit(solution)/shard_map/ppermute | solution.py:298
  21.0 33.1 %collective-permute-start.4 = (bf16[2,3,160,128]{3,2,1,0:T(8,128)(2,1)}, bf16[2,3,160,128]{3,2,1,0:T(8,128)(2,1)}, u32[]{:S(2)}, u32[]{:S(2)}) collective-permute-start(bf16[2,3,160,128]{3,2,1,0:T(8,128)(2,1)} %get-tuple-element.46), channel_id=1, source_target_pairs={{0,10},{1,11},{2,8},{3,9},{4,14},{5,15},{6,12},{7,13},{8,2},{9,3},... | collective-permute-start | bytes 737288 | tf_op jit(solution)/shard_map/ppermute | solution.py:298
  23.1 36.3 %copy-start.2 = (bf16[2,3,160,128]{3,2,1,0:T(8,128)(2,1)}, bf16[2,3,160,128]{3,2,1,0:T(8,128)(2,1)S(1)}, u32[]{:S(2)}) copy-start(bf16[2,3,160,128]{3,2,1,0:T(8,128)(2,1)S(1)} %collective-permute-done.rest_1_) | copy-start | bytes 737284
  23.1 40.4 %collective-permute-start.5 = (bf16[2,3,160,128]{3,2,1,0:T(8,128)(2,1)}, bf16[2,3,160,128]{3,2,1,0:T(8,128)(2,1)}, u32[]{:S(2)}, u32[]{:S(2)}) collective-permute-start(bf16[2,3,160,128]{3,2,1,0:T(8,128)(2,1)} %get-tuple-element.47), channel_id=1, source_target_pairs={{0,12},{1,13},{2,14},{3,15},{4,8},{5,9},{6,10},{7,11},{8,4},{9,5},... | collective-permute-start | bytes 737288 | tf_op jit(solution)/shard_map/ppermute | solution.py:298
  33.2 26.3 %copy-start.3 = (bf16[2,3,160,128]{3,2,1,0:T(8,128)(2,1)}, bf16[2,3,160,128]{3,2,1,0:T(8,128)(2,1)S(1)}, u32[]{:S(2)}) copy-start(bf16[2,3,160,128]{3,2,1,0:T(8,128)(2,1)S(1)} %collective-permute-done.1.rest_2_) | copy-start | bytes 737284
  33.2 40.5 %collective-permute-start.6 = (bf16[2,3,160,128]{3,2,1,0:T(8,128)(2,1)}, bf16[2,3,160,128]{3,2,1,0:T(8,128)(2,1)}, u32[]{:S(2)}, u32[]{:S(2)}) collective-permute-start(bf16[2,3,160,128]{3,2,1,0:T(8,128)(2,1)} %get-tuple-element.48), channel_id=1, source_target_pairs={{0,14},{1,15},{2,12},{3,13},{4,10},{5,11},{6,8},{7,9},{8,6},{9,7},... | collective-permute-start | bytes 737288 | tf_op jit(solution)/shard_map/ppermute | solution.py:298
  40.3 64.3 %collective-permute-start.17 = (bf16[2,3,160,128]{3,2,1,0:T(8,128)(2,1)}, bf16[2,3,160,128]{3,2,1,0:T(8,128)(2,1)}, u32[]{:S(2)}, u32[]{:S(2)}) collective-permute-start(bf16[2,3,160,128]{3,2,1,0:T(8,128)(2,1)} %get-tuple-element.60), channel_id=1, source_target_pairs={{0,2},{1,3},{2,0},{3,1},{4,6},{5,7},{6,4},{7,5},{8,10},{9,11},{10,... | collective-permute-start | bytes 737288 | tf_op jit(solution)/shard_map/ppermute | solution.py:298
  42.9 65.0 %collective-permute-start.18 = (bf16[2,3,160,128]{3,2,1,0:T(8,128)(2,1)}, bf16[2,3,160,128]{3,2,1,0:T(8,128)(2,1)}, u32[]{:S(2)}, u32[]{:S(2)}) collective-permute-start(bf16[2,3,160,128]{3,2,1,0:T(8,128)(2,1)} %get-tuple-element.61), channel_id=1, source_target_pairs={{0,4},{1,5},{2,6},{3,7},{4,0},{5,1},{6,2},{7,3},{8,12},{9,13},{10,... | collective-permute-start | bytes 737288 | tf_op jit(solution)/shard_map/ppermute | solution.py:298
  54.2 54.0 %collective-permute-start.19 = (bf16[2,3,160,128]{3,2,1,0:T(8,128)(2,1)}, bf16[2,3,160,128]{3,2,1,0:T(8,128)(2,1)}, u32[]{:S(2)}, u32[]{:S(2)}) collective-permute-start(bf16[2,3,160,128]{3,2,1,0:T(8,128)(2,1)} %get-tuple-element.62), channel_id=1, source_target_pairs={{0,6},{1,7},{2,4},{3,5},{4,2},{5,3},{6,0},{7,1},{8,14},{9,15},{10,... | collective-permute-start | bytes 737288 | tf_op jit(solution)/shard_map/ppermute | solution.py:298
  59.5 4.1 copy-start.30
  59.5 14.2 %copy-start.29 = (bf16[2,3,160,128]{3,2,1,0:T(8,128)(2,1)S(1)}, bf16[2,3,160,128]{3,2,1,0:T(8,128)(2,1)}, u32[]{:S(2)}) copy-start(bf16[2,3,160,128]{3,2,1,0:T(8,128)(2,1)} %get-tuple-element.64) | copy-start | bytes 737284
  63.6 41.1 %copy-start.28 = (bf16[2,3,160,128]{3,2,1,0:T(8,128)(2,1)S(1)}, bf16[2,3,160,128]{3,2,1,0:T(8,128)(2,1)}, u32[]{:S(2)}) copy-start(bf16[2,3,160,128]{3,2,1,0:T(8,128)(2,1)} %get-tuple-element.65) | copy-start | bytes 737284
  63.6 44.3 %copy-start.27 = (bf16[2,3,160,128]{3,2,1,0:T(8,128)(2,1)S(1)}, bf16[2,3,160,128]{3,2,1,0:T(8,128)(2,1)}, u32[]{:S(2)}) copy-start(bf16[2,3,160,128]{3,2,1,0:T(8,128)(2,1)} %get-tuple-element.66) | copy-start | bytes 737284
  63.6 45.9 %collective-permute-start.20 = (bf16[2,3,160,128]{3,2,1,0:T(8,128)(2,1)S(1)}, bf16[2,3,160,128]{3,2,1,0:T(8,128)(2,1)S(1)}, u32[]{:S(2)}, u32[]{:S(2)}) collective-permute-start(bf16[2,3,160,128]{3,2,1,0:T(8,128)(2,1)S(1)} %copy-done.30), channel_id=1, source_target_pairs={{0,8},{1,9},{2,10},{3,11},{4,12},{5,13},{6,14},{7,15},{8,0},{9,1},... | collective-permute-start | bytes 737288 | tf_op jit(solution)/shard_map/ppermute | solution.py:298
  73.7 35.8 %collective-permute-start.21 = (bf16[2,3,160,128]{3,2,1,0:T(8,128)(2,1)S(1)}, bf16[2,3,160,128]{3,2,1,0:T(8,128)(2,1)S(1)}, u32[]{:S(2)}, u32[]{:S(2)}) collective-permute-start(bf16[2,3,160,128]{3,2,1,0:T(8,128)(2,1)S(1)} %copy-done.29), channel_id=1, source_target_pairs={{0,10},{1,11},{2,8},{3,9},{4,14},{5,15},{6,12},{7,13},{8,2},{9,3},... | collective-permute-start | bytes 737288 | tf_op jit(solution)/shard_map/ppermute | solution.py:298
  104.6 9.6 %collective-permute-start.22 = (bf16[2,3,160,128]{3,2,1,0:T(8,128)(2,1)S(1)}, bf16[2,3,160,128]{3,2,1,0:T(8,128)(2,1)S(1)}, u32[]{:S(2)}, u32[]{:S(2)}) collective-permute-start(bf16[2,3,160,128]{3,2,1,0:T(8,128)(2,1)S(1)} %copy-done.28), channel_id=1, source_target_pairs={{0,12},{1,13},{2,14},{3,15},{4,8},{5,9},{6,10},{7,11},{8,4},{9,5},... | collective-permute-start | bytes 737288 | tf_op jit(solution)/shard_map/ppermute | solution.py:298
  107.9 12.4 %collective-permute-start.23 = (bf16[2,3,160,128]{3,2,1,0:T(8,128)(2,1)S(1)}, bf16[2,3,160,128]{3,2,1,0:T(8,128)(2,1)S(1)}, u32[]{:S(2)}, u32[]{:S(2)}) collective-permute-start(bf16[2,3,160,128]{3,2,1,0:T(8,128)(2,1)S(1)} %copy-done.27), channel_id=1, source_target_pairs={{0,14},{1,15},{2,12},{3,13},{4,10},{5,11},{6,8},{7,9},{8,6},{9,7},... | collective-permute-start | bytes 737288 | tf_op jit(solution)/shard_map/ppermute | solution.py:298
  108.2 45.5 %collective-permute-start.7 = (bf16[8,3,160,128]{3,2,1,0:T(8,128)(2,1)}, bf16[8,3,160,128]{3,2,1,0:T(8,128)(2,1)}, u32[]{:S(2)}, u32[]{:S(2)}) collective-permute-start(bf16[8,3,160,128]{3,2,1,0:T(8,128)(2,1)} %pick.2), channel_id=1, source_target_pairs={{0,1},{1,0},{2,3},{3,2},{4,5},{5,4},{6,7},{7,6},{8,9},{9,8},{10,11... | collective-permute-start | bytes 2949128 | tf_op jit(solution)/shard_map/ppermute | solution.py:303
  109.5 10.8 %copy-start.4 = (bf16[2,3,160,128]{3,2,1,0:T(8,128)(2,1)}, bf16[2,3,160,128]{3,2,1,0:T(8,128)(2,1)S(1)}, u32[]{:S(2)}) copy-start(bf16[2,3,160,128]{3,2,1,0:T(8,128)(2,1)S(1)} %collective-permute-done.20.rest_4_) | copy-start | bytes 737284
  109.5 10.8 %copy-start.5 = (bf16[2,3,160,128]{3,2,1,0:T(8,128)(2,1)}, bf16[2,3,160,128]{3,2,1,0:T(8,128)(2,1)S(1)}, u32[]{:S(2)}) copy-start(bf16[2,3,160,128]{3,2,1,0:T(8,128)(2,1)S(1)} %collective-permute-done.21.rest_5_) | copy-start | bytes 737284
  114.2 6.0 %copy-start.6 = (bf16[2,3,160,128]{3,2,1,0:T(8,128)(2,1)}, bf16[2,3,160,128]{3,2,1,0:T(8,128)(2,1)S(1)}, u32[]{:S(2)}) copy-start(bf16[2,3,160,128]{3,2,1,0:T(8,128)(2,1)S(1)} %collective-permute-done.22.rest_6_) | copy-start | bytes 737284
  151.9 12.5 %collective-permute-start.24 = (bf16[8,3,160,128]{3,2,1,0:T(8,128)(2,1)}, bf16[8,3,160,128]{3,2,1,0:T(8,128)(2,1)S(1)}, u32[]{:S(2)}, u32[]{:S(2)}) collective-permute-start(bf16[8,3,160,128]{3,2,1,0:T(8,128)(2,1)} %pick.3), channel_id=1, source_target_pairs={{0,1},{1,0},{2,3},{3,2},{4,5},{5,4},{6,7},{7,6},{8,9},{9,8},{10,11... | collective-permute-start | bytes 2949128 | tf_op jit(solution)/shard_map/ppermute | solution.py:303
  162.8 46.1 %collective-permute-start.8 = (bf16[3,128,1280]{2,1,0:T(8,128)(2,1)}, bf16[3,128,1280]{2,1,0:T(8,128)(2,1)S(1)}, u32[]{:S(2)}, u32[]{:S(2)}) collective-permute-start(bf16[3,128,1280]{2,1,0:T(8,128)(2,1)} %analyse.2.own_ref), channel_id=1, source_target_pairs={{0,16},{16,0},{1,17},{17,1},{2,18},{18,2},{3,19},{19,3},{4,20},{20... | collective-permute-start | bytes 2949128 | tf_op jit(solution)/shard_map/ppermute | solution.py:335
  164.4 1.0 copy-start.9
  172.2 27.5 %collective-permute-start.25 = (bf16[3,128,640]{2,1,0:T(8,128)(2,1)}, bf16[3,128,640]{2,1,0:T(8,128)(2,1)S(1)}, u32[]{:S(2)}, u32[]{:S(2)}) collective-permute-start(bf16[3,128,640]{2,1,0:T(8,128)(2,1)} %analyse.3.own_ref), channel_id=1, source_target_pairs={{0,16},{16,0},{1,17},{17,1},{2,18},{18,2},{3,19},{19,3},{4,20},{20... | collective-permute-start | bytes 1474568 | tf_op jit(solution)/shard_map/ppermute | solution.py:335
  199.7 0.8 copy-start.12
  208.1 12.1 %collective-permute-start.26 = (bf16[8,3,160,128]{3,2,1,0:T(8,128)(2,1)}, bf16[8,3,160,128]{3,2,1,0:T(8,128)(2,1)S(1)}, u32[]{:S(2)}, u32[]{:S(2)}) collective-permute-start(bf16[8,3,160,128]{3,2,1,0:T(8,128)(2,1)} %get-tuple-element.68), channel_id=1, source_target_pairs={{0,1},{1,0},{2,3},{3,2},{4,5},{5,4},{6,7},{7,6},{8,9},{9,8},{10,11... | collective-permute-start | bytes 2949128 | tf_op jit(solution)/shard_map/ppermute | solution.py:303
  209.0 1.0 copy-start.8
  219.6 67.2 %collective-permute-start.9 = (bf16[8,3,160,128]{3,2,1,0:T(8,128)(2,1)}, bf16[8,3,160,128]{3,2,1,0:T(8,128)(2,1)S(1)}, u32[]{:S(2)}, u32[]{:S(2)}) collective-permute-start(bf16[8,3,160,128]{3,2,1,0:T(8,128)(2,1)} %get-tuple-element.50), channel_id=1, source_target_pairs={{0,1},{1,0},{2,3},{3,2},{4,5},{5,4},{6,7},{7,6},{8,9},{9,8},{10,11... | collective-permute-start | bytes 2949128 | tf_op jit(solution)/shard_map/ppermute | solution.py:303
  220.2 0.9 copy-start.11
  282.0 67.9 %collective-permute-start.27 = (bf16[2,3,160,128]{3,2,1,0:T(8,128)(2,1)}, bf16[2,3,160,128]{3,2,1,0:T(8,128)(2,1)S(1)}, u32[]{:S(2)}, u32[]{:S(2)}) collective-permute-start(bf16[2,3,160,128]{3,2,1,0:T(8,128)(2,1)} %get-tuple-element.70), channel_id=1, source_target_pairs={{0,2},{1,3},{2,0},{3,1},{4,6},{5,7},{6,4},{7,5},{8,10},{9,11},{10,... | collective-permute-start | bytes 737288 | tf_op jit(solution)/shard_map/ppermute | solution.py:298
  283.2 68.8 %collective-permute-start.28 = (bf16[2,3,160,128]{3,2,1,0:T(8,128)(2,1)}, bf16[2,3,160,128]{3,2,1,0:T(8,128)(2,1)S(1)}, u32[]{:S(2)}, u32[]{:S(2)}) collective-permute-start(bf16[2,3,160,128]{3,2,1,0:T(8,128)(2,1)} %get-tuple-element.71), channel_id=1, source_target_pairs={{0,4},{1,5},{2,6},{3,7},{4,0},{5,1},{6,2},{7,3},{8,12},{9,13},{10,... | collective-permute-start | bytes 737288 | tf_op jit(solution)/shard_map/ppermute | solution.py:298
  283.5 68.8 %collective-permute-start.29 = (bf16[2,3,160,128]{3,2,1,0:T(8,128)(2,1)}, bf16[2,3,160,128]{3,2,1,0:T(8,128)(2,1)S(1)}, u32[]{:S(2)}, u32[]{:S(2)}) collective-permute-start(bf16[2,3,160,128]{3,2,1,0:T(8,128)(2,1)} %get-tuple-element.72), channel_id=1, source_target_pairs={{0,6},{1,7},{2,4},{3,5},{4,2},{5,3},{6,0},{7,1},{8,14},{9,15},{10,... | collective-permute-start | bytes 737288 | tf_op jit(solution)/shard_map/ppermute | solution.py:298
  285.5 68.0 %collective-permute-start.30 = (bf16[2,3,160,128]{3,2,1,0:T(8,128)(2,1)}, bf16[2,3,160,128]{3,2,1,0:T(8,128)(2,1)S(1)}, u32[]{:S(2)}, u32[]{:S(2)}) collective-permute-start(bf16[2,3,160,128]{3,2,1,0:T(8,128)(2,1)} %get-tuple-element.73), channel_id=1, source_target_pairs={{0,8},{1,9},{2,10},{3,11},{4,12},{5,13},{6,14},{7,15},{8,0},{9,1},... | collective-permute-start | bytes 737288 | tf_op jit(solution)/shard_map/ppermute | solution.py:298
  286.9 2.2 copy-start.10
  286.9 69.2 %collective-permute-start.31 = (bf16[2,3,160,128]{3,2,1,0:T(8,128)(2,1)}, bf16[2,3,160,128]{3,2,1,0:T(8,128)(2,1)S(1)}, u32[]{:S(2)}, u32[]{:S(2)}) collective-permute-start(bf16[2,3,160,128]{3,2,1,0:T(8,128)(2,1)} %get-tuple-element.74), channel_id=1, source_target_pairs={{0,10},{1,11},{2,8},{3,9},{4,14},{5,15},{6,12},{7,13},{8,2},{9,3},... | collective-permute-start | bytes 737288 | tf_op jit(solution)/shard_map/ppermute | solution.py:298
  349.9 65.6 %copy-start.13 = (bf16[2,3,160,128]{3,2,1,0:T(8,128)(2,1)}, bf16[2,3,160,128]{3,2,1,0:T(8,128)(2,1)S(1)}, u32[]{:S(2)}) copy-start(bf16[2,3,160,128]{3,2,1,0:T(8,128)(2,1)S(1)} %collective-permute-done.27.rest_9_) | copy-start | bytes 737284
  349.9 18.9 %collective-permute-start.32 = (bf16[2,3,160,128]{3,2,1,0:T(8,128)(2,1)}, bf16[2,3,160,128]{3,2,1,0:T(8,128)(2,1)S(1)}, u32[]{:S(2)}, u32[]{:S(2)}) collective-permute-start(bf16[2,3,160,128]{3,2,1,0:T(8,128)(2,1)} %get-tuple-element.75), channel_id=1, source_target_pairs={{0,12},{1,13},{2,14},{3,15},{4,8},{5,9},{6,10},{7,11},{8,4},{9,5},... | collective-permute-start | bytes 737288 | tf_op jit(solution)/shard_map/ppermute | solution.py:298
  352.0 63.5 %copy-start.14 = (bf16[2,3,160,128]{3,2,1,0:T(8,128)(2,1)}, bf16[2,3,160,128]{3,2,1,0:T(8,128)(2,1)S(1)}, u32[]{:S(2)}) copy-start(bf16[2,3,160,128]{3,2,1,0:T(8,128)(2,1)S(1)} %collective-permute-done.28.rest_10_) | copy-start | bytes 737284
  352.0 35.1 %collective-permute-start.33 = (bf16[2,3,160,128]{3,2,1,0:T(8,128)(2,1)}, bf16[2,3,160,128]{3,2,1,0:T(8,128)(2,1)S(1)}, u32[]{:S(2)}, u32[]{:S(2)}) collective-permute-start(bf16[2,3,160,128]{3,2,1,0:T(8,128)(2,1)} %get-tuple-element.76), channel_id=1, source_target_pairs={{0,14},{1,15},{2,12},{3,13},{4,10},{5,11},{6,8},{7,9},{8,6},{9,7},... | collective-permute-start | bytes 737288 | tf_op jit(solution)/shard_map/ppermute | solution.py:298
  352.3 63.2 %copy-start.15 = (bf16[2,3,160,128]{3,2,1,0:T(8,128)(2,1)}, bf16[2,3,160,128]{3,2,1,0:T(8,128)(2,1)S(1)}, u32[]{:S(2)}) copy-start(bf16[2,3,160,128]{3,2,1,0:T(8,128)(2,1)S(1)} %collective-permute-done.29.rest_11_) | copy-start | bytes 737284
  352.3 34.8 %collective-permute-start.10 = (bf16[2,3,160,128]{3,2,1,0:T(8,128)(2,1)}, bf16[2,3,160,128]{3,2,1,0:T(8,128)(2,1)S(1)}, u32[]{:S(2)}, u32[]{:S(2)}) collective-permute-start(bf16[2,3,160,128]{3,2,1,0:T(8,128)(2,1)} %get-tuple-element.52), channel_id=1, source_target_pairs={{0,2},{1,3},{2,0},{3,1},{4,6},{5,7},{6,4},{7,5},{8,10},{9,11},{10,... | collective-permute-start | bytes 737288 | tf_op jit(solution)/shard_map/ppermute | solution.py:298
  353.5 61.9 %copy-start.16 = (bf16[2,3,160,128]{3,2,1,0:T(8,128)(2,1)}, bf16[2,3,160,128]{3,2,1,0:T(8,128)(2,1)S(1)}, u32[]{:S(2)}) copy-start(bf16[2,3,160,128]{3,2,1,0:T(8,128)(2,1)S(1)} %collective-permute-done.30.rest_12_) | copy-start | bytes 737284
  353.5 36.2 %collective-permute-start.11 = (bf16[2,3,160,128]{3,2,1,0:T(8,128)(2,1)}, bf16[2,3,160,128]{3,2,1,0:T(8,128)(2,1)S(1)}, u32[]{:S(2)}, u32[]{:S(2)}) collective-permute-start(bf16[2,3,160,128]{3,2,1,0:T(8,128)(2,1)} %get-tuple-element.53), channel_id=1, source_target_pairs={{0,4},{1,5},{2,6},{3,7},{4,0},{5,1},{6,2},{7,3},{8,12},{9,13},{10,... | collective-permute-start | bytes 737288 | tf_op jit(solution)/shard_map/ppermute | solution.py:298
  356.0 59.4 %copy-start.17 = (bf16[2,3,160,128]{3,2,1,0:T(8,128)(2,1)}, bf16[2,3,160,128]{3,2,1,0:T(8,128)(2,1)S(1)}, u32[]{:S(2)}) copy-start(bf16[2,3,160,128]{3,2,1,0:T(8,128)(2,1)S(1)} %collective-permute-done.31.rest_13_) | copy-start | bytes 737284
  356.0 35.2 %collective-permute-start.12 = (bf16[2,3,160,128]{3,2,1,0:T(8,128)(2,1)}, bf16[2,3,160,128]{3,2,1,0:T(8,128)(2,1)S(1)}, u32[]{:S(2)}, u32[]{:S(2)}) collective-permute-start(bf16[2,3,160,128]{3,2,1,0:T(8,128)(2,1)} %get-tuple-element.54), channel_id=1, source_target_pairs={{0,6},{1,7},{2,4},{3,5},{4,2},{5,3},{6,0},{7,1},{8,14},{9,15},{10,... | collective-permute-start | bytes 737288 | tf_op jit(solution)/shard_map/ppermute | solution.py:298
  368.7 46.7 %copy-start.18 = (bf16[2,3,160,128]{3,2,1,0:T(8,128)(2,1)}, bf16[2,3,160,128]{3,2,1,0:T(8,128)(2,1)S(1)}, u32[]{:S(2)}) copy-start(bf16[2,3,160,128]{3,2,1,0:T(8,128)(2,1)S(1)} %collective-permute-done.32.rest_14_) | copy-start | bytes 737284
  368.7 23.8 %collective-permute-start.13 = (bf16[2,3,160,128]{3,2,1,0:T(8,128)(2,1)}, bf16[2,3,160,128]{3,2,1,0:T(8,128)(2,1)S(1)}, u32[]{:S(2)}, u32[]{:S(2)}) collective-permute-start(bf16[2,3,160,128]{3,2,1,0:T(8,128)(2,1)} %get-tuple-element.55), channel_id=1, source_target_pairs={{0,8},{1,9},{2,10},{3,11},{4,12},{5,13},{6,14},{7,15},{8,0},{9,1},... | collective-permute-start | bytes 737288 | tf_op jit(solution)/shard_map/ppermute | solution.py:298
  387.1 28.4 %copy-start.19 = (bf16[2,3,160,128]{3,2,1,0:T(8,128)(2,1)}, bf16[2,3,160,128]{3,2,1,0:T(8,128)(2,1)S(1)}, u32[]{:S(2)}) copy-start(bf16[2,3,160,128]{3,2,1,0:T(8,128)(2,1)S(1)} %collective-permute-done.33.rest_15_) | copy-start | bytes 737284
  387.1 18.6 %collective-permute-start.14 = (bf16[2,3,160,128]{3,2,1,0:T(8,128)(2,1)}, bf16[2,3,160,128]{3,2,1,0:T(8,128)(2,1)S(1)}, u32[]{:S(2)}, u32[]{:S(2)}) collective-permute-start(bf16[2,3,160,128]{3,2,1,0:T(8,128)(2,1)} %get-tuple-element.56), channel_id=1, source_target_pairs={{0,10},{1,11},{2,8},{3,9},{4,14},{5,15},{6,12},{7,13},{8,2},{9,3},... | collective-permute-start | bytes 737288 | tf_op jit(solution)/shard_map/ppermute | solution.py:298
  387.1 28.4 %copy-start.20 = (bf16[2,3,160,128]{3,2,1,0:T(8,128)(2,1)}, bf16[2,3,160,128]{3,2,1,0:T(8,128)(2,1)S(1)}, u32[]{:S(2)}) copy-start(bf16[2,3,160,128]{3,2,1,0:T(8,128)(2,1)S(1)} %collective-permute-done.10.rest_1_) | copy-start | bytes 737284
  387.1 24.8 %collective-permute-start.15 = (bf16[2,3,160,128]{3,2,1,0:T(8,128)(2,1)}, bf16[2,3,160,128]{3,2,1,0:T(8,128)(2,1)S(1)}, u32[]{:S(2)}, u32[]{:S(2)}) collective-permute-start(bf16[2,3,160,128]{3,2,1,0:T(8,128)(2,1)} %get-tuple-element.57), channel_id=1, source_target_pairs={{0,12},{1,13},{2,14},{3,15},{4,8},{5,9},{6,10},{7,11},{8,4},{9,5},... | collective-permute-start | bytes 737288 | tf_op jit(solution)/shard_map/ppermute | solution.py:298
  389.8 25.7 %copy-start.21 = (bf16[2,3,160,128]{3,2,1,0:T(8,128)(2,1)}, bf16[2,3,160,128]{3,2,1,0:T(8,128)(2,1)S(1)}, u32[]{:S(2)}) copy-start(bf16[2,3,160,128]{3,2,1,0:T(8,128)(2,1)S(1)} %collective-permute-done.11.rest_2_) | copy-start | bytes 737284
  389.8 25.6 %collective-permute-start.16 = (bf16[2,3,160,128]{3,2,1,0:T(8,128)(2,1)}, bf16[2,3,160,128]{3,2,1,0:T(8,128)(2,1)S(1)}, u32[]{:S(2)}, u32[]{:S(2)}) collective-permute-start(bf16[2,3,160,128]{3,2,1,0:T(8,128)(2,1)} %get-tuple-element.58), channel_id=1, source_target_pairs={{0,14},{1,15},{2,12},{3,13},{4,10},{5,11},{6,8},{7,9},{8,6},{9,7},... | collective-permute-start | bytes 737288 | tf_op jit(solution)/shard_map/ppermute | solution.py:298
  391.3 24.2 %copy-start.22 = (bf16[2,3,160,128]{3,2,1,0:T(8,128)(2,1)}, bf16[2,3,160,128]{3,2,1,0:T(8,128)(2,1)S(1)}, u32[]{:S(2)}) copy-start(bf16[2,3,160,128]{3,2,1,0:T(8,128)(2,1)S(1)} %collective-permute-done.12.rest_3_) | copy-start | bytes 737284
  392.5 23.0 %copy-start.23 = (bf16[2,3,160,128]{3,2,1,0:T(8,128)(2,1)}, bf16[2,3,160,128]{3,2,1,0:T(8,128)(2,1)S(1)}, u32[]{:S(2)}) copy-start(bf16[2,3,160,128]{3,2,1,0:T(8,128)(2,1)S(1)} %collective-permute-done.13.rest_4_) | copy-start | bytes 737284
  405.7 9.8 %copy-start.24 = (bf16[2,3,160,128]{3,2,1,0:T(8,128)(2,1)}, bf16[2,3,160,128]{3,2,1,0:T(8,128)(2,1)S(1)}, u32[]{:S(2)}) copy-start(bf16[2,3,160,128]{3,2,1,0:T(8,128)(2,1)S(1)} %collective-permute-done.14.rest_5_) | copy-start | bytes 737284
  411.9 3.6 copy-start.25
  (2 other events, 1.4 us)
Sparse Core Ops, SparseCore 0:
  153.8 23.7 all-reduce.2

commit v4 on v0

v4 whole, which is shorter than its diff:
```python
import functools
import math

import jax
import jax.numpy as jnp
from jax import lax
from jax.experimental import pallas as pl
from jax.experimental.pallas import tpu as pltpu
from jax.sharding import PartitionSpec as P

BF16 = jnp.bfloat16
F32 = jnp.float32
CORES = 2
PERMUTED = (1,)
ANYWHERE = pl.BlockSpec(memory_space=pl.ANY)
IN_SMEM = pl.BlockSpec(memory_space=pltpu.SMEM)
TOKEN = jax.ShapeDtypeStruct((8, 128), F32)


def call(kernel, name, flops, size, mib=40, **kwargs):
    return pl.pallas_call(
        kernel,
        name=name,
        compiler_params=pltpu.CompilerParams(vmem_limit_bytes=mib * 1024 * 1024),
        cost_estimate=pl.CostEstimate(flops=int(flops), bytes_accessed=int(size), transcendentals=0),
        **kwargs,
    )


def run_copies(copies):
    for copy in copies:
        copy.start()
    for copy in copies:
        copy.wait()


def owner_of(me, k, other):
    core = me % CORES
    return ((me // CORES) ^ k) * CORES + (CORES - 1 - core if other else core)


def swap_matrix(rows, columns, picked):
    width = rows * columns
    target = lax.broadcasted_iota(jnp.int32, (len(picked) * rows, width), 0)
    source = lax.broadcasted_iota(jnp.int32, (len(picked) * rows, width), 1)
    step = picked[1] - picked[0] if len(picked) > 1 else 1
    column = (target // rows) * step + picked[0]
    return (source == (target % rows) * columns + column).astype(BF16)


def weigh_kernel(slot, local_slots, permuted, me_ref, gauss_ref, tendency_ref, *rest):
    _, lats, slots, members = tendency_ref.shape
    outs, blocks = (rest[:-1], rest[-1]) if permuted else (rest, None)
    depth, breadth = math.gcd(lats, 16), 16
    matrix = swap_matrix(depth, breadth, range(slot, breadth, local_slots))
    owners = breadth // local_slots
    for j in range(0, lats, depth):
        scale = gauss_ref[j : j + depth, :]
        for s in range(0, slots, 2 * breadth):
            halves = [
                tendency_ref[0, j : j + depth, s + h : s + h + breadth, :].reshape(depth * breadth, members)
                for h in (0, breadth)
            ]
            turned = jnp.dot(matrix, jnp.concatenate(halves, axis=1), preferred_element_type=F32)
            for h in range(2):
                for i in range(owners):
                    value = turned[i * depth : (i + 1) * depth, h * members : (h + 1) * members]
                    owner = (s + h * breadth) // local_slots + i
                    value = (value * scale).astype(BF16)
                    if permuted:
                        blocks[owner, j : j + depth, :] = value
                    else:
                        outs[0][owner, 0, j : j + depth, :] = value
    if permuted:
        for k, out in enumerate(outs):
            for core in range(CORES):
                out[core, 0] = blocks[((me_ref[0] // CORES) ^ k) * CORES + core]


def weigh(tendency, gauss, me, slot, local_slots, permuted):
    rows, lats, slots, members = tendency.shape
    owners = slots // local_slots
    count, chips = (CORES, owners // CORES) if permuted else (owners, 1)
    piece = pl.BlockSpec((count, 1, lats, members), lambda r, m: (0, r, 0, 0))
    return call(
        functools.partial(weigh_kernel, slot, local_slots, permuted),
        "weigh",
        2 * 128 * tendency.size,
        3 * tendency.size,
        out_shape=[jax.ShapeDtypeStruct((count, rows, lats, members), BF16)] * chips,
        grid_spec=pltpu.PrefetchScalarGridSpec(
            num_scalar_prefetch=1,
            grid=(rows,),
            in_specs=[
                pl.BlockSpec((lats, members), lambda r, m: (0, 0)),
                pl.BlockSpec((1, lats, slots, members), lambda r, m: (r, 0, 0, 0)),
            ],
            out_specs=[piece] * chips,
            scratch_shapes=[pltpu.VMEM((owners, lats, members), BF16)] if permuted else [],
        ),
    )(me, gauss, tendency)


def pick_kernel(me_ref, *rest):
    ins, out = rest[:-1], rest[-1]
    for k, ref in enumerate(ins):
        out[k] = ref[0]


def pick(messages, me):
    _, rows, lats, members = messages[0].shape
    chips = len(messages)
    shape = (chips, rows, lats, members)
    return call(
        pick_kernel,
        "pick",
        0,
        4 * math.prod(shape),
        out_shape=jax.ShapeDtypeStruct(shape, BF16),
        grid_spec=pltpu.PrefetchScalarGridSpec(
            num_scalar_prefetch=1,
            grid=(rows,),
            in_specs=[
                pl.BlockSpec((1, 1, lats, members), lambda r, m: (CORES - 1 - m[0] % CORES, r, 0, 0))
            ]
            * chips,
            out_specs=pl.BlockSpec((chips, 1, lats, members), lambda r, m: (0, r, 0, 0)),
        ),
    )(me, *messages)


def pair_kernel(mate_ref, *rest):
    chips = mate_ref.shape[0]
    outs, sems = rest[chips:-1], rest[-1]
    run_copies([pltpu.make_async_copy(mate_ref.at[k], out.at[1], sems.at[k]) for k, out in enumerate(outs)])


def pair(messages, mate):
    chips = len(messages)
    return call(
        pair_kernel,
        "pair",
        0,
        4 * mate.size,
        out_shape=[jax.ShapeDtypeStruct(m.shape, m.dtype) for m in messages],
        in_specs=[pl.BlockSpec(mate.shape, lambda: (0, 0, 0, 0))] + [ANYWHERE] * chips,
        out_specs=[ANYWHERE] * chips,
        scratch_shapes=[pltpu.SemaphoreType.DMA((chips,))],
        input_output_aliases={k + 1: k for k in range(chips)},
    )(mate, *messages)


def analyse_kernel(slot, low, count, me_ref, wave_ref, token_ref, table_ref, state_ref, *rest):
    blocks, out, grid, sems = rest[:count], rest[count], rest[count + 1], rest[count + 2]
    rows, members, _ = out.shape
    owners, lats, _ = grid.shape
    width = table_ref.shape[1]
    step = pl.program_id(0)

    @pl.when(step == 0)
    def _():
        copies = []
        for r in range(rows):
            lanes = pl.ds(r * members, members)
            if count == 1:
                copies.append(pltpu.make_async_copy(blocks[0].at[:, r], grid.at[:, :, lanes], sems.at[0, r]))
            for k in range(count - 1):
                for other in range(CORES):
                    target = grid.at[owner_of(me_ref[0], k, other), :, lanes]
                    source = blocks[-1].at[k, r] if other else blocks[k].at[me_ref[0] % CORES, r]
                    copies.append(pltpu.make_async_copy(source, target, sems.at[CORES * k + other, r]))
        run_copies(copies)

    field = grid[...].reshape(owners * lats, rows * members)
    sums = jnp.dot(table_ref[0], field, preferred_element_type=F32)
    degree = lax.broadcasted_iota(jnp.int32, (members, width), 1) + (low + step * width)
    live = degree >= wave_ref[slot]
    for r in range(rows):
        total = state_ref[r, 0].astype(F32) + sums[:, r * members : (r + 1) * members].T
        out[r] = jnp.where(live, total, 0.0).astype(BF16)


def analyse(blocks, table, state, wave, me, token, slot, low, width):
    _, rows, lats, members = blocks[0].shape
    nspec, nlat = table.shape[1:]
    owners = nlat // lats
    first = low // width
    if lats % 16:
        blocks = [lay_in_place(blocks, me[0], owners)]
        blocks[0] = jnp.transpose(blocks[0], (1, 0, 2, 3)).reshape(1, rows, nlat, members)
        owners, lats = 1, nlat
    return call(
        functools.partial(analyse_kernel, slot, low, len(blocks)),
        "analyse",
        2 * (nspec - low) * nlat * rows * members,
        2 * (nspec - low) * nlat,
        out_shape=jax.ShapeDtypeStruct((rows, members, nspec - low), BF16),
        grid=((nspec - low) // width,),
        in_specs=[
            IN_SMEM,
            IN_SMEM,
            ANYWHERE,
            pl.BlockSpec((1, width, nlat), lambda i: (slot, first + i, 0)),
            pl.BlockSpec((rows, 1, members, width), lambda i: (0, slot, 0, first + i)),
        ]
        + [ANYWHERE] * len(blocks),
        out_specs=pl.BlockSpec((rows, members, width), lambda i: (0, 0, i)),
        scratch_shapes=[
            pltpu.VMEM((owners, lats, rows * members), BF16),
            pltpu.SemaphoreType.DMA((owners, rows)),
        ],
    )(me, wave, token, table, state, *blocks)


def lay_in_place(blocks, here, owners):
    if len(blocks) == 1:
        return blocks[0]
    own = [lax.dynamic_index_in_dim(m, here % CORES, 0, keepdims=False) for m in blocks[:-1]]
    both = jnp.stack([jnp.stack(own), blocks[-1]], axis=1).reshape((owners,) + own[0].shape)
    order = jnp.arange(owners, dtype=jnp.int32)
    order = ((order // CORES) ^ (here // CORES)) * CORES + (order % CORES ^ here % CORES)
    return jnp.take(both, order, axis=0)


def synthesise_kernel(permuted, me_ref, matrix_ref, own_ref, other_ref, table_ref, *rest):
    rows, members, _ = own_ref.shape
    width = table_ref.shape[2]
    step = pl.program_id(0)
    outs, token_ref, mixed = rest[: permuted + 1], rest[permuted + 1], rest[permuted + 2]

    @pl.when(step == 0)
    def _():
        token_ref[...] = jnp.zeros_like(token_ref)
        for f in range(rows):
            total = 0.0
            for g in range(rows):
                total = total + matrix_ref[f * rows + g : f * rows + g + 1, :] * own_ref[g].astype(F32)
                line = rows * rows + f * rows + g
                total = total + matrix_ref[line : line + 1, :] * other_ref[g].astype(F32)
            mixed[f * members : (f + 1) * members, :] = total.astype(BF16)

    sums = jnp.dot(mixed[...], table_ref[0], preferred_element_type=F32)
    grid = rest[permuted + 3] if permuted else outs[0]
    lats = grid.shape[2]
    each = width // lats
    for r in range(rows):
        turned = sums[r * members : (r + 1) * members, :].T.reshape(each, lats, members).astype(BF16)
        if permuted:
            grid[pl.ds(step * each, each), r] = turned
        else:
            grid[:, r] = turned

    if permuted:
        sems = rest[-1]

        @pl.when(step == pl.num_programs(0) - 1)
        def _():
            copies = []
            for k in range(permuted):
                for other in range(CORES):
                    source = grid.at[owner_of(me_ref[0], k, other)]
                    target = outs[-1].at[k] if other else outs[k].at[0]
                    copies.append(pltpu.make_async_copy(source, target, sems.at[k, other]))
            run_copies(copies)


def synthesise(matrix, own, other, table, me, slot, low, lats, permuted):
    rows, members, count = own.shape
    nlat = table.shape[2]
    owners = nlat // lats
    width = math.lcm(lats, 128)
    chips = owners // CORES if permuted else 0
    whole = pl.BlockSpec((rows, members, count), lambda j: (0, 0, 0))
    shapes = [jax.ShapeDtypeStruct((owners, rows, lats, members), BF16)]
    specs = [pl.BlockSpec((width // lats, rows, lats, members), lambda j: (j, 0, 0, 0))]
    scratch = [pltpu.VMEM((rows * members, count), BF16)]
    if permuted:
        shapes = [jax.ShapeDtypeStruct((CORES, rows, lats, members), BF16)] * chips
        shapes += [jax.ShapeDtypeStruct((chips, rows, lats, members), BF16)]
        specs = [ANYWHERE] * (chips + 1)
        scratch += [pltpu.VMEM((owners, rows, lats, members), BF16), pltpu.SemaphoreType.DMA((chips, CORES))]
    return call(
        functools.partial(synthesise_kernel, chips),
        "synthesise",
        2 * count * nlat * rows * members,
        2 * count * nlat,
        out_shape=shapes + [TOKEN],
        grid=(nlat // width,),
        in_specs=[
            IN_SMEM,
            pl.BlockSpec(matrix.shape, lambda j: (0, 0)),
            whole,
            whole,
            pl.BlockSpec((1, count, width), lambda j: (slot, low // count, j)),
        ],
        out_specs=specs + [pl.BlockSpec(TOKEN.shape, lambda j: (0, 0))],
        scratch_shapes=scratch,
    )(me, matrix, own, other, table)


def assemble_kernel(counts, me_ref, *rest):
    ins, out, blocks = rest[: sum(counts)], rest[sum(counts)], rest[sum(counts) + 1 :]
    _, lats, slots, members = out.shape
    local_slots = len(counts)
    views, used, spare = [], 0, 0
    for count in counts:
        refs = ins[used : used + count]
        used += count
        if count == 1:
            views.append(lambda owner, j, ref=refs[0]: ref[owner, 0, j, :])
            continue
        for k, ref in enumerate(refs):
            for other in range(CORES):
                blocks[spare][owner_of(me_ref[0], k, other)] = ref[other, 0]
        views.append(lambda owner, j, ref=blocks[spare]: ref[owner, j, :])
        spare += 1
    depth, breadth = math.gcd(lats, 16), 16
    matrix = swap_matrix(breadth, depth, range(depth))
    for start in range(0, lats, depth):
        j = slice(start, start + depth)
        for s in range(0, slots, 2 * breadth):
            halves = [
                jnp.concatenate(
                    [views[i % local_slots](i // local_slots, j) for i in range(s + h, s + h + breadth)], axis=0
                )
                for h in (0, breadth)
            ]
            turned = jnp.dot(matrix, jnp.concatenate(halves, axis=1), preferred_element_type=F32).astype(BF16)
            for h in range(2):
                value = turned[:, h * members : (h + 1) * members].reshape(depth, breadth, members)
                out[0, j, s + h * breadth : s + (h + 1) * breadth, :] = value


def assemble(pieces, me, lats):
    local_slots = len(pieces)
    _, rows, _, members = pieces[0][0].shape
    owners = max(len(p) * p[0].shape[0] for p in pieces)
    slots = local_slots * owners
    flat = [block for slot in pieces for block in slot]
    moved = sum(len(p) > 1 for p in pieces)
    return call(
        functools.partial(assemble_kernel, [len(p) for p in pieces]),
        "assemble",
        2 * 256 * rows * lats * slots * members,
        4 * rows * lats * slots * members,
        out_shape=jax.ShapeDtypeStruct((rows, lats, slots, members), BF16),
        grid_spec=pltpu.PrefetchScalarGridSpec(
            num_scalar_prefetch=1,
            grid=(rows,),
            in_specs=[
                pl.BlockSpec((block.shape[0], 1, lats, members), lambda r, m: (0, r, 0, 0)) for block in flat
            ],
            out_specs=pl.BlockSpec((1, lats, slots, members), lambda r, m: (r, 0, 0, 0)),
            scratch_shapes=[pltpu.VMEM((owners, lats, members), BF16)] * moved,
        ),
    )(me, *flat)


def between_chips(messages):
    chips = len(messages)
    got = [messages[0]]
    for k in range(1, chips):
        got.append(lax.ppermute(messages[k], "wave", [(d, d ^ (k * CORES)) for d in range(chips * CORES)]))
    return got


def between_cores(blocks, owners):
    return lax.ppermute(blocks, "wave", [(d, d ^ 1) for d in range(owners)])


def to_all(blocks):
    return lax.all_to_all(blocks, "wave", split_axis=0, concat_axis=0, tiled=True)


def per_device(
    tendency, spectral_state, legendre, gauss_weights, block_inverses, pole_coeffs, wavenumbers
):
    rows, lats, slots, members = tendency.shape
    local_slots, nspec, nlat = legendre.shape
    owners = slots // local_slots
    me = lax.axis_index("wave").astype(jnp.int32).reshape(1)
    pole_index = lax.axis_index("pole")
    orientation = (2 * pole_index - 1).astype(F32)
    gauss = jnp.broadcast_to(gauss_weights[:, None], (lats, members))
    received = []
    for slot in range(local_slots):
        permuted = slot in PERMUTED
        blocks = weigh(tendency, gauss, me, slot, local_slots, permuted)
        received.append(between_chips(blocks) if permuted else [to_all(blocks[0])])

    local_pairs = block_inverses.shape[0]
    flat_inverse = block_inverses.reshape(local_pairs, -1).astype(F32)
    weighted_sums = jnp.dot(pole_coeffs.T, flat_inverse, precision=lax.Precision.HIGHEST)
    weighted_sums = weighted_sums.reshape(2, 2, rows, rows, local_slots, nspec)
    real_matrix = weighted_sums[0, 0] - weighted_sums[1, 1]
    imag_matrix = weighted_sums[0, 1] + weighted_sums[1, 0]
    real_matrix, imag_matrix = lax.psum((real_matrix, imag_matrix), "pole")
    matrices = jnp.concatenate([real_matrix, orientation * imag_matrix]).reshape(2 * rows * rows, local_slots, nspec)

    sent = []
    token = jnp.zeros(TOKEN.shape, TOKEN.dtype)
    for slot in range(local_slots):
        permuted = slot in PERMUTED
        low = nspec // 2 if slot % 2 else 0
        blocks = received[slot]
        if permuted:
            blocks = blocks + [between_cores(pick(blocks, me), owners)]
        forced = analyse(blocks, legendre, spectral_state, wavenumbers, me, token, slot, low, nspec // 2)
        other = lax.ppermute(forced, "pole", [(0, 1), (1, 0)])
        matrix = matrices[:, slot, low:]
        *blocks, token = synthesise(matrix, forced, other, legendre, me, slot, low, lats, permuted)
        if permuted:
            sent.append(between_chips(pair(blocks[:-1], between_cores(blocks[-1], owners))))
        else:
            sent.append([to_all(blocks[0])])
    return assemble(sent, me, lats)


def solution(mesh):
    in_specs = (
        P("pole", "wave", None, None),
        P("pole", "wave", None, None),
        P("wave", None, None),
        P("wave"),
        P("pole", None, "wave", None),
        P("pole", None),
        P("wave"),
    )
    out_specs = P("pole", "wave", None, None)
    return jax.shard_map(
        per_device, mesh=mesh, in_specs=in_specs, out_specs=out_specs, check_vma=False
    )
```

time: 306 us -> 299 us (0.977)
  blocking collectives: 93.1 us -> 0 us
  waiting for transfers between devices: 129 us -> 179 us
  Pallas kernels: 0 us -> 35.3 us
  starting transfers between devices: 6.79 us -> 40.9 us
  matrix products: 24 us -> 3.11 us
  other arithmetic: 9.56 us -> 2.84 us
  local copies, waits for them, and re-layouts: 27.6 us -> 23.5 us
    ppermute x0 -> x18, waiting for transfers between devices: none -> 124 us  [the longest x14 107 us: between_chips(): lax.ppermute(messages[k], 'wave', [(d, d ^ k * CORES) for d in range(chip...]
    all_to_all x1 -> x0, blocking collectives: 93.1 us -> none  [per_device(): lax.all_to_all(synthesized, 'wave', split_axis=1, concat_axis=2, tiled=True)]
    all_gather x1 -> x0, waiting for transfers between devices: 53.6 us -> none  [per_device(): full_forced = lax.all_gather(forced, 'pole', axis=0, tiled=True)]
    all_to_all x1 -> x2, waiting for transfers between devices: 75 us -> 29.3 us  [to_all(): lax.all_to_all(blocks, 'wave', split_axis=0, concat_axis=0, tiled=True)]
    pallas_call x0 -> x9, Pallas kernels: none -> 35.3 us  [the longest x2 15.8 us: synthesise(): call(functools.partial(synthesise_kernel, chips), 'synthesise', 2 * count...]
    ppermute x0 -> x18, starting transfers between devices: none -> 28.4 us  [the longest x14 25.3 us: between_chips(): lax.ppermute(messages[k], 'wave', [(d, d ^ k * CORES) for d in range(chip...]
    psum x1, waiting for transfers between devices: 0.02 us -> 25.5 us  [per_device(): real_matrix, imag_matrix = lax.psum((real_matrix, imag_matrix), 'pole')]
    dot_general x2 -> x0, matrix products: 22.7 us -> none  [the longest x1 12.3 us: per_device(): jnp.einsum('rsen,snj->rjse', advanced, legendre, preferred_element_type=j...]
  transfers between devices with their start and end apart: 3 -> 21, of which waited for: 2 -> 18; matrix products, arithmetic and copies ran while one was open for 8% -> 6% of each run, Pallas kernels for 0% -> 6%
where the time goes in v4:
time: 299 us; the launch traced here: 298 us
  waiting for transfers between devices  179 us (60%)
  starting transfers between devices  40.9 us (14%)
  Pallas kernels  35.3 us (12%)
  local copies, waits for them, and re-layouts  23.5 us (8%)
  between operations  13.6 us (5%)
  matrix products  3.11 us (1%)
    ppermute x14, waiting for transfers between devices, between_chips(): lax.ppermute(messages[k], 'wave', [(d, d ^ k * CORES) for d in range(chip...  107 us
    all_to_all x2, waiting for transfers between devices, to_all(): lax.all_to_all(blocks, 'wave', split_axis=0, concat_axis=0, tiled=True)  29.3 us
    psum x1, waiting for transfers between devices, per_device(): real_matrix, imag_matrix = lax.psum((real_matrix, imag_matrix), 'pole')  25.5 us
    ppermute x14, starting transfers between devices, between_chips(): lax.ppermute(messages[k], 'wave', [(d, d ^ k * CORES) for d in range(chip...  25.3 us
    pallas_call x2, Pallas kernels, synthesise(): call(functools.partial(synthesise_kernel, chips), 'synthesise', 2 * count...  15.8 us
    all_to_all x2, starting transfers between devices, to_all(): lax.all_to_all(blocks, 'wave', split_axis=0, concat_axis=0, tiled=True)  12.5 us
    unnamed x27, local copies, waits for them, and re-layouts  12.3 us
    ppermute x2, waiting for transfers between devices, per_device(): other = lax.ppermute(forced, 'pole', [(0, 1), (1, 0)])  11.9 us
  transfers between devices with their start and end apart: 21, of which 18 were waited for; matrix products, arithmetic and copies ran while one was open for 6% of the time, Pallas kernels for 6%

profile of v4, /device:TPU:8, one launch (start us, length us, event | category | flops | bytes accessed | tf_op | source)
XLA Modules:
  0.0 298.1 jit_solution(12607874516779980478)
XLA Ops:
  6.5 0.8 broadcast_in_dim.10.gauss_ref
  7.3 2.1 copy-done.1
  9.4 1.2 weigh.2
  10.6 1.3 copy-done.3
  11.9 6.3 %all-to-all-start = ((bf16[16,3,160,128]{3,2,1,0:T(8,128)(2,1)}), bf16[16,3,160,128]{3,2,1,0:T(8,128)(2,1)S(1)}, u32[]{:S(2)}, u32[]{:S(2)}) async-start(bf16[16,3,160,128]{3,2,1,0:T(8,128)(2,1)} %copy-done.3), calls=%async_computation | async-start | bytes 3932160 | tf_op jit(solution)/shard_map/all_to_all | solution.py:372
  18.3 5.2 %reshape.15 = bf16[32,46080]{1,0:T(8,128)(2,1)} reshape(bf16[32,18,2,1280]{3,2,1,0:T(2,128)(2,1)} %param.11) | data formatting | bytes 5898240 | tf_op jit(solution)/shard_map/reshape | solution.py:392
  23.4 5.2 %dot_general.8 = bf16[2,3,3,2,1280,32]{4,3,2,1,0,5:T(2,128)(2,1)} reshape(bf16[46080,32]{0,1:T(8,128)(2,1)} %bitcast.23) | data formatting | bytes 5898240 | tf_op jit(solution)/shard_map/dot_general | solution.py:393
  28.6 3.1 %fusion = f32[2,2,3,3,2,1280]{5,0,4,3,2,1:T(2,128)S(1)} fusion(bf16[2,3,3,2,1280,32]{4,3,2,1,0,5:T(2,128)(2,1)} %dot_general.8, f32[32,2]{0,1:T(2,128)S(1)} %copy-done), kind=kOutput, calls=%fused_computation | convolution fusion | flops 35389440 | bytes 3318016 | tf_op jit(solution)/shard_map/dot_general | solution.py:393
  31.7 0.2 fusion.4
  31.9 29.3 %all-to-all-done.rest_0_ = bf16[16,3,160,128]{3,2,1,0:T(8,128)(2,1)S(1)} async-done(((bf16[16,3,160,128]{3,2,1,0:T(8,128)(2,1)}), bf16[16,3,160,128]{3,2,1,0:T(8,128)(2,1)S(1)}, u32[]{:S(2)}, u32[]{:S(2)}) %all-to-all-start) | async-done | bytes 1966112 | tf_op jit(solution)/shard_map/all_to_all | solution.py:372
  61.3 1.5 copy-done.4
  62.8 6.8 %analyse.2.own_ref = bf16[3,128,1280]{2,1,0:T(8,128)(2,1)S(1)} custom-call(s32[1]{0:T(128)} %bitcast.me_ref, s32[2]{0:T(128)S(1)} %copy-done.11, f32[8,128]{1,0:T(8,128)S(1)} %broadcast_in_dim.4.token_ref, bf16[2,1280,2560]{2,1,0:T(8,128)(2,1)} %table_ref.7, bf16[3,2,128,1280]{3,2,1,0:T(8,128)(2,1)S(1)} %copy-done.4, ...), custom_call_target="tpu_custom_call" | custom-call | flops 2516582400 | bytes 6553600 | tf_op jit(solution)/shard_map/analyse/pallas_call | solution.py:192
  69.7 1.6 collective-permute-start
  71.3 0.7 fusion.2
  72.0 0.7 copy.40
  72.7 25.5 %all-reduce.3.cloned.1.call-done = (f32[3,3,2,1280]{3,2,1,0:T(2,128)}, f32[3,3,2,1280]{3,2,1,0:T(2,128)}) async-done(((f32[3,3,2,1280]{3,2,1,0:T(2,128)}, f32[3,3,2,1280]{3,2,1,0:T(2,128)}), (f32[3,3,2,1280]{3,2,1,0:T(2,128)}, f32[3,3,2,1280]{3,2,1,0:T(2,128)})) %all-reduce.3.cloned.1.call-update) | async-done | bytes 184336 | tf_op jit(solution)/shard_map/psum | solution.py:397
  98.2 0.9 broadcast_multiply_fusion
  99.1 1.0 pad_maximum_fusion
  100.1 0.1 slice.28
  100.2 7.2 %synthesise.2 = (bf16[16,3,160,128]{3,2,1,0:T(8,128)(2,1)S(1)}, f32[8,128]{1,0:T(8,128)S(1)}) custom-call(s32[1]{0:T(128)} %bitcast.me_ref, f32[18,1280]{1,0:T(8,128)S(1)} %bitcast.21, bf16[3,128,1280]{2,1,0:T(8,128)(2,1)S(1)} %analyse.2.own_ref, bf16[3,128,1280]{2,1,0:T(8,128)(2,1)S(1)} %collective-permute-done.other_ref, bf16[2,1280,2560]{2,1,0:T(8,128)(2,1)} %table_ref.7), custom_call_target="tpu_custom_call" | custom-call | flops 2516582400 | bytes 6553600 | tf_op jit(solution)/shard_map/synthesise/pallas_call | solution.py:282
  107.5 1.3 copy-done.6
  108.7 6.2 %all-to-all-start.1 = ((bf16[16,3,160,128]{3,2,1,0:T(8,128)(2,1)}), bf16[16,3,160,128]{3,2,1,0:T(8,128)(2,1)S(1)}, u32[]{:S(2)}, u32[]{:S(2)}) async-start(bf16[16,3,160,128]{3,2,1,0:T(8,128)(2,1)} %copy-done.6), calls=%async_computation.1 | async-start | bytes 3932160 | tf_op jit(solution)/shard_map/all_to_all | solution.py:372
  114.9 2.1 copy-done.2
  117.0 1.4 weigh.3
  118.5 1.5 collective-permute-start.1
  120.0 0.6 collective-permute-start.2
  120.5 1.5 collective-permute-start.3
  122.0 2.4 collective-permute-start.4
  124.4 1.5 collective-permute-start.5
  125.8 5.6 %collective-permute-done.1.rest_1_ = bf16[2,3,160,128]{3,2,1,0:T(8,128)(2,1)S(1)} collective-permute-done((bf16[2,3,160,128]{3,2,1,0:T(8,128)(2,1)S(1)}, bf16[2,3,160,128]{3,2,1,0:T(8,128)(2,1)S(1)}, u32[]{:S(2)}, u32[]{:S(2)}) %collective-permute-start.1) | collective-permute-done | bytes 245792 | tf_op jit(solution)/shard_map/ppermute | solution.py:363
  131.5 4.1 %collective-permute-start.6 = (bf16[2,3,160,128]{3,2,1,0:T(8,128)(2,1)S(1)}, bf16[2,3,160,128]{3,2,1,0:T(8,128)(2,1)S(1)}, u32[]{:S(2)}, u32[]{:S(2)}) collective-permute-start(bf16[2,3,160,128]{3,2,1,0:T(8,128)(2,1)S(1)} %get-tuple-element.40), channel_id=1, source_target_pairs={{0,12},{1,13},{2,14},{3,15},{4,8},{5,9},{6,10},{7,11},{8,4},{9,5},... | collective-permute-start | bytes 737288 | tf_op jit(solution)/shard_map/ppermute | solution.py:363
  135.6 18.2 %collective-permute-done.2.rest_2_ = bf16[2,3,160,128]{3,2,1,0:T(8,128)(2,1)S(1)} collective-permute-done((bf16[2,3,160,128]{3,2,1,0:T(8,128)(2,1)S(1)}, bf16[2,3,160,128]{3,2,1,0:T(8,128)(2,1)S(1)}, u32[]{:S(2)}, u32[]{:S(2)}) %collective-permute-start.2) | collective-permute-done | bytes 245792 | tf_op jit(solution)/shard_map/ppermute | solution.py:363
  153.8 3.8 %collective-permute-start.7 = (bf16[2,3,160,128]{3,2,1,0:T(8,128)(2,1)S(1)}, bf16[2,3,160,128]{3,2,1,0:T(8,128)(2,1)S(1)}, u32[]{:S(2)}, u32[]{:S(2)}) collective-permute-start(bf16[2,3,160,128]{3,2,1,0:T(8,128)(2,1)S(1)} %get-tuple-element.41), channel_id=1, source_target_pairs={{0,14},{1,15},{2,12},{3,13},{4,10},{5,11},{6,8},{7,9},{8,6},{9,7},... | collective-permute-start | bytes 737288 | tf_op jit(solution)/shard_map/ppermute | solution.py:363
  157.7 5.4 %collective-permute-done.3.rest_3_ = bf16[2,3,160,128]{3,2,1,0:T(8,128)(2,1)S(1)} collective-permute-done((bf16[2,3,160,128]{3,2,1,0:T(8,128)(2,1)S(1)}, bf16[2,3,160,128]{3,2,1,0:T(8,128)(2,1)S(1)}, u32[]{:S(2)}, u32[]{:S(2)}) %collective-permute-start.3) | collective-permute-done | bytes 245792 | tf_op jit(solution)/shard_map/ppermute | solution.py:363
  163.1 21.7 %collective-permute-done.4.rest_4_ = bf16[2,3,160,128]{3,2,1,0:T(8,128)(2,1)S(1)} collective-permute-done((bf16[2,3,160,128]{3,2,1,0:T(8,128)(2,1)S(1)}, bf16[2,3,160,128]{3,2,1,0:T(8,128)(2,1)S(1)}, u32[]{:S(2)}, u32[]{:S(2)}) %collective-permute-start.4) | collective-permute-done | bytes 245792 | tf_op jit(solution)/shard_map/ppermute | solution.py:363
  184.8 5.3 %collective-permute-done.5.rest_5_ = bf16[2,3,160,128]{3,2,1,0:T(8,128)(2,1)S(1)} collective-permute-done((bf16[2,3,160,128]{3,2,1,0:T(8,128)(2,1)S(1)}, bf16[2,3,160,128]{3,2,1,0:T(8,128)(2,1)S(1)}, u32[]{:S(2)}, u32[]{:S(2)}) %collective-permute-start.5) | collective-permute-done | bytes 245792 | tf_op jit(solution)/shard_map/ppermute | solution.py:363
  190.1 8.1 %collective-permute-done.6.rest_6_ = bf16[2,3,160,128]{3,2,1,0:T(8,128)(2,1)S(1)} collective-permute-done((bf16[2,3,160,128]{3,2,1,0:T(8,128)(2,1)S(1)}, bf16[2,3,160,128]{3,2,1,0:T(8,128)(2,1)S(1)}, u32[]{:S(2)}, u32[]{:S(2)}) %collective-permute-start.6) | collective-permute-done | bytes 245792 | tf_op jit(solution)/shard_map/ppermute | solution.py:363
  198.2 5.8 %collective-permute-done.7.rest_7_ = bf16[2,3,160,128]{3,2,1,0:T(8,128)(2,1)S(1)} collective-permute-done((bf16[2,3,160,128]{3,2,1,0:T(8,128)(2,1)S(1)}, bf16[2,3,160,128]{3,2,1,0:T(8,128)(2,1)S(1)}, u32[]{:S(2)}, u32[]{:S(2)}) %collective-permute-start.7) | collective-permute-done | bytes 245792 | tf_op jit(solution)/shard_map/ppermute | solution.py:363
  204.0 0.2 pick.1
  204.2 0.1 collective-permute-start.8
  204.3 2.6 collective-permute-done.8.rest_8_
  206.8 4.9 %analyse.3.own_ref = bf16[3,128,640]{2,1,0:T(8,128)(2,1)S(1)} custom-call(s32[1]{0:T(128)} %bitcast.me_ref, s32[2]{0:T(128)S(1)} %copy-done.11, f32[8,128]{1,0:T(8,128)S(1)} %get-tuple-element.33.token_ref, bf16[2,1280,2560]{2,1,0:T(8,128)(2,1)} %table_ref.7, bf16[3,2,128,1280]{3,2,1,0:T(8,128)(2,1)S(1)} %copy-done.5, ...), custom_call_target="tpu_custom_call" | custom-call | flops 1258291200 | bytes 3276800 | tf_op jit(solution)/shard_map/analyse/pallas_call | solution.py:192
  211.7 1.4 collective-permute-start.9
  213.1 11.9 %collective-permute-done.9.other_ref = bf16[3,128,640]{2,1,0:T(8,128)(2,1)S(1)} collective-permute-done((bf16[3,128,640]{2,1,0:T(8,128)(2,1)S(1)}, bf16[3,128,640]{2,1,0:T(8,128)(2,1)S(1)}, u32[]{:S(2)}, u32[]{:S(2)}) %collective-permute-start.9) | collective-permute-done | bytes 491552 | tf_op jit(solution)/shard_map/ppermute | solution.py:409
  225.0 8.6 %synthesise.3 = (bf16[2,3,160,128]{3,2,1,0:T(8,128)(2,1)S(1)}, bf16[2,3,160,128]{3,2,1,0:T(8,128)(2,1)S(1)}, bf16[2,3,160,128]{3,2,1,0:T(8,128)(2,1)S(1)}, bf16[...) custom-call(s32[1]{0:T(128)} %bitcast.me_ref, ...), custom_call_target="tpu_custom_call" | custom-call | flops 1258291200 | bytes 3276800 | tf_op jit(solution)/shard_map/synthesise/pallas_call | solution.py:282
  233.6 0.1 collective-permute-start.10
  233.7 2.6 collective-permute-done.10.mate_ref
  236.2 1.6 pair.1
  237.8 0.5 collective-permute-start.11
  238.3 3.1 %collective-permute-start.13 = (bf16[2,3,160,128]{3,2,1,0:T(8,128)(2,1)S(1)}, bf16[2,3,160,128]{3,2,1,0:T(8,128)(2,1)S(1)}, u32[]{:S(2)}, u32[]{:S(2)}) collective-permute-start(bf16[2,3,160,128]{3,2,1,0:T(8,128)(2,1)S(1)} %get-tuple-element.54), channel_id=1, source_target_pairs={{0,6},{1,7},{2,4},{3,5},{4,2},{5,3},{6,0},{7,1},{8,14},{9,15},{10,... | collective-permute-start | bytes 737288 | tf_op jit(solution)/shard_map/ppermute | solution.py:363
  241.4 2.7 collective-permute-start.15
  244.1 1.7 collective-permute-done.11.rest_2_
  245.9 0.6 collective-permute-start.16
  246.5 6.5 %collective-permute-done.12.rest_3_ = bf16[2,3,160,128]{3,2,1,0:T(8,128)(2,1)S(1)} collective-permute-done((bf16[2,3,160,128]{3,2,1,0:T(8,128)(2,1)S(1)}, bf16[2,3,160,128]{3,2,1,0:T(8,128)(2,1)S(1)}, u32[]{:S(2)}, u32[]{:S(2)}) %collective-permute-start.12) | collective-permute-done | bytes 245792 | tf_op jit(solution)/shard_map/ppermute | solution.py:363
  252.9 3.0 %collective-permute-start.17 = (bf16[2,3,160,128]{3,2,1,0:T(8,128)(2,1)S(1)}, bf16[2,3,160,128]{3,2,1,0:T(8,128)(2,1)S(1)}, u32[]{:S(2)}, u32[]{:S(2)}) collective-permute-start(bf16[2,3,160,128]{3,2,1,0:T(8,128)(2,1)S(1)} %get-tuple-element.58), channel_id=1, source_target_pairs={{0,14},{1,15},{2,12},{3,13},{4,10},{5,11},{6,8},{7,9},{8,6},{9,7},... | collective-permute-start | bytes 737288 | tf_op jit(solution)/shard_map/ppermute | solution.py:363
  256.0 1.4 collective-permute-done.13.rest_4_
  257.4 16.7 %collective-permute-done.15.rest_6_ = bf16[2,3,160,128]{3,2,1,0:T(8,128)(2,1)S(1)} collective-permute-done((bf16[2,3,160,128]{3,2,1,0:T(8,128)(2,1)S(1)}, bf16[2,3,160,128]{3,2,1,0:T(8,128)(2,1)S(1)}, u32[]{:S(2)}, u32[]{:S(2)}) %collective-permute-start.15) | collective-permute-done | bytes 245792 | tf_op jit(solution)/shard_map/ppermute | solution.py:363
  274.1 7.1 %collective-permute-done.16.rest_7_ = bf16[2,3,160,128]{3,2,1,0:T(8,128)(2,1)S(1)} collective-permute-done((bf16[2,3,160,128]{3,2,1,0:T(8,128)(2,1)S(1)}, bf16[2,3,160,128]{3,2,1,0:T(8,128)(2,1)S(1)}, u32[]{:S(2)}, u32[]{:S(2)}) %collective-permute-start.16) | collective-permute-done | bytes 245792 | tf_op jit(solution)/shard_map/ppermute | solution.py:363
  281.3 0.7 copy-done.7
  282.0 3.2 %collective-permute-done.17.rest_8_ = bf16[2,3,160,128]{3,2,1,0:T(8,128)(2,1)S(1)} collective-permute-done((bf16[2,3,160,128]{3,2,1,0:T(8,128)(2,1)S(1)}, bf16[2,3,160,128]{3,2,1,0:T(8,128)(2,1)S(1)}, u32[]{:S(2)}, u32[]{:S(2)}) %collective-permute-start.17) | collective-permute-done | bytes 245792 | tf_op jit(solution)/shard_map/ppermute | solution.py:363
  285.2 0.7 copy-done.9
  285.8 0.9 copy-done.8
  286.8 0.9 copy-done.10
  287.7 3.5 %assemble.1 = bf16[3,160,32,128]{3,2,1,0:T(8,128)(2,1)} custom-call(s32[1]{0:T(128)} %bitcast.me_ref, bf16[16,3,160,128]{3,2,1,0:T(8,128)(2,1)S(1)} %all-to-all-done.1.rest_0_, bf16[2,3,160,128]{3,2,1,0:T(8,128)(2,1)S(1)} %get-tuple-element.51.rest_1_, bf16[2,3,160,128]{3,2,1,0:T(8,128)(2,1)S(1)} %collective-permute-done.11.rest_2_, ...), custom_call_target="tpu_custom_call" | custom-call | flops 1006632960 | bytes 7864320 | tf_op jit(solution)/shard_map/assemble/pallas_call | solution.py:341
  (26 shorter events, 0.2 us)
Async XLA Ops:
  6.5 22.0 %copy-start = (f32[32,2]{0,1:T(2,128)S(1)}, f32[32,2]{0,1:T(2,128)}, u32[]{:S(2)}) copy-start(f32[32,2]{0,1:T(2,128)} %param.12) | copy-start | bytes 772
  7.3 2.1 copy-start.1
  10.6 1.3 copy-start.3
  11.9 49.3 %all-to-all-start = ((bf16[16,3,160,128]{3,2,1,0:T(8,128)(2,1)}), bf16[16,3,160,128]{3,2,1,0:T(8,128)(2,1)S(1)}, u32[]{:S(2)}, u32[]{:S(2)}) async-start(bf16[16,3,160,128]{3,2,1,0:T(8,128)(2,1)} %copy-done.3), calls=%async_computation | async-start | bytes 3932160 | tf_op jit(solution)/shard_map/all_to_all | solution.py:372
  18.2 80.0 %all-reduce.3.cloned.1.call-start = ((), (), s32[]{:S(2)}) async-start(), calls=%async_computation.2 | async-start | bytes 368640 | tf_op jit(solution)/shard_map/psum | solution.py:397
  28.6 32.7 %copy-start.11 = (s32[2]{0:T(128)S(1)}, s32[2]{0:T(128)}, u32[]{:S(2)}) copy-start(s32[2]{0:T(128)} %wave_ref.3) | copy-start | bytes 28
  61.3 1.5 copy-start.4
  69.7 30.5 %collective-permute-start = (bf16[3,128,1280]{2,1,0:T(8,128)(2,1)S(1)}, bf16[3,128,1280]{2,1,0:T(8,128)(2,1)S(1)}, u32[]{:S(2)}, u32[]{:S(2)}) collective-permute-start(bf16[3,128,1280]{2,1,0:T(8,128)(2,1)S(1)} %analyse.2.own_ref), channel_id=1, source_target_pairs={{0,16},{16,0},{1,17},{17,1},{2,18},{18,2},{3,19},{19,3},{4,20},{20... | collective-permute-start | bytes 2949128 | tf_op jit(solution)/shard_map/ppermute | solution.py:409
  107.4 1.3 copy-start.6
  108.7 177.1 %all-to-all-start.1 = ((bf16[16,3,160,128]{3,2,1,0:T(8,128)(2,1)}), bf16[16,3,160,128]{3,2,1,0:T(8,128)(2,1)S(1)}, u32[]{:S(2)}, u32[]{:S(2)}) async-start(bf16[16,3,160,128]{3,2,1,0:T(8,128)(2,1)} %copy-done.6), calls=%async_computation.1 | async-start | bytes 3932160 | tf_op jit(solution)/shard_map/all_to_all | solution.py:372
  114.9 2.1 copy-start.2
  117.0 89.8 %copy-start.5 = (bf16[3,2,128,1280]{3,2,1,0:T(8,128)(2,1)S(1)}, bf16[3,2,128,1280]{3,2,1,0:T(8,128)(2,1)}, u32[]{:S(2)}) copy-start(bf16[3,2,128,1280]{3,2,1,0:T(8,128)(2,1)} %state_ref.3) | copy-start | bytes 5898244
  118.5 13.0 %collective-permute-start.1 = (bf16[2,3,160,128]{3,2,1,0:T(8,128)(2,1)S(1)}, bf16[2,3,160,128]{3,2,1,0:T(8,128)(2,1)S(1)}, u32[]{:S(2)}, u32[]{:S(2)}) collective-permute-start(bf16[2,3,160,128]{3,2,1,0:T(8,128)(2,1)S(1)} %get-tuple-element.35), channel_id=1, source_target_pairs={{0,2},{1,3},{2,0},{3,1},{4,6},{5,7},{6,4},{7,5},{8,10},{9,11},{10,... | collective-permute-start | bytes 737288 | tf_op jit(solution)/shard_map/ppermute | solution.py:363
  120.0 33.8 %collective-permute-start.2 = (bf16[2,3,160,128]{3,2,1,0:T(8,128)(2,1)S(1)}, bf16[2,3,160,128]{3,2,1,0:T(8,128)(2,1)S(1)}, u32[]{:S(2)}, u32[]{:S(2)}) collective-permute-start(bf16[2,3,160,128]{3,2,1,0:T(8,128)(2,1)S(1)} %get-tuple-element.36), channel_id=1, source_target_pairs={{0,4},{1,5},{2,6},{3,7},{4,0},{5,1},{6,2},{7,3},{8,12},{9,13},{10,... | collective-permute-start | bytes 737288 | tf_op jit(solution)/shard_map/ppermute | solution.py:363
  120.5 42.6 %collective-permute-start.3 = (bf16[2,3,160,128]{3,2,1,0:T(8,128)(2,1)S(1)}, bf16[2,3,160,128]{3,2,1,0:T(8,128)(2,1)S(1)}, u32[]{:S(2)}, u32[]{:S(2)}) collective-permute-start(bf16[2,3,160,128]{3,2,1,0:T(8,128)(2,1)S(1)} %get-tuple-element.37), channel_id=1, source_target_pairs={{0,6},{1,7},{2,4},{3,5},{4,2},{5,3},{6,0},{7,1},{8,14},{9,15},{10,... | collective-permute-start | bytes 737288 | tf_op jit(solution)/shard_map/ppermute | solution.py:363
  122.0 62.8 %collective-permute-start.4 = (bf16[2,3,160,128]{3,2,1,0:T(8,128)(2,1)S(1)}, bf16[2,3,160,128]{3,2,1,0:T(8,128)(2,1)S(1)}, u32[]{:S(2)}, u32[]{:S(2)}) collective-permute-start(bf16[2,3,160,128]{3,2,1,0:T(8,128)(2,1)S(1)} %get-tuple-element.38), channel_id=1, source_target_pairs={{0,8},{1,9},{2,10},{3,11},{4,12},{5,13},{6,14},{7,15},{8,0},{9,1},... | collective-permute-start | bytes 737288 | tf_op jit(solution)/shard_map/ppermute | solution.py:363
  124.4 65.7 %collective-permute-start.5 = (bf16[2,3,160,128]{3,2,1,0:T(8,128)(2,1)S(1)}, bf16[2,3,160,128]{3,2,1,0:T(8,128)(2,1)S(1)}, u32[]{:S(2)}, u32[]{:S(2)}) collective-permute-start(bf16[2,3,160,128]{3,2,1,0:T(8,128)(2,1)S(1)} %get-tuple-element.39), channel_id=1, source_target_pairs={{0,10},{1,11},{2,8},{3,9},{4,14},{5,15},{6,12},{7,13},{8,2},{9,3},... | collective-permute-start | bytes 737288 | tf_op jit(solution)/shard_map/ppermute | solution.py:363
  131.5 66.7 %collective-permute-start.6 = (bf16[2,3,160,128]{3,2,1,0:T(8,128)(2,1)S(1)}, bf16[2,3,160,128]{3,2,1,0:T(8,128)(2,1)S(1)}, u32[]{:S(2)}, u32[]{:S(2)}) collective-permute-start(bf16[2,3,160,128]{3,2,1,0:T(8,128)(2,1)S(1)} %get-tuple-element.40), channel_id=1, source_target_pairs={{0,12},{1,13},{2,14},{3,15},{4,8},{5,9},{6,10},{7,11},{8,4},{9,5},... | collective-permute-start | bytes 737288 | tf_op jit(solution)/shard_map/ppermute | solution.py:363
  153.8 50.2 %collective-permute-start.7 = (bf16[2,3,160,128]{3,2,1,0:T(8,128)(2,1)S(1)}, bf16[2,3,160,128]{3,2,1,0:T(8,128)(2,1)S(1)}, u32[]{:S(2)}, u32[]{:S(2)}) collective-permute-start(bf16[2,3,160,128]{3,2,1,0:T(8,128)(2,1)S(1)} %get-tuple-element.41), channel_id=1, source_target_pairs={{0,14},{1,15},{2,12},{3,13},{4,10},{5,11},{6,8},{7,9},{8,6},{9,7},... | collective-permute-start | bytes 737288 | tf_op jit(solution)/shard_map/ppermute | solution.py:363
  204.2 2.6 collective-permute-start.8
  211.7 13.3 %collective-permute-start.9 = (bf16[3,128,640]{2,1,0:T(8,128)(2,1)S(1)}, bf16[3,128,640]{2,1,0:T(8,128)(2,1)S(1)}, u32[]{:S(2)}, u32[]{:S(2)}) collective-permute-start(bf16[3,128,640]{2,1,0:T(8,128)(2,1)S(1)} %analyse.3.own_ref), channel_id=1, source_target_pairs={{0,16},{16,0},{1,17},{17,1},{2,18},{18,2},{3,19},{19,3},{4,20},{20... | collective-permute-start | bytes 1474568 | tf_op jit(solution)/shard_map/ppermute | solution.py:409
  233.6 2.6 collective-permute-start.10
  237.8 8.1 %collective-permute-start.11 = (bf16[2,3,160,128]{3,2,1,0:T(8,128)(2,1)S(1)}, bf16[2,3,160,128]{3,2,1,0:T(8,128)(2,1)S(1)}, u32[]{:S(2)}, u32[]{:S(2)}) collective-permute-start(bf16[2,3,160,128]{3,2,1,0:T(8,128)(2,1)S(1)} %get-tuple-element.52), channel_id=1, source_target_pairs={{0,2},{1,3},{2,0},{3,1},{4,6},{5,7},{6,4},{7,5},{8,10},{9,11},{10,... | collective-permute-start | bytes 737288 | tf_op jit(solution)/shard_map/ppermute | solution.py:363
  238.3 14.7 %collective-permute-start.12 = (bf16[2,3,160,128]{3,2,1,0:T(8,128)(2,1)S(1)}, bf16[2,3,160,128]{3,2,1,0:T(8,128)(2,1)S(1)}, u32[]{:S(2)}, u32[]{:S(2)}) collective-permute-start(bf16[2,3,160,128]{3,2,1,0:T(8,128)(2,1)S(1)} %get-tuple-element.53), channel_id=1, source_target_pairs={{0,4},{1,5},{2,6},{3,7},{4,0},{5,1},{6,2},{7,3},{8,12},{9,13},{10,... | collective-permute-start | bytes 737288 | tf_op jit(solution)/shard_map/ppermute | solution.py:363
  238.3 19.1 %collective-permute-start.13 = (bf16[2,3,160,128]{3,2,1,0:T(8,128)(2,1)S(1)}, bf16[2,3,160,128]{3,2,1,0:T(8,128)(2,1)S(1)}, u32[]{:S(2)}, u32[]{:S(2)}) collective-permute-start(bf16[2,3,160,128]{3,2,1,0:T(8,128)(2,1)S(1)} %get-tuple-element.54), channel_id=1, source_target_pairs={{0,6},{1,7},{2,4},{3,5},{4,2},{5,3},{6,0},{7,1},{8,14},{9,15},{10,... | collective-permute-start | bytes 737288 | tf_op jit(solution)/shard_map/ppermute | solution.py:363
  241.4 16.1 %collective-permute-start.14 = (bf16[2,3,160,128]{3,2,1,0:T(8,128)(2,1)S(1)}, bf16[2,3,160,128]{3,2,1,0:T(8,128)(2,1)S(1)}, u32[]{:S(2)}, u32[]{:S(2)}) collective-permute-start(bf16[2,3,160,128]{3,2,1,0:T(8,128)(2,1)S(1)} %get-tuple-element.55), channel_id=1, source_target_pairs={{0,8},{1,9},{2,10},{3,11},{4,12},{5,13},{6,14},{7,15},{8,0},{9,1},... | collective-permute-start | bytes 737288 | tf_op jit(solution)/shard_map/ppermute | solution.py:363
  241.4 32.7 %collective-permute-start.15 = (bf16[2,3,160,128]{3,2,1,0:T(8,128)(2,1)S(1)}, bf16[2,3,160,128]{3,2,1,0:T(8,128)(2,1)S(1)}, u32[]{:S(2)}, u32[]{:S(2)}) collective-permute-start(bf16[2,3,160,128]{3,2,1,0:T(8,128)(2,1)S(1)} %get-tuple-element.56), channel_id=1, source_target_pairs={{0,10},{1,11},{2,8},{3,9},{4,14},{5,15},{6,12},{7,13},{8,2},{9,3},... | collective-permute-start | bytes 737288 | tf_op jit(solution)/shard_map/ppermute | solution.py:363
  245.9 35.4 %collective-permute-start.16 = (bf16[2,3,160,128]{3,2,1,0:T(8,128)(2,1)S(1)}, bf16[2,3,160,128]{3,2,1,0:T(8,128)(2,1)S(1)}, u32[]{:S(2)}, u32[]{:S(2)}) collective-permute-start(bf16[2,3,160,128]{3,2,1,0:T(8,128)(2,1)S(1)} %get-tuple-element.57), channel_id=1, source_target_pairs={{0,12},{1,13},{2,14},{3,15},{4,8},{5,9},{6,10},{7,11},{8,4},{9,5},... | collective-permute-start | bytes 737288 | tf_op jit(solution)/shard_map/ppermute | solution.py:363
  252.9 32.2 %collective-permute-start.17 = (bf16[2,3,160,128]{3,2,1,0:T(8,128)(2,1)S(1)}, bf16[2,3,160,128]{3,2,1,0:T(8,128)(2,1)S(1)}, u32[]{:S(2)}, u32[]{:S(2)}) collective-permute-start(bf16[2,3,160,128]{3,2,1,0:T(8,128)(2,1)S(1)} %get-tuple-element.58), channel_id=1, source_target_pairs={{0,14},{1,15},{2,12},{3,13},{4,10},{5,11},{6,8},{7,9},{8,6},{9,7},... | collective-permute-start | bytes 737288 | tf_op jit(solution)/shard_map/ppermute | solution.py:363
  281.3 0.7 copy-start.7
  285.1 0.7 copy-start.9
  285.8 0.9 copy-start.8
  286.8 0.9 copy-start.10
Sparse Core Ops, SparseCore 0:
  72.8 25.3 all-reduce.2

commit v5 on v4

--- a/solution.py
+++ b/solution.py
@@ -11,7 +11,7 @@
 BF16 = jnp.bfloat16
 F32 = jnp.float32
 CORES = 2
-PERMUTED = (1,)
+PERMUTED = ()
 ANYWHERE = pl.BlockSpec(memory_space=pl.ANY)
 IN_SMEM = pl.BlockSpec(memory_space=pltpu.SMEM)
 TOKEN = jax.ShapeDtypeStruct((8, 128), F32)

time: 299 us -> 242 us (0.81)
  waiting for transfers between devices: 179 us -> 92.8 us
  blocking collectives: 0 us -> 51.3 us
  starting transfers between devices: 40.9 us -> 21.7 us
  local copies, waits for them, and re-layouts: 23.5 us -> 19.9 us
    ppermute x16 -> x0, waiting for transfers between devices: 112 us -> none  [the longest x14 107 us: between_chips(): lax.ppermute(messages[k], 'wave', [(d, d ^ k * CORES) for d in range(chip...]
    all_to_all x0 -> x1, blocking collectives: none -> 51.3 us  [to_all(): lax.all_to_all(blocks, 'wave', split_axis=0, concat_axis=0, tiled=True)]
    all_to_all x2 -> x3, waiting for transfers between devices: 29.3 us -> 55.8 us  [to_all(): lax.all_to_all(blocks, 'wave', split_axis=0, concat_axis=0, tiled=True)]
    ppermute x16 -> x0, starting transfers between devices: 25.4 us -> none  [the longest x14 25.3 us: between_chips(): lax.ppermute(messages[k], 'wave', [(d, d ^ k * CORES) for d in range(chip...]
    all_to_all x2 -> x3, starting transfers between devices: 12.5 us -> 18.8 us  [to_all(): lax.all_to_all(blocks, 'wave', split_axis=0, concat_axis=0, tiled=True)]
    unnamed x27 -> x23, local copies, waits for them, and re-layouts: 12.3 us -> 8.74 us
  transfers between devices with their start and end apart: 21 -> 6, of which waited for: 18 -> 4; matrix products, arithmetic and copies ran while one was open for 6% -> 7% of each run, Pallas kernels for 6% -> 12%
where the time goes in v5:
time: 242 us; the launch traced here: 239 us
  waiting for transfers between devices  92.8 us (38%)
  blocking collectives  51.3 us (21%)
  Pallas kernels  34 us (14%)
  starting transfers between devices  21.7 us (9%)
  local copies, waits for them, and re-layouts  19.9 us (8%)
  between operations  13.6 us (6%)
  matrix products  3.24 us (1%)
  other arithmetic  2.83 us (1%)
    all_to_all x3, waiting for transfers between devices, to_all(): lax.all_to_all(blocks, 'wave', split_axis=0, concat_axis=0, tiled=True)  55.8 us
    all_to_all x1, blocking collectives, to_all(): lax.all_to_all(blocks, 'wave', split_axis=0, concat_axis=0, tiled=True)  51.3 us
    psum x1, waiting for transfers between devices, per_device(): real_matrix, imag_matrix = lax.psum((real_matrix, imag_matrix), 'pole')  25.1 us
    all_to_all x3, starting transfers between devices, to_all(): lax.all_to_all(blocks, 'wave', split_axis=0, concat_axis=0, tiled=True)  18.8 us
    pallas_call x2, Pallas kernels, synthesise(): call(functools.partial(synthesise_kernel, chips), 'synthesise', 2 * count...  12.9 us
    pallas_call x2, Pallas kernels, analyse(): call(functools.partial(analyse_kernel, slot, low, len(blocks)), 'analyse'...  12.7 us
    ppermute x2, waiting for transfers between devices, per_device(): other = lax.ppermute(forced, 'pole', [(0, 1), (1, 0)])  11.9 us
    unnamed x23, local copies, waits for them, and re-layouts  8.74 us
  transfers between devices with their start and end apart: 6, of which 4 were waited for; matrix products, arithmetic and copies ran while one was open for 7% of the time, Pallas kernels for 12%

profile of v5, /device:TPU:8, one launch (start us, length us, event | category | flops | bytes accessed | tf_op | source)
XLA Modules:
  0.0 239.5 jit_solution(7597841704050241040)
XLA Ops:
  6.5 0.0 copy-start
  6.5 0.8 broadcast_in_dim.10.gauss_ref
  7.3 0.0 copy-start.1
  7.3 2.1 copy-done.1
  9.4 1.2 weigh.2
  10.6 0.0 copy-start.6
  10.6 1.3 copy-done.6
  11.9 6.3 %all-to-all-start = ((bf16[16,3,160,128]{3,2,1,0:T(8,128)(2,1)}), bf16[16,3,160,128]{3,2,1,0:T(8,128)(2,1)S(1)}, u32[]{:S(2)}, u32[]{:S(2)}) async-start(bf16[16,3,160,128]{3,2,1,0:T(8,128)(2,1)} %copy-done.6), calls=%async_computation | async-start | bytes 3932160 | tf_op jit(solution)/shard_map/all_to_all | solution.py:372
  18.2 0.0 copy-start.2
  18.2 2.1 copy-done.2
  20.3 2.4 %weigh.3 = bf16[16,3,160,128]{3,2,1,0:T(8,128)(2,1)} custom-call(s32[1]{0:T(128)} %bitcast.me_ref, f32[160,128]{1,0:T(8,128)S(1)} %broadcast_in_dim.10.gauss_ref, bf16[3,160,32,128]{3,2,1,0:T(8,128)(2,1)S(1)} %copy-done.2), custom_call_target="tpu_custom_call" | custom-call | flops 503316480 | bytes 5898240 | tf_op jit(solution)/shard_map/weigh/pallas_call | solution.py:85
  22.7 38.5 %all-to-all-done.rest_0_ = bf16[16,3,160,128]{3,2,1,0:T(8,128)(2,1)S(1)} async-done(((bf16[16,3,160,128]{3,2,1,0:T(8,128)(2,1)}), bf16[16,3,160,128]{3,2,1,0:T(8,128)(2,1)S(1)}, u32[]{:S(2)}, u32[]{:S(2)}) %all-to-all-start) | async-done | bytes 1966112 | tf_op jit(solution)/shard_map/all_to_all | solution.py:372
  61.2 0.0 copy-start.4
  61.2 6.4 %all-to-all-start.2 = ((bf16[16,3,160,128]{3,2,1,0:T(8,128)(2,1)}), bf16[16,3,160,128]{3,2,1,0:T(8,128)(2,1)}, u32[]{:S(2)}, u32[]{:S(2)}) async-start(bf16[16,3,160,128]{3,2,1,0:T(8,128)(2,1)} %weigh.3), calls=%async_computation.2 | async-start | bytes 3932160 | tf_op jit(solution)/shard_map/all_to_all | solution.py:372
  67.7 0.0 all-reduce.3.cloned.1.call-start
  67.7 5.2 %reshape.15 = bf16[32,46080]{1,0:T(8,128)(2,1)} reshape(bf16[32,18,2,1280]{3,2,1,0:T(2,128)(2,1)} %param.11) | data formatting | bytes 5898240 | tf_op jit(solution)/shard_map/reshape | solution.py:392
  72.9 0.0 copy-done.4
  72.9 5.2 %dot_general.8 = bf16[2,3,3,2,1280,32]{4,3,2,1,0,5:T(2,128)(2,1)} reshape(bf16[46080,32]{0,1:T(8,128)(2,1)} %bitcast.23) | data formatting | bytes 5898240 | tf_op jit(solution)/shard_map/dot_general | solution.py:393
  78.1 0.0 copy-done
  78.1 0.0 copy-start.3
  78.1 0.0 copy-start.5
  78.1 0.0 copy-start.9
  78.1 3.2 %fusion = f32[2,2,3,3,2,1280]{5,0,4,3,2,1:T(2,128)S(1)} fusion(bf16[2,3,3,2,1280,32]{4,3,2,1,0,5:T(2,128)(2,1)} %dot_general.8, f32[32,2]{0,1:T(2,128)S(1)} %copy-done), kind=kOutput, calls=%fused_computation | convolution fusion | flops 35389440 | bytes 3318016 | tf_op jit(solution)/shard_map/dot_general | solution.py:393
  81.3 0.2 fusion.4
  81.6 0.0 copy-done.3
  81.6 0.0 copy-done.5
  81.6 0.0 copy-done.9
  81.6 6.8 %analyse.2.own_ref = bf16[3,128,1280]{2,1,0:T(8,128)(2,1)S(1)} custom-call(s32[1]{0:T(128)} %bitcast.me_ref, s32[2]{0:T(128)S(1)} %copy-done.9, f32[8,128]{1,0:T(8,128)S(1)} %broadcast_in_dim.4.token_ref, bf16[2,1280,2560]{2,1,0:T(8,128)(2,1)} %table_ref.7, bf16[3,2,128,1280]{3,2,1,0:T(8,128)(2,1)S(1)} %copy-done.3, bf16[16,3,160,128]{3,2,1,0:T(8,128)(2,1)S(1)} %copy-done.5), custom_call_target="tpu_custom_call" | custom-call | flops 2516582400 | bytes 6553600 | tf_op jit(solution)/shard_map/analyse/pallas_call | solution.py:192
  88.5 1.6 collective-permute-start
  90.1 0.7 fusion.2
  90.8 0.7 copy.32
  91.4 0.0 all-reduce.3.cloned.1.call-update
  91.5 25.1 %all-reduce.3.cloned.1.call-done = (f32[3,3,2,1280]{3,2,1,0:T(2,128)}, f32[3,3,2,1280]{3,2,1,0:T(2,128)}) async-done(((f32[3,3,2,1280]{3,2,1,0:T(2,128)}, f32[3,3,2,1280]{3,2,1,0:T(2,128)}), (f32[3,3,2,1280]{3,2,1,0:T(2,128)}, f32[3,3,2,1280]{3,2,1,0:T(2,128)})) %all-reduce.3.cloned.1.call-update) | async-done | bytes 184336 | tf_op jit(solution)/shard_map/psum | solution.py:397
  116.6 0.9 broadcast_multiply_fusion
  117.5 1.0 pad_maximum_fusion
  118.5 0.1 slice.28
  118.6 0.0 collective-permute-done.other_ref
  118.6 7.6 %synthesise.2 = (bf16[16,3,160,128]{3,2,1,0:T(8,128)(2,1)S(1)}, f32[8,128]{1,0:T(8,128)S(1)}) custom-call(s32[1]{0:T(128)} %bitcast.me_ref, f32[18,1280]{1,0:T(8,128)S(1)} %bitcast.21, bf16[3,128,1280]{2,1,0:T(8,128)(2,1)S(1)} %analyse.2.own_ref, bf16[3,128,1280]{2,1,0:T(8,128)(2,1)} %collective-permute-done.other_ref, bf16[2,1280,2560]{2,1,0:T(8,128)(2,1)} %table_ref.7), custom_call_target="tpu_custom_call" | custom-call | flops 2516582400 | bytes 6553600 | tf_op jit(solution)/shard_map/synthesise/pallas_call | solution.py:282
  126.2 0.0 copy-start.7
  126.2 1.3 copy-done.7
  127.5 0.0 all-to-all-done.2.rest_0_
  127.5 6.0 %all-to-all-start.1 = ((bf16[16,3,160,128]{3,2,1,0:T(8,128)(2,1)}), bf16[16,3,160,128]{3,2,1,0:T(8,128)(2,1)}, u32[]{:S(2)}, u32[]{:S(2)}) async-start(bf16[16,3,160,128]{3,2,1,0:T(8,128)(2,1)} %copy-done.7), calls=%async_computation.1 | async-start | bytes 3932160 | tf_op jit(solution)/shard_map/all_to_all | solution.py:372
  133.5 5.9 %analyse.3.own_ref = bf16[3,128,640]{2,1,0:T(8,128)(2,1)S(1)} custom-call(s32[1]{0:T(128)} %bitcast.me_ref, s32[2]{0:T(128)S(1)} %copy-done.9, f32[8,128]{1,0:T(8,128)S(1)} %get-tuple-element.9.token_ref, bf16[2,1280,2560]{2,1,0:T(8,128)(2,1)} %table_ref.7, bf16[3,2,128,1280]{3,2,1,0:T(8,128)(2,1)S(1)} %copy-done.3, ...), custom_call_target="tpu_custom_call" | custom-call | flops 1258291200 | bytes 3276800 | tf_op jit(solution)/shard_map/analyse/pallas_call | solution.py:192
  139.4 1.4 collective-permute-start.1
  140.8 0.1 slice.29
  140.8 11.9 %collective-permute-done.1.other_ref = bf16[3,128,640]{2,1,0:T(8,128)(2,1)S(1)} collective-permute-done((bf16[3,128,640]{2,1,0:T(8,128)(2,1)S(1)}, bf16[3,128,640]{2,1,0:T(8,128)(2,1)S(1)}, u32[]{:S(2)}, u32[]{:S(2)}) %collective-permute-start.1) | collective-permute-done | bytes 491552 | tf_op jit(solution)/shard_map/ppermute | solution.py:409
  152.7 5.3 %synthesise.3 = (bf16[16,3,160,128]{3,2,1,0:T(8,128)(2,1)S(1)}, f32[8,128]{1,0:T(8,128)}) custom-call(s32[1]{0:T(128)} %bitcast.me_ref, f32[18,640]{1,0:T(8,128)S(1)} %bitcast.22, bf16[3,128,640]{2,1,0:T(8,128)(2,1)S(1)} %analyse.3.own_ref, bf16[3,128,640]{2,1,0:T(8,128)(2,1)S(1)} %collective-permute-done.1.other_ref, bf16[2,1280,2560]{2,1,0:T(8,128)(2,1)} %table_ref.7), custom_call_target="tpu_custom_call" | custom-call | flops 1258291200 | bytes 3276800 | tf_op jit(solution)/shard_map/synthesise/pallas_call | solution.py:282
  158.1 0.0 copy-start.8
  158.1 1.3 copy-done.8
  159.4 17.2 %all-to-all-done.1.rest_0_ = bf16[16,3,160,128]{3,2,1,0:T(8,128)(2,1)} async-done(((bf16[16,3,160,128]{3,2,1,0:T(8,128)(2,1)}), bf16[16,3,160,128]{3,2,1,0:T(8,128)(2,1)}, u32[]{:S(2)}, u32[]{:S(2)}) %all-to-all-start.1) | async-done | bytes 1966112 | tf_op jit(solution)/shard_map/all_to_all | solution.py:372
  176.6 51.3 %all_to_all.20.rest_1_ = bf16[16,3,160,128]{3,2,1,0:T(8,128)(2,1)S(1)} all-to-all(bf16[16,3,160,128]{3,2,1,0:T(8,128)(2,1)} %copy-done.8), channel_id=1, replica_groups=mesh['pole'=2,'wave'=16] {'wave'}, dimensions={0} | all-to-all | bytes 3932160 | tf_op jit(solution)/shard_map/all_to_all | solution.py:372
  227.9 4.8 %assemble.1 = bf16[3,160,32,128]{3,2,1,0:T(8,128)(2,1)} custom-call(s32[1]{0:T(128)} %bitcast.me_ref, bf16[16,3,160,128]{3,2,1,0:T(8,128)(2,1)} %all-to-all-done.1.rest_0_, bf16[16,3,160,128]{3,2,1,0:T(8,128)(2,1)S(1)} %all_to_all.20.rest_1_), custom_call_target="tpu_custom_call" | custom-call | flops 1006632960 | bytes 7864320 | tf_op jit(solution)/shard_map/assemble/pallas_call | solution.py:341
  (3 shorter events, 0.0 us)
Async XLA Ops:
  6.5 71.5 %copy-start = (f32[32,2]{0,1:T(2,128)S(1)}, f32[32,2]{0,1:T(2,128)}, u32[]{:S(2)}) copy-start(f32[32,2]{0,1:T(2,128)} %param.12) | copy-start | bytes 772
  7.3 2.1 copy-start.1
  10.6 1.3 copy-start.6
  11.9 49.3 %all-to-all-start = ((bf16[16,3,160,128]{3,2,1,0:T(8,128)(2,1)}), bf16[16,3,160,128]{3,2,1,0:T(8,128)(2,1)S(1)}, u32[]{:S(2)}, u32[]{:S(2)}) async-start(bf16[16,3,160,128]{3,2,1,0:T(8,128)(2,1)} %copy-done.6), calls=%async_computation | async-start | bytes 3932160 | tf_op jit(solution)/shard_map/all_to_all | solution.py:372
  18.2 2.1 copy-start.2
  61.2 11.7 %copy-start.4 = (bf16[16,3,160,128]{3,2,1,0:T(8,128)(2,1)}, bf16[16,3,160,128]{3,2,1,0:T(8,128)(2,1)S(1)}, u32[]{:S(2)}) copy-start(bf16[16,3,160,128]{3,2,1,0:T(8,128)(2,1)S(1)} %all-to-all-done.rest_0_) | copy-start | bytes 5898244
  61.2 66.2 %all-to-all-start.2 = ((bf16[16,3,160,128]{3,2,1,0:T(8,128)(2,1)}), bf16[16,3,160,128]{3,2,1,0:T(8,128)(2,1)}, u32[]{:S(2)}, u32[]{:S(2)}) async-start(bf16[16,3,160,128]{3,2,1,0:T(8,128)(2,1)} %weigh.3), calls=%async_computation.2 | async-start | bytes 3932160 | tf_op jit(solution)/shard_map/all_to_all | solution.py:372
  67.7 48.9 %all-reduce.3.cloned.1.call-start = ((), (), s32[]{:S(2)}) async-start(), calls=%async_computation.4 | async-start | bytes 368640 | tf_op jit(solution)/shard_map/psum | solution.py:397
  78.1 3.5 %copy-start.3 = (bf16[3,2,128,1280]{3,2,1,0:T(8,128)(2,1)S(1)}, bf16[3,2,128,1280]{3,2,1,0:T(8,128)(2,1)}, u32[]{:S(2)}) copy-start(bf16[3,2,128,1280]{3,2,1,0:T(8,128)(2,1)} %state_ref.3) | copy-start | bytes 5898244
  78.1 3.5 %copy-start.5 = (bf16[16,3,160,128]{3,2,1,0:T(8,128)(2,1)S(1)}, bf16[16,3,160,128]{3,2,1,0:T(8,128)(2,1)}, u32[]{:S(2)}) copy-start(bf16[16,3,160,128]{3,2,1,0:T(8,128)(2,1)} %copy-done.4) | copy-start | bytes 5898244
  78.1 3.5 %copy-start.9 = (s32[2]{0:T(128)S(1)}, s32[2]{0:T(128)}, u32[]{:S(2)}) copy-start(s32[2]{0:T(128)} %wave_ref.3) | copy-start | bytes 28
  88.5 30.1 %collective-permute-start = (bf16[3,128,1280]{2,1,0:T(8,128)(2,1)S(1)}, bf16[3,128,1280]{2,1,0:T(8,128)(2,1)}, u32[]{:S(2)}, u32[]{:S(2)}) collective-permute-start(bf16[3,128,1280]{2,1,0:T(8,128)(2,1)S(1)} %analyse.2.own_ref), channel_id=1, source_target_pairs={{0,16},{16,0},{1,17},{17,1},{2,18},{18,2},{3,19},{19,3},{4,20},{20... | collective-permute-start | bytes 2949128 | tf_op jit(solution)/shard_map/ppermute | solution.py:409
  126.2 1.3 copy-start.7
  127.5 49.1 %all-to-all-start.1 = ((bf16[16,3,160,128]{3,2,1,0:T(8,128)(2,1)}), bf16[16,3,160,128]{3,2,1,0:T(8,128)(2,1)}, u32[]{:S(2)}, u32[]{:S(2)}) async-start(bf16[16,3,160,128]{3,2,1,0:T(8,128)(2,1)} %copy-done.7), calls=%async_computation.1 | async-start | bytes 3932160 | tf_op jit(solution)/shard_map/all_to_all | solution.py:372
  139.4 13.3 %collective-permute-start.1 = (bf16[3,128,640]{2,1,0:T(8,128)(2,1)S(1)}, bf16[3,128,640]{2,1,0:T(8,128)(2,1)S(1)}, u32[]{:S(2)}, u32[]{:S(2)}) collective-permute-start(bf16[3,128,640]{2,1,0:T(8,128)(2,1)S(1)} %analyse.3.own_ref), channel_id=1, source_target_pairs={{0,16},{16,0},{1,17},{17,1},{2,18},{18,2},{3,19},{19,3},{4,20},{20... | collective-permute-start | bytes 1474568 | tf_op jit(solution)/shard_map/ppermute | solution.py:409
  158.1 1.3 copy-start.8
Sparse Core Ops, SparseCore 0:
  91.6 24.9 all-reduce.2

commit v6 on v5

--- a/solution.py
+++ b/solution.py
@@ -51,6 +51,8 @@
 def weigh_kernel(slot, local_slots, permuted, me_ref, gauss_ref, tendency_ref, *rest):
     _, lats, slots, members = tendency_ref.shape
     outs, blocks = (rest[:-1], rest[-1]) if permuted else (rest, None)
+    outs, token_ref = outs[:-1], outs[-1]
+    token_ref[...] = jnp.zeros_like(token_ref)
     depth, breadth = math.gcd(lats, 16), 16
     matrix = swap_matrix(depth, breadth, range(slot, breadth, local_slots))
     owners = breadth // local_slots
@@ -87,7 +89,8 @@
         "weigh",
         2 * 128 * tendency.size,
         3 * tendency.size,
-        out_shape=[jax.ShapeDtypeStruct((count, rows, lats, members), BF16)] * chips,
+        58,
+        out_shape=[jax.ShapeDtypeStruct((count, rows, lats, members), BF16)] * chips + [TOKEN],
         grid_spec=pltpu.PrefetchScalarGridSpec(
             num_scalar_prefetch=1,
             grid=(rows,),
@@ -95,7 +98,7 @@
                 pl.BlockSpec((lats, members), lambda r, m: (0, 0)),
                 pl.BlockSpec((1, lats, slots, members), lambda r, m: (r, 0, 0, 0)),
             ],
-            out_specs=[piece] * chips,
+            out_specs=[piece] * chips + [pl.BlockSpec(TOKEN.shape, lambda r, m: (0, 0))],
             scratch_shapes=[pltpu.VMEM((owners, lats, members), BF16)] if permuted else [],
         ),
     )(me, gauss, tendency)
@@ -222,7 +225,37 @@
     return jnp.take(both, order, axis=0)
 
 
-def synthesise_kernel(permuted, me_ref, matrix_ref, own_ref, other_ref, table_ref, *rest):
+def sum_pairs_kernel(coeff_ref, token_ref, inverse_ref, out_ref):
+    pairs, entries = inverse_ref.shape[:2]
+    half = entries // 2
+
+    def one(entry, carry):
+        real = imag = 0.0
+        for k in range(pairs):
+            first, second = inverse_ref[k, entry].astype(F32), inverse_ref[k, half + entry].astype(F32)
+            a, b = coeff_ref[k, 0], coeff_ref[k, 1]
+            real = real + (a * first - b * second)
+            imag = imag + (a * second + b * first)
+        out_ref[entry] = real
+        out_ref[half + entry] = imag
+        return carry
+
+    lax.fori_loop(0, half, one, 0)
+
+
+def sum_pairs(block_inverses, pole_coeffs, token):
+    return call(
+        sum_pairs_kernel,
+        "sum_pairs",
+        4 * block_inverses.size,
+        2 * block_inverses.size,
+        out_shape=jax.ShapeDtypeStruct(block_inverses.shape[1:], F32),
+        in_specs=[IN_SMEM, ANYWHERE, pl.BlockSpec(block_inverses.shape, lambda: (0, 0, 0, 0))],
+        out_specs=pl.BlockSpec(block_inverses.shape[1:], lambda: (0, 0, 0)),
+    )(pole_coeffs, token, block_inverses)
+
+
+def synthesise_kernel(slot, low, permuted, me_ref, sign_ref, here_ref, there_ref, own_ref, other_ref, table_ref, *rest):
     rows, members, _ = own_ref.shape
     width = table_ref.shape[2]
     step = pl.program_id(0)
@@ -231,12 +264,15 @@
     @pl.when(step == 0)
     def _():
         token_ref[...] = jnp.zeros_like(token_ref)
+
+        def line(entry):
+            return here_ref[entry, slot : slot + 1, low:] + there_ref[entry, slot : slot + 1, low:]
+
         for f in range(rows):
             total = 0.0
             for g in range(rows):
-                total = total + matrix_ref[f * rows + g : f * rows + g + 1, :] * own_ref[g].astype(F32)
-                line = rows * rows + f * rows + g
-                total = total + matrix_ref[line : line + 1, :] * other_ref[g].astype(F32)
+                total = total + line(f * rows + g) * own_ref[g].astype(F32)
+                total = total + sign_ref[0] * line(rows * rows + f * rows + g) * other_ref[g].astype(F32)
             mixed[f * members : (f + 1) * members, :] = total.astype(BF16)
 
     sums = jnp.dot(mixed[...], table_ref[0], preferred_element_type=F32)
@@ -264,12 +300,13 @@
             run_copies(copies)
 
 
-def synthesise(matrix, own, other, table, me, slot, low, lats, permuted):
+def synthesise(here, there, sign, own, other, table, me, slot, low, lats, permuted):
     rows, members, count = own.shape
     nlat = table.shape[2]
     owners = nlat // lats
     width = math.lcm(lats, 128)
     chips = owners // CORES if permuted else 0
+    matrix = pl.BlockSpec(here.shape, lambda j: (0, 0, 0))
     whole = pl.BlockSpec((rows, members, count), lambda j: (0, 0, 0))
     shapes = [jax.ShapeDtypeStruct((owners, rows, lats, members), BF16)]
     specs = [pl.BlockSpec((width // lats, rows, lats, members), lambda j: (j, 0, 0, 0))]
@@ -280,7 +317,7 @@
         specs = [ANYWHERE] * (chips + 1)
         scratch += [pltpu.VMEM((owners, rows, lats, members), BF16), pltpu.SemaphoreType.DMA((chips, CORES))]
     return call(
-        functools.partial(synthesise_kernel, chips),
+        functools.partial(synthesise_kernel, slot, low, chips),
         "synthesise",
         2 * count * nlat * rows * members,
         2 * count * nlat,
@@ -288,14 +325,16 @@
         grid=(nlat // width,),
         in_specs=[
             IN_SMEM,
-            pl.BlockSpec(matrix.shape, lambda j: (0, 0)),
+            IN_SMEM,
+            matrix,
+            matrix,
             whole,
             whole,
             pl.BlockSpec((1, count, width), lambda j: (slot, low // count, j)),
         ],
         out_specs=specs + [pl.BlockSpec(TOKEN.shape, lambda j: (0, 0))],
         scratch_shapes=scratch,
-    )(me, matrix, own, other, table)
+    )(me, sign, here, there, own, other, table)
 
 
 def assemble_kernel(counts, me_ref, *rest):
@@ -380,25 +419,19 @@
     owners = slots // local_slots
     me = lax.axis_index("wave").astype(jnp.int32).reshape(1)
     pole_index = lax.axis_index("pole")
-    orientation = (2 * pole_index - 1).astype(F32)
+    sign = (2 * pole_index - 1).astype(F32).reshape(1)
     gauss = jnp.broadcast_to(gauss_weights[:, None], (lats, members))
-    received = []
+    received, tokens = [], []
     for slot in range(local_slots):
         permuted = slot in PERMUTED
-        blocks = weigh(tendency, gauss, me, slot, local_slots, permuted)
+        *blocks, token = weigh(tendency, gauss, me, slot, local_slots, permuted)
+        tokens.append(token)
         received.append(between_chips(blocks) if permuted else [to_all(blocks[0])])
 
-    local_pairs = block_inverses.shape[0]
-    flat_inverse = block_inverses.reshape(local_pairs, -1).astype(F32)
-    weighted_sums = jnp.dot(pole_coeffs.T, flat_inverse, precision=lax.Precision.HIGHEST)
-    weighted_sums = weighted_sums.reshape(2, 2, rows, rows, local_slots, nspec)
-    real_matrix = weighted_sums[0, 0] - weighted_sums[1, 1]
-    imag_matrix = weighted_sums[0, 1] + weighted_sums[1, 0]
-    real_matrix, imag_matrix = lax.psum((real_matrix, imag_matrix), "pole")
-    matrices = jnp.concatenate([real_matrix, orientation * imag_matrix]).reshape(2 * rows * rows, local_slots, nspec)
-
+    here = sum_pairs(block_inverses, pole_coeffs, tokens[0])
+    there = lax.ppermute(here, "pole", [(0, 1), (1, 0)])
     sent = []
-    token = jnp.zeros(TOKEN.shape, TOKEN.dtype)
+    token = there
     for slot in range(local_slots):
         permuted = slot in PERMUTED
         low = nspec // 2 if slot % 2 else 0
@@ -407,8 +440,7 @@
             blocks = blocks + [between_cores(pick(blocks, me), owners)]
         forced = analyse(blocks, legendre, spectral_state, wavenumbers, me, token, slot, low, nspec // 2)
         other = lax.ppermute(forced, "pole", [(0, 1), (1, 0)])
-        matrix = matrices[:, slot, low:]
-        *blocks, token = synthesise(matrix, forced, other, legendre, me, slot, low, lats, permuted)
+        *blocks, token = synthesise(here, there, sign, forced, other, legendre, me, slot, low, lats, permuted)
         if permuted:
             sent.append(between_chips(pair(blocks[:-1], between_cores(blocks[-1], owners))))
         else:

time: 242 us -> 222 us (0.917)
  between operations: 13.6 us -> 0.06 us
  local copies, waits for them, and re-layouts: 19.9 us -> 7.53 us
  Pallas kernels: 34 us -> 42.2 us
  matrix products: 3.24 us -> 0 us
  other arithmetic: 2.83 us -> 0 us
  waiting for transfers between devices: 92.8 us -> 95.4 us
    psum x1 -> x0, waiting for transfers between devices: 25.1 us -> none  [per_device(): real_matrix, imag_matrix = lax.psum((real_matrix, imag_matrix), 'pole')]
    ppermute x2, waiting for transfers between devices: 11.9 us -> 33.4 us  [per_device(): other = lax.ppermute(forced, 'pole', [(0, 1), (1, 0)])]
    pallas_call x2, Pallas kernels: 3.62 us -> 9.42 us  [weigh(): call(functools.partial(weigh_kernel, slot, local_slots, permuted), 'weigh...]
    ppermute x0 -> x1, waiting for transfers between devices: none -> 5.17 us  [per_device(): there = lax.ppermute(here, 'pole', [(0, 1), (1, 0)])]
    reshape x1 -> x0, local copies, waits for them, and re-layouts: 5.16 us -> none  [per_device(): flat_inverse = block_inverses.reshape(local_pairs, -1).astype(F32)]
    dot_general x1 -> x0, local copies, waits for them, and re-layouts: 5.16 us -> none  [per_device(): jnp.dot(pole_coeffs.T, flat_inverse, precision=lax.Precision.HIGHEST)]
    dot_general x1 -> x0, matrix products: 3.24 us -> none  [per_device(): jnp.dot(pole_coeffs.T, flat_inverse, precision=lax.Precision.HIGHEST)]
    unnamed x23 -> x17, local copies, waits for them, and re-layouts: 8.74 us -> 6.14 us
  transfers between devices with their start and end apart: 6 -> 6, of which waited for: 4 -> 5; matrix products, arithmetic and copies ran while one was open for 7% -> 0% of each run, Pallas kernels for 12% -> 15%
where the time goes in v6:
time: 222 us; the launch traced here: 220 us
  waiting for transfers between devices  95.4 us (43%)
  blocking collectives  51.1 us (23%)
  Pallas kernels  42.2 us (19%)
  starting transfers between devices  23.5 us (11%)
  local copies, waits for them, and re-layouts  7.53 us (3%)
    all_to_all x3, waiting for transfers between devices, to_all(): lax.all_to_all(blocks, 'wave', split_axis=0, concat_axis=0, tiled=True)  56.8 us
    all_to_all x1, blocking collectives, to_all(): lax.all_to_all(blocks, 'wave', split_axis=0, concat_axis=0, tiled=True)  51.1 us
    ppermute x2, waiting for transfers between devices, per_device(): other = lax.ppermute(forced, 'pole', [(0, 1), (1, 0)])  33.4 us
    all_to_all x3, starting transfers between devices, to_all(): lax.all_to_all(blocks, 'wave', split_axis=0, concat_axis=0, tiled=True)  18.7 us
    pallas_call x2, Pallas kernels, synthesise(): call(functools.partial(synthesise_kernel, slot, low, chips), 'synthesise'...  12.9 us
    pallas_call x2, Pallas kernels, analyse(): call(functools.partial(analyse_kernel, slot, low, len(blocks)), 'analyse'...  12.7 us
    pallas_call x2, Pallas kernels, weigh(): call(functools.partial(weigh_kernel, slot, local_slots, permuted), 'weigh...  9.42 us
    unnamed x17, local copies, waits for them, and re-layouts  6.14 us
  transfers between devices with their start and end apart: 6, of which 5 were waited for; matrix products, arithmetic and copies ran while one was open for 0% of the time, Pallas kernels for 15%

profile of v6, /device:TPU:8, one launch (start us, length us, event | category | flops | bytes accessed | tf_op | source)
XLA Modules:
  0.0 219.7 jit_solution(14934891432091400960)
XLA Ops:
  0.0 1.4 broadcast_in_dim.2.gauss_ref
  1.4 4.7 %weigh.2 = (bf16[16,3,160,128]{3,2,1,0:T(8,128)(2,1)}, f32[8,128]{1,0:T(8,128)}) custom-call(s32[1]{0:T(128)} %bitcast.me_ref, f32[160,128]{1,0:T(8,128)} %broadcast_in_dim.2.gauss_ref, bf16[3,160,32,128]{3,2,1,0:T(8,128)(2,1)} %tendency_ref.3), custom_call_target="tpu_custom_call" | custom-call | flops 503316480 | bytes 5898240 | tf_op jit(solution)/shard_map/weigh/pallas_call | solution.py:87
  6.1 6.3 %all-to-all-start = ((bf16[16,3,160,128]{3,2,1,0:T(8,128)(2,1)}), bf16[16,3,160,128]{3,2,1,0:T(8,128)(2,1)S(1)}, u32[]{:S(2)}, u32[]{:S(2)}) async-start(bf16[16,3,160,128]{3,2,1,0:T(8,128)(2,1)} %get-tuple-element.12), calls=%async_computation | async-start | bytes 3932160 | tf_op jit(solution)/shard_map/all_to_all | solution.py:411
  12.3 4.7 %weigh.3 = (bf16[16,3,160,128]{3,2,1,0:T(8,128)(2,1)}, f32[8,128]{1,0:T(8,128)}) custom-call(s32[1]{0:T(128)} %bitcast.me_ref, f32[160,128]{1,0:T(8,128)} %broadcast_in_dim.2.gauss_ref, bf16[3,160,32,128]{3,2,1,0:T(8,128)(2,1)} %tendency_ref.3), custom_call_target="tpu_custom_call" | custom-call | flops 503316480 | bytes 5898240 | tf_op jit(solution)/shard_map/weigh/pallas_call | solution.py:87
  17.1 38.3 %all-to-all-done.rest_0_ = bf16[16,3,160,128]{3,2,1,0:T(8,128)(2,1)S(1)} async-done(((bf16[16,3,160,128]{3,2,1,0:T(8,128)(2,1)}), bf16[16,3,160,128]{3,2,1,0:T(8,128)(2,1)S(1)}, u32[]{:S(2)}, u32[]{:S(2)}) %all-to-all-start) | async-done | bytes 1966112 | tf_op jit(solution)/shard_map/all_to_all | solution.py:411
  55.4 0.0 copy-start.1
  55.4 0.0 copy-start.7
  55.4 0.0 copy-start.5
  55.4 0.0 copy-start.6
  55.4 1.3 copy-done.1
  56.7 6.4 %all-to-all-start.2 = ((bf16[16,3,160,128]{3,2,1,0:T(8,128)(2,1)}), bf16[16,3,160,128]{3,2,1,0:T(8,128)(2,1)}, u32[]{:S(2)}, u32[]{:S(2)}) async-start(bf16[16,3,160,128]{3,2,1,0:T(8,128)(2,1)} %get-tuple-element.15), calls=%async_computation.2 | async-start | bytes 3932160 | tf_op jit(solution)/shard_map/all_to_all | solution.py:411
  63.1 0.0 copy-done.7
  63.1 0.0 copy-start
  63.1 0.1 copy.8.coeff_ref
  63.2 0.0 copy-done.5
  63.2 0.0 copy-start.3
  63.2 2.0 copy-done.3
  65.2 2.4 %sum_pairs.1.here_ref = f32[18,2,1280]{2,1,0:T(2,128)S(1)} custom-call(f32[32,2]{1,0:T(8,128)S(1)} %copy.8.coeff_ref, f32[8,128]{1,0:T(8,128)S(1)} %copy-done.5, bf16[32,18,2,1280]{3,2,1,0:T(2,128)(2,1)S(1)} %copy-done.3), custom_call_target="tpu_custom_call" | custom-call | flops 5898240 | bytes 2949120 | tf_op jit(solution)/shard_map/sum_pairs/pallas_call | solution.py:247
  67.6 1.6 collective-permute-start
  69.1 5.2 %collective-permute-done.token_ref.there_ref = f32[18,2,1280]{2,1,0:T(2,128)S(1)} collective-permute-done((f32[18,2,1280]{2,1,0:T(2,128)S(1)}, f32[18,2,1280]{2,1,0:T(2,128)S(1)}, u32[]{:S(2)}, u32[]{:S(2)}) %collective-permute-start) | collective-permute-done | bytes 184352 | tf_op jit(solution)/shard_map/ppermute | solution.py:432
  74.3 0.0 copy-done.6
  74.3 0.0 copy-done
  74.3 0.0 copy-start.2
  74.3 1.5 copy-done.2
  75.9 6.8 %analyse.2.own_ref = bf16[3,128,1280]{2,1,0:T(8,128)(2,1)S(1)} custom-call(s32[1]{0:T(128)} %bitcast.me_ref, s32[2]{0:T(128)S(1)} %copy-done.6, f32[18,2,1280]{2,1,0:T(2,128)S(1)} %collective-permute-done.token_ref.there_ref, bf16[2,1280,2560]{2,1,0:T(8,128)(2,1)} %table_ref.7, bf16[3,2,128,1280]{3,2,1,0:T(8,128)(2,1)S(1)} %copy-done, ...), custom_call_target="tpu_custom_call" | custom-call | flops 2516582400 | bytes 6553600 | tf_op jit(solution)/shard_map/analyse/pallas_call | solution.py:195
  82.7 1.6 collective-permute-start.1
  84.3 21.7 %collective-permute-done.1.other_ref = bf16[3,128,1280]{2,1,0:T(8,128)(2,1)} collective-permute-done((bf16[3,128,1280]{2,1,0:T(8,128)(2,1)S(1)}, bf16[3,128,1280]{2,1,0:T(8,128)(2,1)}, u32[]{:S(2)}, u32[]{:S(2)}) %collective-permute-start.1) | collective-permute-done | bytes 983072 | tf_op jit(solution)/shard_map/ppermute | solution.py:442
  106.0 7.6 %synthesise.2 = (bf16[16,3,160,128]{3,2,1,0:T(8,128)(2,1)S(1)}, f32[8,128]{1,0:T(8,128)S(1)}) custom-call(s32[1]{0:T(128)} %bitcast.me_ref, f32[1]{0:T(128)} %bitcast.1.sign_ref, f32[18,2,1280]{2,1,0:T(2,128)S(1)} %sum_pairs.1.here_ref, f32[18,2,1280]{2,1,0:T(2,128)S(1)} %collective-permute-done.token_ref.there_ref, ...), custom_call_target="tpu_custom_call" | custom-call | flops 2516582400 | bytes 6553600 | tf_op jit(solution)/shard_map/synthesise/pallas_call | solution.py:319
  113.5 0.0 copy-start.4
  113.5 1.3 copy-done.4
  114.8 0.0 all-to-all-done.2.rest_0_
  114.8 6.0 %all-to-all-start.1 = ((bf16[16,3,160,128]{3,2,1,0:T(8,128)(2,1)}), bf16[16,3,160,128]{3,2,1,0:T(8,128)(2,1)}, u32[]{:S(2)}, u32[]{:S(2)}) async-start(bf16[16,3,160,128]{3,2,1,0:T(8,128)(2,1)} %copy-done.4), calls=%async_computation.1 | async-start | bytes 3932160 | tf_op jit(solution)/shard_map/all_to_all | solution.py:411
  120.8 5.9 %analyse.3.own_ref = bf16[3,128,640]{2,1,0:T(8,128)(2,1)S(1)} custom-call(s32[1]{0:T(128)} %bitcast.me_ref, s32[2]{0:T(128)S(1)} %copy-done.6, f32[8,128]{1,0:T(8,128)S(1)} %get-tuple-element.14.token_ref, bf16[2,1280,2560]{2,1,0:T(8,128)(2,1)} %table_ref.7, bf16[3,2,128,1280]{3,2,1,0:T(8,128)(2,1)S(1)} %copy-done, ...), custom_call_target="tpu_custom_call" | custom-call | flops 1258291200 | bytes 3276800 | tf_op jit(solution)/shard_map/analyse/pallas_call | solution.py:195
  126.7 1.6 collective-permute-start.2
  128.3 11.8 %collective-permute-done.2.other_ref = bf16[3,128,640]{2,1,0:T(8,128)(2,1)S(1)} collective-permute-done((bf16[3,128,640]{2,1,0:T(8,128)(2,1)S(1)}, bf16[3,128,640]{2,1,0:T(8,128)(2,1)S(1)}, u32[]{:S(2)}, u32[]{:S(2)}) %collective-permute-start.2) | collective-permute-done | bytes 491552 | tf_op jit(solution)/shard_map/ppermute | solution.py:442
  140.0 5.3 %synthesise.3 = (bf16[16,3,160,128]{3,2,1,0:T(8,128)(2,1)S(1)}, f32[8,128]{1,0:T(8,128)}) custom-call(s32[1]{0:T(128)} %bitcast.me_ref, f32[1]{0:T(128)} %bitcast.1.sign_ref, f32[18,2,1280]{2,1,0:T(2,128)S(1)} %sum_pairs.1.here_ref, f32[18,2,1280]{2,1,0:T(2,128)S(1)} %collective-permute-done.token_ref.there_ref, bf16[3,128,640]{2,1,0:T(8,128)(2,1)S(1)} %analyse.3.own_ref, ...), custom_call_target="tpu_custom_call" | custom-call | flops 1258291200 | bytes 3276800 | tf_op jit(solution)/shard_map/synthesise/pallas_call | solution.py:319
  145.4 18.5 %all-to-all-done.1.rest_0_ = bf16[16,3,160,128]{3,2,1,0:T(8,128)(2,1)} async-done(((bf16[16,3,160,128]{3,2,1,0:T(8,128)(2,1)}), bf16[16,3,160,128]{3,2,1,0:T(8,128)(2,1)}, u32[]{:S(2)}, u32[]{:S(2)}) %all-to-all-start.1) | async-done | bytes 1966112 | tf_op jit(solution)/shard_map/all_to_all | solution.py:411
  163.9 51.1 %all_to_all.20.rest_1_ = bf16[16,3,160,128]{3,2,1,0:T(8,128)(2,1)S(1)} all-to-all(bf16[16,3,160,128]{3,2,1,0:T(8,128)(2,1)S(1)} %get-tuple-element.16), channel_id=1, replica_groups=mesh['pole'=2,'wave'=16] {'wave'}, dimensions={0} | all-to-all | bytes 3932160 | tf_op jit(solution)/shard_map/all_to_all | solution.py:411
  214.9 4.8 %assemble.1 = bf16[3,160,32,128]{3,2,1,0:T(8,128)(2,1)} custom-call(s32[1]{0:T(128)} %bitcast.me_ref, bf16[16,3,160,128]{3,2,1,0:T(8,128)(2,1)} %all-to-all-done.1.rest_0_, bf16[16,3,160,128]{3,2,1,0:T(8,128)(2,1)S(1)} %all_to_all.20.rest_1_), custom_call_target="tpu_custom_call" | custom-call | flops 1006632960 | bytes 7864320 | tf_op jit(solution)/shard_map/assemble/pallas_call | solution.py:380
Async XLA Ops:
  6.1 49.3 %all-to-all-start = ((bf16[16,3,160,128]{3,2,1,0:T(8,128)(2,1)}), bf16[16,3,160,128]{3,2,1,0:T(8,128)(2,1)S(1)}, u32[]{:S(2)}, u32[]{:S(2)}) async-start(bf16[16,3,160,128]{3,2,1,0:T(8,128)(2,1)} %get-tuple-element.12), calls=%async_computation | async-start | bytes 3932160 | tf_op jit(solution)/shard_map/all_to_all | solution.py:411
  55.4 1.3 copy-start.1
  55.4 7.7 %copy-start.7 = (f32[32,2]{0,1:T(2,128)S(1)}, f32[32,2]{0,1:T(2,128)}, u32[]{:S(2)}) copy-start(f32[32,2]{0,1:T(2,128)} %param.12) | copy-start | bytes 772
  55.4 7.8 %copy-start.5 = (f32[8,128]{1,0:T(8,128)S(1)}, f32[8,128]{1,0:T(8,128)}, u32[]{:S(2)}) copy-start(f32[8,128]{1,0:T(8,128)} %get-tuple-element.11.token_ref) | copy-start | bytes 12292
  55.4 18.9 %copy-start.6 = (s32[2]{0:T(128)S(1)}, s32[2]{0:T(128)}, u32[]{:S(2)}) copy-start(s32[2]{0:T(128)} %wave_ref.3) | copy-start | bytes 28
  56.7 58.1 %all-to-all-start.2 = ((bf16[16,3,160,128]{3,2,1,0:T(8,128)(2,1)}), bf16[16,3,160,128]{3,2,1,0:T(8,128)(2,1)}, u32[]{:S(2)}, u32[]{:S(2)}) async-start(bf16[16,3,160,128]{3,2,1,0:T(8,128)(2,1)} %get-tuple-element.15), calls=%async_computation.2 | async-start | bytes 3932160 | tf_op jit(solution)/shard_map/all_to_all | solution.py:411
  63.1 11.2 %copy-start = (bf16[3,2,128,1280]{3,2,1,0:T(8,128)(2,1)S(1)}, bf16[3,2,128,1280]{3,2,1,0:T(8,128)(2,1)}, u32[]{:S(2)}) copy-start(bf16[3,2,128,1280]{3,2,1,0:T(8,128)(2,1)} %state_ref.3) | copy-start | bytes 5898244
  63.2 2.0 copy-start.3
  67.6 6.8 %collective-permute-start = (f32[18,2,1280]{2,1,0:T(2,128)S(1)}, f32[18,2,1280]{2,1,0:T(2,128)S(1)}, u32[]{:S(2)}, u32[]{:S(2)}) collective-permute-start(f32[18,2,1280]{2,1,0:T(2,128)S(1)} %sum_pairs.1.here_ref), channel_id=1, source_target_pairs={{0,16},{16,0},{1,17},{17,1},{2,18},{18,2},{3,19},{19,3},{4,20},{20... | collective-permute-start | bytes 552968 | tf_op jit(solution)/shard_map/ppermute | solution.py:432
  74.3 1.5 copy-start.2
  82.7 23.3 %collective-permute-start.1 = (bf16[3,128,1280]{2,1,0:T(8,128)(2,1)S(1)}, bf16[3,128,1280]{2,1,0:T(8,128)(2,1)}, u32[]{:S(2)}, u32[]{:S(2)}) collective-permute-start(bf16[3,128,1280]{2,1,0:T(8,128)(2,1)S(1)} %analyse.2.own_ref), channel_id=1, source_target_pairs={{0,16},{16,0},{1,17},{17,1},{2,18},{18,2},{3,19},{19,3},{4,20},{20... | collective-permute-start | bytes 2949128 | tf_op jit(solution)/shard_map/ppermute | solution.py:442
  113.5 1.3 copy-start.4
  114.8 49.1 %all-to-all-start.1 = ((bf16[16,3,160,128]{3,2,1,0:T(8,128)(2,1)}), bf16[16,3,160,128]{3,2,1,0:T(8,128)(2,1)}, u32[]{:S(2)}, u32[]{:S(2)}) async-start(bf16[16,3,160,128]{3,2,1,0:T(8,128)(2,1)} %copy-done.4), calls=%async_computation.1 | async-start | bytes 3932160 | tf_op jit(solution)/shard_map/all_to_all | solution.py:411
  126.7 13.3 %collective-permute-start.2 = (bf16[3,128,640]{2,1,0:T(8,128)(2,1)S(1)}, bf16[3,128,640]{2,1,0:T(8,128)(2,1)S(1)}, u32[]{:S(2)}, u32[]{:S(2)}) collective-permute-start(bf16[3,128,640]{2,1,0:T(8,128)(2,1)S(1)} %analyse.3.own_ref), channel_id=1, source_target_pairs={{0,16},{16,0},{1,17},{17,1},{2,18},{18,2},{3,19},{19,3},{4,20},{20... | collective-permute-start | bytes 1474568 | tf_op jit(solution)/shard_map/ppermute | solution.py:442

commit v7 on v6

--- a/solution.py
+++ b/solution.py
@@ -48,8 +48,10 @@
     return (source == (target % rows) * columns + column).astype(BF16)
 
 
-def weigh_kernel(slot, local_slots, permuted, me_ref, gauss_ref, tendency_ref, *rest):
+def weigh_kernel(slot, local_slots, permuted, waits, me_ref, gauss_ref, tendency_ref, *rest):
     _, lats, slots, members = tendency_ref.shape
+    rest = rest[waits:]
+    first = pl.program_id(1) * lats
     outs, blocks = (rest[:-1], rest[-1]) if permuted else (rest, None)
     outs, token_ref = outs[:-1], outs[-1]
     token_ref[...] = jnp.zeros_like(token_ref)
@@ -57,7 +59,10 @@
     matrix = swap_matrix(depth, breadth, range(slot, breadth, local_slots))
     owners = breadth // local_slots
     for j in range(0, lats, depth):
-        scale = gauss_ref[j : j + depth, :]
+        line = jnp.broadcast_to(gauss_ref[...], (depth, gauss_ref.shape[1]))
+        here = lax.broadcasted_iota(jnp.int32, line.shape, 0) + (first + j)
+        mine = lax.broadcasted_iota(jnp.int32, line.shape, 1) == here
+        scale = jnp.sum(jnp.where(mine, line, 0.0), axis=1, keepdims=True)
         for s in range(0, slots, 2 * breadth):
             halves = [
                 tendency_ref[0, j : j + depth, s + h : s + h + breadth, :].reshape(depth * breadth, members)
@@ -79,13 +84,18 @@
                 out[core, 0] = blocks[((me_ref[0] // CORES) ^ k) * CORES + core]
 
 
-def weigh(tendency, gauss, me, slot, local_slots, permuted):
+def lat_block(lats):
+    return lats // 2 if lats % 32 == 0 else lats
+
+
+def weigh(tendency, gauss, me, slot, local_slots, permuted, waits):
     rows, lats, slots, members = tendency.shape
+    each = lat_block(lats)
     owners = slots // local_slots
     count, chips = (CORES, owners // CORES) if permuted else (owners, 1)
-    piece = pl.BlockSpec((count, 1, lats, members), lambda r, m: (0, r, 0, 0))
-    return call(
-        functools.partial(weigh_kernel, slot, local_slots, permuted),
+    piece = pl.BlockSpec((count, 1, each, members), lambda r, j, m: (0, r, j, 0))
+    return call(
+        functools.partial(weigh_kernel, slot, local_slots, permuted, len(waits)),
         "weigh",
         2 * 128 * tendency.size,
         3 * tendency.size,
@@ -93,29 +103,30 @@
         out_shape=[jax.ShapeDtypeStruct((count, rows, lats, members), BF16)] * chips + [TOKEN],
         grid_spec=pltpu.PrefetchScalarGridSpec(
             num_scalar_prefetch=1,
-            grid=(rows,),
+            grid=(rows, lats // each),
             in_specs=[
-                pl.BlockSpec((lats, members), lambda r, m: (0, 0)),
-                pl.BlockSpec((1, lats, slots, members), lambda r, m: (r, 0, 0, 0)),
-            ],
-            out_specs=[piece] * chips + [pl.BlockSpec(TOKEN.shape, lambda r, m: (0, 0))],
-            scratch_shapes=[pltpu.VMEM((owners, lats, members), BF16)] if permuted else [],
+                pl.BlockSpec((1, lats), lambda r, j, m: (0, 0)),
+                pl.BlockSpec((1, each, slots, members), lambda r, j, m: (r, j, 0, 0)),
+            ]
+            + [ANYWHERE] * len(waits),
+            out_specs=[piece] * chips + [pl.BlockSpec(TOKEN.shape, lambda r, j, m: (0, 0))],
+            scratch_shapes=[pltpu.VMEM((owners, each, members), BF16)] if permuted else [],
         ),
-    )(me, gauss, tendency)
-
-
-def pick_kernel(me_ref, *rest):
-    ins, out = rest[:-1], rest[-1]
+    )(me, gauss, tendency, *waits)
+
+
+def pick_kernel(waits, me_ref, *rest):
+    ins, out = rest[waits:-1], rest[-1]
     for k, ref in enumerate(ins):
         out[k] = ref[0]
 
 
-def pick(messages, me):
+def pick(messages, me, waits):
     _, rows, lats, members = messages[0].shape
     chips = len(messages)
     shape = (chips, rows, lats, members)
     return call(
-        pick_kernel,
+        functools.partial(pick_kernel, len(waits)),
         "pick",
         0,
         4 * math.prod(shape),
@@ -123,13 +134,14 @@
         grid_spec=pltpu.PrefetchScalarGridSpec(
             num_scalar_prefetch=1,
             grid=(rows,),
-            in_specs=[
+            in_specs=[ANYWHERE] * len(waits)
+            + [
                 pl.BlockSpec((1, 1, lats, members), lambda r, m: (CORES - 1 - m[0] % CORES, r, 0, 0))
             ]
             * chips,
             out_specs=pl.BlockSpec((chips, 1, lats, members), lambda r, m: (0, r, 0, 0)),
         ),
-    )(me, *messages)
+    )(me, *waits, *messages)
 
 
 def pair_kernel(mate_ref, *rest):
@@ -375,6 +387,7 @@
     _, rows, _, members = pieces[0][0].shape
     owners = max(len(p) * p[0].shape[0] for p in pieces)
     slots = local_slots * owners
+    each = lat_block(lats)
     flat = [block for slot in pieces for block in slot]
     moved = sum(len(p) > 1 for p in pieces)
     return call(
@@ -385,12 +398,12 @@
         out_shape=jax.ShapeDtypeStruct((rows, lats, slots, members), BF16),
         grid_spec=pltpu.PrefetchScalarGridSpec(
             num_scalar_prefetch=1,
-            grid=(rows,),
+            grid=(rows, lats // each),
             in_specs=[
-                pl.BlockSpec((block.shape[0], 1, lats, members), lambda r, m: (0, r, 0, 0)) for block in flat
+                pl.BlockSpec((block.shape[0], 1, each, members), lambda r, j, m: (0, r, j, 0)) for block in flat
             ],
-            out_specs=pl.BlockSpec((1, lats, slots, members), lambda r, m: (r, 0, 0, 0)),
-            scratch_shapes=[pltpu.VMEM((owners, lats, members), BF16)] * moved,
+            out_specs=pl.BlockSpec((1, each, slots, members), lambda r, j, m: (r, j, 0, 0)),
+            scratch_shapes=[pltpu.VMEM((owners, each, members), BF16)] * moved,
         ),
     )(me, *flat)
 
@@ -420,24 +433,23 @@
     me = lax.axis_index("wave").astype(jnp.int32).reshape(1)
     pole_index = lax.axis_index("pole")
     sign = (2 * pole_index - 1).astype(F32).reshape(1)
-    gauss = jnp.broadcast_to(gauss_weights[:, None], (lats, members))
-    received, tokens = [], []
+    received, waits = [], []
     for slot in range(local_slots):
         permuted = slot in PERMUTED
-        *blocks, token = weigh(tendency, gauss, me, slot, local_slots, permuted)
-        tokens.append(token)
+        *blocks, token = weigh(tendency, gauss_weights[None], me, slot, local_slots, permuted, waits)
         received.append(between_chips(blocks) if permuted else [to_all(blocks[0])])
-
-    here = sum_pairs(block_inverses, pole_coeffs, tokens[0])
-    there = lax.ppermute(here, "pole", [(0, 1), (1, 0)])
+        if slot == 0:
+            here = sum_pairs(block_inverses, pole_coeffs, token)
+            there = lax.ppermute(here, "pole", [(0, 1), (1, 0)])
+            waits = [here if permuted else there]
+
     sent = []
-    token = there
     for slot in range(local_slots):
         permuted = slot in PERMUTED
         low = nspec // 2 if slot % 2 else 0
         blocks = received[slot]
         if permuted:
-            blocks = blocks + [between_cores(pick(blocks, me), owners)]
+            blocks = blocks + [between_cores(pick(blocks, me, [token, there]), owners)]
         forced = analyse(blocks, legendre, spectral_state, wavenumbers, me, token, slot, low, nspec // 2)
         other = lax.ppermute(forced, "pole", [(0, 1), (1, 0)])
         *blocks, token = synthesise(here, there, sign, forced, other, legendre, me, slot, low, lats, permuted)

time: 222 us -> 215 us (0.968)
  waiting for transfers between devices: 95.4 us -> 85.2 us
  Pallas kernels: 42.2 us -> 45.5 us
    all_to_all x3, waiting for transfers between devices: 56.8 us -> 45.8 us  [to_all(): lax.all_to_all(blocks, 'wave', split_axis=0, concat_axis=0, tiled=True)]
    unnamed x17 -> x23, local copies, waits for them, and re-layouts: 6.14 us -> 6.69 us
  transfers between devices with their start and end apart: 6 -> 6, of which waited for: 5 -> 6; matrix products, arithmetic and copies ran while one was open for 0% -> 0% of each run, Pallas kernels for 15% -> 16%
where the time goes in v7:
time: 215 us; the launch traced here: 213 us
  waiting for transfers between devices  85.2 us (40%)
  blocking collectives  51.1 us (24%)
  Pallas kernels  45.5 us (21%)
  starting transfers between devices  24.3 us (11%)
  local copies, waits for them, and re-layouts  6.69 us (3%)
    all_to_all x1, blocking collectives, to_all(): lax.all_to_all(blocks, 'wave', split_axis=0, concat_axis=0, tiled=True)  51.1 us
    all_to_all x3, waiting for transfers between devices, to_all(): lax.all_to_all(blocks, 'wave', split_axis=0, concat_axis=0, tiled=True)  45.8 us
    ppermute x2, waiting for transfers between devices, per_device(): other = lax.ppermute(forced, 'pole', [(0, 1), (1, 0)])  34.2 us
    all_to_all x3, starting transfers between devices, to_all(): lax.all_to_all(blocks, 'wave', split_axis=0, concat_axis=0, tiled=True)  19.5 us
    pallas_call x2, Pallas kernels, synthesise(): call(functools.partial(synthesise_kernel, slot, low, chips), 'synthesise'...  12.9 us
    pallas_call x2, Pallas kernels, analyse(): call(functools.partial(analyse_kernel, slot, low, len(blocks)), 'analyse'...  12.8 us
    pallas_call x2, Pallas kernels, weigh(): call(functools.partial(weigh_kernel, slot, local_slots, permuted, len(wai...  11.6 us
    unnamed x23, local copies, waits for them, and re-layouts  6.69 us
  transfers between devices with their start and end apart: 6, of which 6 were waited for; matrix products, arithmetic and copies ran while one was open for 0% of the time, Pallas kernels for 16%

profile of v7, /device:TPU:8, one launch (start us, length us, event | category | flops | bytes accessed | tf_op | source)
XLA Modules:
  0.0 212.7 jit_solution(15581883716879517761)
XLA Ops:
  0.0 5.7 %weigh.2 = (bf16[16,3,160,128]{3,2,1,0:T(8,128)(2,1)}, f32[8,128]{1,0:T(8,128)}) custom-call(s32[1]{0:T(128)} %bitcast.me_ref, f32[1,160]{1,0:T(1,128)} %bitcast.3, bf16[3,160,32,128]{3,2,1,0:T(8,128)(2,1)} %tendency_ref.3), custom_call_target="tpu_custom_call" | custom-call | flops 503316480 | bytes 5898240 | tf_op jit(solution)/shard_map/weigh/pallas_call | solution.py:97
  5.7 0.0 copy-start.10
  5.7 0.0 copy-start.8
  5.7 6.4 %all-to-all-start = ((bf16[16,3,160,128]{3,2,1,0:T(8,128)(2,1)}), bf16[16,3,160,128]{3,2,1,0:T(8,128)(2,1)S(1)}, u32[]{:S(2)}, u32[]{:S(2)}) async-start(bf16[16,3,160,128]{3,2,1,0:T(8,128)(2,1)} %get-tuple-element.14), calls=%async_computation | async-start | bytes 3932160 | tf_op jit(solution)/shard_map/all_to_all | solution.py:424
  12.1 0.0 copy-done.10
  12.1 0.1 copy.8.coeff_ref
  12.2 0.0 copy-done.8
  12.2 0.0 copy-start.3
  12.2 1.8 copy-done.3
  14.1 2.4 %sum_pairs.1.here_ref = f32[18,2,1280]{2,1,0:T(2,128)S(1)} custom-call(f32[32,2]{1,0:T(8,128)S(1)} %copy.8.coeff_ref, f32[8,128]{1,0:T(8,128)S(1)} %copy-done.8, bf16[32,18,2,1280]{3,2,1,0:T(2,128)(2,1)S(1)} %copy-done.3), custom_call_target="tpu_custom_call" | custom-call | flops 5898240 | bytes 2949120 | tf_op jit(solution)/shard_map/sum_pairs/pallas_call | solution.py:259
  16.4 1.6 collective-permute-start
  18.0 5.2 %collective-permute-done.rest_0_.there_ref = f32[18,2,1280]{2,1,0:T(2,128)S(1)} collective-permute-done((f32[18,2,1280]{2,1,0:T(2,128)S(1)}, f32[18,2,1280]{2,1,0:T(2,128)S(1)}, u32[]{:S(2)}, u32[]{:S(2)}) %collective-permute-start) | collective-permute-done | bytes 184352 | tf_op jit(solution)/shard_map/ppermute | solution.py:443
  23.2 0.0 copy-start.5
  23.2 0.7 copy-done.5
  23.9 5.8 %weigh.3 = (bf16[16,3,160,128]{3,2,1,0:T(8,128)(2,1)}, f32[8,128]{1,0:T(8,128)}) custom-call(s32[1]{0:T(128)} %bitcast.me_ref, f32[1,160]{1,0:T(1,128)} %bitcast.4, bf16[3,160,32,128]{3,2,1,0:T(8,128)(2,1)} %tendency_ref.3, f32[18,2,1280]{2,1,0:T(2,128)} %copy-done.5), custom_call_target="tpu_custom_call" | custom-call | flops 503316480 | bytes 5898240 | tf_op jit(solution)/shard_map/weigh/pallas_call | solution.py:97
  29.7 25.5 %all-to-all-done.rest_0_ = bf16[16,3,160,128]{3,2,1,0:T(8,128)(2,1)S(1)} async-done(((bf16[16,3,160,128]{3,2,1,0:T(8,128)(2,1)}), bf16[16,3,160,128]{3,2,1,0:T(8,128)(2,1)S(1)}, u32[]{:S(2)}, u32[]{:S(2)}) %all-to-all-start) | async-done | bytes 1966112 | tf_op jit(solution)/shard_map/all_to_all | solution.py:424
  55.2 0.0 copy-start.1
  55.2 1.3 copy-done.1
  56.5 0.0 copy-start
  56.5 0.0 copy-start.7
  56.5 0.0 copy-start.9
  56.5 6.6 %all-to-all-start.2 = ((bf16[16,3,160,128]{3,2,1,0:T(8,128)(2,1)}), bf16[16,3,160,128]{3,2,1,0:T(8,128)(2,1)}, u32[]{:S(2)}, u32[]{:S(2)}) async-start(bf16[16,3,160,128]{3,2,1,0:T(8,128)(2,1)} %get-tuple-element.17), calls=%async_computation.2 | async-start | bytes 3932160 | tf_op jit(solution)/shard_map/all_to_all | solution.py:424
  63.1 0.0 copy-done
  63.1 0.0 copy-done.7
  63.1 0.0 copy-done.9
  63.1 0.0 copy-start.2
  63.1 1.5 copy-done.2
  64.6 0.0 copy-start.6
  64.6 6.9 %analyse.2.own_ref = bf16[3,128,1280]{2,1,0:T(8,128)(2,1)S(1)} custom-call(s32[1]{0:T(128)} %bitcast.me_ref, s32[2]{0:T(128)S(1)} %copy-done.9, f32[8,128]{1,0:T(8,128)S(1)} %copy-done.7, bf16[2,1280,2560]{2,1,0:T(8,128)(2,1)} %table_ref.7, bf16[3,2,128,1280]{3,2,1,0:T(8,128)(2,1)S(1)} %copy-done, bf16[16,3,160,128]{3,2,1,0:T(8,128)(2,1)S(1)} %copy-done.2), custom_call_target="tpu_custom_call" | custom-call | flops 2516582400 | bytes 6553600 | tf_op jit(solution)/shard_map/analyse/pallas_call | solution.py:207
  71.5 1.6 collective-permute-start.1
  73.1 22.4 %collective-permute-done.1.other_ref = bf16[3,128,1280]{2,1,0:T(8,128)(2,1)} collective-permute-done((bf16[3,128,1280]{2,1,0:T(8,128)(2,1)S(1)}, bf16[3,128,1280]{2,1,0:T(8,128)(2,1)}, u32[]{:S(2)}, u32[]{:S(2)}) %collective-permute-start.1) | collective-permute-done | bytes 983072 | tf_op jit(solution)/shard_map/ppermute | solution.py:454
  95.5 0.0 copy-done.6
  95.5 7.5 %synthesise.2 = (bf16[16,3,160,128]{3,2,1,0:T(8,128)(2,1)S(1)}, f32[8,128]{1,0:T(8,128)S(1)}) custom-call(s32[1]{0:T(128)} %bitcast.me_ref, f32[1]{0:T(128)} %bitcast.1.sign_ref, f32[18,2,1280]{2,1,0:T(2,128)S(1)} %sum_pairs.1.here_ref, f32[18,2,1280]{2,1,0:T(2,128)S(1)} %copy-done.6, bf16[3,128,1280]{2,1,0:T(8,128)(2,1)S(1)} %analyse.2.own_ref, ...), custom_call_target="tpu_custom_call" | custom-call | flops 2516582400 | bytes 6553600 | tf_op jit(solution)/shard_map/synthesise/pallas_call | solution.py:331
  103.1 0.0 copy-start.4
  103.1 1.3 copy-done.4
  104.3 1.8 all-to-all-done.2.rest_0_
  106.1 6.6 %all-to-all-start.1 = ((bf16[16,3,160,128]{3,2,1,0:T(8,128)(2,1)}), bf16[16,3,160,128]{3,2,1,0:T(8,128)(2,1)}, u32[]{:S(2)}, u32[]{:S(2)}) async-start(bf16[16,3,160,128]{3,2,1,0:T(8,128)(2,1)} %copy-done.4), calls=%async_computation.1 | async-start | bytes 3932160 | tf_op jit(solution)/shard_map/all_to_all | solution.py:424
  112.7 5.9 %analyse.3.own_ref = bf16[3,128,640]{2,1,0:T(8,128)(2,1)S(1)} custom-call(s32[1]{0:T(128)} %bitcast.me_ref, s32[2]{0:T(128)S(1)} %copy-done.9, f32[8,128]{1,0:T(8,128)S(1)} %get-tuple-element.16.token_ref, bf16[2,1280,2560]{2,1,0:T(8,128)(2,1)} %table_ref.7, bf16[3,2,128,1280]{3,2,1,0:T(8,128)(2,1)S(1)} %copy-done, ...), custom_call_target="tpu_custom_call" | custom-call | flops 1258291200 | bytes 3276800 | tf_op jit(solution)/shard_map/analyse/pallas_call | solution.py:207
  118.6 1.6 collective-permute-start.2
  120.2 11.8 %collective-permute-done.2.other_ref = bf16[3,128,640]{2,1,0:T(8,128)(2,1)S(1)} collective-permute-done((bf16[3,128,640]{2,1,0:T(8,128)(2,1)S(1)}, bf16[3,128,640]{2,1,0:T(8,128)(2,1)S(1)}, u32[]{:S(2)}, u32[]{:S(2)}) %collective-permute-start.2) | collective-permute-done | bytes 491552 | tf_op jit(solution)/shard_map/ppermute | solution.py:454
  131.9 5.3 %synthesise.3 = (bf16[16,3,160,128]{3,2,1,0:T(8,128)(2,1)S(1)}, f32[8,128]{1,0:T(8,128)}) custom-call(s32[1]{0:T(128)} %bitcast.me_ref, f32[1]{0:T(128)} %bitcast.1.sign_ref, f32[18,2,1280]{2,1,0:T(2,128)S(1)} %sum_pairs.1.here_ref, f32[18,2,1280]{2,1,0:T(2,128)S(1)} %copy-done.6, bf16[3,128,640]{2,1,0:T(8,128)(2,1)S(1)} %analyse.3.own_ref, ...), custom_call_target="tpu_custom_call" | custom-call | flops 1258291200 | bytes 3276800 | tf_op jit(solution)/shard_map/synthesise/pallas_call | solution.py:331
  137.3 18.5 %all-to-all-done.1.rest_0_ = bf16[16,3,160,128]{3,2,1,0:T(8,128)(2,1)} async-done(((bf16[16,3,160,128]{3,2,1,0:T(8,128)(2,1)}), bf16[16,3,160,128]{3,2,1,0:T(8,128)(2,1)}, u32[]{:S(2)}, u32[]{:S(2)}) %all-to-all-start.1) | async-done | bytes 1966112 | tf_op jit(solution)/shard_map/all_to_all | solution.py:424
  155.8 51.1 %all_to_all.20.rest_1_ = bf16[16,3,160,128]{3,2,1,0:T(8,128)(2,1)S(1)} all-to-all(bf16[16,3,160,128]{3,2,1,0:T(8,128)(2,1)S(1)} %get-tuple-element.18), channel_id=1, replica_groups=mesh['pole'=2,'wave'=16] {'wave'}, dimensions={0} | all-to-all | bytes 3932160 | tf_op jit(solution)/shard_map/all_to_all | solution.py:424
  206.8 5.9 %assemble.1 = bf16[3,160,32,128]{3,2,1,0:T(8,128)(2,1)} custom-call(s32[1]{0:T(128)} %bitcast.me_ref, bf16[16,3,160,128]{3,2,1,0:T(8,128)(2,1)} %all-to-all-done.1.rest_0_, bf16[16,3,160,128]{3,2,1,0:T(8,128)(2,1)S(1)} %all_to_all.20.rest_1_), custom_call_target="tpu_custom_call" | custom-call | flops 1006632960 | bytes 7864320 | tf_op jit(solution)/shard_map/assemble/pallas_call | solution.py:393
Async XLA Ops:
  5.7 6.4 %copy-start.10 = (f32[32,2]{0,1:T(2,128)S(1)}, f32[32,2]{0,1:T(2,128)}, u32[]{:S(2)}) copy-start(f32[32,2]{0,1:T(2,128)} %param.12) | copy-start | bytes 772
  5.7 6.5 %copy-start.8 = (f32[8,128]{1,0:T(8,128)S(1)}, f32[8,128]{1,0:T(8,128)}, u32[]{:S(2)}) copy-start(f32[8,128]{1,0:T(8,128)} %get-tuple-element.12.token_ref) | copy-start | bytes 12292
  5.7 49.5 %all-to-all-start = ((bf16[16,3,160,128]{3,2,1,0:T(8,128)(2,1)}), bf16[16,3,160,128]{3,2,1,0:T(8,128)(2,1)S(1)}, u32[]{:S(2)}, u32[]{:S(2)}) async-start(bf16[16,3,160,128]{3,2,1,0:T(8,128)(2,1)} %get-tuple-element.14), calls=%async_computation | async-start | bytes 3932160 | tf_op jit(solution)/shard_map/all_to_all | solution.py:424
  12.2 1.8 copy-start.3
  16.4 6.8 %collective-permute-start = (f32[18,2,1280]{2,1,0:T(2,128)S(1)}, f32[18,2,1280]{2,1,0:T(2,128)S(1)}, u32[]{:S(2)}, u32[]{:S(2)}) collective-permute-start(f32[18,2,1280]{2,1,0:T(2,128)S(1)} %sum_pairs.1.here_ref), channel_id=1, source_target_pairs={{0,16},{16,0},{1,17},{17,1},{2,18},{18,2},{3,19},{19,3},{4,20},{20... | collective-permute-start | bytes 552968 | tf_op jit(solution)/shard_map/ppermute | solution.py:443
  23.2 0.7 copy-start.5
  55.2 1.3 copy-start.1
  56.5 6.6 %copy-start = (bf16[3,2,128,1280]{3,2,1,0:T(8,128)(2,1)S(1)}, bf16[3,2,128,1280]{3,2,1,0:T(8,128)(2,1)}, u32[]{:S(2)}) copy-start(bf16[3,2,128,1280]{3,2,1,0:T(8,128)(2,1)} %state_ref.3) | copy-start | bytes 5898244
  56.5 6.6 %copy-start.7 = (f32[8,128]{1,0:T(8,128)S(1)}, f32[8,128]{1,0:T(8,128)}, u32[]{:S(2)}) copy-start(f32[8,128]{1,0:T(8,128)} %get-tuple-element.13.token_ref) | copy-start | bytes 12292
  56.5 6.6 %copy-start.9 = (s32[2]{0:T(128)S(1)}, s32[2]{0:T(128)}, u32[]{:S(2)}) copy-start(s32[2]{0:T(128)} %wave_ref.3) | copy-start | bytes 28
  56.5 49.7 %all-to-all-start.2 = ((bf16[16,3,160,128]{3,2,1,0:T(8,128)(2,1)}), bf16[16,3,160,128]{3,2,1,0:T(8,128)(2,1)}, u32[]{:S(2)}, u32[]{:S(2)}) async-start(bf16[16,3,160,128]{3,2,1,0:T(8,128)(2,1)} %get-tuple-element.17), calls=%async_computation.2 | async-start | bytes 3932160 | tf_op jit(solution)/shard_map/all_to_all | solution.py:424
  63.1 1.5 copy-start.2
  64.6 30.9 %copy-start.6 = (f32[18,2,1280]{2,1,0:T(2,128)S(1)}, f32[18,2,1280]{2,1,0:T(2,128)}, u32[]{:S(2)}) copy-start(f32[18,2,1280]{2,1,0:T(2,128)} %copy-done.5) | copy-start | bytes 552964
  71.5 24.0 %collective-permute-start.1 = (bf16[3,128,1280]{2,1,0:T(8,128)(2,1)S(1)}, bf16[3,128,1280]{2,1,0:T(8,128)(2,1)}, u32[]{:S(2)}, u32[]{:S(2)}) collective-permute-start(bf16[3,128,1280]{2,1,0:T(8,128)(2,1)S(1)} %analyse.2.own_ref), channel_id=1, source_target_pairs={{0,16},{16,0},{1,17},{17,1},{2,18},{18,2},{3,19},{19,3},{4,20},{20... | collective-permute-start | bytes 2949128 | tf_op jit(solution)/shard_map/ppermute | solution.py:454
  103.1 1.3 copy-start.4
  106.1 49.6 %all-to-all-start.1 = ((bf16[16,3,160,128]{3,2,1,0:T(8,128)(2,1)}), bf16[16,3,160,128]{3,2,1,0:T(8,128)(2,1)}, u32[]{:S(2)}, u32[]{:S(2)}) async-start(bf16[16,3,160,128]{3,2,1,0:T(8,128)(2,1)} %copy-done.4), calls=%async_computation.1 | async-start | bytes 3932160 | tf_op jit(solution)/shard_map/all_to_all | solution.py:424
  118.6 13.3 %collective-permute-start.2 = (bf16[3,128,640]{2,1,0:T(8,128)(2,1)S(1)}, bf16[3,128,640]{2,1,0:T(8,128)(2,1)S(1)}, u32[]{:S(2)}, u32[]{:S(2)}) collective-permute-start(bf16[3,128,640]{2,1,0:T(8,128)(2,1)S(1)} %analyse.3.own_ref), channel_id=1, source_target_pairs={{0,16},{16,0},{1,17},{17,1},{2,18},{18,2},{3,19},{19,3},{4,20},{20... | collective-permute-start | bytes 1474568 | tf_op jit(solution)/shard_map/ppermute | solution.py:454

commit v8 on v7

--- a/solution.py
+++ b/solution.py
@@ -3,6 +3,7 @@
 
 import jax
 import jax.numpy as jnp
+import numpy as np
 from jax import lax
 from jax.experimental import pallas as pl
 from jax.experimental.pallas import tpu as pltpu
@@ -11,7 +12,7 @@
 BF16 = jnp.bfloat16
 F32 = jnp.float32
 CORES = 2
-PERMUTED = ()
+PERMUTED = (0, 1)
 ANYWHERE = pl.BlockSpec(memory_space=pl.ANY)
 IN_SMEM = pl.BlockSpec(memory_space=pltpu.SMEM)
 TOKEN = jax.ShapeDtypeStruct((8, 128), F32)
@@ -40,29 +41,35 @@
 
 
 def swap_matrix(rows, columns, picked):
-    width = rows * columns
-    target = lax.broadcasted_iota(jnp.int32, (len(picked) * rows, width), 0)
-    source = lax.broadcasted_iota(jnp.int32, (len(picked) * rows, width), 1)
-    step = picked[1] - picked[0] if len(picked) > 1 else 1
-    column = (target // rows) * step + picked[0]
-    return (source == (target % rows) * columns + column).astype(BF16)
-
-
-def weigh_kernel(slot, local_slots, permuted, waits, me_ref, gauss_ref, tendency_ref, *rest):
+    matrix = np.zeros((len(picked), rows, rows, columns), np.float32)
+    for i, c in enumerate(picked):
+        matrix[i, np.arange(rows), np.arange(rows), c] = 1.0
+    return jnp.asarray(matrix.reshape(len(picked) * rows, rows * columns), BF16)
+
+
+def weigh_kernel(slot, local_slots, permuted, waits, me_ref, matrix_ref, gauss_ref, tendency_ref, *rest):
     _, lats, slots, members = tendency_ref.shape
-    rest = rest[waits:]
+    rest, column = rest[waits:-1], rest[-1]
     first = pl.program_id(1) * lats
     outs, blocks = (rest[:-1], rest[-1]) if permuted else (rest, None)
     outs, token_ref = outs[:-1], outs[-1]
     token_ref[...] = jnp.zeros_like(token_ref)
     depth, breadth = math.gcd(lats, 16), 16
-    matrix = swap_matrix(depth, breadth, range(slot, breadth, local_slots))
+    matrix = matrix_ref[...]
     owners = breadth // local_slots
+
+    @pl.when((pl.program_id(0) == 0) & (pl.program_id(1) == 0))
+    def _():
+        total = gauss_ref.shape[1]
+        for j in range(0, total, depth):
+            line = jnp.broadcast_to(gauss_ref[...], (depth, total))
+            here = lax.broadcasted_iota(jnp.int32, line.shape, 0) + j
+            mine = lax.broadcasted_iota(jnp.int32, line.shape, 1) == here
+            value = jnp.sum(jnp.where(mine, line, 0.0), axis=1, keepdims=True)
+            column[j : j + depth, :] = jnp.broadcast_to(value, (depth, members))
+
     for j in range(0, lats, depth):
-        line = jnp.broadcast_to(gauss_ref[...], (depth, gauss_ref.shape[1]))
-        here = lax.broadcasted_iota(jnp.int32, line.shape, 0) + (first + j)
-        mine = lax.broadcasted_iota(jnp.int32, line.shape, 1) == here
-        scale = jnp.sum(jnp.where(mine, line, 0.0), axis=1, keepdims=True)
+        scale = column[pl.ds(pl.multiple_of(first + j, depth), depth), :]
         for s in range(0, slots, 2 * breadth):
             halves = [
                 tendency_ref[0, j : j + depth, s + h : s + h + breadth, :].reshape(depth * breadth, members)
@@ -91,6 +98,7 @@
 def weigh(tendency, gauss, me, slot, local_slots, permuted, waits):
     rows, lats, slots, members = tendency.shape
     each = lat_block(lats)
+    matrix = swap_matrix(math.gcd(each, 16), 16, range(slot, 16, local_slots))
     owners = slots // local_slots
     count, chips = (CORES, owners // CORES) if permuted else (owners, 1)
     piece = pl.BlockSpec((count, 1, each, members), lambda r, j, m: (0, r, j, 0))
@@ -105,14 +113,16 @@
             num_scalar_prefetch=1,
             grid=(rows, lats // each),
             in_specs=[
+                pl.BlockSpec(matrix.shape, lambda r, j, m: (0, 0)),
                 pl.BlockSpec((1, lats), lambda r, j, m: (0, 0)),
                 pl.BlockSpec((1, each, slots, members), lambda r, j, m: (r, j, 0, 0)),
             ]
             + [ANYWHERE] * len(waits),
             out_specs=[piece] * chips + [pl.BlockSpec(TOKEN.shape, lambda r, j, m: (0, 0))],
-            scratch_shapes=[pltpu.VMEM((owners, each, members), BF16)] if permuted else [],
+            scratch_shapes=([pltpu.VMEM((owners, each, members), BF16)] if permuted else [])
+            + [pltpu.VMEM((lats, members), F32)],
         ),
-    )(me, gauss, tendency, *waits)
+    )(me, matrix, gauss, tendency, *waits)
 
 
 def pick_kernel(waits, me_ref, *rest):
@@ -349,7 +359,7 @@
     )(me, sign, here, there, own, other, table)
 
 
-def assemble_kernel(counts, me_ref, *rest):
+def assemble_kernel(counts, me_ref, matrix_ref, *rest):
     ins, out, blocks = rest[: sum(counts)], rest[sum(counts)], rest[sum(counts) + 1 :]
     _, lats, slots, members = out.shape
     local_slots = len(counts)
@@ -366,7 +376,7 @@
         views.append(lambda owner, j, ref=blocks[spare]: ref[owner, j, :])
         spare += 1
     depth, breadth = math.gcd(lats, 16), 16
-    matrix = swap_matrix(breadth, depth, range(depth))
+    matrix = matrix_ref[...]
     for start in range(0, lats, depth):
         j = slice(start, start + depth)
         for s in range(0, slots, 2 * breadth):
@@ -388,6 +398,7 @@
     owners = max(len(p) * p[0].shape[0] for p in pieces)
     slots = local_slots * owners
     each = lat_block(lats)
+    matrix = swap_matrix(16, math.gcd(each, 16), range(math.gcd(each, 16)))
     flat = [block for slot in pieces for block in slot]
     moved = sum(len(p) > 1 for p in pieces)
     return call(
@@ -399,13 +410,14 @@
         grid_spec=pltpu.PrefetchScalarGridSpec(
             num_scalar_prefetch=1,
             grid=(rows, lats // each),
-            in_specs=[
+            in_specs=[pl.BlockSpec(matrix.shape, lambda r, j, m: (0, 0))]
+            + [
                 pl.BlockSpec((block.shape[0], 1, each, members), lambda r, j, m: (0, r, j, 0)) for block in flat
             ],
             out_specs=pl.BlockSpec((1, each, slots, members), lambda r, j, m: (r, j, 0, 0)),
             scratch_shapes=[pltpu.VMEM((owners, each, members), BF16)] * moved,
         ),
-    )(me, *flat)
+    )(me, matrix, *flat)
 
 
 def between_chips(messages):

time: 215 us -> 253 us (1.18)
  waiting for transfers between devices: 85.2 us -> 144 us
  blocking collectives: 51.1 us -> 0 us
  starting transfers between devices: 24.3 us -> 44.5 us
  Pallas kernels: 45.5 us -> 58 us
    ppermute x0 -> x32, waiting for transfers between devices: none -> 127 us  [the longest x28 122 us: between_chips(): lax.ppermute(messages[k], 'wave', [(d, d ^ k * CORES) for d in range(chip...]
    all_to_all x1 -> x0, blocking collectives: 51.1 us -> none  [to_all(): lax.all_to_all(blocks, 'wave', split_axis=0, concat_axis=0, tiled=True)]
    all_to_all x3 -> x0, waiting for transfers between devices: 45.8 us -> none  [to_all(): lax.all_to_all(blocks, 'wave', split_axis=0, concat_axis=0, tiled=True)]
    ppermute x0 -> x32, starting transfers between devices: none -> 40.8 us  [the longest x28 40.5 us: between_chips(): lax.ppermute(messages[k], 'wave', [(d, d ^ k * CORES) for d in range(chip...]
    all_to_all x3 -> x0, starting transfers between devices: 19.5 us -> none  [to_all(): lax.all_to_all(blocks, 'wave', split_axis=0, concat_axis=0, tiled=True)]
    ppermute x2, waiting for transfers between devices: 34.2 us -> 17.3 us  [per_device(): other = lax.ppermute(forced, 'pole', [(0, 1), (1, 0)])]
    pallas_call x0 -> x4, Pallas kernels: none -> 6.93 us  [the longest x2 3.73 us: pick(): call(functools.partial(pick_kernel, len(waits)), 'pick', 0, 4 * math.prod...]
    pallas_call x2, Pallas kernels: 12.9 us -> 18.6 us  [synthesise(): call(functools.partial(synthesise_kernel, slot, low, chips), 'synthesise'...]
  transfers between devices with their start and end apart: 6 -> 35, of which waited for: 6 -> 23; matrix products, arithmetic and copies ran while one was open for 0% -> 0% of each run, Pallas kernels for 16% -> 12%
where the time goes in v8:
time: 253 us
  waiting for transfers between devices  144 us (57%)
  Pallas kernels  58 us (23%)
  starting transfers between devices  44.5 us (18%)
  local copies, waits for them, and re-layouts  5.75 us (2%)
    ppermute x28, waiting for transfers between devices, between_chips(): lax.ppermute(messages[k], 'wave', [(d, d ^ k * CORES) for d in range(chip...  122 us
    ppermute x28, starting transfers between devices, between_chips(): lax.ppermute(messages[k], 'wave', [(d, d ^ k * CORES) for d in range(chip...  40.5 us
    pallas_call x2, Pallas kernels, synthesise(): call(functools.partial(synthesise_kernel, slot, low, chips), 'synthesise'...  18.6 us
    ppermute x2, waiting for transfers between devices, per_device(): other = lax.ppermute(forced, 'pole', [(0, 1), (1, 0)])  17.3 us
    pallas_call x2, Pallas kernels, analyse(): call(functools.partial(analyse_kernel, slot, low, len(blocks)), 'analyse'...  13.4 us
    pallas_call x2, Pallas kernels, weigh(): call(functools.partial(weigh_kernel, slot, local_slots, permuted, len(wai...  12 us
    unnamed x41, local copies, waits for them, and re-layouts  5.75 us
    ppermute x4, waiting for transfers between devices, between_cores(): return lax.ppermute(blocks, 'wave', [(d, d ^ 1) for d in range(owners)])  5.11 us
  transfers between devices with their start and end apart: 35, of which 23 were waited for; matrix products, arithmetic and copies ran while one was open for 0% of the time, Pallas kernels for 12%

profile of v8, /device:TPU:8, one launch (start us, length us, event | category | flops | bytes accessed | tf_op | source)
XLA Modules:
  0.0 252.6 jit_solution(698887497208401710)
XLA Ops:
  0.0 6.0 %weigh.2 = (bf16[2,3,160,128]{3,2,1,0:T(8,128)(2,1)}, bf16[2,3,160,128]{3,2,1,0:T(8,128)(2,1)}, bf16[2,3,160,128]{3,2,1,0:T(8,128)(2,1)}, bf16[2,3,160,128]{3,2,...) custom-call(s32[1]{0:T(128)} %bitcast.me_ref, ...), custom_call_target="tpu_custom_call" | custom-call | flops 503316480 | bytes 5898240 | tf_op jit(solution)/shard_map/weigh/pallas_call | solution.py:105
  6.1 1.6 collective-permute-start.1
  7.6 0.4 collective-permute-start.2
  8.2 0.7 copy-done.15
  8.9 2.4 sum_pairs.1.rest_0_.here_ref
  11.3 1.6 collective-permute-start
  12.9 1.5 collective-permute-start.3
  14.4 2.6 %collective-permute-start.4 = (bf16[2,3,160,128]{3,2,1,0:T(8,128)(2,1)}, bf16[2,3,160,128]{3,2,1,0:T(8,128)(2,1)S(1)}, u32[]{:S(2)}, u32[]{:S(2)}) collective-permute-start(bf16[2,3,160,128]{3,2,1,0:T(8,128)(2,1)} %get-tuple-element.64), channel_id=1, source_target_pairs={{0,8},{1,9},{2,10},{3,11},{4,12},{5,13},{6,14},{7,15},{8,0},{9,1},... | collective-permute-start | bytes 737288 | tf_op jit(solution)/shard_map/ppermute | solution.py:427
  17.2 2.6 %collective-permute-start.5 = (bf16[2,3,160,128]{3,2,1,0:T(8,128)(2,1)}, bf16[2,3,160,128]{3,2,1,0:T(8,128)(2,1)S(1)}, u32[]{:S(2)}, u32[]{:S(2)}) collective-permute-start(bf16[2,3,160,128]{3,2,1,0:T(8,128)(2,1)} %get-tuple-element.65), channel_id=1, source_target_pairs={{0,10},{1,11},{2,8},{3,9},{4,14},{5,15},{6,12},{7,13},{8,2},{9,3},... | collective-permute-start | bytes 737288 | tf_op jit(solution)/shard_map/ppermute | solution.py:427
  19.7 0.5 collective-permute-start.6
  20.2 2.5 collective-permute-start.7
  22.7 6.0 %weigh.3 = (bf16[2,3,160,128]{3,2,1,0:T(8,128)(2,1)}, bf16[2,3,160,128]{3,2,1,0:T(8,128)(2,1)}, bf16[2,3,160,128]{3,2,1,0:T(8,128)(2,1)}, bf16[2,3,160,128]{3,2,...) custom-call(s32[1]{0:T(128)} %bitcast.me_ref, ...), custom_call_target="tpu_custom_call" | custom-call | flops 503316480 | bytes 5898240 | tf_op jit(solution)/shard_map/weigh/pallas_call | solution.py:105
  28.7 16.0 %collective-permute-done.4.rest_6_.rest_4_ = bf16[2,3,160,128]{3,2,1,0:T(8,128)(2,1)S(1)} collective-permute-done((bf16[2,3,160,128]{3,2,1,0:T(8,128)(2,1)}, bf16[2,3,160,128]{3,2,1,0:T(8,128)(2,1)S(1)}, u32[]{:S(2)}, u32[]{:S(2)}) %collective-permute-start.4) | collective-permute-done | bytes 245792 | tf_op jit(solution)/shard_map/ppermute | solution.py:427
  44.7 5.3 %collective-permute-done.5.rest_7_.rest_5_ = bf16[2,3,160,128]{3,2,1,0:T(8,128)(2,1)S(1)} collective-permute-done((bf16[2,3,160,128]{3,2,1,0:T(8,128)(2,1)}, bf16[2,3,160,128]{3,2,1,0:T(8,128)(2,1)S(1)}, u32[]{:S(2)}, u32[]{:S(2)}) %collective-permute-start.5) | collective-permute-done | bytes 245792 | tf_op jit(solution)/shard_map/ppermute | solution.py:427
  50.0 5.3 %collective-permute-done.6.rest_8_.rest_6_ = bf16[2,3,160,128]{3,2,1,0:T(8,128)(2,1)S(1)} collective-permute-done((bf16[2,3,160,128]{3,2,1,0:T(8,128)(2,1)}, bf16[2,3,160,128]{3,2,1,0:T(8,128)(2,1)S(1)}, u32[]{:S(2)}, u32[]{:S(2)}) %collective-permute-start.6) | collective-permute-done | bytes 245792 | tf_op jit(solution)/shard_map/ppermute | solution.py:427
  55.2 3.7 %collective-permute-done.7.rest_9_.rest_7_ = bf16[2,3,160,128]{3,2,1,0:T(8,128)(2,1)S(1)} collective-permute-done((bf16[2,3,160,128]{3,2,1,0:T(8,128)(2,1)}, bf16[2,3,160,128]{3,2,1,0:T(8,128)(2,1)S(1)}, u32[]{:S(2)}, u32[]{:S(2)}) %collective-permute-start.7) | collective-permute-done | bytes 245792 | tf_op jit(solution)/shard_map/ppermute | solution.py:427
  58.9 0.7 copy-done.13
  59.6 1.8 pick.2
  61.5 2.6 %collective-permute-done.8.rest_8_ = bf16[8,3,160,128]{3,2,1,0:T(8,128)(2,1)S(1)} collective-permute-done((bf16[8,3,160,128]{3,2,1,0:T(8,128)(2,1)S(1)}, bf16[8,3,160,128]{3,2,1,0:T(8,128)(2,1)S(1)}, u32[]{:S(2)}, u32[]{:S(2)}) %collective-permute-start.8) | collective-permute-done | bytes 983072 | tf_op jit(solution)/shard_map/ppermute | solution.py:432
  64.1 0.7 copy-done.14
  64.7 7.8 %analyse.2.own_ref = bf16[3,128,1280]{2,1,0:T(8,128)(2,1)S(1)} custom-call(s32[1]{0:T(128)} %bitcast.me_ref, s32[2]{0:T(128)S(1)} %copy-done.16, f32[8,128]{1,0:T(8,128)S(1)} %copy-done.14, bf16[2,1280,2560]{2,1,0:T(8,128)(2,1)} %table_ref.7, bf16[3,2,128,1280]{3,2,1,0:T(8,128)(2,1)S(1)} %copy-done, bf16[2,3,160,128]{3,2,1,0:T(8,128)(2,1)S(1)} %copy-done.11, ...), custom_call_target="tpu_custom_call" | custom-call | flops 2516582400 | bytes 6553600 | tf_op jit(solution)/shard_map/analyse/pallas_call | solution.py:217
  72.6 0.6 collective-permute-start.9
  73.2 0.9 collective-permute-start.18
  74.0 2.6 %collective-permute-start.20 = (bf16[2,3,160,128]{3,2,1,0:T(8,128)(2,1)}, bf16[2,3,160,128]{3,2,1,0:T(8,128)(2,1)}, u32[]{:S(2)}, u32[]{:S(2)}) collective-permute-start(bf16[2,3,160,128]{3,2,1,0:T(8,128)(2,1)} %get-tuple-element.89), channel_id=1, source_target_pairs={{0,6},{1,7},{2,4},{3,5},{4,2},{5,3},{6,0},{7,1},{8,14},{9,15},{10,... | collective-permute-start | bytes 737288 | tf_op jit(solution)/shard_map/ppermute | solution.py:427
  76.6 2.1 collective-permute-start.21
  78.8 2.3 collective-permute-done.18.rest_3_.rest_1_
  81.1 0.7 copy-done.7
  81.8 7.5 %collective-permute-done.19.rest_4_.rest_2_ = bf16[2,3,160,128]{3,2,1,0:T(8,128)(2,1)S(1)} collective-permute-done((bf16[2,3,160,128]{3,2,1,0:T(8,128)(2,1)S(1)}, bf16[2,3,160,128]{3,2,1,0:T(8,128)(2,1)S(1)}, u32[]{:S(2)}, u32[]{:S(2)}) %collective-permute-start.19) | collective-permute-done | bytes 245792 | tf_op jit(solution)/shard_map/ppermute | solution.py:427
  89.3 0.7 copy-done.9
  90.0 0.8 collective-permute-start.23
  90.8 5.6 %collective-permute-done.9.other_ref = bf16[3,128,1280]{2,1,0:T(8,128)(2,1)S(1)} collective-permute-done((bf16[3,128,1280]{2,1,0:T(8,128)(2,1)S(1)}, bf16[3,128,1280]{2,1,0:T(8,128)(2,1)S(1)}, u32[]{:S(2)}, u32[]{:S(2)}) %collective-permute-start.9) | collective-permute-done | bytes 983072 | tf_op jit(solution)/shard_map/ppermute | solution.py:466
  96.4 0.9 copy-done.4
  97.4 2.7 %collective-permute-start.24 = (bf16[2,3,160,128]{3,2,1,0:T(8,128)(2,1)}, bf16[2,3,160,128]{3,2,1,0:T(8,128)(2,1)}, u32[]{:S(2)}, u32[]{:S(2)}) collective-permute-start(bf16[2,3,160,128]{3,2,1,0:T(8,128)(2,1)} %get-tuple-element.93), channel_id=1, source_target_pairs={{0,14},{1,15},{2,12},{3,13},{4,10},{5,11},{6,8},{7,9},{8,6},{9,7},... | collective-permute-start | bytes 737288 | tf_op jit(solution)/shard_map/ppermute | solution.py:427
  100.1 1.2 copy-done.5
  101.3 10.1 %synthesise.2 = (bf16[2,3,160,128]{3,2,1,0:T(8,128)(2,1)S(1)}, bf16[2,3,160,128]{3,2,1,0:T(8,128)(2,1)S(1)}, bf16[2,3,160,128]{3,2,1,0:T(8,128)(2,1)S(1)}, bf16[...) custom-call(s32[1]{0:T(128)} %bitcast.me_ref, ...), custom_call_target="tpu_custom_call" | custom-call | flops 2516582400 | bytes 6553600 | tf_op jit(solution)/shard_map/synthesise/pallas_call | solution.py:341
  111.4 0.5 collective-permute-done.22.rest_7_.rest_5_
  111.8 6.2 %collective-permute-done.23.rest_8_.rest_6_ = bf16[2,3,160,128]{3,2,1,0:T(8,128)(2,1)} collective-permute-done((bf16[2,3,160,128]{3,2,1,0:T(8,128)(2,1)}, bf16[2,3,160,128]{3,2,1,0:T(8,128)(2,1)}, u32[]{:S(2)}, u32[]{:S(2)}) %collective-permute-start.23) | collective-permute-done | bytes 245792 | tf_op jit(solution)/shard_map/ppermute | solution.py:427
  118.0 3.6 %collective-permute-done.24.rest_9_.rest_7_ = bf16[2,3,160,128]{3,2,1,0:T(8,128)(2,1)} collective-permute-done((bf16[2,3,160,128]{3,2,1,0:T(8,128)(2,1)}, bf16[2,3,160,128]{3,2,1,0:T(8,128)(2,1)}, u32[]{:S(2)}, u32[]{:S(2)}) %collective-permute-start.24) | collective-permute-done | bytes 245792 | tf_op jit(solution)/shard_map/ppermute | solution.py:427
  121.7 1.9 pick.3
  123.7 2.6 %collective-permute-done.25.rest_8_ = bf16[8,3,160,128]{3,2,1,0:T(8,128)(2,1)S(1)} collective-permute-done((bf16[8,3,160,128]{3,2,1,0:T(8,128)(2,1)S(1)}, bf16[8,3,160,128]{3,2,1,0:T(8,128)(2,1)S(1)}, u32[]{:S(2)}, u32[]{:S(2)}) %collective-permute-start.25) | collective-permute-done | bytes 983072 | tf_op jit(solution)/shard_map/ppermute | solution.py:432
  126.3 5.6 %analyse.3.own_ref = bf16[3,128,640]{2,1,0:T(8,128)(2,1)S(1)} custom-call(s32[1]{0:T(128)} %bitcast.me_ref, s32[2]{0:T(128)S(1)} %copy-done.16, f32[8,128]{1,0:T(8,128)S(1)} %get-tuple-element.85.rest_0_.token_ref, bf16[2,1280,2560]{2,1,0:T(8,128)(2,1)} %table_ref.7, bf16[3,2,128,1280]{3,2,1,0:T(8,128)(2,1)S(1)} %copy-done, ...), custom_call_target="tpu_custom_call" | custom-call | flops 1258291200 | bytes 3276800 | tf_op jit(solution)/shard_map/analyse/pallas_call | solution.py:217
  131.8 1.6 collective-permute-start.26
  133.4 11.7 %collective-permute-done.26.other_ref = bf16[3,128,640]{2,1,0:T(8,128)(2,1)S(1)} collective-permute-done((bf16[3,128,640]{2,1,0:T(8,128)(2,1)S(1)}, bf16[3,128,640]{2,1,0:T(8,128)(2,1)S(1)}, u32[]{:S(2)}, u32[]{:S(2)}) %collective-permute-start.26) | collective-permute-done | bytes 491552 | tf_op jit(solution)/shard_map/ppermute | solution.py:466
  145.2 8.6 %synthesise.3 = (bf16[2,3,160,128]{3,2,1,0:T(8,128)(2,1)S(1)}, bf16[2,3,160,128]{3,2,1,0:T(8,128)(2,1)S(1)}, bf16[2,3,160,128]{3,2,1,0:T(8,128)(2,1)S(1)}, bf16[...) custom-call(s32[1]{0:T(128)} %bitcast.me_ref, ...), custom_call_target="tpu_custom_call" | custom-call | flops 1258291200 | bytes 3276800 | tf_op jit(solution)/shard_map/synthesise/pallas_call | solution.py:341
  153.8 1.6 pair.2
  155.5 1.6 collective-permute-start.11
  157.0 2.0 collective-permute-start.13
  159.0 0.9 collective-permute-start.14
  159.9 2.9 %collective-permute-start.15 = (bf16[2,3,160,128]{3,2,1,0:T(8,128)(2,1)S(1)}, bf16[2,3,160,128]{3,2,1,0:T(8,128)(2,1)S(1)}, u32[]{:S(2)}, u32[]{:S(2)}) collective-permute-start(bf16[2,3,160,128]{3,2,1,0:T(8,128)(2,1)S(1)} %get-tuple-element.82), channel_id=1, source_target_pairs={{0,10},{1,11},{2,8},{3,9},{4,14},{5,15},{6,12},{7,13},{8,2},{9,3},... | collective-permute-start | bytes 737288 | tf_op jit(solution)/shard_map/ppermute | solution.py:427
  162.9 1.6 pair.3
  164.5 1.5 collective-permute-start.16
  166.0 7.2 %collective-permute-done.12.rest_2_ = bf16[2,3,160,128]{3,2,1,0:T(8,128)(2,1)S(1)} collective-permute-done((bf16[2,3,160,128]{3,2,1,0:T(8,128)(2,1)S(1)}, bf16[2,3,160,128]{3,2,1,0:T(8,128)(2,1)S(1)}, u32[]{:S(2)}, u32[]{:S(2)}) %collective-permute-start.12) | collective-permute-done | bytes 245792 | tf_op jit(solution)/shard_map/ppermute | solution.py:427
  173.2 4.8 %collective-permute-done.13.rest_3_ = bf16[2,3,160,128]{3,2,1,0:T(8,128)(2,1)S(1)} collective-permute-done((bf16[2,3,160,128]{3,2,1,0:T(8,128)(2,1)S(1)}, bf16[2,3,160,128]{3,2,1,0:T(8,128)(2,1)S(1)}, u32[]{:S(2)}, u32[]{:S(2)}) %collective-permute-start.13) | collective-permute-done | bytes 245792 | tf_op jit(solution)/shard_map/ppermute | solution.py:427
  178.1 3.9 %collective-permute-start.29 = (bf16[2,3,160,128]{3,2,1,0:T(8,128)(2,1)S(1)}, bf16[2,3,160,128]{3,2,1,0:T(8,128)(2,1)S(1)}, u32[]{:S(2)}, u32[]{:S(2)}) collective-permute-start(bf16[2,3,160,128]{3,2,1,0:T(8,128)(2,1)S(1)} %get-tuple-element.105), channel_id=1, source_target_pairs={{0,4},{1,5},{2,6},{3,7},{4,0},{5,1},{6,2},{7,3},{8,12},{9,13},{10,... | collective-permute-start | bytes 737288 | tf_op jit(solution)/shard_map/ppermute | solution.py:427
  182.0 10.7 %collective-permute-done.15.rest_5_ = bf16[2,3,160,128]{3,2,1,0:T(8,128)(2,1)S(1)} collective-permute-done((bf16[2,3,160,128]{3,2,1,0:T(8,128)(2,1)S(1)}, bf16[2,3,160,128]{3,2,1,0:T(8,128)(2,1)S(1)}, u32[]{:S(2)}, u32[]{:S(2)}) %collective-permute-start.15) | collective-permute-done | bytes 245792 | tf_op jit(solution)/shard_map/ppermute | solution.py:427
  192.7 3.4 %collective-permute-start.30 = (bf16[2,3,160,128]{3,2,1,0:T(8,128)(2,1)S(1)}, bf16[2,3,160,128]{3,2,1,0:T(8,128)(2,1)S(1)}, u32[]{:S(2)}, u32[]{:S(2)}) collective-permute-start(bf16[2,3,160,128]{3,2,1,0:T(8,128)(2,1)S(1)} %get-tuple-element.106), channel_id=1, source_target_pairs={{0,6},{1,7},{2,4},{3,5},{4,2},{5,3},{6,0},{7,1},{8,14},{9,15},{10,... | collective-permute-start | bytes 737288 | tf_op jit(solution)/shard_map/ppermute | solution.py:427
  196.0 2.9 %collective-permute-done.16.rest_6_ = bf16[2,3,160,128]{3,2,1,0:T(8,128)(2,1)S(1)} collective-permute-done((bf16[2,3,160,128]{3,2,1,0:T(8,128)(2,1)S(1)}, bf16[2,3,160,128]{3,2,1,0:T(8,128)(2,1)S(1)}, u32[]{:S(2)}, u32[]{:S(2)}) %collective-permute-start.16) | collective-permute-done | bytes 245792 | tf_op jit(solution)/shard_map/ppermute | solution.py:427
  199.0 16.7 %collective-permute-done.17.rest_7_ = bf16[2,3,160,128]{3,2,1,0:T(8,128)(2,1)S(1)} collective-permute-done((bf16[2,3,160,128]{3,2,1,0:T(8,128)(2,1)S(1)}, bf16[2,3,160,128]{3,2,1,0:T(8,128)(2,1)S(1)}, u32[]{:S(2)}, u32[]{:S(2)}) %collective-permute-start.17) | collective-permute-done | bytes 245792 | tf_op jit(solution)/shard_map/ppermute | solution.py:427
  215.7 3.4 %collective-permute-start.34 = (bf16[2,3,160,128]{3,2,1,0:T(8,128)(2,1)S(1)}, bf16[2,3,160,128]{3,2,1,0:T(8,128)(2,1)S(1)}, u32[]{:S(2)}, u32[]{:S(2)}) collective-permute-start(bf16[2,3,160,128]{3,2,1,0:T(8,128)(2,1)S(1)} %get-tuple-element.110), channel_id=1, source_target_pairs={{0,14},{1,15},{2,12},{3,13},{4,10},{5,11},{6,8},{7,9},{8,6},{9,7},... | collective-permute-start | bytes 737288 | tf_op jit(solution)/shard_map/ppermute | solution.py:427
  219.2 12.3 %collective-permute-done.31.rest_12_ = bf16[2,3,160,128]{3,2,1,0:T(8,128)(2,1)S(1)} collective-permute-done((bf16[2,3,160,128]{3,2,1,0:T(8,128)(2,1)S(1)}, bf16[2,3,160,128]{3,2,1,0:T(8,128)(2,1)S(1)}, u32[]{:S(2)}, u32[]{:S(2)}) %collective-permute-start.31) | collective-permute-done | bytes 245792 | tf_op jit(solution)/shard_map/ppermute | solution.py:427
  231.5 5.3 %collective-permute-done.32.rest_13_ = bf16[2,3,160,128]{3,2,1,0:T(8,128)(2,1)S(1)} collective-permute-done((bf16[2,3,160,128]{3,2,1,0:T(8,128)(2,1)S(1)}, bf16[2,3,160,128]{3,2,1,0:T(8,128)(2,1)S(1)}, u32[]{:S(2)}, u32[]{:S(2)}) %collective-permute-start.32) | collective-permute-done | bytes 245792 | tf_op jit(solution)/shard_map/ppermute | solution.py:427
  236.8 6.8 %collective-permute-done.33.rest_14_ = bf16[2,3,160,128]{3,2,1,0:T(8,128)(2,1)S(1)} collective-permute-done((bf16[2,3,160,128]{3,2,1,0:T(8,128)(2,1)S(1)}, bf16[2,3,160,128]{3,2,1,0:T(8,128)(2,1)S(1)}, u32[]{:S(2)}, u32[]{:S(2)}) %collective-permute-start.33) | collective-permute-done | bytes 245792 | tf_op jit(solution)/shard_map/ppermute | solution.py:427
  243.5 4.4 %collective-permute-done.34.rest_15_ = bf16[2,3,160,128]{3,2,1,0:T(8,128)(2,1)S(1)} collective-permute-done((bf16[2,3,160,128]{3,2,1,0:T(8,128)(2,1)S(1)}, bf16[2,3,160,128]{3,2,1,0:T(8,128)(2,1)S(1)}, u32[]{:S(2)}, u32[]{:S(2)}) %collective-permute-start.34) | collective-permute-done | bytes 245792 | tf_op jit(solution)/shard_map/ppermute | solution.py:427
  248.0 4.7 %assemble.1 = bf16[3,160,32,128]{3,2,1,0:T(8,128)(2,1)} custom-call(s32[1]{0:T(128)} %bitcast.me_ref, bf16[256,256]{1,0:T(8,128)(2,1)S(1)} %copy-done.12, bf16[2,3,160,128]{3,2,1,0:T(8,128)(2,1)S(1)} %get-tuple-element.77.rest_0_, bf16[2,3,160,128]{3,2,1,0:T(8,128)(2,1)S(1)} %collective-permute-done.11.rest_1_, ...), custom_call_target="tpu_custom_call" | custom-call | flops 1006632960 | bytes 7864320 | tf_op jit(solution)/shard_map/assemble/pallas_call | solution.py:404
  (59 shorter events, 0.7 us)
Async XLA Ops:
  0.0 8.1 %copy-start.17 = (f32[32,2]{0,1:T(2,128)S(1)}, f32[32,2]{0,1:T(2,128)}, u32[]{:S(2)}) copy-start(f32[32,2]{0,1:T(2,128)} %param.15) | copy-start | bytes 772
  0.0 8.2 %copy-start.3 = (bf16[32,18,2,1280]{3,2,1,0:T(2,128)(2,1)S(1)}, bf16[32,18,2,1280]{3,2,1,0:T(2,128)(2,1)}, u32[]{:S(2)}) copy-start(bf16[32,18,2,1280]{3,2,1,0:T(2,128)(2,1)} %inverse_ref.1) | copy-start | bytes 8847364
  6.1 13.7 %collective-permute-start.1 = (bf16[2,3,160,128]{3,2,1,0:T(8,128)(2,1)}, bf16[2,3,160,128]{3,2,1,0:T(8,128)(2,1)}, u32[]{:S(2)}, u32[]{:S(2)}) collective-permute-start(bf16[2,3,160,128]{3,2,1,0:T(8,128)(2,1)} %get-tuple-element.61), channel_id=1, source_target_pairs={{0,2},{1,3},{2,0},{3,1},{4,6},{5,7},{6,4},{7,5},{8,10},{9,11},{10,... | collective-permute-start | bytes 737288 | tf_op jit(solution)/shard_map/ppermute | solution.py:427
  7.6 12.5 %collective-permute-start.2 = (bf16[2,3,160,128]{3,2,1,0:T(8,128)(2,1)}, bf16[2,3,160,128]{3,2,1,0:T(8,128)(2,1)}, u32[]{:S(2)}, u32[]{:S(2)}) collective-permute-start(bf16[2,3,160,128]{3,2,1,0:T(8,128)(2,1)} %get-tuple-element.62), channel_id=1, source_target_pairs={{0,4},{1,5},{2,6},{3,7},{4,0},{5,1},{6,2},{7,3},{8,12},{9,13},{10,... | collective-permute-start | bytes 737288 | tf_op jit(solution)/shard_map/ppermute | solution.py:427
  8.2 50.8 %copy-start.11 = (bf16[2,3,160,128]{3,2,1,0:T(8,128)(2,1)S(1)}, bf16[2,3,160,128]{3,2,1,0:T(8,128)(2,1)}, u32[]{:S(2)}) copy-start(bf16[2,3,160,128]{3,2,1,0:T(8,128)(2,1)} %get-tuple-element.60.rest_2_.rest_0_) | copy-start | bytes 737284
  8.2 0.7 copy-start.15
  11.2 11.4 %copy-start.1 = (f32[18,2,1280]{2,1,0:T(2,128)}, f32[18,2,1280]{2,1,0:T(2,128)S(1)}, u32[]{:S(2)}) copy-start(f32[18,2,1280]{2,1,0:T(2,128)S(1)} %sum_pairs.1.rest_0_.here_ref) | copy-start | bytes 552964
  11.3 52.8 %copy-start = (bf16[3,2,128,1280]{3,2,1,0:T(8,128)(2,1)S(1)}, bf16[3,2,128,1280]{3,2,1,0:T(8,128)(2,1)}, u32[]{:S(2)}) copy-start(bf16[3,2,128,1280]{3,2,1,0:T(8,128)(2,1)} %state_ref.3) | copy-start | bytes 5898244
  11.3 52.8 %copy-start.16 = (s32[2]{0:T(128)S(1)}, s32[2]{0:T(128)}, u32[]{:S(2)}) copy-start(s32[2]{0:T(128)} %wave_ref.3) | copy-start | bytes 28
  11.3 5.9 %collective-permute-start = (f32[18,2,1280]{2,1,0:T(2,128)S(1)}, f32[18,2,1280]{2,1,0:T(2,128)S(1)}, u32[]{:S(2)}, u32[]{:S(2)}) collective-permute-start(f32[18,2,1280]{2,1,0:T(2,128)S(1)} %sum_pairs.1.rest_0_.here_ref), channel_id=1, source_target_pairs={{0,16},{16,0},{1,17},{17,1},{2,18},{18,2},{3,19},{19,3},{4,20},{20... | collective-permute-start | bytes 552968 | tf_op jit(solution)/shard_map/ppermute | solution.py:455
  12.9 15.8 %collective-permute-start.3 = (bf16[2,3,160,128]{3,2,1,0:T(8,128)(2,1)}, bf16[2,3,160,128]{3,2,1,0:T(8,128)(2,1)S(1)}, u32[]{:S(2)}, u32[]{:S(2)}) collective-permute-start(bf16[2,3,160,128]{3,2,1,0:T(8,128)(2,1)} %get-tuple-element.63), channel_id=1, source_target_pairs={{0,6},{1,7},{2,4},{3,5},{4,2},{5,3},{6,0},{7,1},{8,14},{9,15},{10,... | collective-permute-start | bytes 737288 | tf_op jit(solution)/shard_map/ppermute | solution.py:427
  14.4 30.3 %collective-permute-start.4 = (bf16[2,3,160,128]{3,2,1,0:T(8,128)(2,1)}, bf16[2,3,160,128]{3,2,1,0:T(8,128)(2,1)S(1)}, u32[]{:S(2)}, u32[]{:S(2)}) collective-permute-start(bf16[2,3,160,128]{3,2,1,0:T(8,128)(2,1)} %get-tuple-element.64), channel_id=1, source_target_pairs={{0,8},{1,9},{2,10},{3,11},{4,12},{5,13},{6,14},{7,15},{8,0},{9,1},... | collective-permute-start | bytes 737288 | tf_op jit(solution)/shard_map/ppermute | solution.py:427
  17.2 32.8 %collective-permute-start.5 = (bf16[2,3,160,128]{3,2,1,0:T(8,128)(2,1)}, bf16[2,3,160,128]{3,2,1,0:T(8,128)(2,1)S(1)}, u32[]{:S(2)}, u32[]{:S(2)}) collective-permute-start(bf16[2,3,160,128]{3,2,1,0:T(8,128)(2,1)} %get-tuple-element.65), channel_id=1, source_target_pairs={{0,10},{1,11},{2,8},{3,9},{4,14},{5,15},{6,12},{7,13},{8,2},{9,3},... | collective-permute-start | bytes 737288 | tf_op jit(solution)/shard_map/ppermute | solution.py:427
  19.7 35.5 %collective-permute-start.6 = (bf16[2,3,160,128]{3,2,1,0:T(8,128)(2,1)}, bf16[2,3,160,128]{3,2,1,0:T(8,128)(2,1)S(1)}, u32[]{:S(2)}, u32[]{:S(2)}) collective-permute-start(bf16[2,3,160,128]{3,2,1,0:T(8,128)(2,1)} %get-tuple-element.66), channel_id=1, source_target_pairs={{0,12},{1,13},{2,14},{3,15},{4,8},{5,9},{6,10},{7,11},{8,4},{9,5},... | collective-permute-start | bytes 737288 | tf_op jit(solution)/shard_map/ppermute | solution.py:427
  20.2 38.7 %collective-permute-start.7 = (bf16[2,3,160,128]{3,2,1,0:T(8,128)(2,1)}, bf16[2,3,160,128]{3,2,1,0:T(8,128)(2,1)S(1)}, u32[]{:S(2)}, u32[]{:S(2)}) collective-permute-start(bf16[2,3,160,128]{3,2,1,0:T(8,128)(2,1)} %get-tuple-element.67), channel_id=1, source_target_pairs={{0,14},{1,15},{2,12},{3,13},{4,10},{5,11},{6,8},{7,9},{8,6},{9,7},... | collective-permute-start | bytes 737288 | tf_op jit(solution)/shard_map/ppermute | solution.py:427
  58.9 0.7 copy-start.13
  59.6 13.5 %copy-start.19 = (bf16[2,3,160,128]{3,2,1,0:T(8,128)(2,1)S(1)}, bf16[2,3,160,128]{3,2,1,0:T(8,128)(2,1)}, u32[]{:S(2)}) copy-start(bf16[2,3,160,128]{3,2,1,0:T(8,128)(2,1)} %get-tuple-element.87) | copy-start | bytes 737284
  59.6 14.4 %copy-start.18 = (bf16[2,3,160,128]{3,2,1,0:T(8,128)(2,1)S(1)}, bf16[2,3,160,128]{3,2,1,0:T(8,128)(2,1)}, u32[]{:S(2)}) copy-start(bf16[2,3,160,128]{3,2,1,0:T(8,128)(2,1)} %get-tuple-element.88) | copy-start | bytes 737284
  61.4 38.6 %copy-start.2 = (f32[18,2,1280]{2,1,0:T(2,128)S(1)}, f32[18,2,1280]{2,1,0:T(2,128)}, u32[]{:S(2)}) copy-start(f32[18,2,1280]{2,1,0:T(2,128)} %copy-done.1) | copy-start | bytes 552964
  61.4 2.6 %collective-permute-start.8 = (bf16[8,3,160,128]{3,2,1,0:T(8,128)(2,1)S(1)}, bf16[8,3,160,128]{3,2,1,0:T(8,128)(2,1)S(1)}, u32[]{:S(2)}, u32[]{:S(2)}) collective-permute-start(bf16[8,3,160,128]{3,2,1,0:T(8,128)(2,1)S(1)} %pick.2), channel_id=1, source_target_pairs={{0,1},{1,0},{2,3},{3,2},{4,5},{5,4},{6,7},{7,6},{8,9},{9,8},{10,11... | collective-permute-start | bytes 2949128 | tf_op jit(solution)/shard_map/ppermute | solution.py:432
  64.1 0.7 copy-start.14
  72.6 23.9 %collective-permute-start.9 = (bf16[3,128,1280]{2,1,0:T(8,128)(2,1)S(1)}, bf16[3,128,1280]{2,1,0:T(8,128)(2,1)S(1)}, u32[]{:S(2)}, u32[]{:S(2)}) collective-permute-start(bf16[3,128,1280]{2,1,0:T(8,128)(2,1)S(1)} %analyse.2.own_ref), channel_id=1, source_target_pairs={{0,16},{16,0},{1,17},{17,1},{2,18},{18,2},{3,19},{19,3},{4,20},{20... | collective-permute-start | bytes 2949128 | tf_op jit(solution)/shard_map/ppermute | solution.py:466
  73.2 8.0 %collective-permute-start.18 = (bf16[2,3,160,128]{3,2,1,0:T(8,128)(2,1)S(1)}, bf16[2,3,160,128]{3,2,1,0:T(8,128)(2,1)S(1)}, u32[]{:S(2)}, u32[]{:S(2)}) collective-permute-start(bf16[2,3,160,128]{3,2,1,0:T(8,128)(2,1)S(1)} %copy-done.19), channel_id=1, source_target_pairs={{0,2},{1,3},{2,0},{3,1},{4,6},{5,7},{6,4},{7,5},{8,10},{9,11},{10,... | collective-permute-start | bytes 737288 | tf_op jit(solution)/shard_map/ppermute | solution.py:427
  74.0 15.3 %collective-permute-start.19 = (bf16[2,3,160,128]{3,2,1,0:T(8,128)(2,1)S(1)}, bf16[2,3,160,128]{3,2,1,0:T(8,128)(2,1)S(1)}, u32[]{:S(2)}, u32[]{:S(2)}) collective-permute-start(bf16[2,3,160,128]{3,2,1,0:T(8,128)(2,1)S(1)} %copy-done.18), channel_id=1, source_target_pairs={{0,4},{1,5},{2,6},{3,7},{4,0},{5,1},{6,2},{7,3},{8,12},{9,13},{10,... | collective-permute-start | bytes 737288 | tf_op jit(solution)/shard_map/ppermute | solution.py:427
  74.0 37.3 %collective-permute-start.20 = (bf16[2,3,160,128]{3,2,1,0:T(8,128)(2,1)}, bf16[2,3,160,128]{3,2,1,0:T(8,128)(2,1)}, u32[]{:S(2)}, u32[]{:S(2)}) collective-permute-start(bf16[2,3,160,128]{3,2,1,0:T(8,128)(2,1)} %get-tuple-element.89), channel_id=1, source_target_pairs={{0,6},{1,7},{2,4},{3,5},{4,2},{5,3},{6,0},{7,1},{8,14},{9,15},{10,... | collective-permute-start | bytes 737288 | tf_op jit(solution)/shard_map/ppermute | solution.py:427
  76.6 34.7 %collective-permute-start.21 = (bf16[2,3,160,128]{3,2,1,0:T(8,128)(2,1)}, bf16[2,3,160,128]{3,2,1,0:T(8,128)(2,1)}, u32[]{:S(2)}, u32[]{:S(2)}) collective-permute-start(bf16[2,3,160,128]{3,2,1,0:T(8,128)(2,1)} %get-tuple-element.90), channel_id=1, source_target_pairs={{0,8},{1,9},{2,10},{3,11},{4,12},{5,13},{6,14},{7,15},{8,0},{9,1},... | collective-permute-start | bytes 737288 | tf_op jit(solution)/shard_map/ppermute | solution.py:427
  81.1 0.7 copy-start.7
  81.8 30.0 %collective-permute-start.22 = (bf16[2,3,160,128]{3,2,1,0:T(8,128)(2,1)}, bf16[2,3,160,128]{3,2,1,0:T(8,128)(2,1)}, u32[]{:S(2)}, u32[]{:S(2)}) collective-permute-start(bf16[2,3,160,128]{3,2,1,0:T(8,128)(2,1)} %get-tuple-element.91), channel_id=1, source_target_pairs={{0,10},{1,11},{2,8},{3,9},{4,14},{5,15},{6,12},{7,13},{8,2},{9,3},... | collective-permute-start | bytes 737288 | tf_op jit(solution)/shard_map/ppermute | solution.py:427
  89.3 0.7 copy-start.9
  90.0 28.0 %collective-permute-start.23 = (bf16[2,3,160,128]{3,2,1,0:T(8,128)(2,1)}, bf16[2,3,160,128]{3,2,1,0:T(8,128)(2,1)}, u32[]{:S(2)}, u32[]{:S(2)}) collective-permute-start(bf16[2,3,160,128]{3,2,1,0:T(8,128)(2,1)} %get-tuple-element.92), channel_id=1, source_target_pairs={{0,12},{1,13},{2,14},{3,15},{4,8},{5,9},{6,10},{7,11},{8,4},{9,5},... | collective-permute-start | bytes 737288 | tf_op jit(solution)/shard_map/ppermute | solution.py:427
  96.4 0.9 copy-start.4
  97.4 24.3 %collective-permute-start.24 = (bf16[2,3,160,128]{3,2,1,0:T(8,128)(2,1)}, bf16[2,3,160,128]{3,2,1,0:T(8,128)(2,1)}, u32[]{:S(2)}, u32[]{:S(2)}) collective-permute-start(bf16[2,3,160,128]{3,2,1,0:T(8,128)(2,1)} %get-tuple-element.93), channel_id=1, source_target_pairs={{0,14},{1,15},{2,12},{3,13},{4,10},{5,11},{6,8},{7,9},{8,6},{9,7},... | collective-permute-start | bytes 737288 | tf_op jit(solution)/shard_map/ppermute | solution.py:427
  100.1 1.2 copy-start.5
  101.3 20.4 %copy-start.6 = (bf16[2,3,160,128]{3,2,1,0:T(8,128)(2,1)S(1)}, bf16[2,3,160,128]{3,2,1,0:T(8,128)(2,1)}, u32[]{:S(2)}) copy-start(bf16[2,3,160,128]{3,2,1,0:T(8,128)(2,1)} %get-tuple-element.86.rest_2_.rest_0_) | copy-start | bytes 737284
  101.3 20.4 %copy-start.8 = (bf16[2,3,160,128]{3,2,1,0:T(8,128)(2,1)S(1)}, bf16[2,3,160,128]{3,2,1,0:T(8,128)(2,1)}, u32[]{:S(2)}) copy-start(bf16[2,3,160,128]{3,2,1,0:T(8,128)(2,1)} %copy-done.7) | copy-start | bytes 737284
  101.3 20.4 %copy-start.10 = (bf16[2,3,160,128]{3,2,1,0:T(8,128)(2,1)S(1)}, bf16[2,3,160,128]{3,2,1,0:T(8,128)(2,1)}, u32[]{:S(2)}) copy-start(bf16[2,3,160,128]{3,2,1,0:T(8,128)(2,1)} %copy-done.9) | copy-start | bytes 737284
  123.6 2.6 %collective-permute-start.25 = (bf16[8,3,160,128]{3,2,1,0:T(8,128)(2,1)S(1)}, bf16[8,3,160,128]{3,2,1,0:T(8,128)(2,1)S(1)}, u32[]{:S(2)}, u32[]{:S(2)}) collective-permute-start(bf16[8,3,160,128]{3,2,1,0:T(8,128)(2,1)S(1)} %pick.3), channel_id=1, source_target_pairs={{0,1},{1,0},{2,3},{3,2},{4,5},{5,4},{6,7},{7,6},{8,9},{9,8},{10,11... | collective-permute-start | bytes 2949128 | tf_op jit(solution)/shard_map/ppermute | solution.py:432
  131.8 13.3 %collective-permute-start.26 = (bf16[3,128,640]{2,1,0:T(8,128)(2,1)S(1)}, bf16[3,128,640]{2,1,0:T(8,128)(2,1)S(1)}, u32[]{:S(2)}, u32[]{:S(2)}) collective-permute-start(bf16[3,128,640]{2,1,0:T(8,128)(2,1)S(1)} %analyse.3.own_ref), channel_id=1, source_target_pairs={{0,16},{16,0},{1,17},{17,1},{2,18},{18,2},{3,19},{19,3},{4,20},{20... | collective-permute-start | bytes 1474568 | tf_op jit(solution)/shard_map/ppermute | solution.py:466
  133.4 20.4 %collective-permute-start.10 = (bf16[8,3,160,128]{3,2,1,0:T(8,128)(2,1)S(1)}, bf16[8,3,160,128]{3,2,1,0:T(8,128)(2,1)S(1)}, u32[]{:S(2)}, u32[]{:S(2)}) collective-permute-start(bf16[8,3,160,128]{3,2,1,0:T(8,128)(2,1)S(1)} %get-tuple-element.68), channel_id=1, source_target_pairs={{0,1},{1,0},{2,3},{3,2},{4,5},{5,4},{6,7},{7,6},{8,9},{9,8},{10,11... | collective-permute-start | bytes 2949128 | tf_op jit(solution)/shard_map/ppermute | solution.py:432
  153.7 94.2 %copy-start.12 = (bf16[256,256]{1,0:T(8,128)(2,1)S(1)}, bf16[256,256]{1,0:T(8,128)(2,1)}, u32[]{:S(2)}) copy-start(bf16[256,256]{1,0:T(8,128)(2,1)} %constant.22.clone.matrix_ref) | copy-start | bytes 393220
  153.7 6.2 %collective-permute-start.27 = (bf16[8,3,160,128]{3,2,1,0:T(8,128)(2,1)S(1)}, bf16[8,3,160,128]{3,2,1,0:T(8,128)(2,1)S(1)}, u32[]{:S(2)}, u32[]{:S(2)}) collective-permute-start(bf16[8,3,160,128]{3,2,1,0:T(8,128)(2,1)S(1)} %get-tuple-element.94), channel_id=1, source_target_pairs={{0,1},{1,0},{2,3},{3,2},{4,5},{5,4},{6,7},{7,6},{8,9},{9,8},{10,11... | collective-permute-start | bytes 2949128 | tf_op jit(solution)/shard_map/ppermute | solution.py:432
  155.5 9.0 %collective-permute-start.11 = (bf16[2,3,160,128]{3,2,1,0:T(8,128)(2,1)S(1)}, bf16[2,3,160,128]{3,2,1,0:T(8,128)(2,1)S(1)}, u32[]{:S(2)}, u32[]{:S(2)}) collective-permute-start(bf16[2,3,160,128]{3,2,1,0:T(8,128)(2,1)S(1)} %get-tuple-element.78), channel_id=1, source_target_pairs={{0,2},{1,3},{2,0},{3,1},{4,6},{5,7},{6,4},{7,5},{8,10},{9,11},{10,... | collective-permute-start | bytes 737288 | tf_op jit(solution)/shard_map/ppermute | solution.py:427
  157.0 16.2 %collective-permute-start.12 = (bf16[2,3,160,128]{3,2,1,0:T(8,128)(2,1)S(1)}, bf16[2,3,160,128]{3,2,1,0:T(8,128)(2,1)S(1)}, u32[]{:S(2)}, u32[]{:S(2)}) collective-permute-start(bf16[2,3,160,128]{3,2,1,0:T(8,128)(2,1)S(1)} %get-tuple-element.79), channel_id=1, source_target_pairs={{0,4},{1,5},{2,6},{3,7},{4,0},{5,1},{6,2},{7,3},{8,12},{9,13},{10,... | collective-permute-start | bytes 737288 | tf_op jit(solution)/shard_map/ppermute | solution.py:427
  157.0 21.0 %collective-permute-start.13 = (bf16[2,3,160,128]{3,2,1,0:T(8,128)(2,1)S(1)}, bf16[2,3,160,128]{3,2,1,0:T(8,128)(2,1)S(1)}, u32[]{:S(2)}, u32[]{:S(2)}) collective-permute-start(bf16[2,3,160,128]{3,2,1,0:T(8,128)(2,1)S(1)} %get-tuple-element.80), channel_id=1, source_target_pairs={{0,6},{1,7},{2,4},{3,5},{4,2},{5,3},{6,0},{7,1},{8,14},{9,15},{10,... | collective-permute-start | bytes 737288 | tf_op jit(solution)/shard_map/ppermute | solution.py:427
  159.0 19.0 %collective-permute-start.14 = (bf16[2,3,160,128]{3,2,1,0:T(8,128)(2,1)S(1)}, bf16[2,3,160,128]{3,2,1,0:T(8,128)(2,1)S(1)}, u32[]{:S(2)}, u32[]{:S(2)}) collective-permute-start(bf16[2,3,160,128]{3,2,1,0:T(8,128)(2,1)S(1)} %get-tuple-element.81), channel_id=1, source_target_pairs={{0,8},{1,9},{2,10},{3,11},{4,12},{5,13},{6,14},{7,15},{8,0},{9,1},... | collective-permute-start | bytes 737288 | tf_op jit(solution)/shard_map/ppermute | solution.py:427
  159.9 32.7 %collective-permute-start.15 = (bf16[2,3,160,128]{3,2,1,0:T(8,128)(2,1)S(1)}, bf16[2,3,160,128]{3,2,1,0:T(8,128)(2,1)S(1)}, u32[]{:S(2)}, u32[]{:S(2)}) collective-permute-start(bf16[2,3,160,128]{3,2,1,0:T(8,128)(2,1)S(1)} %get-tuple-element.82), channel_id=1, source_target_pairs={{0,10},{1,11},{2,8},{3,9},{4,14},{5,15},{6,12},{7,13},{8,2},{9,3},... | collective-permute-start | bytes 737288 | tf_op jit(solution)/shard_map/ppermute | solution.py:427
  164.5 34.5 %collective-permute-start.16 = (bf16[2,3,160,128]{3,2,1,0:T(8,128)(2,1)S(1)}, bf16[2,3,160,128]{3,2,1,0:T(8,128)(2,1)S(1)}, u32[]{:S(2)}, u32[]{:S(2)}) collective-permute-start(bf16[2,3,160,128]{3,2,1,0:T(8,128)(2,1)S(1)} %get-tuple-element.83), channel_id=1, source_target_pairs={{0,12},{1,13},{2,14},{3,15},{4,8},{5,9},{6,10},{7,11},{8,4},{9,5},... | collective-permute-start | bytes 737288 | tf_op jit(solution)/shard_map/ppermute | solution.py:427
  173.2 42.5 %collective-permute-start.17 = (bf16[2,3,160,128]{3,2,1,0:T(8,128)(2,1)S(1)}, bf16[2,3,160,128]{3,2,1,0:T(8,128)(2,1)S(1)}, u32[]{:S(2)}, u32[]{:S(2)}) collective-permute-start(bf16[2,3,160,128]{3,2,1,0:T(8,128)(2,1)S(1)} %get-tuple-element.84), channel_id=1, source_target_pairs={{0,14},{1,15},{2,12},{3,13},{4,10},{5,11},{6,8},{7,9},{8,6},{9,7},... | collective-permute-start | bytes 737288 | tf_op jit(solution)/shard_map/ppermute | solution.py:427
  178.0 37.7 %collective-permute-start.28 = (bf16[2,3,160,128]{3,2,1,0:T(8,128)(2,1)S(1)}, bf16[2,3,160,128]{3,2,1,0:T(8,128)(2,1)S(1)}, u32[]{:S(2)}, u32[]{:S(2)}) collective-permute-start(bf16[2,3,160,128]{3,2,1,0:T(8,128)(2,1)S(1)} %get-tuple-element.104), channel_id=1, source_target_pairs={{0,2},{1,3},{2,0},{3,1},{4,6},{5,7},{6,4},{7,5},{8,10},{9,11},{10,... | collective-permute-start | bytes 737288 | tf_op jit(solution)/shard_map/ppermute | solution.py:427
  178.1 37.6 %collective-permute-start.29 = (bf16[2,3,160,128]{3,2,1,0:T(8,128)(2,1)S(1)}, bf16[2,3,160,128]{3,2,1,0:T(8,128)(2,1)S(1)}, u32[]{:S(2)}, u32[]{:S(2)}) collective-permute-start(bf16[2,3,160,128]{3,2,1,0:T(8,128)(2,1)S(1)} %get-tuple-element.105), channel_id=1, source_target_pairs={{0,4},{1,5},{2,6},{3,7},{4,0},{5,1},{6,2},{7,3},{8,12},{9,13},{10,... | collective-permute-start | bytes 737288 | tf_op jit(solution)/shard_map/ppermute | solution.py:427
  192.7 26.5 %collective-permute-start.30 = (bf16[2,3,160,128]{3,2,1,0:T(8,128)(2,1)S(1)}, bf16[2,3,160,128]{3,2,1,0:T(8,128)(2,1)S(1)}, u32[]{:S(2)}, u32[]{:S(2)}) collective-permute-start(bf16[2,3,160,128]{3,2,1,0:T(8,128)(2,1)S(1)} %get-tuple-element.106), channel_id=1, source_target_pairs={{0,6},{1,7},{2,4},{3,5},{4,2},{5,3},{6,0},{7,1},{8,14},{9,15},{10,... | collective-permute-start | bytes 737288 | tf_op jit(solution)/shard_map/ppermute | solution.py:427
  199.0 32.5 %collective-permute-start.31 = (bf16[2,3,160,128]{3,2,1,0:T(8,128)(2,1)S(1)}, bf16[2,3,160,128]{3,2,1,0:T(8,128)(2,1)S(1)}, u32[]{:S(2)}, u32[]{:S(2)}) collective-permute-start(bf16[2,3,160,128]{3,2,1,0:T(8,128)(2,1)S(1)} %get-tuple-element.107), channel_id=1, source_target_pairs={{0,8},{1,9},{2,10},{3,11},{4,12},{5,13},{6,14},{7,15},{8,0},{9,1},... | collective-permute-start | bytes 737288 | tf_op jit(solution)/shard_map/ppermute | solution.py:427
  215.7 21.1 %collective-permute-start.32 = (bf16[2,3,160,128]{3,2,1,0:T(8,128)(2,1)S(1)}, bf16[2,3,160,128]{3,2,1,0:T(8,128)(2,1)S(1)}, u32[]{:S(2)}, u32[]{:S(2)}) collective-permute-start(bf16[2,3,160,128]{3,2,1,0:T(8,128)(2,1)S(1)} %get-tuple-element.108), channel_id=1, source_target_pairs={{0,10},{1,11},{2,8},{3,9},{4,14},{5,15},{6,12},{7,13},{8,2},{9,3},... | collective-permute-start | bytes 737288 | tf_op jit(solution)/shard_map/ppermute | solution.py:427
  215.7 27.8 %collective-permute-start.33 = (bf16[2,3,160,128]{3,2,1,0:T(8,128)(2,1)S(1)}, bf16[2,3,160,128]{3,2,1,0:T(8,128)(2,1)S(1)}, u32[]{:S(2)}, u32[]{:S(2)}) collective-permute-start(bf16[2,3,160,128]{3,2,1,0:T(8,128)(2,1)S(1)} %get-tuple-element.109), channel_id=1, source_target_pairs={{0,12},{1,13},{2,14},{3,15},{4,8},{5,9},{6,10},{7,11},{8,4},{9,5},... | collective-permute-start | bytes 737288 | tf_op jit(solution)/shard_map/ppermute | solution.py:427
  215.7 32.3 %collective-permute-start.34 = (bf16[2,3,160,128]{3,2,1,0:T(8,128)(2,1)S(1)}, bf16[2,3,160,128]{3,2,1,0:T(8,128)(2,1)S(1)}, u32[]{:S(2)}, u32[]{:S(2)}) collective-permute-start(bf16[2,3,160,128]{3,2,1,0:T(8,128)(2,1)S(1)} %get-tuple-element.110), channel_id=1, source_target_pairs={{0,14},{1,15},{2,12},{3,13},{4,10},{5,11},{6,8},{7,9},{8,6},{9,7},... | collective-permute-start | bytes 737288 | tf_op jit(solution)/shard_map/ppermute | solution.py:427

commit v9 on v8

--- a/solution.py
+++ b/solution.py
@@ -12,7 +12,6 @@
 BF16 = jnp.bfloat16
 F32 = jnp.float32
 CORES = 2
-PERMUTED = (0, 1)
 ANYWHERE = pl.BlockSpec(memory_space=pl.ANY)
 IN_SMEM = pl.BlockSpec(memory_space=pltpu.SMEM)
 TOKEN = jax.ShapeDtypeStruct((8, 128), F32)
@@ -38,6 +37,10 @@
 def owner_of(me, k, other):
     core = me % CORES
     return ((me // CORES) ^ k) * CORES + (CORES - 1 - core if other else core)
+
+
+def partners(chips):
+    return [0] + list(range(chips // 2, chips)) + list(range(1, chips // 2))
 
 
 def swap_matrix(rows, columns, picked):
@@ -86,7 +89,7 @@
                     else:
                         outs[0][owner, 0, j : j + depth, :] = value
     if permuted:
-        for k, out in enumerate(outs):
+        for k, out in zip(partners(len(outs)), outs):
             for core in range(CORES):
                 out[core, 0] = blocks[((me_ref[0] // CORES) ^ k) * CORES + core]
 
@@ -156,23 +159,24 @@
 
 def pair_kernel(mate_ref, *rest):
     chips = mate_ref.shape[0]
-    outs, sems = rest[chips:-1], rest[-1]
+    outs, token_ref, sems = rest[-2 - chips : -2], rest[-2], rest[-1]
+    token_ref[...] = jnp.zeros_like(token_ref)
     run_copies([pltpu.make_async_copy(mate_ref.at[k], out.at[1], sems.at[k]) for k, out in enumerate(outs)])
 
 
-def pair(messages, mate):
+def pair(messages, mate, waits):
     chips = len(messages)
     return call(
         pair_kernel,
         "pair",
         0,
         4 * mate.size,
-        out_shape=[jax.ShapeDtypeStruct(m.shape, m.dtype) for m in messages],
-        in_specs=[pl.BlockSpec(mate.shape, lambda: (0, 0, 0, 0))] + [ANYWHERE] * chips,
-        out_specs=[ANYWHERE] * chips,
+        out_shape=[jax.ShapeDtypeStruct(m.shape, m.dtype) for m in messages] + [TOKEN],
+        in_specs=[pl.BlockSpec(mate.shape, lambda: (0, 0, 0, 0))] + [ANYWHERE] * (chips + len(waits)),
+        out_specs=[ANYWHERE] * chips + [pl.BlockSpec(TOKEN.shape, lambda: (0, 0))],
         scratch_shapes=[pltpu.SemaphoreType.DMA((chips,))],
         input_output_aliases={k + 1: k for k in range(chips)},
-    )(mate, *messages)
+    )(mate, *messages, *waits)
 
 
 def analyse_kernel(slot, low, count, me_ref, wave_ref, token_ref, table_ref, state_ref, *rest):
@@ -189,11 +193,11 @@
             lanes = pl.ds(r * members, members)
             if count == 1:
                 copies.append(pltpu.make_async_copy(blocks[0].at[:, r], grid.at[:, :, lanes], sems.at[0, r]))
-            for k in range(count - 1):
+            for i, k in enumerate(partners(count - 1) if count > 1 else []):
                 for other in range(CORES):
                     target = grid.at[owner_of(me_ref[0], k, other), :, lanes]
-                    source = blocks[-1].at[k, r] if other else blocks[k].at[me_ref[0] % CORES, r]
-                    copies.append(pltpu.make_async_copy(source, target, sems.at[CORES * k + other, r]))
+                    source = blocks[-1].at[i, r] if other else blocks[i].at[me_ref[0] % CORES, r]
+                    copies.append(pltpu.make_async_copy(source, target, sems.at[CORES * i + other, r]))
         run_copies(copies)
 
     field = grid[...].reshape(owners * lats, rows * members)
@@ -241,7 +245,8 @@
     if len(blocks) == 1:
         return blocks[0]
     own = [lax.dynamic_index_in_dim(m, here % CORES, 0, keepdims=False) for m in blocks[:-1]]
-    both = jnp.stack([jnp.stack(own), blocks[-1]], axis=1).reshape((owners,) + own[0].shape)
+    place = np.argsort(partners(len(own)))
+    both = jnp.stack([jnp.stack(own)[place], blocks[-1][place]], axis=1).reshape((owners,) + own[0].shape)
     order = jnp.arange(owners, dtype=jnp.int32)
     order = ((order // CORES) ^ (here // CORES)) * CORES + (order % CORES ^ here % CORES)
     return jnp.take(both, order, axis=0)
@@ -314,11 +319,11 @@
         @pl.when(step == pl.num_programs(0) - 1)
         def _():
             copies = []
-            for k in range(permuted):
+            for i, k in enumerate(partners(permuted)):
                 for other in range(CORES):
                     source = grid.at[owner_of(me_ref[0], k, other)]
-                    target = outs[-1].at[k] if other else outs[k].at[0]
-                    copies.append(pltpu.make_async_copy(source, target, sems.at[k, other]))
+                    target = outs[-1].at[i] if other else outs[i].at[0]
+                    copies.append(pltpu.make_async_copy(source, target, sems.at[i, other]))
             run_copies(copies)
 
 
@@ -370,7 +375,7 @@
         if count == 1:
             views.append(lambda owner, j, ref=refs[0]: ref[owner, 0, j, :])
             continue
-        for k, ref in enumerate(refs):
+        for k, ref in zip(partners(count), refs):
             for other in range(CORES):
                 blocks[spare][owner_of(me_ref[0], k, other)] = ref[other, 0]
         views.append(lambda owner, j, ref=blocks[spare]: ref[owner, j, :])
@@ -423,8 +428,8 @@
 def between_chips(messages):
     chips = len(messages)
     got = [messages[0]]
-    for k in range(1, chips):
-        got.append(lax.ppermute(messages[k], "wave", [(d, d ^ (k * CORES)) for d in range(chips * CORES)]))
+    for k, message in list(zip(partners(chips), messages))[1:]:
+        got.append(lax.ppermute(message, "wave", [(d, d ^ (k * CORES)) for d in range(chips * CORES)]))
     return got
 
 
@@ -445,31 +450,33 @@
     me = lax.axis_index("wave").astype(jnp.int32).reshape(1)
     pole_index = lax.axis_index("pole")
     sign = (2 * pole_index - 1).astype(F32).reshape(1)
-    received, waits = [], []
-    for slot in range(local_slots):
-        permuted = slot in PERMUTED
+    order = list(range(local_slots))[::-1]
+    received, waits = {}, []
+    for slot in order:
+        permuted = slot == order[0]
         *blocks, token = weigh(tendency, gauss_weights[None], me, slot, local_slots, permuted, waits)
-        received.append(between_chips(blocks) if permuted else [to_all(blocks[0])])
-        if slot == 0:
+        received[slot] = between_chips(blocks) if permuted else [to_all(blocks[0])]
+        if permuted:
             here = sum_pairs(block_inverses, pole_coeffs, token)
             there = lax.ppermute(here, "pole", [(0, 1), (1, 0)])
-            waits = [here if permuted else there]
-
-    sent = []
-    for slot in range(local_slots):
-        permuted = slot in PERMUTED
+            waits = [here, received[slot][1]]
+
+    sent = {}
+    for slot in order:
+        incoming = slot == order[0]
         low = nspec // 2 if slot % 2 else 0
         blocks = received[slot]
-        if permuted:
+        if incoming:
             blocks = blocks + [between_cores(pick(blocks, me, [token, there]), owners)]
         forced = analyse(blocks, legendre, spectral_state, wavenumbers, me, token, slot, low, nspec // 2)
         other = lax.ppermute(forced, "pole", [(0, 1), (1, 0)])
-        *blocks, token = synthesise(here, there, sign, forced, other, legendre, me, slot, low, lats, permuted)
-        if permuted:
-            sent.append(between_chips(pair(blocks[:-1], between_cores(blocks[-1], owners))))
+        *blocks, token = synthesise(here, there, sign, forced, other, legendre, me, slot, low, lats, not incoming)
+        if incoming:
+            sent[slot] = [to_all(blocks[0])]
         else:
-            sent.append([to_all(blocks[0])])
-    return assemble(sent, me, lats)
+            *blocks, token = pair(blocks[:-1], between_cores(blocks[-1], owners), [])
+            sent[slot] = between_chips(blocks)
+    return assemble([sent[slot] for slot in range(local_slots)], me, lats)
 
 
 def solution(mesh):

time: 253 us -> 249 us (0.984)
  Pallas kernels: 58 us -> 51.1 us
  waiting for transfers between devices: 144 us -> 148 us
    ppermute x2, waiting for transfers between devices: 17.3 us -> 34.1 us  [per_device(): other = lax.ppermute(forced, 'pole', [(0, 1), (1, 0)])]
    ppermute x28 -> x14, waiting for transfers between devices: 122 us -> 108 us  [between_chips(): lax.ppermute(message, 'wave', [(d, d ^ k * CORES) for d in range(chips *...]
    ppermute x28 -> x14, starting transfers between devices: 40.5 us -> 27 us  [between_chips(): lax.ppermute(message, 'wave', [(d, d ^ k * CORES) for d in range(chips *...]
    all_to_all x0 -> x2, starting transfers between devices: none -> 11.4 us  [to_all(): lax.all_to_all(blocks, 'wave', split_axis=0, concat_axis=0, tiled=True)]
    pallas_call x2 -> x1, Pallas kernels: 3.73 us -> 0.23 us  [pick(): call(functools.partial(pick_kernel, len(waits)), 'pick', 0, 4 * math.prod...]
    unnamed x41 -> x33, local copies, waits for them, and re-layouts: 5.75 us -> 4.96 us
    ppermute x4 -> x2, waiting for transfers between devices: 5.11 us -> 5.11 us  [between_cores(): return lax.ppermute(blocks, 'wave', [(d, d ^ 1) for d in range(owners)])]
  transfers between devices with their start and end apart: 35 -> 21, of which waited for: 23 -> 13; matrix products, arithmetic and copies ran while one was open for 0% -> 0% of each run, Pallas kernels for 12% -> 13%
where the time goes in v9:
time: 249 us; the launch traced here: 248 us
  waiting for transfers between devices  148 us (59%)
  Pallas kernels  51.1 us (21%)
  starting transfers between devices  43.3 us (17%)
  local copies, waits for them, and re-layouts  4.96 us (2%)
    ppermute x14, waiting for transfers between devices, between_chips(): lax.ppermute(message, 'wave', [(d, d ^ k * CORES) for d in range(chips *...  108 us
    ppermute x2, waiting for transfers between devices, per_device(): other = lax.ppermute(forced, 'pole', [(0, 1), (1, 0)])  34.1 us
    ppermute x14, starting transfers between devices, between_chips(): lax.ppermute(message, 'wave', [(d, d ^ k * CORES) for d in range(chips *...  27 us
    pallas_call x2, Pallas kernels, synthesise(): call(functools.partial(synthesise_kernel, slot, low, chips), 'synthesise'...  16.1 us
    pallas_call x2, Pallas kernels, weigh(): call(functools.partial(weigh_kernel, slot, local_slots, permuted, len(wai...  11.9 us
    pallas_call x2, Pallas kernels, analyse(): call(functools.partial(analyse_kernel, slot, low, len(blocks)), 'analyse'...  11.7 us
    all_to_all x2, starting transfers between devices, to_all(): lax.all_to_all(blocks, 'wave', split_axis=0, concat_axis=0, tiled=True)  11.4 us
    pallas_call x1, Pallas kernels, assemble(): call(functools.partial(assemble_kernel, [len(p) for p in pieces]), 'assem...  6.17 us
  transfers between devices with their start and end apart: 21, of which 13 were waited for; matrix products, arithmetic and copies ran while one was open for 0% of the time, Pallas kernels for 13%

profile of v9, /device:TPU:8, one launch (start us, length us, event | category | flops | bytes accessed | tf_op | source)
XLA Modules:
  0.0 247.6 jit_solution(14235291109577004893)
XLA Ops:
  0.0 6.0 %weigh.2 = (bf16[2,3,160,128]{3,2,1,0:T(8,128)(2,1)}, bf16[2,3,160,128]{3,2,1,0:T(8,128)(2,1)}, bf16[2,3,160,128]{3,2,1,0:T(8,128)(2,1)}, bf16[2,3,160,128]{3,2,...) custom-call(s32[1]{0:T(128)} %bitcast.me_ref, ...), custom_call_target="tpu_custom_call" | custom-call | flops 503316480 | bytes 5898240 | tf_op jit(solution)/shard_map/weigh/pallas_call | solution.py:108
  6.0 2.7 %collective-permute-start.1 = (bf16[2,3,160,128]{3,2,1,0:T(8,128)(2,1)}, bf16[2,3,160,128]{3,2,1,0:T(8,128)(2,1)S(1)}, u32[]{:S(2)}, u32[]{:S(2)}) collective-permute-start(bf16[2,3,160,128]{3,2,1,0:T(8,128)(2,1)} %get-tuple-element.36), channel_id=1, source_target_pairs={{0,8},{1,9},{2,10},{3,11},{4,12},{5,13},{6,14},{7,15},{8,0},{9,1},... | collective-permute-start | bytes 737288 | tf_op jit(solution)/shard_map/ppermute | solution.py:432
  8.7 0.1 copy.19.coeff_ref
  8.8 0.7 copy-done.11
  9.5 2.4 sum_pairs.1.rest_0_.here_ref
  11.8 0.0 copy-start.2
  11.8 0.7 copy-done.2
  12.5 6.9 %collective-permute-done.1.rest_1_.rest_3_ = bf16[2,3,160,128]{3,2,1,0:T(8,128)(2,1)S(1)} collective-permute-done((bf16[2,3,160,128]{3,2,1,0:T(8,128)(2,1)}, bf16[2,3,160,128]{3,2,1,0:T(8,128)(2,1)S(1)}, u32[]{:S(2)}, u32[]{:S(2)}) %collective-permute-start.1) | collective-permute-done | bytes 245792 | tf_op jit(solution)/shard_map/ppermute | solution.py:432
  19.4 0.7 copy-done.5
  20.1 5.8 %weigh.3 = (bf16[16,3,160,128]{3,2,1,0:T(8,128)(2,1)}, f32[8,128]{1,0:T(8,128)}) custom-call(s32[1]{0:T(128)} %bitcast.me_ref, bf16[128,256]{1,0:T(8,128)(2,1)} %constant.21.clone.matrix_ref, f32[1,160]{1,0:T(1,128)} %bitcast.4, bf16[3,160,32,128]{3,2,1,0:T(8,128)(2,1)} %tendency_ref.3, f32[18,2,1280]{2,1,0:T(2,128)} %copy-done.2, ...), custom_call_target="tpu_custom_call" | custom-call | flops 503316480 | bytes 5898240 | tf_op jit(solution)/shard_map/weigh/pallas_call | solution.py:108
  25.9 7.1 %all-to-all-start = ((bf16[16,3,160,128]{3,2,1,0:T(8,128)(2,1)}), bf16[16,3,160,128]{3,2,1,0:T(8,128)(2,1)S(1)}, u32[]{:S(2)}, u32[]{:S(2)}) async-start(bf16[16,3,160,128]{3,2,1,0:T(8,128)(2,1)} %get-tuple-element.46), calls=%async_computation | async-start | bytes 3932160 | tf_op jit(solution)/shard_map/all_to_all | solution.py:441
  33.1 0.0 copy-start.12
  33.1 3.3 %collective-permute-start.2 = (bf16[2,3,160,128]{3,2,1,0:T(8,128)(2,1)}, bf16[2,3,160,128]{3,2,1,0:T(8,128)(2,1)S(1)}, u32[]{:S(2)}, u32[]{:S(2)}) collective-permute-start(bf16[2,3,160,128]{3,2,1,0:T(8,128)(2,1)} %get-tuple-element.39), channel_id=1, source_target_pairs={{0,10},{1,11},{2,8},{3,9},{4,14},{5,15},{6,12},{7,13},{8,2},{9,3},... | collective-permute-start | bytes 737288 | tf_op jit(solution)/shard_map/ppermute | solution.py:432
  36.4 1.5 collective-permute-start
  37.9 0.0 collective-permute-start.3
  37.9 2.0 collective-permute-start.4
  40.0 1.5 collective-permute-start.5
  41.4 1.4 collective-permute-done.rest_1_.there_ref
  42.8 0.0 copy-done.15
  42.8 1.0 collective-permute-start.6
  43.8 54.0 %collective-permute-done.2.rest_4_.rest_2_ = bf16[2,3,160,128]{3,2,1,0:T(8,128)(2,1)S(1)} collective-permute-done((bf16[2,3,160,128]{3,2,1,0:T(8,128)(2,1)}, bf16[2,3,160,128]{3,2,1,0:T(8,128)(2,1)S(1)}, u32[]{:S(2)}, u32[]{:S(2)}) %collective-permute-start.2) | collective-permute-done | bytes 245792 | tf_op jit(solution)/shard_map/ppermute | solution.py:432
  97.7 0.0 copy-done.14
  97.8 4.1 %collective-permute-start.7 = (bf16[2,3,160,128]{3,2,1,0:T(8,128)(2,1)S(1)}, bf16[2,3,160,128]{3,2,1,0:T(8,128)(2,1)S(1)}, u32[]{:S(2)}, u32[]{:S(2)}) collective-permute-start(bf16[2,3,160,128]{3,2,1,0:T(8,128)(2,1)S(1)} %copy-done.14), channel_id=1, source_target_pairs={{0,6},{1,7},{2,4},{3,5},{4,2},{5,3},{6,0},{7,1},{8,14},{9,15},{10,... | collective-permute-start | bytes 737288 | tf_op jit(solution)/shard_map/ppermute | solution.py:432
  101.8 2.9 %collective-permute-done.3.rest_5_.rest_3_ = bf16[2,3,160,128]{3,2,1,0:T(8,128)(2,1)S(1)} collective-permute-done((bf16[2,3,160,128]{3,2,1,0:T(8,128)(2,1)}, bf16[2,3,160,128]{3,2,1,0:T(8,128)(2,1)S(1)}, u32[]{:S(2)}, u32[]{:S(2)}) %collective-permute-start.3) | collective-permute-done | bytes 245792 | tf_op jit(solution)/shard_map/ppermute | solution.py:432
  104.8 7.6 %collective-permute-done.4.rest_6_.rest_4_ = bf16[2,3,160,128]{3,2,1,0:T(8,128)(2,1)S(1)} collective-permute-done((bf16[2,3,160,128]{3,2,1,0:T(8,128)(2,1)}, bf16[2,3,160,128]{3,2,1,0:T(8,128)(2,1)S(1)}, u32[]{:S(2)}, u32[]{:S(2)}) %collective-permute-start.4) | collective-permute-done | bytes 245792 | tf_op jit(solution)/shard_map/ppermute | solution.py:432
  112.4 0.0 collective-permute-done.5.rest_7_.rest_5_
  112.4 0.0 collective-permute-done.6.rest_8_.rest_6_
  112.4 0.0 collective-permute-done.7.rest_9_.rest_7_
  112.4 0.2 pick.1
  112.7 0.1 collective-permute-start.8
  112.8 2.6 %collective-permute-done.8.rest_8_ = bf16[8,3,160,128]{3,2,1,0:T(8,128)(2,1)S(1)} collective-permute-done((bf16[8,3,160,128]{3,2,1,0:T(8,128)(2,1)S(1)}, bf16[8,3,160,128]{3,2,1,0:T(8,128)(2,1)S(1)}, u32[]{:S(2)}, u32[]{:S(2)}) %collective-permute-start.8) | collective-permute-done | bytes 983072 | tf_op jit(solution)/shard_map/ppermute | solution.py:437
  115.3 4.9 %analyse.2.own_ref = bf16[3,128,640]{2,1,0:T(8,128)(2,1)S(1)} custom-call(s32[1]{0:T(128)} %bitcast.me_ref, s32[2]{0:T(128)S(1)} %copy-done.12, f32[8,128]{1,0:T(8,128)S(1)} %copy-done.10, bf16[2,1280,2560]{2,1,0:T(8,128)(2,1)} %table_ref.7, bf16[3,2,128,1280]{3,2,1,0:T(8,128)(2,1)S(1)} %copy-done, bf16[2,3,160,128]{3,2,1,0:T(8,128)(2,1)S(1)} %copy-done.8, ...), custom_call_target="tpu_custom_call" | custom-call | flops 1258291200 | bytes 3276800 | tf_op jit(solution)/shard_map/analyse/pallas_call | solution.py:221
  120.2 1.6 collective-permute-start.9
  121.8 11.9 %collective-permute-done.9.other_ref = bf16[3,128,640]{2,1,0:T(8,128)(2,1)} collective-permute-done((bf16[3,128,640]{2,1,0:T(8,128)(2,1)S(1)}, bf16[3,128,640]{2,1,0:T(8,128)(2,1)}, u32[]{:S(2)}, u32[]{:S(2)}) %collective-permute-start.9) | collective-permute-done | bytes 491552 | tf_op jit(solution)/shard_map/ppermute | solution.py:472
  133.6 5.3 %synthesise.2 = (bf16[16,3,160,128]{3,2,1,0:T(8,128)(2,1)S(1)}, f32[8,128]{1,0:T(8,128)S(1)}) custom-call(s32[1]{0:T(128)} %bitcast.me_ref, f32[1]{0:T(128)} %bitcast.1.sign_ref, f32[18,2,1280]{2,1,0:T(2,128)S(1)} %copy-done.3, f32[18,2,1280]{2,1,0:T(2,128)S(1)} %collective-permute-done.rest_1_.there_ref, bf16[3,128,640]{2,1,0:T(8,128)(2,1)S(1)} %analyse.2.own_ref, ...), custom_call_target="tpu_custom_call" | custom-call | flops 1258291200 | bytes 3276800 | tf_op jit(solution)/shard_map/synthesise/pallas_call | solution.py:346
  138.9 1.2 copy-done.7
  140.2 0.0 all-to-all-done.rest_0_
  140.2 4.3 %all-to-all-start.1 = ((bf16[16,3,160,128]{3,2,1,0:T(8,128)(2,1)}), bf16[16,3,160,128]{3,2,1,0:T(8,128)(2,1)}, u32[]{:S(2)}, u32[]{:S(2)}) async-start(bf16[16,3,160,128]{3,2,1,0:T(8,128)(2,1)} %copy-done.7), calls=%async_computation.1 | async-start | bytes 3932160 | tf_op jit(solution)/shard_map/all_to_all | solution.py:441
  144.5 0.0 copy-start.1
  144.5 1.5 copy-done.1
  146.1 6.8 %analyse.3.own_ref = bf16[3,128,1280]{2,1,0:T(8,128)(2,1)S(1)} custom-call(s32[1]{0:T(128)} %bitcast.me_ref, s32[2]{0:T(128)S(1)} %copy-done.12, f32[8,128]{1,0:T(8,128)S(1)} %get-tuple-element.45.token_ref, bf16[2,1280,2560]{2,1,0:T(8,128)(2,1)} %table_ref.7, bf16[3,2,128,1280]{3,2,1,0:T(8,128)(2,1)S(1)} %copy-done.1, ...), custom_call_target="tpu_custom_call" | custom-call | flops 2516582400 | bytes 6553600 | tf_op jit(solution)/shard_map/analyse/pallas_call | solution.py:221
  152.9 1.6 collective-permute-start.10
  154.5 22.3 %collective-permute-done.10.other_ref = bf16[3,128,1280]{2,1,0:T(8,128)(2,1)S(1)} collective-permute-done((bf16[3,128,1280]{2,1,0:T(8,128)(2,1)S(1)}, bf16[3,128,1280]{2,1,0:T(8,128)(2,1)S(1)}, u32[]{:S(2)}, u32[]{:S(2)}) %collective-permute-start.10) | collective-permute-done | bytes 983072 | tf_op jit(solution)/shard_map/ppermute | solution.py:472
  176.7 10.9 %synthesise.3 = (bf16[2,3,160,128]{3,2,1,0:T(8,128)(2,1)S(1)}, bf16[2,3,160,128]{3,2,1,0:T(8,128)(2,1)S(1)}, bf16[2,3,160,128]{3,2,1,0:T(8,128)(2,1)S(1)}, bf16[...) custom-call(s32[1]{0:T(128)} %bitcast.me_ref, ...), custom_call_target="tpu_custom_call" | custom-call | flops 2516582400 | bytes 6553600 | tf_op jit(solution)/shard_map/synthesise/pallas_call | solution.py:346
  187.6 0.0 copy-start.9
  187.6 0.1 collective-permute-start.11
  187.7 2.6 %collective-permute-done.11.mate_ref = bf16[8,3,160,128]{3,2,1,0:T(8,128)(2,1)S(1)} collective-permute-done((bf16[8,3,160,128]{3,2,1,0:T(8,128)(2,1)S(1)}, bf16[8,3,160,128]{3,2,1,0:T(8,128)(2,1)S(1)}, u32[]{:S(2)}, u32[]{:S(2)}) %collective-permute-start.11) | collective-permute-done | bytes 983072 | tf_op jit(solution)/shard_map/ppermute | solution.py:437
  190.2 2.6 %pair.1 = (bf16[2,3,160,128]{3,2,1,0:T(8,128)(2,1)S(1)}, bf16[2,3,160,128]{3,2,1,0:T(8,128)(2,1)S(1)}, bf16[2,3,160,128]{3,2,1,0:T(8,128)(2,1)S(1)}, bf16[2,3,16...) custom-call(bf16[8,3,160,128]{3,2,1,0:T(8,128)(2,1)S(1)} %collective, ...), custom_call_target="tpu_custom_call", output_to_operand_aliasing={{0}: (1, {}), {1}: (2, {}), {2}: (3, {}), {3}: (4, {}), {4}... | custom-call | bytes 1966080 | tf_op jit(solution)/shard_map/pair/pallas_call | solution.py:169
  192.9 2.4 collective-permute-start.12
  195.3 1.5 collective-permute-start.13
  196.8 1.5 collective-permute-start.14
  198.2 0.6 collective-permute-start.15
  198.8 1.5 collective-permute-start.16
  200.2 21.7 %collective-permute-done.12.rest_1_ = bf16[2,3,160,128]{3,2,1,0:T(8,128)(2,1)S(1)} collective-permute-done((bf16[2,3,160,128]{3,2,1,0:T(8,128)(2,1)S(1)}, bf16[2,3,160,128]{3,2,1,0:T(8,128)(2,1)S(1)}, u32[]{:S(2)}, u32[]{:S(2)}) %collective-permute-start.12) | collective-permute-done | bytes 245792 | tf_op jit(solution)/shard_map/ppermute | solution.py:432
  222.0 2.1 collective-permute-start.17
  224.1 3.2 %collective-permute-done.13.rest_2_ = bf16[2,3,160,128]{3,2,1,0:T(8,128)(2,1)S(1)} collective-permute-done((bf16[2,3,160,128]{3,2,1,0:T(8,128)(2,1)S(1)}, bf16[2,3,160,128]{3,2,1,0:T(8,128)(2,1)S(1)}, u32[]{:S(2)}, u32[]{:S(2)}) %collective-permute-start.13) | collective-permute-done | bytes 245792 | tf_op jit(solution)/shard_map/ppermute | solution.py:432
  227.3 3.0 %collective-permute-start.18 = (bf16[2,3,160,128]{3,2,1,0:T(8,128)(2,1)}, bf16[2,3,160,128]{3,2,1,0:T(8,128)(2,1)S(1)}, u32[]{:S(2)}, u32[]{:S(2)}) collective-permute-start(bf16[2,3,160,128]{3,2,1,0:T(8,128)(2,1)} %get-tuple-element.63), channel_id=1, source_target_pairs={{0,6},{1,7},{2,4},{3,5},{4,2},{5,3},{6,0},{7,1},{8,14},{9,15},{10,... | collective-permute-start | bytes 737288 | tf_op jit(solution)/shard_map/ppermute | solution.py:432
  230.3 0.0 all-to-all-done.1.rest_8_
  230.3 2.9 %collective-permute-done.14.rest_3_ = bf16[2,3,160,128]{3,2,1,0:T(8,128)(2,1)S(1)} collective-permute-done((bf16[2,3,160,128]{3,2,1,0:T(8,128)(2,1)S(1)}, bf16[2,3,160,128]{3,2,1,0:T(8,128)(2,1)S(1)}, u32[]{:S(2)}, u32[]{:S(2)}) %collective-permute-start.14) | collective-permute-done | bytes 245792 | tf_op jit(solution)/shard_map/ppermute | solution.py:432
  233.2 8.3 %collective-permute-done.15.rest_4_ = bf16[2,3,160,128]{3,2,1,0:T(8,128)(2,1)S(1)} collective-permute-done((bf16[2,3,160,128]{3,2,1,0:T(8,128)(2,1)S(1)}, bf16[2,3,160,128]{3,2,1,0:T(8,128)(2,1)S(1)}, u32[]{:S(2)}, u32[]{:S(2)}) %collective-permute-start.15) | collective-permute-done | bytes 245792 | tf_op jit(solution)/shard_map/ppermute | solution.py:432
  241.4 0.0 collective-permute-done.16.rest_5_
  241.4 0.0 collective-permute-done.17.rest_6_
  241.4 0.0 collective-permute-done.18.rest_7_
  241.5 6.2 %assemble.1 = bf16[3,160,32,128]{3,2,1,0:T(8,128)(2,1)} custom-call(s32[1]{0:T(128)} %bitcast.me_ref, bf16[256,256]{1,0:T(8,128)(2,1)S(1)} %copy-done.9, bf16[2,3,160,128]{3,2,1,0:T(8,128)(2,1)S(1)} %get-tuple-element.56.rest_0_, bf16[2,3,160,128]{3,2,1,0:T(8,128)(2,1)S(1)} %collective-permute-done.12.rest_1_, ...), custom_call_target="tpu_custom_call" | custom-call | flops 1006632960 | bytes 7864320 | tf_op jit(solution)/shard_map/assemble/pallas_call | solution.py:409
  (21 shorter events, 0.0 us)
Async XLA Ops:
  0.0 8.7 %copy-start.13 = (f32[32,2]{0,1:T(2,128)S(1)}, f32[32,2]{0,1:T(2,128)}, u32[]{:S(2)}) copy-start(f32[32,2]{0,1:T(2,128)} %param.15) | copy-start | bytes 772
  0.0 8.8 %copy-start.4 = (bf16[32,18,2,1280]{3,2,1,0:T(2,128)(2,1)S(1)}, bf16[32,18,2,1280]{3,2,1,0:T(2,128)(2,1)}, u32[]{:S(2)}) copy-start(bf16[32,18,2,1280]{3,2,1,0:T(2,128)(2,1)} %inverse_ref.1) | copy-start | bytes 8847364
  6.0 13.3 %collective-permute-start.1 = (bf16[2,3,160,128]{3,2,1,0:T(8,128)(2,1)}, bf16[2,3,160,128]{3,2,1,0:T(8,128)(2,1)S(1)}, u32[]{:S(2)}, u32[]{:S(2)}) collective-permute-start(bf16[2,3,160,128]{3,2,1,0:T(8,128)(2,1)} %get-tuple-element.36), channel_id=1, source_target_pairs={{0,8},{1,9},{2,10},{3,11},{4,12},{5,13},{6,14},{7,15},{8,0},{9,1},... | collective-permute-start | bytes 737288 | tf_op jit(solution)/shard_map/ppermute | solution.py:432
  8.8 0.7 copy-start.11
  11.8 0.7 copy-start.2
  19.4 0.7 copy-start.5
  25.9 10.5 %copy-start.3 = (f32[18,2,1280]{2,1,0:T(2,128)S(1)}, f32[18,2,1280]{2,1,0:T(2,128)}, u32[]{:S(2)}) copy-start(f32[18,2,1280]{2,1,0:T(2,128)} %copy-done.2) | copy-start | bytes 552964
  25.9 16.9 %copy-start.15 = (bf16[2,3,160,128]{3,2,1,0:T(8,128)(2,1)S(1)}, bf16[2,3,160,128]{3,2,1,0:T(8,128)(2,1)}, u32[]{:S(2)}) copy-start(bf16[2,3,160,128]{3,2,1,0:T(8,128)(2,1)} %get-tuple-element.43) | copy-start | bytes 737284
  25.9 71.8 %copy-start.14 = (bf16[2,3,160,128]{3,2,1,0:T(8,128)(2,1)S(1)}, bf16[2,3,160,128]{3,2,1,0:T(8,128)(2,1)}, u32[]{:S(2)}) copy-start(bf16[2,3,160,128]{3,2,1,0:T(8,128)(2,1)} %get-tuple-element.44) | copy-start | bytes 737284
  25.9 86.5 %copy-start.6 = (bf16[2,3,160,128]{3,2,1,0:T(8,128)(2,1)S(1)}, bf16[2,3,160,128]{3,2,1,0:T(8,128)(2,1)}, u32[]{:S(2)}) copy-start(bf16[2,3,160,128]{3,2,1,0:T(8,128)(2,1)} %copy-done.5) | copy-start | bytes 737284
  25.9 86.5 %copy-start.8 = (bf16[2,3,160,128]{3,2,1,0:T(8,128)(2,1)S(1)}, bf16[2,3,160,128]{3,2,1,0:T(8,128)(2,1)}, u32[]{:S(2)}) copy-start(bf16[2,3,160,128]{3,2,1,0:T(8,128)(2,1)} %get-tuple-element.38.rest_2_.rest_0_) | copy-start | bytes 737284
  25.9 86.5 %copy-start.10 = (f32[8,128]{1,0:T(8,128)S(1)}, f32[8,128]{1,0:T(8,128)}, u32[]{:S(2)}) copy-start(f32[8,128]{1,0:T(8,128)} %get-tuple-element.37.rest_0_.token_ref) | copy-start | bytes 12292
  25.9 114.2 %all-to-all-start = ((bf16[16,3,160,128]{3,2,1,0:T(8,128)(2,1)}), bf16[16,3,160,128]{3,2,1,0:T(8,128)(2,1)S(1)}, u32[]{:S(2)}, u32[]{:S(2)}) async-start(bf16[16,3,160,128]{3,2,1,0:T(8,128)(2,1)} %get-tuple-element.46), calls=%async_computation | async-start | bytes 3932160 | tf_op jit(solution)/shard_map/all_to_all | solution.py:441
  33.1 82.3 %copy-start = (bf16[3,2,128,1280]{3,2,1,0:T(8,128)(2,1)S(1)}, bf16[3,2,128,1280]{3,2,1,0:T(8,128)(2,1)}, u32[]{:S(2)}) copy-start(bf16[3,2,128,1280]{3,2,1,0:T(8,128)(2,1)} %state_ref.3) | copy-start | bytes 5898244
  33.1 82.3 %copy-start.12 = (s32[2]{0:T(128)S(1)}, s32[2]{0:T(128)}, u32[]{:S(2)}) copy-start(s32[2]{0:T(128)} %wave_ref.3) | copy-start | bytes 28
  33.1 64.7 %collective-permute-start.2 = (bf16[2,3,160,128]{3,2,1,0:T(8,128)(2,1)}, bf16[2,3,160,128]{3,2,1,0:T(8,128)(2,1)S(1)}, u32[]{:S(2)}, u32[]{:S(2)}) collective-permute-start(bf16[2,3,160,128]{3,2,1,0:T(8,128)(2,1)} %get-tuple-element.39), channel_id=1, source_target_pairs={{0,10},{1,11},{2,8},{3,9},{4,14},{5,15},{6,12},{7,13},{8,2},{9,3},... | collective-permute-start | bytes 737288 | tf_op jit(solution)/shard_map/ppermute | solution.py:432
  36.4 6.4 %collective-permute-start = (f32[18,2,1280]{2,1,0:T(2,128)S(1)}, f32[18,2,1280]{2,1,0:T(2,128)S(1)}, u32[]{:S(2)}, u32[]{:S(2)}) collective-permute-start(f32[18,2,1280]{2,1,0:T(2,128)S(1)} %copy-done.3), channel_id=1, source_target_pairs={{0,16},{16,0},{1,17},{17,1},{2,18},{18,2},{3,19},{19,3},{4,20},{20... | collective-permute-start | bytes 552968 | tf_op jit(solution)/shard_map/ppermute | solution.py:461
  37.9 66.8 %collective-permute-start.3 = (bf16[2,3,160,128]{3,2,1,0:T(8,128)(2,1)}, bf16[2,3,160,128]{3,2,1,0:T(8,128)(2,1)S(1)}, u32[]{:S(2)}, u32[]{:S(2)}) collective-permute-start(bf16[2,3,160,128]{3,2,1,0:T(8,128)(2,1)} %get-tuple-element.40), channel_id=1, source_target_pairs={{0,12},{1,13},{2,14},{3,15},{4,8},{5,9},{6,10},{7,11},{8,4},{9,5},... | collective-permute-start | bytes 737288 | tf_op jit(solution)/shard_map/ppermute | solution.py:432
  37.9 74.5 %collective-permute-start.4 = (bf16[2,3,160,128]{3,2,1,0:T(8,128)(2,1)}, bf16[2,3,160,128]{3,2,1,0:T(8,128)(2,1)S(1)}, u32[]{:S(2)}, u32[]{:S(2)}) collective-permute-start(bf16[2,3,160,128]{3,2,1,0:T(8,128)(2,1)} %get-tuple-element.41), channel_id=1, source_target_pairs={{0,14},{1,15},{2,12},{3,13},{4,10},{5,11},{6,8},{7,9},{8,6},{9,7},... | collective-permute-start | bytes 737288 | tf_op jit(solution)/shard_map/ppermute | solution.py:432
  40.0 72.5 %collective-permute-start.5 = (bf16[2,3,160,128]{3,2,1,0:T(8,128)(2,1)}, bf16[2,3,160,128]{3,2,1,0:T(8,128)(2,1)S(1)}, u32[]{:S(2)}, u32[]{:S(2)}) collective-permute-start(bf16[2,3,160,128]{3,2,1,0:T(8,128)(2,1)} %get-tuple-element.42), channel_id=1, source_target_pairs={{0,2},{1,3},{2,0},{3,1},{4,6},{5,7},{6,4},{7,5},{8,10},{9,11},{10,... | collective-permute-start | bytes 737288 | tf_op jit(solution)/shard_map/ppermute | solution.py:432
  42.8 69.6 %collective-permute-start.6 = (bf16[2,3,160,128]{3,2,1,0:T(8,128)(2,1)S(1)}, bf16[2,3,160,128]{3,2,1,0:T(8,128)(2,1)S(1)}, u32[]{:S(2)}, u32[]{:S(2)}) collective-permute-start(bf16[2,3,160,128]{3,2,1,0:T(8,128)(2,1)S(1)} %copy-done.15), channel_id=1, source_target_pairs={{0,4},{1,5},{2,6},{3,7},{4,0},{5,1},{6,2},{7,3},{8,12},{9,13},{10,... | collective-permute-start | bytes 737288 | tf_op jit(solution)/shard_map/ppermute | solution.py:432
  97.8 14.7 %collective-permute-start.7 = (bf16[2,3,160,128]{3,2,1,0:T(8,128)(2,1)S(1)}, bf16[2,3,160,128]{3,2,1,0:T(8,128)(2,1)S(1)}, u32[]{:S(2)}, u32[]{:S(2)}) collective-permute-start(bf16[2,3,160,128]{3,2,1,0:T(8,128)(2,1)S(1)} %copy-done.14), channel_id=1, source_target_pairs={{0,6},{1,7},{2,4},{3,5},{4,2},{5,3},{6,0},{7,1},{8,14},{9,15},{10,... | collective-permute-start | bytes 737288 | tf_op jit(solution)/shard_map/ppermute | solution.py:432
  112.7 2.6 %collective-permute-start.8 = (bf16[8,3,160,128]{3,2,1,0:T(8,128)(2,1)S(1)}, bf16[8,3,160,128]{3,2,1,0:T(8,128)(2,1)S(1)}, u32[]{:S(2)}, u32[]{:S(2)}) collective-permute-start(bf16[8,3,160,128]{3,2,1,0:T(8,128)(2,1)S(1)} %pick.1), channel_id=1, source_target_pairs={{0,1},{1,0},{2,3},{3,2},{4,5},{5,4},{6,7},{7,6},{8,9},{9,8},{10,11... | collective-permute-start | bytes 2949128 | tf_op jit(solution)/shard_map/ppermute | solution.py:437
  120.2 13.4 %collective-permute-start.9 = (bf16[3,128,640]{2,1,0:T(8,128)(2,1)S(1)}, bf16[3,128,640]{2,1,0:T(8,128)(2,1)}, u32[]{:S(2)}, u32[]{:S(2)}) collective-permute-start(bf16[3,128,640]{2,1,0:T(8,128)(2,1)S(1)} %analyse.2.own_ref), channel_id=1, source_target_pairs={{0,16},{16,0},{1,17},{17,1},{2,18},{18,2},{3,19},{19,3},{4,20},{20... | collective-permute-start | bytes 1474568 | tf_op jit(solution)/shard_map/ppermute | solution.py:472
  138.9 1.3 copy-start.7
  140.2 90.1 %all-to-all-start.1 = ((bf16[16,3,160,128]{3,2,1,0:T(8,128)(2,1)}), bf16[16,3,160,128]{3,2,1,0:T(8,128)(2,1)}, u32[]{:S(2)}, u32[]{:S(2)}) async-start(bf16[16,3,160,128]{3,2,1,0:T(8,128)(2,1)} %copy-done.7), calls=%async_computation.1 | async-start | bytes 3932160 | tf_op jit(solution)/shard_map/all_to_all | solution.py:441
  144.5 1.5 copy-start.1
  152.9 23.8 %collective-permute-start.10 = (bf16[3,128,1280]{2,1,0:T(8,128)(2,1)S(1)}, bf16[3,128,1280]{2,1,0:T(8,128)(2,1)S(1)}, u32[]{:S(2)}, u32[]{:S(2)}) collective-permute-start(bf16[3,128,1280]{2,1,0:T(8,128)(2,1)S(1)} %analyse.3.own_ref), channel_id=1, source_target_pairs={{0,16},{16,0},{1,17},{17,1},{2,18},{18,2},{3,19},{19,3},{4,20},{20... | collective-permute-start | bytes 2949128 | tf_op jit(solution)/shard_map/ppermute | solution.py:472
  187.6 53.9 %copy-start.9 = (bf16[256,256]{1,0:T(8,128)(2,1)S(1)}, bf16[256,256]{1,0:T(8,128)(2,1)}, u32[]{:S(2)}) copy-start(bf16[256,256]{1,0:T(8,128)(2,1)} %constant.22.clone.matrix_ref) | copy-start | bytes 393220
  187.6 2.6 %collective-permute-start.11 = (bf16[8,3,160,128]{3,2,1,0:T(8,128)(2,1)S(1)}, bf16[8,3,160,128]{3,2,1,0:T(8,128)(2,1)S(1)}, u32[]{:S(2)}, u32[]{:S(2)}) collective-permute-start(bf16[8,3,160,128]{3,2,1,0:T(8,128)(2,1)S(1)} %get-tuple-element.47), channel_id=1, source_target_pairs={{0,1},{1,0},{2,3},{3,2},{4,5},{5,4},{6,7},{7,6},{8,9},{9,8},{10,11... | collective-permute-start | bytes 2949128 | tf_op jit(solution)/shard_map/ppermute | solution.py:437
  192.9 29.1 %collective-permute-start.12 = (bf16[2,3,160,128]{3,2,1,0:T(8,128)(2,1)S(1)}, bf16[2,3,160,128]{3,2,1,0:T(8,128)(2,1)S(1)}, u32[]{:S(2)}, u32[]{:S(2)}) collective-permute-start(bf16[2,3,160,128]{3,2,1,0:T(8,128)(2,1)S(1)} %get-tuple-element.57), channel_id=1, source_target_pairs={{0,8},{1,9},{2,10},{3,11},{4,12},{5,13},{6,14},{7,15},{8,0},{9,1},... | collective-permute-start | bytes 737288 | tf_op jit(solution)/shard_map/ppermute | solution.py:432
  195.3 32.0 %collective-permute-start.13 = (bf16[2,3,160,128]{3,2,1,0:T(8,128)(2,1)S(1)}, bf16[2,3,160,128]{3,2,1,0:T(8,128)(2,1)S(1)}, u32[]{:S(2)}, u32[]{:S(2)}) collective-permute-start(bf16[2,3,160,128]{3,2,1,0:T(8,128)(2,1)S(1)} %get-tuple-element.58), channel_id=1, source_target_pairs={{0,10},{1,11},{2,8},{3,9},{4,14},{5,15},{6,12},{7,13},{8,2},{9,3},... | collective-permute-start | bytes 737288 | tf_op jit(solution)/shard_map/ppermute | solution.py:432
  196.8 36.4 %collective-permute-start.14 = (bf16[2,3,160,128]{3,2,1,0:T(8,128)(2,1)S(1)}, bf16[2,3,160,128]{3,2,1,0:T(8,128)(2,1)S(1)}, u32[]{:S(2)}, u32[]{:S(2)}) collective-permute-start(bf16[2,3,160,128]{3,2,1,0:T(8,128)(2,1)S(1)} %get-tuple-element.59), channel_id=1, source_target_pairs={{0,12},{1,13},{2,14},{3,15},{4,8},{5,9},{6,10},{7,11},{8,4},{9,5},... | collective-permute-start | bytes 737288 | tf_op jit(solution)/shard_map/ppermute | solution.py:432
  198.2 43.2 %collective-permute-start.15 = (bf16[2,3,160,128]{3,2,1,0:T(8,128)(2,1)S(1)}, bf16[2,3,160,128]{3,2,1,0:T(8,128)(2,1)S(1)}, u32[]{:S(2)}, u32[]{:S(2)}) collective-permute-start(bf16[2,3,160,128]{3,2,1,0:T(8,128)(2,1)S(1)} %get-tuple-element.60), channel_id=1, source_target_pairs={{0,14},{1,15},{2,12},{3,13},{4,10},{5,11},{6,8},{7,9},{8,6},{9,7},... | collective-permute-start | bytes 737288 | tf_op jit(solution)/shard_map/ppermute | solution.py:432
  198.8 42.7 %collective-permute-start.16 = (bf16[2,3,160,128]{3,2,1,0:T(8,128)(2,1)S(1)}, bf16[2,3,160,128]{3,2,1,0:T(8,128)(2,1)S(1)}, u32[]{:S(2)}, u32[]{:S(2)}) collective-permute-start(bf16[2,3,160,128]{3,2,1,0:T(8,128)(2,1)S(1)} %get-tuple-element.61), channel_id=1, source_target_pairs={{0,2},{1,3},{2,0},{3,1},{4,6},{5,7},{6,4},{7,5},{8,10},{9,11},{10,... | collective-permute-start | bytes 737288 | tf_op jit(solution)/shard_map/ppermute | solution.py:432
  222.0 19.5 %collective-permute-start.17 = (bf16[2,3,160,128]{3,2,1,0:T(8,128)(2,1)S(1)}, bf16[2,3,160,128]{3,2,1,0:T(8,128)(2,1)S(1)}, u32[]{:S(2)}, u32[]{:S(2)}) collective-permute-start(bf16[2,3,160,128]{3,2,1,0:T(8,128)(2,1)S(1)} %get-tuple-element.62), channel_id=1, source_target_pairs={{0,4},{1,5},{2,6},{3,7},{4,0},{5,1},{6,2},{7,3},{8,12},{9,13},{10,... | collective-permute-start | bytes 737288 | tf_op jit(solution)/shard_map/ppermute | solution.py:432
  227.3 14.2 %collective-permute-start.18 = (bf16[2,3,160,128]{3,2,1,0:T(8,128)(2,1)}, bf16[2,3,160,128]{3,2,1,0:T(8,128)(2,1)S(1)}, u32[]{:S(2)}, u32[]{:S(2)}) collective-permute-start(bf16[2,3,160,128]{3,2,1,0:T(8,128)(2,1)} %get-tuple-element.63), channel_id=1, source_target_pairs={{0,6},{1,7},{2,4},{3,5},{4,2},{5,3},{6,0},{7,1},{8,14},{9,15},{10,... | collective-permute-start | bytes 737288 | tf_op jit(solution)/shard_map/ppermute | solution.py:432

commit v10 on v9

v10 whole, which is shorter than its diff:
```python
import functools
import math

import jax
import jax.numpy as jnp
import numpy as np
from jax import lax
from jax.experimental import pallas as pl
from jax.experimental.pallas import tpu as pltpu
from jax.sharding import PartitionSpec as P

BF16 = jnp.bfloat16
F32 = jnp.float32
CORES = 2
ANYWHERE = pl.BlockSpec(memory_space=pl.ANY)
IN_SMEM = pl.BlockSpec(memory_space=pltpu.SMEM)
TOKEN = jax.ShapeDtypeStruct((8, 128), F32)


def call(kernel, name, flops, size, mib=40, **kwargs):
    return pl.pallas_call(
        kernel,
        name=name,
        compiler_params=pltpu.CompilerParams(vmem_limit_bytes=mib * 1024 * 1024),
        cost_estimate=pl.CostEstimate(flops=int(flops), bytes_accessed=int(size), transcendentals=0),
        **kwargs,
    )


def run_copies(copies):
    for copy in copies:
        copy.start()
    for copy in copies:
        copy.wait()


def split_cores(values, core):
    even = [values[i] for i in range(0, len(values), CORES)]
    odd = [values[i] for i in range(1, len(values), CORES)]
    mine = [jnp.where(core == 0, a, b) for a, b in zip(even, odd)]
    others = [jnp.where(core == 0, b, a) for a, b in zip(even, odd)]
    return mine, others


def swap_matrix(rows, columns, picked):
    matrix = np.zeros((len(picked), rows, rows, columns), np.float32)
    for i, c in enumerate(picked):
        matrix[i, np.arange(rows), np.arange(rows), c] = 1.0
    return jnp.asarray(matrix.reshape(len(picked) * rows, rows * columns), BF16)


def weigh_kernel(slot, local_slots, split, waits, me_ref, matrix_ref, gauss_ref, tendency_ref, *rest):
    _, lats, slots, members = tendency_ref.shape
    outs, token_ref, column = rest[waits:-2], rest[-2], rest[-1]
    token_ref[...] = jnp.zeros_like(token_ref)
    first = pl.program_id(1) * lats
    depth, breadth = math.gcd(lats, 16), 16
    matrix = matrix_ref[...]
    owners = breadth // local_slots
    core = me_ref[0] % CORES

    @pl.when((pl.program_id(0) == 0) & (pl.program_id(1) == 0))
    def _():
        total = gauss_ref.shape[1]
        for j in range(0, total, depth):
            line = jnp.broadcast_to(gauss_ref[...], (depth, total))
            here = lax.broadcasted_iota(jnp.int32, line.shape, 0) + j
            mine = lax.broadcasted_iota(jnp.int32, line.shape, 1) == here
            value = jnp.sum(jnp.where(mine, line, 0.0), axis=1, keepdims=True)
            column[j : j + depth, :] = jnp.broadcast_to(value, (depth, members))

    for j in range(0, lats, depth):
        scale = column[pl.ds(pl.multiple_of(first + j, depth), depth), :]
        for s in range(0, slots, 2 * breadth):
            halves = [
                tendency_ref[0, j : j + depth, s + h : s + h + breadth, :].reshape(depth * breadth, members)
                for h in (0, breadth)
            ]
            turned = jnp.dot(matrix, jnp.concatenate(halves, axis=1), preferred_element_type=F32)
            values = [
                turned[i * depth : (i + 1) * depth, h * members : (h + 1) * members] * scale
                for h in range(2)
                for i in range(owners)
            ]
            start = s // local_slots
            if split:
                mine, others = split_cores(values, core)
                for i, (a, b) in enumerate(zip(mine, others)):
                    outs[0][start // CORES + i, 0, 0, j : j + depth, :] = a.astype(BF16)
                    outs[1][start // CORES + i, 0, j : j + depth, :] = b.astype(BF16)
            else:
                for i, value in enumerate(values):
                    chip, target = divmod(start + i, CORES)
                    outs[0][chip, target, 0, j : j + depth, :] = value.astype(BF16)


def lat_block(lats):
    return lats // 2 if lats % 32 == 0 else lats


def weigh(tendency, gauss, me, slot, local_slots, split, waits):
    rows, lats, slots, members = tendency.shape
    each = lat_block(lats)
    matrix = swap_matrix(math.gcd(each, 16), 16, range(slot, 16, local_slots))
    chips = slots // local_slots // CORES
    shapes = [jax.ShapeDtypeStruct((chips, CORES, rows, lats, members), BF16)]
    specs = [pl.BlockSpec((chips, CORES, 1, each, members), lambda r, j, m: (0, 0, r, j, 0))]
    if split:
        shapes += [jax.ShapeDtypeStruct((chips, rows, lats, members), BF16)]
        specs = [pl.BlockSpec((chips, 1, 1, each, members), lambda r, j, m: (0, m[0] % CORES, r, j, 0))]
        specs += [pl.BlockSpec((chips, 1, each, members), lambda r, j, m: (0, r, j, 0))]
    return call(
        functools.partial(weigh_kernel, slot, local_slots, split, len(waits)),
        "weigh",
        2 * 128 * tendency.size,
        3 * tendency.size,
        58,
        out_shape=shapes + [TOKEN],
        grid_spec=pltpu.PrefetchScalarGridSpec(
            num_scalar_prefetch=1,
            grid=(rows, lats // each),
            in_specs=[
                pl.BlockSpec(matrix.shape, lambda r, j, m: (0, 0)),
                pl.BlockSpec((1, lats), lambda r, j, m: (0, 0)),
                pl.BlockSpec((1, each, slots, members), lambda r, j, m: (r, j, 0, 0)),
            ]
            + [ANYWHERE] * len(waits),
            out_specs=specs + [pl.BlockSpec(TOKEN.shape, lambda r, j, m: (0, 0))],
            scratch_shapes=[pltpu.VMEM((lats, members), F32)],
        ),
    )(me, matrix, gauss, tendency, *waits)


def pick_kernel(me_ref, token_ref, in_ref, out_ref):
    out_ref[...] = in_ref[:, 0]


def pick(blocks, me, token):
    chips, _, rows, lats, members = blocks.shape
    return call(
        pick_kernel,
        "pick",
        0,
        2 * blocks.size,
        out_shape=jax.ShapeDtypeStruct((chips, rows, lats, members), BF16),
        grid_spec=pltpu.PrefetchScalarGridSpec(
            num_scalar_prefetch=1,
            grid=(rows,),
            in_specs=[
                ANYWHERE,
                pl.BlockSpec((chips, 1, 1, lats, members), lambda r, m: (0, CORES - 1 - m[0] % CORES, r, 0, 0))
            ],
            out_specs=pl.BlockSpec((chips, 1, lats, members), lambda r, m: (0, r, 0, 0)),
        ),
    )(me, token, blocks)


def pair_kernel(me_ref, mate_ref, blocks_ref, out_ref, token_ref, sem):
    token_ref[...] = jnp.zeros_like(token_ref)
    other = CORES - 1 - me_ref[0] % CORES
    run_copies([pltpu.make_async_copy(mate_ref, out_ref.at[:, other], sem)])


def pair(blocks, mate, me):
    return call(
        pair_kernel,
        "pair",
        0,
        4 * mate.size,
        out_shape=[jax.ShapeDtypeStruct(blocks.shape, blocks.dtype), TOKEN],
        in_specs=[IN_SMEM, pl.BlockSpec(mate.shape, lambda: (0, 0, 0, 0)), ANYWHERE],
        out_specs=[ANYWHERE, pl.BlockSpec(TOKEN.shape, lambda: (0, 0))],
        scratch_shapes=[pltpu.SemaphoreType.DMA],
        input_output_aliases={2: 0},
    )(me, mate, blocks)


def analyse_kernel(slot, low, count, me_ref, wave_ref, token_ref, table_ref, state_ref, *rest):
    blocks, out, grid, sems = rest[:count], rest[count], rest[count + 1], rest[count + 2]
    rows, members, _ = out.shape
    chips, cores, lats, _ = grid.shape
    width = table_ref.shape[1]
    step = pl.program_id(0)

    @pl.when(step == 0)
    def _():
        copies = []
        core = me_ref[0] % CORES
        for r in range(rows):
            lanes = pl.ds(r * members, members)
            if count == 1:
                copies.append(pltpu.make_async_copy(blocks[0].at[:, :, r], grid.at[:, :, :, lanes], sems.at[0, r]))
            else:
                target = grid.at[:, core, :, lanes]
                copies.append(pltpu.make_async_copy(blocks[0].at[:, core, r], target, sems.at[0, r]))
                target = grid.at[:, CORES - 1 - core, :, lanes]
                copies.append(pltpu.make_async_copy(blocks[1].at[:, r], target, sems.at[1, r]))
        run_copies(copies)

    field = grid[...].reshape(chips * cores * lats, rows * members)
    sums = jnp.dot(table_ref[0], field, preferred_element_type=F32)
    degree = lax.broadcasted_iota(jnp.int32, (members, width), 1) + (low + step * width)
    live = degree >= wave_ref[slot]
    for r in range(rows):
        total = state_ref[r, 0].astype(F32) + sums[:, r * members : (r + 1) * members].T
        out[r] = jnp.where(live, total, 0.0).astype(BF16)


def analyse(blocks, table, state, wave, me, token, slot, low, width):
    chips, _, rows, lats, members = blocks[0].shape
    nspec, nlat = table.shape[1:]
    first = low // width
    cores = CORES
    if lats % 16:
        if len(blocks) > 1:
            core = me[0] % CORES
            own = lax.dynamic_index_in_dim(blocks[0], core, 1, keepdims=False)
            pairs = [jnp.where(core == 0, own, blocks[1]), jnp.where(core == 0, blocks[1], own)]
            blocks = [jnp.stack(pairs, axis=1)]
        laid = jnp.transpose(blocks[0], (2, 0, 1, 3, 4)).reshape(1, 1, rows, nlat, members)
        blocks, chips, cores, lats = [laid], 1, 1, nlat
    return call(
        functools.partial(analyse_kernel, slot, low, len(blocks)),
        "analyse",
        2 * (nspec - low) * nlat * rows * members,
        2 * (nspec - low) * nlat,
        out_shape=jax.ShapeDtypeStruct((rows, members, nspec - low), BF16),
        grid=((nspec - low) // width,),
        in_specs=[
            IN_SMEM,
            IN_SMEM,
            ANYWHERE,
            pl.BlockSpec((1, width, nlat), lambda i: (slot, first + i, 0)),
            pl.BlockSpec((rows, 1, members, width), lambda i: (0, slot, 0, first + i)),
        ]
        + [ANYWHERE] * len(blocks),
        out_specs=pl.BlockSpec((rows, members, width), lambda i: (0, 0, i)),
        scratch_shapes=[
            pltpu.VMEM((chips, cores, lats, rows * members), BF16),
            pltpu.SemaphoreType.DMA((CORES, rows)),
        ],
    )(me, wave, token, table, state, *blocks)


def sum_pairs_kernel(coeff_ref, token_ref, inverse_ref, out_ref):
    pairs, entries = inverse_ref.shape[:2]
    half = entries // 2

    def one(entry, carry):
        real = imag = 0.0
        for k in range(pairs):
            first, second = inverse_ref[k, entry].astype(F32), inverse_ref[k, half + entry].astype(F32)
            a, b = coeff_ref[k, 0], coeff_ref[k, 1]
            real = real + (a * first - b * second)
            imag = imag + (a * second + b * first)
        out_ref[entry] = real
        out_ref[half + entry] = imag
        return carry

    lax.fori_loop(0, half, one, 0)


def sum_pairs(block_inverses, pole_coeffs, token):
    return call(
        sum_pairs_kernel,
        "sum_pairs",
        4 * block_inverses.size,
        2 * block_inverses.size,
        out_shape=jax.ShapeDtypeStruct(block_inverses.shape[1:], F32),
        in_specs=[IN_SMEM, ANYWHERE, pl.BlockSpec(block_inverses.shape, lambda: (0, 0, 0, 0))],
        out_specs=pl.BlockSpec(block_inverses.shape[1:], lambda: (0, 0, 0)),
    )(pole_coeffs, token, block_inverses)


def synthesise_kernel(slot, low, me_ref, sign_ref, here_ref, there_ref, own_ref, other_ref, table_ref, *rest):
    rows, members, _ = own_ref.shape
    step = pl.program_id(0)
    own_out, mate_out, mixed = rest

    @pl.when(step == 0)
    def _():
        def line(entry):
            return here_ref[entry, slot : slot + 1, low:] + there_ref[entry, slot : slot + 1, low:]

        for f in range(rows):
            total = 0.0
            for g in range(rows):
                total = total + line(f * rows + g) * own_ref[g].astype(F32)
                total = total + sign_ref[0] * line(rows * rows + f * rows + g) * other_ref[g].astype(F32)
            mixed[f * members : (f + 1) * members, :] = total.astype(BF16)

    sums = jnp.dot(mixed[...], table_ref[0], preferred_element_type=F32)
    lats = own_out.shape[3]
    for r in range(rows):
        turned = sums[r * members : (r + 1) * members, :].T
        values = [turned[i : i + lats] for i in range(0, turned.shape[0], lats)]
        mine, others = split_cores(values, me_ref[0] % CORES)
        for i, (a, b) in enumerate(zip(mine, others)):
            own_out[i, 0, r] = a.astype(BF16)
            mate_out[i, r] = b.astype(BF16)


def synthesise(here, there, sign, own, other, table, me, slot, low, lats):
    rows, members, count = own.shape
    nlat = table.shape[2]
    width = math.lcm(CORES * lats, 128)
    chips, each = nlat // lats // CORES, width // lats // CORES
    matrix = pl.BlockSpec(here.shape, lambda j, m: (0, 0, 0))
    whole = pl.BlockSpec((rows, members, count), lambda j, m: (0, 0, 0))
    smem = pl.BlockSpec(memory_space=pltpu.SMEM)
    return call(
        functools.partial(synthesise_kernel, slot, low),
        "synthesise",
        2 * count * nlat * rows * members,
        2 * count * nlat,
        out_shape=[
            jax.ShapeDtypeStruct((chips, CORES, rows, lats, members), BF16),
            jax.ShapeDtypeStruct((chips, rows, lats, members), BF16),
        ],
        grid_spec=pltpu.PrefetchScalarGridSpec(
            num_scalar_prefetch=1,
            grid=(nlat // width,),
            in_specs=[
                smem,
                matrix,
                matrix,
                whole,
                whole,
                pl.BlockSpec((1, count, width), lambda j, m: (slot, low // count, j)),
            ],
            out_specs=[
                pl.BlockSpec((each, 1, rows, lats, members), lambda j, m: (j, m[0] % CORES, 0, 0, 0)),
                pl.BlockSpec((each, rows, lats, members), lambda j, m: (j, 0, 0, 0)),
            ],
            scratch_shapes=[pltpu.VMEM((rows * members, count), BF16)],
        ),
    )(me, sign, here, there, own, other, table)


def assemble_kernel(matrix_ref, *rest):
    ins, out = rest[:-1], rest[-1]
    _, lats, slots, members = out.shape
    local_slots = len(ins)
    depth, breadth = math.gcd(lats, 16), 16
    matrix = matrix_ref[...]
    for start in range(0, lats, depth):
        j = slice(start, start + depth)
        for s in range(0, slots, 2 * breadth):
            halves = []
            for h in (0, breadth):
                columns = [divmod(i, local_slots) for i in range(s + h, s + h + breadth)]
                columns = [ins[slot][owner // CORES, owner % CORES, 0, j, :] for owner, slot in columns]
                halves.append(jnp.concatenate(columns, axis=0))
            turned = jnp.dot(matrix, jnp.concatenate(halves, axis=1), preferred_element_type=F32).astype(BF16)
            for h in range(2):
                value = turned[:, h * members : (h + 1) * members].reshape(depth, breadth, members)
                out[0, j, s + h * breadth : s + (h + 1) * breadth, :] = value


def assemble(pieces):
    chips, cores, rows, lats, members = pieces[0].shape
    slots = len(pieces) * chips * cores
    each = lat_block(lats)
    matrix = swap_matrix(16, math.gcd(each, 16), range(math.gcd(each, 16)))
    piece = pl.BlockSpec((chips, cores, 1, each, members), lambda r, j: (0, 0, r, j, 0))
    return call(
        assemble_kernel,
        "assemble",
        2 * 256 * rows * lats * slots * members,
        4 * rows * lats * slots * members,
        out_shape=jax.ShapeDtypeStruct((rows, lats, slots, members), BF16),
        grid=(rows, lats // each),
        in_specs=[pl.BlockSpec(matrix.shape, lambda r, j: (0, 0))] + [piece] * len(pieces),
        out_specs=pl.BlockSpec((1, each, slots, members), lambda r, j: (r, j, 0, 0)),
    )(matrix, *pieces)


def between_cores(blocks, owners):
    return lax.ppermute(blocks, "wave", [(d, d ^ 1) for d in range(owners)])


def between_chips(blocks, owners):
    groups = [list(range(core, owners, CORES)) for core in range(CORES)]
    return lax.all_to_all(blocks, "wave", split_axis=0, concat_axis=0, axis_index_groups=groups, tiled=True)


def per_device(
    tendency, spectral_state, legendre, gauss_weights, block_inverses, pole_coeffs, wavenumbers
):
    rows, lats, slots, members = tendency.shape
    local_slots, nspec, nlat = legendre.shape
    owners = slots // local_slots
    me = lax.axis_index("wave").astype(jnp.int32).reshape(1)
    pole_index = lax.axis_index("pole")
    sign = (2 * pole_index - 1).astype(F32).reshape(1)
    order = list(range(local_slots))[::-1]
    received, waits = {}, []
    for slot in order:
        early = slot == order[0]
        *blocks, token = weigh(tendency, gauss_weights[None], me, slot, local_slots, not early, waits)
        if early:
            received[slot] = between_chips(blocks[0], owners)
            here = sum_pairs(block_inverses, pole_coeffs, token)
            there = lax.ppermute(here, "pole", [(0, 1), (1, 0)])
            waits = [there]
        else:
            blocks, token = pair(blocks[0], between_cores(blocks[1], owners), me)
            received[slot] = between_chips(blocks, owners)

    sent = {}
    for slot in order:
        low = nspec // 2 if slot % 2 else 0
        blocks = [received[slot]]
        if slot == order[0]:
            blocks.append(between_cores(pick(blocks[0], me, token), owners))
        forced = analyse(blocks, legendre, spectral_state, wavenumbers, me, token, slot, low, nspec // 2)
        other = lax.ppermute(forced, "pole", [(0, 1), (1, 0)])
        own, for_mate = synthesise(here, there, sign, forced, other, legendre, me, slot, low, lats)
        blocks, token = pair(own, between_cores(for_mate, owners), me)
        sent[slot] = between_chips(blocks, owners)
    return assemble([sent[slot] for slot in range(local_slots)])


def solution(mesh):
    in_specs = (
        P("pole", "wave", None, None),
        P("pole", "wave", None, None),
        P("wave", None, None),
        P("wave"),
        P("pole", None, "wave", None),
        P("pole", None),
        P("wave"),
    )
    out_specs = P("pole", "wave", None, None)
    return jax.shard_map(
        per_device, mesh=mesh, in_specs=in_specs, out_specs=out_specs, check_vma=False
    )
```

time: 249 us -> 214 us (0.86)
  waiting for transfers between devices: 148 us -> 81.2 us
  blocking collectives: 0 us -> 51.3 us
  starting transfers between devices: 43.3 us -> 25.2 us
  Pallas kernels: 51.1 us -> 47.6 us
    ppermute x14 -> x0, waiting for transfers between devices: 108 us -> none  [between_chips(): lax.ppermute(message, 'wave', [(d, d ^ k * CORES) for d in range(chips *...]
    all_to_all x0 -> x1, blocking collectives: none -> 51.3 us  [between_chips(): lax.all_to_all(blocks, 'wave', split_axis=0, concat_axis=0, axis_index_gr...]
    all_to_all x2 -> x3, waiting for transfers between devices: 0.01 us -> 33.7 us  [between_chips(): lax.all_to_all(blocks, 'wave', split_axis=0, concat_axis=0, axis_index_gr...]
    ppermute x14 -> x0, starting transfers between devices: 27 us -> none  [between_chips(): lax.ppermute(message, 'wave', [(d, d ^ k * CORES) for d in range(chips *...]
    all_to_all x2 -> x3, starting transfers between devices: 11.4 us -> 20.3 us  [between_chips(): lax.all_to_all(blocks, 'wave', split_axis=0, concat_axis=0, axis_index_gr...]
    ppermute x2 -> x4, waiting for transfers between devices: 5.11 us -> 10.4 us  [between_cores(): return lax.ppermute(blocks, 'wave', [(d, d ^ 1) for d in range(owners)])]
    pallas_call x6, Pallas kernels: 34.4 us -> 31.3 us  [the longest x2 13.3 us: synthesise(): call(functools.partial(synthesise_kernel, slot, low), 'synthesise', 2 * c...]
    ppermute x1, waiting for transfers between devices: 1.4 us -> 4.3 us  [per_device(): there = lax.ppermute(here, 'pole', [(0, 1), (1, 0)])]
  transfers between devices with their start and end apart: 21 -> 10, of which waited for: 13 -> 10; matrix products, arithmetic and copies ran while one was open for 0% -> 0% of each run, Pallas kernels for 13% -> 17%
where the time goes in v10:
time: 214 us; the launch traced here: 211 us
  waiting for transfers between devices  81.2 us (38%)
  blocking collectives  51.3 us (24%)
  Pallas kernels  47.6 us (22%)
  starting transfers between devices  25.2 us (12%)
  local copies, waits for them, and re-layouts  5.44 us (3%)
    all_to_all x1, blocking collectives, between_chips(): lax.all_to_all(blocks, 'wave', split_axis=0, concat_axis=0, axis_index_gr...  51.3 us
    all_to_all x3, waiting for transfers between devices, between_chips(): lax.all_to_all(blocks, 'wave', split_axis=0, concat_axis=0, axis_index_gr...  33.7 us
    ppermute x2, waiting for transfers between devices, per_device(): other = lax.ppermute(forced, 'pole', [(0, 1), (1, 0)])  32.8 us
    all_to_all x3, starting transfers between devices, between_chips(): lax.all_to_all(blocks, 'wave', split_axis=0, concat_axis=0, axis_index_gr...  20.3 us
    pallas_call x2, Pallas kernels, synthesise(): call(functools.partial(synthesise_kernel, slot, low), 'synthesise', 2 * c...  13.3 us
    pallas_call x2, Pallas kernels, analyse(): call(functools.partial(analyse_kernel, slot, low, len(blocks)), 'analyse'...  12.2 us
    pallas_call x2, Pallas kernels, weigh(): call(functools.partial(weigh_kernel, slot, local_slots, split, len(waits)...  11.7 us
    ppermute x4, waiting for transfers between devices, between_cores(): return lax.ppermute(blocks, 'wave', [(d, d ^ 1) for d in range(owners)])  10.4 us
  transfers between devices with their start and end apart: 10, of which 10 were waited for; matrix products, arithmetic and copies ran while one was open for 0% of the time, Pallas kernels for 17%

profile of v10, /device:TPU:8, one launch (start us, length us, event | category | flops | bytes accessed | tf_op | source)
XLA Modules:
  0.0 210.8 jit_solution(5599543773183358072)
XLA Ops:
  0.0 5.8 %weigh.2 = (bf16[8,2,3,160,128]{4,3,2,1,0:T(8,128)(2,1)}, f32[8,128]{1,0:T(8,128)}) custom-call(s32[1]{0:T(128)} %bitcast.me_ref, bf16[128,256]{1,0:T(8,128)(2,1)} %constant.20.clone.matrix_ref, f32[1,160]{1,0:T(1,128)} %bitcast.3, bf16[3,160,32,128]{3,2,1,0:T(8,128)(2,1)} %tendency_ref.3), custom_call_target="tpu_custom_call" | custom-call | flops 503316480 | bytes 5898240 | tf_op jit(solution)/shard_map/weigh/pallas_call | solution.py:112
  5.8 0.0 copy-start.10
  5.8 0.0 copy-start.8
  5.8 6.4 %all-to-all-start = ((bf16[8,2,3,160,128]{4,3,2,1,0:T(8,128)(2,1)}), bf16[8,2,3,160,128]{4,3,2,1,0:T(8,128)(2,1)S(1)}, u32[]{:S(2)}, u32[]{:S(2)}) async-start(bf16[8,2,3,160,128]{4,3,2,1,0:T(8,128)(2,1)} %get-tuple-element.22), calls=%async_computation | async-start | bytes 3932160 | tf_op jit(solution)/shard_map/all_to_all | solution.py:384
  12.2 0.0 copy-done.10
  12.2 0.1 copy.14.coeff_ref
  12.3 0.0 copy-done.8
  12.3 0.0 copy-start.4
  12.3 1.8 copy-done.4
  14.1 2.4 %sum_pairs.1.here_ref = f32[18,2,1280]{2,1,0:T(2,128)S(1)} custom-call(f32[32,2]{1,0:T(8,128)S(1)} %copy.14.coeff_ref, f32[8,128]{1,0:T(8,128)S(1)} %copy-done.8, bf16[32,18,2,1280]{3,2,1,0:T(2,128)(2,1)S(1)} %copy-done.4), custom_call_target="tpu_custom_call" | custom-call | flops 5898240 | bytes 2949120 | tf_op jit(solution)/shard_map/sum_pairs/pallas_call | solution.py:264
  16.5 1.6 collective-permute-start
  18.1 4.3 %collective-permute-done.rest_0_.there_ref = f32[18,2,1280]{2,1,0:T(2,128)S(1)} collective-permute-done((f32[18,2,1280]{2,1,0:T(2,128)S(1)}, f32[18,2,1280]{2,1,0:T(2,128)S(1)}, u32[]{:S(2)}, u32[]{:S(2)}) %collective-permute-start) | collective-permute-done | bytes 184352 | tf_op jit(solution)/shard_map/ppermute | solution.py:404
  22.4 0.0 copy-start.5
  22.4 0.7 copy-done.5
  23.1 5.9 %weigh.3 = (bf16[8,2,3,160,128]{4,3,2,1,0:T(8,128)(2,1)}, bf16[8,3,160,128]{3,2,1,0:T(8,128)(2,1)}, f32[8,128]{1,0:T(8,128)}) custom-call(s32[1]{0:T(128)} %bitcast.me_ref, bf16[128,256]{1,0:T(8,128)(2,1)} %constant.21.clone.matrix_ref, f32[1,160]{1,0:T(1,128)} %bitcast.4, bf16[3,160,32,128]{3,2,1,0:T(8,128)(2,1)} %tendency_ref.3, f32[18,2,1280]{2,1,0:T(2,128)} %copy-done.5), custom_call_target="tpu_custom_call" | custom-call | flops 503316480 | bytes 5898240 | tf_op jit(solution)/shard_map/weigh/pallas_call | solution.py:112
  29.0 0.0 collective-permute-start.1
  29.0 2.8 %collective-permute-done.1.mate_ref = bf16[8,3,160,128]{3,2,1,0:T(8,128)(2,1)S(1)} collective-permute-done((bf16[8,3,160,128]{3,2,1,0:T(8,128)(2,1)}, bf16[8,3,160,128]{3,2,1,0:T(8,128)(2,1)S(1)}, u32[]{:S(2)}, u32[]{:S(2)}) %collective-permute-start.1) | collective-permute-done | bytes 983072 | tf_op jit(solution)/shard_map/ppermute | solution.py:379
  31.8 0.0 copy-start
  31.8 1.5 copy-done
  33.3 0.1 pair.3
  33.4 0.0 copy-start.1
  33.5 1.3 copy-done.1
  34.7 20.5 %all-to-all-done.in_ref.rest_0_ = bf16[8,2,3,160,128]{4,3,2,1,0:T(8,128)(2,1)S(1)} async-done(((bf16[8,2,3,160,128]{4,3,2,1,0:T(8,128)(2,1)}), bf16[8,2,3,160,128]{4,3,2,1,0:T(8,128)(2,1)S(1)}, u32[]{:S(2)}, u32[]{:S(2)}) %all-to-all-start) | async-done | bytes 1966112 | tf_op jit(solution)/shard_map/all_to_all | solution.py:384
  55.2 6.7 %all-to-all-start.1 = ((bf16[8,2,3,160,128]{4,3,2,1,0:T(8,128)(2,1)}), bf16[8,2,3,160,128]{4,3,2,1,0:T(8,128)(2,1)}, u32[]{:S(2)}, u32[]{:S(2)}) async-start(bf16[8,2,3,160,128]{4,3,2,1,0:T(8,128)(2,1)} %copy-done.1), calls=%async_computation.1 | async-start | bytes 3932160 | tf_op jit(solution)/shard_map/all_to_all | solution.py:384
  61.9 0.0 copy-start.2
  61.9 0.0 copy-start.9
  61.9 0.3 pick.1
  62.2 0.0 copy-start.6
  62.2 0.1 collective-permute-start.2
  62.3 2.6 %collective-permute-done.2.rest_1_ = bf16[8,3,160,128]{3,2,1,0:T(8,128)(2,1)S(1)} collective-permute-done((bf16[8,3,160,128]{3,2,1,0:T(8,128)(2,1)S(1)}, bf16[8,3,160,128]{3,2,1,0:T(8,128)(2,1)S(1)}, u32[]{:S(2)}, u32[]{:S(2)}) %collective-permute-start.2) | collective-permute-done | bytes 983072 | tf_op jit(solution)/shard_map/ppermute | solution.py:379
  64.8 0.0 copy-done.2
  64.8 0.0 copy-done.9
  64.8 4.4 %analyse.2.own_ref = bf16[3,128,640]{2,1,0:T(8,128)(2,1)S(1)} custom-call(s32[1]{0:T(128)} %bitcast.me_ref, s32[2]{0:T(128)S(1)} %copy-done.9, f32[8,128]{1,0:T(8,128)S(1)} %get-tuple-element.21.token_ref, bf16[2,1280,2560]{2,1,0:T(8,128)(2,1)} %table_ref.7, bf16[3,2,128,1280]{3,2,1,0:T(8,128)(2,1)S(1)} %copy-done.2, ...), custom_call_target="tpu_custom_call" | custom-call | flops 1258291200 | bytes 3276800 | tf_op jit(solution)/shard_map/analyse/pallas_call | solution.py:222
  69.2 1.6 collective-permute-start.3
  70.8 11.7 %collective-permute-done.3.other_ref = bf16[3,128,640]{2,1,0:T(8,128)(2,1)S(1)} collective-permute-done((bf16[3,128,640]{2,1,0:T(8,128)(2,1)S(1)}, bf16[3,128,640]{2,1,0:T(8,128)(2,1)S(1)}, u32[]{:S(2)}, u32[]{:S(2)}) %collective-permute-start.3) | collective-permute-done | bytes 491552 | tf_op jit(solution)/shard_map/ppermute | solution.py:417
  82.5 0.0 copy-done.6
  82.5 6.0 %synthesise.2 = (bf16[8,2,3,160,128]{4,3,2,1,0:T(8,128)(2,1)}, bf16[8,3,160,128]{3,2,1,0:T(8,128)(2,1)S(1)}) custom-call(s32[1]{0:T(128)} %bitcast.me_ref, f32[1]{0:T(128)} %bitcast.1.sign_ref, f32[18,2,1280]{2,1,0:T(2,128)S(1)} %sum_pairs.1.here_ref, f32[18,2,1280]{2,1,0:T(2,128)S(1)} %copy-done.6, bf16[3,128,640]{2,1,0:T(8,128)(2,1)S(1)} %analyse.2.own_ref, ...), custom_call_target="tpu_custom_call" | custom-call | flops 1258291200 | bytes 3276800 | tf_op jit(solution)/shard_map/synthesise/pallas_call | solution.py:311
  88.5 0.0 collective-permute-start.4
  88.5 2.6 %collective-permute-done.4.mate_ref = bf16[8,3,160,128]{3,2,1,0:T(8,128)(2,1)S(1)} collective-permute-done((bf16[8,3,160,128]{3,2,1,0:T(8,128)(2,1)S(1)}, bf16[8,3,160,128]{3,2,1,0:T(8,128)(2,1)S(1)}, u32[]{:S(2)}, u32[]{:S(2)}) %collective-permute-start.4) | collective-permute-done | bytes 983072 | tf_op jit(solution)/shard_map/ppermute | solution.py:379
  91.1 1.0 pair.4
  92.0 12.1 %all-to-all-done.1.rest_0_ = bf16[8,2,3,160,128]{4,3,2,1,0:T(8,128)(2,1)} async-done(((bf16[8,2,3,160,128]{4,3,2,1,0:T(8,128)(2,1)}), bf16[8,2,3,160,128]{4,3,2,1,0:T(8,128)(2,1)}, u32[]{:S(2)}, u32[]{:S(2)}) %all-to-all-start.1) | async-done | bytes 1966112 | tf_op jit(solution)/shard_map/all_to_all | solution.py:384
  104.1 0.0 copy-start.3
  104.1 7.2 %all-to-all-start.3 = ((bf16[8,2,3,160,128]{4,3,2,1,0:T(8,128)(2,1)}), bf16[8,2,3,160,128]{4,3,2,1,0:T(8,128)(2,1)}, u32[]{:S(2)}, u32[]{:S(2)}) async-start(bf16[8,2,3,160,128]{4,3,2,1,0:T(8,128)(2,1)} %get-tuple-element.30), calls=%async_computation.3 | async-start | bytes 3932160 | tf_op jit(solution)/shard_map/all_to_all | solution.py:384
  111.4 0.0 copy-done.3
  111.4 7.8 %analyse.3.own_ref = bf16[3,128,1280]{2,1,0:T(8,128)(2,1)S(1)} custom-call(s32[1]{0:T(128)} %bitcast.me_ref, s32[2]{0:T(128)S(1)} %copy-done.9, f32[8,128]{1,0:T(8,128)S(1)} %get-tuple-element.25.token_ref, bf16[2,1280,2560]{2,1,0:T(8,128)(2,1)} %table_ref.7, bf16[3,2,128,1280]{3,2,1,0:T(8,128)(2,1)S(1)} %copy-done.3, ...), custom_call_target="tpu_custom_call" | custom-call | flops 2516582400 | bytes 6553600 | tf_op jit(solution)/shard_map/analyse/pallas_call | solution.py:222
  119.2 1.6 collective-permute-start.5
  120.8 21.0 %collective-permute-done.5.other_ref = bf16[3,128,1280]{2,1,0:T(8,128)(2,1)S(1)} collective-permute-done((bf16[3,128,1280]{2,1,0:T(8,128)(2,1)S(1)}, bf16[3,128,1280]{2,1,0:T(8,128)(2,1)S(1)}, u32[]{:S(2)}, u32[]{:S(2)}) %collective-permute-start.5) | collective-permute-done | bytes 983072 | tf_op jit(solution)/shard_map/ppermute | solution.py:417
  141.8 7.3 %synthesise.3 = (bf16[8,2,3,160,128]{4,3,2,1,0:T(8,128)(2,1)S(1)}, bf16[8,3,160,128]{3,2,1,0:T(8,128)(2,1)S(1)}) custom-call(s32[1]{0:T(128)} %bitcast.me_ref, f32[1]{0:T(128)} %bitcast.1.sign_ref, f32[18,2,1280]{2,1,0:T(2,128)S(1)} %sum_pairs.1.here_ref, f32[18,2,1280]{2,1,0:T(2,128)S(1)} %copy-done.6, bf16[3,128,1280]{2,1,0:T(8,128)(2,1)S(1)} %analyse.3.own_ref, ...), custom_call_target="tpu_custom_call" | custom-call | flops 2516582400 | bytes 6553600 | tf_op jit(solution)/shard_map/synthesise/pallas_call | solution.py:311
  149.1 0.1 collective-permute-start.6
  149.2 2.6 %collective-permute-done.6.mate_ref = bf16[8,3,160,128]{3,2,1,0:T(8,128)(2,1)S(1)} collective-permute-done((bf16[8,3,160,128]{3,2,1,0:T(8,128)(2,1)S(1)}, bf16[8,3,160,128]{3,2,1,0:T(8,128)(2,1)S(1)}, u32[]{:S(2)}, u32[]{:S(2)}) %collective-permute-start.6) | collective-permute-done | bytes 983072 | tf_op jit(solution)/shard_map/ppermute | solution.py:379
  151.8 0.7 pair.5
  152.5 1.1 all-to-all-done.3.rest_1_
  153.6 0.0 copy-start.7
  153.6 51.3 %all_to_all.20.rest_0_ = bf16[8,2,3,160,128]{4,3,2,1,0:T(8,128)(2,1)S(1)} all-to-all(bf16[8,2,3,160,128]{4,3,2,1,0:T(8,128)(2,1)S(1)} %get-tuple-element.29), channel_id=1, replica_groups={{0,2,4,6,8,10,12,14},{1,3,5,7,9,11,13,15},{16,18,20,22,24,26,28,30},{17..., dimensions={0} | all-to-all | bytes 3932160 | tf_op jit(solution)/shard_map/all_to_all | solution.py:384
  204.9 0.0 copy-done.7
  204.9 6.0 %assemble.1 = bf16[3,160,32,128]{3,2,1,0:T(8,128)(2,1)} custom-call(bf16[256,256]{1,0:T(8,128)(2,1)S(1)} %copy-done.7, bf16[8,2,3,160,128]{4,3,2,1,0:T(8,128)(2,1)S(1)} %all_to_all.20.rest_0_, bf16[8,2,3,160,128]{4,3,2,1,0:T(8,128)(2,1)} %all-to-all-done.3.rest_1_), custom_call_target="tpu_custom_call" | custom-call | flops 1006632960 | bytes 7864320 | tf_op jit(solution)/shard_map/assemble/pallas_call | solution.py:366
Async XLA Ops:
  5.8 6.4 %copy-start.10 = (f32[32,2]{0,1:T(2,128)S(1)}, f32[32,2]{0,1:T(2,128)}, u32[]{:S(2)}) copy-start(f32[32,2]{0,1:T(2,128)} %param.15) | copy-start | bytes 772
  5.8 6.5 %copy-start.8 = (f32[8,128]{1,0:T(8,128)S(1)}, f32[8,128]{1,0:T(8,128)}, u32[]{:S(2)}) copy-start(f32[8,128]{1,0:T(8,128)} %get-tuple-element.18.token_ref) | copy-start | bytes 12292
  5.8 49.4 %all-to-all-start = ((bf16[8,2,3,160,128]{4,3,2,1,0:T(8,128)(2,1)}), bf16[8,2,3,160,128]{4,3,2,1,0:T(8,128)(2,1)S(1)}, u32[]{:S(2)}, u32[]{:S(2)}) async-start(bf16[8,2,3,160,128]{4,3,2,1,0:T(8,128)(2,1)} %get-tuple-element.22), calls=%async_computation | async-start | bytes 3932160 | tf_op jit(solution)/shard_map/all_to_all | solution.py:384
  12.3 1.8 copy-start.4
  16.5 5.9 %collective-permute-start = (f32[18,2,1280]{2,1,0:T(2,128)S(1)}, f32[18,2,1280]{2,1,0:T(2,128)S(1)}, u32[]{:S(2)}, u32[]{:S(2)}) collective-permute-start(f32[18,2,1280]{2,1,0:T(2,128)S(1)} %sum_pairs.1.here_ref), channel_id=1, source_target_pairs={{0,16},{16,0},{1,17},{17,1},{2,18},{18,2},{3,19},{19,3},{4,20},{20... | collective-permute-start | bytes 552968 | tf_op jit(solution)/shard_map/ppermute | solution.py:404
  22.4 0.7 copy-start.5
  29.0 2.8 %collective-permute-start.1 = (bf16[8,3,160,128]{3,2,1,0:T(8,128)(2,1)}, bf16[8,3,160,128]{3,2,1,0:T(8,128)(2,1)S(1)}, u32[]{:S(2)}, u32[]{:S(2)}) collective-permute-start(bf16[8,3,160,128]{3,2,1,0:T(8,128)(2,1)} %get-tuple-element.19), channel_id=1, source_target_pairs={{0,1},{1,0},{2,3},{3,2},{4,5},{5,4},{6,7},{7,6},{8,9},{9,8},{10,11... | collective-permute-start | bytes 2949128 | tf_op jit(solution)/shard_map/ppermute | solution.py:379
  31.8 1.5 copy-start
  33.4 1.3 copy-start.1
  55.2 48.9 %all-to-all-start.1 = ((bf16[8,2,3,160,128]{4,3,2,1,0:T(8,128)(2,1)}), bf16[8,2,3,160,128]{4,3,2,1,0:T(8,128)(2,1)}, u32[]{:S(2)}, u32[]{:S(2)}) async-start(bf16[8,2,3,160,128]{4,3,2,1,0:T(8,128)(2,1)} %copy-done.1), calls=%async_computation.1 | async-start | bytes 3932160 | tf_op jit(solution)/shard_map/all_to_all | solution.py:384
  61.9 2.9 %copy-start.2 = (bf16[3,2,128,1280]{3,2,1,0:T(8,128)(2,1)S(1)}, bf16[3,2,128,1280]{3,2,1,0:T(8,128)(2,1)}, u32[]{:S(2)}) copy-start(bf16[3,2,128,1280]{3,2,1,0:T(8,128)(2,1)} %state_ref.3) | copy-start | bytes 5898244
  61.9 3.0 %copy-start.9 = (s32[2]{0:T(128)S(1)}, s32[2]{0:T(128)}, u32[]{:S(2)}) copy-start(s32[2]{0:T(128)} %wave_ref.3) | copy-start | bytes 28
  62.2 20.4 %copy-start.6 = (f32[18,2,1280]{2,1,0:T(2,128)S(1)}, f32[18,2,1280]{2,1,0:T(2,128)}, u32[]{:S(2)}) copy-start(f32[18,2,1280]{2,1,0:T(2,128)} %copy-done.5) | copy-start | bytes 552964
  62.2 2.6 %collective-permute-start.2 = (bf16[8,3,160,128]{3,2,1,0:T(8,128)(2,1)S(1)}, bf16[8,3,160,128]{3,2,1,0:T(8,128)(2,1)S(1)}, u32[]{:S(2)}, u32[]{:S(2)}) collective-permute-start(bf16[8,3,160,128]{3,2,1,0:T(8,128)(2,1)S(1)} %pick.1), channel_id=1, source_target_pairs={{0,1},{1,0},{2,3},{3,2},{4,5},{5,4},{6,7},{7,6},{8,9},{9,8},{10,11... | collective-permute-start | bytes 2949128 | tf_op jit(solution)/shard_map/ppermute | solution.py:379
  69.2 13.3 %collective-permute-start.3 = (bf16[3,128,640]{2,1,0:T(8,128)(2,1)S(1)}, bf16[3,128,640]{2,1,0:T(8,128)(2,1)S(1)}, u32[]{:S(2)}, u32[]{:S(2)}) collective-permute-start(bf16[3,128,640]{2,1,0:T(8,128)(2,1)S(1)} %analyse.2.own_ref), channel_id=1, source_target_pairs={{0,16},{16,0},{1,17},{17,1},{2,18},{18,2},{3,19},{19,3},{4,20},{20... | collective-permute-start | bytes 1474568 | tf_op jit(solution)/shard_map/ppermute | solution.py:417
  88.5 2.6 %collective-permute-start.4 = (bf16[8,3,160,128]{3,2,1,0:T(8,128)(2,1)S(1)}, bf16[8,3,160,128]{3,2,1,0:T(8,128)(2,1)S(1)}, u32[]{:S(2)}, u32[]{:S(2)}) collective-permute-start(bf16[8,3,160,128]{3,2,1,0:T(8,128)(2,1)S(1)} %get-tuple-element.23), channel_id=1, source_target_pairs={{0,1},{1,0},{2,3},{3,2},{4,5},{5,4},{6,7},{7,6},{8,9},{9,8},{10,11... | collective-permute-start | bytes 2949128 | tf_op jit(solution)/shard_map/ppermute | solution.py:379
  104.1 7.2 %copy-start.3 = (bf16[3,2,128,1280]{3,2,1,0:T(8,128)(2,1)S(1)}, bf16[3,2,128,1280]{3,2,1,0:T(8,128)(2,1)}, u32[]{:S(2)}) copy-start(bf16[3,2,128,1280]{3,2,1,0:T(8,128)(2,1)} %state_ref.3) | copy-start | bytes 5898244
  104.1 49.5 %all-to-all-start.3 = ((bf16[8,2,3,160,128]{4,3,2,1,0:T(8,128)(2,1)}), bf16[8,2,3,160,128]{4,3,2,1,0:T(8,128)(2,1)}, u32[]{:S(2)}, u32[]{:S(2)}) async-start(bf16[8,2,3,160,128]{4,3,2,1,0:T(8,128)(2,1)} %get-tuple-element.30), calls=%async_computation.3 | async-start | bytes 3932160 | tf_op jit(solution)/shard_map/all_to_all | solution.py:384
  119.2 22.6 %collective-permute-start.5 = (bf16[3,128,1280]{2,1,0:T(8,128)(2,1)S(1)}, bf16[3,128,1280]{2,1,0:T(8,128)(2,1)S(1)}, u32[]{:S(2)}, u32[]{:S(2)}) collective-permute-start(bf16[3,128,1280]{2,1,0:T(8,128)(2,1)S(1)} %analyse.3.own_ref), channel_id=1, source_target_pairs={{0,16},{16,0},{1,17},{17,1},{2,18},{18,2},{3,19},{19,3},{4,20},{20... | collective-permute-start | bytes 2949128 | tf_op jit(solution)/shard_map/ppermute | solution.py:417
  149.1 2.6 %collective-permute-start.6 = (bf16[8,3,160,128]{3,2,1,0:T(8,128)(2,1)S(1)}, bf16[8,3,160,128]{3,2,1,0:T(8,128)(2,1)S(1)}, u32[]{:S(2)}, u32[]{:S(2)}) collective-permute-start(bf16[8,3,160,128]{3,2,1,0:T(8,128)(2,1)S(1)} %get-tuple-element.27), channel_id=1, source_target_pairs={{0,1},{1,0},{2,3},{3,2},{4,5},{5,4},{6,7},{7,6},{8,9},{9,8},{10,11... | collective-permute-start | bytes 2949128 | tf_op jit(solution)/shard_map/ppermute | solution.py:379
  153.6 51.3 %copy-start.7 = (bf16[256,256]{1,0:T(8,128)(2,1)S(1)}, bf16[256,256]{1,0:T(8,128)(2,1)}, u32[]{:S(2)}) copy-start(bf16[256,256]{1,0:T(8,128)(2,1)} %constant.22.clone.matrix_ref) | copy-start | bytes 393220

commit v11 on v10

--- a/solution.py
+++ b/solution.py
@@ -34,6 +34,10 @@
         copy.wait()
 
 
+def partners(chips):
+    return [0] + list(range(chips // 2, chips)) + list(range(1, chips // 2))
+
+
 def split_cores(values, core):
     even = [values[i] for i in range(0, len(values), CORES)]
     odd = [values[i] for i in range(1, len(values), CORES)]
@@ -50,48 +54,63 @@
 
 
 def weigh_kernel(slot, local_slots, split, waits, me_ref, matrix_ref, gauss_ref, tendency_ref, *rest):
-    _, lats, slots, members = tendency_ref.shape
-    outs, token_ref, column = rest[waits:-2], rest[-2], rest[-1]
+    outs, token_ref, (column, held, done, in_sems, out_sems) = rest[waits:-6], rest[-6], rest[-5:]
+    rows, lats, slots, members = held.shape
+    each = in_sems.shape[1]
+    size = lats // each
+    copies = []
+    for r in range(rows):
+        for i in range(each):
+            part = pl.ds(i * size, size)
+            copies.append(pltpu.make_async_copy(tendency_ref.at[r, part], held.at[r, part], in_sems.at[r, i]))
+            copies[-1].start()
     token_ref[...] = jnp.zeros_like(token_ref)
-    first = pl.program_id(1) * lats
-    depth, breadth = math.gcd(lats, 16), 16
+    depth, breadth = math.gcd(size, 16), 16
     matrix = matrix_ref[...]
     owners = breadth // local_slots
     core = me_ref[0] % CORES
-
-    @pl.when((pl.program_id(0) == 0) & (pl.program_id(1) == 0))
-    def _():
-        total = gauss_ref.shape[1]
-        for j in range(0, total, depth):
-            line = jnp.broadcast_to(gauss_ref[...], (depth, total))
-            here = lax.broadcasted_iota(jnp.int32, line.shape, 0) + j
-            mine = lax.broadcasted_iota(jnp.int32, line.shape, 1) == here
-            value = jnp.sum(jnp.where(mine, line, 0.0), axis=1, keepdims=True)
-            column[j : j + depth, :] = jnp.broadcast_to(value, (depth, members))
-
     for j in range(0, lats, depth):
-        scale = column[pl.ds(pl.multiple_of(first + j, depth), depth), :]
-        for s in range(0, slots, 2 * breadth):
-            halves = [
-                tendency_ref[0, j : j + depth, s + h : s + h + breadth, :].reshape(depth * breadth, members)
-                for h in (0, breadth)
-            ]
-            turned = jnp.dot(matrix, jnp.concatenate(halves, axis=1), preferred_element_type=F32)
-            values = [
-                turned[i * depth : (i + 1) * depth, h * members : (h + 1) * members] * scale
-                for h in range(2)
-                for i in range(owners)
-            ]
-            start = s // local_slots
-            if split:
-                mine, others = split_cores(values, core)
-                for i, (a, b) in enumerate(zip(mine, others)):
-                    outs[0][start // CORES + i, 0, 0, j : j + depth, :] = a.astype(BF16)
-                    outs[1][start // CORES + i, 0, j : j + depth, :] = b.astype(BF16)
-            else:
-                for i, value in enumerate(values):
-                    chip, target = divmod(start + i, CORES)
-                    outs[0][chip, target, 0, j : j + depth, :] = value.astype(BF16)
+        line = jnp.broadcast_to(gauss_ref[...], (depth, lats))
+        here = lax.broadcasted_iota(jnp.int32, line.shape, 0) + j
+        mine = lax.broadcasted_iota(jnp.int32, line.shape, 1) == here
+        value = jnp.sum(jnp.where(mine, line, 0.0), axis=1, keepdims=True)
+        column[j : j + depth, :] = jnp.broadcast_to(value, (depth, members))
+    results = []
+    for r in range(rows):
+        for j in range(0, lats, depth):
+            if j % size == 0:
+                copies[r * each + j // size].wait()
+            scale = column[j : j + depth, :]
+            for s in range(0, slots, 2 * breadth):
+                halves = [
+                    held[r, j : j + depth, s + h : s + h + breadth, :].reshape(depth * breadth, members)
+                    for h in (0, breadth)
+                ]
+                turned = jnp.dot(matrix, jnp.concatenate(halves, axis=1), preferred_element_type=F32)
+                values = [
+                    turned[i * depth : (i + 1) * depth, h * members : (h + 1) * members] * scale
+                    for h in range(2)
+                    for i in range(owners)
+                ]
+                start = s // local_slots
+                if split:
+                    mine, others = split_cores(values, core)
+                    for i, (a, b) in enumerate(zip(mine, others)):
+                        done[start // CORES + i, 0, r, j : j + depth, :] = a.astype(BF16)
+                        done[start // CORES + i, 1, r, j : j + depth, :] = b.astype(BF16)
+                else:
+                    for i, value in enumerate(values):
+                        chip, target = divmod(start + i, CORES)
+                        done[chip, target, r, j : j + depth, :] = value.astype(BF16)
+        if split:
+            results.append(pltpu.make_async_copy(done.at[:, 0, r], outs[0].at[:, core, r], out_sems.at[0, r]))
+            results.append(pltpu.make_async_copy(done.at[:, 1, r], outs[1].at[:, r], out_sems.at[1, r]))
+            results[-2].start()
+        else:
+            results.append(pltpu.make_async_copy(done.at[:, :, r], outs[0].at[:, :, r], out_sems.at[0, r]))
+        results[-1].start()
+    for copy in results:
+        copy.wait()
 
 
 def lat_block(lats):
@@ -100,15 +119,13 @@
 
 def weigh(tendency, gauss, me, slot, local_slots, split, waits):
     rows, lats, slots, members = tendency.shape
-    each = lat_block(lats)
-    matrix = swap_matrix(math.gcd(each, 16), 16, range(slot, 16, local_slots))
+    each = lats // lat_block(lats)
+    depth = math.gcd(lats // each, 16)
+    matrix = swap_matrix(depth, 16, range(slot, 16, local_slots))
     chips = slots // local_slots // CORES
     shapes = [jax.ShapeDtypeStruct((chips, CORES, rows, lats, members), BF16)]
-    specs = [pl.BlockSpec((chips, CORES, 1, each, members), lambda r, j, m: (0, 0, r, j, 0))]
     if split:
         shapes += [jax.ShapeDtypeStruct((chips, rows, lats, members), BF16)]
-        specs = [pl.BlockSpec((chips, 1, 1, each, members), lambda r, j, m: (0, m[0] % CORES, r, j, 0))]
-        specs += [pl.BlockSpec((chips, 1, each, members), lambda r, j, m: (0, r, j, 0))]
     return call(
         functools.partial(weigh_kernel, slot, local_slots, split, len(waits)),
         "weigh",
@@ -116,18 +133,21 @@
         3 * tendency.size,
         58,
         out_shape=shapes + [TOKEN],
-        grid_spec=pltpu.PrefetchScalarGridSpec(
-            num_scalar_prefetch=1,
-            grid=(rows, lats // each),
-            in_specs=[
-                pl.BlockSpec(matrix.shape, lambda r, j, m: (0, 0)),
-                pl.BlockSpec((1, lats), lambda r, j, m: (0, 0)),
-                pl.BlockSpec((1, each, slots, members), lambda r, j, m: (r, j, 0, 0)),
-            ]
-            + [ANYWHERE] * len(waits),
-            out_specs=specs + [pl.BlockSpec(TOKEN.shape, lambda r, j, m: (0, 0))],
-            scratch_shapes=[pltpu.VMEM((lats, members), F32)],
-        ),
+        in_specs=[
+            IN_SMEM,
+            pl.BlockSpec(matrix.shape, lambda: (0, 0)),
+            pl.BlockSpec((1, lats), lambda: (0, 0)),
+            ANYWHERE,
+        ]
+        + [ANYWHERE] * len(waits),
+        out_specs=[ANYWHERE] * len(shapes) + [pl.BlockSpec(TOKEN.shape, lambda: (0, 0))],
+        scratch_shapes=[
+            pltpu.VMEM((lats, members), F32),
+            pltpu.VMEM((rows, lats, slots, members), BF16),
+            pltpu.VMEM((chips, CORES, rows, lats, members), BF16),
+            pltpu.SemaphoreType.DMA((rows, each)),
+            pltpu.SemaphoreType.DMA((CORES, rows)),
+        ],
     )(me, matrix, gauss, tendency, *waits)
 
 
@@ -173,6 +193,33 @@
         scratch_shapes=[pltpu.SemaphoreType.DMA],
         input_output_aliases={2: 0},
     )(me, mate, blocks)
+
+
+def pair_messages_kernel(me_ref, mate_ref, *rest):
+    chips = mate_ref.shape[0]
+    outs, sems = rest[chips:-1], rest[-1]
+    chip, other = me_ref[0] // CORES, CORES - 1 - me_ref[0] % CORES
+    run_copies(
+        [
+            pltpu.make_async_copy(mate_ref.at[chip ^ k], out.at[other], sems.at[i])
+            for i, (k, out) in enumerate(zip(partners(chips), outs))
+        ]
+    )
+
+
+def pair_messages(messages, mate, me):
+    chips = len(messages)
+    return call(
+        pair_messages_kernel,
+        "pair",
+        0,
+        4 * mate.size,
+        out_shape=[jax.ShapeDtypeStruct(m.shape, m.dtype) for m in messages],
+        in_specs=[IN_SMEM, pl.BlockSpec(mate.shape, lambda: (0, 0, 0, 0))] + [ANYWHERE] * chips,
+        out_specs=[ANYWHERE] * chips,
+        scratch_shapes=[pltpu.SemaphoreType.DMA((chips,))],
+        input_output_aliases={i + 2: i for i in range(chips)},
+    )(me, mate, *messages)
 
 
 def analyse_kernel(slot, low, count, me_ref, wave_ref, token_ref, table_ref, state_ref, *rest):
@@ -272,10 +319,13 @@
     )(pole_coeffs, token, block_inverses)
 
 
-def synthesise_kernel(slot, low, me_ref, sign_ref, here_ref, there_ref, own_ref, other_ref, table_ref, *rest):
+def synthesise_kernel(slot, low, apart, me_ref, sign_ref, here_ref, there_ref, own_ref, other_ref, table_ref, *rest):
     rows, members, _ = own_ref.shape
     step = pl.program_id(0)
-    own_out, mate_out, mixed = rest
+    if apart:
+        outs, mate_out, mixed, held, sems = rest[:-4], rest[-4], rest[-3], rest[-2], rest[-1]
+    else:
+        own_out, mate_out, mixed = rest
 
     @pl.when(step == 0)
     def _():
@@ -290,17 +340,33 @@
             mixed[f * members : (f + 1) * members, :] = total.astype(BF16)
 
     sums = jnp.dot(mixed[...], table_ref[0], preferred_element_type=F32)
-    lats = own_out.shape[3]
+    lats = mate_out.shape[2]
+    each = mate_out.shape[0]
     for r in range(rows):
         turned = sums[r * members : (r + 1) * members, :].T
         values = [turned[i : i + lats] for i in range(0, turned.shape[0], lats)]
         mine, others = split_cores(values, me_ref[0] % CORES)
         for i, (a, b) in enumerate(zip(mine, others)):
-            own_out[i, 0, r] = a.astype(BF16)
+            if apart:
+                held[step * each + i, r] = a.astype(BF16)
+            else:
+                own_out[i, 0, r] = a.astype(BF16)
             mate_out[i, r] = b.astype(BF16)
 
-
-def synthesise(here, there, sign, own, other, table, me, slot, low, lats):
+    if apart:
+        chip, core = me_ref[0] // CORES, me_ref[0] % CORES
+        copies = []
+        for i, (k, out) in enumerate(zip(partners(len(outs)), outs)):
+            copies.append(pltpu.make_async_copy(held.at[chip ^ k], out.at[core], sems.at[i]))
+            pl.when((chip ^ k) // each == step)(copies[-1].start)
+
+        @pl.when(step == pl.num_programs(0) - 1)
+        def _():
+            for copy in copies:
+                copy.wait()
+
+
+def synthesise(here, there, sign, own, other, table, me, slot, low, lats, apart):
     rows, members, count = own.shape
     nlat = table.shape[2]
     width = math.lcm(CORES * lats, 128)
@@ -308,15 +374,19 @@
     matrix = pl.BlockSpec(here.shape, lambda j, m: (0, 0, 0))
     whole = pl.BlockSpec((rows, members, count), lambda j, m: (0, 0, 0))
     smem = pl.BlockSpec(memory_space=pltpu.SMEM)
-    return call(
-        functools.partial(synthesise_kernel, slot, low),
+    shapes = [jax.ShapeDtypeStruct((chips, CORES, rows, lats, members), BF16)]
+    specs = [pl.BlockSpec((each, 1, rows, lats, members), lambda j, m: (j, m[0] % CORES, 0, 0, 0))]
+    scratch = [pltpu.VMEM((rows * members, count), BF16)]
+    if apart:
+        shapes = [jax.ShapeDtypeStruct((CORES, rows, lats, members), BF16)] * chips
+        specs = [ANYWHERE] * chips
+        scratch += [pltpu.VMEM((chips, rows, lats, members), BF16), pltpu.SemaphoreType.DMA((chips,))]
+    return call(
+        functools.partial(synthesise_kernel, slot, low, apart),
         "synthesise",
         2 * count * nlat * rows * members,
         2 * count * nlat,
-        out_shape=[
-            jax.ShapeDtypeStruct((chips, CORES, rows, lats, members), BF16),
-            jax.ShapeDtypeStruct((chips, rows, lats, members), BF16),
-        ],
+        out_shape=shapes + [jax.ShapeDtypeStruct((chips, rows, lats, members), BF16)],
         grid_spec=pltpu.PrefetchScalarGridSpec(
             num_scalar_prefetch=1,
             grid=(nlat // width,),
@@ -328,55 +398,99 @@
                 whole,
                 pl.BlockSpec((1, count, width), lambda j, m: (slot, low // count, j)),
             ],
-            out_specs=[
-                pl.BlockSpec((each, 1, rows, lats, members), lambda j, m: (j, m[0] % CORES, 0, 0, 0)),
-                pl.BlockSpec((each, rows, lats, members), lambda j, m: (j, 0, 0, 0)),
-            ],
-            scratch_shapes=[pltpu.VMEM((rows * members, count), BF16)],
+            out_specs=specs + [pl.BlockSpec((each, rows, lats, members), lambda j, m: (j, 0, 0, 0))],
+            scratch_shapes=scratch,
         ),
     )(me, sign, here, there, own, other, table)
 
 
-def assemble_kernel(matrix_ref, *rest):
-    ins, out = rest[:-1], rest[-1]
-    _, lats, slots, members = out.shape
-    local_slots = len(ins)
-    depth, breadth = math.gcd(lats, 16), 16
+def assemble_kernel(counts, me_ref, matrix_ref, *rest):
+    ins, out_ref, (held, done, in_sems, out_sems) = rest[: sum(counts)], rest[-5], rest[-4:]
+    rows, lats, slots, members = done.shape
+    local_slots = len(counts)
+    chip = me_ref[0] // CORES
+    each = out_sems.shape[1]
+    depth, breadth = math.gcd(lats // each, 16), 16
+    size = lats // each
+    copies, used = [], 0
+    for r in range(rows):
+        copies.append([])
+        used = 0
+        for slot, count in enumerate(counts):
+            refs = ins[used : used + count]
+            used += count
+            if count == 1:
+                copies[r].append(
+                    pltpu.make_async_copy(refs[0].at[:, :, r], held.at[slot, :, :, r], in_sems.at[r, slot, 0])
+                )
+                continue
+            for i, (k, ref) in enumerate(zip(partners(count), refs)):
+                copies[r].append(
+                    pltpu.make_async_copy(ref.at[:, r], held.at[slot, chip ^ k, :, r], in_sems.at[r, slot, i])
+                )
+        for copy in copies[r]:
+            copy.start()
     matrix = matrix_ref[...]
-    for start in range(0, lats, depth):
-        j = slice(start, start + depth)
-        for s in range(0, slots, 2 * breadth):
-            halves = []
-            for h in (0, breadth):
-                columns = [divmod(i, local_slots) for i in range(s + h, s + h + breadth)]
-                columns = [ins[slot][owner // CORES, owner % CORES, 0, j, :] for owner, slot in columns]
-                halves.append(jnp.concatenate(columns, axis=0))
-            turned = jnp.dot(matrix, jnp.concatenate(halves, axis=1), preferred_element_type=F32).astype(BF16)
-            for h in range(2):
-                value = turned[:, h * members : (h + 1) * members].reshape(depth, breadth, members)
-                out[0, j, s + h * breadth : s + (h + 1) * breadth, :] = value
-
-
-def assemble(pieces):
-    chips, cores, rows, lats, members = pieces[0].shape
-    slots = len(pieces) * chips * cores
-    each = lat_block(lats)
-    matrix = swap_matrix(16, math.gcd(each, 16), range(math.gcd(each, 16)))
-    piece = pl.BlockSpec((chips, cores, 1, each, members), lambda r, j: (0, 0, r, j, 0))
-    return call(
-        assemble_kernel,
+    results = []
+    for r in range(rows):
+        for copy in copies[r]:
+            copy.wait()
+        for start in range(0, lats, depth):
+            j = slice(start, start + depth)
+            for s in range(0, slots, 2 * breadth):
+                halves = []
+                for h in (0, breadth):
+                    columns = [divmod(i, local_slots) for i in range(s + h, s + h + breadth)]
+                    columns = [held[slot, owner // CORES, owner % CORES, r, j, :] for owner, slot in columns]
+                    halves.append(jnp.concatenate(columns, axis=0))
+                turned = jnp.dot(matrix, jnp.concatenate(halves, axis=1), preferred_element_type=F32).astype(BF16)
+                for h in range(2):
+                    value = turned[:, h * members : (h + 1) * members].reshape(depth, breadth, members)
+                    done[r, j, s + h * breadth : s + (h + 1) * breadth, :] = value
+            if (start + depth) % size == 0:
+                part = pl.ds(start + depth - size, size)
+                results.append(
+                    pltpu.make_async_copy(done.at[r, part], out_ref.at[r, part], out_sems.at[r, start // size])
+                )
+                results[-1].start()
+    for copy in results:
+        copy.wait()
+
+
+def assemble(pieces, me):
+    rows, lats, members = pieces[0][0].shape[-3:]
+    chips = max(len(p) if len(p) > 1 else p[0].shape[0] for p in pieces)
+    slots = len(pieces) * chips * CORES
+    each = lats // lat_block(lats)
+    matrix = swap_matrix(16, math.gcd(lats // each, 16), range(math.gcd(lats // each, 16)))
+    flat = [block for slot in pieces for block in slot]
+    return call(
+        functools.partial(assemble_kernel, [len(p) for p in pieces]),
         "assemble",
         2 * 256 * rows * lats * slots * members,
         4 * rows * lats * slots * members,
         out_shape=jax.ShapeDtypeStruct((rows, lats, slots, members), BF16),
-        grid=(rows, lats // each),
-        in_specs=[pl.BlockSpec(matrix.shape, lambda r, j: (0, 0))] + [piece] * len(pieces),
-        out_specs=pl.BlockSpec((1, each, slots, members), lambda r, j: (r, j, 0, 0)),
-    )(matrix, *pieces)
+        in_specs=[IN_SMEM, pl.BlockSpec(matrix.shape, lambda: (0, 0))] + [ANYWHERE] * len(flat),
+        out_specs=ANYWHERE,
+        scratch_shapes=[
+            pltpu.VMEM((len(pieces), chips, CORES, rows, lats, members), BF16),
+            pltpu.VMEM((rows, lats, slots, members), BF16),
+            pltpu.SemaphoreType.DMA((rows, len(pieces), chips)),
+            pltpu.SemaphoreType.DMA((rows, each)),
+        ],
+    )(me, matrix, *flat)
 
 
 def between_cores(blocks, owners):
     return lax.ppermute(blocks, "wave", [(d, d ^ 1) for d in range(owners)])
+
+
+def by_permutes(messages):
+    owners = len(messages) * CORES
+    got = [messages[0]]
+    for k, message in list(zip(partners(len(messages)), messages))[1:]:
+        got.append(lax.ppermute(message, "wave", [(d, d ^ (k * CORES)) for d in range(owners)]))
+    return got
 
 
 def between_chips(blocks, owners):
@@ -415,10 +529,15 @@
             blocks.append(between_cores(pick(blocks[0], me, token), owners))
         forced = analyse(blocks, legendre, spectral_state, wavenumbers, me, token, slot, low, nspec // 2)
         other = lax.ppermute(forced, "pole", [(0, 1), (1, 0)])
-        own, for_mate = synthesise(here, there, sign, forced, other, legendre, me, slot, low, lats)
-        blocks, token = pair(own, between_cores(for_mate, owners), me)
-        sent[slot] = between_chips(blocks, owners)
-    return assemble([sent[slot] for slot in range(local_slots)])
+        last = slot == order[-1]
+        *own, for_mate = synthesise(here, there, sign, forced, other, legendre, me, slot, low, lats, last)
+        mate = between_cores(for_mate, owners)
+        if last:
+            sent[slot] = by_permutes(pair_messages(own, mate, me))
+        else:
+            blocks, token = pair(own[0], mate, me)
+            sent[slot] = [between_chips(blocks, owners)]
+    return assemble([sent[slot] for slot in range(local_slots)], me)
 
 
 def solution(mesh):

time: 214 us -> 213 us (level)
  blocking collectives: 51.3 us -> 0 us
  waiting for transfers between devices: 81.2 us -> 117 us
  starting transfers between devices: 25.2 us -> 36.8 us
  local copies, waits for them, and re-layouts: 5.44 us -> 11.2 us
    all_to_all x1 -> x0, blocking collectives: 51.3 us -> none  [between_chips(): lax.all_to_all(blocks, 'wave', split_axis=0, concat_axis=0, axis_index_gr...]
    ppermute x0 -> x7, waiting for transfers between devices: none -> 36 us  [by_permutes(): lax.ppermute(message, 'wave', [(d, d ^ k * CORES) for d in range(owners)])]
    ppermute x0 -> x7, starting transfers between devices: none -> 12.4 us  [by_permutes(): lax.ppermute(message, 'wave', [(d, d ^ k * CORES) for d in range(owners)])]
    unnamed x23 -> x31, local copies, waits for them, and re-layouts: 5.44 us -> 11.2 us
    pallas_call x3 -> x4, Pallas kernels: 19.3 us -> 20 us  [the longest x2 14.3 us: synthesise(): call(functools.partial(synthesise_kernel, slot, low, apart), 'synthesise'...]
  transfers between devices with their start and end apart: 10 -> 17, of which waited for: 10 -> 13; matrix products, arithmetic and copies ran while one was open for 0% -> 0% of each run, Pallas kernels for 17% -> 17%
where the time goes in v11:
time: 213 us; the launch traced here: 212 us
  waiting for transfers between devices  117 us (55%)
  Pallas kernels  46.1 us (22%)
  starting transfers between devices  36.8 us (17%)
  local copies, waits for them, and re-layouts  11.2 us (5%)
    ppermute x7, waiting for transfers between devices, by_permutes(): lax.ppermute(message, 'wave', [(d, d ^ k * CORES) for d in range(owners)])  36 us
    ppermute x2, waiting for transfers between devices, per_device(): other = lax.ppermute(forced, 'pole', [(0, 1), (1, 0)])  33.3 us
    all_to_all x3, waiting for transfers between devices, between_chips(): lax.all_to_all(blocks, 'wave', split_axis=0, concat_axis=0, axis_index_gr...  33.3 us
    all_to_all x3, starting transfers between devices, between_chips(): lax.all_to_all(blocks, 'wave', split_axis=0, concat_axis=0, axis_index_gr...  19.5 us
    pallas_call x2, Pallas kernels, synthesise(): call(functools.partial(synthesise_kernel, slot, low, apart), 'synthesise'...  14.3 us
    ppermute x7, starting transfers between devices, by_permutes(): lax.ppermute(message, 'wave', [(d, d ^ k * CORES) for d in range(owners)])  12.4 us
    pallas_call x2, Pallas kernels, analyse(): call(functools.partial(analyse_kernel, slot, low, len(blocks)), 'analyse'...  12.2 us
    unnamed x31, local copies, waits for them, and re-layouts  11.2 us
  transfers between devices with their start and end apart: 17, of which 13 were waited for; matrix products, arithmetic and copies ran while one was open for 0% of the time, Pallas kernels for 17%

profile of v11, /device:TPU:8, one launch (start us, length us, event | category | flops | bytes accessed | tf_op | source)
XLA Modules:
  0.0 211.8 jit_solution(18032469362674781467)
XLA Ops:
  0.0 5.1 %weigh.2 = (bf16[8,2,3,160,128]{4,3,2,1,0:T(8,128)(2,1)}, f32[8,128]{1,0:T(8,128)}) custom-call(s32[1]{0:T(128)} %bitcast.me_ref, bf16[128,256]{1,0:T(8,128)(2,1)} %constant.20.clone.matrix_ref, f32[1,160]{1,0:T(1,128)} %bitcast.3, bf16[3,160,32,128]{3,2,1,0:T(8,128)(2,1)} %tendency_ref.3), custom_call_target="tpu_custom_call" | custom-call | flops 503316480 | bytes 5898240 | tf_op jit(solution)/shard_map/weigh/pallas_call | solution.py:129
  5.1 0.0 copy-start.14
  5.1 0.0 copy-start.12
  5.1 6.3 %all-to-all-start = ((bf16[8,2,3,160,128]{4,3,2,1,0:T(8,128)(2,1)}), bf16[8,2,3,160,128]{4,3,2,1,0:T(8,128)(2,1)S(1)}, u32[]{:S(2)}, u32[]{:S(2)}) async-start(bf16[8,2,3,160,128]{4,3,2,1,0:T(8,128)(2,1)} %get-tuple-element.36), calls=%async_computation | async-start | bytes 3932160 | tf_op jit(solution)/shard_map/all_to_all | solution.py:498
  11.4 0.0 copy-done.14
  11.4 0.1 copy.21.coeff_ref
  11.5 0.0 copy-done.12
  11.5 1.8 copy-done.4
  13.3 2.4 %sum_pairs.1.here_ref = f32[18,2,1280]{2,1,0:T(2,128)S(1)} custom-call(f32[32,2]{1,0:T(8,128)S(1)} %copy.21.coeff_ref, f32[8,128]{1,0:T(8,128)S(1)} %copy-done.12, bf16[32,18,2,1280]{3,2,1,0:T(2,128)(2,1)S(1)} %copy-done.4), custom_call_target="tpu_custom_call" | custom-call | flops 5898240 | bytes 2949120 | tf_op jit(solution)/shard_map/sum_pairs/pallas_call | solution.py:311
  15.7 1.6 collective-permute-start
  17.3 4.3 %collective-permute-done.rest_0_.there_ref = f32[18,2,1280]{2,1,0:T(2,128)S(1)} collective-permute-done((f32[18,2,1280]{2,1,0:T(2,128)S(1)}, f32[18,2,1280]{2,1,0:T(2,128)S(1)}, u32[]{:S(2)}, u32[]{:S(2)}) %collective-permute-start) | collective-permute-done | bytes 184352 | tf_op jit(solution)/shard_map/ppermute | solution.py:518
  21.6 0.7 copy-done.5
  22.2 5.1 %weigh.3 = (bf16[8,2,3,160,128]{4,3,2,1,0:T(8,128)(2,1)}, bf16[8,3,160,128]{3,2,1,0:T(8,128)(2,1)}, f32[8,128]{1,0:T(8,128)}) custom-call(s32[1]{0:T(128)} %bitcast.me_ref, bf16[128,256]{1,0:T(8,128)(2,1)} %constant.21.clone.matrix_ref, f32[1,160]{1,0:T(1,128)} %bitcast.4, bf16[3,160,32,128]{3,2,1,0:T(8,128)(2,1)} %tendency_ref.3, f32[18,2,1280]{2,1,0:T(2,128)} %copy-done.5), custom_call_target="tpu_custom_call" | custom-call | flops 503316480 | bytes 5898240 | tf_op jit(solution)/shard_map/weigh/pallas_call | solution.py:129
  27.4 0.1 collective-permute-start.1
  27.5 2.8 %collective-permute-done.1.mate_ref = bf16[8,3,160,128]{3,2,1,0:T(8,128)(2,1)S(1)} collective-permute-done((bf16[8,3,160,128]{3,2,1,0:T(8,128)(2,1)}, bf16[8,3,160,128]{3,2,1,0:T(8,128)(2,1)S(1)}, u32[]{:S(2)}, u32[]{:S(2)}) %collective-permute-start.1) | collective-permute-done | bytes 983072 | tf_op jit(solution)/shard_map/ppermute | solution.py:485
  30.2 1.5 copy-done
  31.8 0.1 pair.3
  31.9 0.0 copy-start.1
  31.9 1.3 copy-done.1
  33.1 21.2 %all-to-all-done.in_ref.rest_0_ = bf16[8,2,3,160,128]{4,3,2,1,0:T(8,128)(2,1)S(1)} async-done(((bf16[8,2,3,160,128]{4,3,2,1,0:T(8,128)(2,1)}), bf16[8,2,3,160,128]{4,3,2,1,0:T(8,128)(2,1)S(1)}, u32[]{:S(2)}, u32[]{:S(2)}) %all-to-all-start) | async-done | bytes 1966112 | tf_op jit(solution)/shard_map/all_to_all | solution.py:498
  54.4 6.7 %all-to-all-start.1 = ((bf16[8,2,3,160,128]{4,3,2,1,0:T(8,128)(2,1)}), bf16[8,2,3,160,128]{4,3,2,1,0:T(8,128)(2,1)}, u32[]{:S(2)}, u32[]{:S(2)}) async-start(bf16[8,2,3,160,128]{4,3,2,1,0:T(8,128)(2,1)} %copy-done.1), calls=%async_computation.1 | async-start | bytes 3932160 | tf_op jit(solution)/shard_map/all_to_all | solution.py:498
  61.1 0.3 pick.1
  61.4 0.0 copy-start.6
  61.4 0.1 collective-permute-start.2
  61.4 2.6 %collective-permute-done.2.rest_1_ = bf16[8,3,160,128]{3,2,1,0:T(8,128)(2,1)S(1)} collective-permute-done((bf16[8,3,160,128]{3,2,1,0:T(8,128)(2,1)S(1)}, bf16[8,3,160,128]{3,2,1,0:T(8,128)(2,1)S(1)}, u32[]{:S(2)}, u32[]{:S(2)}) %collective-permute-start.2) | collective-permute-done | bytes 983072 | tf_op jit(solution)/shard_map/ppermute | solution.py:485
  64.0 0.0 copy-done.13
  64.0 4.4 %analyse.2.own_ref = bf16[3,128,640]{2,1,0:T(8,128)(2,1)S(1)} custom-call(s32[1]{0:T(128)} %bitcast.me_ref, s32[2]{0:T(128)S(1)} %copy-done.13, f32[8,128]{1,0:T(8,128)S(1)} %get-tuple-element.35.token_ref, bf16[2,1280,2560]{2,1,0:T(8,128)(2,1)} %table_ref.7, bf16[3,2,128,1280]{3,2,1,0:T(8,128)(2,1)S(1)} %copy-done.2, ...), custom_call_target="tpu_custom_call" | custom-call | flops 1258291200 | bytes 3276800 | tf_op jit(solution)/shard_map/analyse/pallas_call | solution.py:269
  68.4 1.6 collective-permute-start.3
  70.0 11.7 %collective-permute-done.3.other_ref = bf16[3,128,640]{2,1,0:T(8,128)(2,1)S(1)} collective-permute-done((bf16[3,128,640]{2,1,0:T(8,128)(2,1)S(1)}, bf16[3,128,640]{2,1,0:T(8,128)(2,1)S(1)}, u32[]{:S(2)}, u32[]{:S(2)}) %collective-permute-start.3) | collective-permute-done | bytes 491552 | tf_op jit(solution)/shard_map/ppermute | solution.py:531
  81.7 6.0 %synthesise.2 = (bf16[8,2,3,160,128]{4,3,2,1,0:T(8,128)(2,1)}, bf16[8,3,160,128]{3,2,1,0:T(8,128)(2,1)S(1)}) custom-call(s32[1]{0:T(128)} %bitcast.me_ref, f32[1]{0:T(128)} %bitcast.1.sign_ref, f32[18,2,1280]{2,1,0:T(2,128)S(1)} %sum_pairs.1.here_ref, f32[18,2,1280]{2,1,0:T(2,128)S(1)} %copy-done.6, bf16[3,128,640]{2,1,0:T(8,128)(2,1)S(1)} %analyse.2.own_ref, ...), custom_call_target="tpu_custom_call" | custom-call | flops 1258291200 | bytes 3276800 | tf_op jit(solution)/shard_map/synthesise/pallas_call | solution.py:384
  87.7 0.0 collective-permute-start.4
  87.7 2.6 %collective-permute-done.4.mate_ref = bf16[8,3,160,128]{3,2,1,0:T(8,128)(2,1)S(1)} collective-permute-done((bf16[8,3,160,128]{3,2,1,0:T(8,128)(2,1)S(1)}, bf16[8,3,160,128]{3,2,1,0:T(8,128)(2,1)S(1)}, u32[]{:S(2)}, u32[]{:S(2)}) %collective-permute-start.4) | collective-permute-done | bytes 983072 | tf_op jit(solution)/shard_map/ppermute | solution.py:485
  90.3 1.0 pair.4
  91.2 12.1 %all-to-all-done.1.rest_0_ = bf16[8,2,3,160,128]{4,3,2,1,0:T(8,128)(2,1)} async-done(((bf16[8,2,3,160,128]{4,3,2,1,0:T(8,128)(2,1)}), bf16[8,2,3,160,128]{4,3,2,1,0:T(8,128)(2,1)}, u32[]{:S(2)}, u32[]{:S(2)}) %all-to-all-start.1) | async-done | bytes 1966112 | tf_op jit(solution)/shard_map/all_to_all | solution.py:498
  103.3 6.5 %all-to-all-start.2 = ((bf16[8,2,3,160,128]{4,3,2,1,0:T(8,128)(2,1)}), bf16[8,2,3,160,128]{4,3,2,1,0:T(8,128)(2,1)S(1)}, u32[]{:S(2)}, u32[]{:S(2)}) async-start(bf16[8,2,3,160,128]{4,3,2,1,0:T(8,128)(2,1)} %get-tuple-element.58), calls=%async_computation.2 | async-start | bytes 3932160 | tf_op jit(solution)/shard_map/all_to_all | solution.py:498
  109.8 1.5 copy-done.3
  111.4 7.8 %analyse.3.own_ref = bf16[3,128,1280]{2,1,0:T(8,128)(2,1)S(1)} custom-call(s32[1]{0:T(128)} %bitcast.me_ref, s32[2]{0:T(128)S(1)} %copy-done.13, f32[8,128]{1,0:T(8,128)S(1)} %get-tuple-element.39.token_ref, bf16[2,1280,2560]{2,1,0:T(8,128)(2,1)} %table_ref.7, bf16[3,2,128,1280]{3,2,1,0:T(8,128)(2,1)S(1)} %copy-done.3, ...), custom_call_target="tpu_custom_call" | custom-call | flops 2516582400 | bytes 6553600 | tf_op jit(solution)/shard_map/analyse/pallas_call | solution.py:269
  119.2 1.6 collective-permute-start.5
  120.8 21.6 %collective-permute-done.5.other_ref = bf16[3,128,1280]{2,1,0:T(8,128)(2,1)S(1)} collective-permute-done((bf16[3,128,1280]{2,1,0:T(8,128)(2,1)S(1)}, bf16[3,128,1280]{2,1,0:T(8,128)(2,1)S(1)}, u32[]{:S(2)}, u32[]{:S(2)}) %collective-permute-start.5) | collective-permute-done | bytes 983072 | tf_op jit(solution)/shard_map/ppermute | solution.py:531
  142.4 8.4 %synthesise.3 = (bf16[2,3,160,128]{3,2,1,0:T(8,128)(2,1)S(1)}, bf16[2,3,160,128]{3,2,1,0:T(8,128)(2,1)S(1)}, bf16[2,3,160,128]{3,2,1,0:T(8,128)(2,1)S(1)}, bf16[...) custom-call(s32[1]{0:T(128)} %bitcast.me_ref, ...), custom_call_target="tpu_custom_call" | custom-call | flops 2516582400 | bytes 6553600 | tf_op jit(solution)/shard_map/synthesise/pallas_call | solution.py:384
  150.8 0.1 collective-permute-start.6
  150.8 2.6 %collective-permute-done.6.mate_ref = bf16[8,3,160,128]{3,2,1,0:T(8,128)(2,1)S(1)} collective-permute-done((bf16[8,3,160,128]{3,2,1,0:T(8,128)(2,1)S(1)}, bf16[8,3,160,128]{3,2,1,0:T(8,128)(2,1)S(1)}, u32[]{:S(2)}, u32[]{:S(2)}) %collective-permute-start.6) | collective-permute-done | bytes 983072 | tf_op jit(solution)/shard_map/ppermute | solution.py:485
  153.4 1.3 pair.5
  154.7 2.4 %collective-permute-start.7 = (bf16[2,3,160,128]{3,2,1,0:T(8,128)(2,1)S(1)}, bf16[2,3,160,128]{3,2,1,0:T(8,128)(2,1)S(1)}, u32[]{:S(2)}, u32[]{:S(2)}) collective-permute-start(bf16[2,3,160,128]{3,2,1,0:T(8,128)(2,1)S(1)} %get-tuple-element.51), channel_id=1, source_target_pairs={{0,8},{1,9},{2,10},{3,11},{4,12},{5,13},{6,14},{7,15},{8,0},{9,1},... | collective-permute-start | bytes 737288 | tf_op jit(solution)/shard_map/ppermute | solution.py:492
  157.2 1.5 collective-permute-start.8
  158.6 1.5 collective-permute-start.9
  160.1 0.6 collective-permute-start.10
  160.6 1.5 collective-permute-start.11
  162.1 21.7 %collective-permute-done.7.rest_1_ = bf16[2,3,160,128]{3,2,1,0:T(8,128)(2,1)S(1)} collective-permute-done((bf16[2,3,160,128]{3,2,1,0:T(8,128)(2,1)S(1)}, bf16[2,3,160,128]{3,2,1,0:T(8,128)(2,1)S(1)}, u32[]{:S(2)}, u32[]{:S(2)}) %collective-permute-start.7) | collective-permute-done | bytes 245792 | tf_op jit(solution)/shard_map/ppermute | solution.py:492
  183.8 2.0 collective-permute-start.12
  185.8 3.3 %collective-permute-done.8.rest_2_ = bf16[2,3,160,128]{3,2,1,0:T(8,128)(2,1)S(1)} collective-permute-done((bf16[2,3,160,128]{3,2,1,0:T(8,128)(2,1)S(1)}, bf16[2,3,160,128]{3,2,1,0:T(8,128)(2,1)S(1)}, u32[]{:S(2)}, u32[]{:S(2)}) %collective-permute-start.8) | collective-permute-done | bytes 245792 | tf_op jit(solution)/shard_map/ppermute | solution.py:492
  189.1 2.9 %collective-permute-start.13 = (bf16[2,3,160,128]{3,2,1,0:T(8,128)(2,1)S(1)}, bf16[2,3,160,128]{3,2,1,0:T(8,128)(2,1)S(1)}, u32[]{:S(2)}, u32[]{:S(2)}) collective-permute-start(bf16[2,3,160,128]{3,2,1,0:T(8,128)(2,1)S(1)} %get-tuple-element.57), channel_id=1, source_target_pairs={{0,6},{1,7},{2,4},{3,5},{4,2},{5,3},{6,0},{7,1},{8,14},{9,15},{10,... | collective-permute-start | bytes 737288 | tf_op jit(solution)/shard_map/ppermute | solution.py:492
  192.1 2.9 %collective-permute-done.9.rest_3_ = bf16[2,3,160,128]{3,2,1,0:T(8,128)(2,1)S(1)} collective-permute-done((bf16[2,3,160,128]{3,2,1,0:T(8,128)(2,1)S(1)}, bf16[2,3,160,128]{3,2,1,0:T(8,128)(2,1)S(1)}, u32[]{:S(2)}, u32[]{:S(2)}) %collective-permute-start.9) | collective-permute-done | bytes 245792 | tf_op jit(solution)/shard_map/ppermute | solution.py:492
  195.0 8.1 %collective-permute-done.10.rest_4_ = bf16[2,3,160,128]{3,2,1,0:T(8,128)(2,1)S(1)} collective-permute-done((bf16[2,3,160,128]{3,2,1,0:T(8,128)(2,1)S(1)}, bf16[2,3,160,128]{3,2,1,0:T(8,128)(2,1)S(1)}, u32[]{:S(2)}, u32[]{:S(2)}) %collective-permute-start.10) | collective-permute-done | bytes 245792 | tf_op jit(solution)/shard_map/ppermute | solution.py:492
  203.1 0.0 collective-permute-done.11.rest_5_
  203.1 0.0 collective-permute-done.12.rest_6_
  203.1 0.7 copy-done.7
  203.8 0.0 collective-permute-done.13.rest_7_
  203.8 0.7 copy-done.9
  204.5 0.0 all-to-all-done.2.rest_8_
  204.5 0.9 copy-done.8
  205.5 0.9 copy-done.10
  206.4 0.9 copy-done.11
  207.3 4.4 %assemble.1 = bf16[3,160,32,128]{3,2,1,0:T(8,128)(2,1)} custom-call(s32[1]{0:T(128)} %bitcast.me_ref, bf16[256,256]{1,0:T(8,128)(2,1)S(1)} %copy-done.11, bf16[2,3,160,128]{3,2,1,0:T(8,128)(2,1)S(1)} %get-tuple-element.50.rest_0_, bf16[2,3,160,128]{3,2,1,0:T(8,128)(2,1)S(1)} %collective-permute-done.7.rest_1_, ...), custom_call_target="tpu_custom_call" | custom-call | flops 1006632960 | bytes 7864320 | tf_op jit(solution)/shard_map/assemble/pallas_call | solution.py:467
  (13 shorter events, 0.0 us)
Async XLA Ops:
  5.1 6.3 %copy-start.14 = (f32[32,2]{0,1:T(2,128)S(1)}, f32[32,2]{0,1:T(2,128)}, u32[]{:S(2)}) copy-start(f32[32,2]{0,1:T(2,128)} %param.15) | copy-start | bytes 772
  5.1 6.4 %copy-start.12 = (f32[8,128]{1,0:T(8,128)S(1)}, f32[8,128]{1,0:T(8,128)}, u32[]{:S(2)}) copy-start(f32[8,128]{1,0:T(8,128)} %get-tuple-element.32.token_ref) | copy-start | bytes 12292
  5.1 49.2 %all-to-all-start = ((bf16[8,2,3,160,128]{4,3,2,1,0:T(8,128)(2,1)}), bf16[8,2,3,160,128]{4,3,2,1,0:T(8,128)(2,1)S(1)}, u32[]{:S(2)}, u32[]{:S(2)}) async-start(bf16[8,2,3,160,128]{4,3,2,1,0:T(8,128)(2,1)} %get-tuple-element.36), calls=%async_computation | async-start | bytes 3932160 | tf_op jit(solution)/shard_map/all_to_all | solution.py:498
  11.5 1.8 copy-start.4
  15.7 5.9 %collective-permute-start = (f32[18,2,1280]{2,1,0:T(2,128)S(1)}, f32[18,2,1280]{2,1,0:T(2,128)S(1)}, u32[]{:S(2)}, u32[]{:S(2)}) collective-permute-start(f32[18,2,1280]{2,1,0:T(2,128)S(1)} %sum_pairs.1.here_ref), channel_id=1, source_target_pairs={{0,16},{16,0},{1,17},{17,1},{2,18},{18,2},{3,19},{19,3},{4,20},{20... | collective-permute-start | bytes 552968 | tf_op jit(solution)/shard_map/ppermute | solution.py:518
  21.6 0.7 copy-start.5
  27.4 2.8 %collective-permute-start.1 = (bf16[8,3,160,128]{3,2,1,0:T(8,128)(2,1)}, bf16[8,3,160,128]{3,2,1,0:T(8,128)(2,1)S(1)}, u32[]{:S(2)}, u32[]{:S(2)}) collective-permute-start(bf16[8,3,160,128]{3,2,1,0:T(8,128)(2,1)} %get-tuple-element.33), channel_id=1, source_target_pairs={{0,1},{1,0},{2,3},{3,2},{4,5},{5,4},{6,7},{7,6},{8,9},{9,8},{10,11... | collective-permute-start | bytes 2949128 | tf_op jit(solution)/shard_map/ppermute | solution.py:485
  30.2 1.5 copy-start
  31.9 1.3 copy-start.1
  54.4 48.9 %all-to-all-start.1 = ((bf16[8,2,3,160,128]{4,3,2,1,0:T(8,128)(2,1)}), bf16[8,2,3,160,128]{4,3,2,1,0:T(8,128)(2,1)}, u32[]{:S(2)}, u32[]{:S(2)}) async-start(bf16[8,2,3,160,128]{4,3,2,1,0:T(8,128)(2,1)} %copy-done.1), calls=%async_computation.1 | async-start | bytes 3932160 | tf_op jit(solution)/shard_map/all_to_all | solution.py:498
  61.0 2.9 %copy-start.2 = (bf16[3,2,128,1280]{3,2,1,0:T(8,128)(2,1)S(1)}, bf16[3,2,128,1280]{3,2,1,0:T(8,128)(2,1)}, u32[]{:S(2)}) copy-start(bf16[3,2,128,1280]{3,2,1,0:T(8,128)(2,1)} %state_ref.3) | copy-start | bytes 5898244
  61.1 3.0 %copy-start.13 = (s32[2]{0:T(128)S(1)}, s32[2]{0:T(128)}, u32[]{:S(2)}) copy-start(s32[2]{0:T(128)} %wave_ref.3) | copy-start | bytes 28
  61.4 20.4 %copy-start.6 = (f32[18,2,1280]{2,1,0:T(2,128)S(1)}, f32[18,2,1280]{2,1,0:T(2,128)}, u32[]{:S(2)}) copy-start(f32[18,2,1280]{2,1,0:T(2,128)} %copy-done.5) | copy-start | bytes 552964
  61.4 2.6 %collective-permute-start.2 = (bf16[8,3,160,128]{3,2,1,0:T(8,128)(2,1)S(1)}, bf16[8,3,160,128]{3,2,1,0:T(8,128)(2,1)S(1)}, u32[]{:S(2)}, u32[]{:S(2)}) collective-permute-start(bf16[8,3,160,128]{3,2,1,0:T(8,128)(2,1)S(1)} %pick.1), channel_id=1, source_target_pairs={{0,1},{1,0},{2,3},{3,2},{4,5},{5,4},{6,7},{7,6},{8,9},{9,8},{10,11... | collective-permute-start | bytes 2949128 | tf_op jit(solution)/shard_map/ppermute | solution.py:485
  68.4 13.3 %collective-permute-start.3 = (bf16[3,128,640]{2,1,0:T(8,128)(2,1)S(1)}, bf16[3,128,640]{2,1,0:T(8,128)(2,1)S(1)}, u32[]{:S(2)}, u32[]{:S(2)}) collective-permute-start(bf16[3,128,640]{2,1,0:T(8,128)(2,1)S(1)} %analyse.2.own_ref), channel_id=1, source_target_pairs={{0,16},{16,0},{1,17},{17,1},{2,18},{18,2},{3,19},{19,3},{4,20},{20... | collective-permute-start | bytes 1474568 | tf_op jit(solution)/shard_map/ppermute | solution.py:531
  87.7 2.6 %collective-permute-start.4 = (bf16[8,3,160,128]{3,2,1,0:T(8,128)(2,1)S(1)}, bf16[8,3,160,128]{3,2,1,0:T(8,128)(2,1)S(1)}, u32[]{:S(2)}, u32[]{:S(2)}) collective-permute-start(bf16[8,3,160,128]{3,2,1,0:T(8,128)(2,1)S(1)} %get-tuple-element.37), channel_id=1, source_target_pairs={{0,1},{1,0},{2,3},{3,2},{4,5},{5,4},{6,7},{7,6},{8,9},{9,8},{10,11... | collective-permute-start | bytes 2949128 | tf_op jit(solution)/shard_map/ppermute | solution.py:485
  103.3 101.2 %all-to-all-start.2 = ((bf16[8,2,3,160,128]{4,3,2,1,0:T(8,128)(2,1)}), bf16[8,2,3,160,128]{4,3,2,1,0:T(8,128)(2,1)S(1)}, u32[]{:S(2)}, u32[]{:S(2)}) async-start(bf16[8,2,3,160,128]{4,3,2,1,0:T(8,128)(2,1)} %get-tuple-element.58), calls=%async_computation.2 | async-start | bytes 3932160 | tf_op jit(solution)/shard_map/all_to_all | solution.py:498
  109.8 1.5 copy-start.3
  119.2 23.2 %collective-permute-start.5 = (bf16[3,128,1280]{2,1,0:T(8,128)(2,1)S(1)}, bf16[3,128,1280]{2,1,0:T(8,128)(2,1)S(1)}, u32[]{:S(2)}, u32[]{:S(2)}) collective-permute-start(bf16[3,128,1280]{2,1,0:T(8,128)(2,1)S(1)} %analyse.3.own_ref), channel_id=1, source_target_pairs={{0,16},{16,0},{1,17},{17,1},{2,18},{18,2},{3,19},{19,3},{4,20},{20... | collective-permute-start | bytes 2949128 | tf_op jit(solution)/shard_map/ppermute | solution.py:531
  150.8 2.6 %collective-permute-start.6 = (bf16[8,3,160,128]{3,2,1,0:T(8,128)(2,1)S(1)}, bf16[8,3,160,128]{3,2,1,0:T(8,128)(2,1)S(1)}, u32[]{:S(2)}, u32[]{:S(2)}) collective-permute-start(bf16[8,3,160,128]{3,2,1,0:T(8,128)(2,1)S(1)} %get-tuple-element.41), channel_id=1, source_target_pairs={{0,1},{1,0},{2,3},{3,2},{4,5},{5,4},{6,7},{7,6},{8,9},{9,8},{10,11... | collective-permute-start | bytes 2949128 | tf_op jit(solution)/shard_map/ppermute | solution.py:485
  154.7 29.1 %collective-permute-start.7 = (bf16[2,3,160,128]{3,2,1,0:T(8,128)(2,1)S(1)}, bf16[2,3,160,128]{3,2,1,0:T(8,128)(2,1)S(1)}, u32[]{:S(2)}, u32[]{:S(2)}) collective-permute-start(bf16[2,3,160,128]{3,2,1,0:T(8,128)(2,1)S(1)} %get-tuple-element.51), channel_id=1, source_target_pairs={{0,8},{1,9},{2,10},{3,11},{4,12},{5,13},{6,14},{7,15},{8,0},{9,1},... | collective-permute-start | bytes 737288 | tf_op jit(solution)/shard_map/ppermute | solution.py:492
  157.2 32.0 %collective-permute-start.8 = (bf16[2,3,160,128]{3,2,1,0:T(8,128)(2,1)S(1)}, bf16[2,3,160,128]{3,2,1,0:T(8,128)(2,1)S(1)}, u32[]{:S(2)}, u32[]{:S(2)}) collective-permute-start(bf16[2,3,160,128]{3,2,1,0:T(8,128)(2,1)S(1)} %get-tuple-element.52), channel_id=1, source_target_pairs={{0,10},{1,11},{2,8},{3,9},{4,14},{5,15},{6,12},{7,13},{8,2},{9,3},... | collective-permute-start | bytes 737288 | tf_op jit(solution)/shard_map/ppermute | solution.py:492
  158.6 36.3 %collective-permute-start.9 = (bf16[2,3,160,128]{3,2,1,0:T(8,128)(2,1)S(1)}, bf16[2,3,160,128]{3,2,1,0:T(8,128)(2,1)S(1)}, u32[]{:S(2)}, u32[]{:S(2)}) collective-permute-start(bf16[2,3,160,128]{3,2,1,0:T(8,128)(2,1)S(1)} %get-tuple-element.53), channel_id=1, source_target_pairs={{0,12},{1,13},{2,14},{3,15},{4,8},{5,9},{6,10},{7,11},{8,4},{9,5},... | collective-permute-start | bytes 737288 | tf_op jit(solution)/shard_map/ppermute | solution.py:492
  160.1 43.0 %collective-permute-start.10 = (bf16[2,3,160,128]{3,2,1,0:T(8,128)(2,1)S(1)}, bf16[2,3,160,128]{3,2,1,0:T(8,128)(2,1)S(1)}, u32[]{:S(2)}, u32[]{:S(2)}) collective-permute-start(bf16[2,3,160,128]{3,2,1,0:T(8,128)(2,1)S(1)} %get-tuple-element.54), channel_id=1, source_target_pairs={{0,14},{1,15},{2,12},{3,13},{4,10},{5,11},{6,8},{7,9},{8,6},{9,7},... | collective-permute-start | bytes 737288 | tf_op jit(solution)/shard_map/ppermute | solution.py:492
  160.6 42.5 %collective-permute-start.11 = (bf16[2,3,160,128]{3,2,1,0:T(8,128)(2,1)S(1)}, bf16[2,3,160,128]{3,2,1,0:T(8,128)(2,1)S(1)}, u32[]{:S(2)}, u32[]{:S(2)}) collective-permute-start(bf16[2,3,160,128]{3,2,1,0:T(8,128)(2,1)S(1)} %get-tuple-element.55), channel_id=1, source_target_pairs={{0,2},{1,3},{2,0},{3,1},{4,6},{5,7},{6,4},{7,5},{8,10},{9,11},{10,... | collective-permute-start | bytes 737288 | tf_op jit(solution)/shard_map/ppermute | solution.py:492
  183.8 19.3 %collective-permute-start.12 = (bf16[2,3,160,128]{3,2,1,0:T(8,128)(2,1)S(1)}, bf16[2,3,160,128]{3,2,1,0:T(8,128)(2,1)S(1)}, u32[]{:S(2)}, u32[]{:S(2)}) collective-permute-start(bf16[2,3,160,128]{3,2,1,0:T(8,128)(2,1)S(1)} %get-tuple-element.56), channel_id=1, source_target_pairs={{0,4},{1,5},{2,6},{3,7},{4,0},{5,1},{6,2},{7,3},{8,12},{9,13},{10,... | collective-permute-start | bytes 737288 | tf_op jit(solution)/shard_map/ppermute | solution.py:492
  189.1 14.7 %collective-permute-start.13 = (bf16[2,3,160,128]{3,2,1,0:T(8,128)(2,1)S(1)}, bf16[2,3,160,128]{3,2,1,0:T(8,128)(2,1)S(1)}, u32[]{:S(2)}, u32[]{:S(2)}) collective-permute-start(bf16[2,3,160,128]{3,2,1,0:T(8,128)(2,1)S(1)} %get-tuple-element.57), channel_id=1, source_target_pairs={{0,6},{1,7},{2,4},{3,5},{4,2},{5,3},{6,0},{7,1},{8,14},{9,15},{10,... | collective-permute-start | bytes 737288 | tf_op jit(solution)/shard_map/ppermute | solution.py:492
  203.1 0.7 copy-start.7
  203.8 0.7 copy-start.9
  204.5 0.9 copy-start.8
  205.5 0.9 copy-start.10
  206.4 0.9 copy-start.11

commit v12 on v11

--- a/solution.py
+++ b/solution.py
@@ -3,7 +3,6 @@
 
 import jax
 import jax.numpy as jnp
-import numpy as np
 from jax import lax
 from jax.experimental import pallas as pl
 from jax.experimental.pallas import tpu as pltpu
@@ -46,15 +45,19 @@
     return mine, others
 
 
-def swap_matrix(rows, columns, picked):
-    matrix = np.zeros((len(picked), rows, rows, columns), np.float32)
-    for i, c in enumerate(picked):
-        matrix[i, np.arange(rows), np.arange(rows), c] = 1.0
-    return jnp.asarray(matrix.reshape(len(picked) * rows, rows * columns), BF16)
-
-
-def weigh_kernel(slot, local_slots, split, waits, me_ref, matrix_ref, gauss_ref, tendency_ref, *rest):
-    outs, token_ref, (column, held, done, in_sems, out_sems) = rest[waits:-6], rest[-6], rest[-5:]
+def swap_matrix(rows, columns, step, skip):
+    shape = (rows * columns // step, rows * columns)
+    shift = rows.bit_length() - 1
+    target = lax.broadcasted_iota(jnp.int32, shape, 0)
+    source = lax.broadcasted_iota(jnp.int32, shape, 1)
+    wanted = (target & (rows - 1)) * columns + (target >> shift) * step + skip
+    return jnp.where(source == wanted, 1.0, 0.0).astype(BF16)
+
+
+def weigh_kernel(slot, local_slots, split, waits, me_ref, gauss_any, tendency_ref, *rest):
+    outs, token_ref, (gauss_ref, column, held, done, gauss_sem, in_sems, out_sems) = rest[waits:-8], rest[-8], rest[-7:]
+    line_copy = pltpu.make_async_copy(gauss_any, gauss_ref, gauss_sem)
+    line_copy.start()
     rows, lats, slots, members = held.shape
     each = in_sems.shape[1]
     size = lats // each
@@ -66,9 +69,10 @@
             copies[-1].start()
     token_ref[...] = jnp.zeros_like(token_ref)
     depth, breadth = math.gcd(size, 16), 16
-    matrix = matrix_ref[...]
+    matrix = swap_matrix(depth, breadth, local_slots, slot)
     owners = breadth // local_slots
     core = me_ref[0] % CORES
+    line_copy.wait()
     for j in range(0, lats, depth):
         line = jnp.broadcast_to(gauss_ref[...], (depth, lats))
         here = lax.broadcasted_iota(jnp.int32, line.shape, 0) + j
@@ -120,8 +124,6 @@
 def weigh(tendency, gauss, me, slot, local_slots, split, waits):
     rows, lats, slots, members = tendency.shape
     each = lats // lat_block(lats)
-    depth = math.gcd(lats // each, 16)
-    matrix = swap_matrix(depth, 16, range(slot, 16, local_slots))
     chips = slots // local_slots // CORES
     shapes = [jax.ShapeDtypeStruct((chips, CORES, rows, lats, members), BF16)]
     if split:
@@ -133,22 +135,18 @@
         3 * tendency.size,
         58,
         out_shape=shapes + [TOKEN],
-        in_specs=[
-            IN_SMEM,
-            pl.BlockSpec(matrix.shape, lambda: (0, 0)),
-            pl.BlockSpec((1, lats), lambda: (0, 0)),
-            ANYWHERE,
-        ]
-        + [ANYWHERE] * len(waits),
+        in_specs=[IN_SMEM] + [ANYWHERE] * (2 + len(waits)),
         out_specs=[ANYWHERE] * len(shapes) + [pl.BlockSpec(TOKEN.shape, lambda: (0, 0))],
         scratch_shapes=[
+            pltpu.VMEM((1, lats), F32),
             pltpu.VMEM((lats, members), F32),
             pltpu.VMEM((rows, lats, slots, members), BF16),
             pltpu.VMEM((chips, CORES, rows, lats, members), BF16),
+            pltpu.SemaphoreType.DMA,
             pltpu.SemaphoreType.DMA((rows, each)),
             pltpu.SemaphoreType.DMA((CORES, rows)),
         ],
-    )(me, matrix, gauss, tendency, *waits)
+    )(me, gauss, tendency, *waits)
 
 
 def pick_kernel(me_ref, token_ref, in_ref, out_ref):
@@ -223,7 +221,7 @@
 
 
 def analyse_kernel(slot, low, count, me_ref, wave_ref, token_ref, table_ref, state_ref, *rest):
-    blocks, out, grid, sems = rest[:count], rest[count], rest[count + 1], rest[count + 2]
+    blocks, out, grid = rest[:count], rest[count], rest[count + 1]
     rows, members, _ = out.shape
     chips, cores, lats, _ = grid.shape
     width = table_ref.shape[1]
@@ -231,18 +229,14 @@
 
     @pl.when(step == 0)
     def _():
-        copies = []
         core = me_ref[0] % CORES
         for r in range(rows):
-            lanes = pl.ds(r * members, members)
+            lanes = slice(r * members, (r + 1) * members)
             if count == 1:
-                copies.append(pltpu.make_async_copy(blocks[0].at[:, :, r], grid.at[:, :, :, lanes], sems.at[0, r]))
+                grid[:, :, :, lanes] = blocks[0][:, :, r]
             else:
-                target = grid.at[:, core, :, lanes]
-                copies.append(pltpu.make_async_copy(blocks[0].at[:, core, r], target, sems.at[0, r]))
-                target = grid.at[:, CORES - 1 - core, :, lanes]
-                copies.append(pltpu.make_async_copy(blocks[1].at[:, r], target, sems.at[1, r]))
-        run_copies(copies)
+                grid[:, core, :, lanes] = blocks[0][:, 0, r]
+                grid[:, CORES - 1 - core, :, lanes] = blocks[1][:, r]
 
     field = grid[...].reshape(chips * cores * lats, rows * members)
     sums = jnp.dot(table_ref[0], field, preferred_element_type=F32)
@@ -266,26 +260,30 @@
             blocks = [jnp.stack(pairs, axis=1)]
         laid = jnp.transpose(blocks[0], (2, 0, 1, 3, 4)).reshape(1, 1, rows, nlat, members)
         blocks, chips, cores, lats = [laid], 1, 1, nlat
+    windows = [pl.BlockSpec(blocks[0].shape, lambda i, m: (0, 0, 0, 0, 0))]
+    if len(blocks) > 1:
+        shape = (chips, 1) + blocks[0].shape[2:]
+        windows = [pl.BlockSpec(shape, lambda i, m: (0, m[0] % CORES, 0, 0, 0))]
+        windows += [pl.BlockSpec(blocks[1].shape, lambda i, m: (0, 0, 0, 0))]
     return call(
         functools.partial(analyse_kernel, slot, low, len(blocks)),
         "analyse",
         2 * (nspec - low) * nlat * rows * members,
         2 * (nspec - low) * nlat,
         out_shape=jax.ShapeDtypeStruct((rows, members, nspec - low), BF16),
-        grid=((nspec - low) // width,),
-        in_specs=[
-            IN_SMEM,
-            IN_SMEM,
-            ANYWHERE,
-            pl.BlockSpec((1, width, nlat), lambda i: (slot, first + i, 0)),
-            pl.BlockSpec((rows, 1, members, width), lambda i: (0, slot, 0, first + i)),
-        ]
-        + [ANYWHERE] * len(blocks),
-        out_specs=pl.BlockSpec((rows, members, width), lambda i: (0, 0, i)),
-        scratch_shapes=[
-            pltpu.VMEM((chips, cores, lats, rows * members), BF16),
-            pltpu.SemaphoreType.DMA((CORES, rows)),
-        ],
+        grid_spec=pltpu.PrefetchScalarGridSpec(
+            num_scalar_prefetch=1,
+            grid=((nspec - low) // width,),
+            in_specs=[
+                IN_SMEM,
+                ANYWHERE,
+                pl.BlockSpec((1, width, nlat), lambda i, m: (slot, first + i, 0)),
+                pl.BlockSpec((rows, 1, members, width), lambda i, m: (0, slot, 0, first + i)),
+            ]
+            + windows,
+            out_specs=pl.BlockSpec((rows, members, width), lambda i, m: (0, 0, i)),
+            scratch_shapes=[pltpu.VMEM((chips, cores, lats, rows * members), BF16)],
+        ),
     )(me, wave, token, table, state, *blocks)
 
 
@@ -329,29 +327,38 @@
 
     @pl.when(step == 0)
     def _():
-        def line(entry):
-            return here_ref[entry, slot : slot + 1, low:] + there_ref[entry, slot : slot + 1, low:]
-
-        for f in range(rows):
-            total = 0.0
-            for g in range(rows):
-                total = total + line(f * rows + g) * own_ref[g].astype(F32)
-                total = total + sign_ref[0] * line(rows * rows + f * rows + g) * other_ref[g].astype(F32)
-            mixed[f * members : (f + 1) * members, :] = total.astype(BF16)
+        count = own_ref.shape[2]
+        for n in range(0, count, 128):
+            lanes = slice(low + n, low + n + 128)
+            lines = [
+                here_ref[entry, slot : slot + 1, lanes] + there_ref[entry, slot : slot + 1, lanes]
+                for entry in range(2 * rows * rows)
+            ]
+            lines[rows * rows :] = [sign_ref[0] * line for line in lines[rows * rows :]]
+            for e in range(0, members, 32):
+                part = (slice(e, e + 32), slice(n, n + 128))
+                owns = [own_ref[(g,) + part].astype(F32) for g in range(rows)]
+                others = [other_ref[(g,) + part].astype(F32) for g in range(rows)]
+                for f in range(rows):
+                    total = 0.0
+                    for g in range(rows):
+                        total = total + lines[f * rows + g] * owns[g]
+                        total = total + lines[rows * rows + f * rows + g] * others[g]
+                    mixed[f * members + e : f * members + e + 32, n : n + 128] = total.astype(BF16)
 
     sums = jnp.dot(mixed[...], table_ref[0], preferred_element_type=F32)
     lats = mate_out.shape[2]
     each = mate_out.shape[0]
     for r in range(rows):
-        turned = sums[r * members : (r + 1) * members, :].T
+        turned = sums[r * members : (r + 1) * members, :].astype(BF16).T
         values = [turned[i : i + lats] for i in range(0, turned.shape[0], lats)]
         mine, others = split_cores(values, me_ref[0] % CORES)
         for i, (a, b) in enumerate(zip(mine, others)):
             if apart:
-                held[step * each + i, r] = a.astype(BF16)
+                held[step * each + i, r] = a
             else:
-                own_out[i, 0, r] = a.astype(BF16)
-            mate_out[i, r] = b.astype(BF16)
+                own_out[i, 0, r] = a
+            mate_out[i, r] = b
 
     if apart:
         chip, core = me_ref[0] // CORES, me_ref[0] % CORES
@@ -404,81 +411,66 @@
     )(me, sign, here, there, own, other, table)
 
 
-def assemble_kernel(counts, me_ref, matrix_ref, *rest):
-    ins, out_ref, (held, done, in_sems, out_sems) = rest[: sum(counts)], rest[-5], rest[-4:]
-    rows, lats, slots, members = done.shape
+def assemble_kernel(counts, me_ref, *rest):
+    ins, out, (held, matrix) = rest[: sum(counts)], rest[-3], rest[-2:]
+    _, lats, slots, members = out.shape
     local_slots = len(counts)
     chip = me_ref[0] // CORES
-    each = out_sems.shape[1]
-    depth, breadth = math.gcd(lats // each, 16), 16
-    size = lats // each
-    copies, used = [], 0
-    for r in range(rows):
-        copies.append([])
-        used = 0
-        for slot, count in enumerate(counts):
-            refs = ins[used : used + count]
-            used += count
-            if count == 1:
-                copies[r].append(
-                    pltpu.make_async_copy(refs[0].at[:, :, r], held.at[slot, :, :, r], in_sems.at[r, slot, 0])
-                )
-                continue
-            for i, (k, ref) in enumerate(zip(partners(count), refs)):
-                copies[r].append(
-                    pltpu.make_async_copy(ref.at[:, r], held.at[slot, chip ^ k, :, r], in_sems.at[r, slot, i])
-                )
-        for copy in copies[r]:
-            copy.start()
-    matrix = matrix_ref[...]
-    results = []
-    for r in range(rows):
-        for copy in copies[r]:
-            copy.wait()
-        for start in range(0, lats, depth):
-            j = slice(start, start + depth)
-            for s in range(0, slots, 2 * breadth):
-                halves = []
-                for h in (0, breadth):
-                    columns = [divmod(i, local_slots) for i in range(s + h, s + h + breadth)]
-                    columns = [held[slot, owner // CORES, owner % CORES, r, j, :] for owner, slot in columns]
-                    halves.append(jnp.concatenate(columns, axis=0))
-                turned = jnp.dot(matrix, jnp.concatenate(halves, axis=1), preferred_element_type=F32).astype(BF16)
-                for h in range(2):
-                    value = turned[:, h * members : (h + 1) * members].reshape(depth, breadth, members)
-                    done[r, j, s + h * breadth : s + (h + 1) * breadth, :] = value
-            if (start + depth) % size == 0:
-                part = pl.ds(start + depth - size, size)
-                results.append(
-                    pltpu.make_async_copy(done.at[r, part], out_ref.at[r, part], out_sems.at[r, start // size])
-                )
-                results[-1].start()
-    for copy in results:
-        copy.wait()
+    depth, breadth = math.gcd(lats, 16), 16
+
+    @pl.when((pl.program_id(0) == 0) & (pl.program_id(1) == 0))
+    def _():
+        matrix[...] = swap_matrix(breadth, depth, 1, 0)
+
+    views, used = [], 0
+    for count in counts:
+        refs = ins[used : used + count]
+        used += count
+        if count == 1:
+            views.append(lambda owner, j, ref=refs[0]: ref[owner // CORES, owner % CORES, 0, j, :])
+        else:
+            for k, ref in zip(partners(count), refs):
+                held[chip ^ k] = ref[:, 0]
+            views.append(lambda owner, j: held[owner // CORES, owner % CORES, j, :])
+    for start in range(0, lats, depth):
+        j = slice(start, start + depth)
+        for s in range(0, slots, 2 * breadth):
+            halves = []
+            for h in (0, breadth):
+                columns = [divmod(i, local_slots) for i in range(s + h, s + h + breadth)]
+                halves.append(jnp.concatenate([views[slot](owner, j) for owner, slot in columns], axis=0))
+            turned = jnp.dot(matrix[...], jnp.concatenate(halves, axis=1), preferred_element_type=F32).astype(BF16)
+            for h in range(2):
+                value = turned[:, h * members : (h + 1) * members].reshape(depth, breadth, members)
+                out[0, j, s + h * breadth : s + (h + 1) * breadth, :] = value
 
 
 def assemble(pieces, me):
     rows, lats, members = pieces[0][0].shape[-3:]
     chips = max(len(p) if len(p) > 1 else p[0].shape[0] for p in pieces)
     slots = len(pieces) * chips * CORES
-    each = lats // lat_block(lats)
-    matrix = swap_matrix(16, math.gcd(lats // each, 16), range(math.gcd(lats // each, 16)))
+    each = lat_block(lats)
+    side = 16 * math.gcd(each, 16)
     flat = [block for slot in pieces for block in slot]
+
+    def window(block):
+        lead = block.shape[:-3]
+        return pl.BlockSpec(lead + (1, each, members), lambda r, j, m: (0,) * len(lead) + (r, j, 0))
+
     return call(
         functools.partial(assemble_kernel, [len(p) for p in pieces]),
         "assemble",
         2 * 256 * rows * lats * slots * members,
         4 * rows * lats * slots * members,
         out_shape=jax.ShapeDtypeStruct((rows, lats, slots, members), BF16),
-        in_specs=[IN_SMEM, pl.BlockSpec(matrix.shape, lambda: (0, 0))] + [ANYWHERE] * len(flat),
-        out_specs=ANYWHERE,
-        scratch_shapes=[
-            pltpu.VMEM((len(pieces), chips, CORES, rows, lats, members), BF16),
-            pltpu.VMEM((rows, lats, slots, members), BF16),
-            pltpu.SemaphoreType.DMA((rows, len(pieces), chips)),
-            pltpu.SemaphoreType.DMA((rows, each)),
-        ],
-    )(me, matrix, *flat)
+        grid_spec=pltpu.PrefetchScalarGridSpec(
+            num_scalar_prefetch=1,
+            grid=(rows, lats // each),
+            in_specs=[window(block) for block in flat],
+            out_specs=pl.BlockSpec((1, each, slots, members), lambda r, j, m: (r, j, 0, 0)),
+            scratch_shapes=[pltpu.VMEM((chips, CORES, each, members), BF16), pltpu.VMEM((side, side), BF16)],
+        ),
+    )(me, *flat)
 
 
 def between_cores(blocks, owners):

time: 213 us -> 211 us (level)
    unnamed x31 -> x29, local copies, waits for them, and re-layouts: 11.2 us -> 10.3 us
where the time goes in v12:
time: 211 us; the launch traced here: 210 us
  waiting for transfers between devices  118 us (56%)
  Pallas kernels  44.3 us (21%)
  starting transfers between devices  36.7 us (17%)
  local copies, waits for them, and re-layouts  10.3 us (5%)
    ppermute x7, waiting for transfers between devices, by_permutes(): lax.ppermute(message, 'wave', [(d, d ^ k * CORES) for d in range(owners)])  36.1 us
    all_to_all x3, waiting for transfers between devices, between_chips(): lax.all_to_all(blocks, 'wave', split_axis=0, concat_axis=0, axis_index_gr...  34 us
    ppermute x2, waiting for transfers between devices, per_device(): other = lax.ppermute(forced, 'pole', [(0, 1), (1, 0)])  33.3 us
    all_to_all x3, starting transfers between devices, between_chips(): lax.all_to_all(blocks, 'wave', split_axis=0, concat_axis=0, axis_index_gr...  19.5 us
    pallas_call x2, Pallas kernels, synthesise(): call(functools.partial(synthesise_kernel, slot, low, apart), 'synthesise'...  13.9 us
    ppermute x7, starting transfers between devices, by_permutes(): lax.ppermute(message, 'wave', [(d, d ^ k * CORES) for d in range(owners)])  12.3 us
    pallas_call x2, Pallas kernels, analyse(): call(functools.partial(analyse_kernel, slot, low, len(blocks)), 'analyse'...  11.1 us
    ppermute x4, waiting for transfers between devices, between_cores(): return lax.ppermute(blocks, 'wave', [(d, d ^ 1) for d in range(owners)])  10.4 us
  transfers between devices with their start and end apart: 17, of which 13 were waited for; matrix products, arithmetic and copies ran while one was open for 0% of the time, Pallas kernels for 17%

profile of v12, /device:TPU:8, one launch (start us, length us, event | category | flops | bytes accessed | tf_op | source)
XLA Modules:
  0.0 209.7 jit_solution(8757065020575927850)
XLA Ops:
  0.0 4.9 %weigh.2 = (bf16[8,2,3,160,128]{4,3,2,1,0:T(8,128)(2,1)}, f32[8,128]{1,0:T(8,128)}) custom-call(s32[1]{0:T(128)} %bitcast.me_ref, f32[1,160]{1,0:T(1,128)} %bitcast.3, bf16[3,160,32,128]{3,2,1,0:T(8,128)(2,1)} %tendency_ref.3), custom_call_target="tpu_custom_call" | custom-call | flops 503316480 | bytes 5898240 | tf_op jit(solution)/shard_map/weigh/pallas_call | solution.py:131
  5.0 0.0 copy-start.13
  5.0 0.0 copy-start.11
  5.0 6.3 %all-to-all-start = ((bf16[8,2,3,160,128]{4,3,2,1,0:T(8,128)(2,1)}), bf16[8,2,3,160,128]{4,3,2,1,0:T(8,128)(2,1)S(1)}, u32[]{:S(2)}, u32[]{:S(2)}) async-start(bf16[8,2,3,160,128]{4,3,2,1,0:T(8,128)(2,1)} %get-tuple-element.36), calls=%async_computation | async-start | bytes 3932160 | tf_op jit(solution)/shard_map/all_to_all | solution.py:490
  11.2 0.0 copy-done.13
  11.2 0.1 copy.18.coeff_ref
  11.3 0.0 copy-done.11
  11.3 1.8 copy-done.4
  13.2 2.4 %sum_pairs.1.here_ref = f32[18,2,1280]{2,1,0:T(2,128)S(1)} custom-call(f32[32,2]{1,0:T(8,128)S(1)} %copy.18.coeff_ref, f32[8,128]{1,0:T(8,128)S(1)} %copy-done.11, bf16[32,18,2,1280]{3,2,1,0:T(2,128)(2,1)S(1)} %copy-done.4), custom_call_target="tpu_custom_call" | custom-call | flops 5898240 | bytes 2949120 | tf_op jit(solution)/shard_map/sum_pairs/pallas_call | solution.py:309
  15.5 1.6 collective-permute-start
  17.1 4.3 %collective-permute-done.rest_0_.there_ref = f32[18,2,1280]{2,1,0:T(2,128)S(1)} collective-permute-done((f32[18,2,1280]{2,1,0:T(2,128)S(1)}, f32[18,2,1280]{2,1,0:T(2,128)S(1)}, u32[]{:S(2)}, u32[]{:S(2)}) %collective-permute-start) | collective-permute-done | bytes 184352 | tf_op jit(solution)/shard_map/ppermute | solution.py:510
  21.4 0.7 copy-done.5
  22.1 5.0 %weigh.3 = (bf16[8,2,3,160,128]{4,3,2,1,0:T(8,128)(2,1)}, bf16[8,3,160,128]{3,2,1,0:T(8,128)(2,1)}, f32[8,128]{1,0:T(8,128)}) custom-call(s32[1]{0:T(128)} %bitcast.me_ref, f32[1,160]{1,0:T(1,128)} %bitcast.4, bf16[3,160,32,128]{3,2,1,0:T(8,128)(2,1)} %tendency_ref.3, f32[18,2,1280]{2,1,0:T(2,128)} %copy-done.5), custom_call_target="tpu_custom_call" | custom-call | flops 503316480 | bytes 5898240 | tf_op jit(solution)/shard_map/weigh/pallas_call | solution.py:131
  27.1 0.1 collective-permute-start.1
  27.1 2.8 %collective-permute-done.1.mate_ref = bf16[8,3,160,128]{3,2,1,0:T(8,128)(2,1)S(1)} collective-permute-done((bf16[8,3,160,128]{3,2,1,0:T(8,128)(2,1)}, bf16[8,3,160,128]{3,2,1,0:T(8,128)(2,1)S(1)}, u32[]{:S(2)}, u32[]{:S(2)}) %collective-permute-start.1) | collective-permute-done | bytes 983072 | tf_op jit(solution)/shard_map/ppermute | solution.py:477
  29.9 1.5 copy-done
  31.5 0.1 pair.3
  31.6 0.0 copy-start.1
  31.6 1.3 copy-done.1
  32.8 21.4 %all-to-all-done.in_ref.rest_0_ = bf16[8,2,3,160,128]{4,3,2,1,0:T(8,128)(2,1)S(1)} async-done(((bf16[8,2,3,160,128]{4,3,2,1,0:T(8,128)(2,1)}), bf16[8,2,3,160,128]{4,3,2,1,0:T(8,128)(2,1)S(1)}, u32[]{:S(2)}, u32[]{:S(2)}) %all-to-all-start) | async-done | bytes 1966112 | tf_op jit(solution)/shard_map/all_to_all | solution.py:490
  54.2 6.7 %all-to-all-start.1 = ((bf16[8,2,3,160,128]{4,3,2,1,0:T(8,128)(2,1)}), bf16[8,2,3,160,128]{4,3,2,1,0:T(8,128)(2,1)}, u32[]{:S(2)}, u32[]{:S(2)}) async-start(bf16[8,2,3,160,128]{4,3,2,1,0:T(8,128)(2,1)} %copy-done.1), calls=%async_computation.1 | async-start | bytes 3932160 | tf_op jit(solution)/shard_map/all_to_all | solution.py:490
  60.9 0.3 pick.1
  61.2 0.0 copy-start.6
  61.2 0.1 collective-permute-start.2
  61.3 2.6 %collective-permute-done.2.rest_1_ = bf16[8,3,160,128]{3,2,1,0:T(8,128)(2,1)S(1)} collective-permute-done((bf16[8,3,160,128]{3,2,1,0:T(8,128)(2,1)S(1)}, bf16[8,3,160,128]{3,2,1,0:T(8,128)(2,1)S(1)}, u32[]{:S(2)}, u32[]{:S(2)}) %collective-permute-start.2) | collective-permute-done | bytes 983072 | tf_op jit(solution)/shard_map/ppermute | solution.py:477
  63.8 0.0 copy-done.2
  63.8 0.0 copy-done.12
  63.8 4.1 %analyse.2.own_ref = bf16[3,128,640]{2,1,0:T(8,128)(2,1)S(1)} custom-call(s32[1]{0:T(128)} %bitcast.me_ref, s32[2]{0:T(128)S(1)} %copy-done.12, f32[8,128]{1,0:T(8,128)S(1)} %get-tuple-element.35.token_ref, bf16[2,1280,2560]{2,1,0:T(8,128)(2,1)} %table_ref.7, bf16[3,2,128,1280]{3,2,1,0:T(8,128)(2,1)S(1)} %copy-done.2, ...), custom_call_target="tpu_custom_call" | custom-call | flops 1258291200 | bytes 3276800 | tf_op jit(solution)/shard_map/analyse/pallas_call | solution.py:268
  67.9 1.6 collective-permute-start.3
  69.5 11.7 %collective-permute-done.3.other_ref = bf16[3,128,640]{2,1,0:T(8,128)(2,1)S(1)} collective-permute-done((bf16[3,128,640]{2,1,0:T(8,128)(2,1)S(1)}, bf16[3,128,640]{2,1,0:T(8,128)(2,1)S(1)}, u32[]{:S(2)}, u32[]{:S(2)}) %collective-permute-start.3) | collective-permute-done | bytes 491552 | tf_op jit(solution)/shard_map/ppermute | solution.py:523
  81.3 5.7 %synthesise.2 = (bf16[8,2,3,160,128]{4,3,2,1,0:T(8,128)(2,1)}, bf16[8,3,160,128]{3,2,1,0:T(8,128)(2,1)S(1)}) custom-call(s32[1]{0:T(128)} %bitcast.me_ref, f32[1]{0:T(128)} %bitcast.1.sign_ref, f32[18,2,1280]{2,1,0:T(2,128)S(1)} %sum_pairs.1.here_ref, f32[18,2,1280]{2,1,0:T(2,128)S(1)} %copy-done.6, bf16[3,128,640]{2,1,0:T(8,128)(2,1)S(1)} %analyse.2.own_ref, ...), custom_call_target="tpu_custom_call" | custom-call | flops 1258291200 | bytes 3276800 | tf_op jit(solution)/shard_map/synthesise/pallas_call | solution.py:391
  87.0 0.0 collective-permute-start.4
  87.0 2.6 %collective-permute-done.4.mate_ref = bf16[8,3,160,128]{3,2,1,0:T(8,128)(2,1)S(1)} collective-permute-done((bf16[8,3,160,128]{3,2,1,0:T(8,128)(2,1)S(1)}, bf16[8,3,160,128]{3,2,1,0:T(8,128)(2,1)S(1)}, u32[]{:S(2)}, u32[]{:S(2)}) %collective-permute-start.4) | collective-permute-done | bytes 983072 | tf_op jit(solution)/shard_map/ppermute | solution.py:477
  89.5 1.0 pair.4
  90.5 12.7 %all-to-all-done.1.rest_0_ = bf16[8,2,3,160,128]{4,3,2,1,0:T(8,128)(2,1)} async-done(((bf16[8,2,3,160,128]{4,3,2,1,0:T(8,128)(2,1)}), bf16[8,2,3,160,128]{4,3,2,1,0:T(8,128)(2,1)}, u32[]{:S(2)}, u32[]{:S(2)}) %all-to-all-start.1) | async-done | bytes 1966112 | tf_op jit(solution)/shard_map/all_to_all | solution.py:490
  103.1 6.5 %all-to-all-start.2 = ((bf16[8,2,3,160,128]{4,3,2,1,0:T(8,128)(2,1)}), bf16[8,2,3,160,128]{4,3,2,1,0:T(8,128)(2,1)S(1)}, u32[]{:S(2)}, u32[]{:S(2)}) async-start(bf16[8,2,3,160,128]{4,3,2,1,0:T(8,128)(2,1)} %get-tuple-element.58), calls=%async_computation.2 | async-start | bytes 3932160 | tf_op jit(solution)/shard_map/all_to_all | solution.py:490
  109.7 1.5 copy-done.3
  111.2 7.0 %analyse.3.own_ref = bf16[3,128,1280]{2,1,0:T(8,128)(2,1)S(1)} custom-call(s32[1]{0:T(128)} %bitcast.me_ref, s32[2]{0:T(128)S(1)} %copy-done.12, f32[8,128]{1,0:T(8,128)S(1)} %get-tuple-element.39.token_ref, bf16[2,1280,2560]{2,1,0:T(8,128)(2,1)} %table_ref.7, bf16[3,2,128,1280]{3,2,1,0:T(8,128)(2,1)S(1)} %copy-done.3, ...), custom_call_target="tpu_custom_call" | custom-call | flops 2516582400 | bytes 6553600 | tf_op jit(solution)/shard_map/analyse/pallas_call | solution.py:268
  118.3 1.6 collective-permute-start.5
  119.8 21.6 %collective-permute-done.5.other_ref = bf16[3,128,1280]{2,1,0:T(8,128)(2,1)S(1)} collective-permute-done((bf16[3,128,1280]{2,1,0:T(8,128)(2,1)S(1)}, bf16[3,128,1280]{2,1,0:T(8,128)(2,1)S(1)}, u32[]{:S(2)}, u32[]{:S(2)}) %collective-permute-start.5) | collective-permute-done | bytes 983072 | tf_op jit(solution)/shard_map/ppermute | solution.py:523
  141.4 8.2 %synthesise.3 = (bf16[2,3,160,128]{3,2,1,0:T(8,128)(2,1)S(1)}, bf16[2,3,160,128]{3,2,1,0:T(8,128)(2,1)S(1)}, bf16[2,3,160,128]{3,2,1,0:T(8,128)(2,1)S(1)}, bf16[...) custom-call(s32[1]{0:T(128)} %bitcast.me_ref, ...), custom_call_target="tpu_custom_call" | custom-call | flops 2516582400 | bytes 6553600 | tf_op jit(solution)/shard_map/synthesise/pallas_call | solution.py:391
  149.6 0.1 collective-permute-start.6
  149.7 2.6 %collective-permute-done.6.mate_ref = bf16[8,3,160,128]{3,2,1,0:T(8,128)(2,1)S(1)} collective-permute-done((bf16[8,3,160,128]{3,2,1,0:T(8,128)(2,1)S(1)}, bf16[8,3,160,128]{3,2,1,0:T(8,128)(2,1)S(1)}, u32[]{:S(2)}, u32[]{:S(2)}) %collective-permute-start.6) | collective-permute-done | bytes 983072 | tf_op jit(solution)/shard_map/ppermute | solution.py:477
  152.3 1.3 pair.5
  153.6 2.4 %collective-permute-start.7 = (bf16[2,3,160,128]{3,2,1,0:T(8,128)(2,1)S(1)}, bf16[2,3,160,128]{3,2,1,0:T(8,128)(2,1)S(1)}, u32[]{:S(2)}, u32[]{:S(2)}) collective-permute-start(bf16[2,3,160,128]{3,2,1,0:T(8,128)(2,1)S(1)} %get-tuple-element.51), channel_id=1, source_target_pairs={{0,8},{1,9},{2,10},{3,11},{4,12},{5,13},{6,14},{7,15},{8,0},{9,1},... | collective-permute-start | bytes 737288 | tf_op jit(solution)/shard_map/ppermute | solution.py:484
  156.0 1.5 collective-permute-start.8
  157.5 1.5 collective-permute-start.9
  158.9 0.6 collective-permute-start.10
  159.5 1.5 collective-permute-start.11
  161.0 21.7 %collective-permute-done.7.rest_1_ = bf16[2,3,160,128]{3,2,1,0:T(8,128)(2,1)S(1)} collective-permute-done((bf16[2,3,160,128]{3,2,1,0:T(8,128)(2,1)S(1)}, bf16[2,3,160,128]{3,2,1,0:T(8,128)(2,1)S(1)}, u32[]{:S(2)}, u32[]{:S(2)}) %collective-permute-start.7) | collective-permute-done | bytes 245792 | tf_op jit(solution)/shard_map/ppermute | solution.py:484
  182.7 2.0 collective-permute-start.12
  184.7 3.3 %collective-permute-done.8.rest_2_ = bf16[2,3,160,128]{3,2,1,0:T(8,128)(2,1)S(1)} collective-permute-done((bf16[2,3,160,128]{3,2,1,0:T(8,128)(2,1)S(1)}, bf16[2,3,160,128]{3,2,1,0:T(8,128)(2,1)S(1)}, u32[]{:S(2)}, u32[]{:S(2)}) %collective-permute-start.8) | collective-permute-done | bytes 245792 | tf_op jit(solution)/shard_map/ppermute | solution.py:484
  188.0 2.9 %collective-permute-start.13 = (bf16[2,3,160,128]{3,2,1,0:T(8,128)(2,1)S(1)}, bf16[2,3,160,128]{3,2,1,0:T(8,128)(2,1)S(1)}, u32[]{:S(2)}, u32[]{:S(2)}) collective-permute-start(bf16[2,3,160,128]{3,2,1,0:T(8,128)(2,1)S(1)} %get-tuple-element.57), channel_id=1, source_target_pairs={{0,6},{1,7},{2,4},{3,5},{4,2},{5,3},{6,0},{7,1},{8,14},{9,15},{10,... | collective-permute-start | bytes 737288 | tf_op jit(solution)/shard_map/ppermute | solution.py:484
  190.9 2.9 %collective-permute-done.9.rest_3_ = bf16[2,3,160,128]{3,2,1,0:T(8,128)(2,1)S(1)} collective-permute-done((bf16[2,3,160,128]{3,2,1,0:T(8,128)(2,1)S(1)}, bf16[2,3,160,128]{3,2,1,0:T(8,128)(2,1)S(1)}, u32[]{:S(2)}, u32[]{:S(2)}) %collective-permute-start.9) | collective-permute-done | bytes 245792 | tf_op jit(solution)/shard_map/ppermute | solution.py:484
  193.8 8.1 %collective-permute-done.10.rest_4_ = bf16[2,3,160,128]{3,2,1,0:T(8,128)(2,1)S(1)} collective-permute-done((bf16[2,3,160,128]{3,2,1,0:T(8,128)(2,1)S(1)}, bf16[2,3,160,128]{3,2,1,0:T(8,128)(2,1)S(1)}, u32[]{:S(2)}, u32[]{:S(2)}) %collective-permute-start.10) | collective-permute-done | bytes 245792 | tf_op jit(solution)/shard_map/ppermute | solution.py:484
  201.9 0.0 collective-permute-done.11.rest_5_
  202.0 0.0 collective-permute-done.12.rest_6_
  202.0 0.7 copy-done.7
  202.7 0.0 collective-permute-done.13.rest_7_
  202.7 0.7 copy-done.9
  203.3 0.0 all-to-all-done.2.rest_8_
  203.4 0.9 copy-done.8
  204.3 0.9 copy-done.10
  205.2 4.4 %assemble.1 = bf16[3,160,32,128]{3,2,1,0:T(8,128)(2,1)} custom-call(s32[1]{0:T(128)} %bitcast.me_ref, bf16[2,3,160,128]{3,2,1,0:T(8,128)(2,1)S(1)} %get-tuple-element.50.rest_0_, bf16[2,3,160,128]{3,2,1,0:T(8,128)(2,1)S(1)} %collective-permute-done.7.rest_1_, bf16[2,3,160,128]{3,2,1,0:T(8,128)(2,1)S(1)} %collective-permute-done.8.rest_2_, ...), custom_call_target="tpu_custom_call" | custom-call | flops 1006632960 | bytes 7864320 | tf_op jit(solution)/shard_map/assemble/pallas_call | solution.py:460
  (11 shorter events, 0.0 us)
Async XLA Ops:
  5.0 6.3 %copy-start.13 = (f32[32,2]{0,1:T(2,128)S(1)}, f32[32,2]{0,1:T(2,128)}, u32[]{:S(2)}) copy-start(f32[32,2]{0,1:T(2,128)} %param.12) | copy-start | bytes 772
  5.0 6.4 %copy-start.11 = (f32[8,128]{1,0:T(8,128)S(1)}, f32[8,128]{1,0:T(8,128)}, u32[]{:S(2)}) copy-start(f32[8,128]{1,0:T(8,128)} %get-tuple-element.32.token_ref) | copy-start | bytes 12292
  5.0 49.2 %all-to-all-start = ((bf16[8,2,3,160,128]{4,3,2,1,0:T(8,128)(2,1)}), bf16[8,2,3,160,128]{4,3,2,1,0:T(8,128)(2,1)S(1)}, u32[]{:S(2)}, u32[]{:S(2)}) async-start(bf16[8,2,3,160,128]{4,3,2,1,0:T(8,128)(2,1)} %get-tuple-element.36), calls=%async_computation | async-start | bytes 3932160 | tf_op jit(solution)/shard_map/all_to_all | solution.py:490
  11.3 1.8 copy-start.4
  15.5 5.9 %collective-permute-start = (f32[18,2,1280]{2,1,0:T(2,128)S(1)}, f32[18,2,1280]{2,1,0:T(2,128)S(1)}, u32[]{:S(2)}, u32[]{:S(2)}) collective-permute-start(f32[18,2,1280]{2,1,0:T(2,128)S(1)} %sum_pairs.1.here_ref), channel_id=1, source_target_pairs={{0,16},{16,0},{1,17},{17,1},{2,18},{18,2},{3,19},{19,3},{4,20},{20... | collective-permute-start | bytes 552968 | tf_op jit(solution)/shard_map/ppermute | solution.py:510
  21.4 0.7 copy-start.5
  27.1 2.8 %collective-permute-start.1 = (bf16[8,3,160,128]{3,2,1,0:T(8,128)(2,1)}, bf16[8,3,160,128]{3,2,1,0:T(8,128)(2,1)S(1)}, u32[]{:S(2)}, u32[]{:S(2)}) collective-permute-start(bf16[8,3,160,128]{3,2,1,0:T(8,128)(2,1)} %get-tuple-element.33), channel_id=1, source_target_pairs={{0,1},{1,0},{2,3},{3,2},{4,5},{5,4},{6,7},{7,6},{8,9},{9,8},{10,11... | collective-permute-start | bytes 2949128 | tf_op jit(solution)/shard_map/ppermute | solution.py:477
  29.9 1.5 copy-start
  31.6 1.3 copy-start.1
  54.2 48.9 %all-to-all-start.1 = ((bf16[8,2,3,160,128]{4,3,2,1,0:T(8,128)(2,1)}), bf16[8,2,3,160,128]{4,3,2,1,0:T(8,128)(2,1)}, u32[]{:S(2)}, u32[]{:S(2)}) async-start(bf16[8,2,3,160,128]{4,3,2,1,0:T(8,128)(2,1)} %copy-done.1), calls=%async_computation.1 | async-start | bytes 3932160 | tf_op jit(solution)/shard_map/all_to_all | solution.py:490
  60.9 2.9 %copy-start.2 = (bf16[3,2,128,1280]{3,2,1,0:T(8,128)(2,1)S(1)}, bf16[3,2,128,1280]{3,2,1,0:T(8,128)(2,1)}, u32[]{:S(2)}) copy-start(bf16[3,2,128,1280]{3,2,1,0:T(8,128)(2,1)} %state_ref.3) | copy-start | bytes 5898244
  60.9 3.0 %copy-start.12 = (s32[2]{0:T(128)S(1)}, s32[2]{0:T(128)}, u32[]{:S(2)}) copy-start(s32[2]{0:T(128)} %wave_ref.3) | copy-start | bytes 28
  61.2 20.1 %copy-start.6 = (f32[18,2,1280]{2,1,0:T(2,128)S(1)}, f32[18,2,1280]{2,1,0:T(2,128)}, u32[]{:S(2)}) copy-start(f32[18,2,1280]{2,1,0:T(2,128)} %copy-done.5) | copy-start | bytes 552964
  61.2 2.6 %collective-permute-start.2 = (bf16[8,3,160,128]{3,2,1,0:T(8,128)(2,1)S(1)}, bf16[8,3,160,128]{3,2,1,0:T(8,128)(2,1)S(1)}, u32[]{:S(2)}, u32[]{:S(2)}) collective-permute-start(bf16[8,3,160,128]{3,2,1,0:T(8,128)(2,1)S(1)} %pick.1), channel_id=1, source_target_pairs={{0,1},{1,0},{2,3},{3,2},{4,5},{5,4},{6,7},{7,6},{8,9},{9,8},{10,11... | collective-permute-start | bytes 2949128 | tf_op jit(solution)/shard_map/ppermute | solution.py:477
  67.9 13.3 %collective-permute-start.3 = (bf16[3,128,640]{2,1,0:T(8,128)(2,1)S(1)}, bf16[3,128,640]{2,1,0:T(8,128)(2,1)S(1)}, u32[]{:S(2)}, u32[]{:S(2)}) collective-permute-start(bf16[3,128,640]{2,1,0:T(8,128)(2,1)S(1)} %analyse.2.own_ref), channel_id=1, source_target_pairs={{0,16},{16,0},{1,17},{17,1},{2,18},{18,2},{3,19},{19,3},{4,20},{20... | collective-permute-start | bytes 1474568 | tf_op jit(solution)/shard_map/ppermute | solution.py:523
  87.0 2.6 %collective-permute-start.4 = (bf16[8,3,160,128]{3,2,1,0:T(8,128)(2,1)S(1)}, bf16[8,3,160,128]{3,2,1,0:T(8,128)(2,1)S(1)}, u32[]{:S(2)}, u32[]{:S(2)}) collective-permute-start(bf16[8,3,160,128]{3,2,1,0:T(8,128)(2,1)S(1)} %get-tuple-element.37), channel_id=1, source_target_pairs={{0,1},{1,0},{2,3},{3,2},{4,5},{5,4},{6,7},{7,6},{8,9},{9,8},{10,11... | collective-permute-start | bytes 2949128 | tf_op jit(solution)/shard_map/ppermute | solution.py:477
  103.1 100.2 %all-to-all-start.2 = ((bf16[8,2,3,160,128]{4,3,2,1,0:T(8,128)(2,1)}), bf16[8,2,3,160,128]{4,3,2,1,0:T(8,128)(2,1)S(1)}, u32[]{:S(2)}, u32[]{:S(2)}) async-start(bf16[8,2,3,160,128]{4,3,2,1,0:T(8,128)(2,1)} %get-tuple-element.58), calls=%async_computation.2 | async-start | bytes 3932160 | tf_op jit(solution)/shard_map/all_to_all | solution.py:490
  109.7 1.5 copy-start.3
  118.3 23.2 %collective-permute-start.5 = (bf16[3,128,1280]{2,1,0:T(8,128)(2,1)S(1)}, bf16[3,128,1280]{2,1,0:T(8,128)(2,1)S(1)}, u32[]{:S(2)}, u32[]{:S(2)}) collective-permute-start(bf16[3,128,1280]{2,1,0:T(8,128)(2,1)S(1)} %analyse.3.own_ref), channel_id=1, source_target_pairs={{0,16},{16,0},{1,17},{17,1},{2,18},{18,2},{3,19},{19,3},{4,20},{20... | collective-permute-start | bytes 2949128 | tf_op jit(solution)/shard_map/ppermute | solution.py:523
  149.6 2.6 %collective-permute-start.6 = (bf16[8,3,160,128]{3,2,1,0:T(8,128)(2,1)S(1)}, bf16[8,3,160,128]{3,2,1,0:T(8,128)(2,1)S(1)}, u32[]{:S(2)}, u32[]{:S(2)}) collective-permute-start(bf16[8,3,160,128]{3,2,1,0:T(8,128)(2,1)S(1)} %get-tuple-element.41), channel_id=1, source_target_pairs={{0,1},{1,0},{2,3},{3,2},{4,5},{5,4},{6,7},{7,6},{8,9},{9,8},{10,11... | collective-permute-start | bytes 2949128 | tf_op jit(solution)/shard_map/ppermute | solution.py:477
  153.6 29.1 %collective-permute-start.7 = (bf16[2,3,160,128]{3,2,1,0:T(8,128)(2,1)S(1)}, bf16[2,3,160,128]{3,2,1,0:T(8,128)(2,1)S(1)}, u32[]{:S(2)}, u32[]{:S(2)}) collective-permute-start(bf16[2,3,160,128]{3,2,1,0:T(8,128)(2,1)S(1)} %get-tuple-element.51), channel_id=1, source_target_pairs={{0,8},{1,9},{2,10},{3,11},{4,12},{5,13},{6,14},{7,15},{8,0},{9,1},... | collective-permute-start | bytes 737288 | tf_op jit(solution)/shard_map/ppermute | solution.py:484
  156.0 32.0 %collective-permute-start.8 = (bf16[2,3,160,128]{3,2,1,0:T(8,128)(2,1)S(1)}, bf16[2,3,160,128]{3,2,1,0:T(8,128)(2,1)S(1)}, u32[]{:S(2)}, u32[]{:S(2)}) collective-permute-start(bf16[2,3,160,128]{3,2,1,0:T(8,128)(2,1)S(1)} %get-tuple-element.52), channel_id=1, source_target_pairs={{0,10},{1,11},{2,8},{3,9},{4,14},{5,15},{6,12},{7,13},{8,2},{9,3},... | collective-permute-start | bytes 737288 | tf_op jit(solution)/shard_map/ppermute | solution.py:484
  157.5 36.3 %collective-permute-start.9 = (bf16[2,3,160,128]{3,2,1,0:T(8,128)(2,1)S(1)}, bf16[2,3,160,128]{3,2,1,0:T(8,128)(2,1)S(1)}, u32[]{:S(2)}, u32[]{:S(2)}) collective-permute-start(bf16[2,3,160,128]{3,2,1,0:T(8,128)(2,1)S(1)} %get-tuple-element.53), channel_id=1, source_target_pairs={{0,12},{1,13},{2,14},{3,15},{4,8},{5,9},{6,10},{7,11},{8,4},{9,5},... | collective-permute-start | bytes 737288 | tf_op jit(solution)/shard_map/ppermute | solution.py:484
  158.9 43.0 %collective-permute-start.10 = (bf16[2,3,160,128]{3,2,1,0:T(8,128)(2,1)S(1)}, bf16[2,3,160,128]{3,2,1,0:T(8,128)(2,1)S(1)}, u32[]{:S(2)}, u32[]{:S(2)}) collective-permute-start(bf16[2,3,160,128]{3,2,1,0:T(8,128)(2,1)S(1)} %get-tuple-element.54), channel_id=1, source_target_pairs={{0,14},{1,15},{2,12},{3,13},{4,10},{5,11},{6,8},{7,9},{8,6},{9,7},... | collective-permute-start | bytes 737288 | tf_op jit(solution)/shard_map/ppermute | solution.py:484
  159.5 42.4 %collective-permute-start.11 = (bf16[2,3,160,128]{3,2,1,0:T(8,128)(2,1)S(1)}, bf16[2,3,160,128]{3,2,1,0:T(8,128)(2,1)S(1)}, u32[]{:S(2)}, u32[]{:S(2)}) collective-permute-start(bf16[2,3,160,128]{3,2,1,0:T(8,128)(2,1)S(1)} %get-tuple-element.55), channel_id=1, source_target_pairs={{0,2},{1,3},{2,0},{3,1},{4,6},{5,7},{6,4},{7,5},{8,10},{9,11},{10,... | collective-permute-start | bytes 737288 | tf_op jit(solution)/shard_map/ppermute | solution.py:484
  182.7 19.3 %collective-permute-start.12 = (bf16[2,3,160,128]{3,2,1,0:T(8,128)(2,1)S(1)}, bf16[2,3,160,128]{3,2,1,0:T(8,128)(2,1)S(1)}, u32[]{:S(2)}, u32[]{:S(2)}) collective-permute-start(bf16[2,3,160,128]{3,2,1,0:T(8,128)(2,1)S(1)} %get-tuple-element.56), channel_id=1, source_target_pairs={{0,4},{1,5},{2,6},{3,7},{4,0},{5,1},{6,2},{7,3},{8,12},{9,13},{10,... | collective-permute-start | bytes 737288 | tf_op jit(solution)/shard_map/ppermute | solution.py:484
  188.0 14.6 %collective-permute-start.13 = (bf16[2,3,160,128]{3,2,1,0:T(8,128)(2,1)S(1)}, bf16[2,3,160,128]{3,2,1,0:T(8,128)(2,1)S(1)}, u32[]{:S(2)}, u32[]{:S(2)}) collective-permute-start(bf16[2,3,160,128]{3,2,1,0:T(8,128)(2,1)S(1)} %get-tuple-element.57), channel_id=1, source_target_pairs={{0,6},{1,7},{2,4},{3,5},{4,2},{5,3},{6,0},{7,1},{8,14},{9,15},{10,... | collective-permute-start | bytes 737288 | tf_op jit(solution)/shard_map/ppermute | solution.py:484
  202.0 0.7 copy-start.7
  202.7 0.7 copy-start.9
  203.4 0.9 copy-start.8
  204.3 0.9 copy-start.10

commit v13 on v12

--- a/solution.py
+++ b/solution.py
@@ -193,64 +193,70 @@
     )(me, mate, blocks)
 
 
-def pair_messages_kernel(me_ref, mate_ref, *rest):
-    chips = mate_ref.shape[0]
-    outs, sems = rest[chips:-1], rest[-1]
+def pair_messages_kernel(first, waits, me_ref, mate_ref, *rest):
+    count = (len(rest) - 1 - waits) // 2
+    outs, sems = rest[-1 - count : -1], rest[-1]
     chip, other = me_ref[0] // CORES, CORES - 1 - me_ref[0] % CORES
+    wanted = partners(mate_ref.shape[0])[first : first + count]
     run_copies(
         [
             pltpu.make_async_copy(mate_ref.at[chip ^ k], out.at[other], sems.at[i])
-            for i, (k, out) in enumerate(zip(partners(chips), outs))
+            for i, (k, out) in enumerate(zip(wanted, outs))
         ]
     )
 
 
-def pair_messages(messages, mate, me):
-    chips = len(messages)
-    return call(
-        pair_messages_kernel,
+def pair_messages(messages, mate, me, first, waits):
+    count = len(messages)
+    return call(
+        functools.partial(pair_messages_kernel, first, len(waits)),
         "pair",
         0,
         4 * mate.size,
         out_shape=[jax.ShapeDtypeStruct(m.shape, m.dtype) for m in messages],
-        in_specs=[IN_SMEM, pl.BlockSpec(mate.shape, lambda: (0, 0, 0, 0))] + [ANYWHERE] * chips,
-        out_specs=[ANYWHERE] * chips,
-        scratch_shapes=[pltpu.SemaphoreType.DMA((chips,))],
-        input_output_aliases={i + 2: i for i in range(chips)},
-    )(me, mate, *messages)
-
-
-def analyse_kernel(slot, low, count, me_ref, wave_ref, token_ref, table_ref, state_ref, *rest):
-    blocks, out, grid = rest[:count], rest[count], rest[count + 1]
-    rows, members, _ = out.shape
+        in_specs=[IN_SMEM, pl.BlockSpec(mate.shape, lambda: (0, 0, 0, 0))] + [ANYWHERE] * (count + len(waits)),
+        out_specs=[ANYWHERE] * count,
+        scratch_shapes=[pltpu.SemaphoreType.DMA((count,))],
+        input_output_aliases={i + 2: i for i in range(count)},
+    )(me, mate, *messages, *waits)
+
+
+def analyse_kernel(slot, low, me_ref, wave_ref, token_ref, table_ref, state_ref, *rest):
+    blocks, out, (grid, table, state, table_sems, state_sem) = rest[:-6], rest[-6], rest[-5:]
+    rows, members, width = out.shape
     chips, cores, lats, _ = grid.shape
-    width = table_ref.shape[1]
-    step = pl.program_id(0)
-
-    @pl.when(step == 0)
-    def _():
-        core = me_ref[0] % CORES
+    cuts = [0] + list(range(width % 256, width + 1, 256))
+    cuts = sorted(set(cuts))
+    copies = []
+    for i, (start, end) in enumerate(zip(cuts, cuts[1:])):
+        source = table_ref.at[slot, pl.ds(low + start, end - start)]
+        copies.append(pltpu.make_async_copy(source, table.at[pl.ds(start, end - start)], table_sems.at[i]))
+        copies[-1].start()
+    state_copy = pltpu.make_async_copy(state_ref.at[:, slot, :, pl.ds(low, width)], state, state_sem)
+    state_copy.start()
+    core = me_ref[0] % CORES
+    for r in range(rows):
+        lanes = slice(r * members, (r + 1) * members)
+        if len(blocks) == 1:
+            grid[:, :, :, lanes] = blocks[0][:, :, r]
+        else:
+            grid[:, core, :, lanes] = blocks[0][:, 0, r]
+            grid[:, CORES - 1 - core, :, lanes] = blocks[1][:, r]
+    field = grid[...].reshape(chips * cores * lats, rows * members)
+    state_copy.wait()
+    for copy, start, end in zip(copies, cuts, cuts[1:]):
+        copy.wait()
+        sums = jnp.dot(table[start:end], field, preferred_element_type=F32)
+        degree = lax.broadcasted_iota(jnp.int32, (members, end - start), 1) + (low + start)
+        live = degree >= wave_ref[slot]
         for r in range(rows):
-            lanes = slice(r * members, (r + 1) * members)
-            if count == 1:
-                grid[:, :, :, lanes] = blocks[0][:, :, r]
-            else:
-                grid[:, core, :, lanes] = blocks[0][:, 0, r]
-                grid[:, CORES - 1 - core, :, lanes] = blocks[1][:, r]
-
-    field = grid[...].reshape(chips * cores * lats, rows * members)
-    sums = jnp.dot(table_ref[0], field, preferred_element_type=F32)
-    degree = lax.broadcasted_iota(jnp.int32, (members, width), 1) + (low + step * width)
-    live = degree >= wave_ref[slot]
-    for r in range(rows):
-        total = state_ref[r, 0].astype(F32) + sums[:, r * members : (r + 1) * members].T
-        out[r] = jnp.where(live, total, 0.0).astype(BF16)
+            total = state[r, :, start:end].astype(F32) + sums[:, r * members : (r + 1) * members].T
+            out[r, :, start:end] = jnp.where(live, total, 0.0).astype(BF16)
 
 
 def analyse(blocks, table, state, wave, me, token, slot, low, width):
     chips, _, rows, lats, members = blocks[0].shape
-    nspec, nlat = table.shape[1:]
-    first = low // width
+    nlat = table.shape[2]
     cores = CORES
     if lats % 16:
         if len(blocks) > 1:
@@ -265,24 +271,25 @@
         shape = (chips, 1) + blocks[0].shape[2:]
         windows = [pl.BlockSpec(shape, lambda i, m: (0, m[0] % CORES, 0, 0, 0))]
         windows += [pl.BlockSpec(blocks[1].shape, lambda i, m: (0, 0, 0, 0))]
-    return call(
-        functools.partial(analyse_kernel, slot, low, len(blocks)),
+    in_hbm = pl.BlockSpec(memory_space=pltpu.HBM)
+    return call(
+        functools.partial(analyse_kernel, slot, low),
         "analyse",
-        2 * (nspec - low) * nlat * rows * members,
-        2 * (nspec - low) * nlat,
-        out_shape=jax.ShapeDtypeStruct((rows, members, nspec - low), BF16),
+        2 * width * nlat * rows * members,
+        2 * width * nlat,
+        out_shape=jax.ShapeDtypeStruct((rows, members, width), BF16),
         grid_spec=pltpu.PrefetchScalarGridSpec(
             num_scalar_prefetch=1,
-            grid=((nspec - low) // width,),
-            in_specs=[
-                IN_SMEM,
-                ANYWHERE,
-                pl.BlockSpec((1, width, nlat), lambda i, m: (slot, first + i, 0)),
-                pl.BlockSpec((rows, 1, members, width), lambda i, m: (0, slot, 0, first + i)),
-            ]
-            + windows,
-            out_specs=pl.BlockSpec((rows, members, width), lambda i, m: (0, 0, i)),
-            scratch_shapes=[pltpu.VMEM((chips, cores, lats, rows * members), BF16)],
+            grid=(1,),
+            in_specs=[IN_SMEM, ANYWHERE, in_hbm, in_hbm] + windows,
+            out_specs=pl.BlockSpec((rows, members, width), lambda i, m: (0, 0, 0)),
+            scratch_shapes=[
+                pltpu.VMEM((chips, cores, lats, rows * members), BF16),
+                pltpu.VMEM((width, nlat), BF16),
+                pltpu.VMEM((rows, members, width), BF16),
+                pltpu.SemaphoreType.DMA((width // 256 + 1,)),
+                pltpu.SemaphoreType.DMA,
+            ],
         ),
     )(me, wave, token, table, state, *blocks)
 
@@ -317,10 +324,16 @@
     )(pole_coeffs, token, block_inverses)
 
 
-def synthesise_kernel(slot, low, apart, me_ref, sign_ref, here_ref, there_ref, own_ref, other_ref, table_ref, *rest):
+def synthesise_kernel(
+    slot, low, apart, more, partial, me_ref, sign_ref, here_ref, there_ref, own_ref, other_ref, table_ref, *rest
+):
     rows, members, _ = own_ref.shape
     step = pl.program_id(0)
-    if apart:
+    if partial:
+        partial_ref, rest = rest[0], rest[1:]
+    if more:
+        sums_out, mixed = rest
+    elif apart:
         outs, mate_out, mixed, held, sems = rest[:-4], rest[-4], rest[-3], rest[-2], rest[-1]
     else:
         own_out, mate_out, mixed = rest
@@ -347,6 +360,11 @@
                     mixed[f * members + e : f * members + e + 32, n : n + 128] = total.astype(BF16)
 
     sums = jnp.dot(mixed[...], table_ref[0], preferred_element_type=F32)
+    if partial:
+        sums = sums + partial_ref[...]
+    if more:
+        sums_out[...] = sums
+        return
     lats = mate_out.shape[2]
     each = mate_out.shape[0]
     for r in range(rows):
@@ -373,7 +391,7 @@
                 copy.wait()
 
 
-def synthesise(here, there, sign, own, other, table, me, slot, low, lats, apart):
+def synthesise(here, there, sign, own, other, table, me, slot, low, lats, apart, more, partial):
     rows, members, count = own.shape
     nlat = table.shape[2]
     width = math.lcm(CORES * lats, 128)
@@ -384,16 +402,21 @@
     shapes = [jax.ShapeDtypeStruct((chips, CORES, rows, lats, members), BF16)]
     specs = [pl.BlockSpec((each, 1, rows, lats, members), lambda j, m: (j, m[0] % CORES, 0, 0, 0))]
     scratch = [pltpu.VMEM((rows * members, count), BF16)]
-    if apart:
-        shapes = [jax.ShapeDtypeStruct((CORES, rows, lats, members), BF16)] * chips
-        specs = [ANYWHERE] * chips
+    shapes += [jax.ShapeDtypeStruct((chips, rows, lats, members), BF16)]
+    specs += [pl.BlockSpec((each, rows, lats, members), lambda j, m: (j, 0, 0, 0))]
+    sums = pl.BlockSpec((rows * members, width), lambda j, m: (0, j))
+    if more:
+        shapes, specs = [jax.ShapeDtypeStruct((rows * members, nlat), F32)], [sums]
+    elif apart:
+        shapes[:1] = [jax.ShapeDtypeStruct((CORES, rows, lats, members), BF16)] * chips
+        specs[:1] = [ANYWHERE] * chips
         scratch += [pltpu.VMEM((chips, rows, lats, members), BF16), pltpu.SemaphoreType.DMA((chips,))]
     return call(
-        functools.partial(synthesise_kernel, slot, low, apart),
+        functools.partial(synthesise_kernel, slot, low, apart, more, len(partial)),
         "synthesise",
         2 * count * nlat * rows * members,
         2 * count * nlat,
-        out_shape=shapes + [jax.ShapeDtypeStruct((chips, rows, lats, members), BF16)],
+        out_shape=shapes,
         grid_spec=pltpu.PrefetchScalarGridSpec(
             num_scalar_prefetch=1,
             grid=(nlat // width,),
@@ -404,11 +427,12 @@
                 whole,
                 whole,
                 pl.BlockSpec((1, count, width), lambda j, m: (slot, low // count, j)),
-            ],
-            out_specs=specs + [pl.BlockSpec((each, rows, lats, members), lambda j, m: (j, 0, 0, 0))],
+            ]
+            + [sums] * len(partial),
+            out_specs=specs,
             scratch_shapes=scratch,
         ),
-    )(me, sign, here, there, own, other, table)
+    )(me, sign, here, there, own, other, table, *partial)
 
 
 def assemble_kernel(counts, me_ref, *rest):
@@ -515,17 +539,26 @@
 
     sent = {}
     for slot in order:
-        low = nspec // 2 if slot % 2 else 0
+        half = nspec // 2
+        lows = [half] if slot % 2 else [0, half]
         blocks = [received[slot]]
         if slot == order[0]:
             blocks.append(between_cores(pick(blocks[0], me, token), owners))
-        forced = analyse(blocks, legendre, spectral_state, wavenumbers, me, token, slot, low, nspec // 2)
-        other = lax.ppermute(forced, "pole", [(0, 1), (1, 0)])
+        forced = [analyse(blocks, legendre, spectral_state, wavenumbers, me, token, slot, low, half) for low in lows]
+        others = [lax.ppermute(part, "pole", [(0, 1), (1, 0)]) for part in forced]
         last = slot == order[-1]
-        *own, for_mate = synthesise(here, there, sign, forced, other, legendre, me, slot, low, lats, last)
+        own = []
+        for low, part, other in zip(lows, forced, others):
+            more = low != lows[-1]
+            own = synthesise(here, there, sign, part, other, legendre, me, slot, low, lats, last, more, own)
+        *own, for_mate = own
         mate = between_cores(for_mate, owners)
         if last:
-            sent[slot] = by_permutes(pair_messages(own, mate, me))
+            far = len(own) // 2 + 1
+            own = list(pair_messages(own[:far], mate, me, 0, [])) + list(
+                pair_messages(own[far:], mate, me, far, sent[order[0]])
+            )
+            sent[slot] = by_permutes(own)
         else:
             blocks, token = pair(own[0], mate, me)
             sent[slot] = [between_chips(blocks, owners)]

time: 211 us -> 207 us (0.981)
  waiting for transfers between devices: 118 us -> 103 us
  starting transfers between devices: 36.7 us -> 42.5 us
  Pallas kernels: 44.3 us -> 49.5 us
    ppermute x7, waiting for transfers between devices: 36.1 us -> 13 us  [by_permutes(): lax.ppermute(message, 'wave', [(d, d ^ k * CORES) for d in range(owners)])]
    all_to_all x3, waiting for transfers between devices: 34 us -> 51.9 us  [between_chips(): lax.all_to_all(blocks, 'wave', split_axis=0, concat_axis=0, axis_index_gr...]
    ppermute x2 -> x3, waiting for transfers between devices: 33.3 us -> 23.1 us  [per_device(): others = [lax.ppermute(part, 'pole', [(0, 1), (1, 0)]) for part in forced]]
    ppermute x7, starting transfers between devices: 12.3 us -> 17.8 us  [by_permutes(): lax.ppermute(message, 'wave', [(d, d ^ k * CORES) for d in range(owners)])]
    pallas_call x5 -> x8, Pallas kernels: 26.3 us -> 30.6 us  [the longest x3 16.3 us: synthesise(): call(functools.partial(synthesise_kernel, slot, low, apart, more, len(par...]
    unnamed x29 -> x27, local copies, waits for them, and re-layouts: 10.3 us -> 11.2 us
  transfers between devices with their start and end apart: 17 -> 18, of which waited for: 13 -> 15; matrix products, arithmetic and copies ran while one was open for 0% -> 0% of each run, Pallas kernels for 17% -> 19%
where the time goes in v13:
time: 207 us; the launch traced here: 206 us
  waiting for transfers between devices  103 us (50%)
  Pallas kernels  49.5 us (24%)
  starting transfers between devices  42.5 us (21%)
  local copies, waits for them, and re-layouts  11.2 us (5%)
    all_to_all x3, waiting for transfers between devices, between_chips(): lax.all_to_all(blocks, 'wave', split_axis=0, concat_axis=0, axis_index_gr...  51.9 us
    ppermute x3, waiting for transfers between devices, per_device(): others = [lax.ppermute(part, 'pole', [(0, 1), (1, 0)]) for part in forced]  23.1 us
    all_to_all x3, starting transfers between devices, between_chips(): lax.all_to_all(blocks, 'wave', split_axis=0, concat_axis=0, axis_index_gr...  19.1 us
    ppermute x7, starting transfers between devices, by_permutes(): lax.ppermute(message, 'wave', [(d, d ^ k * CORES) for d in range(owners)])  17.8 us
    pallas_call x3, Pallas kernels, synthesise(): call(functools.partial(synthesise_kernel, slot, low, apart, more, len(par...  16.3 us
    ppermute x7, waiting for transfers between devices, by_permutes(): lax.ppermute(message, 'wave', [(d, d ^ k * CORES) for d in range(owners)])  13 us
    pallas_call x3, Pallas kernels, analyse(): call(functools.partial(analyse_kernel, slot, low), 'analyse', 2 * width *...  12.8 us
    unnamed x27, local copies, waits for them, and re-layouts  11.2 us
  transfers between devices with their start and end apart: 18, of which 15 were waited for; matrix products, arithmetic and copies ran while one was open for 0% of the time, Pallas kernels for 19%

profile of v13, /device:TPU:8, one launch (start us, length us, event | category | flops | bytes accessed | tf_op | source)
XLA Modules:
  0.0 206.2 jit_solution(9744310810114982462)
XLA Ops:
  0.0 4.9 %weigh.2 = (bf16[8,2,3,160,128]{4,3,2,1,0:T(8,128)(2,1)}, f32[8,128]{1,0:T(8,128)}) custom-call(s32[1]{0:T(128)} %bitcast.me_ref, f32[1,160]{1,0:T(1,128)} %bitcast.3, bf16[3,160,32,128]{3,2,1,0:T(8,128)(2,1)} %tendency_ref.3), custom_call_target="tpu_custom_call" | custom-call | flops 503316480 | bytes 5898240 | tf_op jit(solution)/shard_map/weigh/pallas_call | solution.py:131
  4.9 0.0 copy-start.12
  4.9 0.0 copy-start.11
  5.0 6.3 %all-to-all-start = ((bf16[8,2,3,160,128]{4,3,2,1,0:T(8,128)(2,1)}), bf16[8,2,3,160,128]{4,3,2,1,0:T(8,128)(2,1)S(1)}, u32[]{:S(2)}, u32[]{:S(2)}) async-start(bf16[8,2,3,160,128]{4,3,2,1,0:T(8,128)(2,1)} %get-tuple-element.36), calls=%async_computation | async-start | bytes 3932160 | tf_op jit(solution)/shard_map/all_to_all | solution.py:514
  11.2 0.1 copy.18.coeff_ref
  11.3 1.8 copy-done.9
  13.1 2.4 %sum_pairs.1.here_ref = f32[18,2,1280]{2,1,0:T(2,128)S(1)} custom-call(f32[32,2]{1,0:T(8,128)S(1)} %copy.18.coeff_ref, f32[8,128]{1,0:T(8,128)S(1)} %copy-done.11, bf16[32,18,2,1280]{3,2,1,0:T(2,128)(2,1)S(1)} %copy-done.9), custom_call_target="tpu_custom_call" | custom-call | flops 5898240 | bytes 2949120 | tf_op jit(solution)/shard_map/sum_pairs/pallas_call | solution.py:316
  15.5 1.6 collective-permute-start
  17.1 4.3 %collective-permute-done.rest_0_.there_ref = f32[18,2,1280]{2,1,0:T(2,128)S(1)} collective-permute-done((f32[18,2,1280]{2,1,0:T(2,128)S(1)}, f32[18,2,1280]{2,1,0:T(2,128)S(1)}, u32[]{:S(2)}, u32[]{:S(2)}) %collective-permute-start) | collective-permute-done | bytes 184352 | tf_op jit(solution)/shard_map/ppermute | solution.py:534
  21.4 0.7 copy-done.7
  22.1 5.0 %weigh.3 = (bf16[8,2,3,160,128]{4,3,2,1,0:T(8,128)(2,1)}, bf16[8,3,160,128]{3,2,1,0:T(8,128)(2,1)}, f32[8,128]{1,0:T(8,128)}) custom-call(s32[1]{0:T(128)} %bitcast.me_ref, f32[1,160]{1,0:T(1,128)} %bitcast.4, bf16[3,160,32,128]{3,2,1,0:T(8,128)(2,1)} %tendency_ref.3, f32[18,2,1280]{2,1,0:T(2,128)} %copy-done.7), custom_call_target="tpu_custom_call" | custom-call | flops 503316480 | bytes 5898240 | tf_op jit(solution)/shard_map/weigh/pallas_call | solution.py:131
  27.0 0.1 collective-permute-start.1
  27.1 2.8 %collective-permute-done.1.mate_ref = bf16[8,3,160,128]{3,2,1,0:T(8,128)(2,1)S(1)} collective-permute-done((bf16[8,3,160,128]{3,2,1,0:T(8,128)(2,1)}, bf16[8,3,160,128]{3,2,1,0:T(8,128)(2,1)S(1)}, u32[]{:S(2)}, u32[]{:S(2)}) %collective-permute-start.1) | collective-permute-done | bytes 983072 | tf_op jit(solution)/shard_map/ppermute | solution.py:501
  29.9 1.5 copy-done.5
  31.4 0.1 pair.4
  31.5 1.3 copy-done.6
  32.8 21.4 %all-to-all-done.in_ref.rest_0_ = bf16[8,2,3,160,128]{4,3,2,1,0:T(8,128)(2,1)S(1)} async-done(((bf16[8,2,3,160,128]{4,3,2,1,0:T(8,128)(2,1)}), bf16[8,2,3,160,128]{4,3,2,1,0:T(8,128)(2,1)S(1)}, u32[]{:S(2)}, u32[]{:S(2)}) %all-to-all-start) | async-done | bytes 1966112 | tf_op jit(solution)/shard_map/all_to_all | solution.py:514
  54.2 1.3 copy-done.2
  55.5 6.1 %all-to-all-start.1 = ((bf16[8,2,3,160,128]{4,3,2,1,0:T(8,128)(2,1)}), bf16[8,2,3,160,128]{4,3,2,1,0:T(8,128)(2,1)S(1)}, u32[]{:S(2)}, u32[]{:S(2)}) async-start(bf16[8,2,3,160,128]{4,3,2,1,0:T(8,128)(2,1)} %copy-done.6), calls=%async_computation.1 | async-start | bytes 3932160 | tf_op jit(solution)/shard_map/all_to_all | solution.py:514
  61.6 1.7 copy-done.3
  63.3 0.3 pick.1
  63.6 0.1 collective-permute-start.2
  63.6 2.6 %collective-permute-done.2.rest_1_ = bf16[8,3,160,128]{3,2,1,0:T(8,128)(2,1)S(1)} collective-permute-done((bf16[8,3,160,128]{3,2,1,0:T(8,128)(2,1)S(1)}, bf16[8,3,160,128]{3,2,1,0:T(8,128)(2,1)S(1)}, u32[]{:S(2)}, u32[]{:S(2)}) %collective-permute-start.2) | collective-permute-done | bytes 983072 | tf_op jit(solution)/shard_map/ppermute | solution.py:501
  66.2 0.0 copy-done.10
  66.2 4.3 %analyse.3.own_ref = bf16[3,128,640]{2,1,0:T(8,128)(2,1)S(1)} custom-call(s32[1]{0:T(128)} %bitcast.me_ref, s32[2]{0:T(128)S(1)} %copy-done.10, f32[8,128]{1,0:T(8,128)S(1)} %get-tuple-element.35.token_ref, bf16[2,1280,2560]{2,1,0:T(8,128)(2,1)} %table_ref.11, bf16[3,2,128,1280]{3,2,1,0:T(8,128)(2,1)S(1)} %copy-done, ...), custom_call_target="tpu_custom_call" | custom-call | flops 1258291200 | bytes 3276800 | tf_op jit(solution)/shard_map/analyse/pallas_call | solution.py:275
  70.5 1.6 collective-permute-start.3
  72.0 11.8 %collective-permute-done.3.other_ref = bf16[3,128,640]{2,1,0:T(8,128)(2,1)S(1)} collective-permute-done((bf16[3,128,640]{2,1,0:T(8,128)(2,1)S(1)}, bf16[3,128,640]{2,1,0:T(8,128)(2,1)S(1)}, u32[]{:S(2)}, u32[]{:S(2)}) %collective-permute-start.3) | collective-permute-done | bytes 491552 | tf_op jit(solution)/shard_map/ppermute | solution.py:548
  83.8 4.9 %synthesise.3 = (bf16[8,2,3,160,128]{4,3,2,1,0:T(8,128)(2,1)S(1)}, bf16[8,3,160,128]{3,2,1,0:T(8,128)(2,1)S(1)}) custom-call(s32[1]{0:T(128)} %bitcast.me_ref, f32[1]{0:T(128)} %bitcast.1.sign_ref, f32[18,2,1280]{2,1,0:T(2,128)S(1)} %sum_pairs.1.here_ref, f32[18,2,1280]{2,1,0:T(2,128)S(1)} %copy-done.8, bf16[3,128,640]{2,1,0:T(8,128)(2,1)S(1)} %analyse.3.own_ref, ...), custom_call_target="tpu_custom_call" | custom-call | flops 1258291200 | bytes 3276800 | tf_op jit(solution)/shard_map/synthesise/pallas_call | solution.py:414
  88.8 0.1 collective-permute-start.4
  88.8 2.6 %collective-permute-done.4.mate_ref = bf16[8,3,160,128]{3,2,1,0:T(8,128)(2,1)S(1)} collective-permute-done((bf16[8,3,160,128]{3,2,1,0:T(8,128)(2,1)S(1)}, bf16[8,3,160,128]{3,2,1,0:T(8,128)(2,1)S(1)}, u32[]{:S(2)}, u32[]{:S(2)}) %collective-permute-start.4) | collective-permute-done | bytes 983072 | tf_op jit(solution)/shard_map/ppermute | solution.py:501
  91.4 0.1 pair.5
  91.5 0.0 copy-start.4
  91.5 1.3 copy-done.4
  92.8 11.9 %all-to-all-done.1.rest_0_ = bf16[8,2,3,160,128]{4,3,2,1,0:T(8,128)(2,1)S(1)} async-done(((bf16[8,2,3,160,128]{4,3,2,1,0:T(8,128)(2,1)}), bf16[8,2,3,160,128]{4,3,2,1,0:T(8,128)(2,1)S(1)}, u32[]{:S(2)}, u32[]{:S(2)}) %all-to-all-start.1) | async-done | bytes 1966112 | tf_op jit(solution)/shard_map/all_to_all | solution.py:514
  104.7 6.7 %all-to-all-start.2 = ((bf16[8,2,3,160,128]{4,3,2,1,0:T(8,128)(2,1)}), bf16[8,2,3,160,128]{4,3,2,1,0:T(8,128)(2,1)}, u32[]{:S(2)}, u32[]{:S(2)}) async-start(bf16[8,2,3,160,128]{4,3,2,1,0:T(8,128)(2,1)} %copy-done.4), calls=%async_computation.2 | async-start | bytes 3932160 | tf_op jit(solution)/shard_map/all_to_all | solution.py:514
  111.4 1.5 copy-done.1
  112.9 4.3 %analyse.5.own_ref = bf16[3,128,640]{2,1,0:T(8,128)(2,1)S(1)} custom-call(s32[1]{0:T(128)} %bitcast.me_ref, s32[2]{0:T(128)S(1)} %copy-done.10, f32[8,128]{1,0:T(8,128)S(1)} %get-tuple-element.39.token_ref, bf16[2,1280,2560]{2,1,0:T(8,128)(2,1)} %table_ref.11, bf16[3,2,128,1280]{3,2,1,0:T(8,128)(2,1)S(1)} %copy-done.1, ...), custom_call_target="tpu_custom_call" | custom-call | flops 1258291200 | bytes 3276800 | tf_op jit(solution)/shard_map/analyse/pallas_call | solution.py:275
  117.2 1.6 collective-permute-start.6
  118.8 4.3 %analyse.4.own_ref = bf16[3,128,640]{2,1,0:T(8,128)(2,1)S(1)} custom-call(s32[1]{0:T(128)} %bitcast.me_ref, s32[2]{0:T(128)S(1)} %copy-done.10, f32[8,128]{1,0:T(8,128)S(1)} %get-tuple-element.39.token_ref, bf16[2,1280,2560]{2,1,0:T(8,128)(2,1)} %table_ref.11, bf16[3,2,128,1280]{3,2,1,0:T(8,128)(2,1)S(1)} %copy-done.1, ...), custom_call_target="tpu_custom_call" | custom-call | flops 1258291200 | bytes 3276800 | tf_op jit(solution)/shard_map/analyse/pallas_call | solution.py:275
  123.1 0.6 collective-permute-start.5
  123.6 7.8 %collective-permute-done.6.other_ref = bf16[3,128,640]{2,1,0:T(8,128)(2,1)S(1)} collective-permute-done((bf16[3,128,640]{2,1,0:T(8,128)(2,1)S(1)}, bf16[3,128,640]{2,1,0:T(8,128)(2,1)S(1)}, u32[]{:S(2)}, u32[]{:S(2)}) %collective-permute-start.6) | collective-permute-done | bytes 491552 | tf_op jit(solution)/shard_map/ppermute | solution.py:548
  131.4 4.8 %synthesise.4.rest_0_ = f32[384,2560]{1,0:T(8,128)S(1)} custom-call(s32[1]{0:T(128)} %bitcast.me_ref, f32[1]{0:T(128)} %bitcast.1.sign_ref, f32[18,2,1280]{2,1,0:T(2,128)S(1)} %sum_pairs.1.here_ref, f32[18,2,1280]{2,1,0:T(2,128)S(1)} %copy-done.8, bf16[3,128,640]{2,1,0:T(8,128)(2,1)S(1)} %analyse.5.own_ref, ...), custom_call_target="tpu_custom_call" | custom-call | flops 1258291200 | bytes 3276800 | tf_op jit(solution)/shard_map/synthesise/pallas_call | solution.py:414
  136.3 3.5 %collective-permute-done.5.other_ref = bf16[3,128,640]{2,1,0:T(8,128)(2,1)S(1)} collective-permute-done((bf16[3,128,640]{2,1,0:T(8,128)(2,1)S(1)}, bf16[3,128,640]{2,1,0:T(8,128)(2,1)S(1)}, u32[]{:S(2)}, u32[]{:S(2)}) %collective-permute-start.5) | collective-permute-done | bytes 491552 | tf_op jit(solution)/shard_map/ppermute | solution.py:548
  139.8 6.5 %synthesise.5 = (bf16[2,3,160,128]{3,2,1,0:T(8,128)(2,1)S(1)}, bf16[2,3,160,128]{3,2,1,0:T(8,128)(2,1)S(1)}, bf16[2,3,160,128]{3,2,1,0:T(8,128)(2,1)}, bf16[2,3,...) custom-call(s32[1]{0:T(128)} %bitcast.me_ref, ...), custom_call_target="tpu_custom_call" | custom-call | flops 1258291200 | bytes 3276800 | tf_op jit(solution)/shard_map/synthesise/pallas_call | solution.py:414
  146.3 0.1 collective-permute-start.7
  146.4 2.6 %collective-permute-done.7.mate_ref = bf16[8,3,160,128]{3,2,1,0:T(8,128)(2,1)S(1)} collective-permute-done((bf16[8,3,160,128]{3,2,1,0:T(8,128)(2,1)S(1)}, bf16[8,3,160,128]{3,2,1,0:T(8,128)(2,1)S(1)}, u32[]{:S(2)}, u32[]{:S(2)}) %collective-permute-start.7) | collective-permute-done | bytes 983072 | tf_op jit(solution)/shard_map/ppermute | solution.py:501
  149.0 1.1 pair.6
  150.1 1.7 collective-permute-start.8
  151.7 2.2 %collective-permute-start.9 = (bf16[2,3,160,128]{3,2,1,0:T(8,128)(2,1)}, bf16[2,3,160,128]{3,2,1,0:T(8,128)(2,1)S(1)}, u32[]{:S(2)}, u32[]{:S(2)}) collective-permute-start(bf16[2,3,160,128]{3,2,1,0:T(8,128)(2,1)} %get-tuple-element.49), channel_id=1, source_target_pairs={{0,10},{1,11},{2,8},{3,9},{4,14},{5,15},{6,12},{7,13},{8,2},{9,3},... | collective-permute-start | bytes 737288 | tf_op jit(solution)/shard_map/ppermute | solution.py:508
  154.0 0.8 collective-permute-start.10
  154.8 1.2 collective-permute-start.11
  156.0 18.6 %all-to-all-done.2.rest_3_.rest_8_ = bf16[8,2,3,160,128]{4,3,2,1,0:T(8,128)(2,1)} async-done(((bf16[8,2,3,160,128]{4,3,2,1,0:T(8,128)(2,1)}), bf16[8,2,3,160,128]{4,3,2,1,0:T(8,128)(2,1)}, u32[]{:S(2)}, u32[]{:S(2)}) %all-to-all-start.2) | async-done | bytes 1966112 | tf_op jit(solution)/shard_map/all_to_all | solution.py:514
  174.6 0.5 pair.7
  175.1 1.2 collective-permute-start.12
  176.3 3.5 %collective-permute-done.8.rest_1_ = bf16[2,3,160,128]{3,2,1,0:T(8,128)(2,1)S(1)} collective-permute-done((bf16[2,3,160,128]{3,2,1,0:T(8,128)(2,1)S(1)}, bf16[2,3,160,128]{3,2,1,0:T(8,128)(2,1)S(1)}, u32[]{:S(2)}, u32[]{:S(2)}) %collective-permute-start.8) | collective-permute-done | bytes 245792 | tf_op jit(solution)/shard_map/ppermute | solution.py:508
  179.8 5.0 %collective-permute-start.13 = (bf16[2,3,160,128]{3,2,1,0:T(8,128)(2,1)S(1)}, bf16[2,3,160,128]{3,2,1,0:T(8,128)(2,1)S(1)}, u32[]{:S(2)}, u32[]{:S(2)}) collective-permute-start(bf16[2,3,160,128]{3,2,1,0:T(8,128)(2,1)S(1)} %get-tuple-element.57), channel_id=1, source_target_pairs={{0,4},{1,5},{2,6},{3,7},{4,0},{5,1},{6,2},{7,3},{8,12},{9,13},{10,... | collective-permute-start | bytes 737288 | tf_op jit(solution)/shard_map/ppermute | solution.py:508
  184.8 0.4 collective-permute-done.9.rest_2_
  185.3 5.7 %collective-permute-start.14 = (bf16[2,3,160,128]{3,2,1,0:T(8,128)(2,1)S(1)}, bf16[2,3,160,128]{3,2,1,0:T(8,128)(2,1)S(1)}, u32[]{:S(2)}, u32[]{:S(2)}) collective-permute-start(bf16[2,3,160,128]{3,2,1,0:T(8,128)(2,1)S(1)} %get-tuple-element.58), channel_id=1, source_target_pairs={{0,6},{1,7},{2,4},{3,5},{4,2},{5,3},{6,0},{7,1},{8,14},{9,15},{10,... | collective-permute-start | bytes 737288 | tf_op jit(solution)/shard_map/ppermute | solution.py:508
  190.9 2.9 %collective-permute-done.10.rest_3_ = bf16[2,3,160,128]{3,2,1,0:T(8,128)(2,1)S(1)} collective-permute-done((bf16[2,3,160,128]{3,2,1,0:T(8,128)(2,1)}, bf16[2,3,160,128]{3,2,1,0:T(8,128)(2,1)S(1)}, u32[]{:S(2)}, u32[]{:S(2)}) %collective-permute-start.10) | collective-permute-done | bytes 245792 | tf_op jit(solution)/shard_map/ppermute | solution.py:508
  193.8 6.2 %collective-permute-done.11.rest_4_ = bf16[2,3,160,128]{3,2,1,0:T(8,128)(2,1)S(1)} collective-permute-done((bf16[2,3,160,128]{3,2,1,0:T(8,128)(2,1)}, bf16[2,3,160,128]{3,2,1,0:T(8,128)(2,1)S(1)}, u32[]{:S(2)}, u32[]{:S(2)}) %collective-permute-start.11) | collective-permute-done | bytes 245792 | tf_op jit(solution)/shard_map/ppermute | solution.py:508
  200.0 0.0 collective-permute-done.12.rest_5_
  200.0 0.0 collective-permute-done.13.rest_6_
  200.0 0.0 collective-permute-done.14.rest_7_
  200.0 6.2 %assemble.1 = bf16[3,160,32,128]{3,2,1,0:T(8,128)(2,1)} custom-call(s32[1]{0:T(128)} %bitcast.me_ref, bf16[2,3,160,128]{3,2,1,0:T(8,128)(2,1)S(1)} %get-tuple-element.47.rest_0_, bf16[2,3,160,128]{3,2,1,0:T(8,128)(2,1)S(1)} %collective-permute-done.8.rest_1_, bf16[2,3,160,128]{3,2,1,0:T(8,128)(2,1)S(1)} %collective-permute-done.9.rest_2_, ...), custom_call_target="tpu_custom_call" | custom-call | flops 1006632960 | bytes 7864320 | tf_op jit(solution)/shard_map/assemble/pallas_call | solution.py:484
  (14 shorter events, 0.0 us)
Async XLA Ops:
  4.9 6.3 %copy-start.12 = (f32[32,2]{0,1:T(2,128)S(1)}, f32[32,2]{0,1:T(2,128)}, u32[]{:S(2)}) copy-start(f32[32,2]{0,1:T(2,128)} %param.12) | copy-start | bytes 772
  4.9 6.4 %copy-start.11 = (f32[8,128]{1,0:T(8,128)S(1)}, f32[8,128]{1,0:T(8,128)}, u32[]{:S(2)}) copy-start(f32[8,128]{1,0:T(8,128)} %get-tuple-element.32.token_ref) | copy-start | bytes 12292
  5.0 49.2 %all-to-all-start = ((bf16[8,2,3,160,128]{4,3,2,1,0:T(8,128)(2,1)}), bf16[8,2,3,160,128]{4,3,2,1,0:T(8,128)(2,1)S(1)}, u32[]{:S(2)}, u32[]{:S(2)}) async-start(bf16[8,2,3,160,128]{4,3,2,1,0:T(8,128)(2,1)} %get-tuple-element.36), calls=%async_computation | async-start | bytes 3932160 | tf_op jit(solution)/shard_map/all_to_all | solution.py:514
  11.3 1.8 copy-start.9
  15.5 5.9 %collective-permute-start = (f32[18,2,1280]{2,1,0:T(2,128)S(1)}, f32[18,2,1280]{2,1,0:T(2,128)S(1)}, u32[]{:S(2)}, u32[]{:S(2)}) collective-permute-start(f32[18,2,1280]{2,1,0:T(2,128)S(1)} %sum_pairs.1.here_ref), channel_id=1, source_target_pairs={{0,16},{16,0},{1,17},{17,1},{2,18},{18,2},{3,19},{19,3},{4,20},{20... | collective-permute-start | bytes 552968 | tf_op jit(solution)/shard_map/ppermute | solution.py:534
  21.4 0.7 copy-start.7
  27.0 2.8 %collective-permute-start.1 = (bf16[8,3,160,128]{3,2,1,0:T(8,128)(2,1)}, bf16[8,3,160,128]{3,2,1,0:T(8,128)(2,1)S(1)}, u32[]{:S(2)}, u32[]{:S(2)}) collective-permute-start(bf16[8,3,160,128]{3,2,1,0:T(8,128)(2,1)} %get-tuple-element.33), channel_id=1, source_target_pairs={{0,1},{1,0},{2,3},{3,2},{4,5},{5,4},{6,7},{7,6},{8,9},{9,8},{10,11... | collective-permute-start | bytes 2949128 | tf_op jit(solution)/shard_map/ppermute | solution.py:501
  29.9 1.5 copy-start.5
  31.5 1.3 copy-start.6
  54.2 1.3 copy-start.2
  55.5 49.2 %all-to-all-start.1 = ((bf16[8,2,3,160,128]{4,3,2,1,0:T(8,128)(2,1)}), bf16[8,2,3,160,128]{4,3,2,1,0:T(8,128)(2,1)S(1)}, u32[]{:S(2)}, u32[]{:S(2)}) async-start(bf16[8,2,3,160,128]{4,3,2,1,0:T(8,128)(2,1)} %copy-done.6), calls=%async_computation.1 | async-start | bytes 3932160 | tf_op jit(solution)/shard_map/all_to_all | solution.py:514
  61.6 4.6 %copy-start = (bf16[3,2,128,1280]{3,2,1,0:T(8,128)(2,1)S(1)}, bf16[3,2,128,1280]{3,2,1,0:T(8,128)(2,1)}, u32[]{:S(2)}) copy-start(bf16[3,2,128,1280]{3,2,1,0:T(8,128)(2,1)} %state_ref.5) | copy-start | bytes 5898244
  61.6 1.7 copy-start.3
  63.2 3.0 %copy-start.10 = (s32[2]{0:T(128)S(1)}, s32[2]{0:T(128)}, u32[]{:S(2)}) copy-start(s32[2]{0:T(128)} %wave_ref.5) | copy-start | bytes 28
  63.6 20.3 %copy-start.8 = (f32[18,2,1280]{2,1,0:T(2,128)S(1)}, f32[18,2,1280]{2,1,0:T(2,128)}, u32[]{:S(2)}) copy-start(f32[18,2,1280]{2,1,0:T(2,128)} %copy-done.7) | copy-start | bytes 552964
  63.6 2.6 %collective-permute-start.2 = (bf16[8,3,160,128]{3,2,1,0:T(8,128)(2,1)S(1)}, bf16[8,3,160,128]{3,2,1,0:T(8,128)(2,1)S(1)}, u32[]{:S(2)}, u32[]{:S(2)}) collective-permute-start(bf16[8,3,160,128]{3,2,1,0:T(8,128)(2,1)S(1)} %pick.1), channel_id=1, source_target_pairs={{0,1},{1,0},{2,3},{3,2},{4,5},{5,4},{6,7},{7,6},{8,9},{9,8},{10,11... | collective-permute-start | bytes 2949128 | tf_op jit(solution)/shard_map/ppermute | solution.py:501
  70.5 13.3 %collective-permute-start.3 = (bf16[3,128,640]{2,1,0:T(8,128)(2,1)S(1)}, bf16[3,128,640]{2,1,0:T(8,128)(2,1)S(1)}, u32[]{:S(2)}, u32[]{:S(2)}) collective-permute-start(bf16[3,128,640]{2,1,0:T(8,128)(2,1)S(1)} %analyse.3.own_ref), channel_id=1, source_target_pairs={{0,16},{16,0},{1,17},{17,1},{2,18},{18,2},{3,19},{19,3},{4,20},{20... | collective-permute-start | bytes 1474568 | tf_op jit(solution)/shard_map/ppermute | solution.py:548
  88.8 2.6 %collective-permute-start.4 = (bf16[8,3,160,128]{3,2,1,0:T(8,128)(2,1)S(1)}, bf16[8,3,160,128]{3,2,1,0:T(8,128)(2,1)S(1)}, u32[]{:S(2)}, u32[]{:S(2)}) collective-permute-start(bf16[8,3,160,128]{3,2,1,0:T(8,128)(2,1)S(1)} %get-tuple-element.37), channel_id=1, source_target_pairs={{0,1},{1,0},{2,3},{3,2},{4,5},{5,4},{6,7},{7,6},{8,9},{9,8},{10,11... | collective-permute-start | bytes 2949128 | tf_op jit(solution)/shard_map/ppermute | solution.py:501
  91.5 1.3 copy-start.4
  104.7 69.9 %all-to-all-start.2 = ((bf16[8,2,3,160,128]{4,3,2,1,0:T(8,128)(2,1)}), bf16[8,2,3,160,128]{4,3,2,1,0:T(8,128)(2,1)}, u32[]{:S(2)}, u32[]{:S(2)}) async-start(bf16[8,2,3,160,128]{4,3,2,1,0:T(8,128)(2,1)} %copy-done.4), calls=%async_computation.2 | async-start | bytes 3932160 | tf_op jit(solution)/shard_map/all_to_all | solution.py:514
  111.4 1.5 copy-start.1
  117.2 14.2 %collective-permute-start.6 = (bf16[3,128,640]{2,1,0:T(8,128)(2,1)S(1)}, bf16[3,128,640]{2,1,0:T(8,128)(2,1)S(1)}, u32[]{:S(2)}, u32[]{:S(2)}) collective-permute-start(bf16[3,128,640]{2,1,0:T(8,128)(2,1)S(1)} %analyse.5.own_ref), channel_id=1, source_target_pairs={{0,16},{16,0},{1,17},{17,1},{2,18},{18,2},{3,19},{19,3},{4,20},{20... | collective-permute-start | bytes 1474568 | tf_op jit(solution)/shard_map/ppermute | solution.py:548
  123.1 16.7 %collective-permute-start.5 = (bf16[3,128,640]{2,1,0:T(8,128)(2,1)S(1)}, bf16[3,128,640]{2,1,0:T(8,128)(2,1)S(1)}, u32[]{:S(2)}, u32[]{:S(2)}) collective-permute-start(bf16[3,128,640]{2,1,0:T(8,128)(2,1)S(1)} %analyse.4.own_ref), channel_id=1, source_target_pairs={{0,16},{16,0},{1,17},{17,1},{2,18},{18,2},{3,19},{19,3},{4,20},{20... | collective-permute-start | bytes 1474568 | tf_op jit(solution)/shard_map/ppermute | solution.py:548
  146.3 2.6 %collective-permute-start.7 = (bf16[8,3,160,128]{3,2,1,0:T(8,128)(2,1)S(1)}, bf16[8,3,160,128]{3,2,1,0:T(8,128)(2,1)S(1)}, u32[]{:S(2)}, u32[]{:S(2)}) collective-permute-start(bf16[8,3,160,128]{3,2,1,0:T(8,128)(2,1)S(1)} %get-tuple-element.41), channel_id=1, source_target_pairs={{0,1},{1,0},{2,3},{3,2},{4,5},{5,4},{6,7},{7,6},{8,9},{9,8},{10,11... | collective-permute-start | bytes 2949128 | tf_op jit(solution)/shard_map/ppermute | solution.py:501
  150.1 29.7 %collective-permute-start.8 = (bf16[2,3,160,128]{3,2,1,0:T(8,128)(2,1)S(1)}, bf16[2,3,160,128]{3,2,1,0:T(8,128)(2,1)S(1)}, u32[]{:S(2)}, u32[]{:S(2)}) collective-permute-start(bf16[2,3,160,128]{3,2,1,0:T(8,128)(2,1)S(1)} %get-tuple-element.48), channel_id=1, source_target_pairs={{0,8},{1,9},{2,10},{3,11},{4,12},{5,13},{6,14},{7,15},{8,0},{9,1},... | collective-permute-start | bytes 737288 | tf_op jit(solution)/shard_map/ppermute | solution.py:508
  151.7 33.5 %collective-permute-start.9 = (bf16[2,3,160,128]{3,2,1,0:T(8,128)(2,1)}, bf16[2,3,160,128]{3,2,1,0:T(8,128)(2,1)S(1)}, u32[]{:S(2)}, u32[]{:S(2)}) collective-permute-start(bf16[2,3,160,128]{3,2,1,0:T(8,128)(2,1)} %get-tuple-element.49), channel_id=1, source_target_pairs={{0,10},{1,11},{2,8},{3,9},{4,14},{5,15},{6,12},{7,13},{8,2},{9,3},... | collective-permute-start | bytes 737288 | tf_op jit(solution)/shard_map/ppermute | solution.py:508
  154.0 39.9 %collective-permute-start.10 = (bf16[2,3,160,128]{3,2,1,0:T(8,128)(2,1)}, bf16[2,3,160,128]{3,2,1,0:T(8,128)(2,1)S(1)}, u32[]{:S(2)}, u32[]{:S(2)}) collective-permute-start(bf16[2,3,160,128]{3,2,1,0:T(8,128)(2,1)} %get-tuple-element.50), channel_id=1, source_target_pairs={{0,12},{1,13},{2,14},{3,15},{4,8},{5,9},{6,10},{7,11},{8,4},{9,5},... | collective-permute-start | bytes 737288 | tf_op jit(solution)/shard_map/ppermute | solution.py:508
  154.8 45.2 %collective-permute-start.11 = (bf16[2,3,160,128]{3,2,1,0:T(8,128)(2,1)}, bf16[2,3,160,128]{3,2,1,0:T(8,128)(2,1)S(1)}, u32[]{:S(2)}, u32[]{:S(2)}) collective-permute-start(bf16[2,3,160,128]{3,2,1,0:T(8,128)(2,1)} %get-tuple-element.51), channel_id=1, source_target_pairs={{0,14},{1,15},{2,12},{3,13},{4,10},{5,11},{6,8},{7,9},{8,6},{9,7},... | collective-permute-start | bytes 737288 | tf_op jit(solution)/shard_map/ppermute | solution.py:508
  175.1 24.9 %collective-permute-start.12 = (bf16[2,3,160,128]{3,2,1,0:T(8,128)(2,1)S(1)}, bf16[2,3,160,128]{3,2,1,0:T(8,128)(2,1)S(1)}, u32[]{:S(2)}, u32[]{:S(2)}) collective-permute-start(bf16[2,3,160,128]{3,2,1,0:T(8,128)(2,1)S(1)} %get-tuple-element.56), channel_id=1, source_target_pairs={{0,2},{1,3},{2,0},{3,1},{4,6},{5,7},{6,4},{7,5},{8,10},{9,11},{10,... | collective-permute-start | bytes 737288 | tf_op jit(solution)/shard_map/ppermute | solution.py:508
  179.8 20.2 %collective-permute-start.13 = (bf16[2,3,160,128]{3,2,1,0:T(8,128)(2,1)S(1)}, bf16[2,3,160,128]{3,2,1,0:T(8,128)(2,1)S(1)}, u32[]{:S(2)}, u32[]{:S(2)}) collective-permute-start(bf16[2,3,160,128]{3,2,1,0:T(8,128)(2,1)S(1)} %get-tuple-element.57), channel_id=1, source_target_pairs={{0,4},{1,5},{2,6},{3,7},{4,0},{5,1},{6,2},{7,3},{8,12},{9,13},{10,... | collective-permute-start | bytes 737288 | tf_op jit(solution)/shard_map/ppermute | solution.py:508
  185.3 14.7 %collective-permute-start.14 = (bf16[2,3,160,128]{3,2,1,0:T(8,128)(2,1)S(1)}, bf16[2,3,160,128]{3,2,1,0:T(8,128)(2,1)S(1)}, u32[]{:S(2)}, u32[]{:S(2)}) collective-permute-start(bf16[2,3,160,128]{3,2,1,0:T(8,128)(2,1)S(1)} %get-tuple-element.58), channel_id=1, source_target_pairs={{0,6},{1,7},{2,4},{3,5},{4,2},{5,3},{6,0},{7,1},{8,14},{9,15},{10,... | collective-permute-start | bytes 737288 | tf_op jit(solution)/shard_map/ppermute | solution.py:508

commit v14 on v13

--- a/solution.py
+++ b/solution.py
@@ -13,6 +13,7 @@
 CORES = 2
 ANYWHERE = pl.BlockSpec(memory_space=pl.ANY)
 IN_SMEM = pl.BlockSpec(memory_space=pltpu.SMEM)
+IN_HBM = pl.BlockSpec(memory_space=pltpu.HBM)
 TOKEN = jax.ShapeDtypeStruct((8, 128), F32)
 
 
@@ -149,27 +150,36 @@
     )(me, gauss, tendency, *waits)
 
 
-def pick_kernel(me_ref, token_ref, in_ref, out_ref):
-    out_ref[...] = in_ref[:, 0]
+def pick_kernel(me_ref, token_ref, in_ref, out_ref, held, in_sems, out_sems):
+    other = CORES - 1 - me_ref[0] % CORES
+    rows = held.shape[1]
+    fetched = [pltpu.make_async_copy(in_ref.at[:, other, r], held.at[:, r], in_sems.at[r]) for r in range(rows)]
+    stored = [pltpu.make_async_copy(held.at[:, r], out_ref.at[:, r], out_sems.at[r]) for r in range(rows)]
+    for copy in fetched:
+        copy.start()
+    for fetch, store in zip(fetched, stored):
+        fetch.wait()
+        store.start()
+    for copy in stored:
+        copy.wait()
 
 
 def pick(blocks, me, token):
     chips, _, rows, lats, members = blocks.shape
+    shape = (chips, rows, lats, members)
     return call(
         pick_kernel,
         "pick",
         0,
         2 * blocks.size,
-        out_shape=jax.ShapeDtypeStruct((chips, rows, lats, members), BF16),
-        grid_spec=pltpu.PrefetchScalarGridSpec(
-            num_scalar_prefetch=1,
-            grid=(rows,),
-            in_specs=[
-                ANYWHERE,
-                pl.BlockSpec((chips, 1, 1, lats, members), lambda r, m: (0, CORES - 1 - m[0] % CORES, r, 0, 0))
-            ],
-            out_specs=pl.BlockSpec((chips, 1, lats, members), lambda r, m: (0, r, 0, 0)),
-        ),
+        out_shape=jax.ShapeDtypeStruct(shape, BF16),
+        in_specs=[IN_SMEM, ANYWHERE, IN_HBM],
+        out_specs=IN_HBM,
+        scratch_shapes=[
+            pltpu.VMEM(shape, BF16),
+            pltpu.SemaphoreType.DMA((rows,)),
+            pltpu.SemaphoreType.DMA((rows,)),
+        ],
     )(me, token, blocks)
 
 
@@ -222,26 +232,30 @@
 
 
 def analyse_kernel(slot, low, me_ref, wave_ref, token_ref, table_ref, state_ref, *rest):
-    blocks, out, (grid, table, state, table_sems, state_sem) = rest[:-6], rest[-6], rest[-5:]
+    blocks, out, (grid, table, state, table_sems, state_sem, block_sems) = rest[:-7], rest[-7], rest[-6:]
     rows, members, width = out.shape
     chips, cores, lats, _ = grid.shape
-    cuts = [0] + list(range(width % 256, width + 1, 256))
-    cuts = sorted(set(cuts))
+    core = me_ref[0] % CORES
+    moves = []
+    for r in range(rows):
+        lanes = pl.ds(r * members, members)
+        if len(blocks) == 1:
+            moves.append(pltpu.make_async_copy(blocks[0].at[:, :, r], grid.at[:, :, :, lanes], block_sems.at[0, r]))
+        else:
+            target = grid.at[:, core, :, lanes]
+            moves.append(pltpu.make_async_copy(blocks[0].at[:, core, r], target, block_sems.at[0, r]))
+            target = grid.at[:, CORES - 1 - core, :, lanes]
+            moves.append(pltpu.make_async_copy(blocks[1].at[:, r], target, block_sems.at[1, r]))
+    cuts = sorted(set([0] + list(range(width % 256, width + 1, 256))))
     copies = []
     for i, (start, end) in enumerate(zip(cuts, cuts[1:])):
         source = table_ref.at[slot, pl.ds(low + start, end - start)]
         copies.append(pltpu.make_async_copy(source, table.at[pl.ds(start, end - start)], table_sems.at[i]))
-        copies[-1].start()
     state_copy = pltpu.make_async_copy(state_ref.at[:, slot, :, pl.ds(low, width)], state, state_sem)
-    state_copy.start()
-    core = me_ref[0] % CORES
-    for r in range(rows):
-        lanes = slice(r * members, (r + 1) * members)
-        if len(blocks) == 1:
-            grid[:, :, :, lanes] = blocks[0][:, :, r]
-        else:
-            grid[:, core, :, lanes] = blocks[0][:, 0, r]
-            grid[:, CORES - 1 - core, :, lanes] = blocks[1][:, r]
+    for move in moves + copies + [state_copy]:
+        move.start()
+    for move in moves:
+        move.wait()
     field = grid[...].reshape(chips * cores * lats, rows * members)
     state_copy.wait()
     for copy, start, end in zip(copies, cuts, cuts[1:]):
@@ -266,12 +280,6 @@
             blocks = [jnp.stack(pairs, axis=1)]
         laid = jnp.transpose(blocks[0], (2, 0, 1, 3, 4)).reshape(1, 1, rows, nlat, members)
         blocks, chips, cores, lats = [laid], 1, 1, nlat
-    windows = [pl.BlockSpec(blocks[0].shape, lambda i, m: (0, 0, 0, 0, 0))]
-    if len(blocks) > 1:
-        shape = (chips, 1) + blocks[0].shape[2:]
-        windows = [pl.BlockSpec(shape, lambda i, m: (0, m[0] % CORES, 0, 0, 0))]
-        windows += [pl.BlockSpec(blocks[1].shape, lambda i, m: (0, 0, 0, 0))]
-    in_hbm = pl.BlockSpec(memory_space=pltpu.HBM)
     return call(
         functools.partial(analyse_kernel, slot, low),
         "analyse",
@@ -281,7 +289,7 @@
         grid_spec=pltpu.PrefetchScalarGridSpec(
             num_scalar_prefetch=1,
             grid=(1,),
-            in_specs=[IN_SMEM, ANYWHERE, in_hbm, in_hbm] + windows,
+            in_specs=[IN_SMEM, ANYWHERE] + [IN_HBM] * (2 + len(blocks)),
             out_specs=pl.BlockSpec((rows, members, width), lambda i, m: (0, 0, 0)),
             scratch_shapes=[
                 pltpu.VMEM((chips, cores, lats, rows * members), BF16),
@@ -289,6 +297,7 @@
                 pltpu.VMEM((rows, members, width), BF16),
                 pltpu.SemaphoreType.DMA((width // 256 + 1,)),
                 pltpu.SemaphoreType.DMA,
+                pltpu.SemaphoreType.DMA((CORES, rows)),
             ],
         ),
     )(me, wave, token, table, state, *blocks)
@@ -436,64 +445,74 @@
 
 
 def assemble_kernel(counts, me_ref, *rest):
-    ins, out, (held, matrix) = rest[: sum(counts)], rest[-3], rest[-2:]
-    _, lats, slots, members = out.shape
+    ins, out_ref, (held, done, in_sems, out_sems) = rest[: sum(counts)], rest[-5], rest[-4:]
+    rows, lats, slots, members = done.shape
     local_slots = len(counts)
     chip = me_ref[0] // CORES
-    depth, breadth = math.gcd(lats, 16), 16
-
-    @pl.when((pl.program_id(0) == 0) & (pl.program_id(1) == 0))
-    def _():
-        matrix[...] = swap_matrix(breadth, depth, 1, 0)
-
-    views, used = [], 0
-    for count in counts:
-        refs = ins[used : used + count]
-        used += count
-        if count == 1:
-            views.append(lambda owner, j, ref=refs[0]: ref[owner // CORES, owner % CORES, 0, j, :])
-        else:
-            for k, ref in zip(partners(count), refs):
-                held[chip ^ k] = ref[:, 0]
-            views.append(lambda owner, j: held[owner // CORES, owner % CORES, j, :])
-    for start in range(0, lats, depth):
-        j = slice(start, start + depth)
-        for s in range(0, slots, 2 * breadth):
-            halves = []
-            for h in (0, breadth):
-                columns = [divmod(i, local_slots) for i in range(s + h, s + h + breadth)]
-                halves.append(jnp.concatenate([views[slot](owner, j) for owner, slot in columns], axis=0))
-            turned = jnp.dot(matrix[...], jnp.concatenate(halves, axis=1), preferred_element_type=F32).astype(BF16)
-            for h in range(2):
-                value = turned[:, h * members : (h + 1) * members].reshape(depth, breadth, members)
-                out[0, j, s + h * breadth : s + (h + 1) * breadth, :] = value
+    each = out_sems.shape[1]
+    size = lats // each
+    depth, breadth = math.gcd(size, 16), 16
+    copies = []
+    for r in range(rows):
+        copies.append([])
+        used = 0
+        for slot, count in enumerate(counts):
+            refs = ins[used : used + count]
+            used += count
+            if count == 1:
+                target = held.at[slot, :, :, r]
+                copies[r].append(pltpu.make_async_copy(refs[0].at[:, :, r], target, in_sems.at[r, slot, 0]))
+                continue
+            for i, (k, ref) in enumerate(zip(partners(count), refs)):
+                target = held.at[slot, chip ^ k, :, r]
+                copies[r].append(pltpu.make_async_copy(ref.at[:, r], target, in_sems.at[r, slot, i]))
+        for copy in copies[r]:
+            copy.start()
+    matrix = swap_matrix(breadth, depth, 1, 0)
+    results = []
+    for r in range(rows):
+        for copy in copies[r]:
+            copy.wait()
+        for start in range(0, lats, depth):
+            j = slice(start, start + depth)
+            for s in range(0, slots, 2 * breadth):
+                halves = []
+                for h in (0, breadth):
+                    columns = [divmod(i, local_slots) for i in range(s + h, s + h + breadth)]
+                    columns = [held[slot, owner // CORES, owner % CORES, r, j, :] for owner, slot in columns]
+                    halves.append(jnp.concatenate(columns, axis=0))
+                turned = jnp.dot(matrix, jnp.concatenate(halves, axis=1), preferred_element_type=F32).astype(BF16)
+                for h in range(2):
+                    value = turned[:, h * members : (h + 1) * members].reshape(depth, breadth, members)
+                    done[r, j, s + h * breadth : s + (h + 1) * breadth, :] = value
+            if (start + depth) % size == 0:
+                part = pl.ds(start + depth - size, size)
+                target = out_ref.at[r, part]
+                results.append(pltpu.make_async_copy(done.at[r, part], target, out_sems.at[r, start // size]))
+                results[-1].start()
+    for copy in results:
+        copy.wait()
 
 
 def assemble(pieces, me):
     rows, lats, members = pieces[0][0].shape[-3:]
     chips = max(len(p) if len(p) > 1 else p[0].shape[0] for p in pieces)
     slots = len(pieces) * chips * CORES
-    each = lat_block(lats)
-    side = 16 * math.gcd(each, 16)
     flat = [block for slot in pieces for block in slot]
-
-    def window(block):
-        lead = block.shape[:-3]
-        return pl.BlockSpec(lead + (1, each, members), lambda r, j, m: (0,) * len(lead) + (r, j, 0))
-
     return call(
         functools.partial(assemble_kernel, [len(p) for p in pieces]),
         "assemble",
         2 * 256 * rows * lats * slots * members,
         4 * rows * lats * slots * members,
         out_shape=jax.ShapeDtypeStruct((rows, lats, slots, members), BF16),
-        grid_spec=pltpu.PrefetchScalarGridSpec(
-            num_scalar_prefetch=1,
-            grid=(rows, lats // each),
-            in_specs=[window(block) for block in flat],
-            out_specs=pl.BlockSpec((1, each, slots, members), lambda r, j, m: (r, j, 0, 0)),
-            scratch_shapes=[pltpu.VMEM((chips, CORES, each, members), BF16), pltpu.VMEM((side, side), BF16)],
-        ),
+        in_specs=[IN_SMEM] + [IN_HBM] * len(flat),
+        out_specs=IN_HBM,
+        scratch_shapes=[
+            pltpu.VMEM((len(pieces), chips, CORES, rows, lats, members), BF16),
+            pltpu.VMEM((rows, lats, slots, members), BF16),
+            pltpu.SemaphoreType.DMA((rows, len(pieces), chips)),
+            pltpu.SemaphoreType.DMA((rows, lats // lat_block(lats))),
+        ],
     )(me, *flat)
 
 

time: 207 us -> 206 us (level)
  no operation moved by 1% of the time
where the time goes in v14:
time: 206 us; the launch traced here: 205 us
  waiting for transfers between devices  102 us (50%)
  Pallas kernels  49 us (24%)
  starting transfers between devices  42.4 us (21%)
  local copies, waits for them, and re-layouts  11.2 us (5%)
    all_to_all x3, waiting for transfers between devices, between_chips(): lax.all_to_all(blocks, 'wave', split_axis=0, concat_axis=0, axis_index_gr...  51.2 us
    ppermute x3, waiting for transfers between devices, per_device(): others = [lax.ppermute(part, 'pole', [(0, 1), (1, 0)]) for part in forced]  22.7 us
    all_to_all x3, starting transfers between devices, between_chips(): lax.all_to_all(blocks, 'wave', split_axis=0, concat_axis=0, axis_index_gr...  19.1 us
    ppermute x7, starting transfers between devices, by_permutes(): lax.ppermute(message, 'wave', [(d, d ^ k * CORES) for d in range(owners)])  17.8 us
    pallas_call x3, Pallas kernels, synthesise(): call(functools.partial(synthesise_kernel, slot, low, apart, more, len(par...  16.3 us
    pallas_call x3, Pallas kernels, analyse(): call(functools.partial(analyse_kernel, slot, low), 'analyse', 2 * width *...  14 us
    ppermute x7, waiting for transfers between devices, by_permutes(): lax.ppermute(message, 'wave', [(d, d ^ k * CORES) for d in range(owners)])  13 us
    unnamed x27, local copies, waits for them, and re-layouts  11.2 us
  transfers between devices with their start and end apart: 18, of which 15 were waited for; matrix products, arithmetic and copies ran while one was open for 0% of the time, Pallas kernels for 19%

profile of v14, /device:TPU:8, one launch (start us, length us, event | category | flops | bytes accessed | tf_op | source)
XLA Modules:
  0.0 204.6 jit_solution(5487813669891648130)
XLA Ops:
  0.0 4.9 %weigh.2 = (bf16[8,2,3,160,128]{4,3,2,1,0:T(8,128)(2,1)}, f32[8,128]{1,0:T(8,128)}) custom-call(s32[1]{0:T(128)} %bitcast.me_ref, f32[1,160]{1,0:T(1,128)} %bitcast.3, bf16[3,160,32,128]{3,2,1,0:T(8,128)(2,1)} %tendency_ref.3), custom_call_target="tpu_custom_call" | custom-call | flops 503316480 | bytes 5898240 | tf_op jit(solution)/shard_map/weigh/pallas_call | solution.py:132
  4.9 0.0 copy-start.12
  4.9 0.0 copy-start.11
  5.0 6.3 %all-to-all-start = ((bf16[8,2,3,160,128]{4,3,2,1,0:T(8,128)(2,1)}), bf16[8,2,3,160,128]{4,3,2,1,0:T(8,128)(2,1)S(1)}, u32[]{:S(2)}, u32[]{:S(2)}) async-start(bf16[8,2,3,160,128]{4,3,2,1,0:T(8,128)(2,1)} %get-tuple-element.36), calls=%async_computation | async-start | bytes 3932160 | tf_op jit(solution)/shard_map/all_to_all | solution.py:533
  11.2 0.0 copy-done.12
  11.2 0.1 copy.18.coeff_ref
  11.3 1.8 copy-done.9
  13.1 2.4 %sum_pairs.1.here_ref = f32[18,2,1280]{2,1,0:T(2,128)S(1)} custom-call(f32[32,2]{1,0:T(8,128)S(1)} %copy.18.coeff_ref, f32[8,128]{1,0:T(8,128)S(1)} %copy-done.11, bf16[32,18,2,1280]{3,2,1,0:T(2,128)(2,1)S(1)} %copy-done.9), custom_call_target="tpu_custom_call" | custom-call | flops 5898240 | bytes 2949120 | tf_op jit(solution)/shard_map/sum_pairs/pallas_call | solution.py:325
  15.5 1.6 collective-permute-start
  17.1 4.3 %collective-permute-done.rest_0_.there_ref = f32[18,2,1280]{2,1,0:T(2,128)S(1)} collective-permute-done((f32[18,2,1280]{2,1,0:T(2,128)S(1)}, f32[18,2,1280]{2,1,0:T(2,128)S(1)}, u32[]{:S(2)}, u32[]{:S(2)}) %collective-permute-start) | collective-permute-done | bytes 184352 | tf_op jit(solution)/shard_map/ppermute | solution.py:553
  21.4 0.7 copy-done.7
  22.1 5.0 %weigh.3 = (bf16[8,2,3,160,128]{4,3,2,1,0:T(8,128)(2,1)}, bf16[8,3,160,128]{3,2,1,0:T(8,128)(2,1)}, f32[8,128]{1,0:T(8,128)}) custom-call(s32[1]{0:T(128)} %bitcast.me_ref, f32[1,160]{1,0:T(1,128)} %bitcast.4, bf16[3,160,32,128]{3,2,1,0:T(8,128)(2,1)} %tendency_ref.3, f32[18,2,1280]{2,1,0:T(2,128)} %copy-done.7), custom_call_target="tpu_custom_call" | custom-call | flops 503316480 | bytes 5898240 | tf_op jit(solution)/shard_map/weigh/pallas_call | solution.py:132
  27.0 0.1 collective-permute-start.1
  27.1 2.8 %collective-permute-done.1.mate_ref = bf16[8,3,160,128]{3,2,1,0:T(8,128)(2,1)S(1)} collective-permute-done((bf16[8,3,160,128]{3,2,1,0:T(8,128)(2,1)}, bf16[8,3,160,128]{3,2,1,0:T(8,128)(2,1)S(1)}, u32[]{:S(2)}, u32[]{:S(2)}) %collective-permute-start.1) | collective-permute-done | bytes 983072 | tf_op jit(solution)/shard_map/ppermute | solution.py:520
  29.9 1.5 copy-done.5
  31.4 0.1 pair.4
  31.5 1.3 copy-done.6
  32.8 21.4 %all-to-all-done.in_ref.rest_0_ = bf16[8,2,3,160,128]{4,3,2,1,0:T(8,128)(2,1)S(1)} async-done(((bf16[8,2,3,160,128]{4,3,2,1,0:T(8,128)(2,1)}), bf16[8,2,3,160,128]{4,3,2,1,0:T(8,128)(2,1)S(1)}, u32[]{:S(2)}, u32[]{:S(2)}) %all-to-all-start) | async-done | bytes 1966112 | tf_op jit(solution)/shard_map/all_to_all | solution.py:533
  54.2 1.3 copy-done.2
  55.5 6.1 %all-to-all-start.1 = ((bf16[8,2,3,160,128]{4,3,2,1,0:T(8,128)(2,1)}), bf16[8,2,3,160,128]{4,3,2,1,0:T(8,128)(2,1)S(1)}, u32[]{:S(2)}, u32[]{:S(2)}) async-start(bf16[8,2,3,160,128]{4,3,2,1,0:T(8,128)(2,1)} %copy-done.6), calls=%async_computation.1 | async-start | bytes 3932160 | tf_op jit(solution)/shard_map/all_to_all | solution.py:533
  61.6 1.7 copy-done.3
  63.3 0.2 pick.1
  63.5 0.1 collective-permute-start.2
  63.6 2.6 %collective-permute-done.2.rest_1_ = bf16[8,3,160,128]{3,2,1,0:T(8,128)(2,1)S(1)} collective-permute-done((bf16[8,3,160,128]{3,2,1,0:T(8,128)(2,1)S(1)}, bf16[8,3,160,128]{3,2,1,0:T(8,128)(2,1)S(1)}, u32[]{:S(2)}, u32[]{:S(2)}) %collective-permute-start.2) | collective-permute-done | bytes 983072 | tf_op jit(solution)/shard_map/ppermute | solution.py:520
  66.1 4.7 %analyse.3.own_ref = bf16[3,128,640]{2,1,0:T(8,128)(2,1)S(1)} custom-call(s32[1]{0:T(128)} %bitcast.me_ref, s32[2]{0:T(128)S(1)} %copy-done.10, f32[8,128]{1,0:T(8,128)S(1)} %get-tuple-element.35.token_ref, bf16[2,1280,2560]{2,1,0:T(8,128)(2,1)} %table_ref.11, bf16[3,2,128,1280]{3,2,1,0:T(8,128)(2,1)S(1)} %copy-done, ...), custom_call_target="tpu_custom_call" | custom-call | flops 1258291200 | bytes 3276800 | tf_op jit(solution)/shard_map/analyse/pallas_call | solution.py:283
  70.8 1.6 collective-permute-start.3
  72.4 11.8 %collective-permute-done.3.other_ref = bf16[3,128,640]{2,1,0:T(8,128)(2,1)S(1)} collective-permute-done((bf16[3,128,640]{2,1,0:T(8,128)(2,1)S(1)}, bf16[3,128,640]{2,1,0:T(8,128)(2,1)S(1)}, u32[]{:S(2)}, u32[]{:S(2)}) %collective-permute-start.3) | collective-permute-done | bytes 491552 | tf_op jit(solution)/shard_map/ppermute | solution.py:567
  84.1 4.9 %synthesise.3 = (bf16[8,2,3,160,128]{4,3,2,1,0:T(8,128)(2,1)S(1)}, bf16[8,3,160,128]{3,2,1,0:T(8,128)(2,1)S(1)}) custom-call(s32[1]{0:T(128)} %bitcast.me_ref, f32[1]{0:T(128)} %bitcast.1.sign_ref, f32[18,2,1280]{2,1,0:T(2,128)S(1)} %sum_pairs.1.here_ref, f32[18,2,1280]{2,1,0:T(2,128)S(1)} %copy-done.8, bf16[3,128,640]{2,1,0:T(8,128)(2,1)S(1)} %analyse.3.own_ref, ...), custom_call_target="tpu_custom_call" | custom-call | flops 1258291200 | bytes 3276800 | tf_op jit(solution)/shard_map/synthesise/pallas_call | solution.py:423
  89.1 0.1 collective-permute-start.4
  89.2 2.6 %collective-permute-done.4.mate_ref = bf16[8,3,160,128]{3,2,1,0:T(8,128)(2,1)S(1)} collective-permute-done((bf16[8,3,160,128]{3,2,1,0:T(8,128)(2,1)S(1)}, bf16[8,3,160,128]{3,2,1,0:T(8,128)(2,1)S(1)}, u32[]{:S(2)}, u32[]{:S(2)}) %collective-permute-start.4) | collective-permute-done | bytes 983072 | tf_op jit(solution)/shard_map/ppermute | solution.py:520
  91.7 0.1 pair.5
  91.8 0.0 copy-start.4
  91.8 1.3 copy-done.4
  93.1 11.6 %all-to-all-done.1.rest_0_ = bf16[8,2,3,160,128]{4,3,2,1,0:T(8,128)(2,1)S(1)} async-done(((bf16[8,2,3,160,128]{4,3,2,1,0:T(8,128)(2,1)}), bf16[8,2,3,160,128]{4,3,2,1,0:T(8,128)(2,1)S(1)}, u32[]{:S(2)}, u32[]{:S(2)}) %all-to-all-start.1) | async-done | bytes 1966112 | tf_op jit(solution)/shard_map/all_to_all | solution.py:533
  104.7 6.7 %all-to-all-start.2 = ((bf16[8,2,3,160,128]{4,3,2,1,0:T(8,128)(2,1)}), bf16[8,2,3,160,128]{4,3,2,1,0:T(8,128)(2,1)}, u32[]{:S(2)}, u32[]{:S(2)}) async-start(bf16[8,2,3,160,128]{4,3,2,1,0:T(8,128)(2,1)} %copy-done.4), calls=%async_computation.2 | async-start | bytes 3932160 | tf_op jit(solution)/shard_map/all_to_all | solution.py:533
  111.4 1.5 copy-done.1
  112.9 4.7 %analyse.5.own_ref = bf16[3,128,640]{2,1,0:T(8,128)(2,1)S(1)} custom-call(s32[1]{0:T(128)} %bitcast.me_ref, s32[2]{0:T(128)S(1)} %copy-done.10, f32[8,128]{1,0:T(8,128)S(1)} %get-tuple-element.39.token_ref, bf16[2,1280,2560]{2,1,0:T(8,128)(2,1)} %table_ref.11, bf16[3,2,128,1280]{3,2,1,0:T(8,128)(2,1)S(1)} %copy-done.1, ...), custom_call_target="tpu_custom_call" | custom-call | flops 1258291200 | bytes 3276800 | tf_op jit(solution)/shard_map/analyse/pallas_call | solution.py:283
  117.6 1.6 collective-permute-start.6
  119.2 4.6 %analyse.4.own_ref = bf16[3,128,640]{2,1,0:T(8,128)(2,1)S(1)} custom-call(s32[1]{0:T(128)} %bitcast.me_ref, s32[2]{0:T(128)S(1)} %copy-done.10, f32[8,128]{1,0:T(8,128)S(1)} %get-tuple-element.39.token_ref, bf16[2,1280,2560]{2,1,0:T(8,128)(2,1)} %table_ref.11, bf16[3,2,128,1280]{3,2,1,0:T(8,128)(2,1)S(1)} %copy-done.1, ...), custom_call_target="tpu_custom_call" | custom-call | flops 1258291200 | bytes 3276800 | tf_op jit(solution)/shard_map/analyse/pallas_call | solution.py:283
  123.8 0.6 collective-permute-start.5
  124.4 7.4 %collective-permute-done.6.other_ref = bf16[3,128,640]{2,1,0:T(8,128)(2,1)S(1)} collective-permute-done((bf16[3,128,640]{2,1,0:T(8,128)(2,1)S(1)}, bf16[3,128,640]{2,1,0:T(8,128)(2,1)S(1)}, u32[]{:S(2)}, u32[]{:S(2)}) %collective-permute-start.6) | collective-permute-done | bytes 491552 | tf_op jit(solution)/shard_map/ppermute | solution.py:567
  131.8 4.8 %synthesise.4.rest_0_ = f32[384,2560]{1,0:T(8,128)S(1)} custom-call(s32[1]{0:T(128)} %bitcast.me_ref, f32[1]{0:T(128)} %bitcast.1.sign_ref, f32[18,2,1280]{2,1,0:T(2,128)S(1)} %sum_pairs.1.here_ref, f32[18,2,1280]{2,1,0:T(2,128)S(1)} %copy-done.8, bf16[3,128,640]{2,1,0:T(8,128)(2,1)S(1)} %analyse.5.own_ref, ...), custom_call_target="tpu_custom_call" | custom-call | flops 1258291200 | bytes 3276800 | tf_op jit(solution)/shard_map/synthesise/pallas_call | solution.py:423
  136.7 3.5 %collective-permute-done.5.other_ref = bf16[3,128,640]{2,1,0:T(8,128)(2,1)S(1)} collective-permute-done((bf16[3,128,640]{2,1,0:T(8,128)(2,1)S(1)}, bf16[3,128,640]{2,1,0:T(8,128)(2,1)S(1)}, u32[]{:S(2)}, u32[]{:S(2)}) %collective-permute-start.5) | collective-permute-done | bytes 491552 | tf_op jit(solution)/shard_map/ppermute | solution.py:567
  140.2 6.5 %synthesise.5 = (bf16[2,3,160,128]{3,2,1,0:T(8,128)(2,1)S(1)}, bf16[2,3,160,128]{3,2,1,0:T(8,128)(2,1)S(1)}, bf16[2,3,160,128]{3,2,1,0:T(8,128)(2,1)}, bf16[2,3,...) custom-call(s32[1]{0:T(128)} %bitcast.me_ref, ...), custom_call_target="tpu_custom_call" | custom-call | flops 1258291200 | bytes 3276800 | tf_op jit(solution)/shard_map/synthesise/pallas_call | solution.py:423
  146.7 0.1 collective-permute-start.7
  146.8 2.6 %collective-permute-done.7.mate_ref = bf16[8,3,160,128]{3,2,1,0:T(8,128)(2,1)S(1)} collective-permute-done((bf16[8,3,160,128]{3,2,1,0:T(8,128)(2,1)S(1)}, bf16[8,3,160,128]{3,2,1,0:T(8,128)(2,1)S(1)}, u32[]{:S(2)}, u32[]{:S(2)}) %collective-permute-start.7) | collective-permute-done | bytes 983072 | tf_op jit(solution)/shard_map/ppermute | solution.py:520
  149.4 1.1 pair.6
  150.5 1.7 collective-permute-start.8
  152.1 2.2 %collective-permute-start.9 = (bf16[2,3,160,128]{3,2,1,0:T(8,128)(2,1)}, bf16[2,3,160,128]{3,2,1,0:T(8,128)(2,1)S(1)}, u32[]{:S(2)}, u32[]{:S(2)}) collective-permute-start(bf16[2,3,160,128]{3,2,1,0:T(8,128)(2,1)} %get-tuple-element.49), channel_id=1, source_target_pairs={{0,10},{1,11},{2,8},{3,9},{4,14},{5,15},{6,12},{7,13},{8,2},{9,3},... | collective-permute-start | bytes 737288 | tf_op jit(solution)/shard_map/ppermute | solution.py:527
  154.3 0.8 collective-permute-start.10
  155.2 1.2 collective-permute-start.11
  156.4 18.3 %all-to-all-done.2.rest_3_.rest_8_ = bf16[8,2,3,160,128]{4,3,2,1,0:T(8,128)(2,1)} async-done(((bf16[8,2,3,160,128]{4,3,2,1,0:T(8,128)(2,1)}), bf16[8,2,3,160,128]{4,3,2,1,0:T(8,128)(2,1)}, u32[]{:S(2)}, u32[]{:S(2)}) %all-to-all-start.2) | async-done | bytes 1966112 | tf_op jit(solution)/shard_map/all_to_all | solution.py:533
  174.6 0.5 pair.7
  175.1 1.1 collective-permute-start.12
  176.3 3.5 %collective-permute-done.8.rest_1_ = bf16[2,3,160,128]{3,2,1,0:T(8,128)(2,1)S(1)} collective-permute-done((bf16[2,3,160,128]{3,2,1,0:T(8,128)(2,1)S(1)}, bf16[2,3,160,128]{3,2,1,0:T(8,128)(2,1)S(1)}, u32[]{:S(2)}, u32[]{:S(2)}) %collective-permute-start.8) | collective-permute-done | bytes 245792 | tf_op jit(solution)/shard_map/ppermute | solution.py:527
  179.8 5.0 %collective-permute-start.13 = (bf16[2,3,160,128]{3,2,1,0:T(8,128)(2,1)S(1)}, bf16[2,3,160,128]{3,2,1,0:T(8,128)(2,1)S(1)}, u32[]{:S(2)}, u32[]{:S(2)}) collective-permute-start(bf16[2,3,160,128]{3,2,1,0:T(8,128)(2,1)S(1)} %get-tuple-element.57), channel_id=1, source_target_pairs={{0,4},{1,5},{2,6},{3,7},{4,0},{5,1},{6,2},{7,3},{8,12},{9,13},{10,... | collective-permute-start | bytes 737288 | tf_op jit(solution)/shard_map/ppermute | solution.py:527
  184.8 0.4 collective-permute-done.9.rest_2_
  185.3 5.7 %collective-permute-start.14 = (bf16[2,3,160,128]{3,2,1,0:T(8,128)(2,1)S(1)}, bf16[2,3,160,128]{3,2,1,0:T(8,128)(2,1)S(1)}, u32[]{:S(2)}, u32[]{:S(2)}) collective-permute-start(bf16[2,3,160,128]{3,2,1,0:T(8,128)(2,1)S(1)} %get-tuple-element.58), channel_id=1, source_target_pairs={{0,6},{1,7},{2,4},{3,5},{4,2},{5,3},{6,0},{7,1},{8,14},{9,15},{10,... | collective-permute-start | bytes 737288 | tf_op jit(solution)/shard_map/ppermute | solution.py:527
  190.9 2.9 %collective-permute-done.10.rest_3_ = bf16[2,3,160,128]{3,2,1,0:T(8,128)(2,1)S(1)} collective-permute-done((bf16[2,3,160,128]{3,2,1,0:T(8,128)(2,1)}, bf16[2,3,160,128]{3,2,1,0:T(8,128)(2,1)S(1)}, u32[]{:S(2)}, u32[]{:S(2)}) %collective-permute-start.10) | collective-permute-done | bytes 245792 | tf_op jit(solution)/shard_map/ppermute | solution.py:527
  193.8 6.2 %collective-permute-done.11.rest_4_ = bf16[2,3,160,128]{3,2,1,0:T(8,128)(2,1)S(1)} collective-permute-done((bf16[2,3,160,128]{3,2,1,0:T(8,128)(2,1)}, bf16[2,3,160,128]{3,2,1,0:T(8,128)(2,1)S(1)}, u32[]{:S(2)}, u32[]{:S(2)}) %collective-permute-start.11) | collective-permute-done | bytes 245792 | tf_op jit(solution)/shard_map/ppermute | solution.py:527
  200.0 0.0 collective-permute-done.12.rest_5_
  200.0 0.0 collective-permute-done.13.rest_6_
  200.0 0.0 collective-permute-done.14.rest_7_
  200.0 4.5 %assemble.1 = bf16[3,160,32,128]{3,2,1,0:T(8,128)(2,1)} custom-call(s32[1]{0:T(128)} %bitcast.me_ref, bf16[2,3,160,128]{3,2,1,0:T(8,128)(2,1)S(1)} %get-tuple-element.47.rest_0_, bf16[2,3,160,128]{3,2,1,0:T(8,128)(2,1)S(1)} %collective-permute-done.8.rest_1_, bf16[2,3,160,128]{3,2,1,0:T(8,128)(2,1)S(1)} %collective-permute-done.9.rest_2_, ...), custom_call_target="tpu_custom_call" | custom-call | flops 1006632960 | bytes 7864320 | tf_op jit(solution)/shard_map/assemble/pallas_call | solution.py:502
  (14 shorter events, 0.0 us)
Async XLA Ops:
  4.9 6.3 %copy-start.12 = (f32[32,2]{0,1:T(2,128)S(1)}, f32[32,2]{0,1:T(2,128)}, u32[]{:S(2)}) copy-start(f32[32,2]{0,1:T(2,128)} %param.12) | copy-start | bytes 772
  4.9 6.4 %copy-start.11 = (f32[8,128]{1,0:T(8,128)S(1)}, f32[8,128]{1,0:T(8,128)}, u32[]{:S(2)}) copy-start(f32[8,128]{1,0:T(8,128)} %get-tuple-element.32.token_ref) | copy-start | bytes 12292
  5.0 49.2 %all-to-all-start = ((bf16[8,2,3,160,128]{4,3,2,1,0:T(8,128)(2,1)}), bf16[8,2,3,160,128]{4,3,2,1,0:T(8,128)(2,1)S(1)}, u32[]{:S(2)}, u32[]{:S(2)}) async-start(bf16[8,2,3,160,128]{4,3,2,1,0:T(8,128)(2,1)} %get-tuple-element.36), calls=%async_computation | async-start | bytes 3932160 | tf_op jit(solution)/shard_map/all_to_all | solution.py:533
  11.3 1.8 copy-start.9
  15.5 5.9 %collective-permute-start = (f32[18,2,1280]{2,1,0:T(2,128)S(1)}, f32[18,2,1280]{2,1,0:T(2,128)S(1)}, u32[]{:S(2)}, u32[]{:S(2)}) collective-permute-start(f32[18,2,1280]{2,1,0:T(2,128)S(1)} %sum_pairs.1.here_ref), channel_id=1, source_target_pairs={{0,16},{16,0},{1,17},{17,1},{2,18},{18,2},{3,19},{19,3},{4,20},{20... | collective-permute-start | bytes 552968 | tf_op jit(solution)/shard_map/ppermute | solution.py:553
  21.4 0.7 copy-start.7
  27.0 2.8 %collective-permute-start.1 = (bf16[8,3,160,128]{3,2,1,0:T(8,128)(2,1)}, bf16[8,3,160,128]{3,2,1,0:T(8,128)(2,1)S(1)}, u32[]{:S(2)}, u32[]{:S(2)}) collective-permute-start(bf16[8,3,160,128]{3,2,1,0:T(8,128)(2,1)} %get-tuple-element.33), channel_id=1, source_target_pairs={{0,1},{1,0},{2,3},{3,2},{4,5},{5,4},{6,7},{7,6},{8,9},{9,8},{10,11... | collective-permute-start | bytes 2949128 | tf_op jit(solution)/shard_map/ppermute | solution.py:520
  29.9 1.5 copy-start.5
  31.5 1.3 copy-start.6
  54.2 1.3 copy-start.2
  55.5 49.2 %all-to-all-start.1 = ((bf16[8,2,3,160,128]{4,3,2,1,0:T(8,128)(2,1)}), bf16[8,2,3,160,128]{4,3,2,1,0:T(8,128)(2,1)S(1)}, u32[]{:S(2)}, u32[]{:S(2)}) async-start(bf16[8,2,3,160,128]{4,3,2,1,0:T(8,128)(2,1)} %copy-done.6), calls=%async_computation.1 | async-start | bytes 3932160 | tf_op jit(solution)/shard_map/all_to_all | solution.py:533
  61.6 4.6 %copy-start = (bf16[3,2,128,1280]{3,2,1,0:T(8,128)(2,1)S(1)}, bf16[3,2,128,1280]{3,2,1,0:T(8,128)(2,1)}, u32[]{:S(2)}) copy-start(bf16[3,2,128,1280]{3,2,1,0:T(8,128)(2,1)} %state_ref.5) | copy-start | bytes 5898244
  61.6 1.7 copy-start.3
  63.2 2.9 %copy-start.10 = (s32[2]{0:T(128)S(1)}, s32[2]{0:T(128)}, u32[]{:S(2)}) copy-start(s32[2]{0:T(128)} %wave_ref.5) | copy-start | bytes 28
  63.5 20.6 %copy-start.8 = (f32[18,2,1280]{2,1,0:T(2,128)S(1)}, f32[18,2,1280]{2,1,0:T(2,128)}, u32[]{:S(2)}) copy-start(f32[18,2,1280]{2,1,0:T(2,128)} %copy-done.7) | copy-start | bytes 552964
  63.5 2.6 %collective-permute-start.2 = (bf16[8,3,160,128]{3,2,1,0:T(8,128)(2,1)S(1)}, bf16[8,3,160,128]{3,2,1,0:T(8,128)(2,1)S(1)}, u32[]{:S(2)}, u32[]{:S(2)}) collective-permute-start(bf16[8,3,160,128]{3,2,1,0:T(8,128)(2,1)S(1)} %pick.1), channel_id=1, source_target_pairs={{0,1},{1,0},{2,3},{3,2},{4,5},{5,4},{6,7},{7,6},{8,9},{9,8},{10,11... | collective-permute-start | bytes 2949128 | tf_op jit(solution)/shard_map/ppermute | solution.py:520
  70.8 13.3 %collective-permute-start.3 = (bf16[3,128,640]{2,1,0:T(8,128)(2,1)S(1)}, bf16[3,128,640]{2,1,0:T(8,128)(2,1)S(1)}, u32[]{:S(2)}, u32[]{:S(2)}) collective-permute-start(bf16[3,128,640]{2,1,0:T(8,128)(2,1)S(1)} %analyse.3.own_ref), channel_id=1, source_target_pairs={{0,16},{16,0},{1,17},{17,1},{2,18},{18,2},{3,19},{19,3},{4,20},{20... | collective-permute-start | bytes 1474568 | tf_op jit(solution)/shard_map/ppermute | solution.py:567
  89.1 2.6 %collective-permute-start.4 = (bf16[8,3,160,128]{3,2,1,0:T(8,128)(2,1)S(1)}, bf16[8,3,160,128]{3,2,1,0:T(8,128)(2,1)S(1)}, u32[]{:S(2)}, u32[]{:S(2)}) collective-permute-start(bf16[8,3,160,128]{3,2,1,0:T(8,128)(2,1)S(1)} %get-tuple-element.37), channel_id=1, source_target_pairs={{0,1},{1,0},{2,3},{3,2},{4,5},{5,4},{6,7},{7,6},{8,9},{9,8},{10,11... | collective-permute-start | bytes 2949128 | tf_op jit(solution)/shard_map/ppermute | solution.py:520
  91.8 1.3 copy-start.4
  104.7 69.9 %all-to-all-start.2 = ((bf16[8,2,3,160,128]{4,3,2,1,0:T(8,128)(2,1)}), bf16[8,2,3,160,128]{4,3,2,1,0:T(8,128)(2,1)}, u32[]{:S(2)}, u32[]{:S(2)}) async-start(bf16[8,2,3,160,128]{4,3,2,1,0:T(8,128)(2,1)} %copy-done.4), calls=%async_computation.2 | async-start | bytes 3932160 | tf_op jit(solution)/shard_map/all_to_all | solution.py:533
  111.4 1.5 copy-start.1
  117.6 14.2 %collective-permute-start.6 = (bf16[3,128,640]{2,1,0:T(8,128)(2,1)S(1)}, bf16[3,128,640]{2,1,0:T(8,128)(2,1)S(1)}, u32[]{:S(2)}, u32[]{:S(2)}) collective-permute-start(bf16[3,128,640]{2,1,0:T(8,128)(2,1)S(1)} %analyse.5.own_ref), channel_id=1, source_target_pairs={{0,16},{16,0},{1,17},{17,1},{2,18},{18,2},{3,19},{19,3},{4,20},{20... | collective-permute-start | bytes 1474568 | tf_op jit(solution)/shard_map/ppermute | solution.py:567
  123.8 16.3 %collective-permute-start.5 = (bf16[3,128,640]{2,1,0:T(8,128)(2,1)S(1)}, bf16[3,128,640]{2,1,0:T(8,128)(2,1)S(1)}, u32[]{:S(2)}, u32[]{:S(2)}) collective-permute-start(bf16[3,128,640]{2,1,0:T(8,128)(2,1)S(1)} %analyse.4.own_ref), channel_id=1, source_target_pairs={{0,16},{16,0},{1,17},{17,1},{2,18},{18,2},{3,19},{19,3},{4,20},{20... | collective-permute-start | bytes 1474568 | tf_op jit(solution)/shard_map/ppermute | solution.py:567
  146.7 2.6 %collective-permute-start.7 = (bf16[8,3,160,128]{3,2,1,0:T(8,128)(2,1)S(1)}, bf16[8,3,160,128]{3,2,1,0:T(8,128)(2,1)S(1)}, u32[]{:S(2)}, u32[]{:S(2)}) collective-permute-start(bf16[8,3,160,128]{3,2,1,0:T(8,128)(2,1)S(1)} %get-tuple-element.41), channel_id=1, source_target_pairs={{0,1},{1,0},{2,3},{3,2},{4,5},{5,4},{6,7},{7,6},{8,9},{9,8},{10,11... | collective-permute-start | bytes 2949128 | tf_op jit(solution)/shard_map/ppermute | solution.py:520
  150.5 29.3 %collective-permute-start.8 = (bf16[2,3,160,128]{3,2,1,0:T(8,128)(2,1)S(1)}, bf16[2,3,160,128]{3,2,1,0:T(8,128)(2,1)S(1)}, u32[]{:S(2)}, u32[]{:S(2)}) collective-permute-start(bf16[2,3,160,128]{3,2,1,0:T(8,128)(2,1)S(1)} %get-tuple-element.48), channel_id=1, source_target_pairs={{0,8},{1,9},{2,10},{3,11},{4,12},{5,13},{6,14},{7,15},{8,0},{9,1},... | collective-permute-start | bytes 737288 | tf_op jit(solution)/shard_map/ppermute | solution.py:527
  152.1 33.1 %collective-permute-start.9 = (bf16[2,3,160,128]{3,2,1,0:T(8,128)(2,1)}, bf16[2,3,160,128]{3,2,1,0:T(8,128)(2,1)S(1)}, u32[]{:S(2)}, u32[]{:S(2)}) collective-permute-start(bf16[2,3,160,128]{3,2,1,0:T(8,128)(2,1)} %get-tuple-element.49), channel_id=1, source_target_pairs={{0,10},{1,11},{2,8},{3,9},{4,14},{5,15},{6,12},{7,13},{8,2},{9,3},... | collective-permute-start | bytes 737288 | tf_op jit(solution)/shard_map/ppermute | solution.py:527
  154.3 39.5 %collective-permute-start.10 = (bf16[2,3,160,128]{3,2,1,0:T(8,128)(2,1)}, bf16[2,3,160,128]{3,2,1,0:T(8,128)(2,1)S(1)}, u32[]{:S(2)}, u32[]{:S(2)}) collective-permute-start(bf16[2,3,160,128]{3,2,1,0:T(8,128)(2,1)} %get-tuple-element.50), channel_id=1, source_target_pairs={{0,12},{1,13},{2,14},{3,15},{4,8},{5,9},{6,10},{7,11},{8,4},{9,5},... | collective-permute-start | bytes 737288 | tf_op jit(solution)/shard_map/ppermute | solution.py:527
  155.2 44.8 %collective-permute-start.11 = (bf16[2,3,160,128]{3,2,1,0:T(8,128)(2,1)}, bf16[2,3,160,128]{3,2,1,0:T(8,128)(2,1)S(1)}, u32[]{:S(2)}, u32[]{:S(2)}) collective-permute-start(bf16[2,3,160,128]{3,2,1,0:T(8,128)(2,1)} %get-tuple-element.51), channel_id=1, source_target_pairs={{0,14},{1,15},{2,12},{3,13},{4,10},{5,11},{6,8},{7,9},{8,6},{9,7},... | collective-permute-start | bytes 737288 | tf_op jit(solution)/shard_map/ppermute | solution.py:527
  175.1 24.9 %collective-permute-start.12 = (bf16[2,3,160,128]{3,2,1,0:T(8,128)(2,1)S(1)}, bf16[2,3,160,128]{3,2,1,0:T(8,128)(2,1)S(1)}, u32[]{:S(2)}, u32[]{:S(2)}) collective-permute-start(bf16[2,3,160,128]{3,2,1,0:T(8,128)(2,1)S(1)} %get-tuple-element.56), channel_id=1, source_target_pairs={{0,2},{1,3},{2,0},{3,1},{4,6},{5,7},{6,4},{7,5},{8,10},{9,11},{10,... | collective-permute-start | bytes 737288 | tf_op jit(solution)/shard_map/ppermute | solution.py:527
  179.8 20.2 %collective-permute-start.13 = (bf16[2,3,160,128]{3,2,1,0:T(8,128)(2,1)S(1)}, bf16[2,3,160,128]{3,2,1,0:T(8,128)(2,1)S(1)}, u32[]{:S(2)}, u32[]{:S(2)}) collective-permute-start(bf16[2,3,160,128]{3,2,1,0:T(8,128)(2,1)S(1)} %get-tuple-element.57), channel_id=1, source_target_pairs={{0,4},{1,5},{2,6},{3,7},{4,0},{5,1},{6,2},{7,3},{8,12},{9,13},{10,... | collective-permute-start | bytes 737288 | tf_op jit(solution)/shard_map/ppermute | solution.py:527
  185.3 14.7 %collective-permute-start.14 = (bf16[2,3,160,128]{3,2,1,0:T(8,128)(2,1)S(1)}, bf16[2,3,160,128]{3,2,1,0:T(8,128)(2,1)S(1)}, u32[]{:S(2)}, u32[]{:S(2)}) collective-permute-start(bf16[2,3,160,128]{3,2,1,0:T(8,128)(2,1)S(1)} %get-tuple-element.58), channel_id=1, source_target_pairs={{0,6},{1,7},{2,4},{3,5},{4,2},{5,3},{6,0},{7,1},{8,14},{9,15},{10,... | collective-permute-start | bytes 737288 | tf_op jit(solution)/shard_map/ppermute | solution.py:527

commit v15 on v14

--- a/solution.py
+++ b/solution.py
@@ -14,6 +14,7 @@
 ANYWHERE = pl.BlockSpec(memory_space=pl.ANY)
 IN_SMEM = pl.BlockSpec(memory_space=pltpu.SMEM)
 IN_HBM = pl.BlockSpec(memory_space=pltpu.HBM)
+IN_VMEM = pl.BlockSpec(memory_space=pltpu.VMEM)
 TOKEN = jax.ShapeDtypeStruct((8, 128), F32)
 
 
@@ -107,13 +108,18 @@
                     for i, value in enumerate(values):
                         chip, target = divmod(start + i, CORES)
                         done[chip, target, r, j : j + depth, :] = value.astype(BF16)
-        if split:
-            results.append(pltpu.make_async_copy(done.at[:, 0, r], outs[0].at[:, core, r], out_sems.at[0, r]))
-            results.append(pltpu.make_async_copy(done.at[:, 1, r], outs[1].at[:, r], out_sems.at[1, r]))
-            results[-2].start()
-        else:
-            results.append(pltpu.make_async_copy(done.at[:, :, r], outs[0].at[:, :, r], out_sems.at[0, r]))
-        results[-1].start()
+            if (j + depth) % size == 0:
+                part = pl.ds(j + depth - size, size)
+                source, target = done.at[:, :, r, part], outs[0].at[:, :, r, part]
+                if split:
+                    source, target = done.at[:, 0, r, part], outs[0].at[:, core, r, part]
+                    other = pltpu.make_async_copy(
+                        done.at[:, 1, r, part], outs[1].at[:, r, part], out_sems.at[1, r, j // size]
+                    )
+                    other.start()
+                    results.append(other)
+                results.append(pltpu.make_async_copy(source, target, out_sems.at[0, r, j // size]))
+                results[-1].start()
     for copy in results:
         copy.wait()
 
@@ -145,42 +151,9 @@
             pltpu.VMEM((chips, CORES, rows, lats, members), BF16),
             pltpu.SemaphoreType.DMA,
             pltpu.SemaphoreType.DMA((rows, each)),
-            pltpu.SemaphoreType.DMA((CORES, rows)),
+            pltpu.SemaphoreType.DMA((CORES, rows, each)),
         ],
     )(me, gauss, tendency, *waits)
-
-
-def pick_kernel(me_ref, token_ref, in_ref, out_ref, held, in_sems, out_sems):
-    other = CORES - 1 - me_ref[0] % CORES
-    rows = held.shape[1]
-    fetched = [pltpu.make_async_copy(in_ref.at[:, other, r], held.at[:, r], in_sems.at[r]) for r in range(rows)]
-    stored = [pltpu.make_async_copy(held.at[:, r], out_ref.at[:, r], out_sems.at[r]) for r in range(rows)]
-    for copy in fetched:
-        copy.start()
-    for fetch, store in zip(fetched, stored):
-        fetch.wait()
-        store.start()
-    for copy in stored:
-        copy.wait()
-
-
-def pick(blocks, me, token):
-    chips, _, rows, lats, members = blocks.shape
-    shape = (chips, rows, lats, members)
-    return call(
-        pick_kernel,
-        "pick",
-        0,
-        2 * blocks.size,
-        out_shape=jax.ShapeDtypeStruct(shape, BF16),
-        in_specs=[IN_SMEM, ANYWHERE, IN_HBM],
-        out_specs=IN_HBM,
-        scratch_shapes=[
-            pltpu.VMEM(shape, BF16),
-            pltpu.SemaphoreType.DMA((rows,)),
-            pltpu.SemaphoreType.DMA((rows,)),
-        ],
-    )(me, token, blocks)
 
 
 def pair_kernel(me_ref, mate_ref, blocks_ref, out_ref, token_ref, sem):
@@ -231,21 +204,14 @@
     )(me, mate, *messages, *waits)
 
 
-def analyse_kernel(slot, low, me_ref, wave_ref, token_ref, table_ref, state_ref, *rest):
-    blocks, out, (grid, table, state, table_sems, state_sem, block_sems) = rest[:-7], rest[-7], rest[-6:]
+def analyse_kernel(slot, low, wave_ref, token_ref, table_ref, state_ref, blocks_ref, out, *scratch):
+    grid, table, state, table_sems, state_sem, block_sems = scratch
     rows, members, width = out.shape
     chips, cores, lats, _ = grid.shape
-    core = me_ref[0] % CORES
     moves = []
     for r in range(rows):
-        lanes = pl.ds(r * members, members)
-        if len(blocks) == 1:
-            moves.append(pltpu.make_async_copy(blocks[0].at[:, :, r], grid.at[:, :, :, lanes], block_sems.at[0, r]))
-        else:
-            target = grid.at[:, core, :, lanes]
-            moves.append(pltpu.make_async_copy(blocks[0].at[:, core, r], target, block_sems.at[0, r]))
-            target = grid.at[:, CORES - 1 - core, :, lanes]
-            moves.append(pltpu.make_async_copy(blocks[1].at[:, r], target, block_sems.at[1, r]))
+        target = grid.at[:, :, :, pl.ds(r * members, members)]
+        moves.append(pltpu.make_async_copy(blocks_ref.at[:, :, r], target, block_sems.at[r]))
     cuts = sorted(set([0] + list(range(width % 256, width + 1, 256))))
     copies = []
     for i, (start, end) in enumerate(zip(cuts, cuts[1:])):
@@ -268,39 +234,29 @@
             out[r, :, start:end] = jnp.where(live, total, 0.0).astype(BF16)
 
 
-def analyse(blocks, table, state, wave, me, token, slot, low, width):
-    chips, _, rows, lats, members = blocks[0].shape
+def analyse(blocks, table, state, wave, token, slot, low, width):
+    chips, cores, rows, lats, members = blocks.shape
     nlat = table.shape[2]
-    cores = CORES
     if lats % 16:
-        if len(blocks) > 1:
-            core = me[0] % CORES
-            own = lax.dynamic_index_in_dim(blocks[0], core, 1, keepdims=False)
-            pairs = [jnp.where(core == 0, own, blocks[1]), jnp.where(core == 0, blocks[1], own)]
-            blocks = [jnp.stack(pairs, axis=1)]
-        laid = jnp.transpose(blocks[0], (2, 0, 1, 3, 4)).reshape(1, 1, rows, nlat, members)
-        blocks, chips, cores, lats = [laid], 1, 1, nlat
+        blocks = jnp.transpose(blocks, (2, 0, 1, 3, 4)).reshape(1, 1, rows, nlat, members)
+        chips, cores, lats = 1, 1, nlat
     return call(
         functools.partial(analyse_kernel, slot, low),
         "analyse",
         2 * width * nlat * rows * members,
         2 * width * nlat,
         out_shape=jax.ShapeDtypeStruct((rows, members, width), BF16),
-        grid_spec=pltpu.PrefetchScalarGridSpec(
-            num_scalar_prefetch=1,
-            grid=(1,),
-            in_specs=[IN_SMEM, ANYWHERE] + [IN_HBM] * (2 + len(blocks)),
-            out_specs=pl.BlockSpec((rows, members, width), lambda i, m: (0, 0, 0)),
-            scratch_shapes=[
-                pltpu.VMEM((chips, cores, lats, rows * members), BF16),
-                pltpu.VMEM((width, nlat), BF16),
-                pltpu.VMEM((rows, members, width), BF16),
-                pltpu.SemaphoreType.DMA((width // 256 + 1,)),
-                pltpu.SemaphoreType.DMA,
-                pltpu.SemaphoreType.DMA((CORES, rows)),
-            ],
-        ),
-    )(me, wave, token, table, state, *blocks)
+        in_specs=[IN_SMEM, ANYWHERE] + [IN_HBM] * 3,
+        out_specs=pl.BlockSpec((rows, members, width), lambda: (0, 0, 0)),
+        scratch_shapes=[
+            pltpu.VMEM((chips, cores, lats, rows * members), BF16),
+            pltpu.VMEM((width, nlat), BF16),
+            pltpu.VMEM((rows, members, width), BF16),
+            pltpu.SemaphoreType.DMA((width // 256 + 1,)),
+            pltpu.SemaphoreType.DMA,
+            pltpu.SemaphoreType.DMA((rows,)),
+        ],
+    )(wave, token, table, state, blocks)
 
 
 def sum_pairs_kernel(coeff_ref, token_ref, inverse_ref, out_ref):
@@ -452,7 +408,7 @@
     each = out_sems.shape[1]
     size = lats // each
     depth, breadth = math.gcd(size, 16), 16
-    copies = []
+    copies, whole = [], {}
     for r in range(rows):
         copies.append([])
         used = 0
@@ -460,10 +416,11 @@
             refs = ins[used : used + count]
             used += count
             if count == 1:
-                target = held.at[slot, :, :, r]
-                copies[r].append(pltpu.make_async_copy(refs[0].at[:, :, r], target, in_sems.at[r, slot, 0]))
+                whole[slot] = refs[0]
                 continue
-            for i, (k, ref) in enumerate(zip(partners(count), refs)):
+            if r == 0:
+                held[slot, chip] = refs[0][...]
+            for i, (k, ref) in list(enumerate(zip(partners(count), refs)))[1:]:
                 target = held.at[slot, chip ^ k, :, r]
                 copies[r].append(pltpu.make_async_copy(ref.at[:, r], target, in_sems.at[r, slot, i]))
         for copy in copies[r]:
@@ -479,7 +436,10 @@
                 halves = []
                 for h in (0, breadth):
                     columns = [divmod(i, local_slots) for i in range(s + h, s + h + breadth)]
-                    columns = [held[slot, owner // CORES, owner % CORES, r, j, :] for owner, slot in columns]
+                    columns = [
+                        whole.get(slot, held.at[slot])[owner // CORES, owner % CORES, r, j, :]
+                        for owner, slot in columns
+                    ]
                     halves.append(jnp.concatenate(columns, axis=0))
                 turned = jnp.dot(matrix, jnp.concatenate(halves, axis=1), preferred_element_type=F32).astype(BF16)
                 for h in range(2):
@@ -505,7 +465,8 @@
         2 * 256 * rows * lats * slots * members,
         4 * rows * lats * slots * members,
         out_shape=jax.ShapeDtypeStruct((rows, lats, slots, members), BF16),
-        in_specs=[IN_SMEM] + [IN_HBM] * len(flat),
+        in_specs=[IN_SMEM]
+        + [IN_VMEM if i == 0 else IN_HBM for p in pieces for i in range(len(p))],
         out_specs=IN_HBM,
         scratch_shapes=[
             pltpu.VMEM((len(pieces), chips, CORES, rows, lats, members), BF16),
@@ -526,6 +487,11 @@
     for k, message in list(zip(partners(len(messages)), messages))[1:]:
         got.append(lax.ppermute(message, "wave", [(d, d ^ (k * CORES)) for d in range(owners)]))
     return got
+
+
+def between_all(blocks):
+    flat = blocks.reshape((-1,) + blocks.shape[2:])
+    return lax.all_to_all(flat, "wave", split_axis=0, concat_axis=0, tiled=True).reshape(blocks.shape)
 
 
 def between_chips(blocks, owners):
@@ -548,7 +514,7 @@
         early = slot == order[0]
         *blocks, token = weigh(tendency, gauss_weights[None], me, slot, local_slots, not early, waits)
         if early:
-            received[slot] = between_chips(blocks[0], owners)
+            received[slot] = between_all(blocks[0])
             here = sum_pairs(block_inverses, pole_coeffs, token)
             there = lax.ppermute(here, "pole", [(0, 1), (1, 0)])
             waits = [there]
@@ -560,10 +526,7 @@
     for slot in order:
         half = nspec // 2
         lows = [half] if slot % 2 else [0, half]
-        blocks = [received[slot]]
-        if slot == order[0]:
-            blocks.append(between_cores(pick(blocks[0], me, token), owners))
-        forced = [analyse(blocks, legendre, spectral_state, wavenumbers, me, token, slot, low, half) for low in lows]
+        forced = [analyse(received[slot], legendre, spectral_state, wavenumbers, token, slot, low, half) for low in lows]
         others = [lax.ppermute(part, "pole", [(0, 1), (1, 0)]) for part in forced]
         last = slot == order[-1]
         own = []

time: 206 us -> 208 us (level)
  local copies, waits for them, and re-layouts: 11.2 us -> 18.3 us
  starting transfers between devices: 42.4 us -> 38.4 us
    all_to_all x3 -> x2, waiting for transfers between devices: 51.2 us -> 13.8 us  [between_chips(): lax.all_to_all(blocks, 'wave', split_axis=0, concat_axis=0, axis_index_gr...]
    all_to_all x0 -> x1, waiting for transfers between devices: none -> 20.6 us  [between_all(): lax.all_to_all(flat, 'wave', split_axis=0, concat_axis=0, tiled=True)]
    ppermute x7, waiting for transfers between devices: 13 us -> 31.3 us  [by_permutes(): lax.ppermute(message, 'wave', [(d, d ^ k * CORES) for d in range(owners)])]
    unnamed x27 -> x43, local copies, waits for them, and re-layouts: 11.2 us -> 18.3 us
    all_to_all x3 -> x2, starting transfers between devices: 19.1 us -> 12.7 us  [between_chips(): lax.all_to_all(blocks, 'wave', split_axis=0, concat_axis=0, axis_index_gr...]
    all_to_all x0 -> x1, starting transfers between devices: none -> 6.28 us  [between_all(): lax.all_to_all(flat, 'wave', split_axis=0, concat_axis=0, tiled=True)]
    ppermute x7, starting transfers between devices: 17.8 us -> 14 us  [by_permutes(): lax.ppermute(message, 'wave', [(d, d ^ k * CORES) for d in range(owners)])]
    ppermute x4 -> x3, waiting for transfers between devices: 10.4 us -> 7.87 us  [between_cores(): return lax.ppermute(blocks, 'wave', [(d, d ^ 1) for d in range(owners)])]
  transfers between devices with their start and end apart: 18 -> 17, of which waited for: 15 -> 13; matrix products, arithmetic and copies ran while one was open for 0% -> 0% of each run, Pallas kernels for 19% -> 19%
where the time goes in v15:
time: 208 us; the launch traced here: 207 us
  waiting for transfers between devices  102 us (49%)
  Pallas kernels  47.8 us (23%)
  starting transfers between devices  38.4 us (18%)
  local copies, waits for them, and re-layouts  18.3 us (9%)
    ppermute x7, waiting for transfers between devices, by_permutes(): lax.ppermute(message, 'wave', [(d, d ^ k * CORES) for d in range(owners)])  31.3 us
    ppermute x3, waiting for transfers between devices, per_device(): others = [lax.ppermute(part, 'pole', [(0, 1), (1, 0)]) for part in forced]  22.9 us
    all_to_all x1, waiting for transfers between devices, between_all(): lax.all_to_all(flat, 'wave', split_axis=0, concat_axis=0, tiled=True)  20.6 us
    unnamed x43, local copies, waits for them, and re-layouts  18.3 us
    pallas_call x3, Pallas kernels, synthesise(): call(functools.partial(synthesise_kernel, slot, low, apart, more, len(par...  16.2 us
    ppermute x7, starting transfers between devices, by_permutes(): lax.ppermute(message, 'wave', [(d, d ^ k * CORES) for d in range(owners)])  14 us
    pallas_call x3, Pallas kernels, analyse(): call(functools.partial(analyse_kernel, slot, low), 'analyse', 2 * width *...  13.9 us
    all_to_all x2, waiting for transfers between devices, between_chips(): lax.all_to_all(blocks, 'wave', split_axis=0, concat_axis=0, axis_index_gr...  13.8 us
  transfers between devices with their start and end apart: 17, of which 13 were waited for; matrix products, arithmetic and copies ran while one was open for 0% of the time, Pallas kernels for 19%

profile of v15, /device:TPU:8, one launch (start us, length us, event | category | flops | bytes accessed | tf_op | source)
XLA Modules:
  0.0 206.6 jit_solution(11138301455826851787)
XLA Ops:
  0.0 4.9 %weigh.2 = (bf16[8,2,3,160,128]{4,3,2,1,0:T(8,128)(2,1)}, f32[8,128]{1,0:T(8,128)}) custom-call(s32[1]{0:T(128)} %bitcast.me_ref, f32[1,160]{1,0:T(1,128)} %bitcast.7, bf16[3,160,32,128]{3,2,1,0:T(8,128)(2,1)} %tendency_ref.3), custom_call_target="tpu_custom_call" | custom-call | flops 503316480 | bytes 5898240 | tf_op jit(solution)/shard_map/weigh/pallas_call | solution.py:138
  4.9 0.0 copy-start.20
  4.9 6.3 %all-to-all-start = ((bf16[16,3,160,128]{3,2,1,0:T(8,128)(2,1)}), bf16[16,3,160,128]{3,2,1,0:T(8,128)(2,1)S(1)}, u32[]{:S(2)}, u32[]{:S(2)}) async-start(bf16[16,3,160,128]{3,2,1,0:T(8,128)(2,1)} %bitcast.6), calls=%async_computation | async-start | bytes 3932160 | tf_op jit(solution)/shard_map/all_to_all | solution.py:494
  11.2 0.1 copy.18.coeff_ref
  11.3 1.8 copy-done.11
  13.1 2.4 %sum_pairs.1.here_ref = f32[18,2,1280]{2,1,0:T(2,128)S(1)} custom-call(f32[32,2]{1,0:T(8,128)S(1)} %copy.18.coeff_ref, f32[8,128]{1,0:T(8,128)S(1)} %copy-done.19, bf16[32,18,2,1280]{3,2,1,0:T(2,128)(2,1)S(1)} %copy-done.11), custom_call_target="tpu_custom_call" | custom-call | flops 5898240 | bytes 2949120 | tf_op jit(solution)/shard_map/sum_pairs/pallas_call | solution.py:281
  15.5 1.6 collective-permute-start
  17.1 5.2 %collective-permute-done.rest_0_.there_ref = f32[18,2,1280]{2,1,0:T(2,128)S(1)} collective-permute-done((f32[18,2,1280]{2,1,0:T(2,128)S(1)}, f32[18,2,1280]{2,1,0:T(2,128)S(1)}, u32[]{:S(2)}, u32[]{:S(2)}) %collective-permute-start) | collective-permute-done | bytes 184352 | tf_op jit(solution)/shard_map/ppermute | solution.py:519
  22.2 0.7 copy-done.9
  22.9 4.9 %weigh.3 = (bf16[8,2,3,160,128]{4,3,2,1,0:T(8,128)(2,1)}, bf16[8,3,160,128]{3,2,1,0:T(8,128)(2,1)}, f32[8,128]{1,0:T(8,128)}) custom-call(s32[1]{0:T(128)} %bitcast.me_ref, f32[1,160]{1,0:T(1,128)} %bitcast.8, bf16[3,160,32,128]{3,2,1,0:T(8,128)(2,1)} %tendency_ref.3, f32[18,2,1280]{2,1,0:T(2,128)} %copy-done.9), custom_call_target="tpu_custom_call" | custom-call | flops 503316480 | bytes 5898240 | tf_op jit(solution)/shard_map/weigh/pallas_call | solution.py:138
  27.8 0.1 collective-permute-start.1
  27.9 2.8 %collective-permute-done.1.mate_ref = bf16[8,3,160,128]{3,2,1,0:T(8,128)(2,1)S(1)} collective-permute-done((bf16[8,3,160,128]{3,2,1,0:T(8,128)(2,1)}, bf16[8,3,160,128]{3,2,1,0:T(8,128)(2,1)S(1)}, u32[]{:S(2)}, u32[]{:S(2)}) %collective-permute-start.1) | collective-permute-done | bytes 983072 | tf_op jit(solution)/shard_map/ppermute | solution.py:481
  30.7 1.5 copy-done.5
  32.2 0.1 pair.4
  32.3 1.3 copy-done.6
  33.6 20.6 %all-to-all-done = bf16[16,3,160,128]{3,2,1,0:T(8,128)(2,1)S(1)} async-done(((bf16[16,3,160,128]{3,2,1,0:T(8,128)(2,1)}), bf16[16,3,160,128]{3,2,1,0:T(8,128)(2,1)S(1)}, u32[]{:S(2)}, u32[]{:S(2)}) %all-to-all-start) | async-done | bytes 1966112 | tf_op jit(solution)/shard_map/all_to_all | solution.py:494
  54.3 1.3 copy-done.7
  55.5 6.6 %all-to-all-start.1 = ((bf16[8,2,3,160,128]{4,3,2,1,0:T(8,128)(2,1)}), bf16[8,2,3,160,128]{4,3,2,1,0:T(8,128)(2,1)S(1)}, u32[]{:S(2)}, u32[]{:S(2)}) async-start(bf16[8,2,3,160,128]{4,3,2,1,0:T(8,128)(2,1)} %copy-done.6), calls=%async_computation.1 | async-start | bytes 3932160 | tf_op jit(solution)/shard_map/all_to_all | solution.py:499
  62.1 1.5 copy-done.2
  63.7 1.5 copy-done.8
  65.2 4.6 %analyse.3.own_ref = bf16[3,128,640]{2,1,0:T(8,128)(2,1)S(1)} custom-call(s32[2]{0:T(128)S(1)} %copy-done.18, f32[8,128]{1,0:T(8,128)S(1)} %get-tuple-element.35.token_ref, bf16[2,1280,2560]{2,1,0:T(8,128)(2,1)} %table_ref.11, bf16[3,2,128,1280]{3,2,1,0:T(8,128)(2,1)S(1)} %copy-done.2, bf16[8,2,3,160,128]{4,3,2,1,0:T(8,128)(2,1)S(1)} %bitcast.5), custom_call_target="tpu_custom_call" | custom-call | flops 1258291200 | bytes 3276800 | tf_op jit(solution)/shard_map/analyse/pallas_call | solution.py:243
  69.8 1.6 collective-permute-start.2
  71.4 11.4 %collective-permute-done.2.other_ref = bf16[3,128,640]{2,1,0:T(8,128)(2,1)S(1)} collective-permute-done((bf16[3,128,640]{2,1,0:T(8,128)(2,1)S(1)}, bf16[3,128,640]{2,1,0:T(8,128)(2,1)S(1)}, u32[]{:S(2)}, u32[]{:S(2)}) %collective-permute-start.2) | collective-permute-done | bytes 491552 | tf_op jit(solution)/shard_map/ppermute | solution.py:530
  82.8 4.9 %synthesise.3 = (bf16[8,2,3,160,128]{4,3,2,1,0:T(8,128)(2,1)S(1)}, bf16[8,3,160,128]{3,2,1,0:T(8,128)(2,1)S(1)}) custom-call(s32[1]{0:T(128)} %bitcast.me_ref, f32[1]{0:T(128)} %bitcast.1.sign_ref, f32[18,2,1280]{2,1,0:T(2,128)S(1)} %sum_pairs.1.here_ref, f32[18,2,1280]{2,1,0:T(2,128)S(1)} %copy-done.10, bf16[3,128,640]{2,1,0:T(8,128)(2,1)S(1)} %analyse.3.own_ref, ...), custom_call_target="tpu_custom_call" | custom-call | flops 1258291200 | bytes 3276800 | tf_op jit(solution)/shard_map/synthesise/pallas_call | solution.py:379
  87.7 0.1 collective-permute-start.3
  87.8 2.6 %collective-permute-done.3.mate_ref = bf16[8,3,160,128]{3,2,1,0:T(8,128)(2,1)S(1)} collective-permute-done((bf16[8,3,160,128]{3,2,1,0:T(8,128)(2,1)S(1)}, bf16[8,3,160,128]{3,2,1,0:T(8,128)(2,1)S(1)}, u32[]{:S(2)}, u32[]{:S(2)}) %collective-permute-start.3) | collective-permute-done | bytes 983072 | tf_op jit(solution)/shard_map/ppermute | solution.py:481
  90.4 0.1 pair.5
  90.5 1.3 copy-done.4
  91.8 13.8 %all-to-all-done.1.blocks_ref = bf16[8,2,3,160,128]{4,3,2,1,0:T(8,128)(2,1)S(1)} async-done(((bf16[8,2,3,160,128]{4,3,2,1,0:T(8,128)(2,1)}), bf16[8,2,3,160,128]{4,3,2,1,0:T(8,128)(2,1)S(1)}, u32[]{:S(2)}, u32[]{:S(2)}) %all-to-all-start.1) | async-done | bytes 1966112 | tf_op jit(solution)/shard_map/all_to_all | solution.py:499
  105.5 1.3 copy-done
  106.8 6.1 %all-to-all-start.2 = ((bf16[8,2,3,160,128]{4,3,2,1,0:T(8,128)(2,1)}), bf16[8,2,3,160,128]{4,3,2,1,0:T(8,128)(2,1)S(1)}, u32[]{:S(2)}, u32[]{:S(2)}) async-start(bf16[8,2,3,160,128]{4,3,2,1,0:T(8,128)(2,1)} %copy-done.4), calls=%async_computation.2 | async-start | bytes 3932160 | tf_op jit(solution)/shard_map/all_to_all | solution.py:499
  112.9 1.5 copy-done.1
  114.5 1.5 copy-done.3
  116.0 4.6 %analyse.5.own_ref = bf16[3,128,640]{2,1,0:T(8,128)(2,1)S(1)} custom-call(s32[2]{0:T(128)S(1)} %copy-done.18, f32[8,128]{1,0:T(8,128)S(1)} %get-tuple-element.39.token_ref, bf16[2,1280,2560]{2,1,0:T(8,128)(2,1)} %table_ref.11, bf16[3,2,128,1280]{3,2,1,0:T(8,128)(2,1)S(1)} %copy-done.3, bf16[8,2,3,160,128]{4,3,2,1,0:T(8,128)(2,1)S(1)} %copy-done.1), custom_call_target="tpu_custom_call" | custom-call | flops 1258291200 | bytes 3276800 | tf_op jit(solution)/shard_map/analyse/pallas_call | solution.py:243
  120.6 1.6 collective-permute-start.5
  122.2 4.6 %analyse.4.own_ref = bf16[3,128,640]{2,1,0:T(8,128)(2,1)S(1)} custom-call(s32[2]{0:T(128)S(1)} %copy-done.18, f32[8,128]{1,0:T(8,128)S(1)} %get-tuple-element.39.token_ref, bf16[2,1280,2560]{2,1,0:T(8,128)(2,1)} %table_ref.11, bf16[3,2,128,1280]{3,2,1,0:T(8,128)(2,1)S(1)} %copy-done.3, bf16[8,2,3,160,128]{4,3,2,1,0:T(8,128)(2,1)S(1)} %copy-done.1), custom_call_target="tpu_custom_call" | custom-call | flops 1258291200 | bytes 3276800 | tf_op jit(solution)/shard_map/analyse/pallas_call | solution.py:243
  126.8 0.6 collective-permute-start.4
  127.4 7.4 %collective-permute-done.5.other_ref = bf16[3,128,640]{2,1,0:T(8,128)(2,1)S(1)} collective-permute-done((bf16[3,128,640]{2,1,0:T(8,128)(2,1)S(1)}, bf16[3,128,640]{2,1,0:T(8,128)(2,1)S(1)}, u32[]{:S(2)}, u32[]{:S(2)}) %collective-permute-start.5) | collective-permute-done | bytes 491552 | tf_op jit(solution)/shard_map/ppermute | solution.py:530
  134.9 4.8 %synthesise.4.rest_0_ = f32[384,2560]{1,0:T(8,128)S(1)} custom-call(s32[1]{0:T(128)} %bitcast.me_ref, f32[1]{0:T(128)} %bitcast.1.sign_ref, f32[18,2,1280]{2,1,0:T(2,128)S(1)} %sum_pairs.1.here_ref, f32[18,2,1280]{2,1,0:T(2,128)S(1)} %copy-done.10, bf16[3,128,640]{2,1,0:T(8,128)(2,1)S(1)} %analyse.5.own_ref, ...), custom_call_target="tpu_custom_call" | custom-call | flops 1258291200 | bytes 3276800 | tf_op jit(solution)/shard_map/synthesise/pallas_call | solution.py:379
  139.7 4.1 %collective-permute-done.4.other_ref = bf16[3,128,640]{2,1,0:T(8,128)(2,1)S(1)} collective-permute-done((bf16[3,128,640]{2,1,0:T(8,128)(2,1)S(1)}, bf16[3,128,640]{2,1,0:T(8,128)(2,1)S(1)}, u32[]{:S(2)}, u32[]{:S(2)}) %collective-permute-start.4) | collective-permute-done | bytes 491552 | tf_op jit(solution)/shard_map/ppermute | solution.py:530
  143.8 6.4 %synthesise.5 = (bf16[2,3,160,128]{3,2,1,0:T(8,128)(2,1)S(1)}, bf16[2,3,160,128]{3,2,1,0:T(8,128)(2,1)}, bf16[2,3,160,128]{3,2,1,0:T(8,128)(2,1)}, bf16[2,3,160,...) custom-call(s32[1]{0:T(128)} %bitcast.me_ref, ...), custom_call_target="tpu_custom_call" | custom-call | flops 1258291200 | bytes 3276800 | tf_op jit(solution)/shard_map/synthesise/pallas_call | solution.py:379
  150.2 0.1 collective-permute-start.6
  150.3 2.6 %collective-permute-done.6.mate_ref = bf16[8,3,160,128]{3,2,1,0:T(8,128)(2,1)S(1)} collective-permute-done((bf16[8,3,160,128]{3,2,1,0:T(8,128)(2,1)S(1)}, bf16[8,3,160,128]{3,2,1,0:T(8,128)(2,1)S(1)}, u32[]{:S(2)}, u32[]{:S(2)}) %collective-permute-start.6) | collective-permute-done | bytes 983072 | tf_op jit(solution)/shard_map/ppermute | solution.py:481
  152.9 0.9 pair.6
  153.8 1.8 collective-permute-start.7
  155.6 2.1 %collective-permute-start.8 = (bf16[2,3,160,128]{3,2,1,0:T(8,128)(2,1)}, bf16[2,3,160,128]{3,2,1,0:T(8,128)(2,1)}, u32[]{:S(2)}, u32[]{:S(2)}) collective-permute-start(bf16[2,3,160,128]{3,2,1,0:T(8,128)(2,1)} %get-tuple-element.49), channel_id=1, source_target_pairs={{0,10},{1,11},{2,8},{3,9},{4,14},{5,15},{6,12},{7,13},{8,2},{9,3},... | collective-permute-start | bytes 737288 | tf_op jit(solution)/shard_map/ppermute | solution.py:488
  157.7 0.8 collective-permute-start.9
  158.5 1.3 collective-permute-start.10
  159.8 0.0 all-to-all-done.2.rest_3_.rest_8_
  159.8 0.9 copy-done.13
  160.8 0.9 copy-done.15
  161.7 0.9 copy-done.17
  162.7 0.5 pair.7
  163.1 1.5 collective-permute-start.11
  164.7 17.9 %collective-permute-done.7.rest_1_ = bf16[2,3,160,128]{3,2,1,0:T(8,128)(2,1)S(1)} collective-permute-done((bf16[2,3,160,128]{3,2,1,0:T(8,128)(2,1)}, bf16[2,3,160,128]{3,2,1,0:T(8,128)(2,1)S(1)}, u32[]{:S(2)}, u32[]{:S(2)}) %collective-permute-start.7) | collective-permute-done | bytes 245792 | tf_op jit(solution)/shard_map/ppermute | solution.py:488
  182.6 2.7 %collective-permute-start.12 = (bf16[2,3,160,128]{3,2,1,0:T(8,128)(2,1)S(1)}, bf16[2,3,160,128]{3,2,1,0:T(8,128)(2,1)S(1)}, u32[]{:S(2)}, u32[]{:S(2)}) collective-permute-start(bf16[2,3,160,128]{3,2,1,0:T(8,128)(2,1)S(1)} %get-tuple-element.57), channel_id=1, source_target_pairs={{0,4},{1,5},{2,6},{3,7},{4,0},{5,1},{6,2},{7,3},{8,12},{9,13},{10,... | collective-permute-start | bytes 737288 | tf_op jit(solution)/shard_map/ppermute | solution.py:488
  185.3 2.6 %collective-permute-done.8.rest_2_ = bf16[2,3,160,128]{3,2,1,0:T(8,128)(2,1)} collective-permute-done((bf16[2,3,160,128]{3,2,1,0:T(8,128)(2,1)}, bf16[2,3,160,128]{3,2,1,0:T(8,128)(2,1)}, u32[]{:S(2)}, u32[]{:S(2)}) %collective-permute-start.8) | collective-permute-done | bytes 245792 | tf_op jit(solution)/shard_map/ppermute | solution.py:488
  187.9 3.7 %collective-permute-start.13 = (bf16[2,3,160,128]{3,2,1,0:T(8,128)(2,1)S(1)}, bf16[2,3,160,128]{3,2,1,0:T(8,128)(2,1)S(1)}, u32[]{:S(2)}, u32[]{:S(2)}) collective-permute-start(bf16[2,3,160,128]{3,2,1,0:T(8,128)(2,1)S(1)} %get-tuple-element.58), channel_id=1, source_target_pairs={{0,6},{1,7},{2,4},{3,5},{4,2},{5,3},{6,0},{7,1},{8,14},{9,15},{10,... | collective-permute-start | bytes 737288 | tf_op jit(solution)/shard_map/ppermute | solution.py:488
  191.6 2.9 %collective-permute-done.9.rest_3_ = bf16[2,3,160,128]{3,2,1,0:T(8,128)(2,1)} collective-permute-done((bf16[2,3,160,128]{3,2,1,0:T(8,128)(2,1)}, bf16[2,3,160,128]{3,2,1,0:T(8,128)(2,1)}, u32[]{:S(2)}, u32[]{:S(2)}) %collective-permute-start.9) | collective-permute-done | bytes 245792 | tf_op jit(solution)/shard_map/ppermute | solution.py:488
  194.5 7.8 %collective-permute-done.10.rest_4_ = bf16[2,3,160,128]{3,2,1,0:T(8,128)(2,1)} collective-permute-done((bf16[2,3,160,128]{3,2,1,0:T(8,128)(2,1)}, bf16[2,3,160,128]{3,2,1,0:T(8,128)(2,1)}, u32[]{:S(2)}, u32[]{:S(2)}) %collective-permute-start.10) | collective-permute-done | bytes 245792 | tf_op jit(solution)/shard_map/ppermute | solution.py:488
  202.4 0.0 collective-permute-done.11.rest_5_
  202.4 0.0 collective-permute-done.12.rest_6_
  202.4 0.0 collective-permute-done.13.rest_7_
  202.4 4.0 %assemble.1 = bf16[3,160,32,128]{3,2,1,0:T(8,128)(2,1)} custom-call(s32[1]{0:T(128)} %bitcast.me_ref, bf16[2,3,160,128]{3,2,1,0:T(8,128)(2,1)S(1)} %get-tuple-element.47.rest_0_, bf16[2,3,160,128]{3,2,1,0:T(8,128)(2,1)S(1)} %collective-permute-done.7.rest_1_, bf16[2,3,160,128]{3,2,1,0:T(8,128)(2,1)} %collective-permute-done.8.rest_2_, ...), custom_call_target="tpu_custom_call" | custom-call | flops 1006632960 | bytes 7864320 | tf_op jit(solution)/shard_map/assemble/pallas_call | solution.py:462
  (27 shorter events, 0.0 us)
Async XLA Ops:
  4.9 6.3 %copy-start.20 = (f32[32,2]{0,1:T(2,128)S(1)}, f32[32,2]{0,1:T(2,128)}, u32[]{:S(2)}) copy-start(f32[32,2]{0,1:T(2,128)} %param.12) | copy-start | bytes 772
  4.9 6.4 %copy-start.19 = (f32[8,128]{1,0:T(8,128)S(1)}, f32[8,128]{1,0:T(8,128)}, u32[]{:S(2)}) copy-start(f32[8,128]{1,0:T(8,128)} %get-tuple-element.32.token_ref) | copy-start | bytes 12292
  4.9 49.4 %all-to-all-start = ((bf16[16,3,160,128]{3,2,1,0:T(8,128)(2,1)}), bf16[16,3,160,128]{3,2,1,0:T(8,128)(2,1)S(1)}, u32[]{:S(2)}, u32[]{:S(2)}) async-start(bf16[16,3,160,128]{3,2,1,0:T(8,128)(2,1)} %bitcast.6), calls=%async_computation | async-start | bytes 3932160 | tf_op jit(solution)/shard_map/all_to_all | solution.py:494
  11.3 1.8 copy-start.11
  15.5 6.8 %collective-permute-start = (f32[18,2,1280]{2,1,0:T(2,128)S(1)}, f32[18,2,1280]{2,1,0:T(2,128)S(1)}, u32[]{:S(2)}, u32[]{:S(2)}) collective-permute-start(f32[18,2,1280]{2,1,0:T(2,128)S(1)} %sum_pairs.1.here_ref), channel_id=1, source_target_pairs={{0,16},{16,0},{1,17},{17,1},{2,18},{18,2},{3,19},{19,3},{4,20},{20... | collective-permute-start | bytes 552968 | tf_op jit(solution)/shard_map/ppermute | solution.py:519
  22.2 0.7 copy-start.9
  27.8 2.8 %collective-permute-start.1 = (bf16[8,3,160,128]{3,2,1,0:T(8,128)(2,1)}, bf16[8,3,160,128]{3,2,1,0:T(8,128)(2,1)S(1)}, u32[]{:S(2)}, u32[]{:S(2)}) collective-permute-start(bf16[8,3,160,128]{3,2,1,0:T(8,128)(2,1)} %get-tuple-element.33), channel_id=1, source_target_pairs={{0,1},{1,0},{2,3},{3,2},{4,5},{5,4},{6,7},{7,6},{8,9},{9,8},{10,11... | collective-permute-start | bytes 2949128 | tf_op jit(solution)/shard_map/ppermute | solution.py:481
  30.7 1.5 copy-start.5
  32.3 1.3 copy-start.6
  54.3 1.3 copy-start.7
  55.5 6.6 %copy-start.18 = (s32[2]{0:T(128)S(1)}, s32[2]{0:T(128)}, u32[]{:S(2)}) copy-start(s32[2]{0:T(128)} %wave_ref.5) | copy-start | bytes 28
  55.5 50.0 %all-to-all-start.1 = ((bf16[8,2,3,160,128]{4,3,2,1,0:T(8,128)(2,1)}), bf16[8,2,3,160,128]{4,3,2,1,0:T(8,128)(2,1)S(1)}, u32[]{:S(2)}, u32[]{:S(2)}) async-start(bf16[8,2,3,160,128]{4,3,2,1,0:T(8,128)(2,1)} %copy-done.6), calls=%async_computation.1 | async-start | bytes 3932160 | tf_op jit(solution)/shard_map/all_to_all | solution.py:499
  62.1 1.5 copy-start.2
  63.6 1.5 copy-start.8
  65.2 17.6 %copy-start.10 = (f32[18,2,1280]{2,1,0:T(2,128)S(1)}, f32[18,2,1280]{2,1,0:T(2,128)}, u32[]{:S(2)}) copy-start(f32[18,2,1280]{2,1,0:T(2,128)} %copy-done.9) | copy-start | bytes 552964
  69.8 12.9 %collective-permute-start.2 = (bf16[3,128,640]{2,1,0:T(8,128)(2,1)S(1)}, bf16[3,128,640]{2,1,0:T(8,128)(2,1)S(1)}, u32[]{:S(2)}, u32[]{:S(2)}) collective-permute-start(bf16[3,128,640]{2,1,0:T(8,128)(2,1)S(1)} %analyse.3.own_ref), channel_id=1, source_target_pairs={{0,16},{16,0},{1,17},{17,1},{2,18},{18,2},{3,19},{19,3},{4,20},{20... | collective-permute-start | bytes 1474568 | tf_op jit(solution)/shard_map/ppermute | solution.py:530
  87.7 2.6 %collective-permute-start.3 = (bf16[8,3,160,128]{3,2,1,0:T(8,128)(2,1)S(1)}, bf16[8,3,160,128]{3,2,1,0:T(8,128)(2,1)S(1)}, u32[]{:S(2)}, u32[]{:S(2)}) collective-permute-start(bf16[8,3,160,128]{3,2,1,0:T(8,128)(2,1)S(1)} %get-tuple-element.37), channel_id=1, source_target_pairs={{0,1},{1,0},{2,3},{3,2},{4,5},{5,4},{6,7},{7,6},{8,9},{9,8},{10,11... | collective-permute-start | bytes 2949128 | tf_op jit(solution)/shard_map/ppermute | solution.py:481
  90.5 1.3 copy-start.4
  105.5 1.3 copy-start
  106.8 53.0 %all-to-all-start.2 = ((bf16[8,2,3,160,128]{4,3,2,1,0:T(8,128)(2,1)}), bf16[8,2,3,160,128]{4,3,2,1,0:T(8,128)(2,1)S(1)}, u32[]{:S(2)}, u32[]{:S(2)}) async-start(bf16[8,2,3,160,128]{4,3,2,1,0:T(8,128)(2,1)} %copy-done.4), calls=%async_computation.2 | async-start | bytes 3932160 | tf_op jit(solution)/shard_map/all_to_all | solution.py:499
  112.9 1.5 copy-start.1
  114.5 1.5 copy-start.3
  120.6 14.2 %collective-permute-start.5 = (bf16[3,128,640]{2,1,0:T(8,128)(2,1)S(1)}, bf16[3,128,640]{2,1,0:T(8,128)(2,1)S(1)}, u32[]{:S(2)}, u32[]{:S(2)}) collective-permute-start(bf16[3,128,640]{2,1,0:T(8,128)(2,1)S(1)} %analyse.5.own_ref), channel_id=1, source_target_pairs={{0,16},{16,0},{1,17},{17,1},{2,18},{18,2},{3,19},{19,3},{4,20},{20... | collective-permute-start | bytes 1474568 | tf_op jit(solution)/shard_map/ppermute | solution.py:530
  126.8 17.0 %collective-permute-start.4 = (bf16[3,128,640]{2,1,0:T(8,128)(2,1)S(1)}, bf16[3,128,640]{2,1,0:T(8,128)(2,1)S(1)}, u32[]{:S(2)}, u32[]{:S(2)}) collective-permute-start(bf16[3,128,640]{2,1,0:T(8,128)(2,1)S(1)} %analyse.4.own_ref), channel_id=1, source_target_pairs={{0,16},{16,0},{1,17},{17,1},{2,18},{18,2},{3,19},{19,3},{4,20},{20... | collective-permute-start | bytes 1474568 | tf_op jit(solution)/shard_map/ppermute | solution.py:530
  150.2 8.3 %copy-start.12 = (bf16[2,3,160,128]{3,2,1,0:T(8,128)(2,1)}, bf16[2,3,160,128]{3,2,1,0:T(8,128)(2,1)S(1)}, u32[]{:S(2)}) copy-start(bf16[2,3,160,128]{3,2,1,0:T(8,128)(2,1)S(1)} %get-tuple-element.52.rest_0_) | copy-start | bytes 737284
  150.2 8.3 %copy-start.14 = (bf16[2,3,160,128]{3,2,1,0:T(8,128)(2,1)}, bf16[2,3,160,128]{3,2,1,0:T(8,128)(2,1)S(1)}, u32[]{:S(2)}) copy-start(bf16[2,3,160,128]{3,2,1,0:T(8,128)(2,1)S(1)} %get-tuple-element.53.rest_1_) | copy-start | bytes 737284
  150.2 8.3 %copy-start.16 = (bf16[2,3,160,128]{3,2,1,0:T(8,128)(2,1)}, bf16[2,3,160,128]{3,2,1,0:T(8,128)(2,1)S(1)}, u32[]{:S(2)}) copy-start(bf16[2,3,160,128]{3,2,1,0:T(8,128)(2,1)S(1)} %get-tuple-element.54.rest_2_) | copy-start | bytes 737284
  150.2 2.6 %collective-permute-start.6 = (bf16[8,3,160,128]{3,2,1,0:T(8,128)(2,1)S(1)}, bf16[8,3,160,128]{3,2,1,0:T(8,128)(2,1)S(1)}, u32[]{:S(2)}, u32[]{:S(2)}) collective-permute-start(bf16[8,3,160,128]{3,2,1,0:T(8,128)(2,1)S(1)} %get-tuple-element.41), channel_id=1, source_target_pairs={{0,1},{1,0},{2,3},{3,2},{4,5},{5,4},{6,7},{7,6},{8,9},{9,8},{10,11... | collective-permute-start | bytes 2949128 | tf_op jit(solution)/shard_map/ppermute | solution.py:481
  153.8 28.8 %collective-permute-start.7 = (bf16[2,3,160,128]{3,2,1,0:T(8,128)(2,1)}, bf16[2,3,160,128]{3,2,1,0:T(8,128)(2,1)S(1)}, u32[]{:S(2)}, u32[]{:S(2)}) collective-permute-start(bf16[2,3,160,128]{3,2,1,0:T(8,128)(2,1)} %get-tuple-element.48), channel_id=1, source_target_pairs={{0,8},{1,9},{2,10},{3,11},{4,12},{5,13},{6,14},{7,15},{8,0},{9,1},... | collective-permute-start | bytes 737288 | tf_op jit(solution)/shard_map/ppermute | solution.py:488
  155.6 32.3 %collective-permute-start.8 = (bf16[2,3,160,128]{3,2,1,0:T(8,128)(2,1)}, bf16[2,3,160,128]{3,2,1,0:T(8,128)(2,1)}, u32[]{:S(2)}, u32[]{:S(2)}) collective-permute-start(bf16[2,3,160,128]{3,2,1,0:T(8,128)(2,1)} %get-tuple-element.49), channel_id=1, source_target_pairs={{0,10},{1,11},{2,8},{3,9},{4,14},{5,15},{6,12},{7,13},{8,2},{9,3},... | collective-permute-start | bytes 737288 | tf_op jit(solution)/shard_map/ppermute | solution.py:488
  157.7 36.8 %collective-permute-start.9 = (bf16[2,3,160,128]{3,2,1,0:T(8,128)(2,1)}, bf16[2,3,160,128]{3,2,1,0:T(8,128)(2,1)}, u32[]{:S(2)}, u32[]{:S(2)}) collective-permute-start(bf16[2,3,160,128]{3,2,1,0:T(8,128)(2,1)} %get-tuple-element.50), channel_id=1, source_target_pairs={{0,12},{1,13},{2,14},{3,15},{4,8},{5,9},{6,10},{7,11},{8,4},{9,5},... | collective-permute-start | bytes 737288 | tf_op jit(solution)/shard_map/ppermute | solution.py:488
  158.5 43.8 %collective-permute-start.10 = (bf16[2,3,160,128]{3,2,1,0:T(8,128)(2,1)}, bf16[2,3,160,128]{3,2,1,0:T(8,128)(2,1)}, u32[]{:S(2)}, u32[]{:S(2)}) collective-permute-start(bf16[2,3,160,128]{3,2,1,0:T(8,128)(2,1)} %get-tuple-element.51), channel_id=1, source_target_pairs={{0,14},{1,15},{2,12},{3,13},{4,10},{5,11},{6,8},{7,9},{8,6},{9,7},... | collective-permute-start | bytes 737288 | tf_op jit(solution)/shard_map/ppermute | solution.py:488
  159.8 0.9 copy-start.13
  160.8 0.9 copy-start.15
  161.7 0.9 copy-start.17
  163.1 39.2 %collective-permute-start.11 = (bf16[2,3,160,128]{3,2,1,0:T(8,128)(2,1)S(1)}, bf16[2,3,160,128]{3,2,1,0:T(8,128)(2,1)S(1)}, u32[]{:S(2)}, u32[]{:S(2)}) collective-permute-start(bf16[2,3,160,128]{3,2,1,0:T(8,128)(2,1)S(1)} %get-tuple-element.56), channel_id=1, source_target_pairs={{0,2},{1,3},{2,0},{3,1},{4,6},{5,7},{6,4},{7,5},{8,10},{9,11},{10,... | collective-permute-start | bytes 737288 | tf_op jit(solution)/shard_map/ppermute | solution.py:488
  182.6 19.8 %collective-permute-start.12 = (bf16[2,3,160,128]{3,2,1,0:T(8,128)(2,1)S(1)}, bf16[2,3,160,128]{3,2,1,0:T(8,128)(2,1)S(1)}, u32[]{:S(2)}, u32[]{:S(2)}) collective-permute-start(bf16[2,3,160,128]{3,2,1,0:T(8,128)(2,1)S(1)} %get-tuple-element.57), channel_id=1, source_target_pairs={{0,4},{1,5},{2,6},{3,7},{4,0},{5,1},{6,2},{7,3},{8,12},{9,13},{10,... | collective-permute-start | bytes 737288 | tf_op jit(solution)/shard_map/ppermute | solution.py:488
  187.9 14.5 %collective-permute-start.13 = (bf16[2,3,160,128]{3,2,1,0:T(8,128)(2,1)S(1)}, bf16[2,3,160,128]{3,2,1,0:T(8,128)(2,1)S(1)}, u32[]{:S(2)}, u32[]{:S(2)}) collective-permute-start(bf16[2,3,160,128]{3,2,1,0:T(8,128)(2,1)S(1)} %get-tuple-element.58), channel_id=1, source_target_pairs={{0,6},{1,7},{2,4},{3,5},{4,2},{5,3},{6,0},{7,1},{8,14},{9,15},{10,... | collective-permute-start | bytes 737288 | tf_op jit(solution)/shard_map/ppermute | solution.py:488

commit v16 on v14

--- a/solution.py
+++ b/solution.py
@@ -14,6 +14,7 @@
 ANYWHERE = pl.BlockSpec(memory_space=pl.ANY)
 IN_SMEM = pl.BlockSpec(memory_space=pltpu.SMEM)
 IN_HBM = pl.BlockSpec(memory_space=pltpu.HBM)
+IN_VMEM = pl.BlockSpec(memory_space=pltpu.VMEM)
 TOKEN = jax.ShapeDtypeStruct((8, 128), F32)
 
 
@@ -25,6 +26,10 @@
         cost_estimate=pl.CostEstimate(flops=int(flops), bytes_accessed=int(size), transcendentals=0),
         **kwargs,
     )
+
+
+def in_hbm(array):
+    return pltpu.with_memory_space_constraint(array, pltpu.HBM)
 
 
 def run_copies(copies):
@@ -107,13 +112,18 @@
                     for i, value in enumerate(values):
                         chip, target = divmod(start + i, CORES)
                         done[chip, target, r, j : j + depth, :] = value.astype(BF16)
-        if split:
-            results.append(pltpu.make_async_copy(done.at[:, 0, r], outs[0].at[:, core, r], out_sems.at[0, r]))
-            results.append(pltpu.make_async_copy(done.at[:, 1, r], outs[1].at[:, r], out_sems.at[1, r]))
-            results[-2].start()
-        else:
-            results.append(pltpu.make_async_copy(done.at[:, :, r], outs[0].at[:, :, r], out_sems.at[0, r]))
-        results[-1].start()
+            if (j + depth) % size == 0:
+                part = pl.ds(j + depth - size, size)
+                source, target = done.at[:, :, r, part], outs[0].at[:, :, r, part]
+                if split:
+                    source, target = done.at[:, 0, r, part], outs[0].at[:, core, r, part]
+                    other = pltpu.make_async_copy(
+                        done.at[:, 1, r, part], outs[1].at[:, r, part], out_sems.at[1, r, j // size]
+                    )
+                    other.start()
+                    results.append(other)
+                results.append(pltpu.make_async_copy(source, target, out_sems.at[0, r, j // size]))
+                results[-1].start()
     for copy in results:
         copy.wait()
 
@@ -145,7 +155,7 @@
             pltpu.VMEM((chips, CORES, rows, lats, members), BF16),
             pltpu.SemaphoreType.DMA,
             pltpu.SemaphoreType.DMA((rows, each)),
-            pltpu.SemaphoreType.DMA((CORES, rows)),
+            pltpu.SemaphoreType.DMA((CORES, rows, each)),
         ],
     )(me, gauss, tendency, *waits)
 
@@ -180,7 +190,7 @@
             pltpu.SemaphoreType.DMA((rows,)),
             pltpu.SemaphoreType.DMA((rows,)),
         ],
-    )(me, token, blocks)
+    )(me, token, in_hbm(blocks))
 
 
 def pair_kernel(me_ref, mate_ref, blocks_ref, out_ref, token_ref, sem):
@@ -300,7 +310,7 @@
                 pltpu.SemaphoreType.DMA((CORES, rows)),
             ],
         ),
-    )(me, wave, token, table, state, *blocks)
+    )(me, wave, token, in_hbm(table), in_hbm(state), in_hbm(blocks[0]), *blocks[1:])
 
 
 def sum_pairs_kernel(coeff_ref, token_ref, inverse_ref, out_ref):
@@ -452,7 +462,7 @@
     each = out_sems.shape[1]
     size = lats // each
     depth, breadth = math.gcd(size, 16), 16
-    copies = []
+    copies, whole = [], {}
     for r in range(rows):
         copies.append([])
         used = 0
@@ -460,10 +470,11 @@
             refs = ins[used : used + count]
             used += count
             if count == 1:
-                target = held.at[slot, :, :, r]
-                copies[r].append(pltpu.make_async_copy(refs[0].at[:, :, r], target, in_sems.at[r, slot, 0]))
+                whole[slot] = refs[0]
                 continue
-            for i, (k, ref) in enumerate(zip(partners(count), refs)):
+            if r == 0:
+                held[slot, chip] = refs[0][...]
+            for i, (k, ref) in list(enumerate(zip(partners(count), refs)))[1:]:
                 target = held.at[slot, chip ^ k, :, r]
                 copies[r].append(pltpu.make_async_copy(ref.at[:, r], target, in_sems.at[r, slot, i]))
         for copy in copies[r]:
@@ -479,7 +490,10 @@
                 halves = []
                 for h in (0, breadth):
                     columns = [divmod(i, local_slots) for i in range(s + h, s + h + breadth)]
-                    columns = [held[slot, owner // CORES, owner % CORES, r, j, :] for owner, slot in columns]
+                    columns = [
+                        whole.get(slot, held.at[slot])[owner // CORES, owner % CORES, r, j, :]
+                        for owner, slot in columns
+                    ]
                     halves.append(jnp.concatenate(columns, axis=0))
                 turned = jnp.dot(matrix, jnp.concatenate(halves, axis=1), preferred_element_type=F32).astype(BF16)
                 for h in range(2):
@@ -505,7 +519,8 @@
         2 * 256 * rows * lats * slots * members,
         4 * rows * lats * slots * members,
         out_shape=jax.ShapeDtypeStruct((rows, lats, slots, members), BF16),
-        in_specs=[IN_SMEM] + [IN_HBM] * len(flat),
+        in_specs=[IN_SMEM]
+        + [IN_VMEM if i == 0 else IN_HBM for p in pieces for i in range(len(p))],
         out_specs=IN_HBM,
         scratch_shapes=[
             pltpu.VMEM((len(pieces), chips, CORES, rows, lats, members), BF16),

time: 206 us -> 204 us (level)
  Pallas kernels: 49 us -> 52.5 us
  starting transfers between devices: 42.4 us -> 40.1 us
    pallas_call x3, Pallas kernels: 14 us -> 17.3 us  [analyse(): call(functools.partial(analyse_kernel, slot, low), 'analyse', 2 * width *...]
    ppermute x7, starting transfers between devices: 17.8 us -> 14.9 us  [by_permutes(): lax.ppermute(message, 'wave', [(d, d ^ k * CORES) for d in range(owners)])]
    unnamed x27 -> x31, local copies, waits for them, and re-layouts: 11.2 us -> 9.57 us
  transfers between devices with their start and end apart: 18 -> 18, of which waited for: 15 -> 15; matrix products, arithmetic and copies ran while one was open for 0% -> 0% of each run, Pallas kernels for 19% -> 22%
where the time goes in v16:
time: 204 us; the launch traced here: 203 us
  waiting for transfers between devices  100 us (49%)
  Pallas kernels  52.5 us (26%)
  starting transfers between devices  40.1 us (20%)
  local copies, waits for them, and re-layouts  9.57 us (5%)
    all_to_all x3, waiting for transfers between devices, between_chips(): lax.all_to_all(blocks, 'wave', split_axis=0, concat_axis=0, axis_index_gr...  51.1 us
    ppermute x3, waiting for transfers between devices, per_device(): others = [lax.ppermute(part, 'pole', [(0, 1), (1, 0)]) for part in forced]  22.1 us
    all_to_all x3, starting transfers between devices, between_chips(): lax.all_to_all(blocks, 'wave', split_axis=0, concat_axis=0, axis_index_gr...  19.6 us
    pallas_call x3, Pallas kernels, analyse(): call(functools.partial(analyse_kernel, slot, low), 'analyse', 2 * width *...  17.3 us
    pallas_call x3, Pallas kernels, synthesise(): call(functools.partial(synthesise_kernel, slot, low, apart, more, len(par...  16.2 us
    ppermute x7, starting transfers between devices, by_permutes(): lax.ppermute(message, 'wave', [(d, d ^ k * CORES) for d in range(owners)])  14.9 us
    ppermute x7, waiting for transfers between devices, by_permutes(): lax.ppermute(message, 'wave', [(d, d ^ k * CORES) for d in range(owners)])  12.4 us
    ppermute x4, waiting for transfers between devices, between_cores(): return lax.ppermute(blocks, 'wave', [(d, d ^ 1) for d in range(owners)])  10.4 us
  transfers between devices with their start and end apart: 18, of which 15 were waited for; matrix products, arithmetic and copies ran while one was open for 0% of the time, Pallas kernels for 22%

profile of v16, /device:TPU:8, one launch (start us, length us, event | category | flops | bytes accessed | tf_op | source)
XLA Modules:
  0.0 202.9 jit_solution(10194040144197397032)
XLA Ops:
  0.0 4.9 %weigh.2 = (bf16[8,2,3,160,128]{4,3,2,1,0:T(8,128)(2,1)}, f32[8,128]{1,0:T(8,128)}) custom-call(s32[1]{0:T(128)} %bitcast.me_ref, f32[1,160]{1,0:T(1,128)} %bitcast.3, bf16[3,160,32,128]{3,2,1,0:T(8,128)(2,1)} %tendency_ref.3), custom_call_target="tpu_custom_call" | custom-call | flops 503316480 | bytes 5898240 | tf_op jit(solution)/shard_map/weigh/pallas_call | solution.py:142
  4.9 0.0 copy-start.14
  4.9 0.0 copy-start.13
  4.9 6.3 %all-to-all-start = ((bf16[8,2,3,160,128]{4,3,2,1,0:T(8,128)(2,1)}), bf16[8,2,3,160,128]{4,3,2,1,0:T(8,128)(2,1)}, u32[]{:S(2)}, u32[]{:S(2)}) async-start(bf16[8,2,3,160,128]{4,3,2,1,0:T(8,128)(2,1)} %get-tuple-element.36), calls=%async_computation | async-start | bytes 3932160 | tf_op jit(solution)/shard_map/all_to_all | solution.py:548
  11.2 0.0 copy-done.14
  11.2 0.1 copy.18.coeff_ref
  11.3 1.8 copy-done.5
  13.1 2.4 %sum_pairs.1.here_ref = f32[18,2,1280]{2,1,0:T(2,128)S(1)} custom-call(f32[32,2]{1,0:T(8,128)S(1)} %copy.18.coeff_ref, f32[8,128]{1,0:T(8,128)S(1)} %copy-done.13, bf16[32,18,2,1280]{3,2,1,0:T(2,128)(2,1)S(1)} %copy-done.5), custom_call_target="tpu_custom_call" | custom-call | flops 5898240 | bytes 2949120 | tf_op jit(solution)/shard_map/sum_pairs/pallas_call | solution.py:335
  15.5 1.6 collective-permute-start
  17.0 4.3 %collective-permute-done.rest_0_.there_ref = f32[18,2,1280]{2,1,0:T(2,128)S(1)} collective-permute-done((f32[18,2,1280]{2,1,0:T(2,128)S(1)}, f32[18,2,1280]{2,1,0:T(2,128)S(1)}, u32[]{:S(2)}, u32[]{:S(2)}) %collective-permute-start) | collective-permute-done | bytes 184352 | tf_op jit(solution)/shard_map/ppermute | solution.py:568
  21.3 0.7 copy-done.3
  22.0 4.9 %weigh.3 = (bf16[8,2,3,160,128]{4,3,2,1,0:T(8,128)(2,1)}, bf16[8,3,160,128]{3,2,1,0:T(8,128)(2,1)}, f32[8,128]{1,0:T(8,128)}) custom-call(s32[1]{0:T(128)} %bitcast.me_ref, f32[1,160]{1,0:T(1,128)} %bitcast.4, bf16[3,160,32,128]{3,2,1,0:T(8,128)(2,1)} %tendency_ref.3, f32[18,2,1280]{2,1,0:T(2,128)} %copy-done.3), custom_call_target="tpu_custom_call" | custom-call | flops 503316480 | bytes 5898240 | tf_op jit(solution)/shard_map/weigh/pallas_call | solution.py:142
  26.9 0.1 collective-permute-start.1
  27.0 2.8 %collective-permute-done.1.mate_ref = bf16[8,3,160,128]{3,2,1,0:T(8,128)(2,1)S(1)} collective-permute-done((bf16[8,3,160,128]{3,2,1,0:T(8,128)(2,1)}, bf16[8,3,160,128]{3,2,1,0:T(8,128)(2,1)S(1)}, u32[]{:S(2)}, u32[]{:S(2)}) %collective-permute-start.1) | collective-permute-done | bytes 983072 | tf_op jit(solution)/shard_map/ppermute | solution.py:535
  29.8 1.5 copy-done.1
  31.3 0.1 pair.4
  31.4 1.3 copy-done.2
  32.7 21.4 %all-to-all-done.in_ref.rest_0_ = bf16[8,2,3,160,128]{4,3,2,1,0:T(8,128)(2,1)} async-done(((bf16[8,2,3,160,128]{4,3,2,1,0:T(8,128)(2,1)}), bf16[8,2,3,160,128]{4,3,2,1,0:T(8,128)(2,1)}, u32[]{:S(2)}, u32[]{:S(2)}) %all-to-all-start) | async-done | bytes 1966112 | tf_op jit(solution)/shard_map/all_to_all | solution.py:548
  54.1 6.8 %all-to-all-start.1 = ((bf16[8,2,3,160,128]{4,3,2,1,0:T(8,128)(2,1)}), bf16[8,2,3,160,128]{4,3,2,1,0:T(8,128)(2,1)}, u32[]{:S(2)}, u32[]{:S(2)}) async-start(bf16[8,2,3,160,128]{4,3,2,1,0:T(8,128)(2,1)} %copy-done.2), calls=%async_computation.1 | async-start | bytes 3932160 | tf_op jit(solution)/shard_map/all_to_all | solution.py:548
  60.9 1.3 pick.1
  62.2 0.1 collective-permute-start.2
  62.3 2.6 %collective-permute-done.2.rest_1_ = bf16[8,3,160,128]{3,2,1,0:T(8,128)(2,1)S(1)} collective-permute-done((bf16[8,3,160,128]{3,2,1,0:T(8,128)(2,1)S(1)}, bf16[8,3,160,128]{3,2,1,0:T(8,128)(2,1)S(1)}, u32[]{:S(2)}, u32[]{:S(2)}) %collective-permute-start.2) | collective-permute-done | bytes 983072 | tf_op jit(solution)/shard_map/ppermute | solution.py:535
  64.9 5.6 %analyse.3.own_ref = bf16[3,128,640]{2,1,0:T(8,128)(2,1)S(1)} custom-call(s32[1]{0:T(128)} %bitcast.me_ref, s32[2]{0:T(128)S(1)} %copy-done.12, f32[8,128]{1,0:T(8,128)S(1)} %get-tuple-element.35.token_ref, bf16[2,1280,2560]{2,1,0:T(8,128)(2,1)} %table_ref.11, bf16[3,2,128,1280]{3,2,1,0:T(8,128)(2,1)} %state_ref.5, ...), custom_call_target="tpu_custom_call" | custom-call | flops 1258291200 | bytes 3276800 | tf_op jit(solution)/shard_map/analyse/pallas_call | solution.py:293
  70.5 1.6 collective-permute-start.3
  72.0 11.7 %collective-permute-done.3.other_ref = bf16[3,128,640]{2,1,0:T(8,128)(2,1)S(1)} collective-permute-done((bf16[3,128,640]{2,1,0:T(8,128)(2,1)S(1)}, bf16[3,128,640]{2,1,0:T(8,128)(2,1)S(1)}, u32[]{:S(2)}, u32[]{:S(2)}) %collective-permute-start.3) | collective-permute-done | bytes 491552 | tf_op jit(solution)/shard_map/ppermute | solution.py:582
  83.8 4.9 %synthesise.3 = (bf16[8,2,3,160,128]{4,3,2,1,0:T(8,128)(2,1)S(1)}, bf16[8,3,160,128]{3,2,1,0:T(8,128)(2,1)S(1)}) custom-call(s32[1]{0:T(128)} %bitcast.me_ref, f32[1]{0:T(128)} %bitcast.1.sign_ref, f32[18,2,1280]{2,1,0:T(2,128)S(1)} %sum_pairs.1.here_ref, f32[18,2,1280]{2,1,0:T(2,128)S(1)} %copy-done.4, bf16[3,128,640]{2,1,0:T(8,128)(2,1)S(1)} %analyse.3.own_ref, ...), custom_call_target="tpu_custom_call" | custom-call | flops 1258291200 | bytes 3276800 | tf_op jit(solution)/shard_map/synthesise/pallas_call | solution.py:433
  88.7 0.1 collective-permute-start.4
  88.8 2.6 %collective-permute-done.4.mate_ref = bf16[8,3,160,128]{3,2,1,0:T(8,128)(2,1)S(1)} collective-permute-done((bf16[8,3,160,128]{3,2,1,0:T(8,128)(2,1)S(1)}, bf16[8,3,160,128]{3,2,1,0:T(8,128)(2,1)S(1)}, u32[]{:S(2)}, u32[]{:S(2)}) %collective-permute-start.4) | collective-permute-done | bytes 983072 | tf_op jit(solution)/shard_map/ppermute | solution.py:535
  91.4 0.1 pair.5
  91.5 0.0 copy-start
  91.5 1.3 copy-done
  92.7 10.4 %all-to-all-done.1.rest_0_ = bf16[8,2,3,160,128]{4,3,2,1,0:T(8,128)(2,1)} async-done(((bf16[8,2,3,160,128]{4,3,2,1,0:T(8,128)(2,1)}), bf16[8,2,3,160,128]{4,3,2,1,0:T(8,128)(2,1)}, u32[]{:S(2)}, u32[]{:S(2)}) %all-to-all-start.1) | async-done | bytes 1966112 | tf_op jit(solution)/shard_map/all_to_all | solution.py:548
  103.2 6.5 %all-to-all-start.2 = ((bf16[8,2,3,160,128]{4,3,2,1,0:T(8,128)(2,1)}), bf16[8,2,3,160,128]{4,3,2,1,0:T(8,128)(2,1)S(1)}, u32[]{:S(2)}, u32[]{:S(2)}) async-start(bf16[8,2,3,160,128]{4,3,2,1,0:T(8,128)(2,1)} %copy-done), calls=%async_computation.2 | async-start | bytes 3932160 | tf_op jit(solution)/shard_map/all_to_all | solution.py:548
  109.7 5.8 %analyse.5.own_ref = bf16[3,128,640]{2,1,0:T(8,128)(2,1)S(1)} custom-call(s32[1]{0:T(128)} %bitcast.me_ref, s32[2]{0:T(128)S(1)} %copy-done.12, f32[8,128]{1,0:T(8,128)S(1)} %get-tuple-element.39.token_ref, bf16[2,1280,2560]{2,1,0:T(8,128)(2,1)} %table_ref.11, bf16[3,2,128,1280]{3,2,1,0:T(8,128)(2,1)} %state_ref.5, ...), custom_call_target="tpu_custom_call" | custom-call | flops 1258291200 | bytes 3276800 | tf_op jit(solution)/shard_map/analyse/pallas_call | solution.py:293
  115.5 1.6 collective-permute-start.6
  117.1 5.8 %analyse.4.own_ref = bf16[3,128,640]{2,1,0:T(8,128)(2,1)S(1)} custom-call(s32[1]{0:T(128)} %bitcast.me_ref, s32[2]{0:T(128)S(1)} %copy-done.12, f32[8,128]{1,0:T(8,128)S(1)} %get-tuple-element.39.token_ref, bf16[2,1280,2560]{2,1,0:T(8,128)(2,1)} %table_ref.11, bf16[3,2,128,1280]{3,2,1,0:T(8,128)(2,1)} %state_ref.5, ...), custom_call_target="tpu_custom_call" | custom-call | flops 1258291200 | bytes 3276800 | tf_op jit(solution)/shard_map/analyse/pallas_call | solution.py:293
  123.0 0.6 collective-permute-start.5
  123.5 6.2 %collective-permute-done.6.other_ref = bf16[3,128,640]{2,1,0:T(8,128)(2,1)S(1)} collective-permute-done((bf16[3,128,640]{2,1,0:T(8,128)(2,1)S(1)}, bf16[3,128,640]{2,1,0:T(8,128)(2,1)S(1)}, u32[]{:S(2)}, u32[]{:S(2)}) %collective-permute-start.6) | collective-permute-done | bytes 491552 | tf_op jit(solution)/shard_map/ppermute | solution.py:582
  129.8 4.8 %synthesise.4.rest_0_ = f32[384,2560]{1,0:T(8,128)S(1)} custom-call(s32[1]{0:T(128)} %bitcast.me_ref, f32[1]{0:T(128)} %bitcast.1.sign_ref, f32[18,2,1280]{2,1,0:T(2,128)S(1)} %sum_pairs.1.here_ref, f32[18,2,1280]{2,1,0:T(2,128)S(1)} %copy-done.4, bf16[3,128,640]{2,1,0:T(8,128)(2,1)S(1)} %analyse.5.own_ref, ...), custom_call_target="tpu_custom_call" | custom-call | flops 1258291200 | bytes 3276800 | tf_op jit(solution)/shard_map/synthesise/pallas_call | solution.py:433
  134.6 4.1 %collective-permute-done.5.other_ref = bf16[3,128,640]{2,1,0:T(8,128)(2,1)S(1)} collective-permute-done((bf16[3,128,640]{2,1,0:T(8,128)(2,1)S(1)}, bf16[3,128,640]{2,1,0:T(8,128)(2,1)S(1)}, u32[]{:S(2)}, u32[]{:S(2)}) %collective-permute-start.5) | collective-permute-done | bytes 491552 | tf_op jit(solution)/shard_map/ppermute | solution.py:582
  138.7 6.4 %synthesise.5 = (bf16[2,3,160,128]{3,2,1,0:T(8,128)(2,1)S(1)}, bf16[2,3,160,128]{3,2,1,0:T(8,128)(2,1)}, bf16[2,3,160,128]{3,2,1,0:T(8,128)(2,1)}, bf16[2,3,160,...) custom-call(s32[1]{0:T(128)} %bitcast.me_ref, ...), custom_call_target="tpu_custom_call" | custom-call | flops 1258291200 | bytes 3276800 | tf_op jit(solution)/shard_map/synthesise/pallas_call | solution.py:433
  145.2 0.1 collective-permute-start.7
  145.3 2.6 %collective-permute-done.7.mate_ref = bf16[8,3,160,128]{3,2,1,0:T(8,128)(2,1)S(1)} collective-permute-done((bf16[8,3,160,128]{3,2,1,0:T(8,128)(2,1)S(1)}, bf16[8,3,160,128]{3,2,1,0:T(8,128)(2,1)S(1)}, u32[]{:S(2)}, u32[]{:S(2)}) %collective-permute-start.7) | collective-permute-done | bytes 983072 | tf_op jit(solution)/shard_map/ppermute | solution.py:535
  147.8 1.0 pair.6
  148.8 1.8 collective-permute-start.8
  150.6 2.1 %collective-permute-start.9 = (bf16[2,3,160,128]{3,2,1,0:T(8,128)(2,1)}, bf16[2,3,160,128]{3,2,1,0:T(8,128)(2,1)}, u32[]{:S(2)}, u32[]{:S(2)}) collective-permute-start(bf16[2,3,160,128]{3,2,1,0:T(8,128)(2,1)} %get-tuple-element.49), channel_id=1, source_target_pairs={{0,10},{1,11},{2,8},{3,9},{4,14},{5,15},{6,12},{7,13},{8,2},{9,3},... | collective-permute-start | bytes 737288 | tf_op jit(solution)/shard_map/ppermute | solution.py:542
  152.7 0.8 collective-permute-start.10
  153.5 1.3 collective-permute-start.11
  154.8 19.2 %all-to-all-done.2.rest_3_.rest_8_ = bf16[8,2,3,160,128]{4,3,2,1,0:T(8,128)(2,1)S(1)} async-done(((bf16[8,2,3,160,128]{4,3,2,1,0:T(8,128)(2,1)}), bf16[8,2,3,160,128]{4,3,2,1,0:T(8,128)(2,1)S(1)}, u32[]{:S(2)}, u32[]{:S(2)}) %all-to-all-start.2) | async-done | bytes 1966112 | tf_op jit(solution)/shard_map/all_to_all | solution.py:548
  174.0 0.9 copy-done.7
  175.0 0.9 copy-done.9
  175.9 0.9 copy-done.11
  176.8 0.5 pair.7
  177.3 0.7 collective-permute-start.12
  178.0 1.2 collective-permute-done.8.rest_1_
  179.3 3.6 %collective-permute-start.13 = (bf16[2,3,160,128]{3,2,1,0:T(8,128)(2,1)S(1)}, bf16[2,3,160,128]{3,2,1,0:T(8,128)(2,1)S(1)}, u32[]{:S(2)}, u32[]{:S(2)}) collective-permute-start(bf16[2,3,160,128]{3,2,1,0:T(8,128)(2,1)S(1)} %get-tuple-element.57), channel_id=1, source_target_pairs={{0,4},{1,5},{2,6},{3,7},{4,0},{5,1},{6,2},{7,3},{8,12},{9,13},{10,... | collective-permute-start | bytes 737288 | tf_op jit(solution)/shard_map/ppermute | solution.py:542
  182.9 1.7 collective-permute-done.9.rest_2_
  184.6 4.6 %collective-permute-start.14 = (bf16[2,3,160,128]{3,2,1,0:T(8,128)(2,1)S(1)}, bf16[2,3,160,128]{3,2,1,0:T(8,128)(2,1)S(1)}, u32[]{:S(2)}, u32[]{:S(2)}) collective-permute-start(bf16[2,3,160,128]{3,2,1,0:T(8,128)(2,1)S(1)} %get-tuple-element.58), channel_id=1, source_target_pairs={{0,6},{1,7},{2,4},{3,5},{4,2},{5,3},{6,0},{7,1},{8,14},{9,15},{10,... | collective-permute-start | bytes 737288 | tf_op jit(solution)/shard_map/ppermute | solution.py:542
  189.2 2.9 %collective-permute-done.10.rest_3_ = bf16[2,3,160,128]{3,2,1,0:T(8,128)(2,1)} collective-permute-done((bf16[2,3,160,128]{3,2,1,0:T(8,128)(2,1)}, bf16[2,3,160,128]{3,2,1,0:T(8,128)(2,1)}, u32[]{:S(2)}, u32[]{:S(2)}) %collective-permute-start.10) | collective-permute-done | bytes 245792 | tf_op jit(solution)/shard_map/ppermute | solution.py:542
  192.1 6.6 %collective-permute-done.11.rest_4_ = bf16[2,3,160,128]{3,2,1,0:T(8,128)(2,1)} collective-permute-done((bf16[2,3,160,128]{3,2,1,0:T(8,128)(2,1)}, bf16[2,3,160,128]{3,2,1,0:T(8,128)(2,1)}, u32[]{:S(2)}, u32[]{:S(2)}) %collective-permute-start.11) | collective-permute-done | bytes 245792 | tf_op jit(solution)/shard_map/ppermute | solution.py:542
  198.7 0.0 collective-permute-done.12.rest_5_
  198.7 0.0 collective-permute-done.13.rest_6_
  198.7 0.0 collective-permute-done.14.rest_7_
  198.7 4.0 %assemble.1 = bf16[3,160,32,128]{3,2,1,0:T(8,128)(2,1)} custom-call(s32[1]{0:T(128)} %bitcast.me_ref, bf16[2,3,160,128]{3,2,1,0:T(8,128)(2,1)S(1)} %get-tuple-element.47.rest_0_, bf16[2,3,160,128]{3,2,1,0:T(8,128)(2,1)S(1)} %collective-permute-done.8.rest_1_, bf16[2,3,160,128]{3,2,1,0:T(8,128)(2,1)} %collective-permute-done.9.rest_2_, ...), custom_call_target="tpu_custom_call" | custom-call | flops 1006632960 | bytes 7864320 | tf_op jit(solution)/shard_map/assemble/pallas_call | solution.py:516
  (18 shorter events, 0.0 us)
Async XLA Ops:
  4.9 6.3 %copy-start.14 = (f32[32,2]{0,1:T(2,128)S(1)}, f32[32,2]{0,1:T(2,128)}, u32[]{:S(2)}) copy-start(f32[32,2]{0,1:T(2,128)} %param.12) | copy-start | bytes 772
  4.9 6.4 %copy-start.13 = (f32[8,128]{1,0:T(8,128)S(1)}, f32[8,128]{1,0:T(8,128)}, u32[]{:S(2)}) copy-start(f32[8,128]{1,0:T(8,128)} %get-tuple-element.32.token_ref) | copy-start | bytes 12292
  4.9 49.2 %all-to-all-start = ((bf16[8,2,3,160,128]{4,3,2,1,0:T(8,128)(2,1)}), bf16[8,2,3,160,128]{4,3,2,1,0:T(8,128)(2,1)}, u32[]{:S(2)}, u32[]{:S(2)}) async-start(bf16[8,2,3,160,128]{4,3,2,1,0:T(8,128)(2,1)} %get-tuple-element.36), calls=%async_computation | async-start | bytes 3932160 | tf_op jit(solution)/shard_map/all_to_all | solution.py:548
  11.3 1.8 copy-start.5
  15.5 5.9 %collective-permute-start = (f32[18,2,1280]{2,1,0:T(2,128)S(1)}, f32[18,2,1280]{2,1,0:T(2,128)S(1)}, u32[]{:S(2)}, u32[]{:S(2)}) collective-permute-start(f32[18,2,1280]{2,1,0:T(2,128)S(1)} %sum_pairs.1.here_ref), channel_id=1, source_target_pairs={{0,16},{16,0},{1,17},{17,1},{2,18},{18,2},{3,19},{19,3},{4,20},{20... | collective-permute-start | bytes 552968 | tf_op jit(solution)/shard_map/ppermute | solution.py:568
  21.3 0.7 copy-start.3
  26.9 2.8 %collective-permute-start.1 = (bf16[8,3,160,128]{3,2,1,0:T(8,128)(2,1)}, bf16[8,3,160,128]{3,2,1,0:T(8,128)(2,1)S(1)}, u32[]{:S(2)}, u32[]{:S(2)}) collective-permute-start(bf16[8,3,160,128]{3,2,1,0:T(8,128)(2,1)} %get-tuple-element.33), channel_id=1, source_target_pairs={{0,1},{1,0},{2,3},{3,2},{4,5},{5,4},{6,7},{7,6},{8,9},{9,8},{10,11... | collective-permute-start | bytes 2949128 | tf_op jit(solution)/shard_map/ppermute | solution.py:535
  29.8 1.5 copy-start.1
  31.4 1.3 copy-start.2
  54.1 49.0 %all-to-all-start.1 = ((bf16[8,2,3,160,128]{4,3,2,1,0:T(8,128)(2,1)}), bf16[8,2,3,160,128]{4,3,2,1,0:T(8,128)(2,1)}, u32[]{:S(2)}, u32[]{:S(2)}) async-start(bf16[8,2,3,160,128]{4,3,2,1,0:T(8,128)(2,1)} %copy-done.2), calls=%async_computation.1 | async-start | bytes 3932160 | tf_op jit(solution)/shard_map/all_to_all | solution.py:548
  60.9 3.9 %copy-start.12 = (s32[2]{0:T(128)S(1)}, s32[2]{0:T(128)}, u32[]{:S(2)}) copy-start(s32[2]{0:T(128)} %wave_ref.5) | copy-start | bytes 28
  62.2 21.6 %copy-start.4 = (f32[18,2,1280]{2,1,0:T(2,128)S(1)}, f32[18,2,1280]{2,1,0:T(2,128)}, u32[]{:S(2)}) copy-start(f32[18,2,1280]{2,1,0:T(2,128)} %copy-done.3) | copy-start | bytes 552964
  62.2 2.6 %collective-permute-start.2 = (bf16[8,3,160,128]{3,2,1,0:T(8,128)(2,1)S(1)}, bf16[8,3,160,128]{3,2,1,0:T(8,128)(2,1)S(1)}, u32[]{:S(2)}, u32[]{:S(2)}) collective-permute-start(bf16[8,3,160,128]{3,2,1,0:T(8,128)(2,1)S(1)} %pick.1), channel_id=1, source_target_pairs={{0,1},{1,0},{2,3},{3,2},{4,5},{5,4},{6,7},{7,6},{8,9},{9,8},{10,11... | collective-permute-start | bytes 2949128 | tf_op jit(solution)/shard_map/ppermute | solution.py:535
  70.5 13.3 %collective-permute-start.3 = (bf16[3,128,640]{2,1,0:T(8,128)(2,1)S(1)}, bf16[3,128,640]{2,1,0:T(8,128)(2,1)S(1)}, u32[]{:S(2)}, u32[]{:S(2)}) collective-permute-start(bf16[3,128,640]{2,1,0:T(8,128)(2,1)S(1)} %analyse.3.own_ref), channel_id=1, source_target_pairs={{0,16},{16,0},{1,17},{17,1},{2,18},{18,2},{3,19},{19,3},{4,20},{20... | collective-permute-start | bytes 1474568 | tf_op jit(solution)/shard_map/ppermute | solution.py:582
  88.7 2.6 %collective-permute-start.4 = (bf16[8,3,160,128]{3,2,1,0:T(8,128)(2,1)S(1)}, bf16[8,3,160,128]{3,2,1,0:T(8,128)(2,1)S(1)}, u32[]{:S(2)}, u32[]{:S(2)}) collective-permute-start(bf16[8,3,160,128]{3,2,1,0:T(8,128)(2,1)S(1)} %get-tuple-element.37), channel_id=1, source_target_pairs={{0,1},{1,0},{2,3},{3,2},{4,5},{5,4},{6,7},{7,6},{8,9},{9,8},{10,11... | collective-permute-start | bytes 2949128 | tf_op jit(solution)/shard_map/ppermute | solution.py:535
  91.5 1.3 copy-start
  103.2 70.8 %all-to-all-start.2 = ((bf16[8,2,3,160,128]{4,3,2,1,0:T(8,128)(2,1)}), bf16[8,2,3,160,128]{4,3,2,1,0:T(8,128)(2,1)S(1)}, u32[]{:S(2)}, u32[]{:S(2)}) async-start(bf16[8,2,3,160,128]{4,3,2,1,0:T(8,128)(2,1)} %copy-done), calls=%async_computation.2 | async-start | bytes 3932160 | tf_op jit(solution)/shard_map/all_to_all | solution.py:548
  115.5 14.2 %collective-permute-start.6 = (bf16[3,128,640]{2,1,0:T(8,128)(2,1)S(1)}, bf16[3,128,640]{2,1,0:T(8,128)(2,1)S(1)}, u32[]{:S(2)}, u32[]{:S(2)}) collective-permute-start(bf16[3,128,640]{2,1,0:T(8,128)(2,1)S(1)} %analyse.5.own_ref), channel_id=1, source_target_pairs={{0,16},{16,0},{1,17},{17,1},{2,18},{18,2},{3,19},{19,3},{4,20},{20... | collective-permute-start | bytes 1474568 | tf_op jit(solution)/shard_map/ppermute | solution.py:582
  123.0 15.8 %collective-permute-start.5 = (bf16[3,128,640]{2,1,0:T(8,128)(2,1)S(1)}, bf16[3,128,640]{2,1,0:T(8,128)(2,1)S(1)}, u32[]{:S(2)}, u32[]{:S(2)}) collective-permute-start(bf16[3,128,640]{2,1,0:T(8,128)(2,1)S(1)} %analyse.4.own_ref), channel_id=1, source_target_pairs={{0,16},{16,0},{1,17},{17,1},{2,18},{18,2},{3,19},{19,3},{4,20},{20... | collective-permute-start | bytes 1474568 | tf_op jit(solution)/shard_map/ppermute | solution.py:582
  145.2 8.3 %copy-start.6 = (bf16[2,3,160,128]{3,2,1,0:T(8,128)(2,1)}, bf16[2,3,160,128]{3,2,1,0:T(8,128)(2,1)S(1)}, u32[]{:S(2)}) copy-start(bf16[2,3,160,128]{3,2,1,0:T(8,128)(2,1)S(1)} %get-tuple-element.52.rest_0_) | copy-start | bytes 737284
  145.2 8.3 %copy-start.8 = (bf16[2,3,160,128]{3,2,1,0:T(8,128)(2,1)}, bf16[2,3,160,128]{3,2,1,0:T(8,128)(2,1)S(1)}, u32[]{:S(2)}) copy-start(bf16[2,3,160,128]{3,2,1,0:T(8,128)(2,1)S(1)} %get-tuple-element.53.rest_1_) | copy-start | bytes 737284
  145.2 8.3 %copy-start.10 = (bf16[2,3,160,128]{3,2,1,0:T(8,128)(2,1)}, bf16[2,3,160,128]{3,2,1,0:T(8,128)(2,1)S(1)}, u32[]{:S(2)}) copy-start(bf16[2,3,160,128]{3,2,1,0:T(8,128)(2,1)S(1)} %get-tuple-element.54.rest_2_) | copy-start | bytes 737284
  145.2 2.6 %collective-permute-start.7 = (bf16[8,3,160,128]{3,2,1,0:T(8,128)(2,1)S(1)}, bf16[8,3,160,128]{3,2,1,0:T(8,128)(2,1)S(1)}, u32[]{:S(2)}, u32[]{:S(2)}) collective-permute-start(bf16[8,3,160,128]{3,2,1,0:T(8,128)(2,1)S(1)} %get-tuple-element.41), channel_id=1, source_target_pairs={{0,1},{1,0},{2,3},{3,2},{4,5},{5,4},{6,7},{7,6},{8,9},{9,8},{10,11... | collective-permute-start | bytes 2949128 | tf_op jit(solution)/shard_map/ppermute | solution.py:535
  148.8 30.5 %collective-permute-start.8 = (bf16[2,3,160,128]{3,2,1,0:T(8,128)(2,1)}, bf16[2,3,160,128]{3,2,1,0:T(8,128)(2,1)S(1)}, u32[]{:S(2)}, u32[]{:S(2)}) collective-permute-start(bf16[2,3,160,128]{3,2,1,0:T(8,128)(2,1)} %get-tuple-element.48), channel_id=1, source_target_pairs={{0,8},{1,9},{2,10},{3,11},{4,12},{5,13},{6,14},{7,15},{8,0},{9,1},... | collective-permute-start | bytes 737288 | tf_op jit(solution)/shard_map/ppermute | solution.py:542
  150.6 34.1 %collective-permute-start.9 = (bf16[2,3,160,128]{3,2,1,0:T(8,128)(2,1)}, bf16[2,3,160,128]{3,2,1,0:T(8,128)(2,1)}, u32[]{:S(2)}, u32[]{:S(2)}) collective-permute-start(bf16[2,3,160,128]{3,2,1,0:T(8,128)(2,1)} %get-tuple-element.49), channel_id=1, source_target_pairs={{0,10},{1,11},{2,8},{3,9},{4,14},{5,15},{6,12},{7,13},{8,2},{9,3},... | collective-permute-start | bytes 737288 | tf_op jit(solution)/shard_map/ppermute | solution.py:542
  152.7 39.4 %collective-permute-start.10 = (bf16[2,3,160,128]{3,2,1,0:T(8,128)(2,1)}, bf16[2,3,160,128]{3,2,1,0:T(8,128)(2,1)}, u32[]{:S(2)}, u32[]{:S(2)}) collective-permute-start(bf16[2,3,160,128]{3,2,1,0:T(8,128)(2,1)} %get-tuple-element.50), channel_id=1, source_target_pairs={{0,12},{1,13},{2,14},{3,15},{4,8},{5,9},{6,10},{7,11},{8,4},{9,5},... | collective-permute-start | bytes 737288 | tf_op jit(solution)/shard_map/ppermute | solution.py:542
  153.5 45.2 %collective-permute-start.11 = (bf16[2,3,160,128]{3,2,1,0:T(8,128)(2,1)}, bf16[2,3,160,128]{3,2,1,0:T(8,128)(2,1)}, u32[]{:S(2)}, u32[]{:S(2)}) collective-permute-start(bf16[2,3,160,128]{3,2,1,0:T(8,128)(2,1)} %get-tuple-element.51), channel_id=1, source_target_pairs={{0,14},{1,15},{2,12},{3,13},{4,10},{5,11},{6,8},{7,9},{8,6},{9,7},... | collective-permute-start | bytes 737288 | tf_op jit(solution)/shard_map/ppermute | solution.py:542
  174.0 0.9 copy-start.7
  175.0 0.9 copy-start.9
  175.9 0.9 copy-start.11
  177.3 21.4 %collective-permute-start.12 = (bf16[2,3,160,128]{3,2,1,0:T(8,128)(2,1)S(1)}, bf16[2,3,160,128]{3,2,1,0:T(8,128)(2,1)S(1)}, u32[]{:S(2)}, u32[]{:S(2)}) collective-permute-start(bf16[2,3,160,128]{3,2,1,0:T(8,128)(2,1)S(1)} %get-tuple-element.56), channel_id=1, source_target_pairs={{0,2},{1,3},{2,0},{3,1},{4,6},{5,7},{6,4},{7,5},{8,10},{9,11},{10,... | collective-permute-start | bytes 737288 | tf_op jit(solution)/shard_map/ppermute | solution.py:542
  179.3 19.4 %collective-permute-start.13 = (bf16[2,3,160,128]{3,2,1,0:T(8,128)(2,1)S(1)}, bf16[2,3,160,128]{3,2,1,0:T(8,128)(2,1)S(1)}, u32[]{:S(2)}, u32[]{:S(2)}) collective-permute-start(bf16[2,3,160,128]{3,2,1,0:T(8,128)(2,1)S(1)} %get-tuple-element.57), channel_id=1, source_target_pairs={{0,4},{1,5},{2,6},{3,7},{4,0},{5,1},{6,2},{7,3},{8,12},{9,13},{10,... | collective-permute-start | bytes 737288 | tf_op jit(solution)/shard_map/ppermute | solution.py:542
  184.6 14.1 %collective-permute-start.14 = (bf16[2,3,160,128]{3,2,1,0:T(8,128)(2,1)S(1)}, bf16[2,3,160,128]{3,2,1,0:T(8,128)(2,1)S(1)}, u32[]{:S(2)}, u32[]{:S(2)}) collective-permute-start(bf16[2,3,160,128]{3,2,1,0:T(8,128)(2,1)S(1)} %get-tuple-element.58), channel_id=1, source_target_pairs={{0,6},{1,7},{2,4},{3,5},{4,2},{5,3},{6,0},{7,1},{8,14},{9,15},{10,... | collective-permute-start | bytes 737288 | tf_op jit(solution)/shard_map/ppermute | solution.py:542

commit v17 on v16

--- a/solution.py
+++ b/solution.py
@@ -454,81 +454,79 @@
     )(me, sign, here, there, own, other, table, *partial)
 
 
-def assemble_kernel(counts, me_ref, *rest):
-    ins, out_ref, (held, done, in_sems, out_sems) = rest[: sum(counts)], rest[-5], rest[-4:]
+def assemble_kernel(far, moved, count, me_ref, blocks_ref, *rest):
+    messages, out_ref, (held, done, in_sems, out_sems) = rest[:count], rest[-5], rest[-4:]
     rows, lats, slots, members = done.shape
-    local_slots = len(counts)
+    half = held.shape[0]
+    local_slots = slots // half // CORES
     chip = me_ref[0] // CORES
+    side = chip // half if not far else 1 - chip // half
     each = out_sems.shape[1]
     size = lats // each
     depth, breadth = math.gcd(size, 16), 16
-    copies, whole = [], {}
+    wanted = [k for k in partners(2 * half) if (k >= half) == far]
+    copies = []
     for r in range(rows):
         copies.append([])
-        used = 0
-        for slot, count in enumerate(counts):
-            refs = ins[used : used + count]
-            used += count
-            if count == 1:
-                whole[slot] = refs[0]
-                continue
-            if r == 0:
-                held[slot, chip] = refs[0][...]
-            for i, (k, ref) in list(enumerate(zip(partners(count), refs)))[1:]:
-                target = held.at[slot, chip ^ k, :, r]
-                copies[r].append(pltpu.make_async_copy(ref.at[:, r], target, in_sems.at[r, slot, i]))
-        for copy in copies[r]:
-            copy.start()
+        for i, (k, ref) in enumerate(zip(wanted, messages)):
+            target = held.at[(chip ^ k) & (half - 1), :, r]
+            copies[r].append(pltpu.make_async_copy(ref.at[:, r], target, in_sems.at[r, i]))
+            copies[r][-1].start()
     matrix = swap_matrix(breadth, depth, 1, 0)
     results = []
+
+    def tile(r, start, s):
+        parts = []
+        for i in range(s, s + breadth):
+            owner, slot = divmod(i, local_slots)
+            place = owner // CORES
+            if slot == moved:
+                parts.append(held[place, owner % CORES, r, start : start + depth, :])
+            else:
+                parts.append(blocks_ref[side * half + place, owner % CORES, r, start : start + depth, :])
+        return jnp.concatenate(parts, axis=0)
+
     for r in range(rows):
         for copy in copies[r]:
             copy.wait()
-        for start in range(0, lats, depth):
-            j = slice(start, start + depth)
-            for s in range(0, slots, 2 * breadth):
-                halves = []
-                for h in (0, breadth):
-                    columns = [divmod(i, local_slots) for i in range(s + h, s + h + breadth)]
-                    columns = [
-                        whole.get(slot, held.at[slot])[owner // CORES, owner % CORES, r, j, :]
-                        for owner, slot in columns
-                    ]
-                    halves.append(jnp.concatenate(columns, axis=0))
-                turned = jnp.dot(matrix, jnp.concatenate(halves, axis=1), preferred_element_type=F32).astype(BF16)
-                for h in range(2):
-                    value = turned[:, h * members : (h + 1) * members].reshape(depth, breadth, members)
-                    done[r, j, s + h * breadth : s + (h + 1) * breadth, :] = value
-            if (start + depth) % size == 0:
-                part = pl.ds(start + depth - size, size)
-                target = out_ref.at[r, part]
-                results.append(pltpu.make_async_copy(done.at[r, part], target, out_sems.at[r, start // size]))
-                results[-1].start()
+        for part in range(each):
+            starts = range(part * size, (part + 1) * size, depth)
+            tiles = [(start, s) for start in starts for s in range(0, slots, breadth)]
+            for i in range(0, len(tiles), 2):
+                both = tiles[i : i + 2]
+                wide = jnp.concatenate([tile(r, *place) for place in both], axis=1)
+                turned = jnp.dot(matrix, wide, preferred_element_type=F32).astype(BF16)
+                for n, (start, s) in enumerate(both):
+                    value = turned[:, n * members : (n + 1) * members].reshape(depth, breadth, members)
+                    done[r, start : start + depth, s : s + breadth, :] = value
+            lines = pl.ds(part * size, size)
+            target = out_ref.at[r, lines, pl.ds(pl.multiple_of(side * slots, slots), slots)]
+            results.append(pltpu.make_async_copy(done.at[r, lines], target, out_sems.at[r, part]))
+            results[-1].start()
     for copy in results:
         copy.wait()
 
 
-def assemble(pieces, me):
-    rows, lats, members = pieces[0][0].shape[-3:]
-    chips = max(len(p) if len(p) > 1 else p[0].shape[0] for p in pieces)
-    slots = len(pieces) * chips * CORES
-    flat = [block for slot in pieces for block in slot]
-    return call(
-        functools.partial(assemble_kernel, [len(p) for p in pieces]),
+def assemble(blocks, messages, me, moved, local_slots, far, output):
+    chips, _, rows, lats, members = blocks.shape
+    half = chips // 2
+    slots = local_slots * half * CORES
+    return call(
+        functools.partial(assemble_kernel, far, moved, len(messages)),
         "assemble",
         2 * 256 * rows * lats * slots * members,
         4 * rows * lats * slots * members,
-        out_shape=jax.ShapeDtypeStruct((rows, lats, slots, members), BF16),
-        in_specs=[IN_SMEM]
-        + [IN_VMEM if i == 0 else IN_HBM for p in pieces for i in range(len(p))],
+        out_shape=jax.ShapeDtypeStruct((rows, lats, 2 * slots, members), BF16),
+        in_specs=[IN_SMEM, IN_VMEM] + [IN_HBM] * (len(messages) + len(output)),
         out_specs=IN_HBM,
         scratch_shapes=[
-            pltpu.VMEM((len(pieces), chips, CORES, rows, lats, members), BF16),
+            pltpu.VMEM((half, CORES, rows, lats, members), BF16),
             pltpu.VMEM((rows, lats, slots, members), BF16),
-            pltpu.SemaphoreType.DMA((rows, len(pieces), chips)),
+            pltpu.SemaphoreType.DMA((rows, half)),
             pltpu.SemaphoreType.DMA((rows, lats // lat_block(lats))),
         ],
-    )(me, *flat)
+        input_output_aliases={len(messages) + 2: 0} if output else {},
+    )(me, blocks, *messages, *output)
 
 
 def between_cores(blocks, owners):
@@ -588,15 +586,15 @@
         *own, for_mate = own
         mate = between_cores(for_mate, owners)
         if last:
-            far = len(own) // 2 + 1
-            own = list(pair_messages(own[:far], mate, me, 0, [])) + list(
-                pair_messages(own[far:], mate, me, far, sent[order[0]])
-            )
+            own = pair_messages(own, mate, me, 0, [])
             sent[slot] = by_permutes(own)
         else:
             blocks, token = pair(own[0], mate, me)
             sent[slot] = [between_chips(blocks, owners)]
-    return assemble([sent[slot] for slot in range(local_slots)], me)
+    blocks, messages = sent[order[0]][0], sent[order[-1]]
+    far = len(messages) // 2 + 1
+    near = assemble(blocks, messages[:1] + messages[far:], me, order[-1], local_slots, False, [])
+    return assemble(blocks, messages[1:far], me, order[-1], local_slots, True, [near])
 
 
 def solution(mesh):

time: 204 us -> 202 us (level)
  starting transfers between devices: 40.1 us -> 33.4 us
  waiting for transfers between devices: 100 us -> 103 us
    ppermute x7, waiting for transfers between devices: 12.4 us -> 34.6 us  [by_permutes(): lax.ppermute(message, 'wave', [(d, d ^ k * CORES) for d in range(owners)])]
    all_to_all x3, waiting for transfers between devices: 51.1 us -> 31.8 us  [between_chips(): lax.all_to_all(blocks, 'wave', split_axis=0, concat_axis=0, axis_index_gr...]
    ppermute x7, starting transfers between devices: 14.9 us -> 8.21 us  [by_permutes(): lax.ppermute(message, 'wave', [(d, d ^ k * CORES) for d in range(owners)])]
    pallas_call x1 -> x2, Pallas kernels: 4 us -> 5.82 us  [assemble(): call(functools.partial(assemble_kernel, far, moved, len(messages)), 'asse...]
    unnamed x31 -> x27, local copies, waits for them, and re-layouts: 9.57 us -> 10 us
  transfers between devices with their start and end apart: 18 -> 18, of which waited for: 15 -> 16; matrix products, arithmetic and copies ran while one was open for 0% -> 0% of each run, Pallas kernels for 22% -> 23%
where the time goes in v17:
time: 202 us; the launch traced here: 201 us
  waiting for transfers between devices  103 us (51%)
  Pallas kernels  53.9 us (27%)
  starting transfers between devices  33.4 us (17%)
  local copies, waits for them, and re-layouts  10 us (5%)
    ppermute x7, waiting for transfers between devices, by_permutes(): lax.ppermute(message, 'wave', [(d, d ^ k * CORES) for d in range(owners)])  34.6 us
    all_to_all x3, waiting for transfers between devices, between_chips(): lax.all_to_all(blocks, 'wave', split_axis=0, concat_axis=0, axis_index_gr...  31.8 us
    ppermute x3, waiting for transfers between devices, per_device(): others = [lax.ppermute(part, 'pole', [(0, 1), (1, 0)]) for part in forced]  22.1 us
    all_to_all x3, starting transfers between devices, between_chips(): lax.all_to_all(blocks, 'wave', split_axis=0, concat_axis=0, axis_index_gr...  19.6 us
    pallas_call x3, Pallas kernels, analyse(): call(functools.partial(analyse_kernel, slot, low), 'analyse', 2 * width *...  17.3 us
    pallas_call x3, Pallas kernels, synthesise(): call(functools.partial(synthesise_kernel, slot, low, apart, more, len(par...  16.2 us
    ppermute x4, waiting for transfers between devices, between_cores(): return lax.ppermute(blocks, 'wave', [(d, d ^ 1) for d in range(owners)])  10.4 us
    unnamed x27, local copies, waits for them, and re-layouts  10 us
  transfers between devices with their start and end apart: 18, of which 16 were waited for; matrix products, arithmetic and copies ran while one was open for 0% of the time, Pallas kernels for 23%

profile of v17, /device:TPU:8, one launch (start us, length us, event | category | flops | bytes accessed | tf_op | source)
XLA Modules:
  0.0 200.9 jit_solution(6146754413971032589)
XLA Ops:
  0.0 4.9 %weigh.2 = (bf16[8,2,3,160,128]{4,3,2,1,0:T(8,128)(2,1)}, f32[8,128]{1,0:T(8,128)}) custom-call(s32[1]{0:T(128)} %bitcast.me_ref, f32[1,160]{1,0:T(1,128)} %bitcast.3, bf16[3,160,32,128]{3,2,1,0:T(8,128)(2,1)} %tendency_ref.3), custom_call_target="tpu_custom_call" | custom-call | flops 503316480 | bytes 5898240 | tf_op jit(solution)/shard_map/weigh/pallas_call | solution.py:142
  4.9 0.0 copy-start.12
  4.9 6.3 %all-to-all-start = ((bf16[8,2,3,160,128]{4,3,2,1,0:T(8,128)(2,1)}), bf16[8,2,3,160,128]{4,3,2,1,0:T(8,128)(2,1)}, u32[]{:S(2)}, u32[]{:S(2)}) async-start(bf16[8,2,3,160,128]{4,3,2,1,0:T(8,128)(2,1)} %get-tuple-element.36), calls=%async_computation | async-start | bytes 3932160 | tf_op jit(solution)/shard_map/all_to_all | solution.py:546
  11.2 0.0 copy-done.12
  11.2 0.1 copy.19.coeff_ref
  11.3 1.8 copy-done.5
  13.1 2.4 %sum_pairs.1.here_ref = f32[18,2,1280]{2,1,0:T(2,128)S(1)} custom-call(f32[32,2]{1,0:T(8,128)S(1)} %copy.19.coeff_ref, f32[8,128]{1,0:T(8,128)S(1)} %copy-done.11, bf16[32,18,2,1280]{3,2,1,0:T(2,128)(2,1)S(1)} %copy-done.5), custom_call_target="tpu_custom_call" | custom-call | flops 5898240 | bytes 2949120 | tf_op jit(solution)/shard_map/sum_pairs/pallas_call | solution.py:335
  15.5 1.6 collective-permute-start
  17.0 4.3 %collective-permute-done.rest_0_.there_ref = f32[18,2,1280]{2,1,0:T(2,128)S(1)} collective-permute-done((f32[18,2,1280]{2,1,0:T(2,128)S(1)}, f32[18,2,1280]{2,1,0:T(2,128)S(1)}, u32[]{:S(2)}, u32[]{:S(2)}) %collective-permute-start) | collective-permute-done | bytes 184352 | tf_op jit(solution)/shard_map/ppermute | solution.py:566
  21.3 0.7 copy-done.3
  22.0 5.0 %weigh.3 = (bf16[8,2,3,160,128]{4,3,2,1,0:T(8,128)(2,1)}, bf16[8,3,160,128]{3,2,1,0:T(8,128)(2,1)}, f32[8,128]{1,0:T(8,128)}) custom-call(s32[1]{0:T(128)} %bitcast.me_ref, f32[1,160]{1,0:T(1,128)} %bitcast.4, bf16[3,160,32,128]{3,2,1,0:T(8,128)(2,1)} %tendency_ref.3, f32[18,2,1280]{2,1,0:T(2,128)} %copy-done.3), custom_call_target="tpu_custom_call" | custom-call | flops 503316480 | bytes 5898240 | tf_op jit(solution)/shard_map/weigh/pallas_call | solution.py:142
  27.0 0.1 collective-permute-start.1
  27.1 2.8 %collective-permute-done.1.mate_ref = bf16[8,3,160,128]{3,2,1,0:T(8,128)(2,1)S(1)} collective-permute-done((bf16[8,3,160,128]{3,2,1,0:T(8,128)(2,1)}, bf16[8,3,160,128]{3,2,1,0:T(8,128)(2,1)S(1)}, u32[]{:S(2)}, u32[]{:S(2)}) %collective-permute-start.1) | collective-permute-done | bytes 983072 | tf_op jit(solution)/shard_map/ppermute | solution.py:533
  29.8 1.5 copy-done.1
  31.4 0.1 pair.3
  31.5 1.3 copy-done.2
  32.8 21.3 %all-to-all-done.in_ref.rest_0_ = bf16[8,2,3,160,128]{4,3,2,1,0:T(8,128)(2,1)} async-done(((bf16[8,2,3,160,128]{4,3,2,1,0:T(8,128)(2,1)}), bf16[8,2,3,160,128]{4,3,2,1,0:T(8,128)(2,1)}, u32[]{:S(2)}, u32[]{:S(2)}) %all-to-all-start) | async-done | bytes 1966112 | tf_op jit(solution)/shard_map/all_to_all | solution.py:546
  54.1 6.8 %all-to-all-start.2 = ((bf16[8,2,3,160,128]{4,3,2,1,0:T(8,128)(2,1)}), bf16[8,2,3,160,128]{4,3,2,1,0:T(8,128)(2,1)}, u32[]{:S(2)}, u32[]{:S(2)}) async-start(bf16[8,2,3,160,128]{4,3,2,1,0:T(8,128)(2,1)} %copy-done.2), calls=%async_computation.2 | async-start | bytes 3932160 | tf_op jit(solution)/shard_map/all_to_all | solution.py:546
  60.9 1.3 pick.1
  62.2 0.1 collective-permute-start.2
  62.3 2.6 %collective-permute-done.2.rest_1_ = bf16[8,3,160,128]{3,2,1,0:T(8,128)(2,1)S(1)} collective-permute-done((bf16[8,3,160,128]{3,2,1,0:T(8,128)(2,1)S(1)}, bf16[8,3,160,128]{3,2,1,0:T(8,128)(2,1)S(1)}, u32[]{:S(2)}, u32[]{:S(2)}) %collective-permute-start.2) | collective-permute-done | bytes 983072 | tf_op jit(solution)/shard_map/ppermute | solution.py:533
  64.9 5.6 %analyse.3.own_ref = bf16[3,128,640]{2,1,0:T(8,128)(2,1)S(1)} custom-call(s32[1]{0:T(128)} %bitcast.me_ref, s32[2]{0:T(128)S(1)} %copy-done.10, f32[8,128]{1,0:T(8,128)S(1)} %get-tuple-element.35.token_ref, bf16[2,1280,2560]{2,1,0:T(8,128)(2,1)} %table_ref.11, bf16[3,2,128,1280]{3,2,1,0:T(8,128)(2,1)} %state_ref.5, ...), custom_call_target="tpu_custom_call" | custom-call | flops 1258291200 | bytes 3276800 | tf_op jit(solution)/shard_map/analyse/pallas_call | solution.py:293
  70.5 1.6 collective-permute-start.3
  72.0 11.7 %collective-permute-done.3.other_ref = bf16[3,128,640]{2,1,0:T(8,128)(2,1)S(1)} collective-permute-done((bf16[3,128,640]{2,1,0:T(8,128)(2,1)S(1)}, bf16[3,128,640]{2,1,0:T(8,128)(2,1)S(1)}, u32[]{:S(2)}, u32[]{:S(2)}) %collective-permute-start.3) | collective-permute-done | bytes 491552 | tf_op jit(solution)/shard_map/ppermute | solution.py:580
  83.8 5.0 %synthesise.3 = (bf16[8,2,3,160,128]{4,3,2,1,0:T(8,128)(2,1)S(1)}, bf16[8,3,160,128]{3,2,1,0:T(8,128)(2,1)S(1)}) custom-call(s32[1]{0:T(128)} %bitcast.me_ref, f32[1]{0:T(128)} %bitcast.1.sign_ref, f32[18,2,1280]{2,1,0:T(2,128)S(1)} %sum_pairs.1.here_ref, f32[18,2,1280]{2,1,0:T(2,128)S(1)} %copy-done.4, bf16[3,128,640]{2,1,0:T(8,128)(2,1)S(1)} %analyse.3.own_ref, ...), custom_call_target="tpu_custom_call" | custom-call | flops 1258291200 | bytes 3276800 | tf_op jit(solution)/shard_map/synthesise/pallas_call | solution.py:433
  88.8 0.1 collective-permute-start.4
  88.8 2.6 %collective-permute-done.4.mate_ref = bf16[8,3,160,128]{3,2,1,0:T(8,128)(2,1)S(1)} collective-permute-done((bf16[8,3,160,128]{3,2,1,0:T(8,128)(2,1)S(1)}, bf16[8,3,160,128]{3,2,1,0:T(8,128)(2,1)S(1)}, u32[]{:S(2)}, u32[]{:S(2)}) %collective-permute-start.4) | collective-permute-done | bytes 983072 | tf_op jit(solution)/shard_map/ppermute | solution.py:533
  91.4 0.1 pair.4
  91.5 0.0 copy-start
  91.5 1.3 copy-done
  92.8 10.4 %all-to-all-done.2.rest_0_ = bf16[8,2,3,160,128]{4,3,2,1,0:T(8,128)(2,1)} async-done(((bf16[8,2,3,160,128]{4,3,2,1,0:T(8,128)(2,1)}), bf16[8,2,3,160,128]{4,3,2,1,0:T(8,128)(2,1)}, u32[]{:S(2)}, u32[]{:S(2)}) %all-to-all-start.2) | async-done | bytes 1966112 | tf_op jit(solution)/shard_map/all_to_all | solution.py:546
  103.2 6.5 %all-to-all-start.1 = ((bf16[8,2,3,160,128]{4,3,2,1,0:T(8,128)(2,1)}), bf16[8,2,3,160,128]{4,3,2,1,0:T(8,128)(2,1)S(1)}, u32[]{:S(2)}, u32[]{:S(2)}) async-start(bf16[8,2,3,160,128]{4,3,2,1,0:T(8,128)(2,1)} %copy-done), calls=%async_computation.1 | async-start | bytes 3932160 | tf_op jit(solution)/shard_map/all_to_all | solution.py:546
  109.7 5.8 %analyse.5.own_ref = bf16[3,128,640]{2,1,0:T(8,128)(2,1)S(1)} custom-call(s32[1]{0:T(128)} %bitcast.me_ref, s32[2]{0:T(128)S(1)} %copy-done.10, f32[8,128]{1,0:T(8,128)S(1)} %get-tuple-element.40.token_ref, bf16[2,1280,2560]{2,1,0:T(8,128)(2,1)} %table_ref.11, bf16[3,2,128,1280]{3,2,1,0:T(8,128)(2,1)} %state_ref.5, ...), custom_call_target="tpu_custom_call" | custom-call | flops 1258291200 | bytes 3276800 | tf_op jit(solution)/shard_map/analyse/pallas_call | solution.py:293
  115.6 1.6 collective-permute-start.6
  117.1 5.8 %analyse.4.own_ref = bf16[3,128,640]{2,1,0:T(8,128)(2,1)S(1)} custom-call(s32[1]{0:T(128)} %bitcast.me_ref, s32[2]{0:T(128)S(1)} %copy-done.10, f32[8,128]{1,0:T(8,128)S(1)} %get-tuple-element.40.token_ref, bf16[2,1280,2560]{2,1,0:T(8,128)(2,1)} %table_ref.11, bf16[3,2,128,1280]{3,2,1,0:T(8,128)(2,1)} %state_ref.5, ...), custom_call_target="tpu_custom_call" | custom-call | flops 1258291200 | bytes 3276800 | tf_op jit(solution)/shard_map/analyse/pallas_call | solution.py:293
  123.0 0.6 collective-permute-start.5
  123.6 6.2 %collective-permute-done.6.other_ref = bf16[3,128,640]{2,1,0:T(8,128)(2,1)S(1)} collective-permute-done((bf16[3,128,640]{2,1,0:T(8,128)(2,1)S(1)}, bf16[3,128,640]{2,1,0:T(8,128)(2,1)S(1)}, u32[]{:S(2)}, u32[]{:S(2)}) %collective-permute-start.6) | collective-permute-done | bytes 491552 | tf_op jit(solution)/shard_map/ppermute | solution.py:580
  129.8 4.8 %synthesise.4.rest_0_ = f32[384,2560]{1,0:T(8,128)S(1)} custom-call(s32[1]{0:T(128)} %bitcast.me_ref, f32[1]{0:T(128)} %bitcast.1.sign_ref, f32[18,2,1280]{2,1,0:T(2,128)S(1)} %sum_pairs.1.here_ref, f32[18,2,1280]{2,1,0:T(2,128)S(1)} %copy-done.4, bf16[3,128,640]{2,1,0:T(8,128)(2,1)S(1)} %analyse.5.own_ref, ...), custom_call_target="tpu_custom_call" | custom-call | flops 1258291200 | bytes 3276800 | tf_op jit(solution)/shard_map/synthesise/pallas_call | solution.py:433
  134.6 4.1 %collective-permute-done.5.other_ref = bf16[3,128,640]{2,1,0:T(8,128)(2,1)S(1)} collective-permute-done((bf16[3,128,640]{2,1,0:T(8,128)(2,1)S(1)}, bf16[3,128,640]{2,1,0:T(8,128)(2,1)S(1)}, u32[]{:S(2)}, u32[]{:S(2)}) %collective-permute-start.5) | collective-permute-done | bytes 491552 | tf_op jit(solution)/shard_map/ppermute | solution.py:580
  138.7 6.4 %synthesise.5 = (bf16[2,3,160,128]{3,2,1,0:T(8,128)(2,1)S(1)}, bf16[2,3,160,128]{3,2,1,0:T(8,128)(2,1)}, bf16[2,3,160,128]{3,2,1,0:T(8,128)(2,1)}, bf16[2,3,160,...) custom-call(s32[1]{0:T(128)} %bitcast.me_ref, ...), custom_call_target="tpu_custom_call" | custom-call | flops 1258291200 | bytes 3276800 | tf_op jit(solution)/shard_map/synthesise/pallas_call | solution.py:433
  145.2 0.1 collective-permute-start.7
  145.2 2.6 %collective-permute-done.7.mate_ref = bf16[8,3,160,128]{3,2,1,0:T(8,128)(2,1)S(1)} collective-permute-done((bf16[8,3,160,128]{3,2,1,0:T(8,128)(2,1)S(1)}, bf16[8,3,160,128]{3,2,1,0:T(8,128)(2,1)S(1)}, u32[]{:S(2)}, u32[]{:S(2)}) %collective-permute-start.7) | collective-permute-done | bytes 983072 | tf_op jit(solution)/shard_map/ppermute | solution.py:533
  147.8 1.0 pair.5
  148.8 1.5 collective-permute-start.12
  150.3 0.6 collective-permute-start.13
  150.9 1.4 collective-permute-start.14
  152.3 1.7 collective-permute-start.8
  154.0 2.1 %collective-permute-start.9 = (bf16[2,3,160,128]{3,2,1,0:T(8,128)(2,1)}, bf16[2,3,160,128]{3,2,1,0:T(8,128)(2,1)S(1)}, u32[]{:S(2)}, u32[]{:S(2)}) collective-permute-start(bf16[2,3,160,128]{3,2,1,0:T(8,128)(2,1)} %get-tuple-element.52), channel_id=1, source_target_pairs={{0,10},{1,11},{2,8},{3,9},{4,14},{5,15},{6,12},{7,13},{8,2},{9,3},... | collective-permute-start | bytes 737288 | tf_op jit(solution)/shard_map/ppermute | solution.py:540
  156.2 0.7 collective-permute-done.12.rest_1_
  156.9 0.8 collective-permute-start.10
  157.7 9.7 %collective-permute-done.13.rest_2_ = bf16[2,3,160,128]{3,2,1,0:T(8,128)(2,1)S(1)} collective-permute-done((bf16[2,3,160,128]{3,2,1,0:T(8,128)(2,1)S(1)}, bf16[2,3,160,128]{3,2,1,0:T(8,128)(2,1)S(1)}, u32[]{:S(2)}, u32[]{:S(2)}) %collective-permute-start.13) | collective-permute-done | bytes 245792 | tf_op jit(solution)/shard_map/ppermute | solution.py:540
  167.4 0.7 copy-done.6
  168.1 0.0 collective-permute-start.11
  168.1 4.8 %collective-permute-done.14.rest_3_ = bf16[2,3,160,128]{3,2,1,0:T(8,128)(2,1)S(1)} collective-permute-done((bf16[2,3,160,128]{3,2,1,0:T(8,128)(2,1)S(1)}, bf16[2,3,160,128]{3,2,1,0:T(8,128)(2,1)S(1)}, u32[]{:S(2)}, u32[]{:S(2)}) %collective-permute-start.14) | collective-permute-done | bytes 245792 | tf_op jit(solution)/shard_map/ppermute | solution.py:540
  172.9 0.7 copy-done.8
  173.6 0.0 all-to-all-done.1.blocks_ref
  173.6 0.9 copy-done.7
  174.5 0.9 copy-done.9
  175.5 2.7 %assemble.2.rest_4_ = bf16[3,160,32,128]{3,2,1,0:T(8,128)(2,1)} custom-call(s32[1]{0:T(128)} %bitcast.me_ref, bf16[8,2,3,160,128]{4,3,2,1,0:T(8,128)(2,1)S(1)} %all-to-all-done.1.blocks_ref, bf16[2,3,160,128]{3,2,1,0:T(8,128)(2,1)S(1)} %get-tuple-element.55.rest_0_, bf16[2,3,160,128]{3,2,1,0:T(8,128)(2,1)S(1)} %collective-permute-done.12.rest_1_, ...), custom_call_target="tpu_custom_call" | custom-call | flops 503316480 | bytes 3932160 | tf_op jit(solution)/shard_map/assemble/pallas_call | solution.py:514
  178.2 0.0 collective-permute-done.8.rest_0_
  178.2 8.9 %collective-permute-done.9.rest_1_ = bf16[2,3,160,128]{3,2,1,0:T(8,128)(2,1)S(1)} collective-permute-done((bf16[2,3,160,128]{3,2,1,0:T(8,128)(2,1)}, bf16[2,3,160,128]{3,2,1,0:T(8,128)(2,1)S(1)}, u32[]{:S(2)}, u32[]{:S(2)}) %collective-permute-start.9) | collective-permute-done | bytes 245792 | tf_op jit(solution)/shard_map/ppermute | solution.py:540
  187.1 5.7 %collective-permute-done.10.rest_2_ = bf16[2,3,160,128]{3,2,1,0:T(8,128)(2,1)S(1)} collective-permute-done((bf16[2,3,160,128]{3,2,1,0:T(8,128)(2,1)}, bf16[2,3,160,128]{3,2,1,0:T(8,128)(2,1)S(1)}, u32[]{:S(2)}, u32[]{:S(2)}) %collective-permute-start.10) | collective-permute-done | bytes 245792 | tf_op jit(solution)/shard_map/ppermute | solution.py:540
  192.8 4.9 %collective-permute-done.11.rest_3_ = bf16[2,3,160,128]{3,2,1,0:T(8,128)(2,1)} collective-permute-done((bf16[2,3,160,128]{3,2,1,0:T(8,128)(2,1)}, bf16[2,3,160,128]{3,2,1,0:T(8,128)(2,1)}, u32[]{:S(2)}, u32[]{:S(2)}) %collective-permute-start.11) | collective-permute-done | bytes 245792 | tf_op jit(solution)/shard_map/ppermute | solution.py:540
  197.7 3.1 %assemble.3 = bf16[3,160,32,128]{3,2,1,0:T(8,128)(2,1)} custom-call(s32[1]{0:T(128)} %bitcast.me_ref, bf16[8,2,3,160,128]{4,3,2,1,0:T(8,128)(2,1)S(1)} %all-to-all-done.1.blocks_ref, bf16[2,3,160,128]{3,2,1,0:T(8,128)(2,1)S(1)} %collective-permute-done.8.rest_0_, ...), custom_call_target="tpu_custom_call", output_to_operand_aliasing={{}: (6, {})} | custom-call | flops 503316480 | bytes 3932160 | tf_op jit(solution)/shard_map/assemble/pallas_call | solution.py:514
  (14 shorter events, 0.0 us)
Async XLA Ops:
  4.9 6.3 %copy-start.12 = (f32[32,2]{0,1:T(2,128)S(1)}, f32[32,2]{0,1:T(2,128)}, u32[]{:S(2)}) copy-start(f32[32,2]{0,1:T(2,128)} %param.12) | copy-start | bytes 772
  4.9 6.4 %copy-start.11 = (f32[8,128]{1,0:T(8,128)S(1)}, f32[8,128]{1,0:T(8,128)}, u32[]{:S(2)}) copy-start(f32[8,128]{1,0:T(8,128)} %get-tuple-element.32.token_ref) | copy-start | bytes 12292
  4.9 49.2 %all-to-all-start = ((bf16[8,2,3,160,128]{4,3,2,1,0:T(8,128)(2,1)}), bf16[8,2,3,160,128]{4,3,2,1,0:T(8,128)(2,1)}, u32[]{:S(2)}, u32[]{:S(2)}) async-start(bf16[8,2,3,160,128]{4,3,2,1,0:T(8,128)(2,1)} %get-tuple-element.36), calls=%async_computation | async-start | bytes 3932160 | tf_op jit(solution)/shard_map/all_to_all | solution.py:546
  11.3 1.8 copy-start.5
  15.5 5.9 %collective-permute-start = (f32[18,2,1280]{2,1,0:T(2,128)S(1)}, f32[18,2,1280]{2,1,0:T(2,128)S(1)}, u32[]{:S(2)}, u32[]{:S(2)}) collective-permute-start(f32[18,2,1280]{2,1,0:T(2,128)S(1)} %sum_pairs.1.here_ref), channel_id=1, source_target_pairs={{0,16},{16,0},{1,17},{17,1},{2,18},{18,2},{3,19},{19,3},{4,20},{20... | collective-permute-start | bytes 552968 | tf_op jit(solution)/shard_map/ppermute | solution.py:566
  21.3 0.7 copy-start.3
  27.0 2.8 %collective-permute-start.1 = (bf16[8,3,160,128]{3,2,1,0:T(8,128)(2,1)}, bf16[8,3,160,128]{3,2,1,0:T(8,128)(2,1)S(1)}, u32[]{:S(2)}, u32[]{:S(2)}) collective-permute-start(bf16[8,3,160,128]{3,2,1,0:T(8,128)(2,1)} %get-tuple-element.33), channel_id=1, source_target_pairs={{0,1},{1,0},{2,3},{3,2},{4,5},{5,4},{6,7},{7,6},{8,9},{9,8},{10,11... | collective-permute-start | bytes 2949128 | tf_op jit(solution)/shard_map/ppermute | solution.py:533
  29.8 1.5 copy-start.1
  31.5 1.3 copy-start.2
  54.1 49.0 %all-to-all-start.2 = ((bf16[8,2,3,160,128]{4,3,2,1,0:T(8,128)(2,1)}), bf16[8,2,3,160,128]{4,3,2,1,0:T(8,128)(2,1)}, u32[]{:S(2)}, u32[]{:S(2)}) async-start(bf16[8,2,3,160,128]{4,3,2,1,0:T(8,128)(2,1)} %copy-done.2), calls=%async_computation.2 | async-start | bytes 3932160 | tf_op jit(solution)/shard_map/all_to_all | solution.py:546
  60.9 3.9 %copy-start.10 = (s32[2]{0:T(128)S(1)}, s32[2]{0:T(128)}, u32[]{:S(2)}) copy-start(s32[2]{0:T(128)} %wave_ref.5) | copy-start | bytes 28
  62.2 21.6 %copy-start.4 = (f32[18,2,1280]{2,1,0:T(2,128)S(1)}, f32[18,2,1280]{2,1,0:T(2,128)}, u32[]{:S(2)}) copy-start(f32[18,2,1280]{2,1,0:T(2,128)} %copy-done.3) | copy-start | bytes 552964
  62.2 2.6 %collective-permute-start.2 = (bf16[8,3,160,128]{3,2,1,0:T(8,128)(2,1)S(1)}, bf16[8,3,160,128]{3,2,1,0:T(8,128)(2,1)S(1)}, u32[]{:S(2)}, u32[]{:S(2)}) collective-permute-start(bf16[8,3,160,128]{3,2,1,0:T(8,128)(2,1)S(1)} %pick.1), channel_id=1, source_target_pairs={{0,1},{1,0},{2,3},{3,2},{4,5},{5,4},{6,7},{7,6},{8,9},{9,8},{10,11... | collective-permute-start | bytes 2949128 | tf_op jit(solution)/shard_map/ppermute | solution.py:533
  70.5 13.3 %collective-permute-start.3 = (bf16[3,128,640]{2,1,0:T(8,128)(2,1)S(1)}, bf16[3,128,640]{2,1,0:T(8,128)(2,1)S(1)}, u32[]{:S(2)}, u32[]{:S(2)}) collective-permute-start(bf16[3,128,640]{2,1,0:T(8,128)(2,1)S(1)} %analyse.3.own_ref), channel_id=1, source_target_pairs={{0,16},{16,0},{1,17},{17,1},{2,18},{18,2},{3,19},{19,3},{4,20},{20... | collective-permute-start | bytes 1474568 | tf_op jit(solution)/shard_map/ppermute | solution.py:580
  88.8 2.6 %collective-permute-start.4 = (bf16[8,3,160,128]{3,2,1,0:T(8,128)(2,1)S(1)}, bf16[8,3,160,128]{3,2,1,0:T(8,128)(2,1)S(1)}, u32[]{:S(2)}, u32[]{:S(2)}) collective-permute-start(bf16[8,3,160,128]{3,2,1,0:T(8,128)(2,1)S(1)} %get-tuple-element.37), channel_id=1, source_target_pairs={{0,1},{1,0},{2,3},{3,2},{4,5},{5,4},{6,7},{7,6},{8,9},{9,8},{10,11... | collective-permute-start | bytes 2949128 | tf_op jit(solution)/shard_map/ppermute | solution.py:533
  91.5 1.3 copy-start
  103.2 70.4 %all-to-all-start.1 = ((bf16[8,2,3,160,128]{4,3,2,1,0:T(8,128)(2,1)}), bf16[8,2,3,160,128]{4,3,2,1,0:T(8,128)(2,1)S(1)}, u32[]{:S(2)}, u32[]{:S(2)}) async-start(bf16[8,2,3,160,128]{4,3,2,1,0:T(8,128)(2,1)} %copy-done), calls=%async_computation.1 | async-start | bytes 3932160 | tf_op jit(solution)/shard_map/all_to_all | solution.py:546
  115.6 14.2 %collective-permute-start.6 = (bf16[3,128,640]{2,1,0:T(8,128)(2,1)S(1)}, bf16[3,128,640]{2,1,0:T(8,128)(2,1)S(1)}, u32[]{:S(2)}, u32[]{:S(2)}) collective-permute-start(bf16[3,128,640]{2,1,0:T(8,128)(2,1)S(1)} %analyse.5.own_ref), channel_id=1, source_target_pairs={{0,16},{16,0},{1,17},{17,1},{2,18},{18,2},{3,19},{19,3},{4,20},{20... | collective-permute-start | bytes 1474568 | tf_op jit(solution)/shard_map/ppermute | solution.py:580
  123.0 15.8 %collective-permute-start.5 = (bf16[3,128,640]{2,1,0:T(8,128)(2,1)S(1)}, bf16[3,128,640]{2,1,0:T(8,128)(2,1)S(1)}, u32[]{:S(2)}, u32[]{:S(2)}) collective-permute-start(bf16[3,128,640]{2,1,0:T(8,128)(2,1)S(1)} %analyse.4.own_ref), channel_id=1, source_target_pairs={{0,16},{16,0},{1,17},{17,1},{2,18},{18,2},{3,19},{19,3},{4,20},{20... | collective-permute-start | bytes 1474568 | tf_op jit(solution)/shard_map/ppermute | solution.py:580
  145.2 2.6 %collective-permute-start.7 = (bf16[8,3,160,128]{3,2,1,0:T(8,128)(2,1)S(1)}, bf16[8,3,160,128]{3,2,1,0:T(8,128)(2,1)S(1)}, u32[]{:S(2)}, u32[]{:S(2)}) collective-permute-start(bf16[8,3,160,128]{3,2,1,0:T(8,128)(2,1)S(1)} %get-tuple-element.42), channel_id=1, source_target_pairs={{0,1},{1,0},{2,3},{3,2},{4,5},{5,4},{6,7},{7,6},{8,9},{9,8},{10,11... | collective-permute-start | bytes 2949128 | tf_op jit(solution)/shard_map/ppermute | solution.py:533
  148.8 8.1 %collective-permute-start.12 = (bf16[2,3,160,128]{3,2,1,0:T(8,128)(2,1)S(1)}, bf16[2,3,160,128]{3,2,1,0:T(8,128)(2,1)S(1)}, u32[]{:S(2)}, u32[]{:S(2)}) collective-permute-start(bf16[2,3,160,128]{3,2,1,0:T(8,128)(2,1)S(1)} %get-tuple-element.56), channel_id=1, source_target_pairs={{0,2},{1,3},{2,0},{3,1},{4,6},{5,7},{6,4},{7,5},{8,10},{9,11},{10,... | collective-permute-start | bytes 737288 | tf_op jit(solution)/shard_map/ppermute | solution.py:540
  150.3 17.1 %collective-permute-start.13 = (bf16[2,3,160,128]{3,2,1,0:T(8,128)(2,1)S(1)}, bf16[2,3,160,128]{3,2,1,0:T(8,128)(2,1)S(1)}, u32[]{:S(2)}, u32[]{:S(2)}) collective-permute-start(bf16[2,3,160,128]{3,2,1,0:T(8,128)(2,1)S(1)} %get-tuple-element.57), channel_id=1, source_target_pairs={{0,4},{1,5},{2,6},{3,7},{4,0},{5,1},{6,2},{7,3},{8,12},{9,13},{10,... | collective-permute-start | bytes 737288 | tf_op jit(solution)/shard_map/ppermute | solution.py:540
  150.9 22.0 %collective-permute-start.14 = (bf16[2,3,160,128]{3,2,1,0:T(8,128)(2,1)S(1)}, bf16[2,3,160,128]{3,2,1,0:T(8,128)(2,1)S(1)}, u32[]{:S(2)}, u32[]{:S(2)}) collective-permute-start(bf16[2,3,160,128]{3,2,1,0:T(8,128)(2,1)S(1)} %get-tuple-element.58), channel_id=1, source_target_pairs={{0,6},{1,7},{2,4},{3,5},{4,2},{5,3},{6,0},{7,1},{8,14},{9,15},{10,... | collective-permute-start | bytes 737288 | tf_op jit(solution)/shard_map/ppermute | solution.py:540
  152.3 25.9 %collective-permute-start.8 = (bf16[2,3,160,128]{3,2,1,0:T(8,128)(2,1)}, bf16[2,3,160,128]{3,2,1,0:T(8,128)(2,1)S(1)}, u32[]{:S(2)}, u32[]{:S(2)}) collective-permute-start(bf16[2,3,160,128]{3,2,1,0:T(8,128)(2,1)} %get-tuple-element.51), channel_id=1, source_target_pairs={{0,8},{1,9},{2,10},{3,11},{4,12},{5,13},{6,14},{7,15},{8,0},{9,1},... | collective-permute-start | bytes 737288 | tf_op jit(solution)/shard_map/ppermute | solution.py:540
  154.0 33.1 %collective-permute-start.9 = (bf16[2,3,160,128]{3,2,1,0:T(8,128)(2,1)}, bf16[2,3,160,128]{3,2,1,0:T(8,128)(2,1)S(1)}, u32[]{:S(2)}, u32[]{:S(2)}) collective-permute-start(bf16[2,3,160,128]{3,2,1,0:T(8,128)(2,1)} %get-tuple-element.52), channel_id=1, source_target_pairs={{0,10},{1,11},{2,8},{3,9},{4,14},{5,15},{6,12},{7,13},{8,2},{9,3},... | collective-permute-start | bytes 737288 | tf_op jit(solution)/shard_map/ppermute | solution.py:540
  156.9 35.9 %collective-permute-start.10 = (bf16[2,3,160,128]{3,2,1,0:T(8,128)(2,1)}, bf16[2,3,160,128]{3,2,1,0:T(8,128)(2,1)S(1)}, u32[]{:S(2)}, u32[]{:S(2)}) collective-permute-start(bf16[2,3,160,128]{3,2,1,0:T(8,128)(2,1)} %get-tuple-element.53), channel_id=1, source_target_pairs={{0,12},{1,13},{2,14},{3,15},{4,8},{5,9},{6,10},{7,11},{8,4},{9,5},... | collective-permute-start | bytes 737288 | tf_op jit(solution)/shard_map/ppermute | solution.py:540
  167.4 0.7 copy-start.6
  168.1 29.6 %collective-permute-start.11 = (bf16[2,3,160,128]{3,2,1,0:T(8,128)(2,1)}, bf16[2,3,160,128]{3,2,1,0:T(8,128)(2,1)}, u32[]{:S(2)}, u32[]{:S(2)}) collective-permute-start(bf16[2,3,160,128]{3,2,1,0:T(8,128)(2,1)} %get-tuple-element.54), channel_id=1, source_target_pairs={{0,14},{1,15},{2,12},{3,13},{4,10},{5,11},{6,8},{7,9},{8,6},{9,7},... | collective-permute-start | bytes 737288 | tf_op jit(solution)/shard_map/ppermute | solution.py:540
  172.9 0.7 copy-start.8
  173.6 0.9 copy-start.7
  174.5 0.9 copy-start.9

commit v18 on v17

--- a/solution.py
+++ b/solution.py
@@ -39,8 +39,10 @@
         copy.wait()
 
 
-def partners(chips):
-    return [0] + list(range(chips // 2, chips)) + list(range(1, chips // 2))
+def messages_of(chips, rows):
+    near, far = range(1, chips // 2), range(chips // 2, chips)
+    first = [(k, 0, rows - 1) for k in far]
+    return [(0, 0, rows)] + first + [(k, rows - 1, 1) for k in far] + [(k, 0, rows) for k in near]
 
 
 def split_cores(values, core):
@@ -129,7 +131,7 @@
 
 
 def lat_block(lats):
-    return lats // 2 if lats % 32 == 0 else lats
+    return 32 if lats % 32 == 0 else lats
 
 
 def weigh(tendency, gauss, me, slot, local_slots, split, waits):
@@ -213,32 +215,29 @@
     )(me, mate, blocks)
 
 
-def pair_messages_kernel(first, waits, me_ref, mate_ref, *rest):
-    count = (len(rest) - 1 - waits) // 2
-    outs, sems = rest[-1 - count : -1], rest[-1]
+def pair_messages_kernel(me_ref, mate_ref, *rest):
+    outs, sems = rest[len(rest) // 2 : -1], rest[-1]
     chip, other = me_ref[0] // CORES, CORES - 1 - me_ref[0] % CORES
-    wanted = partners(mate_ref.shape[0])[first : first + count]
-    run_copies(
-        [
-            pltpu.make_async_copy(mate_ref.at[chip ^ k], out.at[other], sems.at[i])
-            for i, (k, out) in enumerate(zip(wanted, outs))
-        ]
-    )
-
-
-def pair_messages(messages, mate, me, first, waits):
+    copies = []
+    for i, (k, row, rows) in enumerate(messages_of(*mate_ref.shape[:2])):
+        source = mate_ref.at[chip ^ k, pl.ds(row, rows)]
+        copies.append(pltpu.make_async_copy(source, outs[i].at[other], sems.at[i]))
+    run_copies(copies)
+
+
+def pair_messages(messages, mate, me):
     count = len(messages)
     return call(
-        functools.partial(pair_messages_kernel, first, len(waits)),
+        pair_messages_kernel,
         "pair",
         0,
         4 * mate.size,
         out_shape=[jax.ShapeDtypeStruct(m.shape, m.dtype) for m in messages],
-        in_specs=[IN_SMEM, pl.BlockSpec(mate.shape, lambda: (0, 0, 0, 0))] + [ANYWHERE] * (count + len(waits)),
+        in_specs=[IN_SMEM, pl.BlockSpec(mate.shape, lambda: (0, 0, 0, 0))] + [ANYWHERE] * count,
         out_specs=[ANYWHERE] * count,
         scratch_shapes=[pltpu.SemaphoreType.DMA((count,))],
         input_output_aliases={i + 2: i for i in range(count)},
-    )(me, mate, *messages, *waits)
+    )(me, mate, *messages)
 
 
 def analyse_kernel(slot, low, me_ref, wave_ref, token_ref, table_ref, state_ref, *rest):
@@ -400,8 +399,9 @@
     if apart:
         chip, core = me_ref[0] // CORES, me_ref[0] % CORES
         copies = []
-        for i, (k, out) in enumerate(zip(partners(len(outs)), outs)):
-            copies.append(pltpu.make_async_copy(held.at[chip ^ k], out.at[core], sems.at[i]))
+        for i, (k, row, some) in enumerate(messages_of(held.shape[0], rows)):
+            source = held.at[chip ^ k, pl.ds(row, some)]
+            copies.append(pltpu.make_async_copy(source, outs[i].at[core], sems.at[i]))
             pl.when((chip ^ k) // each == step)(copies[-1].start)
 
         @pl.when(step == pl.num_programs(0) - 1)
@@ -427,9 +427,10 @@
     if more:
         shapes, specs = [jax.ShapeDtypeStruct((rows * members, nlat), F32)], [sums]
     elif apart:
-        shapes[:1] = [jax.ShapeDtypeStruct((CORES, rows, lats, members), BF16)] * chips
-        specs[:1] = [ANYWHERE] * chips
-        scratch += [pltpu.VMEM((chips, rows, lats, members), BF16), pltpu.SemaphoreType.DMA((chips,))]
+        counts = [some for _, _, some in messages_of(chips, rows)]
+        shapes[:1] = [jax.ShapeDtypeStruct((CORES, some, lats, members), BF16) for some in counts]
+        specs[:1] = [ANYWHERE] * len(counts)
+        scratch += [pltpu.VMEM((chips, rows, lats, members), BF16), pltpu.SemaphoreType.DMA((len(counts),))]
     return call(
         functools.partial(synthesise_kernel, slot, low, apart, more, len(partial)),
         "synthesise",
@@ -454,9 +455,10 @@
     )(me, sign, here, there, own, other, table, *partial)
 
 
-def assemble_kernel(far, moved, count, me_ref, blocks_ref, *rest):
-    messages, out_ref, (held, done, in_sems, out_sems) = rest[:count], rest[-5], rest[-4:]
+def assemble_kernel(far, moved, wanted, me_ref, blocks_ref, *rest):
+    messages, out_ref, (held, done, in_sems, out_sems) = rest[: len(wanted)], rest[-5], rest[-4:]
     rows, lats, slots, members = done.shape
+    first = wanted[0][1]
     half = held.shape[0]
     local_slots = slots // half // CORES
     chip = me_ref[0] // CORES
@@ -464,11 +466,10 @@
     each = out_sems.shape[1]
     size = lats // each
     depth, breadth = math.gcd(size, 16), 16
-    wanted = [k for k in partners(2 * half) if (k >= half) == far]
     copies = []
     for r in range(rows):
         copies.append([])
-        for i, (k, ref) in enumerate(zip(wanted, messages)):
+        for i, ((k, _, _), ref) in enumerate(zip(wanted, messages)):
             target = held.at[(chip ^ k) & (half - 1), :, r]
             copies[r].append(pltpu.make_async_copy(ref.at[:, r], target, in_sems.at[r, i]))
             copies[r][-1].start()
@@ -483,7 +484,7 @@
             if slot == moved:
                 parts.append(held[place, owner % CORES, r, start : start + depth, :])
             else:
-                parts.append(blocks_ref[side * half + place, owner % CORES, r, start : start + depth, :])
+                parts.append(blocks_ref[side * half + place, owner % CORES, first + r, start : start + depth, :])
         return jnp.concatenate(parts, axis=0)
 
     for r in range(rows):
@@ -500,44 +501,48 @@
                     value = turned[:, n * members : (n + 1) * members].reshape(depth, breadth, members)
                     done[r, start : start + depth, s : s + breadth, :] = value
             lines = pl.ds(part * size, size)
-            target = out_ref.at[r, lines, pl.ds(pl.multiple_of(side * slots, slots), slots)]
+            target = out_ref.at[first + r, lines, pl.ds(pl.multiple_of(side * slots, slots), slots)]
             results.append(pltpu.make_async_copy(done.at[r, lines], target, out_sems.at[r, part]))
             results[-1].start()
     for copy in results:
         copy.wait()
 
 
-def assemble(blocks, messages, me, moved, local_slots, far, output):
+def assemble(blocks, messages, me, moved, local_slots, far, first, output):
     chips, _, rows, lats, members = blocks.shape
     half = chips // 2
     slots = local_slots * half * CORES
-    return call(
-        functools.partial(assemble_kernel, far, moved, len(messages)),
+    parts = zip(messages_of(chips, rows), messages)
+    parts = [(part, m) for part, m in parts if (part[0] >= half) == far and part[1] == first]
+    wanted, used = [part for part, _ in parts], [m for _, m in parts]
+    some = wanted[0][2]
+    return call(
+        functools.partial(assemble_kernel, far, moved, wanted),
         "assemble",
-        2 * 256 * rows * lats * slots * members,
-        4 * rows * lats * slots * members,
+        2 * 256 * some * lats * slots * members,
+        4 * some * lats * slots * members,
         out_shape=jax.ShapeDtypeStruct((rows, lats, 2 * slots, members), BF16),
-        in_specs=[IN_SMEM, IN_VMEM] + [IN_HBM] * (len(messages) + len(output)),
+        in_specs=[IN_SMEM, IN_VMEM] + [IN_HBM] * (len(used) + len(output)),
         out_specs=IN_HBM,
         scratch_shapes=[
-            pltpu.VMEM((half, CORES, rows, lats, members), BF16),
-            pltpu.VMEM((rows, lats, slots, members), BF16),
-            pltpu.SemaphoreType.DMA((rows, half)),
-            pltpu.SemaphoreType.DMA((rows, lats // lat_block(lats))),
+            pltpu.VMEM((half, CORES, some, lats, members), BF16),
+            pltpu.VMEM((some, lats, slots, members), BF16),
+            pltpu.SemaphoreType.DMA((some, half)),
+            pltpu.SemaphoreType.DMA((some, lats // lat_block(lats))),
         ],
-        input_output_aliases={len(messages) + 2: 0} if output else {},
-    )(me, blocks, *messages, *output)
+        input_output_aliases={len(used) + 2: 0} if output else {},
+    )(me, blocks, *used, *output)
 
 
 def between_cores(blocks, owners):
     return lax.ppermute(blocks, "wave", [(d, d ^ 1) for d in range(owners)])
 
 
-def by_permutes(messages):
-    owners = len(messages) * CORES
-    got = [messages[0]]
-    for k, message in list(zip(partners(len(messages)), messages))[1:]:
-        got.append(lax.ppermute(message, "wave", [(d, d ^ (k * CORES)) for d in range(owners)]))
+def by_permutes(messages, chips, rows):
+    got = []
+    for (k, _, _), message in zip(messages_of(chips, rows), messages):
+        moves = [(d, d ^ (k * CORES)) for d in range(chips * CORES)]
+        got.append(lax.ppermute(message, "wave", moves) if k else message)
     return got
 
 
@@ -586,15 +591,15 @@
         *own, for_mate = own
         mate = between_cores(for_mate, owners)
         if last:
-            own = pair_messages(own, mate, me, 0, [])
-            sent[slot] = by_permutes(own)
+            sent[slot] = by_permutes(pair_messages(own, mate, me), owners // CORES, rows)
         else:
             blocks, token = pair(own[0], mate, me)
             sent[slot] = [between_chips(blocks, owners)]
     blocks, messages = sent[order[0]][0], sent[order[-1]]
-    far = len(messages) // 2 + 1
-    near = assemble(blocks, messages[:1] + messages[far:], me, order[-1], local_slots, False, [])
-    return assemble(blocks, messages[1:far], me, order[-1], local_slots, True, [near])
+    output = []
+    for far, first in ((False, 0), (True, 0), (True, rows - 1)):
+        output = [assemble(blocks, messages, me, order[-1], local_slots, far, first, output)]
+    return output[0]
 
 
 def solution(mesh):

time: 202 us -> 202 us (level)
  waiting for transfers between devices: 103 us -> 92.3 us
  starting transfers between devices: 33.4 us -> 42.7 us
  Pallas kernels: 53.9 us -> 60.3 us
  local copies, waits for them, and re-layouts: 10 us -> 5.22 us
    ppermute x7 -> x11, waiting for transfers between devices: 34.6 us -> 23.3 us  [by_permutes(): got.append(lax.ppermute(message, 'wave', moves) if k else message)]
    ppermute x7 -> x11, starting transfers between devices: 8.21 us -> 17.5 us  [by_permutes(): got.append(lax.ppermute(message, 'wave', moves) if k else message)]
    unnamed x27 -> x23, local copies, waits for them, and re-layouts: 10 us -> 5.22 us
    pallas_call x2, Pallas kernels: 9.87 us -> 12.9 us  [weigh(): call(functools.partial(weigh_kernel, slot, local_slots, split, len(waits)...]
    pallas_call x3 -> x4, Pallas kernels: 6.79 us -> 8.99 us  [the longest x3 7.65 us: assemble(): call(functools.partial(assemble_kernel, far, moved, wanted), 'assemble',...]
  transfers between devices with their start and end apart: 18 -> 22, of which waited for: 16 -> 16; matrix products, arithmetic and copies ran while one was open for 0% -> 0% of each run, Pallas kernels for 23% -> 26%
where the time goes in v18:
time: 202 us; the launch traced here: 201 us
  waiting for transfers between devices  92.3 us (46%)
  Pallas kernels  60.3 us (30%)
  starting transfers between devices  42.7 us (21%)
  local copies, waits for them, and re-layouts  5.22 us (3%)
    all_to_all x3, waiting for transfers between devices, between_chips(): lax.all_to_all(blocks, 'wave', split_axis=0, concat_axis=0, axis_index_gr...  32.3 us
    ppermute x11, waiting for transfers between devices, by_permutes(): got.append(lax.ppermute(message, 'wave', moves) if k else message)  23.3 us
    ppermute x3, waiting for transfers between devices, per_device(): others = [lax.ppermute(part, 'pole', [(0, 1), (1, 0)]) for part in forced]  22.1 us
    all_to_all x3, starting transfers between devices, between_chips(): lax.all_to_all(blocks, 'wave', split_axis=0, concat_axis=0, axis_index_gr...  19.6 us
    ppermute x11, starting transfers between devices, by_permutes(): got.append(lax.ppermute(message, 'wave', moves) if k else message)  17.5 us
    pallas_call x3, Pallas kernels, analyse(): call(functools.partial(analyse_kernel, slot, low), 'analyse', 2 * width *...  17.3 us
    pallas_call x3, Pallas kernels, synthesise(): call(functools.partial(synthesise_kernel, slot, low, apart, more, len(par...  16.5 us
    pallas_call x2, Pallas kernels, weigh(): call(functools.partial(weigh_kernel, slot, local_slots, split, len(waits)...  12.9 us
  transfers between devices with their start and end apart: 22, of which 16 were waited for; matrix products, arithmetic and copies ran while one was open for 0% of the time, Pallas kernels for 26%

profile of v18, /device:TPU:8, one launch (start us, length us, event | category | flops | bytes accessed | tf_op | source)
XLA Modules:
  0.0 201.0 jit_solution(10758838986720458822)
XLA Ops:
  0.0 6.4 %weigh.2 = (bf16[8,2,3,160,128]{4,3,2,1,0:T(8,128)(2,1)}, f32[8,128]{1,0:T(8,128)}) custom-call(s32[1]{0:T(128)} %bitcast.me_ref, f32[1,160]{1,0:T(1,128)} %bitcast.3, bf16[3,160,32,128]{3,2,1,0:T(8,128)(2,1)} %tendency_ref.3), custom_call_target="tpu_custom_call" | custom-call | flops 503316480 | bytes 5898240 | tf_op jit(solution)/shard_map/weigh/pallas_call | solution.py:144
  6.4 0.0 copy-start.10
  6.5 6.3 %all-to-all-start = ((bf16[8,2,3,160,128]{4,3,2,1,0:T(8,128)(2,1)}), bf16[8,2,3,160,128]{4,3,2,1,0:T(8,128)(2,1)}, u32[]{:S(2)}, u32[]{:S(2)}) async-start(bf16[8,2,3,160,128]{4,3,2,1,0:T(8,128)(2,1)} %get-tuple-element.44), calls=%async_computation | async-start | bytes 3932160 | tf_op jit(solution)/shard_map/all_to_all | solution.py:551
  12.7 0.1 copy.24.coeff_ref
  12.8 1.8 copy-done.3
  14.6 2.4 %sum_pairs.1.here_ref = f32[18,2,1280]{2,1,0:T(2,128)S(1)} custom-call(f32[32,2]{1,0:T(8,128)S(1)} %copy.24.coeff_ref, f32[8,128]{1,0:T(8,128)S(1)} %copy-done.9, bf16[32,18,2,1280]{3,2,1,0:T(2,128)(2,1)S(1)} %copy-done.3), custom_call_target="tpu_custom_call" | custom-call | flops 5898240 | bytes 2949120 | tf_op jit(solution)/shard_map/sum_pairs/pallas_call | solution.py:334
  17.0 1.6 collective-permute-start
  18.6 4.3 %collective-permute-done.rest_0_.there_ref = f32[18,2,1280]{2,1,0:T(2,128)S(1)} collective-permute-done((f32[18,2,1280]{2,1,0:T(2,128)S(1)}, f32[18,2,1280]{2,1,0:T(2,128)S(1)}, u32[]{:S(2)}, u32[]{:S(2)}) %collective-permute-start) | collective-permute-done | bytes 184352 | tf_op jit(solution)/shard_map/ppermute | solution.py:571
  22.9 0.7 copy-done.1
  23.6 6.5 %weigh.3 = (bf16[8,2,3,160,128]{4,3,2,1,0:T(8,128)(2,1)}, bf16[8,3,160,128]{3,2,1,0:T(8,128)(2,1)}, f32[8,128]{1,0:T(8,128)}) custom-call(s32[1]{0:T(128)} %bitcast.me_ref, f32[1,160]{1,0:T(1,128)} %bitcast.4, bf16[3,160,32,128]{3,2,1,0:T(8,128)(2,1)} %tendency_ref.3, f32[18,2,1280]{2,1,0:T(2,128)} %copy-done.1), custom_call_target="tpu_custom_call" | custom-call | flops 503316480 | bytes 5898240 | tf_op jit(solution)/shard_map/weigh/pallas_call | solution.py:144
  30.0 0.1 collective-permute-start.1
  30.1 2.8 %collective-permute-done.1.mate_ref = bf16[8,3,160,128]{3,2,1,0:T(8,128)(2,1)S(1)} collective-permute-done((bf16[8,3,160,128]{3,2,1,0:T(8,128)(2,1)}, bf16[8,3,160,128]{3,2,1,0:T(8,128)(2,1)S(1)}, u32[]{:S(2)}, u32[]{:S(2)}) %collective-permute-start.1) | collective-permute-done | bytes 983072 | tf_op jit(solution)/shard_map/ppermute | solution.py:538
  32.9 0.9 pair.3
  33.8 21.9 %all-to-all-done.in_ref.rest_0_ = bf16[8,2,3,160,128]{4,3,2,1,0:T(8,128)(2,1)} async-done(((bf16[8,2,3,160,128]{4,3,2,1,0:T(8,128)(2,1)}), bf16[8,2,3,160,128]{4,3,2,1,0:T(8,128)(2,1)}, u32[]{:S(2)}, u32[]{:S(2)}) %all-to-all-start) | async-done | bytes 1966112 | tf_op jit(solution)/shard_map/all_to_all | solution.py:551
  55.7 6.8 %all-to-all-start.2 = ((bf16[8,2,3,160,128]{4,3,2,1,0:T(8,128)(2,1)}), bf16[8,2,3,160,128]{4,3,2,1,0:T(8,128)(2,1)}, u32[]{:S(2)}, u32[]{:S(2)}) async-start(bf16[8,2,3,160,128]{4,3,2,1,0:T(8,128)(2,1)} %get-tuple-element.49), calls=%async_computation.2 | async-start | bytes 3932160 | tf_op jit(solution)/shard_map/all_to_all | solution.py:551
  62.5 1.3 pick.1
  63.8 0.1 collective-permute-start.2
  63.9 2.6 %collective-permute-done.2.rest_1_ = bf16[8,3,160,128]{3,2,1,0:T(8,128)(2,1)S(1)} collective-permute-done((bf16[8,3,160,128]{3,2,1,0:T(8,128)(2,1)S(1)}, bf16[8,3,160,128]{3,2,1,0:T(8,128)(2,1)S(1)}, u32[]{:S(2)}, u32[]{:S(2)}) %collective-permute-start.2) | collective-permute-done | bytes 983072 | tf_op jit(solution)/shard_map/ppermute | solution.py:538
  66.4 5.6 %analyse.3.own_ref = bf16[3,128,640]{2,1,0:T(8,128)(2,1)S(1)} custom-call(s32[1]{0:T(128)} %bitcast.me_ref, s32[2]{0:T(128)S(1)} %copy-done.8, f32[8,128]{1,0:T(8,128)S(1)} %get-tuple-element.43.token_ref, bf16[2,1280,2560]{2,1,0:T(8,128)(2,1)} %table_ref.11, bf16[3,2,128,1280]{3,2,1,0:T(8,128)(2,1)} %state_ref.5, ...), custom_call_target="tpu_custom_call" | custom-call | flops 1258291200 | bytes 3276800 | tf_op jit(solution)/shard_map/analyse/pallas_call | solution.py:292
  72.0 1.6 collective-permute-start.3
  73.6 11.7 %collective-permute-done.3.other_ref = bf16[3,128,640]{2,1,0:T(8,128)(2,1)S(1)} collective-permute-done((bf16[3,128,640]{2,1,0:T(8,128)(2,1)S(1)}, bf16[3,128,640]{2,1,0:T(8,128)(2,1)S(1)}, u32[]{:S(2)}, u32[]{:S(2)}) %collective-permute-start.3) | collective-permute-done | bytes 491552 | tf_op jit(solution)/shard_map/ppermute | solution.py:585
  85.3 4.9 %synthesise.3 = (bf16[8,2,3,160,128]{4,3,2,1,0:T(8,128)(2,1)S(1)}, bf16[8,3,160,128]{3,2,1,0:T(8,128)(2,1)S(1)}) custom-call(s32[1]{0:T(128)} %bitcast.me_ref, f32[1]{0:T(128)} %bitcast.1.sign_ref, f32[18,2,1280]{2,1,0:T(2,128)S(1)} %sum_pairs.1.here_ref, f32[18,2,1280]{2,1,0:T(2,128)S(1)} %copy-done.2, bf16[3,128,640]{2,1,0:T(8,128)(2,1)S(1)} %analyse.3.own_ref, ...), custom_call_target="tpu_custom_call" | custom-call | flops 1258291200 | bytes 3276800 | tf_op jit(solution)/shard_map/synthesise/pallas_call | solution.py:434
  90.3 0.1 collective-permute-start.4
  90.4 2.6 %collective-permute-done.4.mate_ref = bf16[8,3,160,128]{3,2,1,0:T(8,128)(2,1)S(1)} collective-permute-done((bf16[8,3,160,128]{3,2,1,0:T(8,128)(2,1)S(1)}, bf16[8,3,160,128]{3,2,1,0:T(8,128)(2,1)S(1)}, u32[]{:S(2)}, u32[]{:S(2)}) %collective-permute-start.4) | collective-permute-done | bytes 983072 | tf_op jit(solution)/shard_map/ppermute | solution.py:538
  92.9 0.1 pair.4
  93.0 0.0 copy-start
  93.0 1.3 copy-done
  94.3 10.4 %all-to-all-done.2.rest_0_ = bf16[8,2,3,160,128]{4,3,2,1,0:T(8,128)(2,1)} async-done(((bf16[8,2,3,160,128]{4,3,2,1,0:T(8,128)(2,1)}), bf16[8,2,3,160,128]{4,3,2,1,0:T(8,128)(2,1)}, u32[]{:S(2)}, u32[]{:S(2)}) %all-to-all-start.2) | async-done | bytes 1966112 | tf_op jit(solution)/shard_map/all_to_all | solution.py:551
  104.7 6.5 %all-to-all-start.1 = ((bf16[8,2,3,160,128]{4,3,2,1,0:T(8,128)(2,1)}), bf16[8,2,3,160,128]{4,3,2,1,0:T(8,128)(2,1)S(1)}, u32[]{:S(2)}, u32[]{:S(2)}) async-start(bf16[8,2,3,160,128]{4,3,2,1,0:T(8,128)(2,1)} %copy-done), calls=%async_computation.1 | async-start | bytes 3932160 | tf_op jit(solution)/shard_map/all_to_all | solution.py:551
  111.2 5.8 %analyse.5.own_ref = bf16[3,128,640]{2,1,0:T(8,128)(2,1)S(1)} custom-call(s32[1]{0:T(128)} %bitcast.me_ref, s32[2]{0:T(128)S(1)} %copy-done.8, f32[8,128]{1,0:T(8,128)S(1)} %get-tuple-element.48.token_ref, bf16[2,1280,2560]{2,1,0:T(8,128)(2,1)} %table_ref.11, bf16[3,2,128,1280]{3,2,1,0:T(8,128)(2,1)} %state_ref.5, ...), custom_call_target="tpu_custom_call" | custom-call | flops 1258291200 | bytes 3276800 | tf_op jit(solution)/shard_map/analyse/pallas_call | solution.py:292
  117.1 1.6 collective-permute-start.6
  118.7 5.8 %analyse.4.own_ref = bf16[3,128,640]{2,1,0:T(8,128)(2,1)S(1)} custom-call(s32[1]{0:T(128)} %bitcast.me_ref, s32[2]{0:T(128)S(1)} %copy-done.8, f32[8,128]{1,0:T(8,128)S(1)} %get-tuple-element.48.token_ref, bf16[2,1280,2560]{2,1,0:T(8,128)(2,1)} %table_ref.11, bf16[3,2,128,1280]{3,2,1,0:T(8,128)(2,1)} %state_ref.5, ...), custom_call_target="tpu_custom_call" | custom-call | flops 1258291200 | bytes 3276800 | tf_op jit(solution)/shard_map/analyse/pallas_call | solution.py:292
  124.5 0.6 collective-permute-start.5
  125.1 6.2 %collective-permute-done.6.other_ref = bf16[3,128,640]{2,1,0:T(8,128)(2,1)S(1)} collective-permute-done((bf16[3,128,640]{2,1,0:T(8,128)(2,1)S(1)}, bf16[3,128,640]{2,1,0:T(8,128)(2,1)S(1)}, u32[]{:S(2)}, u32[]{:S(2)}) %collective-permute-start.6) | collective-permute-done | bytes 491552 | tf_op jit(solution)/shard_map/ppermute | solution.py:585
  131.3 4.8 %synthesise.4.rest_0_ = f32[384,2560]{1,0:T(8,128)S(1)} custom-call(s32[1]{0:T(128)} %bitcast.me_ref, f32[1]{0:T(128)} %bitcast.1.sign_ref, f32[18,2,1280]{2,1,0:T(2,128)S(1)} %sum_pairs.1.here_ref, f32[18,2,1280]{2,1,0:T(2,128)S(1)} %copy-done.2, bf16[3,128,640]{2,1,0:T(8,128)(2,1)S(1)} %analyse.5.own_ref, ...), custom_call_target="tpu_custom_call" | custom-call | flops 1258291200 | bytes 3276800 | tf_op jit(solution)/shard_map/synthesise/pallas_call | solution.py:434
  136.2 4.1 %collective-permute-done.5.other_ref = bf16[3,128,640]{2,1,0:T(8,128)(2,1)S(1)} collective-permute-done((bf16[3,128,640]{2,1,0:T(8,128)(2,1)S(1)}, bf16[3,128,640]{2,1,0:T(8,128)(2,1)S(1)}, u32[]{:S(2)}, u32[]{:S(2)}) %collective-permute-start.5) | collective-permute-done | bytes 491552 | tf_op jit(solution)/shard_map/ppermute | solution.py:585
  140.3 6.7 %synthesise.5 = (bf16[2,3,160,128]{3,2,1,0:T(8,128)(2,1)S(1)}, bf16[2,2,160,128]{3,2,1,0:T(8,128)(2,1)S(1)}, bf16[2,2,160,128]{3,2,1,0:T(8,128)(2,1)S(1)}, bf16[...) custom-call(s32[1]{0:T(128)} %bitcast.me_ref, ...), custom_call_target="tpu_custom_call" | custom-call | flops 1258291200 | bytes 3276800 | tf_op jit(solution)/shard_map/synthesise/pallas_call | solution.py:434
  147.0 0.1 collective-permute-start.7
  147.1 2.6 %collective-permute-done.7.mate_ref = bf16[8,3,160,128]{3,2,1,0:T(8,128)(2,1)S(1)} collective-permute-done((bf16[8,3,160,128]{3,2,1,0:T(8,128)(2,1)S(1)}, bf16[8,3,160,128]{3,2,1,0:T(8,128)(2,1)S(1)}, u32[]{:S(2)}, u32[]{:S(2)}) %collective-permute-start.7) | collective-permute-done | bytes 983072 | tf_op jit(solution)/shard_map/ppermute | solution.py:538
  149.6 1.3 pair.5
  151.0 1.8 collective-permute-start.12
  152.8 2.1 %collective-permute-start.13 = (bf16[2,2,160,128]{3,2,1,0:T(8,128)(2,1)S(1)}, bf16[2,2,160,128]{3,2,1,0:T(8,128)(2,1)S(1)}, u32[]{:S(2)}, u32[]{:S(2)}) collective-permute-start(bf16[2,2,160,128]{3,2,1,0:T(8,128)(2,1)S(1)} %get-tuple-element.68), channel_id=1, source_target_pairs={{0,10},{1,11},{2,8},{3,9},{4,14},{5,15},{6,12},{7,13},{8,2},{9,3},... | collective-permute-start | bytes 491528 | tf_op jit(solution)/shard_map/ppermute | solution.py:545
  154.9 0.6 collective-permute-start.16
  155.4 0.3 collective-permute-start.17
  155.7 2.6 %collective-permute-start.18 = (bf16[2,3,160,128]{3,2,1,0:T(8,128)(2,1)S(1)}, bf16[2,3,160,128]{3,2,1,0:T(8,128)(2,1)S(1)}, u32[]{:S(2)}, u32[]{:S(2)}) collective-permute-start(bf16[2,3,160,128]{3,2,1,0:T(8,128)(2,1)S(1)} %get-tuple-element.74), channel_id=1, source_target_pairs={{0,6},{1,7},{2,4},{3,5},{4,2},{5,3},{6,0},{7,1},{8,14},{9,15},{10,... | collective-permute-start | bytes 737288 | tf_op jit(solution)/shard_map/ppermute | solution.py:545
  158.3 6.6 %collective-permute-done.12.rest_0_ = bf16[2,2,160,128]{3,2,1,0:T(8,128)(2,1)S(1)} collective-permute-done((bf16[2,2,160,128]{3,2,1,0:T(8,128)(2,1)S(1)}, bf16[2,2,160,128]{3,2,1,0:T(8,128)(2,1)S(1)}, u32[]{:S(2)}, u32[]{:S(2)}) %collective-permute-start.12) | collective-permute-done | bytes 163872 | tf_op jit(solution)/shard_map/ppermute | solution.py:545
  165.0 1.8 collective-permute-start.14
  166.8 1.7 collective-permute-done.13.rest_1_
  168.5 0.7 copy-done.4
  169.1 2.5 %collective-permute-start.15 = (bf16[2,2,160,128]{3,2,1,0:T(8,128)(2,1)S(1)}, bf16[2,2,160,128]{3,2,1,0:T(8,128)(2,1)}, u32[]{:S(2)}, u32[]{:S(2)}) collective-permute-start(bf16[2,2,160,128]{3,2,1,0:T(8,128)(2,1)S(1)} %get-tuple-element.70), channel_id=1, source_target_pairs={{0,14},{1,15},{2,12},{3,13},{4,10},{5,11},{6,8},{7,9},{8,6},{9,7},... | collective-permute-start | bytes 491528 | tf_op jit(solution)/shard_map/ppermute | solution.py:545
  171.6 9.6 %collective-permute-done.14.rest_2_ = bf16[2,2,160,128]{3,2,1,0:T(8,128)(2,1)S(1)} collective-permute-done((bf16[2,2,160,128]{3,2,1,0:T(8,128)(2,1)S(1)}, bf16[2,2,160,128]{3,2,1,0:T(8,128)(2,1)S(1)}, u32[]{:S(2)}, u32[]{:S(2)}) %collective-permute-start.14) | collective-permute-done | bytes 163872 | tf_op jit(solution)/shard_map/ppermute | solution.py:545
  181.3 0.7 copy-done.6
  182.0 0.0 collective-permute-done.16.rest_1_
  182.0 4.5 %collective-permute-start.9 = (bf16[2,1,160,128]{3,2,1,0:T(8,128)(2,1)}, bf16[2,1,160,128]{3,2,1,0:T(8,128)(2,1)S(1)}, u32[]{:S(2)}, u32[]{:S(2)}) collective-permute-start(bf16[2,1,160,128]{3,2,1,0:T(8,128)(2,1)} %get-tuple-element.64), channel_id=1, source_target_pairs={{0,10},{1,11},{2,8},{3,9},{4,14},{5,15},{6,12},{7,13},{8,2},{9,3},... | collective-permute-start | bytes 245768 | tf_op jit(solution)/shard_map/ppermute | solution.py:545
  186.4 0.0 collective-permute-done.17.rest_2_
  186.4 0.0 collective-permute-start.10
  186.4 0.0 collective-permute-done.18.rest_3_
  186.4 1.4 collective-permute-start.11
  187.8 2.7 %assemble.3.rest_4_ = bf16[3,160,32,128]{3,2,1,0:T(8,128)(2,1)} custom-call(s32[1]{0:T(128)} %bitcast.me_ref, bf16[8,2,3,160,128]{4,3,2,1,0:T(8,128)(2,1)S(1)} %all-to-all-done.1.blocks_ref, bf16[2,3,160,128]{3,2,1,0:T(8,128)(2,1)S(1)} %get-tuple-element.71.rest_0_, bf16[2,3,160,128]{3,2,1,0:T(8,128)(2,1)S(1)} %collective-permute-done.16.rest_1_, ...), custom_call_target="tpu_custom_call" | custom-call | flops 503316480 | bytes 3932160 | tf_op jit(solution)/shard_map/assemble/pallas_call | solution.py:519
  190.6 2.7 %assemble.4.rest_4_ = bf16[3,160,32,128]{3,2,1,0:T(8,128)(2,1)} custom-call(s32[1]{0:T(128)} %bitcast.me_ref, bf16[8,2,3,160,128]{4,3,2,1,0:T(8,128)(2,1)S(1)} %all-to-all-done.1.blocks_ref, bf16[2,2,160,128]{3,2,1,0:T(8,128)(2,1)S(1)} %collective-permute-done.12.rest_0_, bf16[2,2,160,128]{3,2,1,0:T(8,128)(2,1)S(1)} %copy-done.5, ...), custom_call_target="tpu_custom_call", output_to_operand_aliasing={{}: (6, {})} | custom-call | flops 335544320 | bytes 2621440 | tf_op jit(solution)/shard_map/assemble/pallas_call | solution.py:519
  193.3 0.7 collective-permute-done.9.rest_1_
  193.9 2.4 %collective-permute-done.10.rest_2_ = bf16[2,1,160,128]{3,2,1,0:T(8,128)(2,1)} collective-permute-done((bf16[2,1,160,128]{3,2,1,0:T(8,128)(2,1)}, bf16[2,1,160,128]{3,2,1,0:T(8,128)(2,1)}, u32[]{:S(2)}, u32[]{:S(2)}) %collective-permute-start.10) | collective-permute-done | bytes 81952 | tf_op jit(solution)/shard_map/ppermute | solution.py:545
  196.3 2.3 %collective-permute-done.11.rest_3_ = bf16[2,1,160,128]{3,2,1,0:T(8,128)(2,1)} collective-permute-done((bf16[2,1,160,128]{3,2,1,0:T(8,128)(2,1)}, bf16[2,1,160,128]{3,2,1,0:T(8,128)(2,1)}, u32[]{:S(2)}, u32[]{:S(2)}) %collective-permute-start.11) | collective-permute-done | bytes 81952 | tf_op jit(solution)/shard_map/ppermute | solution.py:545
  198.6 2.2 %assemble.5 = bf16[3,160,32,128]{3,2,1,0:T(8,128)(2,1)} custom-call(s32[1]{0:T(128)} %bitcast.me_ref, bf16[8,2,3,160,128]{4,3,2,1,0:T(8,128)(2,1)S(1)} %all-to-all-done.1.blocks_ref, bf16[2,1,160,128]{3,2,1,0:T(8,128)(2,1)S(1)} %collective-permute-done.8.rest_0_, ...), custom_call_target="tpu_custom_call", output_to_operand_aliasing={{}: (6, {})} | custom-call | flops 167772160 | bytes 1310720 | tf_op jit(solution)/shard_map/assemble/pallas_call | solution.py:519
  (19 shorter events, 0.0 us)
Async XLA Ops:
  6.4 6.3 %copy-start.10 = (f32[32,2]{0,1:T(2,128)S(1)}, f32[32,2]{0,1:T(2,128)}, u32[]{:S(2)}) copy-start(f32[32,2]{0,1:T(2,128)} %param.12) | copy-start | bytes 772
  6.4 6.4 %copy-start.9 = (f32[8,128]{1,0:T(8,128)S(1)}, f32[8,128]{1,0:T(8,128)}, u32[]{:S(2)}) copy-start(f32[8,128]{1,0:T(8,128)} %get-tuple-element.40.token_ref) | copy-start | bytes 12292
  6.5 49.2 %all-to-all-start = ((bf16[8,2,3,160,128]{4,3,2,1,0:T(8,128)(2,1)}), bf16[8,2,3,160,128]{4,3,2,1,0:T(8,128)(2,1)}, u32[]{:S(2)}, u32[]{:S(2)}) async-start(bf16[8,2,3,160,128]{4,3,2,1,0:T(8,128)(2,1)} %get-tuple-element.44), calls=%async_computation | async-start | bytes 3932160 | tf_op jit(solution)/shard_map/all_to_all | solution.py:551
  12.8 1.8 copy-start.3
  17.0 5.9 %collective-permute-start = (f32[18,2,1280]{2,1,0:T(2,128)S(1)}, f32[18,2,1280]{2,1,0:T(2,128)S(1)}, u32[]{:S(2)}, u32[]{:S(2)}) collective-permute-start(f32[18,2,1280]{2,1,0:T(2,128)S(1)} %sum_pairs.1.here_ref), channel_id=1, source_target_pairs={{0,16},{16,0},{1,17},{17,1},{2,18},{18,2},{3,19},{19,3},{4,20},{20... | collective-permute-start | bytes 552968 | tf_op jit(solution)/shard_map/ppermute | solution.py:571
  22.9 0.7 copy-start.1
  30.0 2.8 %collective-permute-start.1 = (bf16[8,3,160,128]{3,2,1,0:T(8,128)(2,1)}, bf16[8,3,160,128]{3,2,1,0:T(8,128)(2,1)S(1)}, u32[]{:S(2)}, u32[]{:S(2)}) collective-permute-start(bf16[8,3,160,128]{3,2,1,0:T(8,128)(2,1)} %get-tuple-element.41), channel_id=1, source_target_pairs={{0,1},{1,0},{2,3},{3,2},{4,5},{5,4},{6,7},{7,6},{8,9},{9,8},{10,11... | collective-permute-start | bytes 2949128 | tf_op jit(solution)/shard_map/ppermute | solution.py:538
  55.7 49.0 %all-to-all-start.2 = ((bf16[8,2,3,160,128]{4,3,2,1,0:T(8,128)(2,1)}), bf16[8,2,3,160,128]{4,3,2,1,0:T(8,128)(2,1)}, u32[]{:S(2)}, u32[]{:S(2)}) async-start(bf16[8,2,3,160,128]{4,3,2,1,0:T(8,128)(2,1)} %get-tuple-element.49), calls=%async_computation.2 | async-start | bytes 3932160 | tf_op jit(solution)/shard_map/all_to_all | solution.py:551
  62.5 3.9 %copy-start.8 = (s32[2]{0:T(128)S(1)}, s32[2]{0:T(128)}, u32[]{:S(2)}) copy-start(s32[2]{0:T(128)} %wave_ref.5) | copy-start | bytes 28
  63.8 21.6 %copy-start.2 = (f32[18,2,1280]{2,1,0:T(2,128)S(1)}, f32[18,2,1280]{2,1,0:T(2,128)}, u32[]{:S(2)}) copy-start(f32[18,2,1280]{2,1,0:T(2,128)} %copy-done.1) | copy-start | bytes 552964
  63.8 2.6 %collective-permute-start.2 = (bf16[8,3,160,128]{3,2,1,0:T(8,128)(2,1)S(1)}, bf16[8,3,160,128]{3,2,1,0:T(8,128)(2,1)S(1)}, u32[]{:S(2)}, u32[]{:S(2)}) collective-permute-start(bf16[8,3,160,128]{3,2,1,0:T(8,128)(2,1)S(1)} %pick.1), channel_id=1, source_target_pairs={{0,1},{1,0},{2,3},{3,2},{4,5},{5,4},{6,7},{7,6},{8,9},{9,8},{10,11... | collective-permute-start | bytes 2949128 | tf_op jit(solution)/shard_map/ppermute | solution.py:538
  72.0 13.3 %collective-permute-start.3 = (bf16[3,128,640]{2,1,0:T(8,128)(2,1)S(1)}, bf16[3,128,640]{2,1,0:T(8,128)(2,1)S(1)}, u32[]{:S(2)}, u32[]{:S(2)}) collective-permute-start(bf16[3,128,640]{2,1,0:T(8,128)(2,1)S(1)} %analyse.3.own_ref), channel_id=1, source_target_pairs={{0,16},{16,0},{1,17},{17,1},{2,18},{18,2},{3,19},{19,3},{4,20},{20... | collective-permute-start | bytes 1474568 | tf_op jit(solution)/shard_map/ppermute | solution.py:585
  90.3 2.6 %collective-permute-start.4 = (bf16[8,3,160,128]{3,2,1,0:T(8,128)(2,1)S(1)}, bf16[8,3,160,128]{3,2,1,0:T(8,128)(2,1)S(1)}, u32[]{:S(2)}, u32[]{:S(2)}) collective-permute-start(bf16[8,3,160,128]{3,2,1,0:T(8,128)(2,1)S(1)} %get-tuple-element.45), channel_id=1, source_target_pairs={{0,1},{1,0},{2,3},{3,2},{4,5},{5,4},{6,7},{7,6},{8,9},{9,8},{10,11... | collective-permute-start | bytes 2949128 | tf_op jit(solution)/shard_map/ppermute | solution.py:538
  93.0 1.3 copy-start
  104.7 83.1 %all-to-all-start.1 = ((bf16[8,2,3,160,128]{4,3,2,1,0:T(8,128)(2,1)}), bf16[8,2,3,160,128]{4,3,2,1,0:T(8,128)(2,1)S(1)}, u32[]{:S(2)}, u32[]{:S(2)}) async-start(bf16[8,2,3,160,128]{4,3,2,1,0:T(8,128)(2,1)} %copy-done), calls=%async_computation.1 | async-start | bytes 3932160 | tf_op jit(solution)/shard_map/all_to_all | solution.py:551
  117.1 14.2 %collective-permute-start.6 = (bf16[3,128,640]{2,1,0:T(8,128)(2,1)S(1)}, bf16[3,128,640]{2,1,0:T(8,128)(2,1)S(1)}, u32[]{:S(2)}, u32[]{:S(2)}) collective-permute-start(bf16[3,128,640]{2,1,0:T(8,128)(2,1)S(1)} %analyse.5.own_ref), channel_id=1, source_target_pairs={{0,16},{16,0},{1,17},{17,1},{2,18},{18,2},{3,19},{19,3},{4,20},{20... | collective-permute-start | bytes 1474568 | tf_op jit(solution)/shard_map/ppermute | solution.py:585
  124.5 15.7 %collective-permute-start.5 = (bf16[3,128,640]{2,1,0:T(8,128)(2,1)S(1)}, bf16[3,128,640]{2,1,0:T(8,128)(2,1)S(1)}, u32[]{:S(2)}, u32[]{:S(2)}) collective-permute-start(bf16[3,128,640]{2,1,0:T(8,128)(2,1)S(1)} %analyse.4.own_ref), channel_id=1, source_target_pairs={{0,16},{16,0},{1,17},{17,1},{2,18},{18,2},{3,19},{19,3},{4,20},{20... | collective-permute-start | bytes 1474568 | tf_op jit(solution)/shard_map/ppermute | solution.py:585
  147.0 2.6 %collective-permute-start.7 = (bf16[8,3,160,128]{3,2,1,0:T(8,128)(2,1)S(1)}, bf16[8,3,160,128]{3,2,1,0:T(8,128)(2,1)S(1)}, u32[]{:S(2)}, u32[]{:S(2)}) collective-permute-start(bf16[8,3,160,128]{3,2,1,0:T(8,128)(2,1)S(1)} %get-tuple-element.50), channel_id=1, source_target_pairs={{0,1},{1,0},{2,3},{3,2},{4,5},{5,4},{6,7},{7,6},{8,9},{9,8},{10,11... | collective-permute-start | bytes 2949128 | tf_op jit(solution)/shard_map/ppermute | solution.py:538
  151.0 14.0 %collective-permute-start.12 = (bf16[2,2,160,128]{3,2,1,0:T(8,128)(2,1)S(1)}, bf16[2,2,160,128]{3,2,1,0:T(8,128)(2,1)S(1)}, u32[]{:S(2)}, u32[]{:S(2)}) collective-permute-start(bf16[2,2,160,128]{3,2,1,0:T(8,128)(2,1)S(1)} %get-tuple-element.67), channel_id=1, source_target_pairs={{0,8},{1,9},{2,10},{3,11},{4,12},{5,13},{6,14},{7,15},{8,0},{9,1},... | collective-permute-start | bytes 491528 | tf_op jit(solution)/shard_map/ppermute | solution.py:545
  152.8 15.7 %collective-permute-start.13 = (bf16[2,2,160,128]{3,2,1,0:T(8,128)(2,1)S(1)}, bf16[2,2,160,128]{3,2,1,0:T(8,128)(2,1)S(1)}, u32[]{:S(2)}, u32[]{:S(2)}) collective-permute-start(bf16[2,2,160,128]{3,2,1,0:T(8,128)(2,1)S(1)} %get-tuple-element.68), channel_id=1, source_target_pairs={{0,10},{1,11},{2,8},{3,9},{4,14},{5,15},{6,12},{7,13},{8,2},{9,3},... | collective-permute-start | bytes 491528 | tf_op jit(solution)/shard_map/ppermute | solution.py:545
  154.9 27.1 %collective-permute-start.16 = (bf16[2,3,160,128]{3,2,1,0:T(8,128)(2,1)S(1)}, bf16[2,3,160,128]{3,2,1,0:T(8,128)(2,1)S(1)}, u32[]{:S(2)}, u32[]{:S(2)}) collective-permute-start(bf16[2,3,160,128]{3,2,1,0:T(8,128)(2,1)S(1)} %get-tuple-element.72), channel_id=1, source_target_pairs={{0,2},{1,3},{2,0},{3,1},{4,6},{5,7},{6,4},{7,5},{8,10},{9,11},{10,... | collective-permute-start | bytes 737288 | tf_op jit(solution)/shard_map/ppermute | solution.py:545
  155.4 31.0 %collective-permute-start.17 = (bf16[2,3,160,128]{3,2,1,0:T(8,128)(2,1)S(1)}, bf16[2,3,160,128]{3,2,1,0:T(8,128)(2,1)S(1)}, u32[]{:S(2)}, u32[]{:S(2)}) collective-permute-start(bf16[2,3,160,128]{3,2,1,0:T(8,128)(2,1)S(1)} %get-tuple-element.73), channel_id=1, source_target_pairs={{0,4},{1,5},{2,6},{3,7},{4,0},{5,1},{6,2},{7,3},{8,12},{9,13},{10,... | collective-permute-start | bytes 737288 | tf_op jit(solution)/shard_map/ppermute | solution.py:545
  155.7 30.7 %collective-permute-start.18 = (bf16[2,3,160,128]{3,2,1,0:T(8,128)(2,1)S(1)}, bf16[2,3,160,128]{3,2,1,0:T(8,128)(2,1)S(1)}, u32[]{:S(2)}, u32[]{:S(2)}) collective-permute-start(bf16[2,3,160,128]{3,2,1,0:T(8,128)(2,1)S(1)} %get-tuple-element.74), channel_id=1, source_target_pairs={{0,6},{1,7},{2,4},{3,5},{4,2},{5,3},{6,0},{7,1},{8,14},{9,15},{10,... | collective-permute-start | bytes 737288 | tf_op jit(solution)/shard_map/ppermute | solution.py:545
  165.0 16.3 %collective-permute-start.14 = (bf16[2,2,160,128]{3,2,1,0:T(8,128)(2,1)S(1)}, bf16[2,2,160,128]{3,2,1,0:T(8,128)(2,1)S(1)}, u32[]{:S(2)}, u32[]{:S(2)}) collective-permute-start(bf16[2,2,160,128]{3,2,1,0:T(8,128)(2,1)S(1)} %get-tuple-element.69), channel_id=1, source_target_pairs={{0,12},{1,13},{2,14},{3,15},{4,8},{5,9},{6,10},{7,11},{8,4},{9,5},... | collective-permute-start | bytes 491528 | tf_op jit(solution)/shard_map/ppermute | solution.py:545
  168.5 0.7 copy-start.4
  169.1 21.4 %collective-permute-start.15 = (bf16[2,2,160,128]{3,2,1,0:T(8,128)(2,1)S(1)}, bf16[2,2,160,128]{3,2,1,0:T(8,128)(2,1)}, u32[]{:S(2)}, u32[]{:S(2)}) collective-permute-start(bf16[2,2,160,128]{3,2,1,0:T(8,128)(2,1)S(1)} %get-tuple-element.70), channel_id=1, source_target_pairs={{0,14},{1,15},{2,12},{3,13},{4,10},{5,11},{6,8},{7,9},{8,6},{9,7},... | collective-permute-start | bytes 491528 | tf_op jit(solution)/shard_map/ppermute | solution.py:545
  181.3 0.7 copy-start.6
  182.0 11.3 %collective-permute-start.8 = (bf16[2,1,160,128]{3,2,1,0:T(8,128)(2,1)}, bf16[2,1,160,128]{3,2,1,0:T(8,128)(2,1)S(1)}, u32[]{:S(2)}, u32[]{:S(2)}) collective-permute-start(bf16[2,1,160,128]{3,2,1,0:T(8,128)(2,1)} %get-tuple-element.63), channel_id=1, source_target_pairs={{0,8},{1,9},{2,10},{3,11},{4,12},{5,13},{6,14},{7,15},{8,0},{9,1},... | collective-permute-start | bytes 245768 | tf_op jit(solution)/shard_map/ppermute | solution.py:545
  182.0 12.0 %collective-permute-start.9 = (bf16[2,1,160,128]{3,2,1,0:T(8,128)(2,1)}, bf16[2,1,160,128]{3,2,1,0:T(8,128)(2,1)S(1)}, u32[]{:S(2)}, u32[]{:S(2)}) collective-permute-start(bf16[2,1,160,128]{3,2,1,0:T(8,128)(2,1)} %get-tuple-element.64), channel_id=1, source_target_pairs={{0,10},{1,11},{2,8},{3,9},{4,14},{5,15},{6,12},{7,13},{8,2},{9,3},... | collective-permute-start | bytes 245768 | tf_op jit(solution)/shard_map/ppermute | solution.py:545
  186.4 9.9 %collective-permute-start.10 = (bf16[2,1,160,128]{3,2,1,0:T(8,128)(2,1)}, bf16[2,1,160,128]{3,2,1,0:T(8,128)(2,1)}, u32[]{:S(2)}, u32[]{:S(2)}) collective-permute-start(bf16[2,1,160,128]{3,2,1,0:T(8,128)(2,1)} %get-tuple-element.65), channel_id=1, source_target_pairs={{0,12},{1,13},{2,14},{3,15},{4,8},{5,9},{6,10},{7,11},{8,4},{9,5},... | collective-permute-start | bytes 245768 | tf_op jit(solution)/shard_map/ppermute | solution.py:545
  186.4 12.1 %collective-permute-start.11 = (bf16[2,1,160,128]{3,2,1,0:T(8,128)(2,1)}, bf16[2,1,160,128]{3,2,1,0:T(8,128)(2,1)}, u32[]{:S(2)}, u32[]{:S(2)}) collective-permute-start(bf16[2,1,160,128]{3,2,1,0:T(8,128)(2,1)} %get-tuple-element.66), channel_id=1, source_target_pairs={{0,14},{1,15},{2,12},{3,13},{4,10},{5,11},{6,8},{7,9},{8,6},{9,7},... | collective-permute-start | bytes 245768 | tf_op jit(solution)/shard_map/ppermute | solution.py:545
  187.8 2.8 %copy-start.5 = (bf16[2,2,160,128]{3,2,1,0:T(8,128)(2,1)S(1)}, bf16[2,2,160,128]{3,2,1,0:T(8,128)(2,1)}, u32[]{:S(2)}) copy-start(bf16[2,2,160,128]{3,2,1,0:T(8,128)(2,1)} %copy-done.4) | copy-start | bytes 491524
  187.8 2.8 %copy-start.7 = (bf16[2,2,160,128]{3,2,1,0:T(8,128)(2,1)S(1)}, bf16[2,2,160,128]{3,2,1,0:T(8,128)(2,1)}, u32[]{:S(2)}) copy-start(bf16[2,2,160,128]{3,2,1,0:T(8,128)(2,1)} %copy-done.6) | copy-start | bytes 491524

commit v19 on v18

--- a/solution.py
+++ b/solution.py
@@ -130,13 +130,9 @@
         copy.wait()
 
 
-def lat_block(lats):
-    return 32 if lats % 32 == 0 else lats
-
-
 def weigh(tendency, gauss, me, slot, local_slots, split, waits):
     rows, lats, slots, members = tendency.shape
-    each = lats // lat_block(lats)
+    each = 1
     chips = slots // local_slots // CORES
     shapes = [jax.ShapeDtypeStruct((chips, CORES, rows, lats, members), BF16)]
     if split:
@@ -528,7 +524,7 @@
             pltpu.VMEM((half, CORES, some, lats, members), BF16),
             pltpu.VMEM((some, lats, slots, members), BF16),
             pltpu.SemaphoreType.DMA((some, half)),
-            pltpu.SemaphoreType.DMA((some, lats // lat_block(lats))),
+            pltpu.SemaphoreType.DMA((some, 1)),
         ],
         input_output_aliases={len(used) + 2: 0} if output else {},
     )(me, blocks, *used, *output)

time: 202 us -> 199 us (0.985)
  Pallas kernels: 60.3 us -> 55.8 us
  waiting for transfers between devices: 92.3 us -> 94.6 us
    pallas_call x2, Pallas kernels: 12.9 us -> 8.28 us  [weigh(): call(functools.partial(weigh_kernel, slot, local_slots, split, len(waits)...]
    all_to_all x3, waiting for transfers between devices: 32.3 us -> 34.6 us  [between_chips(): lax.all_to_all(blocks, 'wave', split_axis=0, concat_axis=0, axis_index_gr...]
  transfers between devices with their start and end apart: 22 -> 22, of which waited for: 16 -> 16; matrix products, arithmetic and copies ran while one was open for 0% -> 0% of each run, Pallas kernels for 26% -> 25%
where the time goes in v19:
time: 199 us
  waiting for transfers between devices  94.6 us (48%)
  Pallas kernels  55.8 us (28%)
  starting transfers between devices  42.7 us (21%)
  local copies, waits for them, and re-layouts  5.22 us (3%)
    all_to_all x3, waiting for transfers between devices, between_chips(): lax.all_to_all(blocks, 'wave', split_axis=0, concat_axis=0, axis_index_gr...  34.6 us
    ppermute x11, waiting for transfers between devices, by_permutes(): got.append(lax.ppermute(message, 'wave', moves) if k else message)  23.2 us
    ppermute x3, waiting for transfers between devices, per_device(): others = [lax.ppermute(part, 'pole', [(0, 1), (1, 0)]) for part in forced]  22.1 us
    all_to_all x3, starting transfers between devices, between_chips(): lax.all_to_all(blocks, 'wave', split_axis=0, concat_axis=0, axis_index_gr...  19.6 us
    ppermute x11, starting transfers between devices, by_permutes(): got.append(lax.ppermute(message, 'wave', moves) if k else message)  17.5 us
    pallas_call x3, Pallas kernels, analyse(): call(functools.partial(analyse_kernel, slot, low), 'analyse', 2 * width *...  17.3 us
    pallas_call x3, Pallas kernels, synthesise(): call(functools.partial(synthesise_kernel, slot, low, apart, more, len(par...  16.5 us
    ppermute x4, waiting for transfers between devices, between_cores(): return lax.ppermute(blocks, 'wave', [(d, d ^ 1) for d in range(owners)])  10.4 us
  transfers between devices with their start and end apart: 22, of which 16 were waited for; matrix products, arithmetic and copies ran while one was open for 0% of the time, Pallas kernels for 25%

profile of v19, /device:TPU:8, one launch (start us, length us, event | category | flops | bytes accessed | tf_op | source)
XLA Modules:
  0.0 198.8 jit_solution(16493536688897969622)
XLA Ops:
  0.0 4.1 %weigh.2 = (bf16[8,2,3,160,128]{4,3,2,1,0:T(8,128)(2,1)}, f32[8,128]{1,0:T(8,128)}) custom-call(s32[1]{0:T(128)} %bitcast.me_ref, f32[1,160]{1,0:T(1,128)} %bitcast.3, bf16[3,160,32,128]{3,2,1,0:T(8,128)(2,1)} %tendency_ref.3), custom_call_target="tpu_custom_call" | custom-call | flops 503316480 | bytes 5898240 | tf_op jit(solution)/shard_map/weigh/pallas_call | solution.py:140
  4.1 0.0 copy-start.10
  4.1 6.3 %all-to-all-start = ((bf16[8,2,3,160,128]{4,3,2,1,0:T(8,128)(2,1)}), bf16[8,2,3,160,128]{4,3,2,1,0:T(8,128)(2,1)}, u32[]{:S(2)}, u32[]{:S(2)}) async-start(bf16[8,2,3,160,128]{4,3,2,1,0:T(8,128)(2,1)} %get-tuple-element.44), calls=%async_computation | async-start | bytes 3932160 | tf_op jit(solution)/shard_map/all_to_all | solution.py:547
  10.4 0.1 copy.24.coeff_ref
  10.5 1.8 copy-done.3
  12.3 2.4 %sum_pairs.1.here_ref = f32[18,2,1280]{2,1,0:T(2,128)S(1)} custom-call(f32[32,2]{1,0:T(8,128)S(1)} %copy.24.coeff_ref, f32[8,128]{1,0:T(8,128)S(1)} %copy-done.9, bf16[32,18,2,1280]{3,2,1,0:T(2,128)(2,1)S(1)} %copy-done.3), custom_call_target="tpu_custom_call" | custom-call | flops 5898240 | bytes 2949120 | tf_op jit(solution)/shard_map/sum_pairs/pallas_call | solution.py:330
  14.7 1.6 collective-permute-start
  16.3 4.3 %collective-permute-done.rest_0_.there_ref = f32[18,2,1280]{2,1,0:T(2,128)S(1)} collective-permute-done((f32[18,2,1280]{2,1,0:T(2,128)S(1)}, f32[18,2,1280]{2,1,0:T(2,128)S(1)}, u32[]{:S(2)}, u32[]{:S(2)}) %collective-permute-start) | collective-permute-done | bytes 184352 | tf_op jit(solution)/shard_map/ppermute | solution.py:567
  20.6 0.7 copy-done.1
  21.3 4.2 %weigh.3 = (bf16[8,2,3,160,128]{4,3,2,1,0:T(8,128)(2,1)}, bf16[8,3,160,128]{3,2,1,0:T(8,128)(2,1)}, f32[8,128]{1,0:T(8,128)}) custom-call(s32[1]{0:T(128)} %bitcast.me_ref, f32[1,160]{1,0:T(1,128)} %bitcast.4, bf16[3,160,32,128]{3,2,1,0:T(8,128)(2,1)} %tendency_ref.3, f32[18,2,1280]{2,1,0:T(2,128)} %copy-done.1), custom_call_target="tpu_custom_call" | custom-call | flops 503316480 | bytes 5898240 | tf_op jit(solution)/shard_map/weigh/pallas_call | solution.py:140
  25.4 0.1 collective-permute-start.1
  25.5 2.8 %collective-permute-done.1.mate_ref = bf16[8,3,160,128]{3,2,1,0:T(8,128)(2,1)S(1)} collective-permute-done((bf16[8,3,160,128]{3,2,1,0:T(8,128)(2,1)}, bf16[8,3,160,128]{3,2,1,0:T(8,128)(2,1)S(1)}, u32[]{:S(2)}, u32[]{:S(2)}) %collective-permute-start.1) | collective-permute-done | bytes 983072 | tf_op jit(solution)/shard_map/ppermute | solution.py:534
  28.3 0.9 pair.3
  29.2 24.2 %all-to-all-done.in_ref.rest_0_ = bf16[8,2,3,160,128]{4,3,2,1,0:T(8,128)(2,1)} async-done(((bf16[8,2,3,160,128]{4,3,2,1,0:T(8,128)(2,1)}), bf16[8,2,3,160,128]{4,3,2,1,0:T(8,128)(2,1)}, u32[]{:S(2)}, u32[]{:S(2)}) %all-to-all-start) | async-done | bytes 1966112 | tf_op jit(solution)/shard_map/all_to_all | solution.py:547
  53.4 6.8 %all-to-all-start.2 = ((bf16[8,2,3,160,128]{4,3,2,1,0:T(8,128)(2,1)}), bf16[8,2,3,160,128]{4,3,2,1,0:T(8,128)(2,1)}, u32[]{:S(2)}, u32[]{:S(2)}) async-start(bf16[8,2,3,160,128]{4,3,2,1,0:T(8,128)(2,1)} %get-tuple-element.49), calls=%async_computation.2 | async-start | bytes 3932160 | tf_op jit(solution)/shard_map/all_to_all | solution.py:547
  60.2 1.3 pick.1
  61.5 0.1 collective-permute-start.2
  61.5 2.6 %collective-permute-done.2.rest_1_ = bf16[8,3,160,128]{3,2,1,0:T(8,128)(2,1)S(1)} collective-permute-done((bf16[8,3,160,128]{3,2,1,0:T(8,128)(2,1)S(1)}, bf16[8,3,160,128]{3,2,1,0:T(8,128)(2,1)S(1)}, u32[]{:S(2)}, u32[]{:S(2)}) %collective-permute-start.2) | collective-permute-done | bytes 983072 | tf_op jit(solution)/shard_map/ppermute | solution.py:534
  64.1 5.6 %analyse.3.own_ref = bf16[3,128,640]{2,1,0:T(8,128)(2,1)S(1)} custom-call(s32[1]{0:T(128)} %bitcast.me_ref, s32[2]{0:T(128)S(1)} %copy-done.8, f32[8,128]{1,0:T(8,128)S(1)} %get-tuple-element.43.token_ref, bf16[2,1280,2560]{2,1,0:T(8,128)(2,1)} %table_ref.11, bf16[3,2,128,1280]{3,2,1,0:T(8,128)(2,1)} %state_ref.5, ...), custom_call_target="tpu_custom_call" | custom-call | flops 1258291200 | bytes 3276800 | tf_op jit(solution)/shard_map/analyse/pallas_call | solution.py:288
  69.7 1.6 collective-permute-start.3
  71.3 11.7 %collective-permute-done.3.other_ref = bf16[3,128,640]{2,1,0:T(8,128)(2,1)S(1)} collective-permute-done((bf16[3,128,640]{2,1,0:T(8,128)(2,1)S(1)}, bf16[3,128,640]{2,1,0:T(8,128)(2,1)S(1)}, u32[]{:S(2)}, u32[]{:S(2)}) %collective-permute-start.3) | collective-permute-done | bytes 491552 | tf_op jit(solution)/shard_map/ppermute | solution.py:581
  83.0 4.9 %synthesise.3 = (bf16[8,2,3,160,128]{4,3,2,1,0:T(8,128)(2,1)S(1)}, bf16[8,3,160,128]{3,2,1,0:T(8,128)(2,1)S(1)}) custom-call(s32[1]{0:T(128)} %bitcast.me_ref, f32[1]{0:T(128)} %bitcast.1.sign_ref, f32[18,2,1280]{2,1,0:T(2,128)S(1)} %sum_pairs.1.here_ref, f32[18,2,1280]{2,1,0:T(2,128)S(1)} %copy-done.2, bf16[3,128,640]{2,1,0:T(8,128)(2,1)S(1)} %analyse.3.own_ref, ...), custom_call_target="tpu_custom_call" | custom-call | flops 1258291200 | bytes 3276800 | tf_op jit(solution)/shard_map/synthesise/pallas_call | solution.py:430
  88.0 0.1 collective-permute-start.4
  88.1 2.6 %collective-permute-done.4.mate_ref = bf16[8,3,160,128]{3,2,1,0:T(8,128)(2,1)S(1)} collective-permute-done((bf16[8,3,160,128]{3,2,1,0:T(8,128)(2,1)S(1)}, bf16[8,3,160,128]{3,2,1,0:T(8,128)(2,1)S(1)}, u32[]{:S(2)}, u32[]{:S(2)}) %collective-permute-start.4) | collective-permute-done | bytes 983072 | tf_op jit(solution)/shard_map/ppermute | solution.py:534
  90.6 0.1 pair.4
  90.7 0.0 copy-start
  90.7 1.3 copy-done
  92.0 10.4 %all-to-all-done.2.rest_0_ = bf16[8,2,3,160,128]{4,3,2,1,0:T(8,128)(2,1)} async-done(((bf16[8,2,3,160,128]{4,3,2,1,0:T(8,128)(2,1)}), bf16[8,2,3,160,128]{4,3,2,1,0:T(8,128)(2,1)}, u32[]{:S(2)}, u32[]{:S(2)}) %all-to-all-start.2) | async-done | bytes 1966112 | tf_op jit(solution)/shard_map/all_to_all | solution.py:547
  102.4 6.5 %all-to-all-start.1 = ((bf16[8,2,3,160,128]{4,3,2,1,0:T(8,128)(2,1)}), bf16[8,2,3,160,128]{4,3,2,1,0:T(8,128)(2,1)S(1)}, u32[]{:S(2)}, u32[]{:S(2)}) async-start(bf16[8,2,3,160,128]{4,3,2,1,0:T(8,128)(2,1)} %copy-done), calls=%async_computation.1 | async-start | bytes 3932160 | tf_op jit(solution)/shard_map/all_to_all | solution.py:547
  108.9 5.8 %analyse.5.own_ref = bf16[3,128,640]{2,1,0:T(8,128)(2,1)S(1)} custom-call(s32[1]{0:T(128)} %bitcast.me_ref, s32[2]{0:T(128)S(1)} %copy-done.8, f32[8,128]{1,0:T(8,128)S(1)} %get-tuple-element.48.token_ref, bf16[2,1280,2560]{2,1,0:T(8,128)(2,1)} %table_ref.11, bf16[3,2,128,1280]{3,2,1,0:T(8,128)(2,1)} %state_ref.5, ...), custom_call_target="tpu_custom_call" | custom-call | flops 1258291200 | bytes 3276800 | tf_op jit(solution)/shard_map/analyse/pallas_call | solution.py:288
  114.8 1.6 collective-permute-start.6
  116.4 5.8 %analyse.4.own_ref = bf16[3,128,640]{2,1,0:T(8,128)(2,1)S(1)} custom-call(s32[1]{0:T(128)} %bitcast.me_ref, s32[2]{0:T(128)S(1)} %copy-done.8, f32[8,128]{1,0:T(8,128)S(1)} %get-tuple-element.48.token_ref, bf16[2,1280,2560]{2,1,0:T(8,128)(2,1)} %table_ref.11, bf16[3,2,128,1280]{3,2,1,0:T(8,128)(2,1)} %state_ref.5, ...), custom_call_target="tpu_custom_call" | custom-call | flops 1258291200 | bytes 3276800 | tf_op jit(solution)/shard_map/analyse/pallas_call | solution.py:288
  122.2 0.6 collective-permute-start.5
  122.8 6.2 %collective-permute-done.6.other_ref = bf16[3,128,640]{2,1,0:T(8,128)(2,1)S(1)} collective-permute-done((bf16[3,128,640]{2,1,0:T(8,128)(2,1)S(1)}, bf16[3,128,640]{2,1,0:T(8,128)(2,1)S(1)}, u32[]{:S(2)}, u32[]{:S(2)}) %collective-permute-start.6) | collective-permute-done | bytes 491552 | tf_op jit(solution)/shard_map/ppermute | solution.py:581
  129.0 4.8 %synthesise.4.rest_0_ = f32[384,2560]{1,0:T(8,128)S(1)} custom-call(s32[1]{0:T(128)} %bitcast.me_ref, f32[1]{0:T(128)} %bitcast.1.sign_ref, f32[18,2,1280]{2,1,0:T(2,128)S(1)} %sum_pairs.1.here_ref, f32[18,2,1280]{2,1,0:T(2,128)S(1)} %copy-done.2, bf16[3,128,640]{2,1,0:T(8,128)(2,1)S(1)} %analyse.5.own_ref, ...), custom_call_target="tpu_custom_call" | custom-call | flops 1258291200 | bytes 3276800 | tf_op jit(solution)/shard_map/synthesise/pallas_call | solution.py:430
  133.8 4.1 %collective-permute-done.5.other_ref = bf16[3,128,640]{2,1,0:T(8,128)(2,1)S(1)} collective-permute-done((bf16[3,128,640]{2,1,0:T(8,128)(2,1)S(1)}, bf16[3,128,640]{2,1,0:T(8,128)(2,1)S(1)}, u32[]{:S(2)}, u32[]{:S(2)}) %collective-permute-start.5) | collective-permute-done | bytes 491552 | tf_op jit(solution)/shard_map/ppermute | solution.py:581
  138.0 6.7 %synthesise.5 = (bf16[2,3,160,128]{3,2,1,0:T(8,128)(2,1)S(1)}, bf16[2,2,160,128]{3,2,1,0:T(8,128)(2,1)S(1)}, bf16[2,2,160,128]{3,2,1,0:T(8,128)(2,1)S(1)}, bf16[...) custom-call(s32[1]{0:T(128)} %bitcast.me_ref, ...), custom_call_target="tpu_custom_call" | custom-call | flops 1258291200 | bytes 3276800 | tf_op jit(solution)/shard_map/synthesise/pallas_call | solution.py:430
  144.7 0.1 collective-permute-start.7
  144.8 2.6 %collective-permute-done.7.mate_ref = bf16[8,3,160,128]{3,2,1,0:T(8,128)(2,1)S(1)} collective-permute-done((bf16[8,3,160,128]{3,2,1,0:T(8,128)(2,1)S(1)}, bf16[8,3,160,128]{3,2,1,0:T(8,128)(2,1)S(1)}, u32[]{:S(2)}, u32[]{:S(2)}) %collective-permute-start.7) | collective-permute-done | bytes 983072 | tf_op jit(solution)/shard_map/ppermute | solution.py:534
  147.3 1.3 pair.5
  148.7 1.8 collective-permute-start.12
  150.5 2.1 %collective-permute-start.13 = (bf16[2,2,160,128]{3,2,1,0:T(8,128)(2,1)S(1)}, bf16[2,2,160,128]{3,2,1,0:T(8,128)(2,1)S(1)}, u32[]{:S(2)}, u32[]{:S(2)}) collective-permute-start(bf16[2,2,160,128]{3,2,1,0:T(8,128)(2,1)S(1)} %get-tuple-element.68), channel_id=1, source_target_pairs={{0,10},{1,11},{2,8},{3,9},{4,14},{5,15},{6,12},{7,13},{8,2},{9,3},... | collective-permute-start | bytes 491528 | tf_op jit(solution)/shard_map/ppermute | solution.py:541
  152.6 0.6 collective-permute-start.16
  153.1 0.3 collective-permute-start.17
  153.4 2.6 %collective-permute-start.18 = (bf16[2,3,160,128]{3,2,1,0:T(8,128)(2,1)S(1)}, bf16[2,3,160,128]{3,2,1,0:T(8,128)(2,1)S(1)}, u32[]{:S(2)}, u32[]{:S(2)}) collective-permute-start(bf16[2,3,160,128]{3,2,1,0:T(8,128)(2,1)S(1)} %get-tuple-element.74), channel_id=1, source_target_pairs={{0,6},{1,7},{2,4},{3,5},{4,2},{5,3},{6,0},{7,1},{8,14},{9,15},{10,... | collective-permute-start | bytes 737288 | tf_op jit(solution)/shard_map/ppermute | solution.py:541
  156.0 6.6 %collective-permute-done.12.rest_0_ = bf16[2,2,160,128]{3,2,1,0:T(8,128)(2,1)S(1)} collective-permute-done((bf16[2,2,160,128]{3,2,1,0:T(8,128)(2,1)S(1)}, bf16[2,2,160,128]{3,2,1,0:T(8,128)(2,1)S(1)}, u32[]{:S(2)}, u32[]{:S(2)}) %collective-permute-start.12) | collective-permute-done | bytes 163872 | tf_op jit(solution)/shard_map/ppermute | solution.py:541
  162.7 1.8 collective-permute-start.14
  164.5 1.7 collective-permute-done.13.rest_1_
  166.2 0.7 copy-done.4
  166.8 2.5 %collective-permute-start.15 = (bf16[2,2,160,128]{3,2,1,0:T(8,128)(2,1)S(1)}, bf16[2,2,160,128]{3,2,1,0:T(8,128)(2,1)}, u32[]{:S(2)}, u32[]{:S(2)}) collective-permute-start(bf16[2,2,160,128]{3,2,1,0:T(8,128)(2,1)S(1)} %get-tuple-element.70), channel_id=1, source_target_pairs={{0,14},{1,15},{2,12},{3,13},{4,10},{5,11},{6,8},{7,9},{8,6},{9,7},... | collective-permute-start | bytes 491528 | tf_op jit(solution)/shard_map/ppermute | solution.py:541
  169.3 9.6 %collective-permute-done.14.rest_2_ = bf16[2,2,160,128]{3,2,1,0:T(8,128)(2,1)S(1)} collective-permute-done((bf16[2,2,160,128]{3,2,1,0:T(8,128)(2,1)S(1)}, bf16[2,2,160,128]{3,2,1,0:T(8,128)(2,1)S(1)}, u32[]{:S(2)}, u32[]{:S(2)}) %collective-permute-start.14) | collective-permute-done | bytes 163872 | tf_op jit(solution)/shard_map/ppermute | solution.py:541
  179.0 0.7 copy-done.6
  179.6 0.0 collective-permute-start.8
  179.6 4.5 %collective-permute-start.9 = (bf16[2,1,160,128]{3,2,1,0:T(8,128)(2,1)}, bf16[2,1,160,128]{3,2,1,0:T(8,128)(2,1)S(1)}, u32[]{:S(2)}, u32[]{:S(2)}) collective-permute-start(bf16[2,1,160,128]{3,2,1,0:T(8,128)(2,1)} %get-tuple-element.64), channel_id=1, source_target_pairs={{0,10},{1,11},{2,8},{3,9},{4,14},{5,15},{6,12},{7,13},{8,2},{9,3},... | collective-permute-start | bytes 245768 | tf_op jit(solution)/shard_map/ppermute | solution.py:541
  184.1 0.0 collective-permute-done.18.rest_3_
  184.1 1.4 collective-permute-start.11
  185.5 2.7 %assemble.3.rest_4_ = bf16[3,160,32,128]{3,2,1,0:T(8,128)(2,1)} custom-call(s32[1]{0:T(128)} %bitcast.me_ref, bf16[8,2,3,160,128]{4,3,2,1,0:T(8,128)(2,1)S(1)} %all-to-all-done.1.blocks_ref, bf16[2,3,160,128]{3,2,1,0:T(8,128)(2,1)S(1)} %get-tuple-element.71.rest_0_, bf16[2,3,160,128]{3,2,1,0:T(8,128)(2,1)S(1)} %collective-permute-done.16.rest_1_, ...), custom_call_target="tpu_custom_call" | custom-call | flops 503316480 | bytes 3932160 | tf_op jit(solution)/shard_map/assemble/pallas_call | solution.py:515
  188.3 0.0 collective-permute-done.15.rest_3_
  188.3 2.7 %assemble.4.rest_4_ = bf16[3,160,32,128]{3,2,1,0:T(8,128)(2,1)} custom-call(s32[1]{0:T(128)} %bitcast.me_ref, bf16[8,2,3,160,128]{4,3,2,1,0:T(8,128)(2,1)S(1)} %all-to-all-done.1.blocks_ref, bf16[2,2,160,128]{3,2,1,0:T(8,128)(2,1)S(1)} %collective-permute-done.12.rest_0_, bf16[2,2,160,128]{3,2,1,0:T(8,128)(2,1)S(1)} %copy-done.5, ...), custom_call_target="tpu_custom_call", output_to_operand_aliasing={{}: (6, {})} | custom-call | flops 335544320 | bytes 2621440 | tf_op jit(solution)/shard_map/assemble/pallas_call | solution.py:515
  191.0 0.0 collective-permute-done.8.rest_0_
  191.0 0.6 collective-permute-done.9.rest_1_
  191.6 2.4 %collective-permute-done.10.rest_2_ = bf16[2,1,160,128]{3,2,1,0:T(8,128)(2,1)} collective-permute-done((bf16[2,1,160,128]{3,2,1,0:T(8,128)(2,1)}, bf16[2,1,160,128]{3,2,1,0:T(8,128)(2,1)}, u32[]{:S(2)}, u32[]{:S(2)}) %collective-permute-start.10) | collective-permute-done | bytes 81952 | tf_op jit(solution)/shard_map/ppermute | solution.py:541
  194.0 2.3 %collective-permute-done.11.rest_3_ = bf16[2,1,160,128]{3,2,1,0:T(8,128)(2,1)} collective-permute-done((bf16[2,1,160,128]{3,2,1,0:T(8,128)(2,1)}, bf16[2,1,160,128]{3,2,1,0:T(8,128)(2,1)}, u32[]{:S(2)}, u32[]{:S(2)}) %collective-permute-start.11) | collective-permute-done | bytes 81952 | tf_op jit(solution)/shard_map/ppermute | solution.py:541
  196.3 2.3 %assemble.5 = bf16[3,160,32,128]{3,2,1,0:T(8,128)(2,1)} custom-call(s32[1]{0:T(128)} %bitcast.me_ref, bf16[8,2,3,160,128]{4,3,2,1,0:T(8,128)(2,1)S(1)} %all-to-all-done.1.blocks_ref, bf16[2,1,160,128]{3,2,1,0:T(8,128)(2,1)S(1)} %collective-permute-done.8.rest_0_, ...), custom_call_target="tpu_custom_call", output_to_operand_aliasing={{}: (6, {})} | custom-call | flops 167772160 | bytes 1310720 | tf_op jit(solution)/shard_map/assemble/pallas_call | solution.py:515
  (19 shorter events, 0.0 us)
Async XLA Ops:
  4.1 6.3 %copy-start.10 = (f32[32,2]{0,1:T(2,128)S(1)}, f32[32,2]{0,1:T(2,128)}, u32[]{:S(2)}) copy-start(f32[32,2]{0,1:T(2,128)} %param.12) | copy-start | bytes 772
  4.1 6.4 %copy-start.9 = (f32[8,128]{1,0:T(8,128)S(1)}, f32[8,128]{1,0:T(8,128)}, u32[]{:S(2)}) copy-start(f32[8,128]{1,0:T(8,128)} %get-tuple-element.40.token_ref) | copy-start | bytes 12292
  4.1 49.2 %all-to-all-start = ((bf16[8,2,3,160,128]{4,3,2,1,0:T(8,128)(2,1)}), bf16[8,2,3,160,128]{4,3,2,1,0:T(8,128)(2,1)}, u32[]{:S(2)}, u32[]{:S(2)}) async-start(bf16[8,2,3,160,128]{4,3,2,1,0:T(8,128)(2,1)} %get-tuple-element.44), calls=%async_computation | async-start | bytes 3932160 | tf_op jit(solution)/shard_map/all_to_all | solution.py:547
  10.5 1.8 copy-start.3
  14.7 5.9 %collective-permute-start = (f32[18,2,1280]{2,1,0:T(2,128)S(1)}, f32[18,2,1280]{2,1,0:T(2,128)S(1)}, u32[]{:S(2)}, u32[]{:S(2)}) collective-permute-start(f32[18,2,1280]{2,1,0:T(2,128)S(1)} %sum_pairs.1.here_ref), channel_id=1, source_target_pairs={{0,16},{16,0},{1,17},{17,1},{2,18},{18,2},{3,19},{19,3},{4,20},{20... | collective-permute-start | bytes 552968 | tf_op jit(solution)/shard_map/ppermute | solution.py:567
  20.6 0.7 copy-start.1
  25.4 2.8 %collective-permute-start.1 = (bf16[8,3,160,128]{3,2,1,0:T(8,128)(2,1)}, bf16[8,3,160,128]{3,2,1,0:T(8,128)(2,1)S(1)}, u32[]{:S(2)}, u32[]{:S(2)}) collective-permute-start(bf16[8,3,160,128]{3,2,1,0:T(8,128)(2,1)} %get-tuple-element.41), channel_id=1, source_target_pairs={{0,1},{1,0},{2,3},{3,2},{4,5},{5,4},{6,7},{7,6},{8,9},{9,8},{10,11... | collective-permute-start | bytes 2949128 | tf_op jit(solution)/shard_map/ppermute | solution.py:534
  53.4 49.0 %all-to-all-start.2 = ((bf16[8,2,3,160,128]{4,3,2,1,0:T(8,128)(2,1)}), bf16[8,2,3,160,128]{4,3,2,1,0:T(8,128)(2,1)}, u32[]{:S(2)}, u32[]{:S(2)}) async-start(bf16[8,2,3,160,128]{4,3,2,1,0:T(8,128)(2,1)} %get-tuple-element.49), calls=%async_computation.2 | async-start | bytes 3932160 | tf_op jit(solution)/shard_map/all_to_all | solution.py:547
  60.2 3.9 %copy-start.8 = (s32[2]{0:T(128)S(1)}, s32[2]{0:T(128)}, u32[]{:S(2)}) copy-start(s32[2]{0:T(128)} %wave_ref.5) | copy-start | bytes 28
  61.5 21.6 %copy-start.2 = (f32[18,2,1280]{2,1,0:T(2,128)S(1)}, f32[18,2,1280]{2,1,0:T(2,128)}, u32[]{:S(2)}) copy-start(f32[18,2,1280]{2,1,0:T(2,128)} %copy-done.1) | copy-start | bytes 552964
  61.5 2.6 %collective-permute-start.2 = (bf16[8,3,160,128]{3,2,1,0:T(8,128)(2,1)S(1)}, bf16[8,3,160,128]{3,2,1,0:T(8,128)(2,1)S(1)}, u32[]{:S(2)}, u32[]{:S(2)}) collective-permute-start(bf16[8,3,160,128]{3,2,1,0:T(8,128)(2,1)S(1)} %pick.1), channel_id=1, source_target_pairs={{0,1},{1,0},{2,3},{3,2},{4,5},{5,4},{6,7},{7,6},{8,9},{9,8},{10,11... | collective-permute-start | bytes 2949128 | tf_op jit(solution)/shard_map/ppermute | solution.py:534
  69.7 13.3 %collective-permute-start.3 = (bf16[3,128,640]{2,1,0:T(8,128)(2,1)S(1)}, bf16[3,128,640]{2,1,0:T(8,128)(2,1)S(1)}, u32[]{:S(2)}, u32[]{:S(2)}) collective-permute-start(bf16[3,128,640]{2,1,0:T(8,128)(2,1)S(1)} %analyse.3.own_ref), channel_id=1, source_target_pairs={{0,16},{16,0},{1,17},{17,1},{2,18},{18,2},{3,19},{19,3},{4,20},{20... | collective-permute-start | bytes 1474568 | tf_op jit(solution)/shard_map/ppermute | solution.py:581
  88.0 2.6 %collective-permute-start.4 = (bf16[8,3,160,128]{3,2,1,0:T(8,128)(2,1)S(1)}, bf16[8,3,160,128]{3,2,1,0:T(8,128)(2,1)S(1)}, u32[]{:S(2)}, u32[]{:S(2)}) collective-permute-start(bf16[8,3,160,128]{3,2,1,0:T(8,128)(2,1)S(1)} %get-tuple-element.45), channel_id=1, source_target_pairs={{0,1},{1,0},{2,3},{3,2},{4,5},{5,4},{6,7},{7,6},{8,9},{9,8},{10,11... | collective-permute-start | bytes 2949128 | tf_op jit(solution)/shard_map/ppermute | solution.py:534
  90.7 1.3 copy-start
  102.4 83.1 %all-to-all-start.1 = ((bf16[8,2,3,160,128]{4,3,2,1,0:T(8,128)(2,1)}), bf16[8,2,3,160,128]{4,3,2,1,0:T(8,128)(2,1)S(1)}, u32[]{:S(2)}, u32[]{:S(2)}) async-start(bf16[8,2,3,160,128]{4,3,2,1,0:T(8,128)(2,1)} %copy-done), calls=%async_computation.1 | async-start | bytes 3932160 | tf_op jit(solution)/shard_map/all_to_all | solution.py:547
  114.8 14.2 %collective-permute-start.6 = (bf16[3,128,640]{2,1,0:T(8,128)(2,1)S(1)}, bf16[3,128,640]{2,1,0:T(8,128)(2,1)S(1)}, u32[]{:S(2)}, u32[]{:S(2)}) collective-permute-start(bf16[3,128,640]{2,1,0:T(8,128)(2,1)S(1)} %analyse.5.own_ref), channel_id=1, source_target_pairs={{0,16},{16,0},{1,17},{17,1},{2,18},{18,2},{3,19},{19,3},{4,20},{20... | collective-permute-start | bytes 1474568 | tf_op jit(solution)/shard_map/ppermute | solution.py:581
  122.2 15.8 %collective-permute-start.5 = (bf16[3,128,640]{2,1,0:T(8,128)(2,1)S(1)}, bf16[3,128,640]{2,1,0:T(8,128)(2,1)S(1)}, u32[]{:S(2)}, u32[]{:S(2)}) collective-permute-start(bf16[3,128,640]{2,1,0:T(8,128)(2,1)S(1)} %analyse.4.own_ref), channel_id=1, source_target_pairs={{0,16},{16,0},{1,17},{17,1},{2,18},{18,2},{3,19},{19,3},{4,20},{20... | collective-permute-start | bytes 1474568 | tf_op jit(solution)/shard_map/ppermute | solution.py:581
  144.7 2.6 %collective-permute-start.7 = (bf16[8,3,160,128]{3,2,1,0:T(8,128)(2,1)S(1)}, bf16[8,3,160,128]{3,2,1,0:T(8,128)(2,1)S(1)}, u32[]{:S(2)}, u32[]{:S(2)}) collective-permute-start(bf16[8,3,160,128]{3,2,1,0:T(8,128)(2,1)S(1)} %get-tuple-element.50), channel_id=1, source_target_pairs={{0,1},{1,0},{2,3},{3,2},{4,5},{5,4},{6,7},{7,6},{8,9},{9,8},{10,11... | collective-permute-start | bytes 2949128 | tf_op jit(solution)/shard_map/ppermute | solution.py:534
  148.7 14.0 %collective-permute-start.12 = (bf16[2,2,160,128]{3,2,1,0:T(8,128)(2,1)S(1)}, bf16[2,2,160,128]{3,2,1,0:T(8,128)(2,1)S(1)}, u32[]{:S(2)}, u32[]{:S(2)}) collective-permute-start(bf16[2,2,160,128]{3,2,1,0:T(8,128)(2,1)S(1)} %get-tuple-element.67), channel_id=1, source_target_pairs={{0,8},{1,9},{2,10},{3,11},{4,12},{5,13},{6,14},{7,15},{8,0},{9,1},... | collective-permute-start | bytes 491528 | tf_op jit(solution)/shard_map/ppermute | solution.py:541
  150.5 15.7 %collective-permute-start.13 = (bf16[2,2,160,128]{3,2,1,0:T(8,128)(2,1)S(1)}, bf16[2,2,160,128]{3,2,1,0:T(8,128)(2,1)S(1)}, u32[]{:S(2)}, u32[]{:S(2)}) collective-permute-start(bf16[2,2,160,128]{3,2,1,0:T(8,128)(2,1)S(1)} %get-tuple-element.68), channel_id=1, source_target_pairs={{0,10},{1,11},{2,8},{3,9},{4,14},{5,15},{6,12},{7,13},{8,2},{9,3},... | collective-permute-start | bytes 491528 | tf_op jit(solution)/shard_map/ppermute | solution.py:541
  152.6 27.1 %collective-permute-start.16 = (bf16[2,3,160,128]{3,2,1,0:T(8,128)(2,1)S(1)}, bf16[2,3,160,128]{3,2,1,0:T(8,128)(2,1)S(1)}, u32[]{:S(2)}, u32[]{:S(2)}) collective-permute-start(bf16[2,3,160,128]{3,2,1,0:T(8,128)(2,1)S(1)} %get-tuple-element.72), channel_id=1, source_target_pairs={{0,2},{1,3},{2,0},{3,1},{4,6},{5,7},{6,4},{7,5},{8,10},{9,11},{10,... | collective-permute-start | bytes 737288 | tf_op jit(solution)/shard_map/ppermute | solution.py:541
  153.1 31.0 %collective-permute-start.17 = (bf16[2,3,160,128]{3,2,1,0:T(8,128)(2,1)S(1)}, bf16[2,3,160,128]{3,2,1,0:T(8,128)(2,1)S(1)}, u32[]{:S(2)}, u32[]{:S(2)}) collective-permute-start(bf16[2,3,160,128]{3,2,1,0:T(8,128)(2,1)S(1)} %get-tuple-element.73), channel_id=1, source_target_pairs={{0,4},{1,5},{2,6},{3,7},{4,0},{5,1},{6,2},{7,3},{8,12},{9,13},{10,... | collective-permute-start | bytes 737288 | tf_op jit(solution)/shard_map/ppermute | solution.py:541
  153.4 30.7 %collective-permute-start.18 = (bf16[2,3,160,128]{3,2,1,0:T(8,128)(2,1)S(1)}, bf16[2,3,160,128]{3,2,1,0:T(8,128)(2,1)S(1)}, u32[]{:S(2)}, u32[]{:S(2)}) collective-permute-start(bf16[2,3,160,128]{3,2,1,0:T(8,128)(2,1)S(1)} %get-tuple-element.74), channel_id=1, source_target_pairs={{0,6},{1,7},{2,4},{3,5},{4,2},{5,3},{6,0},{7,1},{8,14},{9,15},{10,... | collective-permute-start | bytes 737288 | tf_op jit(solution)/shard_map/ppermute | solution.py:541
  162.7 16.3 %collective-permute-start.14 = (bf16[2,2,160,128]{3,2,1,0:T(8,128)(2,1)S(1)}, bf16[2,2,160,128]{3,2,1,0:T(8,128)(2,1)S(1)}, u32[]{:S(2)}, u32[]{:S(2)}) collective-permute-start(bf16[2,2,160,128]{3,2,1,0:T(8,128)(2,1)S(1)} %get-tuple-element.69), channel_id=1, source_target_pairs={{0,12},{1,13},{2,14},{3,15},{4,8},{5,9},{6,10},{7,11},{8,4},{9,5},... | collective-permute-start | bytes 491528 | tf_op jit(solution)/shard_map/ppermute | solution.py:541
  166.2 0.7 copy-start.4
  166.8 21.4 %collective-permute-start.15 = (bf16[2,2,160,128]{3,2,1,0:T(8,128)(2,1)S(1)}, bf16[2,2,160,128]{3,2,1,0:T(8,128)(2,1)}, u32[]{:S(2)}, u32[]{:S(2)}) collective-permute-start(bf16[2,2,160,128]{3,2,1,0:T(8,128)(2,1)S(1)} %get-tuple-element.70), channel_id=1, source_target_pairs={{0,14},{1,15},{2,12},{3,13},{4,10},{5,11},{6,8},{7,9},{8,6},{9,7},... | collective-permute-start | bytes 491528 | tf_op jit(solution)/shard_map/ppermute | solution.py:541
  179.0 0.7 copy-start.6
  179.6 11.4 %collective-permute-start.8 = (bf16[2,1,160,128]{3,2,1,0:T(8,128)(2,1)}, bf16[2,1,160,128]{3,2,1,0:T(8,128)(2,1)S(1)}, u32[]{:S(2)}, u32[]{:S(2)}) collective-permute-start(bf16[2,1,160,128]{3,2,1,0:T(8,128)(2,1)} %get-tuple-element.63), channel_id=1, source_target_pairs={{0,8},{1,9},{2,10},{3,11},{4,12},{5,13},{6,14},{7,15},{8,0},{9,1},... | collective-permute-start | bytes 245768 | tf_op jit(solution)/shard_map/ppermute | solution.py:541
  179.6 12.0 %collective-permute-start.9 = (bf16[2,1,160,128]{3,2,1,0:T(8,128)(2,1)}, bf16[2,1,160,128]{3,2,1,0:T(8,128)(2,1)S(1)}, u32[]{:S(2)}, u32[]{:S(2)}) collective-permute-start(bf16[2,1,160,128]{3,2,1,0:T(8,128)(2,1)} %get-tuple-element.64), channel_id=1, source_target_pairs={{0,10},{1,11},{2,8},{3,9},{4,14},{5,15},{6,12},{7,13},{8,2},{9,3},... | collective-permute-start | bytes 245768 | tf_op jit(solution)/shard_map/ppermute | solution.py:541
  184.1 9.9 %collective-permute-start.10 = (bf16[2,1,160,128]{3,2,1,0:T(8,128)(2,1)}, bf16[2,1,160,128]{3,2,1,0:T(8,128)(2,1)}, u32[]{:S(2)}, u32[]{:S(2)}) collective-permute-start(bf16[2,1,160,128]{3,2,1,0:T(8,128)(2,1)} %get-tuple-element.65), channel_id=1, source_target_pairs={{0,12},{1,13},{2,14},{3,15},{4,8},{5,9},{6,10},{7,11},{8,4},{9,5},... | collective-permute-start | bytes 245768 | tf_op jit(solution)/shard_map/ppermute | solution.py:541
  184.1 12.1 %collective-permute-start.11 = (bf16[2,1,160,128]{3,2,1,0:T(8,128)(2,1)}, bf16[2,1,160,128]{3,2,1,0:T(8,128)(2,1)}, u32[]{:S(2)}, u32[]{:S(2)}) collective-permute-start(bf16[2,1,160,128]{3,2,1,0:T(8,128)(2,1)} %get-tuple-element.66), channel_id=1, source_target_pairs={{0,14},{1,15},{2,12},{3,13},{4,10},{5,11},{6,8},{7,9},{8,6},{9,7},... | collective-permute-start | bytes 245768 | tf_op jit(solution)/shard_map/ppermute | solution.py:541
  185.5 2.8 %copy-start.5 = (bf16[2,2,160,128]{3,2,1,0:T(8,128)(2,1)S(1)}, bf16[2,2,160,128]{3,2,1,0:T(8,128)(2,1)}, u32[]{:S(2)}) copy-start(bf16[2,2,160,128]{3,2,1,0:T(8,128)(2,1)} %copy-done.4) | copy-start | bytes 491524
  185.5 2.8 %copy-start.7 = (bf16[2,2,160,128]{3,2,1,0:T(8,128)(2,1)S(1)}, bf16[2,2,160,128]{3,2,1,0:T(8,128)(2,1)}, u32[]{:S(2)}) copy-start(bf16[2,2,160,128]{3,2,1,0:T(8,128)(2,1)} %copy-done.6) | copy-start | bytes 491524

commit v20 on v19

--- a/solution.py
+++ b/solution.py
@@ -11,6 +11,7 @@
 BF16 = jnp.bfloat16
 F32 = jnp.float32
 CORES = 2
+PLANES = (0, 2, 1, 3)
 ANYWHERE = pl.BlockSpec(memory_space=pl.ANY)
 IN_SMEM = pl.BlockSpec(memory_space=pltpu.SMEM)
 IN_HBM = pl.BlockSpec(memory_space=pltpu.HBM)
@@ -37,6 +38,11 @@
         copy.start()
     for copy in copies:
         copy.wait()
+
+
+def place_of(chip, chips):
+    quarter = chips // len(PLANES)
+    return PLANES[chip // quarter] * quarter + chip % quarter
 
 
 def messages_of(chips, rows):
@@ -108,12 +114,13 @@
                 if split:
                     mine, others = split_cores(values, core)
                     for i, (a, b) in enumerate(zip(mine, others)):
-                        done[start // CORES + i, 0, r, j : j + depth, :] = a.astype(BF16)
-                        done[start // CORES + i, 1, r, j : j + depth, :] = b.astype(BF16)
+                        place = place_of(start // CORES + i, done.shape[0])
+                        done[place, 0, r, j : j + depth, :] = a.astype(BF16)
+                        done[place, 1, r, j : j + depth, :] = b.astype(BF16)
                 else:
                     for i, value in enumerate(values):
                         chip, target = divmod(start + i, CORES)
-                        done[chip, target, r, j : j + depth, :] = value.astype(BF16)
+                        done[place_of(chip, done.shape[0]), target, r, j : j + depth, :] = value.astype(BF16)
             if (j + depth) % size == 0:
                 part = pl.ds(j + depth - size, size)
                 source, target = done.at[:, :, r, part], outs[0].at[:, :, r, part]
@@ -242,15 +249,19 @@
     chips, cores, lats, _ = grid.shape
     core = me_ref[0] % CORES
     moves = []
-    for r in range(rows):
-        lanes = pl.ds(r * members, members)
-        if len(blocks) == 1:
-            moves.append(pltpu.make_async_copy(blocks[0].at[:, :, r], grid.at[:, :, :, lanes], block_sems.at[0, r]))
-        else:
-            target = grid.at[:, core, :, lanes]
-            moves.append(pltpu.make_async_copy(blocks[0].at[:, core, r], target, block_sems.at[0, r]))
-            target = grid.at[:, CORES - 1 - core, :, lanes]
-            moves.append(pltpu.make_async_copy(blocks[1].at[:, r], target, block_sems.at[1, r]))
+    quarter = max(chips // len(PLANES), 1)
+    for q in range(chips // quarter):
+        here, there = pl.ds(q * quarter, quarter), pl.ds(place_of(q * quarter, chips) if chips > 1 else 0, quarter)
+        for r in range(rows):
+            lanes = pl.ds(r * members, members)
+            if len(blocks) == 1:
+                source, target = blocks[0].at[there, :, r], grid.at[here, :, :, lanes]
+                moves.append(pltpu.make_async_copy(source, target, block_sems.at[0, r, q]))
+            else:
+                source, target = blocks[0].at[there, core, r], grid.at[here, core, :, lanes]
+                moves.append(pltpu.make_async_copy(source, target, block_sems.at[0, r, q]))
+                source, target = blocks[1].at[there, r], grid.at[here, CORES - 1 - core, :, lanes]
+                moves.append(pltpu.make_async_copy(source, target, block_sems.at[1, r, q]))
     cuts = sorted(set([0] + list(range(width % 256, width + 1, 256))))
     copies = []
     for i, (start, end) in enumerate(zip(cuts, cuts[1:])):
@@ -283,7 +294,9 @@
             own = lax.dynamic_index_in_dim(blocks[0], core, 1, keepdims=False)
             pairs = [jnp.where(core == 0, own, blocks[1]), jnp.where(core == 0, blocks[1], own)]
             blocks = [jnp.stack(pairs, axis=1)]
-        laid = jnp.transpose(blocks[0], (2, 0, 1, 3, 4)).reshape(1, 1, rows, nlat, members)
+        quarter = chips // len(PLANES)
+        laid = jnp.concatenate([blocks[0][q * quarter : (q + 1) * quarter] for q in PLANES])
+        laid = jnp.transpose(laid, (2, 0, 1, 3, 4)).reshape(1, 1, rows, nlat, members)
         blocks, chips, cores, lats = [laid], 1, 1, nlat
     return call(
         functools.partial(analyse_kernel, slot, low),
@@ -302,7 +315,7 @@
                 pltpu.VMEM((rows, members, width), BF16),
                 pltpu.SemaphoreType.DMA((width // 256 + 1,)),
                 pltpu.SemaphoreType.DMA,
-                pltpu.SemaphoreType.DMA((CORES, rows)),
+                pltpu.SemaphoreType.DMA((CORES, rows, len(PLANES))),
             ],
         ),
     )(me, wave, token, in_hbm(table), in_hbm(state), in_hbm(blocks[0]), *blocks[1:])
@@ -415,10 +428,16 @@
     whole = pl.BlockSpec((rows, members, count), lambda j, m: (0, 0, 0))
     smem = pl.BlockSpec(memory_space=pltpu.SMEM)
     shapes = [jax.ShapeDtypeStruct((chips, CORES, rows, lats, members), BF16)]
-    specs = [pl.BlockSpec((each, 1, rows, lats, members), lambda j, m: (j, m[0] % CORES, 0, 0, 0))]
+
+    def place(j):
+        per = chips // len(PLANES) // each
+        q = j // per
+        return j if apart else jnp.where(q == 1, j + per, jnp.where(q == 2, j - per, j))
+
+    specs = [pl.BlockSpec((each, 1, rows, lats, members), lambda j, m: (place(j), m[0] % CORES, 0, 0, 0))]
     scratch = [pltpu.VMEM((rows * members, count), BF16)]
     shapes += [jax.ShapeDtypeStruct((chips, rows, lats, members), BF16)]
-    specs += [pl.BlockSpec((each, rows, lats, members), lambda j, m: (j, 0, 0, 0))]
+    specs += [pl.BlockSpec((each, rows, lats, members), lambda j, m: (place(j), 0, 0, 0))]
     sums = pl.BlockSpec((rows * members, width), lambda j, m: (0, j))
     if more:
         shapes, specs = [jax.ShapeDtypeStruct((rows * members, nlat), F32)], [sums]
@@ -480,7 +499,9 @@
             if slot == moved:
                 parts.append(held[place, owner % CORES, r, start : start + depth, :])
             else:
-                parts.append(blocks_ref[side * half + place, owner % CORES, first + r, start : start + depth, :])
+                plane, rest = divmod(place, half // 2)
+                there = (side + 2 * plane) * (half // 2) + rest
+                parts.append(blocks_ref[there, owner % CORES, first + r, start : start + depth, :])
         return jnp.concatenate(parts, axis=0)
 
     for r in range(rows):
@@ -543,7 +564,8 @@
 
 
 def between_chips(blocks, owners):
-    groups = [list(range(core, owners, CORES)) for core in range(CORES)]
+    chips = owners // CORES
+    groups = [[place_of(i, chips) * CORES + core for i in range(chips)] for core in range(CORES)]
     return lax.all_to_all(blocks, "wave", split_axis=0, concat_axis=0, axis_index_groups=groups, tiled=True)
 
 

time: 199 us -> 203 us (1.020)
  waiting for transfers between devices: 94.6 us -> 101 us
  starting transfers between devices: 42.7 us -> 37.9 us
    all_to_all x3, waiting for transfers between devices: 34.6 us -> 39.3 us  [between_chips(): lax.all_to_all(blocks, 'wave', split_axis=0, concat_axis=0, axis_index_gr...]
    all_to_all x3, starting transfers between devices: 19.6 us -> 17.2 us  [between_chips(): lax.all_to_all(blocks, 'wave', split_axis=0, concat_axis=0, axis_index_gr...]
    ppermute x11, starting transfers between devices: 17.5 us -> 15.1 us  [by_permutes(): got.append(lax.ppermute(message, 'wave', moves) if k else message)]
    ppermute x11, waiting for transfers between devices: 23.2 us -> 25.4 us  [by_permutes(): got.append(lax.ppermute(message, 'wave', moves) if k else message)]
where the time goes in v20:
time: 203 us; the launch traced here: 201 us
  waiting for transfers between devices  101 us (50%)
  Pallas kernels  56.7 us (28%)
  starting transfers between devices  37.9 us (19%)
  local copies, waits for them, and re-layouts  5.22 us (3%)
    all_to_all x3, waiting for transfers between devices, between_chips(): lax.all_to_all(blocks, 'wave', split_axis=0, concat_axis=0, axis_index_gr...  39.3 us
    ppermute x11, waiting for transfers between devices, by_permutes(): got.append(lax.ppermute(message, 'wave', moves) if k else message)  25.4 us
    ppermute x3, waiting for transfers between devices, per_device(): others = [lax.ppermute(part, 'pole', [(0, 1), (1, 0)]) for part in forced]  21.8 us
    pallas_call x3, Pallas kernels, analyse(): call(functools.partial(analyse_kernel, slot, low), 'analyse', 2 * width *...  18.2 us
    all_to_all x3, starting transfers between devices, between_chips(): lax.all_to_all(blocks, 'wave', split_axis=0, concat_axis=0, axis_index_gr...  17.2 us
    pallas_call x3, Pallas kernels, synthesise(): call(functools.partial(synthesise_kernel, slot, low, apart, more, len(par...  16.5 us
    ppermute x11, starting transfers between devices, by_permutes(): got.append(lax.ppermute(message, 'wave', moves) if k else message)  15.1 us
    ppermute x4, waiting for transfers between devices, between_cores(): return lax.ppermute(blocks, 'wave', [(d, d ^ 1) for d in range(owners)])  10.4 us
  transfers between devices with their start and end apart: 22, of which 16 were waited for; matrix products, arithmetic and copies ran while one was open for 0% of the time, Pallas kernels for 25%

profile of v20, /device:TPU:8, one launch (start us, length us, event | category | flops | bytes accessed | tf_op | source)
XLA Modules:
  0.0 201.5 jit_solution(7846010496569744507)
XLA Ops:
  0.0 4.1 %weigh.2 = (bf16[8,2,3,160,128]{4,3,2,1,0:T(8,128)(2,1)}, f32[8,128]{1,0:T(8,128)}) custom-call(s32[1]{0:T(128)} %bitcast.me_ref, f32[1,160]{1,0:T(1,128)} %bitcast.3, bf16[3,160,32,128]{3,2,1,0:T(8,128)(2,1)} %tendency_ref.3), custom_call_target="tpu_custom_call" | custom-call | flops 503316480 | bytes 5898240 | tf_op jit(solution)/shard_map/weigh/pallas_call | solution.py:147
  4.1 0.0 copy-start.10
  4.1 6.3 %all-to-all-start = ((bf16[8,2,3,160,128]{4,3,2,1,0:T(8,128)(2,1)}), bf16[8,2,3,160,128]{4,3,2,1,0:T(8,128)(2,1)}, u32[]{:S(2)}, u32[]{:S(2)}) async-start(bf16[8,2,3,160,128]{4,3,2,1,0:T(8,128)(2,1)} %get-tuple-element.44), calls=%async_computation | async-start | bytes 3932160 | tf_op jit(solution)/shard_map/all_to_all | solution.py:569
  10.4 0.1 copy.24.coeff_ref
  10.5 1.8 copy-done.3
  12.3 2.4 %sum_pairs.1.here_ref = f32[18,2,1280]{2,1,0:T(2,128)S(1)} custom-call(f32[32,2]{1,0:T(8,128)S(1)} %copy.24.coeff_ref, f32[8,128]{1,0:T(8,128)S(1)} %copy-done.9, bf16[32,18,2,1280]{3,2,1,0:T(2,128)(2,1)S(1)} %copy-done.3), custom_call_target="tpu_custom_call" | custom-call | flops 5898240 | bytes 2949120 | tf_op jit(solution)/shard_map/sum_pairs/pallas_call | solution.py:343
  14.7 1.6 collective-permute-start
  16.3 4.3 %collective-permute-done.rest_0_.there_ref = f32[18,2,1280]{2,1,0:T(2,128)S(1)} collective-permute-done((f32[18,2,1280]{2,1,0:T(2,128)S(1)}, f32[18,2,1280]{2,1,0:T(2,128)S(1)}, u32[]{:S(2)}, u32[]{:S(2)}) %collective-permute-start) | collective-permute-done | bytes 184352 | tf_op jit(solution)/shard_map/ppermute | solution.py:589
  20.6 0.7 copy-done.1
  21.3 4.2 %weigh.3 = (bf16[8,2,3,160,128]{4,3,2,1,0:T(8,128)(2,1)}, bf16[8,3,160,128]{3,2,1,0:T(8,128)(2,1)}, f32[8,128]{1,0:T(8,128)}) custom-call(s32[1]{0:T(128)} %bitcast.me_ref, f32[1,160]{1,0:T(1,128)} %bitcast.4, bf16[3,160,32,128]{3,2,1,0:T(8,128)(2,1)} %tendency_ref.3, f32[18,2,1280]{2,1,0:T(2,128)} %copy-done.1), custom_call_target="tpu_custom_call" | custom-call | flops 503316480 | bytes 5898240 | tf_op jit(solution)/shard_map/weigh/pallas_call | solution.py:147
  25.4 0.1 collective-permute-start.1
  25.5 2.8 %collective-permute-done.1.mate_ref = bf16[8,3,160,128]{3,2,1,0:T(8,128)(2,1)S(1)} collective-permute-done((bf16[8,3,160,128]{3,2,1,0:T(8,128)(2,1)}, bf16[8,3,160,128]{3,2,1,0:T(8,128)(2,1)S(1)}, u32[]{:S(2)}, u32[]{:S(2)}) %collective-permute-start.1) | collective-permute-done | bytes 983072 | tf_op jit(solution)/shard_map/ppermute | solution.py:555
  28.3 0.9 pair.3
  29.2 26.2 %all-to-all-done.in_ref.rest_0_ = bf16[8,2,3,160,128]{4,3,2,1,0:T(8,128)(2,1)} async-done(((bf16[8,2,3,160,128]{4,3,2,1,0:T(8,128)(2,1)}), bf16[8,2,3,160,128]{4,3,2,1,0:T(8,128)(2,1)}, u32[]{:S(2)}, u32[]{:S(2)}) %all-to-all-start) | async-done | bytes 1966112 | tf_op jit(solution)/shard_map/all_to_all | solution.py:569
  55.4 5.4 %all-to-all-start.2 = ((bf16[8,2,3,160,128]{4,3,2,1,0:T(8,128)(2,1)}), bf16[8,2,3,160,128]{4,3,2,1,0:T(8,128)(2,1)}, u32[]{:S(2)}, u32[]{:S(2)}) async-start(bf16[8,2,3,160,128]{4,3,2,1,0:T(8,128)(2,1)} %get-tuple-element.49), calls=%async_computation.2 | async-start | bytes 3932160 | tf_op jit(solution)/shard_map/all_to_all | solution.py:569
  60.8 1.3 pick.1
  62.1 0.1 collective-permute-start.2
  62.2 2.6 %collective-permute-done.2.rest_1_ = bf16[8,3,160,128]{3,2,1,0:T(8,128)(2,1)S(1)} collective-permute-done((bf16[8,3,160,128]{3,2,1,0:T(8,128)(2,1)S(1)}, bf16[8,3,160,128]{3,2,1,0:T(8,128)(2,1)S(1)}, u32[]{:S(2)}, u32[]{:S(2)}) %collective-permute-start.2) | collective-permute-done | bytes 983072 | tf_op jit(solution)/shard_map/ppermute | solution.py:555
  64.7 5.9 %analyse.3.own_ref = bf16[3,128,640]{2,1,0:T(8,128)(2,1)S(1)} custom-call(s32[1]{0:T(128)} %bitcast.me_ref, s32[2]{0:T(128)S(1)} %copy-done.8, f32[8,128]{1,0:T(8,128)S(1)} %get-tuple-element.43.token_ref, bf16[2,1280,2560]{2,1,0:T(8,128)(2,1)} %table_ref.11, bf16[3,2,128,1280]{3,2,1,0:T(8,128)(2,1)} %state_ref.5, ...), custom_call_target="tpu_custom_call" | custom-call | flops 1258291200 | bytes 3276800 | tf_op jit(solution)/shard_map/analyse/pallas_call | solution.py:301
  70.6 1.6 collective-permute-start.3
  72.2 11.7 %collective-permute-done.3.other_ref = bf16[3,128,640]{2,1,0:T(8,128)(2,1)S(1)} collective-permute-done((bf16[3,128,640]{2,1,0:T(8,128)(2,1)S(1)}, bf16[3,128,640]{2,1,0:T(8,128)(2,1)S(1)}, u32[]{:S(2)}, u32[]{:S(2)}) %collective-permute-start.3) | collective-permute-done | bytes 491552 | tf_op jit(solution)/shard_map/ppermute | solution.py:603
  83.9 5.0 %synthesise.3 = (bf16[8,2,3,160,128]{4,3,2,1,0:T(8,128)(2,1)S(1)}, bf16[8,3,160,128]{3,2,1,0:T(8,128)(2,1)S(1)}) custom-call(s32[1]{0:T(128)} %bitcast.me_ref, f32[1]{0:T(128)} %bitcast.1.sign_ref, f32[18,2,1280]{2,1,0:T(2,128)S(1)} %sum_pairs.1.here_ref, f32[18,2,1280]{2,1,0:T(2,128)S(1)} %copy-done.2, bf16[3,128,640]{2,1,0:T(8,128)(2,1)S(1)} %analyse.3.own_ref, ...), custom_call_target="tpu_custom_call" | custom-call | flops 1258291200 | bytes 3276800 | tf_op jit(solution)/shard_map/synthesise/pallas_call | solution.py:449
  88.9 0.1 collective-permute-start.4
  89.0 2.6 %collective-permute-done.4.mate_ref = bf16[8,3,160,128]{3,2,1,0:T(8,128)(2,1)S(1)} collective-permute-done((bf16[8,3,160,128]{3,2,1,0:T(8,128)(2,1)S(1)}, bf16[8,3,160,128]{3,2,1,0:T(8,128)(2,1)S(1)}, u32[]{:S(2)}, u32[]{:S(2)}) %collective-permute-start.4) | collective-permute-done | bytes 983072 | tf_op jit(solution)/shard_map/ppermute | solution.py:555
  91.5 0.1 pair.4
  91.6 0.0 copy-start
  91.6 1.3 copy-done
  92.9 13.1 %all-to-all-done.2.rest_0_ = bf16[8,2,3,160,128]{4,3,2,1,0:T(8,128)(2,1)} async-done(((bf16[8,2,3,160,128]{4,3,2,1,0:T(8,128)(2,1)}), bf16[8,2,3,160,128]{4,3,2,1,0:T(8,128)(2,1)}, u32[]{:S(2)}, u32[]{:S(2)}) %all-to-all-start.2) | async-done | bytes 1966112 | tf_op jit(solution)/shard_map/all_to_all | solution.py:569
  106.0 5.5 %all-to-all-start.1 = ((bf16[8,2,3,160,128]{4,3,2,1,0:T(8,128)(2,1)}), bf16[8,2,3,160,128]{4,3,2,1,0:T(8,128)(2,1)S(1)}, u32[]{:S(2)}, u32[]{:S(2)}) async-start(bf16[8,2,3,160,128]{4,3,2,1,0:T(8,128)(2,1)} %copy-done), calls=%async_computation.1 | async-start | bytes 3932160 | tf_op jit(solution)/shard_map/all_to_all | solution.py:569
  111.5 6.1 %analyse.5.own_ref = bf16[3,128,640]{2,1,0:T(8,128)(2,1)S(1)} custom-call(s32[1]{0:T(128)} %bitcast.me_ref, s32[2]{0:T(128)S(1)} %copy-done.8, f32[8,128]{1,0:T(8,128)S(1)} %get-tuple-element.48.token_ref, bf16[2,1280,2560]{2,1,0:T(8,128)(2,1)} %table_ref.11, bf16[3,2,128,1280]{3,2,1,0:T(8,128)(2,1)} %state_ref.5, ...), custom_call_target="tpu_custom_call" | custom-call | flops 1258291200 | bytes 3276800 | tf_op jit(solution)/shard_map/analyse/pallas_call | solution.py:301
  117.7 1.6 collective-permute-start.6
  119.3 6.1 %analyse.4.own_ref = bf16[3,128,640]{2,1,0:T(8,128)(2,1)S(1)} custom-call(s32[1]{0:T(128)} %bitcast.me_ref, s32[2]{0:T(128)S(1)} %copy-done.8, f32[8,128]{1,0:T(8,128)S(1)} %get-tuple-element.48.token_ref, bf16[2,1280,2560]{2,1,0:T(8,128)(2,1)} %table_ref.11, bf16[3,2,128,1280]{3,2,1,0:T(8,128)(2,1)} %state_ref.5, ...), custom_call_target="tpu_custom_call" | custom-call | flops 1258291200 | bytes 3276800 | tf_op jit(solution)/shard_map/analyse/pallas_call | solution.py:301
  125.4 0.6 collective-permute-start.5
  126.0 5.9 %collective-permute-done.6.other_ref = bf16[3,128,640]{2,1,0:T(8,128)(2,1)S(1)} collective-permute-done((bf16[3,128,640]{2,1,0:T(8,128)(2,1)S(1)}, bf16[3,128,640]{2,1,0:T(8,128)(2,1)S(1)}, u32[]{:S(2)}, u32[]{:S(2)}) %collective-permute-start.6) | collective-permute-done | bytes 491552 | tf_op jit(solution)/shard_map/ppermute | solution.py:603
  131.9 4.8 %synthesise.4.rest_0_ = f32[384,2560]{1,0:T(8,128)S(1)} custom-call(s32[1]{0:T(128)} %bitcast.me_ref, f32[1]{0:T(128)} %bitcast.1.sign_ref, f32[18,2,1280]{2,1,0:T(2,128)S(1)} %sum_pairs.1.here_ref, f32[18,2,1280]{2,1,0:T(2,128)S(1)} %copy-done.2, bf16[3,128,640]{2,1,0:T(8,128)(2,1)S(1)} %analyse.5.own_ref, ...), custom_call_target="tpu_custom_call" | custom-call | flops 1258291200 | bytes 3276800 | tf_op jit(solution)/shard_map/synthesise/pallas_call | solution.py:449
  136.7 4.1 %collective-permute-done.5.other_ref = bf16[3,128,640]{2,1,0:T(8,128)(2,1)S(1)} collective-permute-done((bf16[3,128,640]{2,1,0:T(8,128)(2,1)S(1)}, bf16[3,128,640]{2,1,0:T(8,128)(2,1)S(1)}, u32[]{:S(2)}, u32[]{:S(2)}) %collective-permute-start.5) | collective-permute-done | bytes 491552 | tf_op jit(solution)/shard_map/ppermute | solution.py:603
  140.9 6.7 %synthesise.5 = (bf16[2,3,160,128]{3,2,1,0:T(8,128)(2,1)S(1)}, bf16[2,2,160,128]{3,2,1,0:T(8,128)(2,1)S(1)}, bf16[2,2,160,128]{3,2,1,0:T(8,128)(2,1)S(1)}, bf16[...) custom-call(s32[1]{0:T(128)} %bitcast.me_ref, ...), custom_call_target="tpu_custom_call" | custom-call | flops 1258291200 | bytes 3276800 | tf_op jit(solution)/shard_map/synthesise/pallas_call | solution.py:449
  147.6 0.1 collective-permute-start.7
  147.7 2.6 %collective-permute-done.7.mate_ref = bf16[8,3,160,128]{3,2,1,0:T(8,128)(2,1)S(1)} collective-permute-done((bf16[8,3,160,128]{3,2,1,0:T(8,128)(2,1)S(1)}, bf16[8,3,160,128]{3,2,1,0:T(8,128)(2,1)S(1)}, u32[]{:S(2)}, u32[]{:S(2)}) %collective-permute-start.7) | collective-permute-done | bytes 983072 | tf_op jit(solution)/shard_map/ppermute | solution.py:555
  150.2 1.3 pair.5
  151.6 1.8 collective-permute-start.12
  153.3 2.1 %collective-permute-start.13 = (bf16[2,2,160,128]{3,2,1,0:T(8,128)(2,1)S(1)}, bf16[2,2,160,128]{3,2,1,0:T(8,128)(2,1)S(1)}, u32[]{:S(2)}, u32[]{:S(2)}) collective-permute-start(bf16[2,2,160,128]{3,2,1,0:T(8,128)(2,1)S(1)} %get-tuple-element.68), channel_id=1, source_target_pairs={{0,10},{1,11},{2,8},{3,9},{4,14},{5,15},{6,12},{7,13},{8,2},{9,3},... | collective-permute-start | bytes 491528 | tf_op jit(solution)/shard_map/ppermute | solution.py:562
  155.4 0.6 collective-permute-start.16
  156.0 0.3 collective-permute-start.17
  156.3 2.6 %collective-permute-start.18 = (bf16[2,3,160,128]{3,2,1,0:T(8,128)(2,1)S(1)}, bf16[2,3,160,128]{3,2,1,0:T(8,128)(2,1)S(1)}, u32[]{:S(2)}, u32[]{:S(2)}) collective-permute-start(bf16[2,3,160,128]{3,2,1,0:T(8,128)(2,1)S(1)} %get-tuple-element.74), channel_id=1, source_target_pairs={{0,6},{1,7},{2,4},{3,5},{4,2},{5,3},{6,0},{7,1},{8,14},{9,15},{10,... | collective-permute-start | bytes 737288 | tf_op jit(solution)/shard_map/ppermute | solution.py:562
  158.9 7.8 %collective-permute-done.12.rest_0_ = bf16[2,2,160,128]{3,2,1,0:T(8,128)(2,1)S(1)} collective-permute-done((bf16[2,2,160,128]{3,2,1,0:T(8,128)(2,1)S(1)}, bf16[2,2,160,128]{3,2,1,0:T(8,128)(2,1)S(1)}, u32[]{:S(2)}, u32[]{:S(2)}) %collective-permute-start.12) | collective-permute-done | bytes 163872 | tf_op jit(solution)/shard_map/ppermute | solution.py:562
  166.7 0.1 collective-permute-start.14
  166.8 3.4 %collective-permute-done.13.rest_1_ = bf16[2,2,160,128]{3,2,1,0:T(8,128)(2,1)S(1)} collective-permute-done((bf16[2,2,160,128]{3,2,1,0:T(8,128)(2,1)S(1)}, bf16[2,2,160,128]{3,2,1,0:T(8,128)(2,1)S(1)}, u32[]{:S(2)}, u32[]{:S(2)}) %collective-permute-start.13) | collective-permute-done | bytes 163872 | tf_op jit(solution)/shard_map/ppermute | solution.py:562
  170.3 0.7 copy-done.4
  170.9 1.3 collective-permute-start.15
  172.2 8.6 %collective-permute-done.14.rest_2_ = bf16[2,2,160,128]{3,2,1,0:T(8,128)(2,1)S(1)} collective-permute-done((bf16[2,2,160,128]{3,2,1,0:T(8,128)(2,1)S(1)}, bf16[2,2,160,128]{3,2,1,0:T(8,128)(2,1)S(1)}, u32[]{:S(2)}, u32[]{:S(2)}) %collective-permute-start.14) | collective-permute-done | bytes 163872 | tf_op jit(solution)/shard_map/ppermute | solution.py:562
  180.8 0.7 copy-done.6
  181.5 0.0 collective-permute-start.8
  181.5 0.0 collective-permute-done.16.rest_1_
  181.5 4.9 %collective-permute-start.9 = (bf16[2,1,160,128]{3,2,1,0:T(8,128)(2,1)}, bf16[2,1,160,128]{3,2,1,0:T(8,128)(2,1)S(1)}, u32[]{:S(2)}, u32[]{:S(2)}) collective-permute-start(bf16[2,1,160,128]{3,2,1,0:T(8,128)(2,1)} %get-tuple-element.64), channel_id=1, source_target_pairs={{0,10},{1,11},{2,8},{3,9},{4,14},{5,15},{6,12},{7,13},{8,2},{9,3},... | collective-permute-start | bytes 245768 | tf_op jit(solution)/shard_map/ppermute | solution.py:562
  186.4 0.0 collective-permute-done.17.rest_2_
  186.4 0.3 collective-permute-start.10
  186.7 1.2 collective-permute-start.11
  187.8 2.7 %assemble.3.rest_4_ = bf16[3,160,32,128]{3,2,1,0:T(8,128)(2,1)} custom-call(s32[1]{0:T(128)} %bitcast.me_ref, bf16[8,2,3,160,128]{4,3,2,1,0:T(8,128)(2,1)S(1)} %all-to-all-done.1.blocks_ref, bf16[2,3,160,128]{3,2,1,0:T(8,128)(2,1)S(1)} %get-tuple-element.71.rest_0_, bf16[2,3,160,128]{3,2,1,0:T(8,128)(2,1)S(1)} %collective-permute-done.16.rest_1_, ...), custom_call_target="tpu_custom_call" | custom-call | flops 503316480 | bytes 3932160 | tf_op jit(solution)/shard_map/assemble/pallas_call | solution.py:536
  190.6 2.7 %assemble.4.rest_4_ = bf16[3,160,32,128]{3,2,1,0:T(8,128)(2,1)} custom-call(s32[1]{0:T(128)} %bitcast.me_ref, bf16[8,2,3,160,128]{4,3,2,1,0:T(8,128)(2,1)S(1)} %all-to-all-done.1.blocks_ref, bf16[2,2,160,128]{3,2,1,0:T(8,128)(2,1)S(1)} %collective-permute-done.12.rest_0_, bf16[2,2,160,128]{3,2,1,0:T(8,128)(2,1)S(1)} %copy-done.5, ...), custom_call_target="tpu_custom_call", output_to_operand_aliasing={{}: (6, {})} | custom-call | flops 335544320 | bytes 2621440 | tf_op jit(solution)/shard_map/assemble/pallas_call | solution.py:536
  193.4 1.6 collective-permute-done.9.rest_1_
  194.9 2.6 %collective-permute-done.10.rest_2_ = bf16[2,1,160,128]{3,2,1,0:T(8,128)(2,1)} collective-permute-done((bf16[2,1,160,128]{3,2,1,0:T(8,128)(2,1)}, bf16[2,1,160,128]{3,2,1,0:T(8,128)(2,1)}, u32[]{:S(2)}, u32[]{:S(2)}) %collective-permute-start.10) | collective-permute-done | bytes 81952 | tf_op jit(solution)/shard_map/ppermute | solution.py:562
  197.6 1.4 collective-permute-done.11.rest_3_
  199.0 2.3 %assemble.5 = bf16[3,160,32,128]{3,2,1,0:T(8,128)(2,1)} custom-call(s32[1]{0:T(128)} %bitcast.me_ref, bf16[8,2,3,160,128]{4,3,2,1,0:T(8,128)(2,1)S(1)} %all-to-all-done.1.blocks_ref, bf16[2,1,160,128]{3,2,1,0:T(8,128)(2,1)S(1)} %collective-permute-done.8.rest_0_, ...), custom_call_target="tpu_custom_call", output_to_operand_aliasing={{}: (6, {})} | custom-call | flops 167772160 | bytes 1310720 | tf_op jit(solution)/shard_map/assemble/pallas_call | solution.py:536
  (19 shorter events, 0.0 us)
Async XLA Ops:
  4.1 6.3 %copy-start.10 = (f32[32,2]{0,1:T(2,128)S(1)}, f32[32,2]{0,1:T(2,128)}, u32[]{:S(2)}) copy-start(f32[32,2]{0,1:T(2,128)} %param.12) | copy-start | bytes 772
  4.1 6.4 %copy-start.9 = (f32[8,128]{1,0:T(8,128)S(1)}, f32[8,128]{1,0:T(8,128)}, u32[]{:S(2)}) copy-start(f32[8,128]{1,0:T(8,128)} %get-tuple-element.40.token_ref) | copy-start | bytes 12292
  4.1 51.3 %all-to-all-start = ((bf16[8,2,3,160,128]{4,3,2,1,0:T(8,128)(2,1)}), bf16[8,2,3,160,128]{4,3,2,1,0:T(8,128)(2,1)}, u32[]{:S(2)}, u32[]{:S(2)}) async-start(bf16[8,2,3,160,128]{4,3,2,1,0:T(8,128)(2,1)} %get-tuple-element.44), calls=%async_computation | async-start | bytes 3932160 | tf_op jit(solution)/shard_map/all_to_all | solution.py:569
  10.5 1.8 copy-start.3
  14.7 5.9 %collective-permute-start = (f32[18,2,1280]{2,1,0:T(2,128)S(1)}, f32[18,2,1280]{2,1,0:T(2,128)S(1)}, u32[]{:S(2)}, u32[]{:S(2)}) collective-permute-start(f32[18,2,1280]{2,1,0:T(2,128)S(1)} %sum_pairs.1.here_ref), channel_id=1, source_target_pairs={{0,16},{16,0},{1,17},{17,1},{2,18},{18,2},{3,19},{19,3},{4,20},{20... | collective-permute-start | bytes 552968 | tf_op jit(solution)/shard_map/ppermute | solution.py:589
  20.6 0.7 copy-start.1
  25.4 2.8 %collective-permute-start.1 = (bf16[8,3,160,128]{3,2,1,0:T(8,128)(2,1)}, bf16[8,3,160,128]{3,2,1,0:T(8,128)(2,1)S(1)}, u32[]{:S(2)}, u32[]{:S(2)}) collective-permute-start(bf16[8,3,160,128]{3,2,1,0:T(8,128)(2,1)} %get-tuple-element.41), channel_id=1, source_target_pairs={{0,1},{1,0},{2,3},{3,2},{4,5},{5,4},{6,7},{7,6},{8,9},{9,8},{10,11... | collective-permute-start | bytes 2949128 | tf_op jit(solution)/shard_map/ppermute | solution.py:555
  55.4 50.6 %all-to-all-start.2 = ((bf16[8,2,3,160,128]{4,3,2,1,0:T(8,128)(2,1)}), bf16[8,2,3,160,128]{4,3,2,1,0:T(8,128)(2,1)}, u32[]{:S(2)}, u32[]{:S(2)}) async-start(bf16[8,2,3,160,128]{4,3,2,1,0:T(8,128)(2,1)} %get-tuple-element.49), calls=%async_computation.2 | async-start | bytes 3932160 | tf_op jit(solution)/shard_map/all_to_all | solution.py:569
  60.8 3.9 %copy-start.8 = (s32[2]{0:T(128)S(1)}, s32[2]{0:T(128)}, u32[]{:S(2)}) copy-start(s32[2]{0:T(128)} %wave_ref.5) | copy-start | bytes 28
  62.1 21.9 %copy-start.2 = (f32[18,2,1280]{2,1,0:T(2,128)S(1)}, f32[18,2,1280]{2,1,0:T(2,128)}, u32[]{:S(2)}) copy-start(f32[18,2,1280]{2,1,0:T(2,128)} %copy-done.1) | copy-start | bytes 552964
  62.1 2.6 %collective-permute-start.2 = (bf16[8,3,160,128]{3,2,1,0:T(8,128)(2,1)S(1)}, bf16[8,3,160,128]{3,2,1,0:T(8,128)(2,1)S(1)}, u32[]{:S(2)}, u32[]{:S(2)}) collective-permute-start(bf16[8,3,160,128]{3,2,1,0:T(8,128)(2,1)S(1)} %pick.1), channel_id=1, source_target_pairs={{0,1},{1,0},{2,3},{3,2},{4,5},{5,4},{6,7},{7,6},{8,9},{9,8},{10,11... | collective-permute-start | bytes 2949128 | tf_op jit(solution)/shard_map/ppermute | solution.py:555
  70.6 13.3 %collective-permute-start.3 = (bf16[3,128,640]{2,1,0:T(8,128)(2,1)S(1)}, bf16[3,128,640]{2,1,0:T(8,128)(2,1)S(1)}, u32[]{:S(2)}, u32[]{:S(2)}) collective-permute-start(bf16[3,128,640]{2,1,0:T(8,128)(2,1)S(1)} %analyse.3.own_ref), channel_id=1, source_target_pairs={{0,16},{16,0},{1,17},{17,1},{2,18},{18,2},{3,19},{19,3},{4,20},{20... | collective-permute-start | bytes 1474568 | tf_op jit(solution)/shard_map/ppermute | solution.py:603
  88.9 2.6 %collective-permute-start.4 = (bf16[8,3,160,128]{3,2,1,0:T(8,128)(2,1)S(1)}, bf16[8,3,160,128]{3,2,1,0:T(8,128)(2,1)S(1)}, u32[]{:S(2)}, u32[]{:S(2)}) collective-permute-start(bf16[8,3,160,128]{3,2,1,0:T(8,128)(2,1)S(1)} %get-tuple-element.45), channel_id=1, source_target_pairs={{0,1},{1,0},{2,3},{3,2},{4,5},{5,4},{6,7},{7,6},{8,9},{9,8},{10,11... | collective-permute-start | bytes 2949128 | tf_op jit(solution)/shard_map/ppermute | solution.py:555
  91.6 1.3 copy-start
  106.0 81.8 %all-to-all-start.1 = ((bf16[8,2,3,160,128]{4,3,2,1,0:T(8,128)(2,1)}), bf16[8,2,3,160,128]{4,3,2,1,0:T(8,128)(2,1)S(1)}, u32[]{:S(2)}, u32[]{:S(2)}) async-start(bf16[8,2,3,160,128]{4,3,2,1,0:T(8,128)(2,1)} %copy-done), calls=%async_computation.1 | async-start | bytes 3932160 | tf_op jit(solution)/shard_map/all_to_all | solution.py:569
  117.7 14.2 %collective-permute-start.6 = (bf16[3,128,640]{2,1,0:T(8,128)(2,1)S(1)}, bf16[3,128,640]{2,1,0:T(8,128)(2,1)S(1)}, u32[]{:S(2)}, u32[]{:S(2)}) collective-permute-start(bf16[3,128,640]{2,1,0:T(8,128)(2,1)S(1)} %analyse.5.own_ref), channel_id=1, source_target_pairs={{0,16},{16,0},{1,17},{17,1},{2,18},{18,2},{3,19},{19,3},{4,20},{20... | collective-permute-start | bytes 1474568 | tf_op jit(solution)/shard_map/ppermute | solution.py:603
  125.4 15.4 %collective-permute-start.5 = (bf16[3,128,640]{2,1,0:T(8,128)(2,1)S(1)}, bf16[3,128,640]{2,1,0:T(8,128)(2,1)S(1)}, u32[]{:S(2)}, u32[]{:S(2)}) collective-permute-start(bf16[3,128,640]{2,1,0:T(8,128)(2,1)S(1)} %analyse.4.own_ref), channel_id=1, source_target_pairs={{0,16},{16,0},{1,17},{17,1},{2,18},{18,2},{3,19},{19,3},{4,20},{20... | collective-permute-start | bytes 1474568 | tf_op jit(solution)/shard_map/ppermute | solution.py:603
  147.6 2.6 %collective-permute-start.7 = (bf16[8,3,160,128]{3,2,1,0:T(8,128)(2,1)S(1)}, bf16[8,3,160,128]{3,2,1,0:T(8,128)(2,1)S(1)}, u32[]{:S(2)}, u32[]{:S(2)}) collective-permute-start(bf16[8,3,160,128]{3,2,1,0:T(8,128)(2,1)S(1)} %get-tuple-element.50), channel_id=1, source_target_pairs={{0,1},{1,0},{2,3},{3,2},{4,5},{5,4},{6,7},{7,6},{8,9},{9,8},{10,11... | collective-permute-start | bytes 2949128 | tf_op jit(solution)/shard_map/ppermute | solution.py:555
  151.6 15.2 %collective-permute-start.12 = (bf16[2,2,160,128]{3,2,1,0:T(8,128)(2,1)S(1)}, bf16[2,2,160,128]{3,2,1,0:T(8,128)(2,1)S(1)}, u32[]{:S(2)}, u32[]{:S(2)}) collective-permute-start(bf16[2,2,160,128]{3,2,1,0:T(8,128)(2,1)S(1)} %get-tuple-element.67), channel_id=1, source_target_pairs={{0,8},{1,9},{2,10},{3,11},{4,12},{5,13},{6,14},{7,15},{8,0},{9,1},... | collective-permute-start | bytes 491528 | tf_op jit(solution)/shard_map/ppermute | solution.py:562
  153.3 16.9 %collective-permute-start.13 = (bf16[2,2,160,128]{3,2,1,0:T(8,128)(2,1)S(1)}, bf16[2,2,160,128]{3,2,1,0:T(8,128)(2,1)S(1)}, u32[]{:S(2)}, u32[]{:S(2)}) collective-permute-start(bf16[2,2,160,128]{3,2,1,0:T(8,128)(2,1)S(1)} %get-tuple-element.68), channel_id=1, source_target_pairs={{0,10},{1,11},{2,8},{3,9},{4,14},{5,15},{6,12},{7,13},{8,2},{9,3},... | collective-permute-start | bytes 491528 | tf_op jit(solution)/shard_map/ppermute | solution.py:562
  155.4 26.1 %collective-permute-start.16 = (bf16[2,3,160,128]{3,2,1,0:T(8,128)(2,1)S(1)}, bf16[2,3,160,128]{3,2,1,0:T(8,128)(2,1)S(1)}, u32[]{:S(2)}, u32[]{:S(2)}) collective-permute-start(bf16[2,3,160,128]{3,2,1,0:T(8,128)(2,1)S(1)} %get-tuple-element.72), channel_id=1, source_target_pairs={{0,2},{1,3},{2,0},{3,1},{4,6},{5,7},{6,4},{7,5},{8,10},{9,11},{10,... | collective-permute-start | bytes 737288 | tf_op jit(solution)/shard_map/ppermute | solution.py:562
  156.0 30.4 %collective-permute-start.17 = (bf16[2,3,160,128]{3,2,1,0:T(8,128)(2,1)S(1)}, bf16[2,3,160,128]{3,2,1,0:T(8,128)(2,1)S(1)}, u32[]{:S(2)}, u32[]{:S(2)}) collective-permute-start(bf16[2,3,160,128]{3,2,1,0:T(8,128)(2,1)S(1)} %get-tuple-element.73), channel_id=1, source_target_pairs={{0,4},{1,5},{2,6},{3,7},{4,0},{5,1},{6,2},{7,3},{8,12},{9,13},{10,... | collective-permute-start | bytes 737288 | tf_op jit(solution)/shard_map/ppermute | solution.py:562
  156.3 30.4 %collective-permute-start.18 = (bf16[2,3,160,128]{3,2,1,0:T(8,128)(2,1)S(1)}, bf16[2,3,160,128]{3,2,1,0:T(8,128)(2,1)S(1)}, u32[]{:S(2)}, u32[]{:S(2)}) collective-permute-start(bf16[2,3,160,128]{3,2,1,0:T(8,128)(2,1)S(1)} %get-tuple-element.74), channel_id=1, source_target_pairs={{0,6},{1,7},{2,4},{3,5},{4,2},{5,3},{6,0},{7,1},{8,14},{9,15},{10,... | collective-permute-start | bytes 737288 | tf_op jit(solution)/shard_map/ppermute | solution.py:562
  166.7 14.1 %collective-permute-start.14 = (bf16[2,2,160,128]{3,2,1,0:T(8,128)(2,1)S(1)}, bf16[2,2,160,128]{3,2,1,0:T(8,128)(2,1)S(1)}, u32[]{:S(2)}, u32[]{:S(2)}) collective-permute-start(bf16[2,2,160,128]{3,2,1,0:T(8,128)(2,1)S(1)} %get-tuple-element.69), channel_id=1, source_target_pairs={{0,12},{1,13},{2,14},{3,15},{4,8},{5,9},{6,10},{7,11},{8,4},{9,5},... | collective-permute-start | bytes 491528 | tf_op jit(solution)/shard_map/ppermute | solution.py:562
  170.2 0.7 copy-start.4
  170.9 19.7 %collective-permute-start.15 = (bf16[2,2,160,128]{3,2,1,0:T(8,128)(2,1)S(1)}, bf16[2,2,160,128]{3,2,1,0:T(8,128)(2,1)}, u32[]{:S(2)}, u32[]{:S(2)}) collective-permute-start(bf16[2,2,160,128]{3,2,1,0:T(8,128)(2,1)S(1)} %get-tuple-element.70), channel_id=1, source_target_pairs={{0,14},{1,15},{2,12},{3,13},{4,10},{5,11},{6,8},{7,9},{8,6},{9,7},... | collective-permute-start | bytes 491528 | tf_op jit(solution)/shard_map/ppermute | solution.py:562
  180.8 0.7 copy-start.6
  181.5 11.9 %collective-permute-start.8 = (bf16[2,1,160,128]{3,2,1,0:T(8,128)(2,1)}, bf16[2,1,160,128]{3,2,1,0:T(8,128)(2,1)S(1)}, u32[]{:S(2)}, u32[]{:S(2)}) collective-permute-start(bf16[2,1,160,128]{3,2,1,0:T(8,128)(2,1)} %get-tuple-element.63), channel_id=1, source_target_pairs={{0,8},{1,9},{2,10},{3,11},{4,12},{5,13},{6,14},{7,15},{8,0},{9,1},... | collective-permute-start | bytes 245768 | tf_op jit(solution)/shard_map/ppermute | solution.py:562
  181.5 13.4 %collective-permute-start.9 = (bf16[2,1,160,128]{3,2,1,0:T(8,128)(2,1)}, bf16[2,1,160,128]{3,2,1,0:T(8,128)(2,1)S(1)}, u32[]{:S(2)}, u32[]{:S(2)}) collective-permute-start(bf16[2,1,160,128]{3,2,1,0:T(8,128)(2,1)} %get-tuple-element.64), channel_id=1, source_target_pairs={{0,10},{1,11},{2,8},{3,9},{4,14},{5,15},{6,12},{7,13},{8,2},{9,3},... | collective-permute-start | bytes 245768 | tf_op jit(solution)/shard_map/ppermute | solution.py:562
  186.4 11.2 %collective-permute-start.10 = (bf16[2,1,160,128]{3,2,1,0:T(8,128)(2,1)}, bf16[2,1,160,128]{3,2,1,0:T(8,128)(2,1)}, u32[]{:S(2)}, u32[]{:S(2)}) collective-permute-start(bf16[2,1,160,128]{3,2,1,0:T(8,128)(2,1)} %get-tuple-element.65), channel_id=1, source_target_pairs={{0,12},{1,13},{2,14},{3,15},{4,8},{5,9},{6,10},{7,11},{8,4},{9,5},... | collective-permute-start | bytes 245768 | tf_op jit(solution)/shard_map/ppermute | solution.py:562
  186.7 12.3 %collective-permute-start.11 = (bf16[2,1,160,128]{3,2,1,0:T(8,128)(2,1)}, bf16[2,1,160,128]{3,2,1,0:T(8,128)(2,1)}, u32[]{:S(2)}, u32[]{:S(2)}) collective-permute-start(bf16[2,1,160,128]{3,2,1,0:T(8,128)(2,1)} %get-tuple-element.66), channel_id=1, source_target_pairs={{0,14},{1,15},{2,12},{3,13},{4,10},{5,11},{6,8},{7,9},{8,6},{9,7},... | collective-permute-start | bytes 245768 | tf_op jit(solution)/shard_map/ppermute | solution.py:562
  187.8 2.8 %copy-start.5 = (bf16[2,2,160,128]{3,2,1,0:T(8,128)(2,1)S(1)}, bf16[2,2,160,128]{3,2,1,0:T(8,128)(2,1)}, u32[]{:S(2)}) copy-start(bf16[2,2,160,128]{3,2,1,0:T(8,128)(2,1)} %copy-done.4) | copy-start | bytes 491524
  187.8 2.8 %copy-start.7 = (bf16[2,2,160,128]{3,2,1,0:T(8,128)(2,1)S(1)}, bf16[2,2,160,128]{3,2,1,0:T(8,128)(2,1)}, u32[]{:S(2)}) copy-start(bf16[2,2,160,128]{3,2,1,0:T(8,128)(2,1)} %copy-done.6) | copy-start | bytes 491524

commit v21 on v20

--- a/solution.py
+++ b/solution.py
@@ -11,7 +11,7 @@
 BF16 = jnp.bfloat16
 F32 = jnp.float32
 CORES = 2
-PLANES = (0, 2, 1, 3)
+PLANES = (0, 1, 3, 2)
 ANYWHERE = pl.BlockSpec(memory_space=pl.ANY)
 IN_SMEM = pl.BlockSpec(memory_space=pltpu.SMEM)
 IN_HBM = pl.BlockSpec(memory_space=pltpu.HBM)
@@ -432,7 +432,7 @@
     def place(j):
         per = chips // len(PLANES) // each
         q = j // per
-        return j if apart else jnp.where(q == 1, j + per, jnp.where(q == 2, j - per, j))
+        return j if apart else jnp.where(q == 2, j + per, jnp.where(q == 3, j - per, j))
 
     specs = [pl.BlockSpec((each, 1, rows, lats, members), lambda j, m: (place(j), m[0] % CORES, 0, 0, 0))]
     scratch = [pltpu.VMEM((rows * members, count), BF16)]
@@ -500,7 +500,7 @@
                 parts.append(held[place, owner % CORES, r, start : start + depth, :])
             else:
                 plane, rest = divmod(place, half // 2)
-                there = (side + 2 * plane) * (half // 2) + rest
+                there = (2 * side + plane + side * (1 - 2 * plane)) * (half // 2) + rest
                 parts.append(blocks_ref[there, owner % CORES, first + r, start : start + depth, :])
         return jnp.concatenate(parts, axis=0)
 

time: 203 us -> 200 us (0.985)
  waiting for transfers between devices: 101 us -> 93.8 us
  starting transfers between devices: 37.9 us -> 42.8 us
    ppermute x11, starting transfers between devices: 15.1 us -> 20.8 us  [by_permutes(): got.append(lax.ppermute(message, 'wave', moves) if k else message)]
    ppermute x11, waiting for transfers between devices: 25.4 us -> 21.2 us  [by_permutes(): got.append(lax.ppermute(message, 'wave', moves) if k else message)]
    all_to_all x3, waiting for transfers between devices: 39.3 us -> 36.4 us  [between_chips(): lax.all_to_all(blocks, 'wave', split_axis=0, concat_axis=0, axis_index_gr...]
where the time goes in v21:
time: 200 us; the launch traced here: 199 us
  waiting for transfers between devices  93.8 us (47%)
  Pallas kernels  56.7 us (28%)
  starting transfers between devices  42.8 us (21%)
  local copies, waits for them, and re-layouts  5.22 us (3%)
    all_to_all x3, waiting for transfers between devices, between_chips(): lax.all_to_all(blocks, 'wave', split_axis=0, concat_axis=0, axis_index_gr...  36.4 us
    ppermute x3, waiting for transfers between devices, per_device(): others = [lax.ppermute(part, 'pole', [(0, 1), (1, 0)]) for part in forced]  21.5 us
    ppermute x11, waiting for transfers between devices, by_permutes(): got.append(lax.ppermute(message, 'wave', moves) if k else message)  21.2 us
    ppermute x11, starting transfers between devices, by_permutes(): got.append(lax.ppermute(message, 'wave', moves) if k else message)  20.8 us
    pallas_call x3, Pallas kernels, analyse(): call(functools.partial(analyse_kernel, slot, low), 'analyse', 2 * width *...  18.1 us
    pallas_call x3, Pallas kernels, synthesise(): call(functools.partial(synthesise_kernel, slot, low, apart, more, len(par...  16.5 us
    all_to_all x3, starting transfers between devices, between_chips(): lax.all_to_all(blocks, 'wave', split_axis=0, concat_axis=0, axis_index_gr...  16.4 us
    ppermute x4, waiting for transfers between devices, between_cores(): return lax.ppermute(blocks, 'wave', [(d, d ^ 1) for d in range(owners)])  10.4 us
  transfers between devices with their start and end apart: 22, of which 16 were waited for; matrix products, arithmetic and copies ran while one was open for 0% of the time, Pallas kernels for 25%

profile of v21, /device:TPU:8, one launch (start us, length us, event | category | flops | bytes accessed | tf_op | source)
XLA Modules:
  0.0 198.8 jit_solution(7329785879302283786)
XLA Ops:
  0.0 4.1 %weigh.2 = (bf16[8,2,3,160,128]{4,3,2,1,0:T(8,128)(2,1)}, f32[8,128]{1,0:T(8,128)}) custom-call(s32[1]{0:T(128)} %bitcast.me_ref, f32[1,160]{1,0:T(1,128)} %bitcast.3, bf16[3,160,32,128]{3,2,1,0:T(8,128)(2,1)} %tendency_ref.3), custom_call_target="tpu_custom_call" | custom-call | flops 503316480 | bytes 5898240 | tf_op jit(solution)/shard_map/weigh/pallas_call | solution.py:147
  4.1 0.0 copy-start.10
  4.1 6.3 %all-to-all-start = ((bf16[8,2,3,160,128]{4,3,2,1,0:T(8,128)(2,1)}), bf16[8,2,3,160,128]{4,3,2,1,0:T(8,128)(2,1)}, u32[]{:S(2)}, u32[]{:S(2)}) async-start(bf16[8,2,3,160,128]{4,3,2,1,0:T(8,128)(2,1)} %get-tuple-element.44), calls=%async_computation | async-start | bytes 3932160 | tf_op jit(solution)/shard_map/all_to_all | solution.py:569
  10.4 0.1 copy.24.coeff_ref
  10.5 1.8 copy-done.3
  12.3 2.4 %sum_pairs.1.here_ref = f32[18,2,1280]{2,1,0:T(2,128)S(1)} custom-call(f32[32,2]{1,0:T(8,128)S(1)} %copy.24.coeff_ref, f32[8,128]{1,0:T(8,128)S(1)} %copy-done.9, bf16[32,18,2,1280]{3,2,1,0:T(2,128)(2,1)S(1)} %copy-done.3), custom_call_target="tpu_custom_call" | custom-call | flops 5898240 | bytes 2949120 | tf_op jit(solution)/shard_map/sum_pairs/pallas_call | solution.py:343
  14.7 1.6 collective-permute-start
  16.3 4.3 %collective-permute-done.rest_0_.there_ref = f32[18,2,1280]{2,1,0:T(2,128)S(1)} collective-permute-done((f32[18,2,1280]{2,1,0:T(2,128)S(1)}, f32[18,2,1280]{2,1,0:T(2,128)S(1)}, u32[]{:S(2)}, u32[]{:S(2)}) %collective-permute-start) | collective-permute-done | bytes 184352 | tf_op jit(solution)/shard_map/ppermute | solution.py:589
  20.6 0.7 copy-done.1
  21.3 4.2 %weigh.3 = (bf16[8,2,3,160,128]{4,3,2,1,0:T(8,128)(2,1)}, bf16[8,3,160,128]{3,2,1,0:T(8,128)(2,1)}, f32[8,128]{1,0:T(8,128)}) custom-call(s32[1]{0:T(128)} %bitcast.me_ref, f32[1,160]{1,0:T(1,128)} %bitcast.4, bf16[3,160,32,128]{3,2,1,0:T(8,128)(2,1)} %tendency_ref.3, f32[18,2,1280]{2,1,0:T(2,128)} %copy-done.1), custom_call_target="tpu_custom_call" | custom-call | flops 503316480 | bytes 5898240 | tf_op jit(solution)/shard_map/weigh/pallas_call | solution.py:147
  25.4 0.1 collective-permute-start.1
  25.5 2.8 %collective-permute-done.1.mate_ref = bf16[8,3,160,128]{3,2,1,0:T(8,128)(2,1)S(1)} collective-permute-done((bf16[8,3,160,128]{3,2,1,0:T(8,128)(2,1)}, bf16[8,3,160,128]{3,2,1,0:T(8,128)(2,1)S(1)}, u32[]{:S(2)}, u32[]{:S(2)}) %collective-permute-start.1) | collective-permute-done | bytes 983072 | tf_op jit(solution)/shard_map/ppermute | solution.py:555
  28.3 0.9 pair.3
  29.2 25.2 %all-to-all-done.in_ref.rest_0_ = bf16[8,2,3,160,128]{4,3,2,1,0:T(8,128)(2,1)} async-done(((bf16[8,2,3,160,128]{4,3,2,1,0:T(8,128)(2,1)}), bf16[8,2,3,160,128]{4,3,2,1,0:T(8,128)(2,1)}, u32[]{:S(2)}, u32[]{:S(2)}) %all-to-all-start) | async-done | bytes 1966112 | tf_op jit(solution)/shard_map/all_to_all | solution.py:569
  54.4 5.6 %all-to-all-start.2 = ((bf16[8,2,3,160,128]{4,3,2,1,0:T(8,128)(2,1)}), bf16[8,2,3,160,128]{4,3,2,1,0:T(8,128)(2,1)}, u32[]{:S(2)}, u32[]{:S(2)}) async-start(bf16[8,2,3,160,128]{4,3,2,1,0:T(8,128)(2,1)} %get-tuple-element.49), calls=%async_computation.2 | async-start | bytes 3932160 | tf_op jit(solution)/shard_map/all_to_all | solution.py:569
  60.0 1.3 pick.1
  61.3 0.1 collective-permute-start.2
  61.4 2.6 %collective-permute-done.2.rest_1_ = bf16[8,3,160,128]{3,2,1,0:T(8,128)(2,1)S(1)} collective-permute-done((bf16[8,3,160,128]{3,2,1,0:T(8,128)(2,1)S(1)}, bf16[8,3,160,128]{3,2,1,0:T(8,128)(2,1)S(1)}, u32[]{:S(2)}, u32[]{:S(2)}) %collective-permute-start.2) | collective-permute-done | bytes 983072 | tf_op jit(solution)/shard_map/ppermute | solution.py:555
  64.0 5.9 %analyse.3.own_ref = bf16[3,128,640]{2,1,0:T(8,128)(2,1)S(1)} custom-call(s32[1]{0:T(128)} %bitcast.me_ref, s32[2]{0:T(128)S(1)} %copy-done.8, f32[8,128]{1,0:T(8,128)S(1)} %get-tuple-element.43.token_ref, bf16[2,1280,2560]{2,1,0:T(8,128)(2,1)} %table_ref.11, bf16[3,2,128,1280]{3,2,1,0:T(8,128)(2,1)} %state_ref.5, ...), custom_call_target="tpu_custom_call" | custom-call | flops 1258291200 | bytes 3276800 | tf_op jit(solution)/shard_map/analyse/pallas_call | solution.py:301
  69.8 1.6 collective-permute-start.3
  71.4 11.8 %collective-permute-done.3.other_ref = bf16[3,128,640]{2,1,0:T(8,128)(2,1)S(1)} collective-permute-done((bf16[3,128,640]{2,1,0:T(8,128)(2,1)S(1)}, bf16[3,128,640]{2,1,0:T(8,128)(2,1)S(1)}, u32[]{:S(2)}, u32[]{:S(2)}) %collective-permute-start.3) | collective-permute-done | bytes 491552 | tf_op jit(solution)/shard_map/ppermute | solution.py:603
  83.2 5.0 %synthesise.3 = (bf16[8,2,3,160,128]{4,3,2,1,0:T(8,128)(2,1)S(1)}, bf16[8,3,160,128]{3,2,1,0:T(8,128)(2,1)S(1)}) custom-call(s32[1]{0:T(128)} %bitcast.me_ref, f32[1]{0:T(128)} %bitcast.1.sign_ref, f32[18,2,1280]{2,1,0:T(2,128)S(1)} %sum_pairs.1.here_ref, f32[18,2,1280]{2,1,0:T(2,128)S(1)} %copy-done.2, bf16[3,128,640]{2,1,0:T(8,128)(2,1)S(1)} %analyse.3.own_ref, ...), custom_call_target="tpu_custom_call" | custom-call | flops 1258291200 | bytes 3276800 | tf_op jit(solution)/shard_map/synthesise/pallas_call | solution.py:449
  88.2 0.1 collective-permute-start.4
  88.2 2.6 %collective-permute-done.4.mate_ref = bf16[8,3,160,128]{3,2,1,0:T(8,128)(2,1)S(1)} collective-permute-done((bf16[8,3,160,128]{3,2,1,0:T(8,128)(2,1)S(1)}, bf16[8,3,160,128]{3,2,1,0:T(8,128)(2,1)S(1)}, u32[]{:S(2)}, u32[]{:S(2)}) %collective-permute-start.4) | collective-permute-done | bytes 983072 | tf_op jit(solution)/shard_map/ppermute | solution.py:555
  90.8 0.1 pair.4
  90.9 0.0 copy-start
  90.9 1.3 copy-done
  92.2 11.1 %all-to-all-done.2.rest_0_ = bf16[8,2,3,160,128]{4,3,2,1,0:T(8,128)(2,1)} async-done(((bf16[8,2,3,160,128]{4,3,2,1,0:T(8,128)(2,1)}), bf16[8,2,3,160,128]{4,3,2,1,0:T(8,128)(2,1)}, u32[]{:S(2)}, u32[]{:S(2)}) %all-to-all-start.2) | async-done | bytes 1966112 | tf_op jit(solution)/shard_map/all_to_all | solution.py:569
  103.3 4.5 %all-to-all-start.1 = ((bf16[8,2,3,160,128]{4,3,2,1,0:T(8,128)(2,1)}), bf16[8,2,3,160,128]{4,3,2,1,0:T(8,128)(2,1)S(1)}, u32[]{:S(2)}, u32[]{:S(2)}) async-start(bf16[8,2,3,160,128]{4,3,2,1,0:T(8,128)(2,1)} %copy-done), calls=%async_computation.1 | async-start | bytes 3932160 | tf_op jit(solution)/shard_map/all_to_all | solution.py:569
  107.8 6.1 %analyse.5.own_ref = bf16[3,128,640]{2,1,0:T(8,128)(2,1)S(1)} custom-call(s32[1]{0:T(128)} %bitcast.me_ref, s32[2]{0:T(128)S(1)} %copy-done.8, f32[8,128]{1,0:T(8,128)S(1)} %get-tuple-element.48.token_ref, bf16[2,1280,2560]{2,1,0:T(8,128)(2,1)} %table_ref.11, bf16[3,2,128,1280]{3,2,1,0:T(8,128)(2,1)} %state_ref.5, ...), custom_call_target="tpu_custom_call" | custom-call | flops 1258291200 | bytes 3276800 | tf_op jit(solution)/shard_map/analyse/pallas_call | solution.py:301
  114.0 1.6 collective-permute-start.6
  115.6 6.1 %analyse.4.own_ref = bf16[3,128,640]{2,1,0:T(8,128)(2,1)S(1)} custom-call(s32[1]{0:T(128)} %bitcast.me_ref, s32[2]{0:T(128)S(1)} %copy-done.8, f32[8,128]{1,0:T(8,128)S(1)} %get-tuple-element.48.token_ref, bf16[2,1280,2560]{2,1,0:T(8,128)(2,1)} %table_ref.11, bf16[3,2,128,1280]{3,2,1,0:T(8,128)(2,1)} %state_ref.5, ...), custom_call_target="tpu_custom_call" | custom-call | flops 1258291200 | bytes 3276800 | tf_op jit(solution)/shard_map/analyse/pallas_call | solution.py:301
  121.7 0.6 collective-permute-start.5
  122.3 5.9 %collective-permute-done.6.other_ref = bf16[3,128,640]{2,1,0:T(8,128)(2,1)S(1)} collective-permute-done((bf16[3,128,640]{2,1,0:T(8,128)(2,1)S(1)}, bf16[3,128,640]{2,1,0:T(8,128)(2,1)S(1)}, u32[]{:S(2)}, u32[]{:S(2)}) %collective-permute-start.6) | collective-permute-done | bytes 491552 | tf_op jit(solution)/shard_map/ppermute | solution.py:603
  128.2 4.8 %synthesise.4.rest_0_ = f32[384,2560]{1,0:T(8,128)S(1)} custom-call(s32[1]{0:T(128)} %bitcast.me_ref, f32[1]{0:T(128)} %bitcast.1.sign_ref, f32[18,2,1280]{2,1,0:T(2,128)S(1)} %sum_pairs.1.here_ref, f32[18,2,1280]{2,1,0:T(2,128)S(1)} %copy-done.2, bf16[3,128,640]{2,1,0:T(8,128)(2,1)S(1)} %analyse.5.own_ref, ...), custom_call_target="tpu_custom_call" | custom-call | flops 1258291200 | bytes 3276800 | tf_op jit(solution)/shard_map/synthesise/pallas_call | solution.py:449
  133.0 3.8 %collective-permute-done.5.other_ref = bf16[3,128,640]{2,1,0:T(8,128)(2,1)S(1)} collective-permute-done((bf16[3,128,640]{2,1,0:T(8,128)(2,1)S(1)}, bf16[3,128,640]{2,1,0:T(8,128)(2,1)S(1)}, u32[]{:S(2)}, u32[]{:S(2)}) %collective-permute-start.5) | collective-permute-done | bytes 491552 | tf_op jit(solution)/shard_map/ppermute | solution.py:603
  136.8 6.7 %synthesise.5 = (bf16[2,3,160,128]{3,2,1,0:T(8,128)(2,1)S(1)}, bf16[2,2,160,128]{3,2,1,0:T(8,128)(2,1)S(1)}, bf16[2,2,160,128]{3,2,1,0:T(8,128)(2,1)S(1)}, bf16[...) custom-call(s32[1]{0:T(128)} %bitcast.me_ref, ...), custom_call_target="tpu_custom_call" | custom-call | flops 1258291200 | bytes 3276800 | tf_op jit(solution)/shard_map/synthesise/pallas_call | solution.py:449
  143.6 0.1 collective-permute-start.7
  143.6 2.6 %collective-permute-done.7.mate_ref = bf16[8,3,160,128]{3,2,1,0:T(8,128)(2,1)S(1)} collective-permute-done((bf16[8,3,160,128]{3,2,1,0:T(8,128)(2,1)S(1)}, bf16[8,3,160,128]{3,2,1,0:T(8,128)(2,1)S(1)}, u32[]{:S(2)}, u32[]{:S(2)}) %collective-permute-start.7) | collective-permute-done | bytes 983072 | tf_op jit(solution)/shard_map/ppermute | solution.py:555
  146.2 1.3 pair.5
  147.5 1.8 collective-permute-start.12
  149.3 2.1 %collective-permute-start.13 = (bf16[2,2,160,128]{3,2,1,0:T(8,128)(2,1)S(1)}, bf16[2,2,160,128]{3,2,1,0:T(8,128)(2,1)S(1)}, u32[]{:S(2)}, u32[]{:S(2)}) collective-permute-start(bf16[2,2,160,128]{3,2,1,0:T(8,128)(2,1)S(1)} %get-tuple-element.68), channel_id=1, source_target_pairs={{0,10},{1,11},{2,8},{3,9},{4,14},{5,15},{6,12},{7,13},{8,2},{9,3},... | collective-permute-start | bytes 491528 | tf_op jit(solution)/shard_map/ppermute | solution.py:562
  151.4 0.6 collective-permute-start.16
  152.0 0.3 collective-permute-start.17
  152.2 2.7 %collective-permute-start.18 = (bf16[2,3,160,128]{3,2,1,0:T(8,128)(2,1)S(1)}, bf16[2,3,160,128]{3,2,1,0:T(8,128)(2,1)S(1)}, u32[]{:S(2)}, u32[]{:S(2)}) collective-permute-start(bf16[2,3,160,128]{3,2,1,0:T(8,128)(2,1)S(1)} %get-tuple-element.74), channel_id=1, source_target_pairs={{0,6},{1,7},{2,4},{3,5},{4,2},{5,3},{6,0},{7,1},{8,14},{9,15},{10,... | collective-permute-start | bytes 737288 | tf_op jit(solution)/shard_map/ppermute | solution.py:562
  154.9 5.3 %collective-permute-done.12.rest_0_ = bf16[2,2,160,128]{3,2,1,0:T(8,128)(2,1)S(1)} collective-permute-done((bf16[2,2,160,128]{3,2,1,0:T(8,128)(2,1)S(1)}, bf16[2,2,160,128]{3,2,1,0:T(8,128)(2,1)S(1)}, u32[]{:S(2)}, u32[]{:S(2)}) %collective-permute-start.12) | collective-permute-done | bytes 163872 | tf_op jit(solution)/shard_map/ppermute | solution.py:562
  160.2 2.6 %collective-permute-start.14 = (bf16[2,2,160,128]{3,2,1,0:T(8,128)(2,1)S(1)}, bf16[2,2,160,128]{3,2,1,0:T(8,128)(2,1)S(1)}, u32[]{:S(2)}, u32[]{:S(2)}) collective-permute-start(bf16[2,2,160,128]{3,2,1,0:T(8,128)(2,1)S(1)} %get-tuple-element.69), channel_id=1, source_target_pairs={{0,12},{1,13},{2,14},{3,15},{4,8},{5,9},{6,10},{7,11},{8,4},{9,5},... | collective-permute-start | bytes 491528 | tf_op jit(solution)/shard_map/ppermute | solution.py:562
  162.8 0.9 collective-permute-done.13.rest_1_
  163.7 0.7 copy-done.4
  164.4 4.9 %collective-permute-start.15 = (bf16[2,2,160,128]{3,2,1,0:T(8,128)(2,1)S(1)}, bf16[2,2,160,128]{3,2,1,0:T(8,128)(2,1)}, u32[]{:S(2)}, u32[]{:S(2)}) collective-permute-start(bf16[2,2,160,128]{3,2,1,0:T(8,128)(2,1)S(1)} %get-tuple-element.70), channel_id=1, source_target_pairs={{0,14},{1,15},{2,12},{3,13},{4,10},{5,11},{6,8},{7,9},{8,6},{9,7},... | collective-permute-start | bytes 491528 | tf_op jit(solution)/shard_map/ppermute | solution.py:562
  169.3 8.8 %collective-permute-done.14.rest_2_ = bf16[2,2,160,128]{3,2,1,0:T(8,128)(2,1)S(1)} collective-permute-done((bf16[2,2,160,128]{3,2,1,0:T(8,128)(2,1)S(1)}, bf16[2,2,160,128]{3,2,1,0:T(8,128)(2,1)S(1)}, u32[]{:S(2)}, u32[]{:S(2)}) %collective-permute-start.14) | collective-permute-done | bytes 163872 | tf_op jit(solution)/shard_map/ppermute | solution.py:562
  178.2 0.7 copy-done.6
  178.8 0.0 collective-permute-start.8
  178.8 4.5 %collective-permute-start.9 = (bf16[2,1,160,128]{3,2,1,0:T(8,128)(2,1)}, bf16[2,1,160,128]{3,2,1,0:T(8,128)(2,1)S(1)}, u32[]{:S(2)}, u32[]{:S(2)}) collective-permute-start(bf16[2,1,160,128]{3,2,1,0:T(8,128)(2,1)} %get-tuple-element.64), channel_id=1, source_target_pairs={{0,10},{1,11},{2,8},{3,9},{4,14},{5,15},{6,12},{7,13},{8,2},{9,3},... | collective-permute-start | bytes 245768 | tf_op jit(solution)/shard_map/ppermute | solution.py:562
  183.4 0.0 collective-permute-done.18.rest_3_
  183.4 1.3 collective-permute-start.11
  184.7 0.0 all-to-all-done.1.blocks_ref
  184.7 2.7 %assemble.3.rest_4_ = bf16[3,160,32,128]{3,2,1,0:T(8,128)(2,1)} custom-call(s32[1]{0:T(128)} %bitcast.me_ref, bf16[8,2,3,160,128]{4,3,2,1,0:T(8,128)(2,1)S(1)} %all-to-all-done.1.blocks_ref, bf16[2,3,160,128]{3,2,1,0:T(8,128)(2,1)S(1)} %get-tuple-element.71.rest_0_, bf16[2,3,160,128]{3,2,1,0:T(8,128)(2,1)S(1)} %collective-permute-done.16.rest_1_, ...), custom_call_target="tpu_custom_call" | custom-call | flops 503316480 | bytes 3932160 | tf_op jit(solution)/shard_map/assemble/pallas_call | solution.py:536
  187.5 2.1 %collective-permute-done.15.rest_3_ = bf16[2,2,160,128]{3,2,1,0:T(8,128)(2,1)} collective-permute-done((bf16[2,2,160,128]{3,2,1,0:T(8,128)(2,1)S(1)}, bf16[2,2,160,128]{3,2,1,0:T(8,128)(2,1)}, u32[]{:S(2)}, u32[]{:S(2)}) %collective-permute-start.15) | collective-permute-done | bytes 163872 | tf_op jit(solution)/shard_map/ppermute | solution.py:562
  189.5 2.7 %assemble.4.rest_4_ = bf16[3,160,32,128]{3,2,1,0:T(8,128)(2,1)} custom-call(s32[1]{0:T(128)} %bitcast.me_ref, bf16[8,2,3,160,128]{4,3,2,1,0:T(8,128)(2,1)S(1)} %all-to-all-done.1.blocks_ref, bf16[2,2,160,128]{3,2,1,0:T(8,128)(2,1)S(1)} %collective-permute-done.12.rest_0_, bf16[2,2,160,128]{3,2,1,0:T(8,128)(2,1)S(1)} %copy-done.5, ...), custom_call_target="tpu_custom_call", output_to_operand_aliasing={{}: (6, {})} | custom-call | flops 335544320 | bytes 2621440 | tf_op jit(solution)/shard_map/assemble/pallas_call | solution.py:536
  192.2 0.0 collective-permute-done.9.rest_1_
  192.2 0.8 collective-permute-done.10.rest_2_
  193.0 3.3 %collective-permute-done.11.rest_3_ = bf16[2,1,160,128]{3,2,1,0:T(8,128)(2,1)} collective-permute-done((bf16[2,1,160,128]{3,2,1,0:T(8,128)(2,1)}, bf16[2,1,160,128]{3,2,1,0:T(8,128)(2,1)}, u32[]{:S(2)}, u32[]{:S(2)}) %collective-permute-start.11) | collective-permute-done | bytes 81952 | tf_op jit(solution)/shard_map/ppermute | solution.py:562
  196.4 2.3 %assemble.5 = bf16[3,160,32,128]{3,2,1,0:T(8,128)(2,1)} custom-call(s32[1]{0:T(128)} %bitcast.me_ref, bf16[8,2,3,160,128]{4,3,2,1,0:T(8,128)(2,1)S(1)} %all-to-all-done.1.blocks_ref, bf16[2,1,160,128]{3,2,1,0:T(8,128)(2,1)S(1)} %collective-permute-done.8.rest_0_, ...), custom_call_target="tpu_custom_call", output_to_operand_aliasing={{}: (6, {})} | custom-call | flops 167772160 | bytes 1310720 | tf_op jit(solution)/shard_map/assemble/pallas_call | solution.py:536
  (19 shorter events, 0.0 us)
Async XLA Ops:
  4.1 6.3 %copy-start.10 = (f32[32,2]{0,1:T(2,128)S(1)}, f32[32,2]{0,1:T(2,128)}, u32[]{:S(2)}) copy-start(f32[32,2]{0,1:T(2,128)} %param.12) | copy-start | bytes 772
  4.1 6.4 %copy-start.9 = (f32[8,128]{1,0:T(8,128)S(1)}, f32[8,128]{1,0:T(8,128)}, u32[]{:S(2)}) copy-start(f32[8,128]{1,0:T(8,128)} %get-tuple-element.40.token_ref) | copy-start | bytes 12292
  4.1 50.3 %all-to-all-start = ((bf16[8,2,3,160,128]{4,3,2,1,0:T(8,128)(2,1)}), bf16[8,2,3,160,128]{4,3,2,1,0:T(8,128)(2,1)}, u32[]{:S(2)}, u32[]{:S(2)}) async-start(bf16[8,2,3,160,128]{4,3,2,1,0:T(8,128)(2,1)} %get-tuple-element.44), calls=%async_computation | async-start | bytes 3932160 | tf_op jit(solution)/shard_map/all_to_all | solution.py:569
  10.5 1.8 copy-start.3
  14.7 5.9 %collective-permute-start = (f32[18,2,1280]{2,1,0:T(2,128)S(1)}, f32[18,2,1280]{2,1,0:T(2,128)S(1)}, u32[]{:S(2)}, u32[]{:S(2)}) collective-permute-start(f32[18,2,1280]{2,1,0:T(2,128)S(1)} %sum_pairs.1.here_ref), channel_id=1, source_target_pairs={{0,16},{16,0},{1,17},{17,1},{2,18},{18,2},{3,19},{19,3},{4,20},{20... | collective-permute-start | bytes 552968 | tf_op jit(solution)/shard_map/ppermute | solution.py:589
  20.6 0.7 copy-start.1
  25.4 2.8 %collective-permute-start.1 = (bf16[8,3,160,128]{3,2,1,0:T(8,128)(2,1)}, bf16[8,3,160,128]{3,2,1,0:T(8,128)(2,1)S(1)}, u32[]{:S(2)}, u32[]{:S(2)}) collective-permute-start(bf16[8,3,160,128]{3,2,1,0:T(8,128)(2,1)} %get-tuple-element.41), channel_id=1, source_target_pairs={{0,1},{1,0},{2,3},{3,2},{4,5},{5,4},{6,7},{7,6},{8,9},{9,8},{10,11... | collective-permute-start | bytes 2949128 | tf_op jit(solution)/shard_map/ppermute | solution.py:555
  54.4 48.9 %all-to-all-start.2 = ((bf16[8,2,3,160,128]{4,3,2,1,0:T(8,128)(2,1)}), bf16[8,2,3,160,128]{4,3,2,1,0:T(8,128)(2,1)}, u32[]{:S(2)}, u32[]{:S(2)}) async-start(bf16[8,2,3,160,128]{4,3,2,1,0:T(8,128)(2,1)} %get-tuple-element.49), calls=%async_computation.2 | async-start | bytes 3932160 | tf_op jit(solution)/shard_map/all_to_all | solution.py:569
  60.0 3.9 %copy-start.8 = (s32[2]{0:T(128)S(1)}, s32[2]{0:T(128)}, u32[]{:S(2)}) copy-start(s32[2]{0:T(128)} %wave_ref.5) | copy-start | bytes 28
  61.3 21.9 %copy-start.2 = (f32[18,2,1280]{2,1,0:T(2,128)S(1)}, f32[18,2,1280]{2,1,0:T(2,128)}, u32[]{:S(2)}) copy-start(f32[18,2,1280]{2,1,0:T(2,128)} %copy-done.1) | copy-start | bytes 552964
  61.3 2.6 %collective-permute-start.2 = (bf16[8,3,160,128]{3,2,1,0:T(8,128)(2,1)S(1)}, bf16[8,3,160,128]{3,2,1,0:T(8,128)(2,1)S(1)}, u32[]{:S(2)}, u32[]{:S(2)}) collective-permute-start(bf16[8,3,160,128]{3,2,1,0:T(8,128)(2,1)S(1)} %pick.1), channel_id=1, source_target_pairs={{0,1},{1,0},{2,3},{3,2},{4,5},{5,4},{6,7},{7,6},{8,9},{9,8},{10,11... | collective-permute-start | bytes 2949128 | tf_op jit(solution)/shard_map/ppermute | solution.py:555
  69.8 13.3 %collective-permute-start.3 = (bf16[3,128,640]{2,1,0:T(8,128)(2,1)S(1)}, bf16[3,128,640]{2,1,0:T(8,128)(2,1)S(1)}, u32[]{:S(2)}, u32[]{:S(2)}) collective-permute-start(bf16[3,128,640]{2,1,0:T(8,128)(2,1)S(1)} %analyse.3.own_ref), channel_id=1, source_target_pairs={{0,16},{16,0},{1,17},{17,1},{2,18},{18,2},{3,19},{19,3},{4,20},{20... | collective-permute-start | bytes 1474568 | tf_op jit(solution)/shard_map/ppermute | solution.py:603
  88.2 2.6 %collective-permute-start.4 = (bf16[8,3,160,128]{3,2,1,0:T(8,128)(2,1)S(1)}, bf16[8,3,160,128]{3,2,1,0:T(8,128)(2,1)S(1)}, u32[]{:S(2)}, u32[]{:S(2)}) collective-permute-start(bf16[8,3,160,128]{3,2,1,0:T(8,128)(2,1)S(1)} %get-tuple-element.45), channel_id=1, source_target_pairs={{0,1},{1,0},{2,3},{3,2},{4,5},{5,4},{6,7},{7,6},{8,9},{9,8},{10,11... | collective-permute-start | bytes 2949128 | tf_op jit(solution)/shard_map/ppermute | solution.py:555
  90.9 1.3 copy-start
  103.3 81.4 %all-to-all-start.1 = ((bf16[8,2,3,160,128]{4,3,2,1,0:T(8,128)(2,1)}), bf16[8,2,3,160,128]{4,3,2,1,0:T(8,128)(2,1)S(1)}, u32[]{:S(2)}, u32[]{:S(2)}) async-start(bf16[8,2,3,160,128]{4,3,2,1,0:T(8,128)(2,1)} %copy-done), calls=%async_computation.1 | async-start | bytes 3932160 | tf_op jit(solution)/shard_map/all_to_all | solution.py:569
  114.0 14.2 %collective-permute-start.6 = (bf16[3,128,640]{2,1,0:T(8,128)(2,1)S(1)}, bf16[3,128,640]{2,1,0:T(8,128)(2,1)S(1)}, u32[]{:S(2)}, u32[]{:S(2)}) collective-permute-start(bf16[3,128,640]{2,1,0:T(8,128)(2,1)S(1)} %analyse.5.own_ref), channel_id=1, source_target_pairs={{0,16},{16,0},{1,17},{17,1},{2,18},{18,2},{3,19},{19,3},{4,20},{20... | collective-permute-start | bytes 1474568 | tf_op jit(solution)/shard_map/ppermute | solution.py:603
  121.7 15.1 %collective-permute-start.5 = (bf16[3,128,640]{2,1,0:T(8,128)(2,1)S(1)}, bf16[3,128,640]{2,1,0:T(8,128)(2,1)S(1)}, u32[]{:S(2)}, u32[]{:S(2)}) collective-permute-start(bf16[3,128,640]{2,1,0:T(8,128)(2,1)S(1)} %analyse.4.own_ref), channel_id=1, source_target_pairs={{0,16},{16,0},{1,17},{17,1},{2,18},{18,2},{3,19},{19,3},{4,20},{20... | collective-permute-start | bytes 1474568 | tf_op jit(solution)/shard_map/ppermute | solution.py:603
  143.6 2.6 %collective-permute-start.7 = (bf16[8,3,160,128]{3,2,1,0:T(8,128)(2,1)S(1)}, bf16[8,3,160,128]{3,2,1,0:T(8,128)(2,1)S(1)}, u32[]{:S(2)}, u32[]{:S(2)}) collective-permute-start(bf16[8,3,160,128]{3,2,1,0:T(8,128)(2,1)S(1)} %get-tuple-element.50), channel_id=1, source_target_pairs={{0,1},{1,0},{2,3},{3,2},{4,5},{5,4},{6,7},{7,6},{8,9},{9,8},{10,11... | collective-permute-start | bytes 2949128 | tf_op jit(solution)/shard_map/ppermute | solution.py:555
  147.5 12.7 %collective-permute-start.12 = (bf16[2,2,160,128]{3,2,1,0:T(8,128)(2,1)S(1)}, bf16[2,2,160,128]{3,2,1,0:T(8,128)(2,1)S(1)}, u32[]{:S(2)}, u32[]{:S(2)}) collective-permute-start(bf16[2,2,160,128]{3,2,1,0:T(8,128)(2,1)S(1)} %get-tuple-element.67), channel_id=1, source_target_pairs={{0,8},{1,9},{2,10},{3,11},{4,12},{5,13},{6,14},{7,15},{8,0},{9,1},... | collective-permute-start | bytes 491528 | tf_op jit(solution)/shard_map/ppermute | solution.py:562
  149.3 14.4 %collective-permute-start.13 = (bf16[2,2,160,128]{3,2,1,0:T(8,128)(2,1)S(1)}, bf16[2,2,160,128]{3,2,1,0:T(8,128)(2,1)S(1)}, u32[]{:S(2)}, u32[]{:S(2)}) collective-permute-start(bf16[2,2,160,128]{3,2,1,0:T(8,128)(2,1)S(1)} %get-tuple-element.68), channel_id=1, source_target_pairs={{0,10},{1,11},{2,8},{3,9},{4,14},{5,15},{6,12},{7,13},{8,2},{9,3},... | collective-permute-start | bytes 491528 | tf_op jit(solution)/shard_map/ppermute | solution.py:562
  151.4 27.4 %collective-permute-start.16 = (bf16[2,3,160,128]{3,2,1,0:T(8,128)(2,1)S(1)}, bf16[2,3,160,128]{3,2,1,0:T(8,128)(2,1)S(1)}, u32[]{:S(2)}, u32[]{:S(2)}) collective-permute-start(bf16[2,3,160,128]{3,2,1,0:T(8,128)(2,1)S(1)} %get-tuple-element.72), channel_id=1, source_target_pairs={{0,2},{1,3},{2,0},{3,1},{4,6},{5,7},{6,4},{7,5},{8,10},{9,11},{10,... | collective-permute-start | bytes 737288 | tf_op jit(solution)/shard_map/ppermute | solution.py:562
  152.0 31.4 %collective-permute-start.17 = (bf16[2,3,160,128]{3,2,1,0:T(8,128)(2,1)S(1)}, bf16[2,3,160,128]{3,2,1,0:T(8,128)(2,1)S(1)}, u32[]{:S(2)}, u32[]{:S(2)}) collective-permute-start(bf16[2,3,160,128]{3,2,1,0:T(8,128)(2,1)S(1)} %get-tuple-element.73), channel_id=1, source_target_pairs={{0,4},{1,5},{2,6},{3,7},{4,0},{5,1},{6,2},{7,3},{8,12},{9,13},{10,... | collective-permute-start | bytes 737288 | tf_op jit(solution)/shard_map/ppermute | solution.py:562
  152.2 31.1 %collective-permute-start.18 = (bf16[2,3,160,128]{3,2,1,0:T(8,128)(2,1)S(1)}, bf16[2,3,160,128]{3,2,1,0:T(8,128)(2,1)S(1)}, u32[]{:S(2)}, u32[]{:S(2)}) collective-permute-start(bf16[2,3,160,128]{3,2,1,0:T(8,128)(2,1)S(1)} %get-tuple-element.74), channel_id=1, source_target_pairs={{0,6},{1,7},{2,4},{3,5},{4,2},{5,3},{6,0},{7,1},{8,14},{9,15},{10,... | collective-permute-start | bytes 737288 | tf_op jit(solution)/shard_map/ppermute | solution.py:562
  160.2 18.0 %collective-permute-start.14 = (bf16[2,2,160,128]{3,2,1,0:T(8,128)(2,1)S(1)}, bf16[2,2,160,128]{3,2,1,0:T(8,128)(2,1)S(1)}, u32[]{:S(2)}, u32[]{:S(2)}) collective-permute-start(bf16[2,2,160,128]{3,2,1,0:T(8,128)(2,1)S(1)} %get-tuple-element.69), channel_id=1, source_target_pairs={{0,12},{1,13},{2,14},{3,15},{4,8},{5,9},{6,10},{7,11},{8,4},{9,5},... | collective-permute-start | bytes 491528 | tf_op jit(solution)/shard_map/ppermute | solution.py:562
  163.7 0.7 copy-start.4
  164.4 25.1 %collective-permute-start.15 = (bf16[2,2,160,128]{3,2,1,0:T(8,128)(2,1)S(1)}, bf16[2,2,160,128]{3,2,1,0:T(8,128)(2,1)}, u32[]{:S(2)}, u32[]{:S(2)}) collective-permute-start(bf16[2,2,160,128]{3,2,1,0:T(8,128)(2,1)S(1)} %get-tuple-element.70), channel_id=1, source_target_pairs={{0,14},{1,15},{2,12},{3,13},{4,10},{5,11},{6,8},{7,9},{8,6},{9,7},... | collective-permute-start | bytes 491528 | tf_op jit(solution)/shard_map/ppermute | solution.py:562
  178.2 0.7 copy-start.6
  178.8 13.4 %collective-permute-start.8 = (bf16[2,1,160,128]{3,2,1,0:T(8,128)(2,1)}, bf16[2,1,160,128]{3,2,1,0:T(8,128)(2,1)S(1)}, u32[]{:S(2)}, u32[]{:S(2)}) collective-permute-start(bf16[2,1,160,128]{3,2,1,0:T(8,128)(2,1)} %get-tuple-element.63), channel_id=1, source_target_pairs={{0,8},{1,9},{2,10},{3,11},{4,12},{5,13},{6,14},{7,15},{8,0},{9,1},... | collective-permute-start | bytes 245768 | tf_op jit(solution)/shard_map/ppermute | solution.py:562
  178.8 13.4 %collective-permute-start.9 = (bf16[2,1,160,128]{3,2,1,0:T(8,128)(2,1)}, bf16[2,1,160,128]{3,2,1,0:T(8,128)(2,1)S(1)}, u32[]{:S(2)}, u32[]{:S(2)}) collective-permute-start(bf16[2,1,160,128]{3,2,1,0:T(8,128)(2,1)} %get-tuple-element.64), channel_id=1, source_target_pairs={{0,10},{1,11},{2,8},{3,9},{4,14},{5,15},{6,12},{7,13},{8,2},{9,3},... | collective-permute-start | bytes 245768 | tf_op jit(solution)/shard_map/ppermute | solution.py:562
  183.3 9.7 %collective-permute-start.10 = (bf16[2,1,160,128]{3,2,1,0:T(8,128)(2,1)}, bf16[2,1,160,128]{3,2,1,0:T(8,128)(2,1)}, u32[]{:S(2)}, u32[]{:S(2)}) collective-permute-start(bf16[2,1,160,128]{3,2,1,0:T(8,128)(2,1)} %get-tuple-element.65), channel_id=1, source_target_pairs={{0,12},{1,13},{2,14},{3,15},{4,8},{5,9},{6,10},{7,11},{8,4},{9,5},... | collective-permute-start | bytes 245768 | tf_op jit(solution)/shard_map/ppermute | solution.py:562
  183.4 13.0 %collective-permute-start.11 = (bf16[2,1,160,128]{3,2,1,0:T(8,128)(2,1)}, bf16[2,1,160,128]{3,2,1,0:T(8,128)(2,1)}, u32[]{:S(2)}, u32[]{:S(2)}) collective-permute-start(bf16[2,1,160,128]{3,2,1,0:T(8,128)(2,1)} %get-tuple-element.66), channel_id=1, source_target_pairs={{0,14},{1,15},{2,12},{3,13},{4,10},{5,11},{6,8},{7,9},{8,6},{9,7},... | collective-permute-start | bytes 245768 | tf_op jit(solution)/shard_map/ppermute | solution.py:562
  184.7 4.8 %copy-start.5 = (bf16[2,2,160,128]{3,2,1,0:T(8,128)(2,1)S(1)}, bf16[2,2,160,128]{3,2,1,0:T(8,128)(2,1)}, u32[]{:S(2)}) copy-start(bf16[2,2,160,128]{3,2,1,0:T(8,128)(2,1)} %copy-done.4) | copy-start | bytes 491524
  184.7 4.8 %copy-start.7 = (bf16[2,2,160,128]{3,2,1,0:T(8,128)(2,1)S(1)}, bf16[2,2,160,128]{3,2,1,0:T(8,128)(2,1)}, u32[]{:S(2)}) copy-start(bf16[2,2,160,128]{3,2,1,0:T(8,128)(2,1)} %copy-done.6) | copy-start | bytes 491524

commit v22 on v21

--- a/solution.py
+++ b/solution.py
@@ -46,7 +46,7 @@
 
 
 def messages_of(chips, rows):
-    near, far = range(1, chips // 2), range(chips // 2, chips)
+    near, far = range(1, chips // 2), range(chips - 1, chips // 2 - 1, -1)
     first = [(k, 0, rows - 1) for k in far]
     return [(0, 0, rows)] + first + [(k, rows - 1, 1) for k in far] + [(k, 0, rows) for k in near]
 

time: 200 us -> 201 us (level)
  the two profiles are of different devices: /device:TPU:8 before, /device:TPU:0 now
where the time goes in v22:
time: 201 us; the launch traced here: 200 us
  waiting for transfers between devices  87.1 us (43%)
  Pallas kernels  56.7 us (28%)
  starting transfers between devices  50.9 us (25%)
  local copies, waits for them, and re-layouts  5.22 us (3%)
    all_to_all x3, waiting for transfers between devices, between_chips(): lax.all_to_all(blocks, 'wave', split_axis=0, concat_axis=0, axis_index_gr...  34.1 us
    ppermute x11, starting transfers between devices, by_permutes(): got.append(lax.ppermute(message, 'wave', moves) if k else message)  25.9 us
    ppermute x3, waiting for transfers between devices, per_device(): others = [lax.ppermute(part, 'pole', [(0, 1), (1, 0)]) for part in forced]  21.7 us
    all_to_all x3, starting transfers between devices, between_chips(): lax.all_to_all(blocks, 'wave', split_axis=0, concat_axis=0, axis_index_gr...  19.4 us
    pallas_call x3, Pallas kernels, analyse(): call(functools.partial(analyse_kernel, slot, low), 'analyse', 2 * width *...  18.2 us
    pallas_call x3, Pallas kernels, synthesise(): call(functools.partial(synthesise_kernel, slot, low, apart, more, len(par...  16.5 us
    ppermute x11, waiting for transfers between devices, by_permutes(): got.append(lax.ppermute(message, 'wave', moves) if k else message)  16.3 us
    ppermute x4, waiting for transfers between devices, between_cores(): return lax.ppermute(blocks, 'wave', [(d, d ^ 1) for d in range(owners)])  10.4 us
  transfers between devices with their start and end apart: 22, of which 13 were waited for; matrix products, arithmetic and copies ran while one was open for 0% of the time, Pallas kernels for 25%

profile of v22, /device:TPU:0, one launch (start us, length us, event | category | flops | bytes accessed | tf_op | source)
XLA Modules:
  0.0 200.4 jit_solution(5659837791426390609)
XLA Ops:
  0.0 4.1 %weigh.2 = (bf16[8,2,3,160,128]{4,3,2,1,0:T(8,128)(2,1)}, f32[8,128]{1,0:T(8,128)}) custom-call(s32[1]{0:T(128)} %bitcast.me_ref, f32[1,160]{1,0:T(1,128)} %bitcast.3, bf16[3,160,32,128]{3,2,1,0:T(8,128)(2,1)} %tendency_ref.3), custom_call_target="tpu_custom_call" | custom-call | flops 503316480 | bytes 5898240 | tf_op jit(solution)/shard_map/weigh/pallas_call | solution.py:147
  4.1 0.0 copy-start.10
  4.1 7.3 %all-to-all-start = ((bf16[8,2,3,160,128]{4,3,2,1,0:T(8,128)(2,1)}), bf16[8,2,3,160,128]{4,3,2,1,0:T(8,128)(2,1)}, u32[]{:S(2)}, u32[]{:S(2)}) async-start(bf16[8,2,3,160,128]{4,3,2,1,0:T(8,128)(2,1)} %get-tuple-element.44), calls=%async_computation | async-start | bytes 3932160 | tf_op jit(solution)/shard_map/all_to_all | solution.py:569
  11.4 0.1 copy.24.coeff_ref
  11.5 1.8 copy-done.3
  13.3 2.4 %sum_pairs.1.here_ref = f32[18,2,1280]{2,1,0:T(2,128)S(1)} custom-call(f32[32,2]{1,0:T(8,128)S(1)} %copy.24.coeff_ref, f32[8,128]{1,0:T(8,128)S(1)} %copy-done.9, bf16[32,18,2,1280]{3,2,1,0:T(2,128)(2,1)S(1)} %copy-done.3), custom_call_target="tpu_custom_call" | custom-call | flops 5898240 | bytes 2949120 | tf_op jit(solution)/shard_map/sum_pairs/pallas_call | solution.py:343
  15.7 1.6 collective-permute-start
  17.3 4.6 %collective-permute-done.rest_0_.there_ref = f32[18,2,1280]{2,1,0:T(2,128)S(1)} collective-permute-done((f32[18,2,1280]{2,1,0:T(2,128)S(1)}, f32[18,2,1280]{2,1,0:T(2,128)S(1)}, u32[]{:S(2)}, u32[]{:S(2)}) %collective-permute-start) | collective-permute-done | bytes 184352 | tf_op jit(solution)/shard_map/ppermute | solution.py:589
  21.9 0.7 copy-done.1
  22.5 4.2 %weigh.3 = (bf16[8,2,3,160,128]{4,3,2,1,0:T(8,128)(2,1)}, bf16[8,3,160,128]{3,2,1,0:T(8,128)(2,1)}, f32[8,128]{1,0:T(8,128)}) custom-call(s32[1]{0:T(128)} %bitcast.me_ref, f32[1,160]{1,0:T(1,128)} %bitcast.4, bf16[3,160,32,128]{3,2,1,0:T(8,128)(2,1)} %tendency_ref.3, f32[18,2,1280]{2,1,0:T(2,128)} %copy-done.1), custom_call_target="tpu_custom_call" | custom-call | flops 503316480 | bytes 5898240 | tf_op jit(solution)/shard_map/weigh/pallas_call | solution.py:147
  26.7 0.1 collective-permute-start.1
  26.8 2.8 %collective-permute-done.1.mate_ref = bf16[8,3,160,128]{3,2,1,0:T(8,128)(2,1)S(1)} collective-permute-done((bf16[8,3,160,128]{3,2,1,0:T(8,128)(2,1)}, bf16[8,3,160,128]{3,2,1,0:T(8,128)(2,1)S(1)}, u32[]{:S(2)}, u32[]{:S(2)}) %collective-permute-start.1) | collective-permute-done | bytes 983072 | tf_op jit(solution)/shard_map/ppermute | solution.py:555
  29.6 0.9 pair.3
  30.5 24.5 %all-to-all-done.in_ref.rest_0_ = bf16[8,2,3,160,128]{4,3,2,1,0:T(8,128)(2,1)} async-done(((bf16[8,2,3,160,128]{4,3,2,1,0:T(8,128)(2,1)}), bf16[8,2,3,160,128]{4,3,2,1,0:T(8,128)(2,1)}, u32[]{:S(2)}, u32[]{:S(2)}) %all-to-all-start) | async-done | bytes 1966112 | tf_op jit(solution)/shard_map/all_to_all | solution.py:569
  55.0 6.1 %all-to-all-start.2 = ((bf16[8,2,3,160,128]{4,3,2,1,0:T(8,128)(2,1)}), bf16[8,2,3,160,128]{4,3,2,1,0:T(8,128)(2,1)}, u32[]{:S(2)}, u32[]{:S(2)}) async-start(bf16[8,2,3,160,128]{4,3,2,1,0:T(8,128)(2,1)} %get-tuple-element.49), calls=%async_computation.2 | async-start | bytes 3932160 | tf_op jit(solution)/shard_map/all_to_all | solution.py:569
  61.1 1.3 pick.1
  62.3 0.1 collective-permute-start.2
  62.4 2.6 %collective-permute-done.2.rest_1_ = bf16[8,3,160,128]{3,2,1,0:T(8,128)(2,1)S(1)} collective-permute-done((bf16[8,3,160,128]{3,2,1,0:T(8,128)(2,1)S(1)}, bf16[8,3,160,128]{3,2,1,0:T(8,128)(2,1)S(1)}, u32[]{:S(2)}, u32[]{:S(2)}) %collective-permute-start.2) | collective-permute-done | bytes 983072 | tf_op jit(solution)/shard_map/ppermute | solution.py:555
  65.0 5.9 %analyse.3.own_ref = bf16[3,128,640]{2,1,0:T(8,128)(2,1)S(1)} custom-call(s32[1]{0:T(128)} %bitcast.me_ref, s32[2]{0:T(128)S(1)} %copy-done.8, f32[8,128]{1,0:T(8,128)S(1)} %get-tuple-element.43.token_ref, bf16[2,1280,2560]{2,1,0:T(8,128)(2,1)} %table_ref.11, bf16[3,2,128,1280]{3,2,1,0:T(8,128)(2,1)} %state_ref.5, ...), custom_call_target="tpu_custom_call" | custom-call | flops 1258291200 | bytes 3276800 | tf_op jit(solution)/shard_map/analyse/pallas_call | solution.py:301
  70.8 1.6 collective-permute-start.3
  72.4 11.7 %collective-permute-done.3.other_ref = bf16[3,128,640]{2,1,0:T(8,128)(2,1)S(1)} collective-permute-done((bf16[3,128,640]{2,1,0:T(8,128)(2,1)S(1)}, bf16[3,128,640]{2,1,0:T(8,128)(2,1)S(1)}, u32[]{:S(2)}, u32[]{:S(2)}) %collective-permute-start.3) | collective-permute-done | bytes 491552 | tf_op jit(solution)/shard_map/ppermute | solution.py:603
  84.2 5.0 %synthesise.3 = (bf16[8,2,3,160,128]{4,3,2,1,0:T(8,128)(2,1)S(1)}, bf16[8,3,160,128]{3,2,1,0:T(8,128)(2,1)S(1)}) custom-call(s32[1]{0:T(128)} %bitcast.me_ref, f32[1]{0:T(128)} %bitcast.1.sign_ref, f32[18,2,1280]{2,1,0:T(2,128)S(1)} %sum_pairs.1.here_ref, f32[18,2,1280]{2,1,0:T(2,128)S(1)} %copy-done.2, bf16[3,128,640]{2,1,0:T(8,128)(2,1)S(1)} %analyse.3.own_ref, ...), custom_call_target="tpu_custom_call" | custom-call | flops 1258291200 | bytes 3276800 | tf_op jit(solution)/shard_map/synthesise/pallas_call | solution.py:449
  89.1 0.1 collective-permute-start.4
  89.2 2.6 %collective-permute-done.4.mate_ref = bf16[8,3,160,128]{3,2,1,0:T(8,128)(2,1)S(1)} collective-permute-done((bf16[8,3,160,128]{3,2,1,0:T(8,128)(2,1)S(1)}, bf16[8,3,160,128]{3,2,1,0:T(8,128)(2,1)S(1)}, u32[]{:S(2)}, u32[]{:S(2)}) %collective-permute-start.4) | collective-permute-done | bytes 983072 | tf_op jit(solution)/shard_map/ppermute | solution.py:555
  91.8 0.1 pair.4
  91.9 0.0 copy-start
  91.9 1.3 copy-done
  93.1 9.6 %all-to-all-done.2.rest_0_ = bf16[8,2,3,160,128]{4,3,2,1,0:T(8,128)(2,1)} async-done(((bf16[8,2,3,160,128]{4,3,2,1,0:T(8,128)(2,1)}), bf16[8,2,3,160,128]{4,3,2,1,0:T(8,128)(2,1)}, u32[]{:S(2)}, u32[]{:S(2)}) %all-to-all-start.2) | async-done | bytes 1966112 | tf_op jit(solution)/shard_map/all_to_all | solution.py:569
  102.8 6.0 %all-to-all-start.1 = ((bf16[8,2,3,160,128]{4,3,2,1,0:T(8,128)(2,1)}), bf16[8,2,3,160,128]{4,3,2,1,0:T(8,128)(2,1)S(1)}, u32[]{:S(2)}, u32[]{:S(2)}) async-start(bf16[8,2,3,160,128]{4,3,2,1,0:T(8,128)(2,1)} %copy-done), calls=%async_computation.1 | async-start | bytes 3932160 | tf_op jit(solution)/shard_map/all_to_all | solution.py:569
  108.8 6.1 %analyse.5.own_ref = bf16[3,128,640]{2,1,0:T(8,128)(2,1)S(1)} custom-call(s32[1]{0:T(128)} %bitcast.me_ref, s32[2]{0:T(128)S(1)} %copy-done.8, f32[8,128]{1,0:T(8,128)S(1)} %get-tuple-element.48.token_ref, bf16[2,1280,2560]{2,1,0:T(8,128)(2,1)} %table_ref.11, bf16[3,2,128,1280]{3,2,1,0:T(8,128)(2,1)} %state_ref.5, ...), custom_call_target="tpu_custom_call" | custom-call | flops 1258291200 | bytes 3276800 | tf_op jit(solution)/shard_map/analyse/pallas_call | solution.py:301
  115.0 1.6 collective-permute-start.6
  116.6 6.1 %analyse.4.own_ref = bf16[3,128,640]{2,1,0:T(8,128)(2,1)S(1)} custom-call(s32[1]{0:T(128)} %bitcast.me_ref, s32[2]{0:T(128)S(1)} %copy-done.8, f32[8,128]{1,0:T(8,128)S(1)} %get-tuple-element.48.token_ref, bf16[2,1280,2560]{2,1,0:T(8,128)(2,1)} %table_ref.11, bf16[3,2,128,1280]{3,2,1,0:T(8,128)(2,1)} %state_ref.5, ...), custom_call_target="tpu_custom_call" | custom-call | flops 1258291200 | bytes 3276800 | tf_op jit(solution)/shard_map/analyse/pallas_call | solution.py:301
  122.7 0.6 collective-permute-start.5
  123.3 5.9 %collective-permute-done.6.other_ref = bf16[3,128,640]{2,1,0:T(8,128)(2,1)S(1)} collective-permute-done((bf16[3,128,640]{2,1,0:T(8,128)(2,1)S(1)}, bf16[3,128,640]{2,1,0:T(8,128)(2,1)S(1)}, u32[]{:S(2)}, u32[]{:S(2)}) %collective-permute-start.6) | collective-permute-done | bytes 491552 | tf_op jit(solution)/shard_map/ppermute | solution.py:603
  129.2 4.8 %synthesise.4.rest_0_ = f32[384,2560]{1,0:T(8,128)S(1)} custom-call(s32[1]{0:T(128)} %bitcast.me_ref, f32[1]{0:T(128)} %bitcast.1.sign_ref, f32[18,2,1280]{2,1,0:T(2,128)S(1)} %sum_pairs.1.here_ref, f32[18,2,1280]{2,1,0:T(2,128)S(1)} %copy-done.2, bf16[3,128,640]{2,1,0:T(8,128)(2,1)S(1)} %analyse.5.own_ref, ...), custom_call_target="tpu_custom_call" | custom-call | flops 1258291200 | bytes 3276800 | tf_op jit(solution)/shard_map/synthesise/pallas_call | solution.py:449
  134.1 4.0 %collective-permute-done.5.other_ref = bf16[3,128,640]{2,1,0:T(8,128)(2,1)S(1)} collective-permute-done((bf16[3,128,640]{2,1,0:T(8,128)(2,1)S(1)}, bf16[3,128,640]{2,1,0:T(8,128)(2,1)S(1)}, u32[]{:S(2)}, u32[]{:S(2)}) %collective-permute-start.5) | collective-permute-done | bytes 491552 | tf_op jit(solution)/shard_map/ppermute | solution.py:603
  138.1 6.7 %synthesise.5 = (bf16[2,3,160,128]{3,2,1,0:T(8,128)(2,1)S(1)}, bf16[2,2,160,128]{3,2,1,0:T(8,128)(2,1)S(1)}, bf16[2,2,160,128]{3,2,1,0:T(8,128)(2,1)S(1)}, bf16[...) custom-call(s32[1]{0:T(128)} %bitcast.me_ref, ...), custom_call_target="tpu_custom_call" | custom-call | flops 1258291200 | bytes 3276800 | tf_op jit(solution)/shard_map/synthesise/pallas_call | solution.py:449
  144.8 0.1 collective-permute-start.7
  144.9 2.6 %collective-permute-done.7.mate_ref = bf16[8,3,160,128]{3,2,1,0:T(8,128)(2,1)S(1)} collective-permute-done((bf16[8,3,160,128]{3,2,1,0:T(8,128)(2,1)S(1)}, bf16[8,3,160,128]{3,2,1,0:T(8,128)(2,1)S(1)}, u32[]{:S(2)}, u32[]{:S(2)}) %collective-permute-start.7) | collective-permute-done | bytes 983072 | tf_op jit(solution)/shard_map/ppermute | solution.py:555
  147.5 1.3 pair.5
  148.8 3.9 %collective-permute-start.12 = (bf16[2,2,160,128]{3,2,1,0:T(8,128)(2,1)S(1)}, bf16[2,2,160,128]{3,2,1,0:T(8,128)(2,1)S(1)}, u32[]{:S(2)}, u32[]{:S(2)}) collective-permute-start(bf16[2,2,160,128]{3,2,1,0:T(8,128)(2,1)S(1)} %get-tuple-element.67), channel_id=1, source_target_pairs={{0,14},{1,15},{2,12},{3,13},{4,10},{5,11},{6,8},{7,9},{8,6},{9,7},... | collective-permute-start | bytes 491528 | tf_op jit(solution)/shard_map/ppermute | solution.py:562
  152.7 1.2 collective-permute-start.13
  153.9 0.3 collective-permute-start.16
  154.2 0.0 collective-permute-start.17
  154.2 3.2 %collective-permute-start.18 = (bf16[2,3,160,128]{3,2,1,0:T(8,128)(2,1)S(1)}, bf16[2,3,160,128]{3,2,1,0:T(8,128)(2,1)S(1)}, u32[]{:S(2)}, u32[]{:S(2)}) collective-permute-start(bf16[2,3,160,128]{3,2,1,0:T(8,128)(2,1)S(1)} %get-tuple-element.74), channel_id=1, source_target_pairs={{0,6},{1,7},{2,4},{3,5},{4,2},{5,3},{6,0},{7,1},{8,14},{9,15},{10,... | collective-permute-start | bytes 737288 | tf_op jit(solution)/shard_map/ppermute | solution.py:562
  157.4 1.5 collective-permute-done.12.rest_0_
  158.8 8.8 %collective-permute-start.14 = (bf16[2,2,160,128]{3,2,1,0:T(8,128)(2,1)S(1)}, bf16[2,2,160,128]{3,2,1,0:T(8,128)(2,1)S(1)}, u32[]{:S(2)}, u32[]{:S(2)}) collective-permute-start(bf16[2,2,160,128]{3,2,1,0:T(8,128)(2,1)S(1)} %get-tuple-element.69), channel_id=1, source_target_pairs={{0,10},{1,11},{2,8},{3,9},{4,14},{5,15},{6,12},{7,13},{8,2},{9,3},... | collective-permute-start | bytes 491528 | tf_op jit(solution)/shard_map/ppermute | solution.py:562
  167.7 0.0 collective-permute-done.13.rest_1_
  167.7 0.7 copy-done.4
  168.3 0.9 collective-permute-start.15
  169.2 13.0 %collective-permute-done.14.rest_2_ = bf16[2,2,160,128]{3,2,1,0:T(8,128)(2,1)S(1)} collective-permute-done((bf16[2,2,160,128]{3,2,1,0:T(8,128)(2,1)S(1)}, bf16[2,2,160,128]{3,2,1,0:T(8,128)(2,1)S(1)}, u32[]{:S(2)}, u32[]{:S(2)}) %collective-permute-start.14) | collective-permute-done | bytes 163872 | tf_op jit(solution)/shard_map/ppermute | solution.py:562
  182.2 0.7 copy-done.6
  182.8 1.6 collective-permute-start.8
  184.4 0.0 collective-permute-done.16.rest_1_
  184.4 0.0 collective-permute-start.9
  184.4 0.0 collective-permute-done.17.rest_2_
  184.4 0.1 collective-permute-start.10
  184.5 6.0 %collective-permute-start.11 = (bf16[2,1,160,128]{3,2,1,0:T(8,128)(2,1)}, bf16[2,1,160,128]{3,2,1,0:T(8,128)(2,1)}, u32[]{:S(2)}, u32[]{:S(2)}) collective-permute-start(bf16[2,1,160,128]{3,2,1,0:T(8,128)(2,1)} %get-tuple-element.66), channel_id=1, source_target_pairs={{0,8},{1,9},{2,10},{3,11},{4,12},{5,13},{6,14},{7,15},{8,0},{9,1},... | collective-permute-start | bytes 245768 | tf_op jit(solution)/shard_map/ppermute | solution.py:562
  190.5 0.0 all-to-all-done.1.blocks_ref
  190.5 2.7 %assemble.3.rest_4_ = bf16[3,160,32,128]{3,2,1,0:T(8,128)(2,1)} custom-call(s32[1]{0:T(128)} %bitcast.me_ref, bf16[8,2,3,160,128]{4,3,2,1,0:T(8,128)(2,1)S(1)} %all-to-all-done.1.blocks_ref, bf16[2,3,160,128]{3,2,1,0:T(8,128)(2,1)S(1)} %get-tuple-element.71.rest_0_, bf16[2,3,160,128]{3,2,1,0:T(8,128)(2,1)S(1)} %collective-permute-done.16.rest_1_, ...), custom_call_target="tpu_custom_call" | custom-call | flops 503316480 | bytes 3932160 | tf_op jit(solution)/shard_map/assemble/pallas_call | solution.py:536
  193.3 2.7 %assemble.4.rest_4_ = bf16[3,160,32,128]{3,2,1,0:T(8,128)(2,1)} custom-call(s32[1]{0:T(128)} %bitcast.me_ref, bf16[8,2,3,160,128]{4,3,2,1,0:T(8,128)(2,1)S(1)} %all-to-all-done.1.blocks_ref, bf16[2,2,160,128]{3,2,1,0:T(8,128)(2,1)S(1)} %collective-permute-done.12.rest_0_, bf16[2,2,160,128]{3,2,1,0:T(8,128)(2,1)S(1)} %copy-done.5, ...), custom_call_target="tpu_custom_call", output_to_operand_aliasing={{}: (6, {})} | custom-call | flops 335544320 | bytes 2621440 | tf_op jit(solution)/shard_map/assemble/pallas_call | solution.py:536
  196.0 0.0 collective-permute-done.8.rest_0_
  196.0 1.9 collective-permute-done.10.rest_2_
  197.9 2.3 %assemble.5 = bf16[3,160,32,128]{3,2,1,0:T(8,128)(2,1)} custom-call(s32[1]{0:T(128)} %bitcast.me_ref, bf16[8,2,3,160,128]{4,3,2,1,0:T(8,128)(2,1)S(1)} %all-to-all-done.1.blocks_ref, bf16[2,1,160,128]{3,2,1,0:T(8,128)(2,1)S(1)} %collective-permute-done.8.rest_0_, ...), custom_call_target="tpu_custom_call", output_to_operand_aliasing={{}: (6, {})} | custom-call | flops 167772160 | bytes 1310720 | tf_op jit(solution)/shard_map/assemble/pallas_call | solution.py:536
  (19 shorter events, 0.0 us)
Async XLA Ops:
  4.1 7.3 %copy-start.10 = (f32[32,2]{0,1:T(2,128)S(1)}, f32[32,2]{0,1:T(2,128)}, u32[]{:S(2)}) copy-start(f32[32,2]{0,1:T(2,128)} %param.12) | copy-start | bytes 772
  4.1 7.4 %copy-start.9 = (f32[8,128]{1,0:T(8,128)S(1)}, f32[8,128]{1,0:T(8,128)}, u32[]{:S(2)}) copy-start(f32[8,128]{1,0:T(8,128)} %get-tuple-element.40.token_ref) | copy-start | bytes 12292
  4.1 50.8 %all-to-all-start = ((bf16[8,2,3,160,128]{4,3,2,1,0:T(8,128)(2,1)}), bf16[8,2,3,160,128]{4,3,2,1,0:T(8,128)(2,1)}, u32[]{:S(2)}, u32[]{:S(2)}) async-start(bf16[8,2,3,160,128]{4,3,2,1,0:T(8,128)(2,1)} %get-tuple-element.44), calls=%async_computation | async-start | bytes 3932160 | tf_op jit(solution)/shard_map/all_to_all | solution.py:569
  11.5 1.8 copy-start.3
  15.7 6.2 %collective-permute-start = (f32[18,2,1280]{2,1,0:T(2,128)S(1)}, f32[18,2,1280]{2,1,0:T(2,128)S(1)}, u32[]{:S(2)}, u32[]{:S(2)}) collective-permute-start(f32[18,2,1280]{2,1,0:T(2,128)S(1)} %sum_pairs.1.here_ref), channel_id=1, source_target_pairs={{0,16},{16,0},{1,17},{17,1},{2,18},{18,2},{3,19},{19,3},{4,20},{20... | collective-permute-start | bytes 552968 | tf_op jit(solution)/shard_map/ppermute | solution.py:589
  21.9 0.7 copy-start.1
  26.7 2.8 %collective-permute-start.1 = (bf16[8,3,160,128]{3,2,1,0:T(8,128)(2,1)}, bf16[8,3,160,128]{3,2,1,0:T(8,128)(2,1)S(1)}, u32[]{:S(2)}, u32[]{:S(2)}) collective-permute-start(bf16[8,3,160,128]{3,2,1,0:T(8,128)(2,1)} %get-tuple-element.41), channel_id=1, source_target_pairs={{0,1},{1,0},{2,3},{3,2},{4,5},{5,4},{6,7},{7,6},{8,9},{9,8},{10,11... | collective-permute-start | bytes 2949128 | tf_op jit(solution)/shard_map/ppermute | solution.py:555
  55.0 47.8 %all-to-all-start.2 = ((bf16[8,2,3,160,128]{4,3,2,1,0:T(8,128)(2,1)}), bf16[8,2,3,160,128]{4,3,2,1,0:T(8,128)(2,1)}, u32[]{:S(2)}, u32[]{:S(2)}) async-start(bf16[8,2,3,160,128]{4,3,2,1,0:T(8,128)(2,1)} %get-tuple-element.49), calls=%async_computation.2 | async-start | bytes 3932160 | tf_op jit(solution)/shard_map/all_to_all | solution.py:569
  61.0 3.9 %copy-start.8 = (s32[2]{0:T(128)S(1)}, s32[2]{0:T(128)}, u32[]{:S(2)}) copy-start(s32[2]{0:T(128)} %wave_ref.5) | copy-start | bytes 28
  62.3 21.9 %copy-start.2 = (f32[18,2,1280]{2,1,0:T(2,128)S(1)}, f32[18,2,1280]{2,1,0:T(2,128)}, u32[]{:S(2)}) copy-start(f32[18,2,1280]{2,1,0:T(2,128)} %copy-done.1) | copy-start | bytes 552964
  62.3 2.6 %collective-permute-start.2 = (bf16[8,3,160,128]{3,2,1,0:T(8,128)(2,1)S(1)}, bf16[8,3,160,128]{3,2,1,0:T(8,128)(2,1)S(1)}, u32[]{:S(2)}, u32[]{:S(2)}) collective-permute-start(bf16[8,3,160,128]{3,2,1,0:T(8,128)(2,1)S(1)} %pick.1), channel_id=1, source_target_pairs={{0,1},{1,0},{2,3},{3,2},{4,5},{5,4},{6,7},{7,6},{8,9},{9,8},{10,11... | collective-permute-start | bytes 2949128 | tf_op jit(solution)/shard_map/ppermute | solution.py:555
  70.8 13.3 %collective-permute-start.3 = (bf16[3,128,640]{2,1,0:T(8,128)(2,1)S(1)}, bf16[3,128,640]{2,1,0:T(8,128)(2,1)S(1)}, u32[]{:S(2)}, u32[]{:S(2)}) collective-permute-start(bf16[3,128,640]{2,1,0:T(8,128)(2,1)S(1)} %analyse.3.own_ref), channel_id=1, source_target_pairs={{0,16},{16,0},{1,17},{17,1},{2,18},{18,2},{3,19},{19,3},{4,20},{20... | collective-permute-start | bytes 1474568 | tf_op jit(solution)/shard_map/ppermute | solution.py:603
  89.1 2.6 %collective-permute-start.4 = (bf16[8,3,160,128]{3,2,1,0:T(8,128)(2,1)S(1)}, bf16[8,3,160,128]{3,2,1,0:T(8,128)(2,1)S(1)}, u32[]{:S(2)}, u32[]{:S(2)}) collective-permute-start(bf16[8,3,160,128]{3,2,1,0:T(8,128)(2,1)S(1)} %get-tuple-element.45), channel_id=1, source_target_pairs={{0,1},{1,0},{2,3},{3,2},{4,5},{5,4},{6,7},{7,6},{8,9},{9,8},{10,11... | collective-permute-start | bytes 2949128 | tf_op jit(solution)/shard_map/ppermute | solution.py:555
  91.9 1.3 copy-start
  102.8 87.7 %all-to-all-start.1 = ((bf16[8,2,3,160,128]{4,3,2,1,0:T(8,128)(2,1)}), bf16[8,2,3,160,128]{4,3,2,1,0:T(8,128)(2,1)S(1)}, u32[]{:S(2)}, u32[]{:S(2)}) async-start(bf16[8,2,3,160,128]{4,3,2,1,0:T(8,128)(2,1)} %copy-done), calls=%async_computation.1 | async-start | bytes 3932160 | tf_op jit(solution)/shard_map/all_to_all | solution.py:569
  115.0 14.2 %collective-permute-start.6 = (bf16[3,128,640]{2,1,0:T(8,128)(2,1)S(1)}, bf16[3,128,640]{2,1,0:T(8,128)(2,1)S(1)}, u32[]{:S(2)}, u32[]{:S(2)}) collective-permute-start(bf16[3,128,640]{2,1,0:T(8,128)(2,1)S(1)} %analyse.5.own_ref), channel_id=1, source_target_pairs={{0,16},{16,0},{1,17},{17,1},{2,18},{18,2},{3,19},{19,3},{4,20},{20... | collective-permute-start | bytes 1474568 | tf_op jit(solution)/shard_map/ppermute | solution.py:603
  122.7 15.4 %collective-permute-start.5 = (bf16[3,128,640]{2,1,0:T(8,128)(2,1)S(1)}, bf16[3,128,640]{2,1,0:T(8,128)(2,1)S(1)}, u32[]{:S(2)}, u32[]{:S(2)}) collective-permute-start(bf16[3,128,640]{2,1,0:T(8,128)(2,1)S(1)} %analyse.4.own_ref), channel_id=1, source_target_pairs={{0,16},{16,0},{1,17},{17,1},{2,18},{18,2},{3,19},{19,3},{4,20},{20... | collective-permute-start | bytes 1474568 | tf_op jit(solution)/shard_map/ppermute | solution.py:603
  144.8 2.6 %collective-permute-start.7 = (bf16[8,3,160,128]{3,2,1,0:T(8,128)(2,1)S(1)}, bf16[8,3,160,128]{3,2,1,0:T(8,128)(2,1)S(1)}, u32[]{:S(2)}, u32[]{:S(2)}) collective-permute-start(bf16[8,3,160,128]{3,2,1,0:T(8,128)(2,1)S(1)} %get-tuple-element.50), channel_id=1, source_target_pairs={{0,1},{1,0},{2,3},{3,2},{4,5},{5,4},{6,7},{7,6},{8,9},{9,8},{10,11... | collective-permute-start | bytes 2949128 | tf_op jit(solution)/shard_map/ppermute | solution.py:555
  148.8 10.0 %collective-permute-start.12 = (bf16[2,2,160,128]{3,2,1,0:T(8,128)(2,1)S(1)}, bf16[2,2,160,128]{3,2,1,0:T(8,128)(2,1)S(1)}, u32[]{:S(2)}, u32[]{:S(2)}) collective-permute-start(bf16[2,2,160,128]{3,2,1,0:T(8,128)(2,1)S(1)} %get-tuple-element.67), channel_id=1, source_target_pairs={{0,14},{1,15},{2,12},{3,13},{4,10},{5,11},{6,8},{7,9},{8,6},{9,7},... | collective-permute-start | bytes 491528 | tf_op jit(solution)/shard_map/ppermute | solution.py:562
  152.7 15.0 %collective-permute-start.13 = (bf16[2,2,160,128]{3,2,1,0:T(8,128)(2,1)S(1)}, bf16[2,2,160,128]{3,2,1,0:T(8,128)(2,1)S(1)}, u32[]{:S(2)}, u32[]{:S(2)}) collective-permute-start(bf16[2,2,160,128]{3,2,1,0:T(8,128)(2,1)S(1)} %get-tuple-element.68), channel_id=1, source_target_pairs={{0,12},{1,13},{2,14},{3,15},{4,8},{5,9},{6,10},{7,11},{8,4},{9,5},... | collective-permute-start | bytes 491528 | tf_op jit(solution)/shard_map/ppermute | solution.py:562
  153.9 30.5 %collective-permute-start.16 = (bf16[2,3,160,128]{3,2,1,0:T(8,128)(2,1)S(1)}, bf16[2,3,160,128]{3,2,1,0:T(8,128)(2,1)S(1)}, u32[]{:S(2)}, u32[]{:S(2)}) collective-permute-start(bf16[2,3,160,128]{3,2,1,0:T(8,128)(2,1)S(1)} %get-tuple-element.72), channel_id=1, source_target_pairs={{0,2},{1,3},{2,0},{3,1},{4,6},{5,7},{6,4},{7,5},{8,10},{9,11},{10,... | collective-permute-start | bytes 737288 | tf_op jit(solution)/shard_map/ppermute | solution.py:562
  154.2 30.3 %collective-permute-start.17 = (bf16[2,3,160,128]{3,2,1,0:T(8,128)(2,1)S(1)}, bf16[2,3,160,128]{3,2,1,0:T(8,128)(2,1)S(1)}, u32[]{:S(2)}, u32[]{:S(2)}) collective-permute-start(bf16[2,3,160,128]{3,2,1,0:T(8,128)(2,1)S(1)} %get-tuple-element.73), channel_id=1, source_target_pairs={{0,4},{1,5},{2,6},{3,7},{4,0},{5,1},{6,2},{7,3},{8,12},{9,13},{10,... | collective-permute-start | bytes 737288 | tf_op jit(solution)/shard_map/ppermute | solution.py:562
  154.2 30.3 %collective-permute-start.18 = (bf16[2,3,160,128]{3,2,1,0:T(8,128)(2,1)S(1)}, bf16[2,3,160,128]{3,2,1,0:T(8,128)(2,1)S(1)}, u32[]{:S(2)}, u32[]{:S(2)}) collective-permute-start(bf16[2,3,160,128]{3,2,1,0:T(8,128)(2,1)S(1)} %get-tuple-element.74), channel_id=1, source_target_pairs={{0,6},{1,7},{2,4},{3,5},{4,2},{5,3},{6,0},{7,1},{8,14},{9,15},{10,... | collective-permute-start | bytes 737288 | tf_op jit(solution)/shard_map/ppermute | solution.py:562
  158.8 23.3 %collective-permute-start.14 = (bf16[2,2,160,128]{3,2,1,0:T(8,128)(2,1)S(1)}, bf16[2,2,160,128]{3,2,1,0:T(8,128)(2,1)S(1)}, u32[]{:S(2)}, u32[]{:S(2)}) collective-permute-start(bf16[2,2,160,128]{3,2,1,0:T(8,128)(2,1)S(1)} %get-tuple-element.69), channel_id=1, source_target_pairs={{0,10},{1,11},{2,8},{3,9},{4,14},{5,15},{6,12},{7,13},{8,2},{9,3},... | collective-permute-start | bytes 491528 | tf_op jit(solution)/shard_map/ppermute | solution.py:562
  167.7 0.7 copy-start.4
  168.3 24.9 %collective-permute-start.15 = (bf16[2,2,160,128]{3,2,1,0:T(8,128)(2,1)S(1)}, bf16[2,2,160,128]{3,2,1,0:T(8,128)(2,1)}, u32[]{:S(2)}, u32[]{:S(2)}) collective-permute-start(bf16[2,2,160,128]{3,2,1,0:T(8,128)(2,1)S(1)} %get-tuple-element.70), channel_id=1, source_target_pairs={{0,8},{1,9},{2,10},{3,11},{4,12},{5,13},{6,14},{7,15},{8,0},{9,1},... | collective-permute-start | bytes 491528 | tf_op jit(solution)/shard_map/ppermute | solution.py:562
  182.2 0.7 copy-start.6
  182.8 13.2 %collective-permute-start.8 = (bf16[2,1,160,128]{3,2,1,0:T(8,128)(2,1)}, bf16[2,1,160,128]{3,2,1,0:T(8,128)(2,1)S(1)}, u32[]{:S(2)}, u32[]{:S(2)}) collective-permute-start(bf16[2,1,160,128]{3,2,1,0:T(8,128)(2,1)} %get-tuple-element.63), channel_id=1, source_target_pairs={{0,14},{1,15},{2,12},{3,13},{4,10},{5,11},{6,8},{7,9},{8,6},{9,7},... | collective-permute-start | bytes 245768 | tf_op jit(solution)/shard_map/ppermute | solution.py:562
  184.4 11.6 %collective-permute-start.9 = (bf16[2,1,160,128]{3,2,1,0:T(8,128)(2,1)}, bf16[2,1,160,128]{3,2,1,0:T(8,128)(2,1)S(1)}, u32[]{:S(2)}, u32[]{:S(2)}) collective-permute-start(bf16[2,1,160,128]{3,2,1,0:T(8,128)(2,1)} %get-tuple-element.64), channel_id=1, source_target_pairs={{0,12},{1,13},{2,14},{3,15},{4,8},{5,9},{6,10},{7,11},{8,4},{9,5},... | collective-permute-start | bytes 245768 | tf_op jit(solution)/shard_map/ppermute | solution.py:562
  184.4 13.5 %collective-permute-start.10 = (bf16[2,1,160,128]{3,2,1,0:T(8,128)(2,1)}, bf16[2,1,160,128]{3,2,1,0:T(8,128)(2,1)}, u32[]{:S(2)}, u32[]{:S(2)}) collective-permute-start(bf16[2,1,160,128]{3,2,1,0:T(8,128)(2,1)} %get-tuple-element.65), channel_id=1, source_target_pairs={{0,10},{1,11},{2,8},{3,9},{4,14},{5,15},{6,12},{7,13},{8,2},{9,3},... | collective-permute-start | bytes 245768 | tf_op jit(solution)/shard_map/ppermute | solution.py:562
  184.5 13.4 %collective-permute-start.11 = (bf16[2,1,160,128]{3,2,1,0:T(8,128)(2,1)}, bf16[2,1,160,128]{3,2,1,0:T(8,128)(2,1)}, u32[]{:S(2)}, u32[]{:S(2)}) collective-permute-start(bf16[2,1,160,128]{3,2,1,0:T(8,128)(2,1)} %get-tuple-element.66), channel_id=1, source_target_pairs={{0,8},{1,9},{2,10},{3,11},{4,12},{5,13},{6,14},{7,15},{8,0},{9,1},... | collective-permute-start | bytes 245768 | tf_op jit(solution)/shard_map/ppermute | solution.py:562
  190.5 2.8 %copy-start.5 = (bf16[2,2,160,128]{3,2,1,0:T(8,128)(2,1)S(1)}, bf16[2,2,160,128]{3,2,1,0:T(8,128)(2,1)}, u32[]{:S(2)}) copy-start(bf16[2,2,160,128]{3,2,1,0:T(8,128)(2,1)} %copy-done.4) | copy-start | bytes 491524
  190.5 2.8 %copy-start.7 = (bf16[2,2,160,128]{3,2,1,0:T(8,128)(2,1)S(1)}, bf16[2,2,160,128]{3,2,1,0:T(8,128)(2,1)}, u32[]{:S(2)}) copy-start(bf16[2,2,160,128]{3,2,1,0:T(8,128)(2,1)} %copy-done.6) | copy-start | bytes 491524
